TPU v7x, 32 devices: a whole 2x2x4 slice. The times are simulated.
32 devices in a mesh: grp: 1, ep: 8 (over z, y), rep: 2 (over x), sub: 2 (over core).
Axes of the slice: x: 2, y: 2, z: 4, core: 2. Of those that a mesh axis runs over, the one named last changes fastest.
Arguments:
- output_gradient: bfloat16 [2048, 4096], P(('grp', 'ep', 'sub'), 'rep'), may hold values from -6 to 6
- hidden: bfloat16 [2048, 8, 1536], P(('grp', 'ep', 'sub'), None, 'rep'), may hold values from -0.29882812 to 0.29882812
- route_expert_index: int32 [2048, 8], P(('grp', 'ep', 'sub')), may hold values from 0 to 15, all different within a row; in each aligned block of 128 rows (0 to 127, 128 to 255, ...) at most 80 rows name the same one
- route_weight: bfloat16 [2048, 8], P(('grp', 'ep', 'sub')), may hold values from 0.019897461 to 0.5
- down_matrix: bfloat16 [16, 1536, 4096], P(('ep', 'sub'), None, 'rep'), may hold values from -0.15625 to 0.15625
- first_adapter_factor: bfloat16 [16, 1536, 32], P(('grp', 'ep', 'sub'), 'rep'), may hold values from -0.15625 to 0.15625
- second_adapter_factor: bfloat16 [16, 32, 4096], P(('grp', 'ep', 'sub'), None, 'rep'), may hold values from -0.09375 to 0.09375
Outputs:
- grad_hidden: bfloat16 [2048, 8, 1536], P(('grp', 'ep', 'sub'), None, 'rep')
- grad_probs: float32 [2048, 8], P(('grp', 'ep', 'sub'))
- first_factor_gradient: float32 [16, 1536, 32], P(('grp', 'ep', 'sub'), 'rep')
- second_factor_gradient: float32 [16, 32, 4096], P(('grp', 'ep', 'sub'), None, 'rep')
Inputs may be any that keep to these rules, and one draw needn't show every extreme that they name: `route_expert_index`: each row names 8 different experts; among the rows of one device no expert is named more than 80 times, a bound that some block reaches.
All inputs are finite; a program needn't handle non-finite values.
Results may differ from a plain program's by a relative error of at most 0.0059.
Values may be sent and summed in bfloat16 or wider, within the bound.
No kernel may reach another device: no remote copies, remote signals or barrier semaphores. Data moves between devices by JAX's collectives and lax.ppermute only.
A program may use at most 128 MiB of HBM per device.

v0:
```python
import jax
import jax.numpy as jnp
from jax import lax
from jax.sharding import PartitionSpec as P

adapter_scale = 2.0


def router_sums(pair_hidden, grad_wide, tok_rows, top_count):
    prob_part = jnp.sum(pair_hidden.astype(jnp.float32) * grad_wide, axis=1)
    return lax.psum(prob_part, "rep").reshape(tok_rows, top_count)


def body(
    output_gradient,
    hidden,
    route_expert_index,
    route_weight,
    down_matrix,
    first_adapter_factor,
    second_adapter_factor,
):
    tok_rows, top_count = route_expert_index.shape
    exp_local, ff_all, feat_local = down_matrix.shape
    local_hidden_units = first_adapter_factor.shape[1]
    owners = lax.axis_size(("ep", "sub"))
    experts = owners * exp_local
    capacity = min(tok_rows, 5 * tok_rows * top_count // (4 * experts))
    pair_count = tok_rows * top_count
    flat_ids = route_expert_index.reshape(pair_count)
    expert_hits = (flat_ids[:, None] == jnp.arange(experts, dtype=jnp.int32)[None, :]).astype(
        jnp.int32
    )
    before = jnp.cumsum(expert_hits, axis=0) - expert_hits
    position = jnp.sum(before * expert_hits, axis=1)
    target = flat_ids * capacity + position
    source_pair = (
        jnp.full((experts * capacity,), pair_count, jnp.int32)
        .at[target]
        .set(jnp.arange(pair_count, dtype=jnp.int32))
    )
    filled = source_pair < pair_count
    safe_pair = jnp.minimum(source_pair, pair_count - 1)
    pair_hidden = hidden.reshape(pair_count, local_hidden_units)
    send_grad = jnp.where(filled[:, None], output_gradient[safe_pair // top_count], 0)
    send_hidden = jnp.where(filled[:, None], pair_hidden[safe_pair], 0)
    send_prob = jnp.where(filled, route_weight.reshape(pair_count)[safe_pair], 0)
    buffer_shape = (owners, exp_local, capacity)
    received_gradient, received_hidden, recv_prob = (
        lax.all_to_all(
            send_grad.reshape(buffer_shape + (feat_local,)),
            ("ep", "sub"),
            split_axis=0,
            concat_axis=0,
            tiled=True,
        ),
        lax.all_to_all(
            send_hidden.reshape(buffer_shape + (local_hidden_units,)),
            ("ep", "sub"),
            split_axis=0,
            concat_axis=0,
            tiled=True,
        ),
        lax.all_to_all(
            send_prob.reshape(buffer_shape), ("ep", "sub"), split_axis=0, concat_axis=0, tiled=True
        ),
    )
    lowrank_grad = jnp.einsum(
        "gzpu,zwu->gzpw",
        received_gradient,
        second_adapter_factor,
        preferred_element_type=jnp.float32,
    )
    lowrank_hid = jnp.einsum(
        "yght,gtb->yghb", received_hidden, first_adapter_factor, preferred_element_type=jnp.float32
    )
    grad_total, hid_total = lax.psum((lowrank_grad, lowrank_hid), "rep")
    rank_step_body = grad_total.astype(jnp.bfloat16)
    frozen_contrib = jnp.einsum(
        "secd,efd->secf", received_gradient, down_matrix, preferred_element_type=jnp.float32
    )
    adapter_contrib = adapter_scale * jnp.einsum(
        "kpux,phx->kpuh", rank_step_body, first_adapter_factor, preferred_element_type=jnp.float32
    )
    leading_unit = lax.axis_index("rep") * local_hidden_units
    local_unit_slice = (
        lax.dynamic_slice_in_dim(frozen_contrib, leading_unit, local_hidden_units, 3)
        + adapter_contrib
    )
    frozen_contrib = lax.dynamic_update_slice_in_dim(
        frozen_contrib, local_unit_slice, leading_unit, 3
    )
    summed = lax.psum_scatter(
        frozen_contrib.astype(jnp.bfloat16), "rep", scatter_dimension=3, tiled=True
    )
    returned = lax.all_to_all(summed, ("ep", "sub"), split_axis=0, concat_axis=0, tiled=True)
    pair_grad = returned.reshape(experts * capacity, local_hidden_units)[target]
    grad_wide = pair_grad.astype(jnp.float32)
    pair_prob = route_weight.reshape(pair_count).astype(jnp.float32)
    grad_hidden = (
        (pair_prob[:, None] * grad_wide)
        .astype(jnp.bfloat16)
        .reshape(tok_rows, top_count, local_hidden_units)
    )
    grad_probs = router_sums(pair_hidden, grad_wide, tok_rows, top_count)
    weight_prob = recv_prob.astype(jnp.float32)[..., None]
    weighted_gradient = (grad_total * weight_prob).astype(jnp.bfloat16)
    weighted_hidden = (hid_total * weight_prob).astype(jnp.bfloat16)
    first_factor_gradient = adapter_scale * jnp.einsum(
        "secf,secr->efr", received_hidden, weighted_gradient, preferred_element_type=jnp.float32
    )
    second_factor_gradient = adapter_scale * jnp.einsum(
        "secr,secd->erd", weighted_hidden, received_gradient, preferred_element_type=jnp.float32
    )
    return (grad_hidden, grad_probs, first_factor_gradient, second_factor_gradient)


def solution(mesh):
    return jax.shard_map(
        body,
        mesh=mesh,
        in_specs=(
            P(("grp", "ep", "sub"), "rep"),
            P(("grp", "ep", "sub"), None, "rep"),
            P(("grp", "ep", "sub"), None),
            P(("grp", "ep", "sub"), None),
            P(("ep", "sub"), None, "rep"),
            P(("grp", "ep", "sub"), "rep", None),
            P(("grp", "ep", "sub"), None, "rep"),
        ),
        out_specs=(
            P(("grp", "ep", "sub"), None, "rep"),
            P(("grp", "ep", "sub"), None),
            P(("grp", "ep", "sub"), "rep", None),
            P(("grp", "ep", "sub"), None, "rep"),
        ),
        check_vma=False,
    )
```

profile of v0, /device:TPU:8, one launch (start us, length us, event | category | flops | bytes accessed | tf_op | source)
XLA Modules:
  0.0 378.8 jit_solution(1390140285344859712)
XLA Ops:
  7.2 0.0 copy-start
  7.2 0.0 copy-start.1
  7.2 0.8 broadcast_multiply_fusion
  8.0 0.8 copy.34
  8.8 0.1 eq.29
  8.9 0.1 eq.25
  9.0 0.8 copy.41
  9.8 0.1 reshape.175
  9.9 0.1 copy.33
  10.0 0.1 mul.83
  10.1 4.5 %reduce-window.6 = s32[16,8,128]{2,1,0:T(8,128)S(1)} reduce-window(s32[16,8,128]{2,1,0:T(8,128)S(1)} %fusion.49, s32[]{:T(128)} %constant.18.clone.1), window={size=1x1x128 pad=0_0x0_0x127_0}, to_apply=%region_0.0 | reduce-window | flops 2080768 | bytes 131076 | tf_op jit(solution)/shard_map/reduce-window
  14.6 0.1 slice.16
  14.7 0.1 copy.36
  14.9 0.1 copy.37
  15.0 0.1 broadcast_add_fusion
  15.1 4.3 %scatter_custom_fusion = s32[1280]{0:T(1024)S(1)} fusion(s32[1024]{0:T(1024)S(1)} %bitcast.135, s32[1024]{0:T(1024)S(1)} %iota.11, s32[]{:T(128)} %constant.16.clone.1), kind=kCustom, calls=%fused_computation.63 | custom fusion | bytes 5124 | tf_op jit(solution)/shard_map/scatter | solution.py:40
  19.5 8.0 %gather_fusion.3 = bf16[1280]{0:T(1024)(128)(2,1)S(1)} fusion(bf16[1024]{0:T(1024)(128)(2,1)S(1)} %reshape.175, s32[2048]{0:T(1024)S(1)} %get-tuple-element.20), kind=kCustom, calls=%fused_computation.3 | custom fusion | bytes 10240 | tf_op jit(solution)/shard_map/gather | solution.py:47
  27.5 0.1 broadcast_in_dim.44
  27.6 0.0 copy-done.1
  27.6 4.9 %gather_fusion.2 = bf16[1280,768]{1,0:T(8,128)(2,1)} fusion(bf16[1024,768]{1,0:T(8,128)(2,1)S(1)} %bitcast.125, s32[2048]{0:T(1024)S(1)} %get-tuple-element.20), kind=kCustom, calls=%fused_computation.2 | custom fusion | bytes 3937280 | tf_op jit(solution)/shard_map/gather | solution.py:46
  32.5 3.0 broadcast_select_fusion.1
  35.5 6.3 %all-to-all-start.2 = ((bf16[16,1,80,768]{3,2,1,0:T(8,128)(2,1)}), bf16[16,1,80,768]{3,2,1,0:T(8,128)(2,1)}, u32[]{:S(2)}, u32[]{:S(2)}) async-start(bf16[16,1,80,768]{3,2,1,0:T(8,128)(2,1)} %broadcast_select_fusion.1), calls=%async_computation.3 | async-start | bytes 3932160 | tf_op jit(solution)/shard_map/all_to_all | solution.py:57
  41.8 0.0 copy-done
  41.8 6.1 %gather_fusion = bf16[1280,2048]{1,0:T(8,128)(2,1)} fusion(bf16[128,2048]{1,0:T(8,128)(2,1)S(1)} %copy-done, s32[2048]{0:T(1024)S(1)} %get-tuple-element.21), kind=kCustom, calls=%fused_computation | custom fusion | bytes 10490880 | tf_op jit(solution)/shard_map/gather | solution.py:45
  47.9 5.2 %broadcast_select_fusion = bf16[16,1,80,2048]{3,2,1,0:T(8,128)(2,1)} fusion(bf16[16,1,80,2048]{3,2,1,0:T(8,128)(2,1)} %bitcast.126, pred[16,80]{1,0:T(8,128)(4,1)S(1)} %broadcast_in_dim.44), kind=kLoop, calls=%fused_computation.12 | loop fusion | flops 2621440 | bytes 10487040 | tf_op jit(solution)/shard_map/jit(_where)/select_n | solution.py:45
  53.1 0.0 copy-start.5
  53.1 0.0 copy-start.6
  53.1 31.7 %all-to-all-done.2 = bf16[16,1,80,768]{3,2,1,0:T(8,128)(2,1)} async-done(((bf16[16,1,80,768]{3,2,1,0:T(8,128)(2,1)}), bf16[16,1,80,768]{3,2,1,0:T(8,128)(2,1)}, u32[]{:S(2)}, u32[]{:S(2)}) %all-to-all-start.2) | async-done | bytes 1966112 | tf_op jit(solution)/shard_map/all_to_all | solution.py:57
  84.9 6.6 %all-to-all-start = ((bf16[16,1,80,2048]{3,2,1,0:T(8,128)(2,1)}), bf16[16,1,80,2048]{3,2,1,0:T(8,128)(2,1)}, u32[]{:S(2)}, u32[]{:S(2)}) async-start(bf16[16,1,80,2048]{3,2,1,0:T(8,128)(2,1)} %broadcast_select_fusion), calls=%async_computation | async-start | bytes 10485760 | tf_op jit(solution)/shard_map/all_to_all | solution.py:50
  91.4 0.0 all-reduce.3.cloned.1.call-start
  91.5 0.0 copy-done.5
  91.5 3.1 fusion.25
  94.6 110.1 %all-to-all-done = bf16[16,1,80,2048]{3,2,1,0:T(8,128)(2,1)} async-done(((bf16[16,1,80,2048]{3,2,1,0:T(8,128)(2,1)}), bf16[16,1,80,2048]{3,2,1,0:T(8,128)(2,1)}, u32[]{:S(2)}, u32[]{:S(2)}) %all-to-all-start) | async-done | bytes 5242912 | tf_op jit(solution)/shard_map/all_to_all | solution.py:50
  204.7 0.0 copy-done.6
  204.7 5.4 %fusion.22 = f32[16,1,80,32]{2,3,0,1:T(8,128)} fusion(bf16[16,1,80,2048]{3,2,1,0:T(8,128)(2,1)} %all-to-all-done, bf16[1,32,2048]{2,1,0:T(8,128)(2,1)S(1)} %copy-done.6), kind=kOutput, calls=%fused_computation.26 | convolution fusion | flops 167772160 | bytes 5537792 | tf_op jit(solution)/shard_map/gzpu,zwu->gzpw/dot_general | solution.py:68
  210.1 0.0 all-reduce.3.cloned.1.call-update
  210.1 0.0 reduce-scatter.2.cloned.1.call-start
  210.2 12.1 %fusion = f32[16,80,1536]{2,1,0:T(8,128)S(1)} fusion(bf16[1,1536,2048]{2,1,0:T(8,128)(2,1)} %param.11, bf16[16,1,80,2048]{3,2,1,0:T(8,128)(2,1)} %all-to-all-done), kind=kOutput, calls=%fused_computation.5 | convolution fusion | flops 8053063680 | bytes 19398656 | tf_op jit(solution)/shard_map/secd,efd->secf/dot_general | solution.py:79
  222.3 0.0 copy-start.2
  222.3 3.1 copy-done.2
  225.5 3.1 copy.48
  228.5 11.9 %all-reduce.3.cloned.1.call-done = (f32[16,1,80,32]{2,3,0,1:T(8,128)}, f32[16,1,80,32]{2,3,0,1:T(8,128)}) async-done(((f32[16,1,80,32]{2,3,0,1:T(8,128)}, f32[16,1,80,32]{2,3,0,1:T(8,128)}), (f32[16,1,80,32]{2,3,0,1:T(8,128)}, f32[16,1,80,32]{2,3,0,1:T(8,128)})) %all-reduce.3.cloned.1.call-update) | async-done | bytes 327696 | tf_op jit(solution)/shard_map/psum | solution.py:77
  240.5 5.0 %bitcast_dynamic-update-slice_fusion = f32[16,1,80,1536]{3,2,0,1:T(8,128)} fusion(f32[16,1,80,1536]{3,2,0,1:T(8,128)} %copy.48, s32[]{:T(128)S(6)} %select_n.57, f32[16,80,1536]{2,1,0:T(8,128)} %copy-done.2, f32[16,1,80,32]{2,3,0,1:T(8,128)} %get-tuple-element.12, bf16[1,768,32]{1,2,0:T(8,128)(2,1)S(1)} %copy-done.5), kind=kOutput, calls=%fused_computation.13 | convolution fusion | flops 64921600 | bytes 8175620 | tf_op jit(solution)/shard_map/kpux,phx->kpuh/dot_general | solution.py:82
  245.5 5.8 %convert_element_type.53 = bf16[16,1,80,1536]{3,2,0,1:T(8,128)(2,1)} convert(f32[16,1,80,1536]{3,2,0,1:T(8,128)} %bitcast_dynamic-update-slice_fusion) | non-fusion elementwise | flops 1966080 | bytes 11796480 | tf_op jit(solution)/shard_map/convert_element_type | solution.py:94
  251.3 0.0 copy-start.7
  251.3 0.0 copy-start.3
  251.3 0.0 reduce-scatter.2.cloned.1.call-update
  251.3 0.0 copy-start.4
  251.4 0.1 reshape.230
  251.4 11.0 %all_to_all.20 = bf16[16,1,80]{2,1,0:T(2,128)(2,1)S(1)} all-to-all(bf16[16,1,80]{2,1,0:T(2,128)(2,1)S(1)} %reshape.230), channel_id=1, replica_groups=mesh['grp'=1,'ep'=8,'rep'=2,'sub'=2] {'ep','sub'}, dimensions={0} | all-to-all | bytes 5120 | tf_op jit(solution)/shard_map/all_to_all | solution.py:64
  262.4 41.1 %reduce-scatter.2.cloned.1.call-done = bf16[16,1,80,768]{3,2,0,1:T(8,128)(2,1)} async-done(((bf16[16,1,80,1536]{3,2,0,1:T(8,128)(2,1)}), bf16[16,1,80,768]{3,2,0,1:T(8,128)(2,1)}) %reduce-scatter.2.cloned.1.call-update) | async-done | bytes 1966096 | tf_op jit(solution)/shard_map/reduce_scatter | solution.py:93
  303.5 6.1 %all-to-all-start.1 = ((bf16[16,1,80,768]{3,2,1,0:T(8,128)(2,1)}), bf16[16,1,80,768]{3,2,1,0:T(8,128)(2,1)}, u32[]{:S(2)}, u32[]{:S(2)}) async-start(bf16[16,1,80,768]{3,2,1,0:T(8,128)(2,1)} %bitcast.129), calls=%async_computation.2 | async-start | bytes 3932160 | tf_op jit(solution)/shard_map/all_to_all | solution.py:96
  309.6 0.0 copy-done.7
  309.6 0.1 copy.32
  309.7 0.0 copy-done.3
  309.7 2.6 fusion.34
  312.4 0.0 copy-done.4
  312.4 4.3 %fusion.15 = f32[1,32,2048]{2,1,0:T(8,128)} fusion(bf16[16,1,80,2048]{3,2,1,0:T(8,128)(2,1)} %all-to-all-done, f32[16,1,80,32]{2,3,0,1:T(8,128)S(1)} %copy-done.4, f32[16,80]{1,0:T(8,128)S(1)} %bitcast.132), kind=kOutput, calls=%fused_computation.20 | convolution fusion | flops 167919616 | bytes 5673984 | tf_op jit(solution)/shard_map/secr,secd->erd/dot_general | solution.py:112
  316.7 36.0 %all-to-all-done.1 = bf16[16,1,80,768]{3,2,1,0:T(8,128)(2,1)} async-done(((bf16[16,1,80,768]{3,2,1,0:T(8,128)(2,1)}), bf16[16,1,80,768]{3,2,1,0:T(8,128)(2,1)}, u32[]{:S(2)}, u32[]{:S(2)}) %all-to-all-start.1) | async-done | bytes 1966112 | tf_op jit(solution)/shard_map/all_to_all | solution.py:96
  352.6 7.4 %gather_fusion.1 = bf16[1024,768]{1,0:T(8,128)(2,1)} fusion(bf16[1280,768]{1,0:T(8,128)(2,1)} %bitcast.24, s32[1024]{0:T(1024)S(1)} %broadcast_clamp_fusion), kind=kCustom, calls=%fused_computation.1 | custom fusion | bytes 3149824 | tf_op jit(solution)/shard_map/gather | solution.py:97
  360.0 3.4 fusion.8
  363.4 7.9 %psum.22 = f32[128,8]{1,0:T(8,128)S(1)} all-reduce(f32[128,8]{1,0:T(8,128)S(1)} %get-tuple-element.16), channel_id=1, replica_groups=mesh['grp'=1,'ep'=8,'rep'=2,'sub'=2] {'rep'}, use_global_device_ids=true, to_apply=%region_7.8 | all-reduce | flops 1024 | bytes 8192 | tf_op jit(solution)/shard_map/psum | solution.py:11
  371.3 0.7 copy.43
  (11 shorter events, 0.1 us)
Async XLA Ops:
  7.2 34.6 %copy-start = (bf16[128,2048]{1,0:T(8,128)(2,1)S(1)}, bf16[128,2048]{1,0:T(8,128)(2,1)}, u32[]{:S(2)}) copy-start(bf16[128,2048]{1,0:T(8,128)(2,1)} %param.7) | copy-start | bytes 1572868
  7.2 20.4 %copy-start.1 = (bf16[128,8,768]{2,1,0:T(8,128)(2,1)S(1)}, bf16[128,8,768]{2,1,0:T(8,128)(2,1)}, u32[]{:S(2)}) copy-start(bf16[128,8,768]{2,1,0:T(8,128)(2,1)} %param.8) | copy-start | bytes 4718596
  35.5 49.4 %all-to-all-start.2 = ((bf16[16,1,80,768]{3,2,1,0:T(8,128)(2,1)}), bf16[16,1,80,768]{3,2,1,0:T(8,128)(2,1)}, u32[]{:S(2)}, u32[]{:S(2)}) async-start(bf16[16,1,80,768]{3,2,1,0:T(8,128)(2,1)} %broadcast_select_fusion.1), calls=%async_computation.3 | async-start | bytes 3932160 | tf_op jit(solution)/shard_map/all_to_all | solution.py:57
  53.1 38.3 %copy-start.5 = (bf16[1,768,32]{1,2,0:T(8,128)(2,1)S(1)}, bf16[1,768,32]{1,2,0:T(8,128)(2,1)}, u32[]{:S(2)}) copy-start(bf16[1,768,32]{1,2,0:T(8,128)(2,1)} %param.12) | copy-start | bytes 147460
  53.1 151.6 %copy-start.6 = (bf16[1,32,2048]{2,1,0:T(8,128)(2,1)S(1)}, bf16[1,32,2048]{2,1,0:T(8,128)(2,1)}, u32[]{:S(2)}) copy-start(bf16[1,32,2048]{2,1,0:T(8,128)(2,1)} %param.13) | copy-start | bytes 393220
  84.9 119.8 %all-to-all-start = ((bf16[16,1,80,2048]{3,2,1,0:T(8,128)(2,1)}), bf16[16,1,80,2048]{3,2,1,0:T(8,128)(2,1)}, u32[]{:S(2)}, u32[]{:S(2)}) async-start(bf16[16,1,80,2048]{3,2,1,0:T(8,128)(2,1)} %broadcast_select_fusion), calls=%async_computation | async-start | bytes 10485760 | tf_op jit(solution)/shard_map/all_to_all | solution.py:50
  91.4 149.0 %all-reduce.3.cloned.1.call-start = ((), (), s32[]{:S(2)}) async-start(), calls=%async_computation.6 | async-start | bytes 1048576 | tf_op jit(solution)/shard_map/psum | solution.py:77
  210.1 93.4 %reduce-scatter.2.cloned.1.call-start = ((), (), s32[]{:S(2)}) async-start(), calls=%async_computation.5 | async-start | bytes 5898240 | tf_op jit(solution)/shard_map/reduce_scatter | solution.py:93
  222.3 3.2 copy-start.2
  251.3 58.3 %copy-start.7 = (bf16[128,8]{0,1:T(8,128)(2,1)S(1)}, bf16[128,8]{0,1:T(8,128)(2,1)}, u32[]{:S(2)}) copy-start(bf16[128,8]{0,1:T(8,128)(2,1)} %param.10) | copy-start | bytes 6148
  251.3 58.4 %copy-start.3 = (f32[16,1,80,32]{2,3,0,1:T(8,128)S(1)}, f32[16,1,80,32]{2,3,0,1:T(8,128)}, u32[]{:S(2)}) copy-start(f32[16,1,80,32]{2,3,0,1:T(8,128)} %get-tuple-element.12) | copy-start | bytes 491524
  251.3 61.0 %copy-start.4 = (f32[16,1,80,32]{2,3,0,1:T(8,128)S(1)}, f32[16,1,80,32]{2,3,0,1:T(8,128)}, u32[]{:S(2)}) copy-start(f32[16,1,80,32]{2,3,0,1:T(8,128)} %get-tuple-element.13) | copy-start | bytes 491524
  303.5 49.1 %all-to-all-start.1 = ((bf16[16,1,80,768]{3,2,1,0:T(8,128)(2,1)}), bf16[16,1,80,768]{3,2,1,0:T(8,128)(2,1)}, u32[]{:S(2)}, u32[]{:S(2)}) async-start(bf16[16,1,80,768]{3,2,1,0:T(8,128)(2,1)} %bitcast.129), calls=%async_computation.2 | async-start | bytes 3932160 | tf_op jit(solution)/shard_map/all_to_all | solution.py:96
Sparse Core Ops, SparseCore 0:
  210.2 30.1 all-reduce.2
  251.5 51.9 reduce-scatter.1
where the time goes:
time: 381 us; the launch traced here: 379 us
  waiting for transfers between devices  231 us (61%)
  local copies, waits for them, and re-layouts  40.3 us (11%)
  matrix products  32.6 us (9%)
  other arithmetic  23 us (6%)
  starting transfers between devices  19 us (5%)
  blocking collectives  18.9 us (5%)
  between operations  14.2 us (4%)
    all_to_all x1, waiting for transfers between devices, body(): lax.all_to_all(send_grad.reshape(buffer_shape + (feat_local,)), ('ep', 's...  110 us
    reduce_scatter x1, waiting for transfers between devices, body(): lax.psum_scatter(frozen_contrib.astype(jnp.bfloat16), 'rep', scatter_dime...  41.1 us
    all_to_all x1, waiting for transfers between devices, body(): lax.all_to_all(summed, ('ep', 'sub'), split_axis=0, concat_axis=0, tiled=...  36 us
    all_to_all x1, waiting for transfers between devices, body(): lax.all_to_all(send_hidden.reshape(buffer_shape + (local_hidden_units,)),...  31.7 us
    dot_general x1, matrix products, body(): jnp.einsum('secd,efd->secf', received_gradient, down_matrix, preferred_el...  12.1 us
    psum x1, waiting for transfers between devices, body(): grad_total, hid_total = lax.psum((lowrank_grad, lowrank_hid), 'rep')  11.9 us
    all_to_all x1, blocking collectives, body(): lax.all_to_all(send_prob.reshape(buffer_shape), ('ep', 'sub'), split_axis...  11 us
    unnamed x20, local copies, waits for them, and re-layouts  8.5 us
  transfers between devices with their start and end apart: 5, of which 5 were waited for; matrix products, arithmetic and copies ran while one was open for 10% of the time, Pallas kernels for 0%

commit v1 on v0

v1 whole, which is shorter than its diff:
```python
import functools

import jax
import jax.numpy as jnp
from jax import lax
from jax.experimental import pallas as pl
from jax.experimental.pallas import tpu as pltpu
from jax.sharding import PartitionSpec as P

adapter_scale = 2.0
CHUNKS = 3
BF16 = jnp.bfloat16
F32 = jnp.float32
NT = (((1,), (1,)), ((), ()))
TN = (((0,), (0,)), ((), ()))
NN = (((1,), (0,)), ((), ()))


def dot(a, b, dims):
    return lax.dot_general(a, b, dims, preferred_element_type=F32)


def params(mib=48):
    return pltpu.CompilerParams(vmem_limit_bytes=mib * 2**20)


def expert_mask(idx_col, width, rank):
    column = lax.broadcasted_iota(jnp.int32, (idx_col.shape[0], width), 1) // rank
    return column == idx_col


def spread_pairs(dense, top):
    toks, width = dense.shape
    return jnp.broadcast_to(dense[:, None, :], (toks, top, width)).reshape(toks * top, width)


def lowrank_hid_kernel(rank, top, idx_ref, hid_ref, first_ref, out_ref):
    wide = dot(hid_ref[...], first_ref[...], NT)
    wide = jnp.where(expert_mask(idx_ref[...], wide.shape[1], rank), wide, 0.0)
    out_ref[...] = wide.reshape(wide.shape[0] // top, top, wide.shape[1]).sum(axis=1)


def lowrank_hid_call(idx_col, hid, first_all, rank, top):
    pairs, units = hid.shape
    width = first_all.shape[0]
    blk = pairs // 4
    return pl.pallas_call(
        functools.partial(lowrank_hid_kernel, rank, top),
        grid=(4,),
        in_specs=[
            pl.BlockSpec((blk, 1), lambda i: (i, 0)),
            pl.BlockSpec((blk, units), lambda i: (i, 0)),
            pl.BlockSpec((width, units), lambda i: (0, 0)),
        ],
        out_specs=pl.BlockSpec((blk // top, width), lambda i: (i, 0)),
        out_shape=jax.ShapeDtypeStruct((pairs // top, width), F32),
        compiler_params=params(),
        name="lowrank_hid",
    )(idx_col, hid, first_all)


def select_kernel(slots, pos_ref, grad_ref, second_ref, rows_ref, low_ref):
    grad = grad_ref[0]
    slot = lax.broadcasted_iota(jnp.int32, (slots, grad.shape[0]), 0)
    pick = jnp.where(slot == pos_ref[0], 1.0, 0.0).astype(BF16)
    rows_ref[0] = dot(pick, grad, NN).astype(BF16)
    low_ref[0] = dot(second_ref[...], grad, NT).astype(low_ref.dtype)


def select_call(pos, grad_all, second, slots):
    owners, toks, feats = grad_all.shape
    rank = second.shape[0]
    return pl.pallas_call(
        functools.partial(select_kernel, slots),
        grid=(owners,),
        in_specs=[
            pl.BlockSpec((1, 1, toks), lambda i: (i, 0, 0)),
            pl.BlockSpec((1, toks, feats), lambda i: (i, 0, 0)),
            pl.BlockSpec((rank, feats), lambda i: (0, 0)),
        ],
        out_specs=[
            pl.BlockSpec((1, slots, feats), lambda i: (i, 0, 0)),
            pl.BlockSpec((1, rank, toks), lambda i: (i, 0, 0)),
        ],
        out_shape=[
            jax.ShapeDtypeStruct((owners, slots, feats), BF16),
            jax.ShapeDtypeStruct((owners, rank, toks), BF16),
        ],
        compiler_params=params(),
        name="select_rows",
    )(pos, grad_all, second)


def frozen_kernel(shares, rep_ref, rows_ref, *rest):
    rows = rows_ref[...]
    for weight_ref, out_ref in zip(rest[:shares], rest[shares:]):
        out_ref[...] = dot(rows, weight_ref[...], NT).astype(BF16)


def frozen_call(rep_at, rows, down, shares, chunk, chunks):
    count, feats = rows.shape
    units = down.shape[0] // shares // chunks
    blk = 320 if count % 320 == 0 else 256

    def weight_at(offset, i, rep):
        return (lax.rem(rep[0] + offset, shares) * chunks + chunk, 0)

    offsets = [(k + 1) % shares for k in range(shares)]
    return pl.pallas_call(
        functools.partial(frozen_kernel, shares),
        grid_spec=pltpu.PrefetchScalarGridSpec(
            num_scalar_prefetch=1,
            grid=(count // blk,),
            in_specs=[pl.BlockSpec((blk, feats), lambda i, rep: (i, 0))]
            + [pl.BlockSpec((units, feats), functools.partial(weight_at, k)) for k in offsets],
            out_specs=[pl.BlockSpec((blk, units), lambda i, rep: (i, 0))] * shares,
        ),
        out_shape=[jax.ShapeDtypeStruct((count, units), BF16)] * shares,
        compiler_params=params(),
        cost_estimate=pl.CostEstimate(
            flops=2 * shares * count * units * feats,
            bytes_accessed=2 * count * feats,
            transcendentals=0,
        ),
        name="frozen_rows",
    )(rep_at, rows, *[down] * shares)


def second_grad_kernel(scaled_ref, grad_ref, out_ref):
    @pl.when(pl.program_id(0) == 0)
    def _():
        out_ref[...] = jnp.zeros_like(out_ref)

    out_ref[...] += adapter_scale * dot(scaled_ref[0], grad_ref[0], NN)


def second_grad_call(scaled, grad_all):
    owners, rank, toks = scaled.shape
    feats = grad_all.shape[2]
    return pl.pallas_call(
        second_grad_kernel,
        grid=(owners,),
        in_specs=[
            pl.BlockSpec((1, rank, toks), lambda i: (i, 0, 0)),
            pl.BlockSpec((1, toks, feats), lambda i: (i, 0, 0)),
        ],
        out_specs=pl.BlockSpec((rank, feats), lambda i: (0, 0)),
        out_shape=jax.ShapeDtypeStruct((rank, feats), F32),
        compiler_params=params(),
        name="second_grad",
    )(scaled, grad_all)


def first_grad_kernel(rank, top, idx_ref, prob_ref, low_ref, hid_ref, out_ref):
    @pl.when(pl.program_id(0) == 0)
    def _():
        out_ref[...] = jnp.zeros_like(out_ref)

    low = spread_pairs(low_ref[...], top)
    keep = expert_mask(idx_ref[...], low.shape[1], rank)
    scaled = jnp.where(keep, low * prob_ref[...], 0.0).astype(BF16)
    out_ref[...] += adapter_scale * dot(scaled, hid_ref[...], TN)


def first_grad_call(idx_col, prob_col, low, hid, rank, top):
    pairs, units = hid.shape
    width = low.shape[1]
    blk = pairs // 4
    return pl.pallas_call(
        functools.partial(first_grad_kernel, rank, top),
        grid=(4,),
        in_specs=[
            pl.BlockSpec((blk, 1), lambda i: (i, 0)),
            pl.BlockSpec((blk, 1), lambda i: (i, 0)),
            pl.BlockSpec((blk // top, width), lambda i: (i, 0)),
            pl.BlockSpec((blk, units), lambda i: (i, 0)),
        ],
        out_specs=pl.BlockSpec((width, units), lambda i: (0, 0)),
        out_shape=jax.ShapeDtypeStruct((width, units), F32),
        compiler_params=params(),
        name="first_grad",
    )(idx_col, prob_col, low, hid)


def finish_kernel(rank, top, chunks, idx_ref, target_ref, prob_ref, low_ref, hid_ref, first_ref, *rest):
    back, out_ref, sum_ref = rest[:chunks], rest[chunks], rest[chunks + 1]
    slots = back[0].shape[0]
    pairs = hid_ref.shape[0]
    low = spread_pairs(low_ref[...], top)
    keep = expert_mask(idx_ref[...], low.shape[1], rank)
    low = jnp.where(keep, adapter_scale * low.astype(BF16).astype(F32), 0.0).astype(BF16)
    slot = lax.broadcasted_iota(jnp.int32, (pairs, slots), 1)
    pick = jnp.where(slot == target_ref[...], 1.0, 0.0).astype(BF16)
    total = jnp.zeros((pairs, 1), F32)
    units = back[0].shape[1]
    for c in range(chunks):
        at = pl.ds(c * units, units)
        value = dot(pick, back[c][...], NN) + dot(low, first_ref[:, at], NN)
        value = value.astype(BF16).astype(F32)
        out_ref[:, at] = (value * prob_ref[...]).astype(BF16)
        total = total + jnp.sum(value * hid_ref[:, at].astype(F32), axis=1, keepdims=True)
    sum_ref[...] = total


def finish_call(idx_col, target, prob_col, low, hid, first_all, back, rank, top):
    pairs, units = hid.shape
    width = low.shape[1]
    slots, part = back[0].shape
    blk = pairs // 4
    return pl.pallas_call(
        functools.partial(finish_kernel, rank, top, len(back)),
        grid=(4,),
        in_specs=[
            pl.BlockSpec((blk, 1), lambda i: (i, 0)),
            pl.BlockSpec((blk, 1), lambda i: (i, 0)),
            pl.BlockSpec((blk, 1), lambda i: (i, 0)),
            pl.BlockSpec((blk // top, width), lambda i: (i, 0)),
            pl.BlockSpec((blk, units), lambda i: (i, 0)),
            pl.BlockSpec((width, units), lambda i: (0, 0)),
        ]
        + [pl.BlockSpec((slots, part), lambda i: (0, 0))] * len(back),
        out_specs=[
            pl.BlockSpec((blk, units), lambda i: (i, 0)),
            pl.BlockSpec((blk, 1), lambda i: (i, 0)),
        ],
        out_shape=[
            jax.ShapeDtypeStruct((pairs, units), BF16),
            jax.ShapeDtypeStruct((pairs, 1), F32),
        ],
        compiler_params=params(),
        name="finish",
    )(idx_col, target, prob_col, low, hid, first_all, *back)


def body(grad, hidden, index, weight, down, first, second):
    toks, top = index.shape
    exp_local, units_all, feats = down.shape
    assert exp_local == 1
    units, rank = first.shape[1:]
    where = ("ep", "sub")
    owners = lax.axis_size(where)
    cap = min(toks, 5 * toks * top // (4 * owners))
    slots = -(-cap // 16) * 16
    pairs = toks * top
    width = owners * rank
    shares = lax.axis_size("rep")

    def turn(x, offset):
        return lax.ppermute(x, "rep", [(r, (r + offset) % shares) for r in range(shares)])

    def over_rep(x):
        return x + turn(x, 1) if shares == 2 else lax.psum(x, "rep")

    def exchange(x):
        return lax.all_to_all(x, where, split_axis=0, concat_axis=0, tiled=True)

    index_rows = jnp.pad(index.T.astype(BF16), ((0, 0), (0, units - toks)))
    small = jnp.concatenate([first[0].T, index_rows], axis=0)
    small_all = lax.all_gather(small, where)
    grad_all = lax.all_gather(grad, where)

    first_all = small_all[:, :rank].reshape(width, units)
    index_all = small_all[:, rank:, :toks].astype(jnp.int32)
    me = lax.axis_index(where)
    mine = jnp.any(index_all == me, axis=1)
    before = jnp.triu(jnp.ones((toks, toks), BF16), 1)
    pos = jnp.dot(mine.astype(BF16), before, preferred_element_type=F32).astype(jnp.int32)
    pos = jnp.where(mine, pos, -1).reshape(owners, 1, toks)

    hid = hidden.reshape(pairs, units)
    idx_col = index.reshape(pairs, 1)
    prob_col = weight.reshape(pairs, 1).astype(F32)
    hits = index[:, :, None] == jnp.arange(owners, dtype=jnp.int32)
    hit = jnp.any(hits, axis=1)
    place = jnp.dot(before.T, hit.astype(BF16), preferred_element_type=F32).astype(jnp.int32)
    place = place + slots * jnp.arange(owners, dtype=jnp.int32)
    target = jnp.sum(jnp.where(hits, place[:, None, :], 0), axis=2).reshape(pairs, 1)
    prob_dense = jnp.sum(jnp.where(hits, weight[:, :, None].astype(F32), 0.0), axis=1)

    low_hid = over_rep(lowrank_hid_call(idx_col, hid, first_all, rank, top))
    scaled_hid = (low_hid * jnp.repeat(prob_dense, rank, axis=1)).astype(BF16)
    scaled_hid = exchange(scaled_hid.T.reshape(owners, rank, toks))

    rows, low_grad = select_call(pos, grad_all, second[0], slots)
    rows = rows.reshape(owners * slots, feats)
    low_grad = exchange(low_grad).reshape(width, toks).T.astype(F32)
    low_grad = over_rep(low_grad)

    rep_at = lax.axis_index("rep").astype(jnp.int32).reshape(1)
    back = []
    for c in range(CHUNKS):
        *give, keep = frozen_call(rep_at, rows, down[0], shares, c, CHUNKS)
        total = keep.astype(F32)
        for k, share in enumerate(give):
            total = total + turn(share, k + 1).astype(F32)
        total = total.astype(BF16)
        back.append(exchange(total.reshape(owners, slots, -1)).reshape(owners * slots, -1))

    second_grad = second_grad_call(scaled_hid, grad_all)
    first_part = first_grad_call(idx_col, prob_col, low_grad, hid, rank, top)
    first_grad = lax.psum_scatter(
        first_part.reshape(owners, rank, units), where, scatter_dimension=0, tiled=True
    )
    grad_hidden, sums = finish_call(
        idx_col, target, prob_col, low_grad, hid, first_all, back, rank, top
    )
    return (
        grad_hidden.reshape(toks, top, units),
        over_rep(sums.reshape(toks, top)),
        jnp.swapaxes(first_grad, 1, 2),
        second_grad[None],
    )


def solution(mesh):
    return jax.shard_map(
        body,
        mesh=mesh,
        in_specs=(
            P(("grp", "ep", "sub"), "rep"),
            P(("grp", "ep", "sub"), None, "rep"),
            P(("grp", "ep", "sub"), None),
            P(("grp", "ep", "sub"), None),
            P(("ep", "sub"), None, "rep"),
            P(("grp", "ep", "sub"), "rep", None),
            P(("grp", "ep", "sub"), None, "rep"),
        ),
        out_specs=(
            P(("grp", "ep", "sub"), None, "rep"),
            P(("grp", "ep", "sub"), None),
            P(("grp", "ep", "sub"), "rep", None),
            P(("grp", "ep", "sub"), None, "rep"),
        ),
        check_vma=False,
    )
```

time: 381 us -> 258 us (0.68)
  waiting for transfers between devices: 231 us -> 98.2 us
  Pallas kernels: 0 us -> 54.2 us
  matrix products: 32.6 us -> 0.22 us
  local copies, waits for them, and re-layouts: 40.3 us -> 18.2 us
  starting transfers between devices: 19 us -> 36.1 us
  other arithmetic: 23 us -> 9.43 us
  blocking collectives: 18.9 us -> 25 us
    all_to_all x3 -> x5, waiting for transfers between devices: 178 us -> 5.48 us  [exchange(): return lax.all_to_all(x, where, split_axis=0, concat_axis=0, tiled=True)]
    pallas_call x0 -> x8, Pallas kernels: none -> 54.2 us  [the longest x3 18.9 us: frozen_call(): pl.pallas_call(functools.partial(frozen_kernel, shares), grid_spec=pltpu....]
    all_gather x0 -> x1, waiting for transfers between devices: none -> 52.1 us  [body(): grad_all = lax.all_gather(grad, where)]
    reduce_scatter x1, waiting for transfers between devices: 41.1 us -> 0.01 us  [body(): lax.psum_scatter(first_part.reshape(owners, rank, units), where, scatter_...]
    ppermute x0 -> x6, waiting for transfers between devices: none -> 39.9 us  [turn(): lax.ppermute(x, 'rep', [(r, (r + offset) % shares) for r in range(shares)])]
    dot_general x6 -> x2, matrix products: 32.6 us -> 0.22 us  [the longest x1 0.13 us: body(): jnp.dot(mine.astype(BF16), before, preferred_element_type=F32)]
    gather x4 -> x0, local copies, waits for them, and re-layouts: 26.4 us -> none  [the longest x1 7.97 us: body(): route_weight.reshape(pair_count)[safe_pair]]
    all_gather x0 -> x1, blocking collectives: none -> 25 us  [body(): small_all = lax.all_gather(small, where)]
  transfers between devices with their start and end apart: 5 -> 13, of which waited for: 5 -> 6; matrix products, arithmetic and copies ran while one was open for 10% -> 8% of each run, Pallas kernels for 0% -> 14%
where the time goes in v1:
time: 258 us; the launch traced here: 256 us
  waiting for transfers between devices  98.2 us (38%)
  Pallas kernels  54.2 us (21%)
  starting transfers between devices  36.1 us (14%)
  blocking collectives  25 us (10%)
  local copies, waits for them, and re-layouts  18.2 us (7%)
  between operations  14.2 us (6%)
  other arithmetic  9.43 us (4%)
    all_gather x1, waiting for transfers between devices, body(): grad_all = lax.all_gather(grad, where)  52.1 us
    ppermute x6, waiting for transfers between devices, turn(): lax.ppermute(x, 'rep', [(r, (r + offset) % shares) for r in range(shares)])  39.9 us
    all_to_all x5, starting transfers between devices, exchange(): return lax.all_to_all(x, where, split_axis=0, concat_axis=0, tiled=True)  27.9 us
    all_gather x1, blocking collectives, body(): small_all = lax.all_gather(small, where)  25 us
    pallas_call x3, Pallas kernels, frozen_call(): pl.pallas_call(functools.partial(frozen_kernel, shares), grid_spec=pltpu....  18.9 us
    pallas_call x1, Pallas kernels, select_call(): pl.pallas_call(functools.partial(select_kernel, slots), grid=(owners,), i...  12.9 us
    pallas_call x1, Pallas kernels, second_grad_call(): pl.pallas_call(second_grad_kernel, grid=(owners,), in_specs=[pl.BlockSpec...  11.2 us
    unnamed x34, local copies, waits for them, and re-layouts  8.92 us
  transfers between devices with their start and end apart: 13, of which 6 were waited for; matrix products, arithmetic and copies ran while one was open for 8% of the time, Pallas kernels for 14%

profile of v1, /device:TPU:8, one launch (start us, length us, event | category | flops | bytes accessed | tf_op | source)
XLA Modules:
  0.0 255.6 jit_solution(15217637159457637853)
XLA Ops:
  7.2 0.0 all-gather.4.cloned.1.call-start
  7.2 0.7 all-gather.4.cloned.1.call-update
  7.9 0.7 convert_bitcast_fusion
  8.6 0.8 fusion.7
  9.4 25.0 %all-gather = bf16[640,768]{1,0:T(8,128)(2,1)S(1)} all-gather(bf16[40,768]{1,0:T(8,128)(2,1)S(1)} %fusion.7), channel_id=2, replica_groups=mesh['grp'=1,'ep'=8,'rep'=2,'sub'=2] {'ep','sub'}, dimensions={0}, use_global_device_ids=true | all-gather | bytes 1044480 | tf_op jit(solution)/shard_map/all_gather | solution.py:259
  34.4 0.9 copy-done.13
  35.4 0.1 fusion
  35.5 52.1 %all-gather.4.cloned.1.call-done = bf16[2048,2048]{1,0:T(8,128)(2,1)} async-done(((bf16[128,2048]{1,0:T(8,128)(2,1)}), bf16[2048,2048]{1,0:T(8,128)(2,1)}) %all-gather.4.cloned.1.call-update) | async-done | bytes 8388624 | tf_op jit(solution)/shard_map/all_gather | solution.py:260
  87.6 12.9 %select_rows.1 = (bf16[16,80,2048]{2,1,0:T(8,128)(2,1)S(1)}, bf16[16,32,128]{2,1,0:T(8,128)(2,1)}) custom-call(s32[16,1,128]{2,1,0:T(1,128)S(1)} %bitcast.47, bf16[16,128,2048]{2,1,0:T(8,128)(2,1)} %bitcast.54, bf16[32,2048]{1,0:T(8,128)(2,1)S(1)} %bitcast.46), custom_call_target="tpu_custom_call" | custom-call | tf_op jit(solution)/shard_map/select_rows/pallas_call | solution.py:73
  100.6 2.4 copy-done
  103.0 6.0 %frozen_rows.5 = (bf16[1280,256]{1,0:T(8,128)(2,1)S(1)}, bf16[1280,256]{1,0:T(8,128)(2,1)S(1)}) custom-call(s32[1]{0:T(128)} %bitcast.11.rep_ref, bf16[1280,2048]{1,0:T(8,128)(2,1)} %bitcast.35, bf16[1536,2048]{1,0:T(8,128)(2,1)} %bitcast.48, bf16[1536,2048]{1,0:T(8,128)(2,1)} %bitcast.49), custom_call_target="tpu_custom_call" | custom-call | flops 2684354560 | bytes 5242880 | tf_op jit(solution)/shard_map/frozen_rows/pallas_call | solution.py:109
  109.0 1.5 collective-permute-start.3
  110.6 4.5 %all-to-all-start = ((bf16[16,32,128]{2,1,0:T(8,128)(2,1)}), bf16[16,32,128]{2,1,0:T(8,128)(2,1)S(1)}, u32[]{:S(2)}, u32[]{:S(2)}) async-start(bf16[16,32,128]{2,1,0:T(8,128)(2,1)} %get-tuple-element.14), calls=%async_computation | async-start | bytes 262144 | tf_op jit(solution)/shard_map/all_to_all | solution.py:255
  115.0 11.0 %collective-permute-done.3 = bf16[1280,256]{1,0:T(8,128)(2,1)S(1)} collective-permute-done((bf16[1280,256]{1,0:T(8,128)(2,1)S(1)}, bf16[1280,256]{1,0:T(8,128)(2,1)S(1)}, u32[]{:S(2)}, u32[]{:S(2)}) %collective-permute-start.3) | collective-permute-done | bytes 655392 | tf_op jit(solution)/shard_map/ppermute | solution.py:249
  126.0 1.0 add_convert_fusion
  127.0 4.5 %all-to-all-start.3 = ((bf16[16,80,256]{2,1,0:T(8,128)(2,1)}), bf16[16,80,256]{2,1,0:T(8,128)(2,1)S(1)}, u32[]{:S(2)}, u32[]{:S(2)}) async-start(bf16[16,80,256]{2,1,0:T(8,128)(2,1)} %bitcast.18), calls=%async_computation.3 | async-start | bytes 1310720 | tf_op jit(solution)/shard_map/all_to_all | solution.py:255
  131.5 6.1 %frozen_rows.4 = (bf16[1280,256]{1,0:T(8,128)(2,1)S(1)}, bf16[1280,256]{1,0:T(8,128)(2,1)S(1)}) custom-call(s32[1]{0:T(128)} %bitcast.11.rep_ref, bf16[1280,2048]{1,0:T(8,128)(2,1)} %bitcast.36, bf16[1536,2048]{1,0:T(8,128)(2,1)} %bitcast.50, bf16[1536,2048]{1,0:T(8,128)(2,1)} %bitcast.51), custom_call_target="tpu_custom_call" | custom-call | flops 2684354560 | bytes 5242880 | tf_op jit(solution)/shard_map/frozen_rows/pallas_call | solution.py:109
  137.6 1.5 collective-permute-start.2
  139.2 0.1 copy.38
  139.3 0.6 collective-permute-start
  139.9 15.3 %collective-permute-done.2 = bf16[1280,256]{1,0:T(8,128)(2,1)S(1)} collective-permute-done((bf16[1280,256]{1,0:T(8,128)(2,1)S(1)}, bf16[1280,256]{1,0:T(8,128)(2,1)S(1)}, u32[]{:S(2)}, u32[]{:S(2)}) %collective-permute-start.2) | collective-permute-done | bytes 655392 | tf_op jit(solution)/shard_map/ppermute | solution.py:249
  155.2 1.0 add_convert_fusion.1
  156.3 6.1 %all-to-all-start.2 = ((bf16[16,80,256]{2,1,0:T(8,128)(2,1)}), bf16[16,80,256]{2,1,0:T(8,128)(2,1)S(1)}, u32[]{:S(2)}, u32[]{:S(2)}) async-start(bf16[16,80,256]{2,1,0:T(8,128)(2,1)} %bitcast.16), calls=%async_computation.2 | async-start | bytes 1310720 | tf_op jit(solution)/shard_map/all_to_all | solution.py:255
  162.4 0.0 copy-start.15
  162.4 0.0 reduce-scatter.2.cloned.1.call-start
  162.4 6.8 %frozen_rows.3 = (bf16[1280,256]{1,0:T(8,128)(2,1)}, bf16[1280,256]{1,0:T(8,128)(2,1)S(1)}) custom-call(s32[1]{0:T(128)} %bitcast.11.rep_ref, bf16[1280,2048]{1,0:T(8,128)(2,1)} %bitcast.37, bf16[1536,2048]{1,0:T(8,128)(2,1)} %bitcast.52, bf16[1536,2048]{1,0:T(8,128)(2,1)} %bitcast.53), custom_call_target="tpu_custom_call" | custom-call | flops 2684354560 | bytes 5242880 | tf_op jit(solution)/shard_map/frozen_rows/pallas_call | solution.py:109
  169.2 0.8 copy-done.10
  170.1 1.5 collective-permute-start.1
  171.5 0.1 copy.35
  171.6 0.7 copy.37
  172.4 0.2 reshape.111.idx_ref
  172.6 1.0 reshape.112.prob_ref
  173.6 1.0 bitcast_add_fusion.low_ref
  174.6 0.0 copy-start.7
  174.6 2.3 first_grad.1
  176.9 1.2 copy-done.2
  178.1 0.0 reduce-scatter.2.cloned.1.call-update
  178.1 9.0 %collective-permute-done.1 = bf16[1280,256]{1,0:T(8,128)(2,1)} collective-permute-done((bf16[1280,256]{1,0:T(8,128)(2,1)}, bf16[1280,256]{1,0:T(8,128)(2,1)}, u32[]{:S(2)}, u32[]{:S(2)}) %collective-permute-start.1) | collective-permute-done | bytes 655392 | tf_op jit(solution)/shard_map/ppermute | solution.py:249
  187.2 2.3 add_convert_fusion.2
  189.5 0.8 copy-done.5
  190.3 6.0 %all-to-all-start.1 = ((bf16[16,80,256]{2,1,0:T(8,128)(2,1)}), bf16[16,80,256]{2,1,0:T(8,128)(2,1)}, u32[]{:S(2)}, u32[]{:S(2)}) async-start(bf16[16,80,256]{2,1,0:T(8,128)(2,1)} %bitcast.58), calls=%async_computation.1 | async-start | bytes 1310720 | tf_op jit(solution)/shard_map/all_to_all | solution.py:255
  196.4 1.2 slice.9
  197.6 2.7 %lowrank_hid.1 = f32[128,512]{1,0:T(8,128)} custom-call(s32[1024,1]{1,0:T(8,128)S(1)} %reshape.111.idx_ref, bf16[1024,768]{1,0:T(8,128)(2,1)S(1)} %bitcast.40, bf16[512,768]{1,0:T(8,128)(2,1)S(1)} %bitcast.41), custom_call_target="tpu_custom_call" | custom-call | tf_op jit(solution)/shard_map/lowrank_hid/pallas_call | solution.py:47
  200.3 1.5 collective-permute-start.5
  201.8 0.7 broadcast_in_dim.53
  202.5 1.9 copy.45
  204.4 4.5 %collective-permute-done.5 = f32[128,512]{1,0:T(8,128)} collective-permute-done((f32[128,512]{1,0:T(8,128)}, f32[128,512]{1,0:T(8,128)}, u32[]{:S(2)}, u32[]{:S(2)}) %collective-permute-start.5) | collective-permute-done | bytes 262176 | tf_op jit(solution)/shard_map/ppermute | solution.py:249
  209.0 1.2 fusion.2
  210.1 0.7 copy.46
  210.9 5.5 %all-to-all-done.1 = bf16[16,80,256]{2,1,0:T(8,128)(2,1)} async-done(((bf16[16,80,256]{2,1,0:T(8,128)(2,1)}), bf16[16,80,256]{2,1,0:T(8,128)(2,1)}, u32[]{:S(2)}, u32[]{:S(2)}) %all-to-all-start.1) | async-done | bytes 655392 | tf_op jit(solution)/shard_map/all_to_all | solution.py:255
  216.4 6.8 %all-to-all-start.4 = ((bf16[16,32,128]{2,1,0:T(8,128)(2,1)}), bf16[16,32,128]{2,1,0:T(8,128)(2,1)S(1)}, u32[]{:S(2)}, u32[]{:S(2)}) async-start(bf16[16,32,128]{2,1,0:T(8,128)(2,1)} %bitcast.61), calls=%async_computation.5 | async-start | bytes 262144 | tf_op jit(solution)/shard_map/all_to_all | solution.py:255
  223.2 0.1 fusion.1
  223.2 0.1 select_reduce_fusion.1
  223.3 0.7 copy.36
  224.0 1.8 reshape.110.target_ref
  225.9 0.0 copy-start.9
  225.9 1.1 copy-done.9
  226.9 6.2 %finish.1 = (bf16[1024,768]{1,0:T(8,128)(2,1)}, f32[1024,1]{1,0:T(8,128)S(1)}) custom-call(s32[1024,1]{1,0:T(8,128)S(1)} %reshape.111.idx_ref, s32[1024,1]{1,0:T(8,128)S(1)} %copy-done.9, f32[1024,1]{1,0:T(8,128)S(1)} %reshape.112.prob_ref, f32[128,512]{1,0:T(8,128)S(1)} %copy-done.8, bf16[1024,768]{1,0:T(8,128)(2,1)} %bitcast.38, ...), custom_call_target="tpu_custom_call" | custom-call | tf_op jit(solution)/shard_map/finish/pallas_call | solution.py:210
  233.1 0.8 copy-done.11
  233.9 1.2 reduce
  235.2 0.1 reshape.102
  235.3 1.5 collective-permute-start.4
  236.8 11.2 %second_grad.1 = f32[32,2048]{1,0:T(8,128)} custom-call(bf16[16,32,128]{2,1,0:T(8,128)(2,1)S(1)} %all-to-all-done.4.scaled_ref, bf16[16,128,2048]{2,1,0:T(8,128)(2,1)} %bitcast.55), custom_call_target="tpu_custom_call" | custom-call | tf_op jit(solution)/shard_map/second_grad/pallas_call | solution.py:140
  248.0 0.7 copy.47
  (36 shorter events, 0.2 us)
Async XLA Ops:
  7.2 80.5 %copy-start.12 = (bf16[1,32,2048]{2,1,0:T(8,128)(2,1)S(1)}, bf16[1,32,2048]{2,1,0:T(8,128)(2,1)}, u32[]{:S(2)}) copy-start(bf16[1,32,2048]{2,1,0:T(8,128)(2,1)} %param.13) | copy-start | bytes 393220
  7.2 80.5 %all-gather.4.cloned.1.call-start = ((), (), s32[]{:S(2)}) async-start(), calls=%async_computation.7 | async-start | bytes 8912896 | tf_op jit(solution)/shard_map/all_gather | solution.py:260
  34.4 0.9 copy-start.13
  100.6 2.4 copy-start
  109.0 17.0 %collective-permute-start.3 = (bf16[1280,256]{1,0:T(8,128)(2,1)S(1)}, bf16[1280,256]{1,0:T(8,128)(2,1)S(1)}, u32[]{:S(2)}, u32[]{:S(2)}) collective-permute-start(bf16[1280,256]{1,0:T(8,128)(2,1)S(1)} %get-tuple-element.21), channel_id=1, source_target_pairs={{0,2},{2,0},{1,3},{3,1},{4,6},{6,4},{5,7},{7,5},{8,10},{10,8},{9,1... | collective-permute-start | bytes 1966088 | tf_op jit(solution)/shard_map/ppermute | solution.py:249
  110.6 16.4 %all-to-all-start = ((bf16[16,32,128]{2,1,0:T(8,128)(2,1)}), bf16[16,32,128]{2,1,0:T(8,128)(2,1)S(1)}, u32[]{:S(2)}, u32[]{:S(2)}) async-start(bf16[16,32,128]{2,1,0:T(8,128)(2,1)} %get-tuple-element.14), calls=%async_computation | async-start | bytes 262144 | tf_op jit(solution)/shard_map/all_to_all | solution.py:255
  127.0 29.3 %all-to-all-start.3 = ((bf16[16,80,256]{2,1,0:T(8,128)(2,1)}), bf16[16,80,256]{2,1,0:T(8,128)(2,1)S(1)}, u32[]{:S(2)}, u32[]{:S(2)}) async-start(bf16[16,80,256]{2,1,0:T(8,128)(2,1)} %bitcast.18), calls=%async_computation.3 | async-start | bytes 1310720 | tf_op jit(solution)/shard_map/all_to_all | solution.py:255
  137.6 17.6 %collective-permute-start.2 = (bf16[1280,256]{1,0:T(8,128)(2,1)S(1)}, bf16[1280,256]{1,0:T(8,128)(2,1)S(1)}, u32[]{:S(2)}, u32[]{:S(2)}) collective-permute-start(bf16[1280,256]{1,0:T(8,128)(2,1)S(1)} %get-tuple-element.19), channel_id=1, source_target_pairs={{0,2},{2,0},{1,3},{3,1},{4,6},{6,4},{5,7},{7,5},{8,10},{10,8},{9,1... | collective-permute-start | bytes 1966088 | tf_op jit(solution)/shard_map/ppermute | solution.py:249
  139.3 34.3 %collective-permute-start = (f32[128,512]{1,0:T(8,128)S(1)}, f32[128,512]{1,0:T(8,128)}, u32[]{:S(2)}, u32[]{:S(2)}) collective-permute-start(f32[128,512]{1,0:T(8,128)S(1)} %bitcast.59), channel_id=1, source_target_pairs={{0,2},{2,0},{1,3},{3,1},{4,6},{6,4},{5,7},{7,5},{8,10},{10,8},{9,1... | collective-permute-start | bytes 786440 | tf_op jit(solution)/shard_map/ppermute | solution.py:249
  156.3 6.2 %copy-start.3 = (bf16[16,80,256]{2,1,0:T(8,128)(2,1)}, bf16[16,80,256]{2,1,0:T(8,128)(2,1)S(1)}, u32[]{:S(2)}) copy-start(bf16[16,80,256]{2,1,0:T(8,128)(2,1)S(1)} %all-to-all-done.3) | copy-start | bytes 1966084
  156.3 33.2 %all-to-all-start.2 = ((bf16[16,80,256]{2,1,0:T(8,128)(2,1)}), bf16[16,80,256]{2,1,0:T(8,128)(2,1)S(1)}, u32[]{:S(2)}, u32[]{:S(2)}) async-start(bf16[16,80,256]{2,1,0:T(8,128)(2,1)} %bitcast.16), calls=%async_computation.2 | async-start | bytes 1310720 | tf_op jit(solution)/shard_map/all_to_all | solution.py:255
  162.4 9.2 %copy-start.14 = (s32[128,8]{0,1:T(8,128)S(1)}, s32[128,8]{0,1:T(8,128)}, u32[]{:S(2)}) copy-start(s32[128,8]{0,1:T(8,128)} %param.9) | copy-start | bytes 12292
  162.4 9.3 %copy-start.15 = (bf16[128,8]{0,1:T(8,128)(2,1)S(1)}, bf16[128,8]{0,1:T(8,128)(2,1)}, u32[]{:S(2)}) copy-start(bf16[128,8]{0,1:T(8,128)(2,1)} %param.10) | copy-start | bytes 6148
  162.4 86.3 %reduce-scatter.2.cloned.1.call-start = ((), (), s32[]{:S(2)}) async-start(), calls=%async_computation.6 | async-start | bytes 1671168 | tf_op jit(solution)/shard_map/reduce_scatter | solution.py:301
  169.2 0.8 copy-start.10
  170.1 4.5 %copy-start.1 = (bf16[128,8,768]{2,1,0:T(8,128)(2,1)S(1)}, bf16[128,8,768]{2,1,0:T(8,128)(2,1)}, u32[]{:S(2)}) copy-start(bf16[128,8,768]{2,1,0:T(8,128)(2,1)} %param.8) | copy-start | bytes 4718596
  170.1 17.1 %collective-permute-start.1 = (bf16[1280,256]{1,0:T(8,128)(2,1)}, bf16[1280,256]{1,0:T(8,128)(2,1)}, u32[]{:S(2)}, u32[]{:S(2)}) collective-permute-start(bf16[1280,256]{1,0:T(8,128)(2,1)} %get-tuple-element.17), channel_id=1, source_target_pairs={{0,2},{2,0},{1,3},{3,1},{4,6},{6,4},{5,7},{7,5},{8,10},{10,8},{9,1... | collective-permute-start | bytes 1966088 | tf_op jit(solution)/shard_map/ppermute | solution.py:249
  174.6 2.3 copy-start.7
  176.9 1.2 copy-start.2
  189.5 0.8 copy-start.5
  190.3 26.0 %all-to-all-start.1 = ((bf16[16,80,256]{2,1,0:T(8,128)(2,1)}), bf16[16,80,256]{2,1,0:T(8,128)(2,1)}, u32[]{:S(2)}, u32[]{:S(2)}) async-start(bf16[16,80,256]{2,1,0:T(8,128)(2,1)} %bitcast.58), calls=%async_computation.1 | async-start | bytes 1310720 | tf_op jit(solution)/shard_map/all_to_all | solution.py:255
  200.3 8.7 %collective-permute-start.5 = (f32[128,512]{1,0:T(8,128)}, f32[128,512]{1,0:T(8,128)}, u32[]{:S(2)}, u32[]{:S(2)}) collective-permute-start(f32[128,512]{1,0:T(8,128)} %lowrank_hid.1), channel_id=1, source_target_pairs={{0,2},{2,0},{1,3},{3,1},{4,6},{6,4},{5,7},{7,5},{8,10},{10,8},{9,1... | collective-permute-start | bytes 786440 | tf_op jit(solution)/shard_map/ppermute | solution.py:249
  202.5 23.4 %copy-start.4 = (bf16[16,80,256]{2,1,0:T(8,128)(2,1)S(1)}, bf16[16,80,256]{2,1,0:T(8,128)(2,1)}, u32[]{:S(2)}) copy-start(bf16[16,80,256]{2,1,0:T(8,128)(2,1)} %copy-done.3) | copy-start | bytes 1966084
  202.5 23.4 %copy-start.6 = (bf16[16,80,256]{2,1,0:T(8,128)(2,1)S(1)}, bf16[16,80,256]{2,1,0:T(8,128)(2,1)}, u32[]{:S(2)}) copy-start(bf16[16,80,256]{2,1,0:T(8,128)(2,1)} %copy-done.5) | copy-start | bytes 1966084
  202.5 23.4 %copy-start.8 = (f32[128,512]{1,0:T(8,128)S(1)}, f32[128,512]{1,0:T(8,128)}, u32[]{:S(2)}) copy-start(f32[128,512]{1,0:T(8,128)} %copy-done.7) | copy-start | bytes 786436
  216.4 20.4 %all-to-all-start.4 = ((bf16[16,32,128]{2,1,0:T(8,128)(2,1)}), bf16[16,32,128]{2,1,0:T(8,128)(2,1)S(1)}, u32[]{:S(2)}, u32[]{:S(2)}) async-start(bf16[16,32,128]{2,1,0:T(8,128)(2,1)} %bitcast.61), calls=%async_computation.5 | async-start | bytes 262144 | tf_op jit(solution)/shard_map/all_to_all | solution.py:255
  225.9 1.1 copy-start.9
  233.1 0.8 copy-start.11
  235.3 12.8 %collective-permute-start.4 = (f32[128,8]{1,0:T(8,128)S(1)}, f32[128,8]{1,0:T(8,128)S(1)}, u32[]{:S(2)}, u32[]{:S(2)}) collective-permute-start(f32[128,8]{1,0:T(8,128)S(1)} %reshape.102), channel_id=1, source_target_pairs={{0,2},{2,0},{1,3},{3,1},{4,6},{6,4},{5,7},{7,5},{8,10},{10,8},{9,1... | collective-permute-start | bytes 12296 | tf_op jit(solution)/shard_map/ppermute | solution.py:249
Sparse Core Ops, SparseCore 0:
  10.2 77.4 all-gather.3
  178.2 60.4 reduce-scatter.1

commit v2 on v1

v2 whole, which is shorter than its diff:
```python
import functools

import jax
import jax.numpy as jnp
from jax import lax
from jax.experimental import pallas as pl
from jax.experimental.pallas import tpu as pltpu
from jax.sharding import PartitionSpec as P

adapter_scale = 2.0
BF16 = jnp.bfloat16
F32 = jnp.float32
NT = (((1,), (1,)), ((), ()))
TN = (((0,), (0,)), ((), ()))
NN = (((1,), (0,)), ((), ()))


def dot(a, b, dims):
    return lax.dot_general(a, b, dims, preferred_element_type=F32)


def params(mib=48):
    return pltpu.CompilerParams(vmem_limit_bytes=mib * 2**20)


def whole(shape):
    return pl.BlockSpec(shape, lambda *_: (0,) * len(shape))


def expert_mask(idx_col, width, rank):
    column = lax.broadcasted_iota(jnp.int32, (idx_col.shape[0], width), 1) // rank
    return column == idx_col


def spread_pairs(dense, top):
    toks, width = dense.shape
    return jnp.broadcast_to(dense[:, None, :], (toks, top, width)).reshape(toks * top, width)


def lowrank_hid_kernel(rank, top, idx_ref, hid_ref, first_ref, out_ref):
    wide = dot(hid_ref[...], first_ref[...], NT)
    wide = jnp.where(expert_mask(idx_ref[...], wide.shape[1], rank), wide, 0.0)
    out_ref[...] = wide.reshape(wide.shape[0] // top, top, wide.shape[1]).sum(axis=1)


def lowrank_hid_call(idx_col, hid, first_all, rank, top):
    pairs, units = hid.shape
    width = first_all.shape[0]
    blk = pairs // 4
    return pl.pallas_call(
        functools.partial(lowrank_hid_kernel, rank, top),
        grid=(4,),
        in_specs=[
            pl.BlockSpec((blk, 1), lambda i: (i, 0)),
            pl.BlockSpec((blk, units), lambda i: (i, 0)),
            whole((width, units)),
        ],
        out_specs=pl.BlockSpec((blk // top, width), lambda i: (i, 0)),
        out_shape=jax.ShapeDtypeStruct((pairs // top, width), F32),
        compiler_params=params(),
        cost_estimate=pl.CostEstimate(
            flops=4 * pairs * width * units, bytes_accessed=2 * pairs * units, transcendentals=0
        ),
        name="lowrank_hid",
    )(idx_col, hid, first_all)


def expert_rows_kernel(slots, tiles, shares, batch, rep_ref, *rest):
    pos_ref, grads = rest[0], rest[1 : 1 + batch]
    second_ref, weight_ref = rest[1 + batch], rest[2 + batch]
    outs, low_ref, rows_ref = rest[3 + batch : -2], rest[-2], rest[-1]
    step = pl.program_id(0)

    @pl.when(step == 0)
    def _():
        for k, grad_ref in enumerate(grads):
            grad = grad_ref[...]
            slot = lax.broadcasted_iota(jnp.int32, (slots, grad.shape[0]), 0)
            pick = jnp.where(slot == pos_ref[k], 1.0, 0.0).astype(BF16)
            rows_ref[pl.ds(k * slots, slots), :] = dot(pick, grad, NN).astype(BF16)
            low_ref[k] = dot(second_ref[...], grad, NT).astype(BF16)

    value = dot(rows_ref[...], weight_ref[...], NT).astype(BF16)
    for k, out_ref in enumerate(outs):

        @pl.when(step // tiles == k)
        def _():
            out_ref[...] = value


def expert_rows_call(rep_at, pos, grads, second, down, shares, slots):
    batch, (toks, feats) = len(grads), grads[0].shape
    rank = second.shape[0]
    units = down.shape[0] // shares
    tiles = 3
    tile = units // tiles
    rows = batch * slots

    def weight_at(i, rep):
        return (lax.rem(rep[0] + i // tiles + 1, shares) * tiles + lax.rem(i, tiles), 0)

    def out_at(k, i, rep):
        return (0, jnp.clip(i - k * tiles, 0, tiles - 1))

    return pl.pallas_call(
        functools.partial(expert_rows_kernel, slots, tiles, shares, batch),
        grid_spec=pltpu.PrefetchScalarGridSpec(
            num_scalar_prefetch=1,
            grid=(shares * tiles,),
            in_specs=[whole((batch, 1, toks))]
            + [whole((toks, feats))] * batch
            + [whole((rank, feats)), pl.BlockSpec((tile, feats), weight_at)],
            out_specs=[
                pl.BlockSpec((rows, tile), functools.partial(out_at, k)) for k in range(shares)
            ]
            + [whole((batch, rank, toks))],
            scratch_shapes=[pltpu.VMEM((rows, feats), BF16)],
        ),
        out_shape=[jax.ShapeDtypeStruct((rows, units), BF16)] * shares
        + [jax.ShapeDtypeStruct((batch, rank, toks), BF16)],
        compiler_params=params(),
        cost_estimate=pl.CostEstimate(
            flops=2 * rows * down.shape[0] * feats,
            bytes_accessed=2 * down.shape[0] * feats,
            transcendentals=0,
        ),
        name="expert_rows",
    )(rep_at, pos, *grads, second, down)


def share_sum_kernel(parts, *refs):
    outs = refs[parts:]
    slots = outs[0].shape[0]
    for k, out_ref in enumerate(outs):
        at = pl.ds(k * slots, slots)
        total = refs[0][at, :].astype(F32)
        for part in refs[1:parts]:
            total = total + part[at, :].astype(F32)
        out_ref[...] = total.astype(BF16)


def share_sum_call(parts, batch):
    rows, units = parts[0].shape
    return pl.pallas_call(
        functools.partial(share_sum_kernel, len(parts)),
        out_shape=[jax.ShapeDtypeStruct((rows // batch, units), BF16)] * batch,
        compiler_params=params(),
        name="share_sum",
    )(*parts)


def place_kernel(me_ref, *refs):
    out_ref, at = refs[-1], 0
    for ref in refs[:-1]:
        for k in range(ref.shape[0]):
            out_ref[lax.bitwise_xor(me_ref[0], at)] = ref[k]
            at += 1


def place_call(me_at, blocks):
    count = sum(b.shape[0] for b in blocks)
    shape = (count,) + blocks[0].shape[1:]
    return pl.pallas_call(
        place_kernel,
        grid_spec=pltpu.PrefetchScalarGridSpec(
            num_scalar_prefetch=1,
            grid=(1,),
            in_specs=[whole(b.shape) for b in blocks],
            out_specs=whole(shape),
        ),
        out_shape=jax.ShapeDtypeStruct(shape, blocks[0].dtype),
        compiler_params=params(),
        name="place_blocks",
    )(me_at, *blocks)


def second_grad_kernel(me_ref, scaled_ref, *refs):
    out_ref = refs[-1]
    total = jnp.zeros(out_ref.shape, F32)
    for r, grad_ref in enumerate(refs[:-1]):
        total = total + dot(scaled_ref[lax.bitwise_xor(me_ref[0], r)], grad_ref[...], NN)
    out_ref[...] = adapter_scale * total


def second_grad_call(me_at, scaled, grads):
    owners, rank, toks = scaled.shape
    feats = grads[0].shape[1]
    steps = 4
    tile = feats // steps
    return pl.pallas_call(
        second_grad_kernel,
        grid_spec=pltpu.PrefetchScalarGridSpec(
            num_scalar_prefetch=1,
            grid=(steps,),
            in_specs=[whole((owners, rank, toks))]
            + [pl.BlockSpec((toks, tile), lambda i, me: (0, i))] * owners,
            out_specs=pl.BlockSpec((rank, tile), lambda i, me: (0, i)),
        ),
        out_shape=jax.ShapeDtypeStruct((rank, feats), F32),
        compiler_params=params(),
        cost_estimate=pl.CostEstimate(
            flops=2 * rank * feats * toks * owners,
            bytes_accessed=2 * owners * toks * feats,
            transcendentals=0,
        ),
        name="second_grad",
    )(me_at, scaled, *grads)


def first_grad_kernel(rank, top, steps, cores, sub_ref, idx_ref, prob_ref, low_ref, hid_ref, *rest):
    outs, sum_ref = rest[:cores], rest[cores]
    step = pl.program_id(0)
    low = spread_pairs(low_ref[...], top)
    keep = expert_mask(idx_ref[...], low.shape[1], rank)
    scaled = jnp.where(keep, low * prob_ref[...], 0.0).astype(BF16)
    part = adapter_scale * dot(scaled, hid_ref[...], TN)
    part = part.reshape(sum_ref.shape)

    @pl.when(step == 0)
    def _():
        sum_ref[...] = part

    @pl.when(step > 0)
    def _():
        sum_ref[...] += part

    @pl.when(step == steps - 1)
    def _():
        for k, out_ref in enumerate(outs):
            out_ref[...] = sum_ref[:, lax.rem(sub_ref[0] + k, cores)].astype(out_ref.dtype)


def first_grad_call(sub_at, idx_col, prob_col, low, hid, rank, top, cores):
    pairs, units = hid.shape
    width = low.shape[1]
    steps = 4
    blk = pairs // steps
    shape = (width // rank // cores, rank, units)
    return pl.pallas_call(
        functools.partial(first_grad_kernel, rank, top, steps, cores),
        grid_spec=pltpu.PrefetchScalarGridSpec(
            num_scalar_prefetch=1,
            grid=(steps,),
            in_specs=[
                pl.BlockSpec((blk, 1), lambda i, s: (i, 0)),
                pl.BlockSpec((blk, 1), lambda i, s: (i, 0)),
                pl.BlockSpec((blk // top, width), lambda i, s: (i, 0)),
                pl.BlockSpec((blk, units), lambda i, s: (i, 0)),
            ],
            out_specs=[whole(shape)] * cores,
            scratch_shapes=[pltpu.VMEM((shape[0], cores) + shape[1:], F32)],
        ),
        out_shape=[jax.ShapeDtypeStruct(shape, F32)]
        + [jax.ShapeDtypeStruct(shape, BF16)] * (cores - 1),
        compiler_params=params(),
        name="first_grad",
    )(sub_at, idx_col, prob_col, low, hid)


def finish_kernel(rank, top, count, idx_ref, target_ref, prob_ref, low_ref, hid_ref, first_ref, *rest):
    back, out_ref, sum_ref, all_ref = rest[:count], rest[count], rest[count + 1], rest[count + 2]
    slots = back[0].shape[0]
    pairs = hid_ref.shape[0]

    @pl.when(pl.program_id(0) == 0)
    def _():
        for r, ref in enumerate(back):
            all_ref[pl.ds(r * slots, slots), :] = ref[...]

    low = spread_pairs(low_ref[...], top)
    keep = expert_mask(idx_ref[...], low.shape[1], rank)
    low = jnp.where(keep, adapter_scale * low.astype(BF16).astype(F32), 0.0).astype(BF16)
    slot = lax.broadcasted_iota(jnp.int32, (pairs, count * slots), 1)
    pick = jnp.where(slot == target_ref[...], 1.0, 0.0).astype(BF16)
    value = dot(pick, all_ref[...], NN) + dot(low, first_ref[...], NN)
    value = value.astype(BF16).astype(F32)
    out_ref[...] = (value * prob_ref[...]).astype(BF16)
    sum_ref[...] = jnp.sum(value * hid_ref[...].astype(F32), axis=1, keepdims=True)


def finish_call(idx_col, target, prob_col, low, hid, first_all, back, rank, top):
    pairs, units = hid.shape
    width = low.shape[1]
    slots, part = back[0].shape
    blk = pairs // 4
    return pl.pallas_call(
        functools.partial(finish_kernel, rank, top, len(back)),
        grid=(4,),
        in_specs=[
            pl.BlockSpec((blk, 1), lambda i: (i, 0)),
            pl.BlockSpec((blk, 1), lambda i: (i, 0)),
            pl.BlockSpec((blk, 1), lambda i: (i, 0)),
            pl.BlockSpec((blk // top, width), lambda i: (i, 0)),
            pl.BlockSpec((blk, units), lambda i: (i, 0)),
            whole((width, units)),
        ]
        + [whole((slots, part))] * len(back),
        out_specs=[
            pl.BlockSpec((blk, units), lambda i: (i, 0)),
            pl.BlockSpec((blk, 1), lambda i: (i, 0)),
        ],
        out_shape=[
            jax.ShapeDtypeStruct((pairs, units), BF16),
            jax.ShapeDtypeStruct((pairs, 1), F32),
        ],
        scratch_shapes=[pltpu.VMEM((len(back) * slots, units), BF16)],
        compiler_params=params(),
        name="finish",
    )(idx_col, target, prob_col, low, hid, first_all, *back)


def body(grad, hidden, index, weight, down, first, second):
    toks, top = index.shape
    exp_local, units_all, feats = down.shape
    assert exp_local == 1
    units, rank = first.shape[1:]
    where = ("ep", "sub")
    groups, cores, shares = lax.axis_size("ep"), lax.axis_size("sub"), lax.axis_size("rep")
    owners = groups * cores
    assert cores == 2 and groups & (groups - 1) == 0
    cap = min(toks, 5 * toks * top // (4 * owners))
    slots = -(-cap // 16) * 16
    pairs = toks * top
    width = owners * rank
    me = lax.axis_index(where).astype(jnp.int32)
    me_at = me.reshape(1)
    rep_at = lax.axis_index("rep").astype(jnp.int32).reshape(1)
    sub_at = lax.axis_index("sub").astype(jnp.int32).reshape(1)

    def turn(x, offset):
        return lax.ppermute(x, "rep", [(r, (r + offset) % shares) for r in range(shares)])

    def over_rep(x):
        return x + turn(x, 1) if shares == 2 else lax.psum(x, "rep")

    def flip(x, mask, axis="ep"):
        size = groups if axis == "ep" else cores if axis == "sub" else owners
        return lax.ppermute(x, axis, [(i, i ^ mask) for i in range(size)])

    def gather_relative(x):
        known, mask = [0], groups // 2
        held = x[None]
        while mask:
            held = jnp.concatenate([held, flip(held, mask)])
            known = known + [o ^ mask for o in known]
            mask //= 2
        held = jnp.concatenate([held, flip(held, 1, "sub")])
        known = [2 * o for o in known] + [2 * o + 1 for o in known]
        return jnp.stack([held[known.index(r)] for r in range(owners)])

    def exchange(x, axes=where):
        return lax.all_to_all(x, axes, split_axis=0, concat_axis=0, tiled=True)

    index_all = gather_relative(jnp.pad(index.T.astype(BF16), ((0, 16 - top), (0, 0))))[:, :top]
    blocks = {0: grad}
    for o in sorted(range(1, groups), key=lambda o: (o.bit_count(), o)):
        last = o & -o
        blocks[o] = flip(blocks[o ^ last], last)
    first_all = gather_relative(first[0].T)

    mine = jnp.any(index_all.astype(jnp.int32) == me, axis=1)
    before = jnp.triu(jnp.ones((toks, toks), BF16), 1)
    pos = jnp.dot(mine.astype(BF16), before, preferred_element_type=F32).astype(jnp.int32)
    pos = jnp.where(mine, pos, -1).reshape(owners, 1, toks)

    back, grads, low_parts = [], [], []
    for o in range(0, groups, 2):
        batch = [blocks[o], flip(blocks[o], 1, "sub"), blocks[o + 1], flip(blocks[o + 1], 1, "sub")]
        *give, keep, low = expert_rows_call(
            rep_at, pos[2 * o : 2 * o + 4], batch, second[0], down[0], shares, slots
        )
        parts = [keep] + [turn(x, k + 1) for k, x in enumerate(give)]
        for k, rows in enumerate(share_sum_call(parts, 4)):
            r = 2 * o + k
            back.append(flip(rows, r, where) if r else rows)
        grads += batch
        low_parts.append(low)

    hid = hidden.reshape(pairs, units)
    idx_col = index.reshape(pairs, 1)
    prob_col = weight.reshape(pairs, 1).astype(F32)
    hits = index[:, :, None] == jnp.arange(owners, dtype=jnp.int32)
    hit = jnp.any(hits, axis=1)
    place = jnp.dot(before.T, hit.astype(BF16), preferred_element_type=F32).astype(jnp.int32)
    place = place + slots * lax.bitwise_xor(me, jnp.arange(owners, dtype=jnp.int32))
    target = jnp.sum(jnp.where(hits, place[:, None, :], 0), axis=2).reshape(pairs, 1)
    prob_dense = jnp.sum(jnp.where(hits, weight[:, :, None].astype(F32), 0.0), axis=1)

    first_all = place_call(me_at, [first_all]).reshape(width, units)
    low_hid = over_rep(lowrank_hid_call(idx_col, hid, first_all, rank, top))
    scaled_hid = (low_hid * jnp.repeat(prob_dense, rank, axis=1)).astype(BF16)
    scaled_hid = exchange(scaled_hid.T.reshape(owners, rank, toks))
    second_grad = second_grad_call(me_at, scaled_hid, grads)

    low_grad = exchange(place_call(me_at, low_parts))
    low_grad = over_rep(low_grad.reshape(width, toks).T.astype(F32))

    keep, give = first_grad_call(sub_at, idx_col, prob_col, low_grad, hid, rank, top, cores)
    first_part = (keep + flip(give, 1, "sub").astype(F32)).astype(BF16)
    first_grad = jnp.sum(exchange(first_part, "ep").astype(F32), axis=0)

    grad_hidden, sums = finish_call(
        idx_col, target, prob_col, low_grad, hid, first_all, back, rank, top
    )
    return (
        grad_hidden.reshape(toks, top, units),
        over_rep(sums.reshape(toks, top)),
        first_grad.T[None],
        second_grad[None],
    )


def solution(mesh):
    return jax.shard_map(
        body,
        mesh=mesh,
        in_specs=(
            P(("grp", "ep", "sub"), "rep"),
            P(("grp", "ep", "sub"), None, "rep"),
            P(("grp", "ep", "sub"), None),
            P(("grp", "ep", "sub"), None),
            P(("ep", "sub"), None, "rep"),
            P(("grp", "ep", "sub"), "rep", None),
            P(("grp", "ep", "sub"), None, "rep"),
        ),
        out_specs=(
            P(("grp", "ep", "sub"), None, "rep"),
            P(("grp", "ep", "sub"), None),
            P(("grp", "ep", "sub"), "rep", None),
            P(("grp", "ep", "sub"), None, "rep"),
        ),
        check_vma=False,
    )
```

time: 258 us -> 284 us (1.10)
  starting transfers between devices: 36.1 us -> 70.8 us
  local copies, waits for them, and re-layouts: 18.2 us -> 52.3 us
  blocking collectives: 25 us -> 0 us
  between operations: 14.2 us -> 1.26 us
  waiting for transfers between devices: 98.2 us -> 90.4 us
  Pallas kernels: 54.2 us -> 57.8 us
    ppermute x0 -> x39, waiting for transfers between devices: none -> 77.6 us  [flip(): return lax.ppermute(x, axis, [(i, i ^ mask) for i in range(size)])]
    all_gather x1 -> x0, waiting for transfers between devices: 52.1 us -> none  [body(): grad_all = lax.all_gather(grad, where)]
    ppermute x0 -> x39, starting transfers between devices: none -> 44.5 us  [flip(): return lax.ppermute(x, axis, [(i, i ^ mask) for i in range(size)])]
    unnamed x34 -> x174, local copies, waits for them, and re-layouts: 8.92 us -> 45.1 us
    ppermute x6 -> x7, waiting for transfers between devices: 39.9 us -> 10.2 us  [turn(): lax.ppermute(x, 'rep', [(r, (r + offset) % shares) for r in range(shares)])]
    all_gather x1 -> x0, blocking collectives: 25 us -> none  [body(): small_all = lax.all_gather(small, where)]
    all_to_all x5 -> x3, starting transfers between devices: 27.9 us -> 17.7 us  [exchange(): return lax.all_to_all(x, axes, split_axis=0, concat_axis=0, tiled=True)]
    pallas_call x6 -> x12, Pallas kernels: 45.3 us -> 48.7 us  [the longest x4 32.7 us: expert_rows_call(): pl.pallas_call(functools.partial(expert_rows_kernel, slots, tiles, shares...]
  transfers between devices with their start and end apart: 13 -> 49, of which waited for: 6 -> 18; matrix products, arithmetic and copies ran while one was open for 8% -> 9% of each run, Pallas kernels for 14% -> 18%
where the time goes in v2:
time: 284 us; the launch traced here: 281 us
  waiting for transfers between devices  90.4 us (32%)
  starting transfers between devices  70.8 us (25%)
  Pallas kernels  57.8 us (20%)
  local copies, waits for them, and re-layouts  52.3 us (18%)
  other arithmetic  8.59 us (3%)
    ppermute x39, waiting for transfers between devices, flip(): return lax.ppermute(x, axis, [(i, i ^ mask) for i in range(size)])  77.6 us
    unnamed x174, local copies, waits for them, and re-layouts  45.1 us
    ppermute x39, starting transfers between devices, flip(): return lax.ppermute(x, axis, [(i, i ^ mask) for i in range(size)])  44.5 us
    pallas_call x4, Pallas kernels, expert_rows_call(): pl.pallas_call(functools.partial(expert_rows_kernel, slots, tiles, shares...  32.7 us
    all_to_all x3, starting transfers between devices, exchange(): return lax.all_to_all(x, axes, split_axis=0, concat_axis=0, tiled=True)  17.7 us
    ppermute x7, waiting for transfers between devices, turn(): lax.ppermute(x, 'rep', [(r, (r + offset) % shares) for r in range(shares)])  10.2 us
    ppermute x7, starting transfers between devices, turn(): lax.ppermute(x, 'rep', [(r, (r + offset) % shares) for r in range(shares)])  8.66 us
    pallas_call x4, Pallas kernels, share_sum_call(): pl.pallas_call(functools.partial(share_sum_kernel, len(parts)), out_shape...  7.1 us
  transfers between devices with their start and end apart: 49, of which 18 were waited for; matrix products, arithmetic and copies ran while one was open for 9% of the time, Pallas kernels for 18%

profile of v2, /device:TPU:8, one launch (start us, length us, event | category | flops | bytes accessed | tf_op | source)
XLA Modules:
  0.0 281.4 jit_solution(24633372744863290)
XLA Ops:
  1.4 2.6 collective-permute-start
  4.4 1.8 collective-permute-start.5
  6.3 1.6 collective-permute-start.1
  7.9 1.4 constant_dynamic-update-slice_fusion.31
  9.3 18.4 %collective-permute-done.1 = bf16[2,16,128]{2,1,0:T(8,128)(2,1)S(1)} collective-permute-done((bf16[2,16,128]{2,1,0:T(8,128)(2,1)S(1)}, bf16[2,16,128]{2,1,0:T(8,128)(2,1)S(1)}, u32[]{:S(2)}, u32[]{:S(2)}) %collective-permute-start.1) | collective-permute-done | bytes 8224 | tf_op jit(solution)/shard_map/ppermute | solution.py:338
  27.8 1.5 collective-permute-start.2
  31.5 3.8 %collective-permute-start.20 = (bf16[1,32,768]{2,1,0:T(8,128)(2,1)}, bf16[1,32,768]{2,1,0:T(8,128)(2,1)S(1)}, u32[]{:S(2)}, u32[]{:S(2)}) collective-permute-start(bf16[1,32,768]{2,1,0:T(8,128)(2,1)} %bitcast.63), channel_id=1, source_target_pairs={{0,16},{4,20},{8,24},{12,28},{16,0},{20,4},{24,8},{28,12},{1,17},{... | collective-permute-start | bytes 147464 | tf_op jit(solution)/shard_map/ppermute | solution.py:338
  35.3 2.3 collective-permute-done.20
  37.6 1.2 collective-permute-done.3
  39.3 4.4 %collective-permute-done.21 = bf16[2,32,768]{2,1,0:T(8,128)(2,1)S(1)} collective-permute-done((bf16[2,32,768]{2,1,0:T(8,128)(2,1)S(1)}, bf16[2,32,768]{2,1,0:T(8,128)(2,1)S(1)}, u32[]{:S(2)}, u32[]{:S(2)}) %collective-permute-start.21) | collective-permute-done | bytes 98336 | tf_op jit(solution)/shard_map/ppermute | solution.py:338
  43.7 1.6 collective-permute-start.22
  45.3 4.6 %collective-permute-done.22 = bf16[4,32,768]{2,1,0:T(8,128)(2,1)S(1)} collective-permute-done((bf16[4,32,768]{2,1,0:T(8,128)(2,1)S(1)}, bf16[4,32,768]{2,1,0:T(8,128)(2,1)S(1)}, u32[]{:S(2)}, u32[]{:S(2)}) %collective-permute-start.22) | collective-permute-done | bytes 196640 | tf_op jit(solution)/shard_map/ppermute | solution.py:338
  50.6 1.5 collective-permute-start.13
  59.4 5.2 %collective-permute-done.15.rest_1_.refs_12_ = bf16[128,2048]{1,0:T(8,128)(2,1)S(1)} collective-permute-done((bf16[128,2048]{1,0:T(8,128)(2,1)S(1)}, bf16[128,2048]{1,0:T(8,128)(2,1)S(1)}, u32[]{:S(2)}, u32[]{:S(2)}) %collective-permute-start.15) | collective-permute-done | bytes 524320 | tf_op jit(solution)/shard_map/ppermute | solution.py:338
  64.6 1.5 collective-permute-start.17
  66.7 9.9 %collective-permute-done.9.rest_3_.refs_6_ = bf16[128,2048]{1,0:T(8,128)(2,1)S(1)} collective-permute-done((bf16[128,2048]{1,0:T(8,128)(2,1)S(1)}, bf16[128,2048]{1,0:T(8,128)(2,1)S(1)}, u32[]{:S(2)}, u32[]{:S(2)}) %collective-permute-start.9) | collective-permute-done | bytes 524320 | tf_op jit(solution)/shard_map/ppermute | solution.py:338
  79.0 8.1 %collective-permute-done.17.rest_3_.refs_14_ = bf16[128,2048]{1,0:T(8,128)(2,1)S(1)} collective-permute-done((bf16[128,2048]{1,0:T(8,128)(2,1)S(1)}, bf16[128,2048]{1,0:T(8,128)(2,1)S(1)}, u32[]{:S(2)}, u32[]{:S(2)}) %collective-permute-start.17) | collective-permute-done | bytes 524320 | tf_op jit(solution)/shard_map/ppermute | solution.py:338
  87.1 7.9 %expert_rows.4 = (bf16[320,768]{1,0:T(8,128)(2,1)S(1)}, bf16[320,768]{1,0:T(8,128)(2,1)S(1)}, bf16[4,32,128]{2,1,0:T(8,128)(2,1)S(1)}) custom-call(s32[1]{0:T(128)} %bitcast.1.rep_ref, s32[4,1,128]{2,1,0:T(1,128)S(1)} %bitcast.57, bf16[128,2048]{1,0:T(8,128)(2,1)S(1)} %copy-done.4, bf16[128,2048]{1,0:T(8,128)(2,1)} %collective-permute-done.4.rest_2_.refs_1_, ...), custom_call_target="tpu_custom_call" | custom-call | flops 2013265920 | bytes 6291456 | tf_op jit(solution)/shard_map/expert_rows/pallas_call | solution.py:105
  95.1 8.5 %expert_rows.5 = (bf16[320,768]{1,0:T(8,128)(2,1)}, bf16[320,768]{1,0:T(8,128)(2,1)S(1)}, bf16[4,32,128]{2,1,0:T(8,128)(2,1)S(1)}) custom-call(s32[1]{0:T(128)} %bitcast.1.rep_ref, s32[4,1,128]{2,1,0:T(1,128)S(1)} %bitcast.56, bf16[128,2048]{1,0:T(8,128)(2,1)S(1)} %collective-permute-done.7.rest_1_.refs_4_, ...), custom_call_target="tpu_custom_call" | custom-call | flops 2013265920 | bytes 6291456 | tf_op jit(solution)/shard_map/expert_rows/pallas_call | solution.py:105
  103.7 8.5 %expert_rows.6 = (bf16[320,768]{1,0:T(8,128)(2,1)}, bf16[320,768]{1,0:T(8,128)(2,1)S(1)}, bf16[4,32,128]{2,1,0:T(8,128)(2,1)S(1)}) custom-call(s32[1]{0:T(128)} %bitcast.1.rep_ref, s32[4,1,128]{2,1,0:T(1,128)S(1)} %bitcast.55, bf16[128,2048]{1,0:T(8,128)(2,1)S(1)} %collective-permute-done.11.rest_1_.refs_8_, ...), custom_call_target="tpu_custom_call" | custom-call | flops 2013265920 | bytes 6291456 | tf_op jit(solution)/shard_map/expert_rows/pallas_call | solution.py:105
  112.2 7.9 %expert_rows.7 = (bf16[320,768]{1,0:T(8,128)(2,1)S(1)}, bf16[320,768]{1,0:T(8,128)(2,1)S(1)}, bf16[4,32,128]{2,1,0:T(8,128)(2,1)S(1)}) custom-call(s32[1]{0:T(128)} %bitcast.1.rep_ref, s32[4,1,128]{2,1,0:T(1,128)S(1)} %bitcast.54, bf16[128,2048]{1,0:T(8,128)(2,1)S(1)} %collective-permute-done.15.rest_1_.refs_12_, ...), custom_call_target="tpu_custom_call" | custom-call | flops 2013265920 | bytes 6291456 | tf_op jit(solution)/shard_map/expert_rows/pallas_call | solution.py:105
  122.4 7.3 %all-to-all-start = ((bf16[16,32,128]{2,1,0:T(8,128)(2,1)}), bf16[16,32,128]{2,1,0:T(8,128)(2,1)S(1)}, u32[]{:S(2)}, u32[]{:S(2)}) async-start(bf16[16,32,128]{2,1,0:T(8,128)(2,1)} %place_blocks.2), calls=%async_computation | async-start | bytes 262144 | tf_op jit(solution)/shard_map/all_to_all | solution.py:352
  129.7 1.4 constant_dynamic-update-slice_fusion.18
  131.1 1.4 constant_dynamic-update-slice_fusion.17
  132.5 2.6 all-to-all-done
  136.0 1.5 collective-permute-start.19
  137.5 1.4 constant_dynamic-update-slice_fusion.16.refs_0_
  138.9 1.1 copy-done.28
  140.7 2.7 lowrank_hid.1
  143.4 1.5 collective-permute-start.45
  145.4 1.5 collective-permute-start.33
  148.0 3.6 %first_grad.1 = (f32[8,32,768]{2,1,0:T(8,128)S(1)}, bf16[8,32,768]{2,1,0:T(8,128)(2,1)}) custom-call(s32[1]{0:T(128)} %bitcast.23.sub_ref, s32[1024,1]{1,0:T(8,128)S(1)} %reshape.87.idx_ref, f32[1024,1]{1,0:T(8,128)S(1)} %reshape.88.prob_ref, f32[128,512]{1,0:T(8,128)S(1)} %bitcast_add_fusion.low_ref, bf16[1024,768]{1,0:T(8,128)(2,1)S(1)} %bitcast.47), custom_call_target="tpu_custom_call" | custom-call | tf_op jit(solution)/shard_map/first_grad/pallas_call | solution.py:239
  153.4 2.6 collective-permute-done.24.refs_1_
  157.0 1.8 share_sum.4
  159.5 2.2 collective-permute-done.45
  161.6 1.5 collective-permute-start.38
  163.1 1.8 fusion.2
  164.9 1.7 copy.55
  166.6 6.0 %all-to-all-start.2 = ((bf16[16,32,128]{2,1,0:T(8,128)(2,1)}), bf16[16,32,128]{2,1,0:T(8,128)(2,1)S(1)}, u32[]{:S(2)}, u32[]{:S(2)}) async-start(bf16[16,32,128]{2,1,0:T(8,128)(2,1)} %bitcast.67), calls=%async_computation.2 | async-start | bytes 262144 | tf_op jit(solution)/shard_map/all_to_all | solution.py:352
  172.6 1.5 collective-permute-start.26
  174.2 1.8 share_sum.5
  177.2 5.4 %collective-permute-done.33.refs_1_ = bf16[320,768]{1,0:T(8,128)(2,1)} collective-permute-done((bf16[320,768]{1,0:T(8,128)(2,1)}, bf16[320,768]{1,0:T(8,128)(2,1)}, u32[]{:S(2)}, u32[]{:S(2)}) %collective-permute-start.33) | collective-permute-done | bytes 491552 | tf_op jit(solution)/shard_map/ppermute | solution.py:331
  182.7 2.7 collective-permute-start.29
  185.4 1.9 add_convert_fusion
  187.3 4.4 %all-to-all-start.1 = ((bf16[8,32,768]{2,1,0:T(8,128)(2,1)}), bf16[8,32,768]{2,1,0:T(8,128)(2,1)}, u32[]{:S(2)}, u32[]{:S(2)}) async-start(bf16[8,32,768]{2,1,0:T(8,128)(2,1)} %add_convert_fusion), calls=%async_computation.1 | async-start | bytes 786432 | tf_op jit(solution)/shard_map/all_to_all | solution.py:352
  192.7 1.7 share_sum.6
  194.4 1.4 collective-permute-start.31
  195.8 2.6 collective-permute-start.32
  198.4 2.4 collective-permute-start.34
  200.8 2.1 collective-permute-start.36
  203.0 1.9 share_sum.7
  205.5 5.9 %collective-permute-start.37 = (bf16[80,768]{1,0:T(8,128)(2,1)}, bf16[80,768]{1,0:T(8,128)(2,1)S(1)}, u32[]{:S(2)}, u32[]{:S(2)}) collective-permute-start(bf16[80,768]{1,0:T(8,128)(2,1)} %get-tuple-element.57), channel_id=1, source_target_pairs={{0,21},{1,20},{4,17},{5,16},{8,29},{9,28},{12,25},{13,24},{16,5},{... | collective-permute-start | bytes 368648 | tf_op jit(solution)/shard_map/ppermute | solution.py:338
  213.2 8.5 %collective-permute-done.35.rest_9_ = bf16[80,768]{1,0:T(8,128)(2,1)S(1)} collective-permute-done((bf16[80,768]{1,0:T(8,128)(2,1)S(1)}, bf16[80,768]{1,0:T(8,128)(2,1)S(1)}, u32[]{:S(2)}, u32[]{:S(2)}) %collective-permute-start.35) | collective-permute-done | bytes 122912 | tf_op jit(solution)/shard_map/ppermute | solution.py:338
  222.4 2.3 collective-permute-start.41
  224.7 3.0 %collective-permute-start.42 = (bf16[80,768]{1,0:T(8,128)(2,1)}, bf16[80,768]{1,0:T(8,128)(2,1)S(1)}, u32[]{:S(2)}, u32[]{:S(2)}) collective-permute-start(bf16[80,768]{1,0:T(8,128)(2,1)} %get-tuple-element.63), channel_id=1, source_target_pairs={{0,29},{1,28},{4,25},{5,24},{8,21},{9,20},{12,17},{13,16},{16,13},... | collective-permute-start | bytes 368648 | tf_op jit(solution)/shard_map/ppermute | solution.py:338
  229.6 7.3 %collective-permute-done.39.rest_12_ = bf16[80,768]{1,0:T(8,128)(2,1)S(1)} collective-permute-done((bf16[80,768]{1,0:T(8,128)(2,1)}, bf16[80,768]{1,0:T(8,128)(2,1)S(1)}, u32[]{:S(2)}, u32[]{:S(2)}) %collective-permute-start.39) | collective-permute-done | bytes 122912 | tf_op jit(solution)/shard_map/ppermute | solution.py:338
  237.5 3.2 %collective-permute-done.40.rest_13_ = bf16[80,768]{1,0:T(8,128)(2,1)S(1)} collective-permute-done((bf16[80,768]{1,0:T(8,128)(2,1)}, bf16[80,768]{1,0:T(8,128)(2,1)S(1)}, u32[]{:S(2)}, u32[]{:S(2)}) %collective-permute-start.40) | collective-permute-done | bytes 122912 | tf_op jit(solution)/shard_map/ppermute | solution.py:338
  241.4 1.7 collective-permute-done.41.rest_14_
  243.7 2.5 collective-permute-done.42.rest_15_
  257.0 6.4 %finish.1 = (bf16[1024,768]{1,0:T(8,128)(2,1)}, f32[1024,1]{1,0:T(8,128)S(1)}) custom-call(s32[1024,1]{1,0:T(8,128)S(1)} %reshape.87.idx_ref, s32[1024,1]{1,0:T(8,128)S(1)} %copy-done.27, f32[1024,1]{1,0:T(8,128)S(1)} %reshape.88.prob_ref, f32[128,512]{1,0:T(8,128)S(1)} %copy-done.2, bf16[1024,768]{1,0:T(8,128)(2,1)} %bitcast.45, ...), custom_call_target="tpu_custom_call" | custom-call | tf_op jit(solution)/shard_map/finish/pallas_call | solution.py:286
  264.1 1.2 reduce
  265.5 1.6 collective-permute-start.43
  274.4 4.6 %second_grad.1 = f32[32,2048]{1,0:T(8,128)} custom-call(s32[1]{0:T(128)} %bitcast.me_ref, bf16[16,32,128]{2,1,0:T(8,128)(2,1)S(1)} %all-to-all-done.2.scaled_ref, bf16[128,2048]{1,0:T(8,128)(2,1)S(1)} %copy-done.5, bf16[128,2048]{1,0:T(8,128)(2,1)} %collective-permute-done.4.rest_2_.refs_1_, bf16[128,2048]{1,0:T(8,128)(2,1)} %collective-permute-done.5.rest_3_.refs_2_, ...), custom_call_target="tpu_custom_call" | custom-call | flops 268435456 | bytes 8388608 | tf_op jit(solution)/shard_map/second_grad/pallas_call | solution.py:190
  279.7 1.7 convert_reduce_fusion
  (258 shorter events, 52.7 us)
Async XLA Ops:
  0.6 37.0 %copy-start.67 = (bf16[1,768,32]{1,2,0:T(8,128)(2,1)S(1)}, bf16[1,768,32]{1,2,0:T(8,128)(2,1)}, u32[]{:S(2)}) copy-start(bf16[1,768,32]{1,2,0:T(8,128)(2,1)} %param.12) | copy-start | bytes 147460
  1.4 4.9 %collective-permute-start = (bf16[1,16,128]{2,1,0:T(8,128)(2,1)S(1)}, bf16[1,16,128]{2,1,0:T(8,128)(2,1)S(1)}, u32[]{:S(2)}, u32[]{:S(2)}) collective-permute-start(bf16[1,16,128]{2,1,0:T(8,128)(2,1)S(1)} %pad_bitcast_fusion), channel_id=1, source_target_pairs={{0,16},{4,20},{8,24},{12,28},{16,0},{20,4},{24,8},{28,12},{1,17},{... | collective-permute-start | bytes 12296 | tf_op jit(solution)/shard_map/ppermute | solution.py:338
  3.9 46.2 %collective-permute-start.11 = (bf16[128,2048]{1,0:T(8,128)(2,1)}, bf16[128,2048]{1,0:T(8,128)(2,1)S(1)}, u32[]{:S(2)}, u32[]{:S(2)}) collective-permute-start(bf16[128,2048]{1,0:T(8,128)(2,1)} %refs_0_.1), channel_id=1, source_target_pairs={{0,16},{4,20},{8,24},{12,28},{16,0},{20,4},{24,8},{28,12},{1,17},{... | collective-permute-start | bytes 1572872 | tf_op jit(solution)/shard_map/ppermute | solution.py:338
  4.3 46.3 %collective-permute-start.7 = (bf16[128,2048]{1,0:T(8,128)(2,1)}, bf16[128,2048]{1,0:T(8,128)(2,1)S(1)}, u32[]{:S(2)}, u32[]{:S(2)}) collective-permute-start(bf16[128,2048]{1,0:T(8,128)(2,1)} %refs_0_.1), channel_id=1, source_target_pairs={{0,8},{4,12},{8,0},{12,4},{16,24},{20,28},{24,16},{28,20},{1,9},{5... | collective-permute-start | bytes 1572872 | tf_op jit(solution)/shard_map/ppermute | solution.py:338
  4.4 53.8 %collective-permute-start.5 = (bf16[128,2048]{1,0:T(8,128)(2,1)}, bf16[128,2048]{1,0:T(8,128)(2,1)}, u32[]{:S(2)}, u32[]{:S(2)}) collective-permute-start(bf16[128,2048]{1,0:T(8,128)(2,1)} %refs_0_.1), channel_id=1, source_target_pairs={{0,4},{4,0},{8,12},{12,8},{16,20},{20,16},{24,28},{28,24},{1,5},{5... | collective-permute-start | bytes 1572872 | tf_op jit(solution)/shard_map/ppermute | solution.py:338
  6.2 52.6 %collective-permute-start.4 = (bf16[128,2048]{1,0:T(8,128)(2,1)}, bf16[128,2048]{1,0:T(8,128)(2,1)}, u32[]{:S(2)}, u32[]{:S(2)}) collective-permute-start(bf16[128,2048]{1,0:T(8,128)(2,1)} %refs_0_.1), channel_id=1, source_target_pairs={{0,1},{1,0},{2,3},{3,2},{4,5},{5,4},{6,7},{7,6},{8,9},{9,8},{10,11... | collective-permute-start | bytes 1572872 | tf_op jit(solution)/shard_map/ppermute | solution.py:338
  6.3 21.5 %collective-permute-start.1 = (bf16[2,16,128]{2,1,0:T(8,128)(2,1)S(1)}, bf16[2,16,128]{2,1,0:T(8,128)(2,1)S(1)}, u32[]{:S(2)}, u32[]{:S(2)}) collective-permute-start(bf16[2,16,128]{2,1,0:T(8,128)(2,1)S(1)} %pad_maximum_fusion.5), channel_id=1, source_target_pairs={{0,8},{4,12},{8,0},{12,4},{16,24},{20,28},{24,16},{28,20},{1,9},{5... | collective-permute-start | bytes 24584 | tf_op jit(solution)/shard_map/ppermute | solution.py:338
  27.8 3.7 %collective-permute-start.2 = (bf16[4,16,128]{2,1,0:T(8,128)(2,1)S(1)}, bf16[4,16,128]{2,1,0:T(8,128)(2,1)S(1)}, u32[]{:S(2)}, u32[]{:S(2)}) collective-permute-start(bf16[4,16,128]{2,1,0:T(8,128)(2,1)S(1)} %pad_maximum_fusion.4), channel_id=1, source_target_pairs={{0,4},{4,0},{8,12},{12,8},{16,20},{20,16},{24,28},{28,24},{1,5},{5... | collective-permute-start | bytes 49160 | tf_op jit(solution)/shard_map/ppermute | solution.py:338
  31.3 55.9 %copy-start.3 = (bf16[1,32,2048]{2,1,0:T(8,128)(2,1)S(1)}, bf16[1,32,2048]{2,1,0:T(8,128)(2,1)}, u32[]{:S(2)}) copy-start(bf16[1,32,2048]{2,1,0:T(8,128)(2,1)} %param.13) | copy-start | bytes 393220
  31.3 55.9 %copy-start.4 = (bf16[128,2048]{1,0:T(8,128)(2,1)S(1)}, bf16[128,2048]{1,0:T(8,128)(2,1)}, u32[]{:S(2)}) copy-start(bf16[128,2048]{1,0:T(8,128)(2,1)} %refs_0_.1) | copy-start | bytes 1572868
  31.5 6.1 %collective-permute-start.20 = (bf16[1,32,768]{2,1,0:T(8,128)(2,1)}, bf16[1,32,768]{2,1,0:T(8,128)(2,1)S(1)}, u32[]{:S(2)}, u32[]{:S(2)}) collective-permute-start(bf16[1,32,768]{2,1,0:T(8,128)(2,1)} %bitcast.63), channel_id=1, source_target_pairs={{0,16},{4,20},{8,24},{12,28},{16,0},{20,4},{24,8},{28,12},{1,17},{... | collective-permute-start | bytes 147464 | tf_op jit(solution)/shard_map/ppermute | solution.py:338
  37.6 1.2 collective-permute-start.3
  38.8 4.9 %collective-permute-start.21 = (bf16[2,32,768]{2,1,0:T(8,128)(2,1)S(1)}, bf16[2,32,768]{2,1,0:T(8,128)(2,1)S(1)}, u32[]{:S(2)}, u32[]{:S(2)}) collective-permute-start(bf16[2,32,768]{2,1,0:T(8,128)(2,1)S(1)} %pad_maximum_fusion.2), channel_id=1, source_target_pairs={{0,8},{4,12},{8,0},{12,4},{16,24},{20,28},{24,16},{28,20},{1,9},{5... | collective-permute-start | bytes 294920 | tf_op jit(solution)/shard_map/ppermute | solution.py:338
  43.7 6.2 %collective-permute-start.22 = (bf16[4,32,768]{2,1,0:T(8,128)(2,1)S(1)}, bf16[4,32,768]{2,1,0:T(8,128)(2,1)S(1)}, u32[]{:S(2)}, u32[]{:S(2)}) collective-permute-start(bf16[4,32,768]{2,1,0:T(8,128)(2,1)S(1)} %pad_maximum_fusion.1), channel_id=1, source_target_pairs={{0,4},{4,0},{8,12},{12,8},{16,20},{20,16},{24,28},{28,24},{1,5},{5... | collective-permute-start | bytes 589832 | tf_op jit(solution)/shard_map/ppermute | solution.py:338
  49.9 28.7 %copy-start.66 = (bf16[4,32,768]{2,1,0:T(8,128)(2,1)}, bf16[4,32,768]{2,1,0:T(8,128)(2,1)S(1)}, u32[]{:S(2)}) copy-start(bf16[4,32,768]{2,1,0:T(8,128)(2,1)S(1)} %collective-permute-done.22) | copy-start | bytes 589828
  49.9 2.2 collective-permute-start.23
  50.2 53.5 %copy-start.6 = (bf16[128,2048]{1,0:T(8,128)(2,1)}, bf16[128,2048]{1,0:T(8,128)(2,1)S(1)}, u32[]{:S(2)}) copy-start(bf16[128,2048]{1,0:T(8,128)(2,1)S(1)} %collective-permute-done.11.rest_1_.refs_8_) | copy-start | bytes 1572868
  50.2 14.4 %collective-permute-start.15 = (bf16[128,2048]{1,0:T(8,128)(2,1)S(1)}, bf16[128,2048]{1,0:T(8,128)(2,1)S(1)}, u32[]{:S(2)}, u32[]{:S(2)}) collective-permute-start(bf16[128,2048]{1,0:T(8,128)(2,1)S(1)} %collective-permute-done.11.rest_1_.refs_8_), channel_id=1, source_target_pairs={{0,8},{4,12},{8,0},{12,4},{16,24},{20,28},{24,16},{28,20},{1,9},{5... | collective-permute-start | bytes 1572872 | tf_op jit(solution)/shard_map/ppermute | solution.py:338
  50.6 44.5 %copy-start.8 = (bf16[128,2048]{1,0:T(8,128)(2,1)}, bf16[128,2048]{1,0:T(8,128)(2,1)S(1)}, u32[]{:S(2)}) copy-start(bf16[128,2048]{1,0:T(8,128)(2,1)S(1)} %collective-permute-done.7.rest_1_.refs_4_) | copy-start | bytes 1572868
  50.6 26.7 %collective-permute-start.13 = (bf16[128,2048]{1,0:T(8,128)(2,1)S(1)}, bf16[128,2048]{1,0:T(8,128)(2,1)S(1)}, u32[]{:S(2)}, u32[]{:S(2)}) collective-permute-start(bf16[128,2048]{1,0:T(8,128)(2,1)S(1)} %collective-permute-done.11.rest_1_.refs_8_), channel_id=1, source_target_pairs={{0,4},{4,0},{8,12},{12,8},{16,20},{20,16},{24,28},{28,24},{1,5},{5... | collective-permute-start | bytes 1572872 | tf_op jit(solution)/shard_map/ppermute | solution.py:338
  52.1 25.1 %copy-start.68 = (bf16[8,32,768]{2,1,0:T(8,128)(2,1)}, bf16[8,32,768]{2,1,0:T(8,128)(2,1)S(1)}, u32[]{:S(2)}) copy-start(bf16[8,32,768]{2,1,0:T(8,128)(2,1)S(1)} %collective-permute-done.23) | copy-start | bytes 1179652
  52.1 24.5 %collective-permute-start.9 = (bf16[128,2048]{1,0:T(8,128)(2,1)S(1)}, bf16[128,2048]{1,0:T(8,128)(2,1)S(1)}, u32[]{:S(2)}, u32[]{:S(2)}) collective-permute-start(bf16[128,2048]{1,0:T(8,128)(2,1)S(1)} %collective-permute-done.7.rest_1_.refs_4_), channel_id=1, source_target_pairs={{0,4},{4,0},{8,12},{12,8},{16,20},{20,16},{24,28},{28,24},{1,5},{5... | collective-permute-start | bytes 1572872 | tf_op jit(solution)/shard_map/ppermute | solution.py:338
  58.2 19.6 %collective-permute-start.8 = (bf16[128,2048]{1,0:T(8,128)(2,1)S(1)}, bf16[128,2048]{1,0:T(8,128)(2,1)S(1)}, u32[]{:S(2)}, u32[]{:S(2)}) collective-permute-start(bf16[128,2048]{1,0:T(8,128)(2,1)S(1)} %collective-permute-done.7.rest_1_.refs_4_), channel_id=1, source_target_pairs={{0,1},{1,0},{2,3},{3,2},{4,5},{5,4},{6,7},{7,6},{8,9},{9,8},{10,11... | collective-permute-start | bytes 1572872 | tf_op jit(solution)/shard_map/ppermute | solution.py:338
  58.9 19.7 %collective-permute-start.6 = (bf16[128,2048]{1,0:T(8,128)(2,1)}, bf16[128,2048]{1,0:T(8,128)(2,1)S(1)}, u32[]{:S(2)}, u32[]{:S(2)}) collective-permute-start(bf16[128,2048]{1,0:T(8,128)(2,1)} %collective-permute-done.5.rest_3_.refs_2_), channel_id=1, source_target_pairs={{0,1},{1,0},{2,3},{3,2},{4,5},{5,4},{6,7},{7,6},{8,9},{9,8},{10,11... | collective-permute-start | bytes 1572872 | tf_op jit(solution)/shard_map/ppermute | solution.py:338
  64.6 47.7 %copy-start.10 = (bf16[128,2048]{1,0:T(8,128)(2,1)}, bf16[128,2048]{1,0:T(8,128)(2,1)S(1)}, u32[]{:S(2)}) copy-start(bf16[128,2048]{1,0:T(8,128)(2,1)S(1)} %collective-permute-done.15.rest_1_.refs_12_) | copy-start | bytes 1572868
  64.6 22.6 %collective-permute-start.17 = (bf16[128,2048]{1,0:T(8,128)(2,1)S(1)}, bf16[128,2048]{1,0:T(8,128)(2,1)S(1)}, u32[]{:S(2)}, u32[]{:S(2)}) collective-permute-start(bf16[128,2048]{1,0:T(8,128)(2,1)S(1)} %collective-permute-done.15.rest_1_.refs_12_), channel_id=1, source_target_pairs={{0,4},{4,0},{8,12},{12,8},{16,20},{20,16},{24,28},{28,24},{1,5},{5... | collective-permute-start | bytes 1572872 | tf_op jit(solution)/shard_map/ppermute | solution.py:338
  76.6 18.5 %copy-start.13 = (bf16[128,2048]{1,0:T(8,128)(2,1)}, bf16[128,2048]{1,0:T(8,128)(2,1)S(1)}, u32[]{:S(2)}) copy-start(bf16[128,2048]{1,0:T(8,128)(2,1)S(1)} %collective-permute-done.9.rest_3_.refs_6_) | copy-start | bytes 1572868
  76.6 18.5 %collective-permute-start.10 = (bf16[128,2048]{1,0:T(8,128)(2,1)S(1)}, bf16[128,2048]{1,0:T(8,128)(2,1)S(1)}, u32[]{:S(2)}, u32[]{:S(2)}) collective-permute-start(bf16[128,2048]{1,0:T(8,128)(2,1)S(1)} %collective-permute-done.9.rest_3_.refs_6_), channel_id=1, source_target_pairs={{0,1},{1,0},{2,3},{3,2},{4,5},{5,4},{6,7},{7,6},{8,9},{9,8},{10,11... | collective-permute-start | bytes 1572872 | tf_op jit(solution)/shard_map/ppermute | solution.py:338
  77.3 26.4 %copy-start.11 = (bf16[128,2048]{1,0:T(8,128)(2,1)}, bf16[128,2048]{1,0:T(8,128)(2,1)S(1)}, u32[]{:S(2)}) copy-start(bf16[128,2048]{1,0:T(8,128)(2,1)S(1)} %collective-permute-done.13.rest_3_.refs_10_) | copy-start | bytes 1572868
  77.3 26.3 %collective-permute-start.12 = (bf16[128,2048]{1,0:T(8,128)(2,1)S(1)}, bf16[128,2048]{1,0:T(8,128)(2,1)S(1)}, u32[]{:S(2)}, u32[]{:S(2)}) collective-permute-start(bf16[128,2048]{1,0:T(8,128)(2,1)S(1)} %collective-permute-done.11.rest_1_.refs_8_), channel_id=1, source_target_pairs={{0,1},{1,0},{2,3},{3,2},{4,5},{5,4},{6,7},{7,6},{8,9},{9,8},{10,11... | collective-permute-start | bytes 1572872 | tf_op jit(solution)/shard_map/ppermute | solution.py:338
  77.8 25.8 %collective-permute-start.14 = (bf16[128,2048]{1,0:T(8,128)(2,1)S(1)}, bf16[128,2048]{1,0:T(8,128)(2,1)S(1)}, u32[]{:S(2)}, u32[]{:S(2)}) collective-permute-start(bf16[128,2048]{1,0:T(8,128)(2,1)S(1)} %collective-permute-done.13.rest_3_.refs_10_), channel_id=1, source_target_pairs={{0,1},{1,0},{2,3},{3,2},{4,5},{5,4},{6,7},{7,6},{8,9},{9,8},{10,11... | collective-permute-start | bytes 1572872 | tf_op jit(solution)/shard_map/ppermute | solution.py:338
  78.6 33.6 %collective-permute-start.16 = (bf16[128,2048]{1,0:T(8,128)(2,1)S(1)}, bf16[128,2048]{1,0:T(8,128)(2,1)S(1)}, u32[]{:S(2)}, u32[]{:S(2)}) collective-permute-start(bf16[128,2048]{1,0:T(8,128)(2,1)S(1)} %collective-permute-done.15.rest_1_.refs_12_), channel_id=1, source_target_pairs={{0,1},{1,0},{2,3},{3,2},{4,5},{5,4},{6,7},{7,6},{8,9},{9,8},{10,11... | collective-permute-start | bytes 1572872 | tf_op jit(solution)/shard_map/ppermute | solution.py:338
  87.1 25.1 %copy-start.19 = (bf16[128,2048]{1,0:T(8,128)(2,1)}, bf16[128,2048]{1,0:T(8,128)(2,1)S(1)}, u32[]{:S(2)}) copy-start(bf16[128,2048]{1,0:T(8,128)(2,1)S(1)} %collective-permute-done.17.rest_3_.refs_14_) | copy-start | bytes 1572868
  87.1 25.1 %collective-permute-start.18 = (bf16[128,2048]{1,0:T(8,128)(2,1)S(1)}, bf16[128,2048]{1,0:T(8,128)(2,1)S(1)}, u32[]{:S(2)}, u32[]{:S(2)}) collective-permute-start(bf16[128,2048]{1,0:T(8,128)(2,1)S(1)} %collective-permute-done.17.rest_3_.refs_14_), channel_id=1, source_target_pairs={{0,1},{1,0},{2,3},{3,2},{4,5},{5,4},{6,7},{7,6},{8,9},{9,8},{10,11... | collective-permute-start | bytes 1572872 | tf_op jit(solution)/shard_map/ppermute | solution.py:338
  122.4 12.7 %all-to-all-start = ((bf16[16,32,128]{2,1,0:T(8,128)(2,1)}), bf16[16,32,128]{2,1,0:T(8,128)(2,1)S(1)}, u32[]{:S(2)}, u32[]{:S(2)}) async-start(bf16[16,32,128]{2,1,0:T(8,128)(2,1)} %place_blocks.2), calls=%async_computation | async-start | bytes 262144 | tf_op jit(solution)/shard_map/all_to_all | solution.py:352
  136.0 11.0 %collective-permute-start.19 = (f32[128,512]{1,0:T(8,128)}, f32[128,512]{1,0:T(8,128)S(1)}, u32[]{:S(2)}, u32[]{:S(2)}) collective-permute-start(f32[128,512]{1,0:T(8,128)} %bitcast.14), channel_id=1, source_target_pairs={{0,2},{2,0},{1,3},{3,1},{4,6},{6,4},{5,7},{7,5},{8,10},{10,8},{9,1... | collective-permute-start | bytes 786440 | tf_op jit(solution)/shard_map/ppermute | solution.py:331
  140.1 15.9 %collective-permute-start.24 = (bf16[320,768]{1,0:T(8,128)(2,1)}, bf16[320,768]{1,0:T(8,128)(2,1)}, u32[]{:S(2)}, u32[]{:S(2)}) collective-permute-start(bf16[320,768]{1,0:T(8,128)(2,1)} %copy-done.61), channel_id=1, source_target_pairs={{0,2},{2,0},{1,3},{3,1},{4,6},{6,4},{5,7},{7,5},{8,10},{10,8},{9,1... | collective-permute-start | bytes 1474568 | tf_op jit(solution)/shard_map/ppermute | solution.py:331
  143.4 18.2 %collective-permute-start.45 = (f32[128,512]{1,0:T(8,128)}, f32[128,512]{1,0:T(8,128)}, u32[]{:S(2)}, u32[]{:S(2)}) collective-permute-start(f32[128,512]{1,0:T(8,128)} %lowrank_hid.1), channel_id=1, source_target_pairs={{0,2},{2,0},{1,3},{3,1},{4,6},{6,4},{5,7},{7,5},{8,10},{10,8},{9,1... | collective-permute-start | bytes 786440 | tf_op jit(solution)/shard_map/ppermute | solution.py:331
  144.9 27.7 %collective-permute-start.28 = (bf16[320,768]{1,0:T(8,128)(2,1)}, bf16[320,768]{1,0:T(8,128)(2,1)}, u32[]{:S(2)}, u32[]{:S(2)}) collective-permute-start(bf16[320,768]{1,0:T(8,128)(2,1)} %get-tuple-element.47), channel_id=1, source_target_pairs={{0,2},{2,0},{1,3},{3,1},{4,6},{6,4},{5,7},{7,5},{8,10},{10,8},{9,1... | collective-permute-start | bytes 1474568 | tf_op jit(solution)/shard_map/ppermute | solution.py:331
  145.4 37.2 %collective-permute-start.33 = (bf16[320,768]{1,0:T(8,128)(2,1)}, bf16[320,768]{1,0:T(8,128)(2,1)}, u32[]{:S(2)}, u32[]{:S(2)}) collective-permute-start(bf16[320,768]{1,0:T(8,128)(2,1)} %get-tuple-element.53), channel_id=1, source_target_pairs={{0,2},{2,0},{1,3},{3,1},{4,6},{6,4},{5,7},{7,5},{8,10},{10,8},{9,1... | collective-permute-start | bytes 1474568 | tf_op jit(solution)/shard_map/ppermute | solution.py:331
  152.4 33.0 %collective-permute-start.44 = (bf16[8,32,768]{2,1,0:T(8,128)(2,1)}, bf16[8,32,768]{2,1,0:T(8,128)(2,1)}, u32[]{:S(2)}, u32[]{:S(2)}) collective-permute-start(bf16[8,32,768]{2,1,0:T(8,128)(2,1)} %get-tuple-element.67), channel_id=1, source_target_pairs={{0,1},{1,0},{2,3},{3,2},{4,5},{5,4},{6,7},{7,6},{8,9},{9,8},{10,11... | collective-permute-start | bytes 1179656 | tf_op jit(solution)/shard_map/ppermute | solution.py:338
  152.5 21.7 %copy-start.37 = (bf16[320,768]{1,0:T(8,128)(2,1)S(1)}, bf16[320,768]{1,0:T(8,128)(2,1)}, u32[]{:S(2)}) copy-start(bf16[320,768]{1,0:T(8,128)(2,1)} %copy-done.36) | copy-start | bytes 1474564
  157.0 28.4 %copy-start.30 = (f32[8,32,768]{2,1,0:T(8,128)S(1)}, f32[8,32,768]{2,1,0:T(8,128)}, u32[]{:S(2)}) copy-start(f32[8,32,768]{2,1,0:T(8,128)} %copy-done.29) | copy-start | bytes 2359300
  159.4 17.8 %collective-permute-start.25 = (bf16[80,768]{1,0:T(8,128)(2,1)}, bf16[80,768]{1,0:T(8,128)(2,1)S(1)}, u32[]{:S(2)}, u32[]{:S(2)}) collective-permute-start(bf16[80,768]{1,0:T(8,128)(2,1)} %get-tuple-element.43), channel_id=1, source_target_pairs={{0,1},{1,0},{4,5},{5,4},{8,9},{9,8},{12,13},{13,12},{16,17},{17,16... | collective-permute-start | bytes 368648 | tf_op jit(solution)/shard_map/ppermute | solution.py:338
  161.6 39.2 %collective-permute-start.38 = (bf16[320,768]{1,0:T(8,128)(2,1)}, bf16[320,768]{1,0:T(8,128)(2,1)}, u32[]{:S(2)}, u32[]{:S(2)}) collective-permute-start(bf16[320,768]{1,0:T(8,128)(2,1)} %copy-done.60), channel_id=1, source_target_pairs={{0,2},{2,0},{1,3},{3,1},{4,6},{6,4},{5,7},{7,5},{8,10},{10,8},{9,1... | collective-permute-start | bytes 1474568 | tf_op jit(solution)/shard_map/ppermute | solution.py:331
  166.6 20.7 %all-to-all-start.2 = ((bf16[16,32,128]{2,1,0:T(8,128)(2,1)}), bf16[16,32,128]{2,1,0:T(8,128)(2,1)S(1)}, u32[]{:S(2)}, u32[]{:S(2)}) async-start(bf16[16,32,128]{2,1,0:T(8,128)(2,1)} %bitcast.67), calls=%async_computation.2 | async-start | bytes 262144 | tf_op jit(solution)/shard_map/all_to_all | solution.py:352
  172.6 21.8 %collective-permute-start.26 = (bf16[80,768]{1,0:T(8,128)(2,1)}, bf16[80,768]{1,0:T(8,128)(2,1)}, u32[]{:S(2)}, u32[]{:S(2)}) collective-permute-start(bf16[80,768]{1,0:T(8,128)(2,1)} %copy-done.65), channel_id=1, source_target_pairs={{0,4},{1,5},{4,0},{5,1},{8,12},{9,13},{12,8},{13,9},{16,20},{17,21... | collective-permute-start | bytes 368648 | tf_op jit(solution)/shard_map/ppermute | solution.py:338
  177.2 18.6 %collective-permute-start.27 = (bf16[80,768]{1,0:T(8,128)(2,1)}, bf16[80,768]{1,0:T(8,128)(2,1)}, u32[]{:S(2)}, u32[]{:S(2)}) collective-permute-start(bf16[80,768]{1,0:T(8,128)(2,1)} %copy-done.64), channel_id=1, source_target_pairs={{0,5},{1,4},{4,1},{5,0},{8,13},{9,12},{12,9},{13,8},{16,21},{17,20... | collective-permute-start | bytes 368648 | tf_op jit(solution)/shard_map/ppermute | solution.py:338
  182.7 15.7 %collective-permute-start.29 = (bf16[80,768]{1,0:T(8,128)(2,1)}, bf16[80,768]{1,0:T(8,128)(2,1)}, u32[]{:S(2)}, u32[]{:S(2)}) collective-permute-start(bf16[80,768]{1,0:T(8,128)(2,1)} %get-tuple-element.48), channel_id=1, source_target_pairs={{0,8},{1,9},{4,12},{5,13},{8,0},{9,1},{12,4},{13,5},{16,24},{17,25... | collective-permute-start | bytes 368648 | tf_op jit(solution)/shard_map/ppermute | solution.py:338
  185.4 15.4 %collective-permute-start.30 = (bf16[80,768]{1,0:T(8,128)(2,1)}, bf16[80,768]{1,0:T(8,128)(2,1)}, u32[]{:S(2)}, u32[]{:S(2)}) collective-permute-start(bf16[80,768]{1,0:T(8,128)(2,1)} %get-tuple-element.49), channel_id=1, source_target_pairs={{0,9},{1,8},{4,13},{5,12},{8,1},{9,0},{12,5},{13,4},{16,25},{17,24... | collective-permute-start | bytes 368648 | tf_op jit(solution)/shard_map/ppermute | solution.py:338
  187.3 59.7 %copy-start.2 = (f32[128,512]{1,0:T(8,128)S(1)}, f32[128,512]{1,0:T(8,128)}, u32[]{:S(2)}) copy-start(f32[128,512]{1,0:T(8,128)} %copy-done.1) | copy-start | bytes 786436
  187.3 92.4 %all-to-all-start.1 = ((bf16[8,32,768]{2,1,0:T(8,128)(2,1)}), bf16[8,32,768]{2,1,0:T(8,128)(2,1)}, u32[]{:S(2)}, u32[]{:S(2)}) async-start(bf16[8,32,768]{2,1,0:T(8,128)(2,1)} %add_convert_fusion), calls=%async_computation.1 | async-start | bytes 786432 | tf_op jit(solution)/shard_map/all_to_all | solution.py:352
  194.4 10.4 %collective-permute-start.31 = (bf16[80,768]{1,0:T(8,128)(2,1)}, bf16[80,768]{1,0:T(8,128)(2,1)S(1)}, u32[]{:S(2)}, u32[]{:S(2)}) collective-permute-start(bf16[80,768]{1,0:T(8,128)(2,1)} %copy-done.63), channel_id=1, source_target_pairs={{0,12},{1,13},{4,8},{5,9},{8,4},{9,5},{12,0},{13,1},{16,28},{17,29... | collective-permute-start | bytes 368648 | tf_op jit(solution)/shard_map/ppermute | solution.py:338
  195.8 15.6 %collective-permute-start.32 = (bf16[80,768]{1,0:T(8,128)(2,1)}, bf16[80,768]{1,0:T(8,128)(2,1)S(1)}, u32[]{:S(2)}, u32[]{:S(2)}) collective-permute-start(bf16[80,768]{1,0:T(8,128)(2,1)} %copy-done.62), channel_id=1, source_target_pairs={{0,13},{1,12},{4,9},{5,8},{8,5},{9,4},{12,1},{13,0},{16,29},{17,28... | collective-permute-start | bytes 368648 | tf_op jit(solution)/shard_map/ppermute | solution.py:338
  198.4 13.7 %collective-permute-start.34 = (bf16[80,768]{1,0:T(8,128)(2,1)S(1)}, bf16[80,768]{1,0:T(8,128)(2,1)S(1)}, u32[]{:S(2)}, u32[]{:S(2)}) collective-permute-start(bf16[80,768]{1,0:T(8,128)(2,1)S(1)} %get-tuple-element.54), channel_id=1, source_target_pairs={{0,16},{1,17},{4,20},{5,21},{8,24},{9,25},{12,28},{13,29},{16,0},{... | collective-permute-start | bytes 368648 | tf_op jit(solution)/shard_map/ppermute | solution.py:338
  200.8 20.9 %collective-permute-start.35 = (bf16[80,768]{1,0:T(8,128)(2,1)S(1)}, bf16[80,768]{1,0:T(8,128)(2,1)S(1)}, u32[]{:S(2)}, u32[]{:S(2)}) collective-permute-start(bf16[80,768]{1,0:T(8,128)(2,1)S(1)} %get-tuple-element.55), channel_id=1, source_target_pairs={{0,17},{1,16},{4,21},{5,20},{8,25},{9,24},{12,29},{13,28},{16,1},{... | collective-permute-start | bytes 368648 | tf_op jit(solution)/shard_map/ppermute | solution.py:338
  200.8 23.9 %collective-permute-start.36 = (bf16[80,768]{1,0:T(8,128)(2,1)S(1)}, bf16[80,768]{1,0:T(8,128)(2,1)S(1)}, u32[]{:S(2)}, u32[]{:S(2)}) collective-permute-start(bf16[80,768]{1,0:T(8,128)(2,1)S(1)} %get-tuple-element.56), channel_id=1, source_target_pairs={{0,20},{1,21},{4,16},{5,17},{8,28},{9,29},{12,24},{13,25},{16,4},{... | collective-permute-start | bytes 368648 | tf_op jit(solution)/shard_map/ppermute | solution.py:338
  205.5 23.4 %collective-permute-start.37 = (bf16[80,768]{1,0:T(8,128)(2,1)}, bf16[80,768]{1,0:T(8,128)(2,1)S(1)}, u32[]{:S(2)}, u32[]{:S(2)}) collective-permute-start(bf16[80,768]{1,0:T(8,128)(2,1)} %get-tuple-element.57), channel_id=1, source_target_pairs={{0,21},{1,20},{4,17},{5,16},{8,29},{9,28},{12,25},{13,24},{16,5},{... | collective-permute-start | bytes 368648 | tf_op jit(solution)/shard_map/ppermute | solution.py:338
  212.1 24.8 %collective-permute-start.39 = (bf16[80,768]{1,0:T(8,128)(2,1)}, bf16[80,768]{1,0:T(8,128)(2,1)S(1)}, u32[]{:S(2)}, u32[]{:S(2)}) collective-permute-start(bf16[80,768]{1,0:T(8,128)(2,1)} %get-tuple-element.60), channel_id=1, source_target_pairs={{0,24},{1,25},{4,28},{5,29},{8,16},{9,17},{12,20},{13,21},{16,8},{... | collective-permute-start | bytes 368648 | tf_op jit(solution)/shard_map/ppermute | solution.py:338
  212.7 28.0 %collective-permute-start.40 = (bf16[80,768]{1,0:T(8,128)(2,1)}, bf16[80,768]{1,0:T(8,128)(2,1)S(1)}, u32[]{:S(2)}, u32[]{:S(2)}) collective-permute-start(bf16[80,768]{1,0:T(8,128)(2,1)} %get-tuple-element.61), channel_id=1, source_target_pairs={{0,25},{1,24},{4,29},{5,28},{8,17},{9,16},{12,21},{13,20},{16,9},{... | collective-permute-start | bytes 368648 | tf_op jit(solution)/shard_map/ppermute | solution.py:338
  222.4 20.7 %collective-permute-start.41 = (bf16[80,768]{1,0:T(8,128)(2,1)}, bf16[80,768]{1,0:T(8,128)(2,1)S(1)}, u32[]{:S(2)}, u32[]{:S(2)}) collective-permute-start(bf16[80,768]{1,0:T(8,128)(2,1)} %get-tuple-element.62), channel_id=1, source_target_pairs={{0,28},{1,29},{4,24},{5,25},{8,20},{9,21},{12,16},{13,17},{16,12},... | collective-permute-start | bytes 368648 | tf_op jit(solution)/shard_map/ppermute | solution.py:338
  224.7 21.6 %copy-start.48 = (bf16[80,768]{1,0:T(8,128)(2,1)}, bf16[80,768]{1,0:T(8,128)(2,1)S(1)}, u32[]{:S(2)}) copy-start(bf16[80,768]{1,0:T(8,128)(2,1)S(1)} %collective-permute-done.36.rest_10_) | copy-start | bytes 368644
  224.7 21.6 %collective-permute-start.42 = (bf16[80,768]{1,0:T(8,128)(2,1)}, bf16[80,768]{1,0:T(8,128)(2,1)S(1)}, u32[]{:S(2)}, u32[]{:S(2)}) collective-permute-start(bf16[80,768]{1,0:T(8,128)(2,1)} %get-tuple-element.63), channel_id=1, source_target_pairs={{0,29},{1,28},{4,25},{5,24},{8,21},{9,20},{12,17},{13,16},{16,13},... | collective-permute-start | bytes 368648 | tf_op jit(solution)/shard_map/ppermute | solution.py:338
  265.5 13.5 %collective-permute-start.43 = (f32[128,8]{1,0:T(8,128)S(1)}, f32[128,8]{1,0:T(8,128)S(1)}, u32[]{:S(2)}, u32[]{:S(2)}) collective-permute-start(f32[128,8]{1,0:T(8,128)S(1)} %reshape.80), channel_id=1, source_target_pairs={{0,2},{2,0},{1,3},{3,1},{4,6},{6,4},{5,7},{7,5},{8,10},{10,8},{9,1... | collective-permute-start | bytes 12296 | tf_op jit(solution)/shard_map/ppermute | solution.py:331
  (56 other events, 217.1 us)

commit v3 on v2

--- a/solution.py
+++ b/solution.py
@@ -19,8 +19,11 @@
     return lax.dot_general(a, b, dims, preferred_element_type=F32)
 
 
-def params(mib=48):
+def params(mib=16):
     return pltpu.CompilerParams(vmem_limit_bytes=mib * 2**20)
+
+
+SMALL = pl.CostEstimate(flops=1, bytes_accessed=1, transcendentals=0)
 
 
 def whole(shape):
@@ -58,25 +61,31 @@
         out_specs=pl.BlockSpec((blk // top, width), lambda i: (i, 0)),
         out_shape=jax.ShapeDtypeStruct((pairs // top, width), F32),
         compiler_params=params(),
-        cost_estimate=pl.CostEstimate(
-            flops=4 * pairs * width * units, bytes_accessed=2 * pairs * units, transcendentals=0
-        ),
+        cost_estimate=SMALL,
         name="lowrank_hid",
     )(idx_col, hid, first_all)
 
 
-def expert_rows_kernel(slots, tiles, shares, batch, rep_ref, *rest):
-    pos_ref, grads = rest[0], rest[1 : 1 + batch]
-    second_ref, weight_ref = rest[1 + batch], rest[2 + batch]
-    outs, low_ref, rows_ref = rest[3 + batch : -2], rest[-2], rest[-1]
+def expert_rows_kernel(slots, tiles, shares, batch, feats, route_row, at_ref, *rest):
+    grads, second_ref, weight_ref = rest[:batch], rest[batch], rest[batch + 1]
+    outs, low_ref, rows_ref = rest[-2 - shares : -2], rest[-2], rest[-1]
     step = pl.program_id(0)
 
     @pl.when(step == 0)
     def _():
+        toks = grads[0].shape[0]
+        before = lax.broadcasted_iota(jnp.int32, (toks, toks), 0) < lax.broadcasted_iota(
+            jnp.int32, (toks, toks), 1
+        )
+        before = jnp.where(before, 1.0, 0.0).astype(BF16)
+        slot = lax.broadcasted_iota(jnp.int32, (slots, toks), 0).astype(F32)
         for k, grad_ref in enumerate(grads):
-            grad = grad_ref[...]
-            slot = lax.broadcasted_iota(jnp.int32, (slots, grad.shape[0]), 0)
-            pick = jnp.where(slot == pos_ref[k], 1.0, 0.0).astype(BF16)
+            routes = grad_ref[pl.ds(route_row, 16), pl.ds(feats, toks)].astype(F32)
+            hits = jnp.where(routes == at_ref[1].astype(F32), 1.0, 0.0)
+            mine = jnp.max(hits, axis=0, keepdims=True)
+            pos = dot(jnp.broadcast_to(mine, (16, toks)).astype(BF16), before, NN)[:1]
+            pick = jnp.where((slot == pos) & (mine > 0.0), 1.0, 0.0).astype(BF16)
+            grad = grad_ref[:, pl.ds(0, feats)]
             rows_ref[pl.ds(k * slots, slots), :] = dot(pick, grad, NN).astype(BF16)
             low_ref[k] = dot(second_ref[...], grad, NT).astype(BF16)
 
@@ -88,28 +97,28 @@
             out_ref[...] = value
 
 
-def expert_rows_call(rep_at, pos, grads, second, down, shares, slots):
-    batch, (toks, feats) = len(grads), grads[0].shape
-    rank = second.shape[0]
+def expert_rows_call(at, grads, second, down, shares, slots, after):
+    batch, (toks, wide) = len(grads), grads[0].shape
+    rank, feats = second.shape
     units = down.shape[0] // shares
     tiles = 3
     tile = units // tiles
     rows = batch * slots
 
-    def weight_at(i, rep):
-        return (lax.rem(rep[0] + i // tiles + 1, shares) * tiles + lax.rem(i, tiles), 0)
-
-    def out_at(k, i, rep):
+    def weight_at(i, at):
+        return (lax.rem(at[0] + i // tiles + 1, shares) * tiles + lax.rem(i, tiles), 0)
+
+    def out_at(k, i, at):
         return (0, jnp.clip(i - k * tiles, 0, tiles - 1))
 
     return pl.pallas_call(
-        functools.partial(expert_rows_kernel, slots, tiles, shares, batch),
+        functools.partial(expert_rows_kernel, slots, tiles, shares, batch, feats, 3 * rank),
         grid_spec=pltpu.PrefetchScalarGridSpec(
             num_scalar_prefetch=1,
             grid=(shares * tiles,),
-            in_specs=[whole((batch, 1, toks))]
-            + [whole((toks, feats))] * batch
-            + [whole((rank, feats)), pl.BlockSpec((tile, feats), weight_at)],
+            in_specs=[whole((toks, wide))] * batch
+            + [whole((rank, feats)), pl.BlockSpec((tile, feats), weight_at)]
+            + [pl.BlockSpec(memory_space=pl.ANY)] * len(after),
             out_specs=[
                 pl.BlockSpec((rows, tile), functools.partial(out_at, k)) for k in range(shares)
             ]
@@ -119,13 +128,9 @@
         out_shape=[jax.ShapeDtypeStruct((rows, units), BF16)] * shares
         + [jax.ShapeDtypeStruct((batch, rank, toks), BF16)],
         compiler_params=params(),
-        cost_estimate=pl.CostEstimate(
-            flops=2 * rows * down.shape[0] * feats,
-            bytes_accessed=2 * down.shape[0] * feats,
-            transcendentals=0,
-        ),
+        cost_estimate=SMALL,
         name="expert_rows",
-    )(rep_at, pos, *grads, second, down)
+    )(at, *grads, second, down, *after)
 
 
 def share_sum_kernel(parts, *refs):
@@ -145,33 +150,49 @@
         functools.partial(share_sum_kernel, len(parts)),
         out_shape=[jax.ShapeDtypeStruct((rows // batch, units), BF16)] * batch,
         compiler_params=params(),
+        cost_estimate=SMALL,
         name="share_sum",
     )(*parts)
 
 
-def place_kernel(me_ref, *refs):
-    out_ref, at = refs[-1], 0
-    for ref in refs[:-1]:
+def collect_kernel(parts, me_ref, *refs):
+    low_ref, first_ref = refs[-2:]
+    rank = first_ref.shape[1]
+    at = 0
+    for ref in refs[:parts]:
         for k in range(ref.shape[0]):
-            out_ref[lax.bitwise_xor(me_ref[0], at)] = ref[k]
+            low_ref[lax.bitwise_xor(me_ref[0], at)] = ref[k]
             at += 1
-
-
-def place_call(me_at, blocks):
-    count = sum(b.shape[0] for b in blocks)
-    shape = (count,) + blocks[0].shape[1:]
-    return pl.pallas_call(
-        place_kernel,
+    for r, ref in enumerate(refs[parts:-2]):
+        wide = ref.shape[1]
+        for k in range(3):
+            first_ref[lax.bitwise_xor(me_ref[0], r), :, pl.ds(k * wide, wide)] = ref[
+                pl.ds(k * rank, rank), :
+            ]
+
+
+def collect_call(me_at, lows, grads, feats):
+    owners, (toks, wide) = len(grads), grads[0].shape
+    rank = lows[0].shape[1]
+    extra = wide - feats
+    low_shape, first_shape = (owners, rank, toks), (owners, rank, 3 * extra)
+    return pl.pallas_call(
+        functools.partial(collect_kernel, len(lows)),
         grid_spec=pltpu.PrefetchScalarGridSpec(
             num_scalar_prefetch=1,
             grid=(1,),
-            in_specs=[whole(b.shape) for b in blocks],
-            out_specs=whole(shape),
-        ),
-        out_shape=jax.ShapeDtypeStruct(shape, blocks[0].dtype),
-        compiler_params=params(),
-        name="place_blocks",
-    )(me_at, *blocks)
+            in_specs=[whole(b.shape) for b in lows]
+            + [pl.BlockSpec((toks, extra), lambda i, me: (0, feats // extra))] * owners,
+            out_specs=[whole(low_shape), whole(first_shape)],
+        ),
+        out_shape=[
+            jax.ShapeDtypeStruct(low_shape, BF16),
+            jax.ShapeDtypeStruct(first_shape, BF16),
+        ],
+        compiler_params=params(),
+        cost_estimate=SMALL,
+        name="collect_blocks",
+    )(me_at, *lows, *grads)
 
 
 def second_grad_kernel(me_ref, scaled_ref, *refs):
@@ -182,9 +203,8 @@
     out_ref[...] = adapter_scale * total
 
 
-def second_grad_call(me_at, scaled, grads):
+def second_grad_call(me_at, scaled, grads, feats):
     owners, rank, toks = scaled.shape
-    feats = grads[0].shape[1]
     steps = 4
     tile = feats // steps
     return pl.pallas_call(
@@ -198,11 +218,7 @@
         ),
         out_shape=jax.ShapeDtypeStruct((rank, feats), F32),
         compiler_params=params(),
-        cost_estimate=pl.CostEstimate(
-            flops=2 * rank * feats * toks * owners,
-            bytes_accessed=2 * owners * toks * feats,
-            transcendentals=0,
-        ),
+        cost_estimate=SMALL,
         name="second_grad",
     )(me_at, scaled, *grads)
 
@@ -253,6 +269,7 @@
         out_shape=[jax.ShapeDtypeStruct(shape, F32)]
         + [jax.ShapeDtypeStruct(shape, BF16)] * (cores - 1),
         compiler_params=params(),
+        cost_estimate=SMALL,
         name="first_grad",
     )(sub_at, idx_col, prob_col, low, hid)
 
@@ -305,6 +322,7 @@
         ],
         scratch_shapes=[pltpu.VMEM((len(back) * slots, units), BF16)],
         compiler_params=params(),
+        cost_estimate=SMALL,
         name="finish",
     )(idx_col, target, prob_col, low, hid, first_all, *back)
 
@@ -324,7 +342,6 @@
     width = owners * rank
     me = lax.axis_index(where).astype(jnp.int32)
     me_at = me.reshape(1)
-    rep_at = lax.axis_index("rep").astype(jnp.int32).reshape(1)
     sub_at = lax.axis_index("sub").astype(jnp.int32).reshape(1)
 
     def turn(x, offset):
@@ -337,62 +354,57 @@
         size = groups if axis == "ep" else cores if axis == "sub" else owners
         return lax.ppermute(x, axis, [(i, i ^ mask) for i in range(size)])
 
-    def gather_relative(x):
-        known, mask = [0], groups // 2
-        held = x[None]
-        while mask:
-            held = jnp.concatenate([held, flip(held, mask)])
-            known = known + [o ^ mask for o in known]
-            mask //= 2
-        held = jnp.concatenate([held, flip(held, 1, "sub")])
-        known = [2 * o for o in known] + [2 * o + 1 for o in known]
-        return jnp.stack([held[known.index(r)] for r in range(owners)])
-
     def exchange(x, axes=where):
         return lax.all_to_all(x, axes, split_axis=0, concat_axis=0, tiled=True)
 
-    index_all = gather_relative(jnp.pad(index.T.astype(BF16), ((0, 16 - top), (0, 0))))[:, :top]
-    blocks = {0: grad}
+    extra = units // 3
+    factor = first[0].T
+    routes = jnp.pad(
+        index.T.astype(BF16),
+        ((0, toks - 3 * rank - top), (0, extra - toks)),
+        constant_values=-1,
+    )
+    columns = jnp.concatenate([factor[:, k * extra : (k + 1) * extra] for k in range(3)] + [routes])
+    blocks = {0: jnp.concatenate([grad, columns], axis=1)}
     for o in sorted(range(1, groups), key=lambda o: (o.bit_count(), o)):
         last = o & -o
         blocks[o] = flip(blocks[o ^ last], last)
-    first_all = gather_relative(first[0].T)
-
-    mine = jnp.any(index_all.astype(jnp.int32) == me, axis=1)
-    before = jnp.triu(jnp.ones((toks, toks), BF16), 1)
-    pos = jnp.dot(mine.astype(BF16), before, preferred_element_type=F32).astype(jnp.int32)
-    pos = jnp.where(mine, pos, -1).reshape(owners, 1, toks)
-
-    back, grads, low_parts = [], [], []
+
+    at = jnp.stack([lax.axis_index("rep").astype(jnp.int32), me])
+    back, grads, low_parts, after = [], [], [], [[], []]
     for o in range(0, groups, 2):
         batch = [blocks[o], flip(blocks[o], 1, "sub"), blocks[o + 1], flip(blocks[o + 1], 1, "sub")]
         *give, keep, low = expert_rows_call(
-            rep_at, pos[2 * o : 2 * o + 4], batch, second[0], down[0], shares, slots
+            at, batch, second[0], down[0], shares, slots, after[-2]
         )
         parts = [keep] + [turn(x, k + 1) for k, x in enumerate(give)]
-        for k, rows in enumerate(share_sum_call(parts, 4)):
+        sums = share_sum_call(parts, 4)
+        for k, rows in enumerate(sums):
             r = 2 * o + k
             back.append(flip(rows, r, where) if r else rows)
         grads += batch
         low_parts.append(low)
+        after.append(sums[:1])
 
     hid = hidden.reshape(pairs, units)
     idx_col = index.reshape(pairs, 1)
     prob_col = weight.reshape(pairs, 1).astype(F32)
     hits = index[:, :, None] == jnp.arange(owners, dtype=jnp.int32)
     hit = jnp.any(hits, axis=1)
-    place = jnp.dot(before.T, hit.astype(BF16), preferred_element_type=F32).astype(jnp.int32)
+    before = jnp.tril(jnp.ones((toks, toks), BF16), -1)
+    place = jnp.dot(before, hit.astype(BF16), preferred_element_type=F32).astype(jnp.int32)
     place = place + slots * lax.bitwise_xor(me, jnp.arange(owners, dtype=jnp.int32))
     target = jnp.sum(jnp.where(hits, place[:, None, :], 0), axis=2).reshape(pairs, 1)
     prob_dense = jnp.sum(jnp.where(hits, weight[:, :, None].astype(F32), 0.0), axis=1)
 
-    first_all = place_call(me_at, [first_all]).reshape(width, units)
+    low_grad, first_all = collect_call(me_at, low_parts, grads, feats)
+    first_all = first_all.reshape(width, units)
     low_hid = over_rep(lowrank_hid_call(idx_col, hid, first_all, rank, top))
     scaled_hid = (low_hid * jnp.repeat(prob_dense, rank, axis=1)).astype(BF16)
     scaled_hid = exchange(scaled_hid.T.reshape(owners, rank, toks))
-    second_grad = second_grad_call(me_at, scaled_hid, grads)
-
-    low_grad = exchange(place_call(me_at, low_parts))
+    second_grad = second_grad_call(me_at, scaled_hid, grads, feats)
+
+    low_grad = exchange(low_grad)
     low_grad = over_rep(low_grad.reshape(width, toks).T.astype(F32))
 
     keep, give = first_grad_call(sub_at, idx_col, prob_col, low_grad, hid, rank, top, cores)

time: 284 us -> 248 us (0.87)
  starting transfers between devices: 70.8 us -> 51.2 us
  waiting for transfers between devices: 90.4 us -> 73.9 us
  blocking collectives: 0 us -> 12.5 us
  Pallas kernels: 57.8 us -> 50.8 us
  local copies, waits for them, and re-layouts: 52.3 us -> 46.1 us
    ppermute x39 -> x31, starting transfers between devices: 44.5 us -> 29.1 us  [flip(): return lax.ppermute(x, axis, [(i, i ^ mask) for i in range(size)])]
    all_to_all x0 -> x1, blocking collectives: none -> 12.5 us  [exchange(): return lax.all_to_all(x, axes, split_axis=0, concat_axis=0, tiled=True)]
    ppermute x39 -> x31, waiting for transfers between devices: 77.6 us -> 67 us  [flip(): return lax.ppermute(x, axis, [(i, i ^ mask) for i in range(size)])]
    unnamed x174 -> x112, local copies, waits for them, and re-layouts: 45.1 us -> 34.7 us
    ppermute x7, waiting for transfers between devices: 10.2 us -> 2.67 us  [turn(): lax.ppermute(x, 'rep', [(r, (r + offset) % shares) for r in range(shares)])]
    pallas_call x4, Pallas kernels: 32.7 us -> 28.3 us  [expert_rows_call(): pl.pallas_call(functools.partial(expert_rows_kernel, slots, tiles, shares...]
    all_to_all x3 -> x2, starting transfers between devices: 17.7 us -> 13.4 us  [exchange(): return lax.all_to_all(x, axes, split_axis=0, concat_axis=0, tiled=True)]
    pallas_call x4, Pallas kernels: 7.1 us -> 3.23 us  [share_sum_call(): pl.pallas_call(functools.partial(share_sum_kernel, len(parts)), out_shape...]
  transfers between devices with their start and end apart: 49 -> 40, of which waited for: 18 -> 13; matrix products, arithmetic and copies ran while one was open for 9% -> 7% of each run, Pallas kernels for 18% -> 17%
where the time goes in v3:
time: 248 us; the launch traced here: 246 us
  waiting for transfers between devices  73.9 us (30%)
  starting transfers between devices  51.2 us (21%)
  Pallas kernels  50.8 us (20%)
  local copies, waits for them, and re-layouts  46.1 us (19%)
  blocking collectives  12.5 us (5%)
  other arithmetic  9.86 us (4%)
    ppermute x31, waiting for transfers between devices, flip(): return lax.ppermute(x, axis, [(i, i ^ mask) for i in range(size)])  67 us
    unnamed x112, local copies, waits for them, and re-layouts  34.7 us
    ppermute x31, starting transfers between devices, flip(): return lax.ppermute(x, axis, [(i, i ^ mask) for i in range(size)])  29.1 us
    pallas_call x4, Pallas kernels, expert_rows_call(): pl.pallas_call(functools.partial(expert_rows_kernel, slots, tiles, shares...  28.3 us
    all_to_all x2, starting transfers between devices, exchange(): return lax.all_to_all(x, axes, split_axis=0, concat_axis=0, tiled=True)  13.4 us
    all_to_all x1, blocking collectives, exchange(): return lax.all_to_all(x, axes, split_axis=0, concat_axis=0, tiled=True)  12.5 us
    ppermute x7, starting transfers between devices, turn(): lax.ppermute(x, 'rep', [(r, (r + offset) % shares) for r in range(shares)])  8.64 us
    pallas_call x1, Pallas kernels, finish_call(): pl.pallas_call(functools.partial(finish_kernel, rank, top, len(back)), gr...  6.45 us
  transfers between devices with their start and end apart: 40, of which 13 were waited for; matrix products, arithmetic and copies ran while one was open for 7% of the time, Pallas kernels for 17%

profile of v3, /device:TPU:8, one launch (start us, length us, event | category | flops | bytes accessed | tf_op | source)
XLA Modules:
  0.0 245.7 jit_solution(13221265217904233205)
XLA Ops:
  2.1 1.1 fusion.5.rest_0_.refs_4_.refs_0_
  3.3 3.0 %collective-permute-start.7 = (bf16[128,2304]{1,0:T(8,128)(2,1)S(1)}, bf16[128,2304]{1,0:T(8,128)(2,1)}, u32[]{:S(2)}, u32[]{:S(2)}) collective-permute-start(bf16[128,2304]{1,0:T(8,128)(2,1)S(1)} %fusion.5.rest_0_.refs_4_.refs_0_), channel_id=1, source_target_pairs={{0,16},{4,20},{8,24},{12,28},{16,0},{20,4},{24,8},{28,12},{1,17},{... | collective-permute-start | bytes 1769480 | tf_op jit(solution)/shard_map/ppermute | solution.py:355
  6.3 1.5 collective-permute-start.1
  7.8 20.8 %collective-permute-done.3.rest_0_.refs_8_.refs_4_ = bf16[128,2304]{1,0:T(8,128)(2,1)S(1)} collective-permute-done((bf16[128,2304]{1,0:T(8,128)(2,1)S(1)}, bf16[128,2304]{1,0:T(8,128)(2,1)S(1)}, u32[]{:S(2)}, u32[]{:S(2)}) %collective-permute-start.3) | collective-permute-done | bytes 589856 | tf_op jit(solution)/shard_map/ppermute | solution.py:355
  28.7 1.7 collective-permute-start.5
  30.4 1.8 collective-permute-done.7.rest_0_.refs_12_.refs_8_
  32.2 1.6 collective-permute-start.12
  34.3 1.5 collective-permute-start.9
  35.8 9.2 %collective-permute-done.5.rest_2_.refs_10_.refs_6_ = bf16[128,2304]{1,0:T(8,128)(2,1)} collective-permute-done((bf16[128,2304]{1,0:T(8,128)(2,1)S(1)}, bf16[128,2304]{1,0:T(8,128)(2,1)}, u32[]{:S(2)}, u32[]{:S(2)}) %collective-permute-start.5) | collective-permute-done | bytes 589856 | tf_op jit(solution)/shard_map/ppermute | solution.py:355
  45.0 1.6 collective-permute-done.12.rest_0_.refs_16_.refs_12_
  46.7 1.5 collective-permute-start.14
  48.3 2.8 %copy-done = bf16[1,1536,2048]{2,1,0:T(8,128)(2,1)S(1)} copy-done((bf16[1,1536,2048]{2,1,0:T(8,128)(2,1)S(1)}, bf16[1,1536,2048]{2,1,0:T(8,128)(2,1)}, u32[]{:S(2)}) %copy-start) | copy-done | bytes 6291480
  51.0 6.9 %expert_rows.4 = (bf16[320,768]{1,0:T(8,128)(2,1)S(1)}, bf16[320,768]{1,0:T(8,128)(2,1)S(1)}, bf16[4,32,128]{2,1,0:T(8,128)(2,1)S(1)}) custom-call(s32[2]{0:T(128)S(1)} %pad_add_fusion.at_ref, bf16[128,2304]{1,0:T(8,128)(2,1)S(1)} %fusion.5.rest_0_.refs_4_.refs_0_, bf16[128,2304]{1,0:T(8,128)(2,1)S(1)} %collective-permute-done.rest_1_.refs_5_.refs_1_, ...), custom_call_target="tpu_custom_call" | custom-call | flops 1 | bytes 1 | tf_op jit(solution)/shard_map/expert_rows/pallas_call | solution.py:114
  58.0 1.6 collective-permute-start.11
  60.1 8.5 %collective-permute-done.14.rest_2_.refs_18_.refs_14_ = bf16[128,2304]{1,0:T(8,128)(2,1)} collective-permute-done((bf16[128,2304]{1,0:T(8,128)(2,1)}, bf16[128,2304]{1,0:T(8,128)(2,1)}, u32[]{:S(2)}, u32[]{:S(2)}) %collective-permute-start.14) | collective-permute-done | bytes 589856 | tf_op jit(solution)/shard_map/ppermute | solution.py:355
  68.6 7.0 %expert_rows.5 = (bf16[320,768]{1,0:T(8,128)(2,1)S(1)}, bf16[320,768]{1,0:T(8,128)(2,1)S(1)}, bf16[4,32,128]{2,1,0:T(8,128)(2,1)S(1)}) custom-call(s32[2]{0:T(128)S(1)} %pad_add_fusion.at_ref, bf16[128,2304]{1,0:T(8,128)(2,1)S(1)} %collective-permute-done.3.rest_0_.refs_8_.refs_4_, bf16[128,2304]{1,0:T(8,128)(2,1)} %collective-permute-done.4.rest_1_.refs_9_.refs_5_, ...), custom_call_target="tpu_custom_call" | custom-call | flops 1 | bytes 1 | tf_op jit(solution)/shard_map/expert_rows/pallas_call | solution.py:114
  75.6 1.4 collective-permute-start.16
  79.1 7.5 %expert_rows.6 = (bf16[320,768]{1,0:T(8,128)(2,1)}, bf16[320,768]{1,0:T(8,128)(2,1)S(1)}, bf16[4,32,128]{2,1,0:T(8,128)(2,1)S(1)}) custom-call(s32[2]{0:T(128)S(1)} %pad_add_fusion.at_ref, bf16[128,2304]{1,0:T(8,128)(2,1)} %collective-permute-done.7.rest_0_.refs_12_.refs_8_, bf16[128,2304]{1,0:T(8,128)(2,1)S(1)} %collective-permute-done.8.rest_1_.refs_13_.refs_9_, ...), custom_call_target="tpu_custom_call" | custom-call | flops 1 | bytes 1 | tf_op jit(solution)/shard_map/expert_rows/pallas_call | solution.py:114
  86.7 2.7 %collective-permute-done.16.refs_1_ = bf16[320,768]{1,0:T(8,128)(2,1)S(1)} collective-permute-done((bf16[320,768]{1,0:T(8,128)(2,1)S(1)}, bf16[320,768]{1,0:T(8,128)(2,1)S(1)}, u32[]{:S(2)}, u32[]{:S(2)}) %collective-permute-start.16) | collective-permute-done | bytes 491552 | tf_op jit(solution)/shard_map/ppermute | solution.py:348
  91.4 6.8 %expert_rows.7 = (bf16[320,768]{1,0:T(8,128)(2,1)S(1)}, bf16[320,768]{1,0:T(8,128)(2,1)S(1)}, bf16[4,32,128]{2,1,0:T(8,128)(2,1)S(1)}) custom-call(s32[2]{0:T(128)S(1)} %pad_add_fusion.at_ref, bf16[128,2304]{1,0:T(8,128)(2,1)} %collective-permute-done.12.rest_0_.refs_16_.refs_12_, bf16[128,2304]{1,0:T(8,128)(2,1)S(1)} %collective-permute-done.13.rest_1_.refs_17_.refs_13_, ...), custom_call_target="tpu_custom_call" | custom-call | flops 1 | bytes 1 | tf_op jit(solution)/shard_map/expert_rows/pallas_call | solution.py:114
  98.4 1.4 collect_blocks.1
  100.7 12.5 %all_to_all.15 = bf16[16,32,128]{2,1,0:T(8,128)(2,1)S(1)} all-to-all(bf16[16,32,128]{2,1,0:T(8,128)(2,1)S(1)} %get-tuple-element.48), channel_id=1, replica_groups=mesh['grp'=1,'ep'=8,'rep'=2,'sub'=2] {'ep','sub'}, dimensions={0} | all-to-all | bytes 262144 | tf_op jit(solution)/shard_map/all_to_all | solution.py:358
  113.3 1.6 collective-permute-start.17
  117.9 1.9 reshape.79.prob_ref
  119.8 1.1 copy-done.18
  120.9 2.7 %lowrank_hid.1 = f32[128,512]{1,0:T(8,128)} custom-call(s32[1024,1]{1,0:T(8,128)S(1)} %reshape.78.idx_ref, bf16[1024,768]{1,0:T(8,128)(2,1)S(1)} %bitcast.31, bf16[512,768]{1,0:T(8,128)(2,1)S(1)} %bitcast.34), custom_call_target="tpu_custom_call" | custom-call | flops 1 | bytes 1 | tf_op jit(solution)/shard_map/lowrank_hid/pallas_call | solution.py:53
  123.7 1.5 collective-permute-start.37
  125.2 1.1 bitcast_add_fusion.low_ref
  126.2 3.6 %first_grad.1 = (f32[8,32,768]{2,1,0:T(8,128)S(1)}, bf16[8,32,768]{2,1,0:T(8,128)(2,1)}) custom-call(s32[1]{0:T(128)} %bitcast.13.sub_ref, s32[1024,1]{1,0:T(8,128)S(1)} %reshape.78.idx_ref, f32[1024,1]{1,0:T(8,128)S(1)} %copy-done.15, f32[128,512]{1,0:T(8,128)S(1)} %bitcast_add_fusion.low_ref, bf16[1024,768]{1,0:T(8,128)(2,1)S(1)} %bitcast.32), custom_call_target="tpu_custom_call" | custom-call | flops 1 | bytes 1 | tf_op jit(solution)/shard_map/first_grad/pallas_call | solution.py:255
  131.5 1.8 copy.45
  136.1 1.1 share_sum.6
  140.5 1.8 fusion.6
  142.3 1.7 copy.46
  143.9 6.5 %all-to-all-start.2 = ((bf16[16,32,128]{2,1,0:T(8,128)(2,1)}), bf16[16,32,128]{2,1,0:T(8,128)(2,1)}, u32[]{:S(2)}, u32[]{:S(2)}) async-start(bf16[16,32,128]{2,1,0:T(8,128)(2,1)} %bitcast.42), calls=%async_computation.2 | async-start | bytes 262144 | tf_op jit(solution)/shard_map/all_to_all | solution.py:358
  150.5 2.5 %collective-permute-start.26 = (bf16[80,768]{1,0:T(8,128)(2,1)}, bf16[80,768]{1,0:T(8,128)(2,1)}, u32[]{:S(2)}, u32[]{:S(2)}) collective-permute-start(bf16[80,768]{1,0:T(8,128)(2,1)} %copy-done.51), channel_id=1, source_target_pairs={{0,16},{1,17},{4,20},{5,21},{8,24},{9,25},{12,28},{13,29},{16,0},{... | collective-permute-start | bytes 368648 | tf_op jit(solution)/shard_map/ppermute | solution.py:355
  153.0 2.1 add_convert_fusion
  155.1 4.2 %all-to-all-done.2.scaled_ref = bf16[16,32,128]{2,1,0:T(8,128)(2,1)} async-done(((bf16[16,32,128]{2,1,0:T(8,128)(2,1)}), bf16[16,32,128]{2,1,0:T(8,128)(2,1)}, u32[]{:S(2)}, u32[]{:S(2)}) %all-to-all-start.2) | async-done | bytes 131104 | tf_op jit(solution)/shard_map/all_to_all | solution.py:358
  159.3 6.9 %all-to-all-start.1 = ((bf16[8,32,768]{2,1,0:T(8,128)(2,1)}), bf16[8,32,768]{2,1,0:T(8,128)(2,1)}, u32[]{:S(2)}, u32[]{:S(2)}) async-start(bf16[8,32,768]{2,1,0:T(8,128)(2,1)} %add_convert_fusion), calls=%async_computation.1 | async-start | bytes 786432 | tf_op jit(solution)/shard_map/all_to_all | solution.py:358
  166.3 3.8 %collective-permute-start.28 = (bf16[80,768]{1,0:T(8,128)(2,1)}, bf16[80,768]{1,0:T(8,128)(2,1)S(1)}, u32[]{:S(2)}, u32[]{:S(2)}) collective-permute-start(bf16[80,768]{1,0:T(8,128)(2,1)} %copy-done.49), channel_id=1, source_target_pairs={{0,20},{1,21},{4,16},{5,17},{8,28},{9,29},{12,24},{13,25},{16,4},{... | collective-permute-start | bytes 368648 | tf_op jit(solution)/shard_map/ppermute | solution.py:355
  170.1 1.7 collective-permute-start.22
  171.9 1.5 collective-permute-start.23
  174.4 1.9 share_sum.7
  176.2 7.0 %collective-permute-done.28.rest_10_ = bf16[80,768]{1,0:T(8,128)(2,1)S(1)} collective-permute-done((bf16[80,768]{1,0:T(8,128)(2,1)}, bf16[80,768]{1,0:T(8,128)(2,1)S(1)}, u32[]{:S(2)}, u32[]{:S(2)}) %collective-permute-start.28) | collective-permute-done | bytes 122912 | tf_op jit(solution)/shard_map/ppermute | solution.py:355
  183.8 1.8 collective-permute-done.29.rest_11_
  186.3 2.3 collective-permute-start.31
  189.3 2.4 collective-permute-start.32
  194.9 1.8 reshape.77.target_ref
  196.8 3.3 %collective-permute-done.31.rest_12_ = bf16[80,768]{1,0:T(8,128)(2,1)} collective-permute-done((bf16[80,768]{1,0:T(8,128)(2,1)}, bf16[80,768]{1,0:T(8,128)(2,1)}, u32[]{:S(2)}, u32[]{:S(2)}) %collective-permute-start.31) | collective-permute-done | bytes 122912 | tf_op jit(solution)/shard_map/ppermute | solution.py:355
  200.0 7.3 %collective-permute-done.32.rest_13_ = bf16[80,768]{1,0:T(8,128)(2,1)} collective-permute-done((bf16[80,768]{1,0:T(8,128)(2,1)}, bf16[80,768]{1,0:T(8,128)(2,1)}, u32[]{:S(2)}, u32[]{:S(2)}) %collective-permute-start.32) | collective-permute-done | bytes 122912 | tf_op jit(solution)/shard_map/ppermute | solution.py:355
  207.4 2.0 collective-permute-done.33.rest_14_
  209.4 3.6 %collective-permute-done.34.rest_15_ = bf16[80,768]{1,0:T(8,128)(2,1)} collective-permute-done((bf16[80,768]{1,0:T(8,128)(2,1)}, bf16[80,768]{1,0:T(8,128)(2,1)}, u32[]{:S(2)}, u32[]{:S(2)}) %collective-permute-start.34) | collective-permute-done | bytes 122912 | tf_op jit(solution)/shard_map/ppermute | solution.py:355
  213.0 1.0 copy-done.16
  214.0 1.1 copy-done.19
  221.6 6.5 %finish.1 = (bf16[1024,768]{1,0:T(8,128)(2,1)}, f32[1024,1]{1,0:T(8,128)S(1)}) custom-call(s32[1024,1]{1,0:T(8,128)S(1)} %reshape.78.idx_ref, s32[1024,1]{1,0:T(8,128)S(1)} %copy-done.21, f32[1024,1]{1,0:T(8,128)S(1)} %copy-done.16, f32[128,512]{1,0:T(8,128)S(1)} %bitcast_add_fusion.low_ref, bf16[1024,768]{1,0:T(8,128)(2,1)S(1)} %bitcast.33, ...), custom_call_target="tpu_custom_call" | custom-call | flops 1 | bytes 1 | tf_op jit(solution)/shard_map/finish/pallas_call | solution.py:303
  228.9 1.2 reduce
  230.3 1.6 collective-permute-start.35
  231.8 1.1 copy-done.4
  232.9 1.1 copy-done.6
  233.9 1.1 copy-done.8
  235.0 1.1 copy-done.10
  236.1 1.1 copy-done.12
  237.1 1.1 copy-done.14
  238.2 5.1 %second_grad.1 = f32[32,2048]{1,0:T(8,128)} custom-call(s32[1]{0:T(128)} %bitcast.me_ref, bf16[16,32,128]{2,1,0:T(8,128)(2,1)} %all-to-all-done.2.scaled_ref, bf16[128,2304]{1,0:T(8,128)(2,1)S(1)} %fusion.5.rest_0_.refs_4_.refs_0_, bf16[128,2304]{1,0:T(8,128)(2,1)S(1)} %copy-done.6, bf16[128,2304]{1,0:T(8,128)(2,1)S(1)} %copy-done.4, ...), custom_call_target="tpu_custom_call" | custom-call | flops 1 | bytes 1 | tf_op jit(solution)/shard_map/second_grad/pallas_call | solution.py:210
  244.0 1.7 convert_reduce_fusion
  (170 shorter events, 33.1 us)
Async XLA Ops:
  0.6 47.6 %copy-start.20 = (bf16[1,32,2048]{2,1,0:T(8,128)(2,1)S(1)}, bf16[1,32,2048]{2,1,0:T(8,128)(2,1)}, u32[]{:S(2)}) copy-start(bf16[1,32,2048]{2,1,0:T(8,128)(2,1)} %param.13) | copy-start | bytes 393220
  3.2 25.5 %collective-permute-start.3 = (bf16[128,2304]{1,0:T(8,128)(2,1)S(1)}, bf16[128,2304]{1,0:T(8,128)(2,1)S(1)}, u32[]{:S(2)}, u32[]{:S(2)}) collective-permute-start(bf16[128,2304]{1,0:T(8,128)(2,1)S(1)} %fusion.5.rest_0_.refs_4_.refs_0_), channel_id=1, source_target_pairs={{0,8},{4,12},{8,0},{12,4},{16,24},{20,28},{24,16},{28,20},{1,9},{5... | collective-permute-start | bytes 1769480 | tf_op jit(solution)/shard_map/ppermute | solution.py:355
  3.3 28.9 %collective-permute-start.7 = (bf16[128,2304]{1,0:T(8,128)(2,1)S(1)}, bf16[128,2304]{1,0:T(8,128)(2,1)}, u32[]{:S(2)}, u32[]{:S(2)}) collective-permute-start(bf16[128,2304]{1,0:T(8,128)(2,1)S(1)} %fusion.5.rest_0_.refs_4_.refs_0_), channel_id=1, source_target_pairs={{0,16},{4,20},{8,24},{12,28},{16,0},{20,4},{24,8},{28,12},{1,17},{... | collective-permute-start | bytes 1769480 | tf_op jit(solution)/shard_map/ppermute | solution.py:355
  6.3 27.5 %collective-permute-start.1 = (bf16[128,2304]{1,0:T(8,128)(2,1)S(1)}, bf16[128,2304]{1,0:T(8,128)(2,1)S(1)}, u32[]{:S(2)}, u32[]{:S(2)}) collective-permute-start(bf16[128,2304]{1,0:T(8,128)(2,1)S(1)} %fusion.5.rest_0_.refs_4_.refs_0_), channel_id=1, source_target_pairs={{0,4},{4,0},{8,12},{12,8},{16,20},{20,16},{24,28},{28,24},{1,5},{5... | collective-permute-start | bytes 1769480 | tf_op jit(solution)/shard_map/ppermute | solution.py:355
  7.8 26.5 %collective-permute-start = (bf16[128,2304]{1,0:T(8,128)(2,1)S(1)}, bf16[128,2304]{1,0:T(8,128)(2,1)S(1)}, u32[]{:S(2)}, u32[]{:S(2)}) collective-permute-start(bf16[128,2304]{1,0:T(8,128)(2,1)S(1)} %fusion.5.rest_0_.refs_4_.refs_0_), channel_id=1, source_target_pairs={{0,1},{1,0},{2,3},{3,2},{4,5},{5,4},{6,7},{7,6},{8,9},{9,8},{10,11... | collective-permute-start | bytes 1769480 | tf_op jit(solution)/shard_map/ppermute | solution.py:355
  28.7 16.4 %collective-permute-start.5 = (bf16[128,2304]{1,0:T(8,128)(2,1)S(1)}, bf16[128,2304]{1,0:T(8,128)(2,1)}, u32[]{:S(2)}, u32[]{:S(2)}) collective-permute-start(bf16[128,2304]{1,0:T(8,128)(2,1)S(1)} %collective-permute-done.3.rest_0_.refs_8_.refs_4_), channel_id=1, source_target_pairs={{0,4},{4,0},{8,12},{12,8},{16,20},{20,16},{24,28},{28,24},{1,5},{5... | collective-permute-start | bytes 1769480 | tf_op jit(solution)/shard_map/ppermute | solution.py:355
  32.2 14.5 %collective-permute-start.12 = (bf16[128,2304]{1,0:T(8,128)(2,1)}, bf16[128,2304]{1,0:T(8,128)(2,1)}, u32[]{:S(2)}, u32[]{:S(2)}) collective-permute-start(bf16[128,2304]{1,0:T(8,128)(2,1)} %collective-permute-done.7.rest_0_.refs_12_.refs_8_), channel_id=1, source_target_pairs={{0,8},{4,12},{8,0},{12,4},{16,24},{20,28},{24,16},{28,20},{1,9},{5... | collective-permute-start | bytes 1769480 | tf_op jit(solution)/shard_map/ppermute | solution.py:355
  33.8 64.5 %copy-start.3 = (bf16[128,2304]{1,0:T(8,128)(2,1)}, bf16[128,2304]{1,0:T(8,128)(2,1)S(1)}, u32[]{:S(2)}) copy-start(bf16[128,2304]{1,0:T(8,128)(2,1)S(1)} %collective-permute-done.1.rest_2_.refs_6_.refs_2_) | copy-start | bytes 1769476
  33.8 14.5 %collective-permute-start.2 = (bf16[128,2304]{1,0:T(8,128)(2,1)S(1)}, bf16[128,2304]{1,0:T(8,128)(2,1)}, u32[]{:S(2)}, u32[]{:S(2)}) collective-permute-start(bf16[128,2304]{1,0:T(8,128)(2,1)S(1)} %collective-permute-done.1.rest_2_.refs_6_.refs_2_), channel_id=1, source_target_pairs={{0,1},{1,0},{2,3},{3,2},{4,5},{5,4},{6,7},{7,6},{8,9},{9,8},{10,11... | collective-permute-start | bytes 1769480 | tf_op jit(solution)/shard_map/ppermute | solution.py:355
  33.8 25.7 %collective-permute-start.4 = (bf16[128,2304]{1,0:T(8,128)(2,1)S(1)}, bf16[128,2304]{1,0:T(8,128)(2,1)}, u32[]{:S(2)}, u32[]{:S(2)}) collective-permute-start(bf16[128,2304]{1,0:T(8,128)(2,1)S(1)} %collective-permute-done.3.rest_0_.refs_8_.refs_4_), channel_id=1, source_target_pairs={{0,1},{1,0},{2,3},{3,2},{4,5},{5,4},{6,7},{7,6},{8,9},{9,8},{10,11... | collective-permute-start | bytes 1769480 | tf_op jit(solution)/shard_map/ppermute | solution.py:355
  34.3 64.0 %copy-start.5 = (bf16[128,2304]{1,0:T(8,128)(2,1)}, bf16[128,2304]{1,0:T(8,128)(2,1)S(1)}, u32[]{:S(2)}) copy-start(bf16[128,2304]{1,0:T(8,128)(2,1)S(1)} %collective-permute-done.rest_1_.refs_5_.refs_1_) | copy-start | bytes 1769476
  34.3 25.2 %collective-permute-start.9 = (bf16[128,2304]{1,0:T(8,128)(2,1)}, bf16[128,2304]{1,0:T(8,128)(2,1)}, u32[]{:S(2)}, u32[]{:S(2)}) collective-permute-start(bf16[128,2304]{1,0:T(8,128)(2,1)} %collective-permute-done.7.rest_0_.refs_12_.refs_8_), channel_id=1, source_target_pairs={{0,4},{4,0},{8,12},{12,8},{16,20},{20,16},{24,28},{28,24},{1,5},{5... | collective-permute-start | bytes 1769480 | tf_op jit(solution)/shard_map/ppermute | solution.py:355
  45.0 15.0 %collective-permute-start.6 = (bf16[128,2304]{1,0:T(8,128)(2,1)}, bf16[128,2304]{1,0:T(8,128)(2,1)}, u32[]{:S(2)}, u32[]{:S(2)}) collective-permute-start(bf16[128,2304]{1,0:T(8,128)(2,1)} %collective-permute-done.5.rest_2_.refs_10_.refs_6_), channel_id=1, source_target_pairs={{0,1},{1,0},{2,3},{3,2},{4,5},{5,4},{6,7},{7,6},{8,9},{9,8},{10,11... | collective-permute-start | bytes 1769480 | tf_op jit(solution)/shard_map/ppermute | solution.py:355
  46.7 21.9 %collective-permute-start.14 = (bf16[128,2304]{1,0:T(8,128)(2,1)}, bf16[128,2304]{1,0:T(8,128)(2,1)}, u32[]{:S(2)}, u32[]{:S(2)}) collective-permute-start(bf16[128,2304]{1,0:T(8,128)(2,1)} %collective-permute-done.12.rest_0_.refs_16_.refs_12_), channel_id=1, source_target_pairs={{0,4},{4,0},{8,12},{12,8},{16,20},{20,16},{24,28},{28,24},{1,5},{5... | collective-permute-start | bytes 1769480 | tf_op jit(solution)/shard_map/ppermute | solution.py:355
  48.3 2.8 %copy-start = (bf16[1,1536,2048]{2,1,0:T(8,128)(2,1)S(1)}, bf16[1,1536,2048]{2,1,0:T(8,128)(2,1)}, u32[]{:S(2)}) copy-start(bf16[1,1536,2048]{2,1,0:T(8,128)(2,1)} %param.11) | copy-start | bytes 18874372
  51.0 17.5 %copy-start.1 = (bf16[1,1536,2048]{2,1,0:T(8,128)(2,1)S(1)}, bf16[1,1536,2048]{2,1,0:T(8,128)(2,1)}, u32[]{:S(2)}) copy-start(bf16[1,1536,2048]{2,1,0:T(8,128)(2,1)} %param.11) | copy-start | bytes 18874372
  58.0 17.7 %collective-permute-start.11 = (bf16[320,768]{1,0:T(8,128)(2,1)S(1)}, bf16[320,768]{1,0:T(8,128)(2,1)S(1)}, u32[]{:S(2)}, u32[]{:S(2)}) collective-permute-start(bf16[320,768]{1,0:T(8,128)(2,1)S(1)} %get-tuple-element.41), channel_id=1, source_target_pairs={{0,2},{2,0},{1,3},{3,1},{4,6},{6,4},{5,7},{7,5},{8,10},{10,8},{9,1... | collective-permute-start | bytes 1474568 | tf_op jit(solution)/shard_map/ppermute | solution.py:348
  59.5 19.6 %collective-permute-start.8 = (bf16[128,2304]{1,0:T(8,128)(2,1)}, bf16[128,2304]{1,0:T(8,128)(2,1)S(1)}, u32[]{:S(2)}, u32[]{:S(2)}) collective-permute-start(bf16[128,2304]{1,0:T(8,128)(2,1)} %collective-permute-done.7.rest_0_.refs_12_.refs_8_), channel_id=1, source_target_pairs={{0,1},{1,0},{2,3},{3,2},{4,5},{5,4},{6,7},{7,6},{8,9},{9,8},{10,11... | collective-permute-start | bytes 1769480 | tf_op jit(solution)/shard_map/ppermute | solution.py:355
  59.5 19.6 %collective-permute-start.10 = (bf16[128,2304]{1,0:T(8,128)(2,1)}, bf16[128,2304]{1,0:T(8,128)(2,1)S(1)}, u32[]{:S(2)}, u32[]{:S(2)}) collective-permute-start(bf16[128,2304]{1,0:T(8,128)(2,1)} %collective-permute-done.9.rest_2_.refs_14_.refs_10_), channel_id=1, source_target_pairs={{0,1},{1,0},{2,3},{3,2},{4,5},{5,4},{6,7},{7,6},{8,9},{9,8},{10,11... | collective-permute-start | bytes 1769480 | tf_op jit(solution)/shard_map/ppermute | solution.py:355
  60.0 31.4 %collective-permute-start.13 = (bf16[128,2304]{1,0:T(8,128)(2,1)}, bf16[128,2304]{1,0:T(8,128)(2,1)S(1)}, u32[]{:S(2)}, u32[]{:S(2)}) collective-permute-start(bf16[128,2304]{1,0:T(8,128)(2,1)} %collective-permute-done.12.rest_0_.refs_16_.refs_12_), channel_id=1, source_target_pairs={{0,1},{1,0},{2,3},{3,2},{4,5},{5,4},{6,7},{7,6},{8,9},{9,8},{10,11... | collective-permute-start | bytes 1769480 | tf_op jit(solution)/shard_map/ppermute | solution.py:355
  68.6 22.8 %collective-permute-start.15 = (bf16[128,2304]{1,0:T(8,128)(2,1)}, bf16[128,2304]{1,0:T(8,128)(2,1)S(1)}, u32[]{:S(2)}, u32[]{:S(2)}) collective-permute-start(bf16[128,2304]{1,0:T(8,128)(2,1)} %collective-permute-done.14.rest_2_.refs_18_.refs_14_), channel_id=1, source_target_pairs={{0,1},{1,0},{2,3},{3,2},{4,5},{5,4},{6,7},{7,6},{8,9},{9,8},{10,11... | collective-permute-start | bytes 1769480 | tf_op jit(solution)/shard_map/ppermute | solution.py:355
  75.6 13.7 %collective-permute-start.16 = (bf16[320,768]{1,0:T(8,128)(2,1)S(1)}, bf16[320,768]{1,0:T(8,128)(2,1)S(1)}, u32[]{:S(2)}, u32[]{:S(2)}) collective-permute-start(bf16[320,768]{1,0:T(8,128)(2,1)S(1)} %get-tuple-element.45), channel_id=1, source_target_pairs={{0,2},{2,0},{1,3},{3,1},{4,6},{6,4},{5,7},{7,5},{8,10},{10,8},{9,1... | collective-permute-start | bytes 1474568 | tf_op jit(solution)/shard_map/ppermute | solution.py:348
  79.1 7.6 %copy-start.28 = (bf16[80,768]{1,0:T(8,128)(2,1)}, bf16[80,768]{1,0:T(8,128)(2,1)S(1)}, u32[]{:S(2)}) copy-start(bf16[80,768]{1,0:T(8,128)(2,1)S(1)} %get-tuple-element.42.rest_6_.rest_0_) | copy-start | bytes 368644
  79.1 19.2 %copy-start.7 = (bf16[128,2304]{1,0:T(8,128)(2,1)}, bf16[128,2304]{1,0:T(8,128)(2,1)S(1)}, u32[]{:S(2)}) copy-start(bf16[128,2304]{1,0:T(8,128)(2,1)S(1)} %collective-permute-done.8.rest_1_.refs_13_.refs_9_) | copy-start | bytes 1769476
  79.1 19.2 %copy-start.9 = (bf16[128,2304]{1,0:T(8,128)(2,1)}, bf16[128,2304]{1,0:T(8,128)(2,1)S(1)}, u32[]{:S(2)}) copy-start(bf16[128,2304]{1,0:T(8,128)(2,1)S(1)} %collective-permute-done.10.rest_3_.refs_15_.refs_11_) | copy-start | bytes 1769476
  86.7 4.7 %copy-start.26 = (bf16[320,768]{1,0:T(8,128)(2,1)}, bf16[320,768]{1,0:T(8,128)(2,1)S(1)}, u32[]{:S(2)}) copy-start(bf16[320,768]{1,0:T(8,128)(2,1)S(1)} %get-tuple-element.56.refs_0_) | copy-start | bytes 1474564
  91.4 6.9 %copy-start.40 = (bf16[80,768]{1,0:T(8,128)(2,1)}, bf16[80,768]{1,0:T(8,128)(2,1)S(1)}, u32[]{:S(2)}) copy-start(bf16[80,768]{1,0:T(8,128)(2,1)S(1)} %get-tuple-element.46.rest_6_) | copy-start | bytes 368644
  91.4 6.9 %copy-start.11 = (bf16[128,2304]{1,0:T(8,128)(2,1)}, bf16[128,2304]{1,0:T(8,128)(2,1)S(1)}, u32[]{:S(2)}) copy-start(bf16[128,2304]{1,0:T(8,128)(2,1)S(1)} %collective-permute-done.13.rest_1_.refs_17_.refs_13_) | copy-start | bytes 1769476
  91.4 6.9 %copy-start.13 = (bf16[128,2304]{1,0:T(8,128)(2,1)}, bf16[128,2304]{1,0:T(8,128)(2,1)S(1)}, u32[]{:S(2)}) copy-start(bf16[128,2304]{1,0:T(8,128)(2,1)S(1)} %collective-permute-done.15.rest_3_.refs_19_.refs_15_) | copy-start | bytes 1769476
  98.3 1.5 copy-start.24
  98.3 1.5 copy-start.41
  100.7 14.8 %copy-start.53 = (s32[128,8]{0,1:T(8,128)S(1)}, s32[128,8]{0,1:T(8,128)}, u32[]{:S(2)}) copy-start(s32[128,8]{0,1:T(8,128)} %param.9) | copy-start | bytes 12292
  100.7 16.5 %copy-start.54 = (bf16[128,8]{0,1:T(8,128)(2,1)S(1)}, bf16[128,8]{0,1:T(8,128)(2,1)}, u32[]{:S(2)}) copy-start(bf16[128,8]{0,1:T(8,128)(2,1)} %param.10) | copy-start | bytes 6148
  113.2 6.7 %copy-start.2 = (bf16[128,8,768]{2,1,0:T(8,128)(2,1)S(1)}, bf16[128,8,768]{2,1,0:T(8,128)(2,1)}, u32[]{:S(2)}) copy-start(bf16[128,8,768]{2,1,0:T(8,128)(2,1)} %param.8) | copy-start | bytes 4718596
  113.3 10.4 %copy-start.52 = (f32[512,128]{0,1:T(8,128)}, f32[512,128]{0,1:T(8,128)S(1)}, u32[]{:S(2)}) copy-start(f32[512,128]{0,1:T(8,128)S(1)} %copy.38) | copy-start | bytes 786436
  113.3 11.8 %collective-permute-start.17 = (f32[128,512]{1,0:T(8,128)S(1)}, f32[128,512]{1,0:T(8,128)}, u32[]{:S(2)}, u32[]{:S(2)}) collective-permute-start(f32[128,512]{1,0:T(8,128)S(1)} %bitcast.40), channel_id=1, source_target_pairs={{0,2},{2,0},{1,3},{3,1},{4,6},{6,4},{5,7},{7,5},{8,10},{10,8},{9,1... | collective-permute-start | bytes 786440 | tf_op jit(solution)/shard_map/ppermute | solution.py:348
  114.9 19.8 %collective-permute-start.25 = (bf16[320,768]{1,0:T(8,128)(2,1)}, bf16[320,768]{1,0:T(8,128)(2,1)}, u32[]{:S(2)}, u32[]{:S(2)}) collective-permute-start(bf16[320,768]{1,0:T(8,128)(2,1)} %get-tuple-element.57), channel_id=1, source_target_pairs={{0,2},{2,0},{1,3},{3,1},{4,6},{6,4},{5,7},{7,5},{8,10},{10,8},{9,1... | collective-permute-start | bytes 1474568 | tf_op jit(solution)/shard_map/ppermute | solution.py:348
  119.8 1.1 copy-start.18
  120.9 5.3 %copy-start.15 = (f32[1024,1]{1,0:T(8,128)S(1)}, f32[1024,1]{1,0:T(8,128)}, u32[]{:S(2)}) copy-start(f32[1024,1]{1,0:T(8,128)} %reshape.79.prob_ref) | copy-start | bytes 12292
  123.7 16.2 %collective-permute-start.37 = (f32[128,512]{1,0:T(8,128)}, f32[128,512]{1,0:T(8,128)}, u32[]{:S(2)}, u32[]{:S(2)}) collective-permute-start(f32[128,512]{1,0:T(8,128)} %lowrank_hid.1), channel_id=1, source_target_pairs={{0,2},{2,0},{1,3},{3,1},{4,6},{6,4},{5,7},{7,5},{8,10},{10,8},{9,1... | collective-permute-start | bytes 786440 | tf_op jit(solution)/shard_map/ppermute | solution.py:348
  130.7 22.3 %collective-permute-start.36 = (bf16[8,32,768]{2,1,0:T(8,128)(2,1)}, bf16[8,32,768]{2,1,0:T(8,128)(2,1)}, u32[]{:S(2)}, u32[]{:S(2)}) collective-permute-start(bf16[8,32,768]{2,1,0:T(8,128)(2,1)} %get-tuple-element.71), channel_id=1, source_target_pairs={{0,1},{1,0},{2,3},{3,2},{4,5},{5,4},{6,7},{7,6},{8,9},{9,8},{10,11... | collective-permute-start | bytes 1179656 | tf_op jit(solution)/shard_map/ppermute | solution.py:355
  133.3 17.2 %collective-permute-start.18 = (bf16[80,768]{1,0:T(8,128)(2,1)}, bf16[80,768]{1,0:T(8,128)(2,1)}, u32[]{:S(2)}, u32[]{:S(2)}) collective-permute-start(bf16[80,768]{1,0:T(8,128)(2,1)} %copy-done.47), channel_id=1, source_target_pairs={{0,1},{1,0},{4,5},{5,4},{8,9},{9,8},{12,13},{13,12},{16,17},{17,16... | collective-permute-start | bytes 368648 | tf_op jit(solution)/shard_map/ppermute | solution.py:355
  133.8 32.5 %collective-permute-start.19 = (bf16[80,768]{1,0:T(8,128)(2,1)}, bf16[80,768]{1,0:T(8,128)(2,1)}, u32[]{:S(2)}, u32[]{:S(2)}) collective-permute-start(bf16[80,768]{1,0:T(8,128)(2,1)} %copy-done.46), channel_id=1, source_target_pairs={{0,4},{1,5},{4,0},{5,1},{8,12},{9,13},{12,8},{13,9},{16,20},{17,21... | collective-permute-start | bytes 368648 | tf_op jit(solution)/shard_map/ppermute | solution.py:355
  134.7 31.6 %collective-permute-start.20 = (bf16[80,768]{1,0:T(8,128)(2,1)}, bf16[80,768]{1,0:T(8,128)(2,1)}, u32[]{:S(2)}, u32[]{:S(2)}) collective-permute-start(bf16[80,768]{1,0:T(8,128)(2,1)} %copy-done.45), channel_id=1, source_target_pairs={{0,5},{1,4},{4,1},{5,0},{8,13},{9,12},{12,9},{13,8},{16,21},{17,20... | collective-permute-start | bytes 368648 | tf_op jit(solution)/shard_map/ppermute | solution.py:355
  139.9 31.9 %collective-permute-start.30 = (bf16[320,768]{1,0:T(8,128)(2,1)}, bf16[320,768]{1,0:T(8,128)(2,1)}, u32[]{:S(2)}, u32[]{:S(2)}) collective-permute-start(bf16[320,768]{1,0:T(8,128)(2,1)} %copy-done.41), channel_id=1, source_target_pairs={{0,2},{2,0},{1,3},{3,1},{4,6},{6,4},{5,7},{7,5},{8,10},{10,8},{9,1... | collective-permute-start | bytes 1474568 | tf_op jit(solution)/shard_map/ppermute | solution.py:348
  143.9 15.3 %all-to-all-start.2 = ((bf16[16,32,128]{2,1,0:T(8,128)(2,1)}), bf16[16,32,128]{2,1,0:T(8,128)(2,1)}, u32[]{:S(2)}, u32[]{:S(2)}) async-start(bf16[16,32,128]{2,1,0:T(8,128)(2,1)} %bitcast.42), calls=%async_computation.2 | async-start | bytes 262144 | tf_op jit(solution)/shard_map/all_to_all | solution.py:358
  150.5 19.6 %collective-permute-start.26 = (bf16[80,768]{1,0:T(8,128)(2,1)}, bf16[80,768]{1,0:T(8,128)(2,1)}, u32[]{:S(2)}, u32[]{:S(2)}) collective-permute-start(bf16[80,768]{1,0:T(8,128)(2,1)} %copy-done.51), channel_id=1, source_target_pairs={{0,16},{1,17},{4,20},{5,21},{8,24},{9,25},{12,28},{13,29},{16,0},{... | collective-permute-start | bytes 368648 | tf_op jit(solution)/shard_map/ppermute | solution.py:355
  153.0 17.1 %collective-permute-start.27 = (bf16[80,768]{1,0:T(8,128)(2,1)}, bf16[80,768]{1,0:T(8,128)(2,1)}, u32[]{:S(2)}, u32[]{:S(2)}) collective-permute-start(bf16[80,768]{1,0:T(8,128)(2,1)} %copy-done.50), channel_id=1, source_target_pairs={{0,17},{1,16},{4,21},{5,20},{8,25},{9,24},{12,29},{13,28},{16,1},{... | collective-permute-start | bytes 368648 | tf_op jit(solution)/shard_map/ppermute | solution.py:355
  159.3 84.7 %all-to-all-start.1 = ((bf16[8,32,768]{2,1,0:T(8,128)(2,1)}), bf16[8,32,768]{2,1,0:T(8,128)(2,1)}, u32[]{:S(2)}, u32[]{:S(2)}) async-start(bf16[8,32,768]{2,1,0:T(8,128)(2,1)} %add_convert_fusion), calls=%async_computation.1 | async-start | bytes 786432 | tf_op jit(solution)/shard_map/all_to_all | solution.py:358
  166.2 22.4 %collective-permute-start.21 = (bf16[80,768]{1,0:T(8,128)(2,1)}, bf16[80,768]{1,0:T(8,128)(2,1)S(1)}, u32[]{:S(2)}, u32[]{:S(2)}) collective-permute-start(bf16[80,768]{1,0:T(8,128)(2,1)} %copy-done.40), channel_id=1, source_target_pairs={{0,8},{1,9},{4,12},{5,13},{8,0},{9,1},{12,4},{13,5},{16,24},{17,25... | collective-permute-start | bytes 368648 | tf_op jit(solution)/shard_map/ppermute | solution.py:355
  166.3 16.9 %collective-permute-start.28 = (bf16[80,768]{1,0:T(8,128)(2,1)}, bf16[80,768]{1,0:T(8,128)(2,1)S(1)}, u32[]{:S(2)}, u32[]{:S(2)}) collective-permute-start(bf16[80,768]{1,0:T(8,128)(2,1)} %copy-done.49), channel_id=1, source_target_pairs={{0,20},{1,21},{4,16},{5,17},{8,28},{9,29},{12,24},{13,25},{16,4},{... | collective-permute-start | bytes 368648 | tf_op jit(solution)/shard_map/ppermute | solution.py:355
  170.1 15.5 %collective-permute-start.29 = (bf16[80,768]{1,0:T(8,128)(2,1)}, bf16[80,768]{1,0:T(8,128)(2,1)S(1)}, u32[]{:S(2)}, u32[]{:S(2)}) collective-permute-start(bf16[80,768]{1,0:T(8,128)(2,1)} %copy-done.48), channel_id=1, source_target_pairs={{0,21},{1,20},{4,17},{5,16},{8,29},{9,28},{12,25},{13,24},{16,5},{... | collective-permute-start | bytes 368648 | tf_op jit(solution)/shard_map/ppermute | solution.py:355
  170.1 21.5 %collective-permute-start.22 = (bf16[80,768]{1,0:T(8,128)(2,1)}, bf16[80,768]{1,0:T(8,128)(2,1)S(1)}, u32[]{:S(2)}, u32[]{:S(2)}) collective-permute-start(bf16[80,768]{1,0:T(8,128)(2,1)} %copy-done.44), channel_id=1, source_target_pairs={{0,9},{1,8},{4,13},{5,12},{8,1},{9,0},{12,5},{13,4},{16,25},{17,24... | collective-permute-start | bytes 368648 | tf_op jit(solution)/shard_map/ppermute | solution.py:355
  171.9 21.4 %collective-permute-start.23 = (bf16[80,768]{1,0:T(8,128)(2,1)}, bf16[80,768]{1,0:T(8,128)(2,1)S(1)}, u32[]{:S(2)}, u32[]{:S(2)}) collective-permute-start(bf16[80,768]{1,0:T(8,128)(2,1)} %copy-done.43), channel_id=1, source_target_pairs={{0,12},{1,13},{4,8},{5,9},{8,4},{9,5},{12,0},{13,1},{16,28},{17,29... | collective-permute-start | bytes 368648 | tf_op jit(solution)/shard_map/ppermute | solution.py:355
  183.8 12.9 %collective-permute-start.24 = (bf16[80,768]{1,0:T(8,128)(2,1)}, bf16[80,768]{1,0:T(8,128)(2,1)}, u32[]{:S(2)}, u32[]{:S(2)}) collective-permute-start(bf16[80,768]{1,0:T(8,128)(2,1)} %copy-done.42), channel_id=1, source_target_pairs={{0,13},{1,12},{4,9},{5,8},{8,5},{9,4},{12,1},{13,0},{16,29},{17,28... | collective-permute-start | bytes 368648 | tf_op jit(solution)/shard_map/ppermute | solution.py:355
  186.3 13.7 %collective-permute-start.31 = (bf16[80,768]{1,0:T(8,128)(2,1)}, bf16[80,768]{1,0:T(8,128)(2,1)}, u32[]{:S(2)}, u32[]{:S(2)}) collective-permute-start(bf16[80,768]{1,0:T(8,128)(2,1)} %get-tuple-element.64), channel_id=1, source_target_pairs={{0,24},{1,25},{4,28},{5,29},{8,16},{9,17},{12,20},{13,21},{16,8},{... | collective-permute-start | bytes 368648 | tf_op jit(solution)/shard_map/ppermute | solution.py:355
  189.3 18.1 %collective-permute-start.32 = (bf16[80,768]{1,0:T(8,128)(2,1)}, bf16[80,768]{1,0:T(8,128)(2,1)}, u32[]{:S(2)}, u32[]{:S(2)}) collective-permute-start(bf16[80,768]{1,0:T(8,128)(2,1)} %get-tuple-element.65), channel_id=1, source_target_pairs={{0,25},{1,24},{4,29},{5,28},{8,17},{9,16},{12,21},{13,20},{16,9},{... | collective-permute-start | bytes 368648 | tf_op jit(solution)/shard_map/ppermute | solution.py:355
  192.3 17.1 %collective-permute-start.33 = (bf16[80,768]{1,0:T(8,128)(2,1)}, bf16[80,768]{1,0:T(8,128)(2,1)}, u32[]{:S(2)}, u32[]{:S(2)}) collective-permute-start(bf16[80,768]{1,0:T(8,128)(2,1)} %get-tuple-element.66), channel_id=1, source_target_pairs={{0,28},{1,29},{4,24},{5,25},{8,20},{9,21},{12,16},{13,17},{16,12},... | collective-permute-start | bytes 368648 | tf_op jit(solution)/shard_map/ppermute | solution.py:355
  193.9 19.1 %collective-permute-start.34 = (bf16[80,768]{1,0:T(8,128)(2,1)}, bf16[80,768]{1,0:T(8,128)(2,1)}, u32[]{:S(2)}, u32[]{:S(2)}) collective-permute-start(bf16[80,768]{1,0:T(8,128)(2,1)} %get-tuple-element.67), channel_id=1, source_target_pairs={{0,29},{1,28},{4,25},{5,24},{8,21},{9,20},{12,17},{13,16},{16,13},... | collective-permute-start | bytes 368648 | tf_op jit(solution)/shard_map/ppermute | solution.py:355
  214.0 1.1 copy-start.19
  230.3 13.0 %collective-permute-start.35 = (f32[128,8]{1,0:T(8,128)S(1)}, f32[128,8]{1,0:T(8,128)S(1)}, u32[]{:S(2)}, u32[]{:S(2)}) collective-permute-start(f32[128,8]{1,0:T(8,128)S(1)} %reshape.71), channel_id=1, source_target_pairs={{0,2},{2,0},{1,3},{3,1},{4,6},{6,4},{5,7},{7,5},{8,10},{10,8},{9,1... | collective-permute-start | bytes 12296 | tf_op jit(solution)/shard_map/ppermute | solution.py:348
  233.9 1.1 copy-start.8
  235.0 1.1 copy-start.10
  236.1 1.1 copy-start.12
  (31 other events, 25.1 us)

commit v4 on v0

v4 whole, which is shorter than its diff:
```python
import functools

import jax
import jax.numpy as jnp
from jax import lax
from jax.experimental import pallas as pl
from jax.experimental.pallas import tpu as pltpu
from jax.sharding import PartitionSpec as P

adapter_scale = 2.0
BF16 = jnp.bfloat16
F32 = jnp.float32
NT = (((1,), (1,)), ((), ()))
TN = (((0,), (0,)), ((), ()))
NN = (((1,), (0,)), ((), ()))
PARAMS = pltpu.CompilerParams(vmem_limit_bytes=20 * 2**20)
SMALL = pl.CostEstimate(flops=1, bytes_accessed=1, transcendentals=0)
ANY = pl.BlockSpec(memory_space=pl.ANY)


def dot(a, b, dims):
    return lax.dot_general(a, b, dims, preferred_element_type=F32)


def iota(shape, axis):
    return lax.broadcasted_iota(jnp.int32, shape, axis)


def whole(shape):
    return pl.BlockSpec(shape, lambda *_: (0,) * len(shape))


def call(kernel, name, at, arrays, in_specs, outs, out_specs, grid=(1,), scratch=()):
    return pl.pallas_call(
        kernel,
        grid_spec=pltpu.PrefetchScalarGridSpec(
            num_scalar_prefetch=1,
            grid=grid,
            in_specs=in_specs,
            out_specs=out_specs,
            scratch_shapes=scratch,
        ),
        out_shape=[jax.ShapeDtypeStruct(*o) for o in outs],
        compiler_params=PARAMS,
        cost_estimate=SMALL,
        name=name,
    )(at, *arrays)


def relative(at_ref, index, groups):
    o = lax.bitwise_xor(lax.shift_right_logical(index, 1), at_ref[1])
    q = lax.bitwise_xor(lax.bitwise_and(index, 1), at_ref[2])
    return q * groups + o


def spread_pairs(dense, top):
    toks, width = dense.shape
    return jnp.broadcast_to(dense[:, None, :], (toks, top, width)).reshape(toks * top, width)


def diagonal(pairs, top):
    return iota((pairs, top), 1) == lax.bitwise_and(iota((pairs, top), 0), top - 1)


def pair_column(table):
    toks, top = table.shape
    wide = spread_pairs(table, top)
    return jnp.sum(jnp.where(diagonal(toks * top, top), wide, 0.0), axis=1, keepdims=True)


def expert_mask(column, width, rank):
    return iota((column.shape[0], width), 1) // rank == column.astype(jnp.int32)


def pack_kernel(rank, at_ref, grad_ref, first_ref, index_ref, out_ref):
    toks, feats = grad_ref.shape
    extra = out_ref.shape[1] - feats
    out_ref[:, pl.ds(0, feats)] = grad_ref[...]
    same = jnp.where(iota((rank, rank), 0) == iota((rank, rank), 1), 1.0, 0.0).astype(BF16)
    factor = dot(same, first_ref[...], NT).astype(BF16)
    for k in range(3):
        piece = factor[:, k * extra : (k + 1) * extra]
        out_ref[pl.ds(k * rank, rank), pl.ds(feats, extra)] = piece
    top = index_ref.shape[1]
    out_ref[pl.ds(3 * rank, toks - 3 * rank), pl.ds(feats, extra)] = jnp.full(
        (toks - 3 * rank, extra), -1.0, BF16
    )
    turn = jnp.where(iota((16, top), 0) == iota((16, top), 1), 1.0, 0.0).astype(BF16)
    routes = dot(turn, index_ref[...].astype(F32).astype(BF16), NT)
    routes = jnp.where(iota((16, toks), 0) < top, routes, -1.0)
    out_ref[pl.ds(3 * rank, 16), pl.ds(feats, toks)] = routes.astype(BF16)


def pack_call(at, grad, first, index):
    (toks, feats), (units, rank) = grad.shape, first.shape
    extra = units // 3
    shape = (toks, feats + extra)
    return call(
        functools.partial(pack_kernel, rank),
        "pack_block",
        at,
        [grad, first, index],
        [whole(grad.shape), whole(first.shape), whole(index.shape)],
        [(shape, BF16)],
        [whole(shape)],
    )[0]


def expert_rows_kernel(slots, tiles, shares, batch, feats, route_row, at_ref, *rest):
    grads, seconds, weights = rest[:batch], rest[batch : batch + 2], rest[batch + 2 : batch + 4]
    outs, low_ref, rows_ref = rest[-2 - shares : -2], rest[-2], rest[-1]
    step = pl.program_id(0)

    @pl.when(step == 0)
    def _():
        toks = grads[0].shape[0]
        before = jnp.where(iota((toks, toks), 0) < iota((toks, toks), 1), 1.0, 0.0).astype(BF16)
        slot = iota((slots, toks), 0).astype(F32)
        second = jnp.concatenate([ref[...] for ref in seconds], axis=0)
        for k, grad_ref in enumerate(grads):
            routes = grad_ref[pl.ds(route_row, 16), pl.ds(feats, toks)].astype(F32)
            picks = []
            for q in range(2):
                expert = at_ref[1] * 2 + lax.bitwise_xor(at_ref[2], q)
                hits = jnp.where(routes == expert.astype(F32), 1.0, 0.0)
                mine = jnp.max(hits, axis=0, keepdims=True)
                pos = dot(jnp.broadcast_to(mine, (16, toks)).astype(BF16), before, NN)[:1]
                picks.append(jnp.where((slot == pos) & (mine > 0.0), 1.0, 0.0).astype(BF16))
            grad = grad_ref[:, pl.ds(0, feats)]
            rows = dot(jnp.concatenate(picks, axis=0), grad, NN).astype(BF16)
            for q in range(2):
                rows_ref[q, pl.ds(k * slots, slots), :] = rows[q * slots : (q + 1) * slots]
            low_ref[k] = dot(second, grad, NT).astype(BF16)

    turn = step // tiles
    tile = weights[0].shape[0]
    column = pl.ds(pl.multiple_of(lax.rem(step, tiles) * tile, 128), tile)
    for q in range(2):

        @pl.when(lax.rem(turn, 2) == q)
        def _():
            value = dot(rows_ref[q], weights[q][...], NT).astype(BF16)
            for k, out_ref in enumerate(outs):

                @pl.when(turn // 2 == k)
                def _():
                    out_ref[pl.ds(q * batch * slots, batch * slots), column] = value


def expert_rows_call(at, grads, seconds, downs, shares, slots, after):
    batch, (toks, wide) = len(grads), grads[0].shape
    rank, feats = seconds[0].shape
    units = downs[0].shape[0] // shares
    tiles = 3
    tile = units // tiles
    rows = 2 * batch * slots

    def weight_at(q, i, at):
        share = lax.rem(at[0] + i // (2 * tiles) + 1, shares)
        turn = lax.rem(i // tiles, 2)
        idle = (tiles - 1) * (1 - q)
        return (share * tiles + jnp.where(turn == q, lax.rem(i, tiles), idle), 0)

    return call(
        functools.partial(expert_rows_kernel, slots, tiles, shares, batch, feats, 3 * rank),
        "expert_rows",
        at,
        [*grads, *seconds, *downs, *after],
        [whole((toks, wide))] * batch
        + [whole((rank, feats))] * 2
        + [pl.BlockSpec((tile, feats), functools.partial(weight_at, q)) for q in range(2)]
        + [ANY] * len(after),
        [((rows, units), BF16)] * shares + [((batch, 2 * rank, toks), BF16)],
        [whole((rows, units))] * shares + [whole((batch, 2 * rank, toks))],
        grid=(shares * 2 * tiles,),
        scratch=[pltpu.VMEM((2, batch * slots, feats), BF16)],
    )


def share_sum_kernel(parts, slots, at_ref, *refs):
    outs = refs[parts:]
    for k, out_ref in enumerate(outs):
        for q in range(2):
            at = pl.ds((q * len(outs) + k) * slots, slots)
            total = refs[0][at, :].astype(F32)
            for part in refs[1:parts]:
                total = total + part[at, :].astype(F32)
            out_ref[pl.ds(q * slots, slots), :] = total.astype(BF16)


def share_sum_call(at, parts, batch, slots):
    rows, units = parts[0].shape
    shape = (2 * slots, units)
    return call(
        functools.partial(share_sum_kernel, len(parts), slots),
        "share_sum",
        at,
        parts,
        [whole((rows, units))] * len(parts),
        [(shape, BF16)] * batch,
        [whole(shape)] * batch,
    )


def collect_kernel(parts, at_ref, *refs):
    low_ref, first_ref = refs[-2:]
    rank = first_ref.shape[1]
    o = 0
    for ref in refs[:parts]:
        for k in range(ref.shape[0]):
            low_ref[lax.bitwise_xor(at_ref[1], o)] = ref[k]
            o += 1
    for o, ref in enumerate(refs[parts:-2]):
        wide = ref.shape[1]
        for k in range(3):
            first_ref[o, :, pl.ds(k * wide, wide)] = ref[pl.ds(k * rank, rank), :]


def collect_call(at, lows, grads, feats):
    groups, (toks, wide) = len(grads), grads[0].shape
    rank = lows[0].shape[1] // 2
    extra = wide - feats
    low_shape, first_shape = (groups, 2 * rank, toks), (groups, rank, 3 * extra)
    return call(
        functools.partial(collect_kernel, len(lows)),
        "collect_blocks",
        at,
        [*lows, *grads],
        [whole(b.shape) for b in lows]
        + [pl.BlockSpec((toks, extra), lambda i, at: (0, feats // extra))] * groups,
        [(low_shape, BF16), (first_shape, BF16)],
        [whole(low_shape), whole(first_shape)],
    )


def low_dense_kernel(at_ref, *refs):
    out_ref, sum_ref = refs[-2:]
    groups, both, _ = refs[0].shape
    rank = both // 2
    for o in range(groups):
        total = refs[0][lax.bitwise_xor(at_ref[1], o)].astype(F32)
        for ref in refs[1:-2]:
            total = total + ref[lax.bitwise_xor(at_ref[1], o)].astype(F32)
        for q in range(2):
            at = pl.ds((q * groups + o) * rank, rank)
            sum_ref[at, :] = total[q * rank : (q + 1) * rank]
    out_ref[...] = sum_ref[...].T


def low_dense_call(at, parts):
    groups, both, toks = parts[0].shape
    shape = (toks, groups * both)
    return call(
        low_dense_kernel,
        "low_dense",
        at,
        parts,
        [whole(parts[0].shape)] * len(parts),
        [(shape, F32)],
        [whole(shape)],
        scratch=[pltpu.VMEM((groups * both, toks), F32)],
    )[0]


def lowrank_hid_kernel(groups, at_ref, index_ref, hid_ref, *rest):
    firsts, out_ref = rest[:2], rest[2]
    top = index_ref.shape[1]
    rank = firsts[0].shape[0] // groups
    wide = jnp.concatenate([dot(hid_ref[...], ref[...], NT) for ref in firsts], axis=1)
    column = pair_column(relative(at_ref, index_ref[...], groups).astype(F32))
    wide = jnp.where(expert_mask(column, wide.shape[1], rank), wide, 0.0)
    out_ref[...] = wide.reshape(wide.shape[0] // top, top, wide.shape[1]).sum(axis=1)


def lowrank_hid_call(at, index, hid, firsts, groups):
    (toks, top), (pairs, units) = index.shape, hid.shape
    half = firsts[0].shape[0]
    steps = 4
    return call(
        functools.partial(lowrank_hid_kernel, groups),
        "lowrank_hid",
        at,
        [index, hid, *firsts],
        [
            pl.BlockSpec((toks // steps, top), lambda i, at: (i, 0)),
            pl.BlockSpec((pairs // steps, units), lambda i, at: (i, 0)),
        ]
        + [whole((half, units))] * 2,
        [((toks, 2 * half), F32)],
        [pl.BlockSpec((toks // steps, 2 * half), lambda i, at: (i, 0))],
        grid=(steps,),
    )[0]


def scaled_hid_kernel(groups, rank, at_ref, index_ref, prob_ref, *refs):
    out_ref = refs[-1]
    total = refs[0][...]
    for ref in refs[1:-1]:
        total = total + ref[...]
    place = relative(at_ref, index_ref[...], groups)
    prob = prob_ref[...].astype(F32)
    expert = iota(total.shape, 1) // rank
    scale = jnp.zeros(total.shape, F32)
    for k in range(place.shape[1]):
        scale = jnp.where(expert == place[:, k : k + 1], prob[:, k : k + 1], scale)
    scaled = (total * scale).T.astype(BF16)
    for o in range(groups):
        for q in range(2):
            at = (q * groups + o) * rank
            out_ref[lax.bitwise_xor(at_ref[1], o), pl.ds(q * rank, rank), :] = scaled[at : at + rank]


def scaled_hid_call(at, index, prob, parts, groups):
    toks, width = parts[0].shape
    rank = width // groups // 2
    shape = (groups, 2 * rank, toks)
    return call(
        functools.partial(scaled_hid_kernel, groups, rank),
        "scaled_hid",
        at,
        [index, prob, *parts],
        [whole(index.shape), whole(prob.shape)] + [whole((toks, width))] * len(parts),
        [(shape, BF16)],
        [whole(shape)],
    )[0]


def second_grad_kernel(at_ref, scaled_ref, *refs):
    grads, outs = refs[:-2], refs[-2:]
    rank, tile = outs[0].shape
    total = jnp.zeros((2 * rank, tile), F32)
    for o, grad_ref in enumerate(grads):
        total = total + dot(scaled_ref[lax.bitwise_xor(at_ref[1], o)], grad_ref[...], NN)
    for q, out_ref in enumerate(outs):
        out_ref[...] = adapter_scale * total[q * rank : (q + 1) * rank]


def second_grad_call(at, scaled, grads, feats):
    groups, both, toks = scaled.shape
    steps = 4
    tile = feats // steps
    block = pl.BlockSpec((both // 2, tile), lambda i, at: (0, i))
    return call(
        second_grad_kernel,
        "second_grad",
        at,
        [scaled, *grads],
        [whole(scaled.shape)] + [pl.BlockSpec((toks, tile), lambda i, at: (0, i))] * groups,
        [((both // 2, feats), F32)] * 2,
        [block] * 2,
        grid=(steps,),
    )


def first_grad_kernel(groups, steps, at_ref, index_ref, prob_ref, low_ref, hid_ref, *rest):
    keep_ref, give_ref, sum_ref = rest
    step = pl.program_id(0)
    top = index_ref.shape[1]
    rank = keep_ref.shape[1]
    low = spread_pairs(low_ref[...], top)
    column = pair_column(relative(at_ref, index_ref[...], groups).astype(F32))
    keep = expert_mask(column, low.shape[1], rank)
    scaled = jnp.where(keep, low * pair_column(prob_ref[...].astype(F32)), 0.0).astype(BF16)
    part = adapter_scale * dot(scaled, hid_ref[...], TN)

    @pl.when(step == 0)
    def _():
        sum_ref[...] = part

    @pl.when(step > 0)
    def _():
        sum_ref[...] += part

    @pl.when(step == steps - 1)
    def _():
        for q, out_ref in enumerate((keep_ref, give_ref)):
            half = sum_ref[pl.ds(q * groups * rank, groups * rank), :]
            out_ref[...] = half.reshape(out_ref.shape).astype(out_ref.dtype)


def first_grad_call(at, index, prob, low, hid, groups):
    (toks, top), (pairs, units) = index.shape, hid.shape
    width = low.shape[1]
    steps = 4
    shape = (groups, width // groups // 2, units)
    return call(
        functools.partial(first_grad_kernel, groups, steps),
        "first_grad",
        at,
        [index, prob, low, hid],
        [
            pl.BlockSpec((toks // steps, top), lambda i, at: (i, 0)),
            pl.BlockSpec((toks // steps, top), lambda i, at: (i, 0)),
            pl.BlockSpec((toks // steps, width), lambda i, at: (i, 0)),
            pl.BlockSpec((pairs // steps, units), lambda i, at: (i, 0)),
        ],
        [(shape, F32), (shape, BF16)],
        [whole(shape)] * 2,
        grid=(steps,),
        scratch=[pltpu.VMEM((width, units), F32)],
    )


def first_sum_kernel(at_ref, keep_ref, got_ref, out_ref):
    for o in range(keep_ref.shape[0]):
        total = keep_ref[o] + got_ref[o].astype(F32)
        out_ref[lax.bitwise_xor(at_ref[1], o)] = total.astype(BF16)


def first_sum_call(at, keep, got):
    shape = keep.shape
    return call(
        first_sum_kernel,
        "first_sum",
        at,
        [keep, got],
        [whole(shape)] * 2,
        [(shape, BF16)],
        [whole(shape)],
    )[0]


def finish_kernel(count, slots, at_ref, index_all_ref, index_ref, prob_ref, low_ref, hid_ref, *rest):
    firsts, back = rest[:2], rest[2 : 2 + count]
    out_ref, sum_ref, all_ref, place_ref = rest[2 + count :]
    top = index_ref.shape[1]
    toks = index_all_ref.shape[0]
    experts = 2 * count

    @pl.when(pl.program_id(0) == 0)
    def _():
        for o, ref in enumerate(back):
            for q in range(2):
                all_ref[pl.ds((q * count + o) * slots, slots), :] = ref[pl.ds(q * slots, slots), :]
        experts_all = relative(at_ref, index_all_ref[...], count)
        hit = jnp.zeros((toks, experts), F32)
        for k in range(top):
            hit = jnp.where(iota((toks, experts), 1) == experts_all[:, k : k + 1], 1.0, hit)
        before = jnp.where(iota((toks, toks), 0) > iota((toks, toks), 1), 1.0, 0.0).astype(BF16)
        place_ref[...] = dot(before, hit.astype(BF16), NN)

    pairs = hid_ref.shape[0]
    some = index_ref.shape[0]
    column = pair_column(relative(at_ref, index_ref[...], count).astype(F32))
    place = spread_pairs(place_ref[pl.ds(pl.program_id(0) * some, some), :], top)
    mine = iota((pairs, experts), 1) == column.astype(jnp.int32)
    target = column * slots + jnp.sum(jnp.where(mine, place, 0.0), axis=1, keepdims=True)
    low = spread_pairs(low_ref[...], top)
    keep = expert_mask(column, low.shape[1], low.shape[1] // experts)
    low = jnp.where(keep, adapter_scale * low.astype(BF16).astype(F32), 0.0).astype(BF16)
    slot = iota((pairs, experts * slots), 1)
    pick = jnp.where(slot == target.astype(jnp.int32), 1.0, 0.0).astype(BF16)
    half = low.shape[1] // 2
    value = dot(pick, all_ref[...], NN)
    value = value + dot(low[:, :half], firsts[0][...], NN) + dot(low[:, half:], firsts[1][...], NN)
    value = value.astype(BF16).astype(F32)
    out_ref[...] = (value * pair_column(prob_ref[...].astype(F32))).astype(BF16)
    sums = jnp.sum(value * hid_ref[...].astype(F32), axis=1, keepdims=True)
    sums = jnp.where(diagonal(pairs, top), sums, 0.0)
    sum_ref[...] = sums.reshape(some, top, top).sum(axis=1)


def finish_call(at, index, prob, low, hid, firsts, back):
    (toks, top), (pairs, units) = index.shape, hid.shape
    width = low.shape[1]
    both = back[0].shape[0]
    steps = 4
    count = len(back)

    def rows(n, columns):
        return pl.BlockSpec((n // steps, columns), lambda i, at: (i, 0))

    return call(
        functools.partial(finish_kernel, count, both // 2),
        "finish",
        at,
        [index, index, prob, low, hid, *firsts, *back],
        [whole(index.shape), rows(toks, top), rows(toks, top), rows(toks, width), rows(pairs, units)]
        + [whole(firsts[0].shape)] * 2
        + [whole((both, units))] * count,
        [((pairs, units), BF16), ((toks, top), F32)],
        [rows(pairs, units), rows(toks, top)],
        grid=(steps,),
        scratch=[pltpu.VMEM((count * both, units), BF16), pltpu.VMEM((toks, 2 * count), F32)],
    )


def body(grad, hidden, index, weight, down, first, second):
    toks, top = index.shape
    exp_local, units_all, feats = down.shape
    units, rank = first.shape[1:]
    groups, cores, shares = lax.axis_size("ep"), lax.axis_size("sub"), lax.axis_size("rep")
    assert exp_local == 1 and cores == 2 and groups & (groups - 1) == 0
    cap = min(toks, 5 * toks * top // (4 * groups * cores))
    slots = -(-cap // 16) * 16
    pairs = toks * top
    at = jnp.stack([lax.axis_index(name).astype(jnp.int32) for name in ("rep", "ep", "sub")])

    def turn(x, offset):
        return lax.ppermute(x, "rep", [(r, (r + offset) % shares) for r in range(shares)])

    def all_shares(x):
        return [x] + [turn(x, k) for k in range(1, shares)]

    def flip(x, mask):
        return lax.ppermute(x, "ep", [(i, i ^ mask) for i in range(groups)])

    def swap(x):
        return lax.ppermute(x, "sub", [(0, 1), (1, 0)])

    def exchange(x):
        return lax.all_to_all(x, "ep", split_axis=0, concat_axis=0, tiled=True)

    blocks = [pack_call(at, grad, first[0], index)]
    for o in range(1, groups):
        last = o & -o
        blocks.append(flip(blocks[o ^ last], last))
        if last == o and o >= 4:
            blocks[o], blocks[o - 1] = lax.optimization_barrier((blocks[o], blocks[o - 1]))
    downs = [pltpu.with_memory_space_constraint(down[0], pltpu.HBM), swap(down[0])]
    seconds = [second[0], swap(second[0])]

    back, lows, after = [], [], [[], []]
    for o in range(0, groups, 2):
        *give, keep, low = expert_rows_call(
            at, blocks[o : o + 2], seconds, downs, shares, slots, after[-2]
        )
        parts = [keep] + [turn(x, k + 1) for k, x in enumerate(give)]
        sums = share_sum_call(at, parts, 2, slots)
        back += [flip(rows, o + k) if o + k else rows for k, rows in enumerate(sums)]
        lows.append(low)
        after.append(sums[:1])

    hid = hidden.reshape(pairs, units)
    low_grad, first_own = collect_call(at, lows, blocks, feats)
    firsts = [x.reshape(groups * rank, units) for x in (first_own, swap(first_own))]

    low_hid = all_shares(lowrank_hid_call(at, index, hid, firsts, groups))
    scaled_hid = exchange(scaled_hid_call(at, index, weight, low_hid, groups))
    second_keep, second_give = second_grad_call(at, scaled_hid, blocks, feats)
    second_grad = second_keep + swap(second_give)

    low_grad = low_dense_call(at, all_shares(exchange(low_grad)))
    first_keep, first_give = first_grad_call(at, index, weight, low_grad, hid, groups)
    first_part = exchange(first_sum_call(at, first_keep, swap(first_give)))
    first_grad = jnp.sum(first_part.astype(F32), axis=0)

    grad_hidden, sums = finish_call(at, index, weight, low_grad, hid, firsts, back)
    sums = sums + turn(sums, 1) if shares == 2 else lax.psum(sums, "rep")
    return (
        grad_hidden.reshape(toks, top, units),
        sums,
        first_grad.T[None],
        second_grad[None],
    )


def solution(mesh):
    return jax.shard_map(
        body,
        mesh=mesh,
        in_specs=(
            P(("grp", "ep", "sub"), "rep"),
            P(("grp", "ep", "sub"), None, "rep"),
            P(("grp", "ep", "sub"), None),
            P(("grp", "ep", "sub"), None),
            P(("ep", "sub"), None, "rep"),
            P(("grp", "ep", "sub"), "rep", None),
            P(("grp", "ep", "sub"), None, "rep"),
        ),
        out_specs=(
            P(("grp", "ep", "sub"), None, "rep"),
            P(("grp", "ep", "sub"), None),
            P(("grp", "ep", "sub"), "rep", None),
            P(("grp", "ep", "sub"), None, "rep"),
        ),
        check_vma=False,
    )
```

time: 381 us -> 267 us (0.70)
  the two profiles are of different devices: /device:TPU:8 before, /device:TPU:0 now
where the time goes in v4:
time: 267 us; the launch traced here: 265 us
  waiting for transfers between devices  94.8 us (36%)
  Pallas kernels  87.2 us (33%)
  starting transfers between devices  39.5 us (15%)
  local copies, waits for them, and re-layouts  25.3 us (9%)
  blocking collectives  13.5 us (5%)
  other arithmetic  3.49 us (1%)
    pallas_call x17, Pallas kernels, call(): pl.pallas_call(kernel, grid_spec=pltpu.PrefetchScalarGridSpec(num_scalar_...  87.2 us
    ppermute x14, waiting for transfers between devices, flip(): return lax.ppermute(x, 'ep', [(i, i ^ mask) for i in range(groups)])  84.4 us
    unnamed x92, local copies, waits for them, and re-layouts  25.3 us
    ppermute x14, starting transfers between devices, flip(): return lax.ppermute(x, 'ep', [(i, i ^ mask) for i in range(groups)])  21.7 us
    all_to_all x1, blocking collectives, exchange(): return lax.all_to_all(x, 'ep', split_axis=0, concat_axis=0, tiled=True)  13.5 us
    ppermute x7, starting transfers between devices, turn(): lax.ppermute(x, 'rep', [(r, (r + offset) % shares) for r in range(shares)])  8.67 us
    all_to_all x2, starting transfers between devices, exchange(): return lax.all_to_all(x, 'ep', split_axis=0, concat_axis=0, tiled=True)  8.55 us
    all_to_all x2, waiting for transfers between devices, exchange(): return lax.all_to_all(x, 'ep', split_axis=0, concat_axis=0, tiled=True)  6.25 us
  transfers between devices with their start and end apart: 28, of which 10 were waited for; matrix products, arithmetic and copies ran while one was open for 2% of the time, Pallas kernels for 27%

profile of v4, /device:TPU:0, one launch (start us, length us, event | category | flops | bytes accessed | tf_op | source)
XLA Modules:
  0.0 264.8 jit_solution(1008771463705962881)
XLA Ops:
  1.1 0.8 copy.13.index_ref.index_all_ref
  1.9 1.0 copy.11
  3.0 1.0 copy-done.17
  4.0 0.8 pack_block.1.rest_0_.refs_4_.refs_0_
  4.8 2.6 collective-permute-start.3
  7.4 2.6 collective-permute-start.4
  10.0 23.9 %collective-permute-done.3.rest_0_.refs_6_.refs_2_ = bf16[128,2304]{1,0:T(8,128)(2,1)S(1)} collective-permute-done((bf16[128,2304]{1,0:T(8,128)(2,1)S(1)}, bf16[128,2304]{1,0:T(8,128)(2,1)S(1)}, u32[]{:S(2)}, u32[]{:S(2)}) %collective-permute-start.3) | collective-permute-done | bytes 589856 | tf_op jit(solution)/shard_map/ppermute | solution.py:506
  33.9 1.7 collective-permute-start.5
  35.6 0.8 collective-permute-done.4.rest_0_.refs_8_.refs_4_
  36.5 12.6 %collective-permute-done.5.rest_1_.refs_7_.refs_3_ = bf16[128,2304]{1,0:T(8,128)(2,1)S(1)} collective-permute-done((bf16[128,2304]{1,0:T(8,128)(2,1)S(1)}, bf16[128,2304]{1,0:T(8,128)(2,1)S(1)}, u32[]{:S(2)}, u32[]{:S(2)}) %collective-permute-start.5) | collective-permute-done | bytes 589856 | tf_op jit(solution)/shard_map/ppermute | solution.py:506
  49.1 1.5 collective-permute-start
  50.6 12.8 %collective-permute-done.8.rest_0_.refs_10_.refs_6_ = bf16[128,2304]{1,0:T(8,128)(2,1)S(1)} collective-permute-done((bf16[128,2304]{1,0:T(8,128)(2,1)S(1)}, bf16[128,2304]{1,0:T(8,128)(2,1)S(1)}, u32[]{:S(2)}, u32[]{:S(2)}) %collective-permute-start.8) | collective-permute-done | bytes 589856 | tf_op jit(solution)/shard_map/ppermute | solution.py:506
  63.4 1.2 collective-permute-start.9
  64.6 0.8 collective-permute-start.6
  65.4 0.9 copy-done.13
  66.3 13.6 %expert_rows.5 = (bf16[320,768]{1,0:T(8,128)(2,1)S(1)}, bf16[320,768]{1,0:T(8,128)(2,1)S(1)}, bf16[2,64,128]{2,1,0:T(8,128)(2,1)S(1)}) custom-call(s32[3]{0:T(128)S(1)} %pad_add_fusion.at_ref, bf16[128,2304]{1,0:T(8,128)(2,1)S(1)} %collective-permute-done.3.rest_0_.refs_6_.refs_2_, bf16[128,2304]{1,0:T(8,128)(2,1)S(1)} %collective-permute-done.5.rest_1_.refs_7_.refs_3_, ...), custom_call_target="tpu_custom_call" | custom-call | flops 1 | bytes 1 | tf_op jit(solution)/shard_map/expert_rows/pallas_call | solution.py:34
  79.9 1.3 collective-permute-start.10
  81.2 13.6 %expert_rows.4 = (bf16[320,768]{1,0:T(8,128)(2,1)S(1)}, bf16[320,768]{1,0:T(8,128)(2,1)S(1)}, bf16[2,64,128]{2,1,0:T(8,128)(2,1)S(1)}) custom-call(s32[3]{0:T(128)S(1)} %pad_add_fusion.at_ref, bf16[128,2304]{1,0:T(8,128)(2,1)S(1)} %pack_block.1.rest_0_.refs_4_.refs_0_, bf16[128,2304]{1,0:T(8,128)(2,1)S(1)} %collective-permute-done.rest_1_.refs_5_.refs_1_, ...), custom_call_target="tpu_custom_call" | custom-call | flops 1 | bytes 1 | tf_op jit(solution)/shard_map/expert_rows/pallas_call | solution.py:34
  94.8 0.9 collective-permute-start.7
  97.0 13.6 %expert_rows.7 = (bf16[320,768]{1,0:T(8,128)(2,1)S(1)}, bf16[320,768]{1,0:T(8,128)(2,1)S(1)}, bf16[2,64,128]{2,1,0:T(8,128)(2,1)S(1)}) custom-call(s32[3]{0:T(128)S(1)} %pad_add_fusion.at_ref, bf16[128,2304]{1,0:T(8,128)(2,1)S(1)} %collective-permute-done.8.rest_0_.refs_10_.refs_6_, bf16[128,2304]{1,0:T(8,128)(2,1)S(1)} %collective-permute-done.9.rest_1_.refs_11_.refs_7_, ...), custom_call_target="tpu_custom_call" | custom-call | flops 1 | bytes 1 | tf_op jit(solution)/shard_map/expert_rows/pallas_call | solution.py:34
  112.0 13.8 %expert_rows.6 = (bf16[320,768]{1,0:T(8,128)(2,1)S(1)}, bf16[320,768]{1,0:T(8,128)(2,1)S(1)}, bf16[2,64,128]{2,1,0:T(8,128)(2,1)S(1)}) custom-call(s32[3]{0:T(128)S(1)} %pad_add_fusion.at_ref, bf16[128,2304]{1,0:T(8,128)(2,1)S(1)} %collective-permute-done.4.rest_0_.refs_8_.refs_4_, bf16[128,2304]{1,0:T(8,128)(2,1)S(1)} %collective-permute-done.6.rest_1_.refs_9_.refs_5_, ...), custom_call_target="tpu_custom_call" | custom-call | flops 1 | bytes 1 | tf_op jit(solution)/shard_map/expert_rows/pallas_call | solution.py:34
  125.9 1.4 collect_blocks.1
  127.3 4.5 %all-to-all-start = ((bf16[8,64,128]{2,1,0:T(8,128)(2,1)}), bf16[8,64,128]{2,1,0:T(8,128)(2,1)}, u32[]{:S(2)}, u32[]{:S(2)}) async-start(bf16[8,64,128]{2,1,0:T(8,128)(2,1)} %get-tuple-element.46), calls=%async_computation | async-start | bytes 262144 | tf_op jit(solution)/shard_map/all_to_all | solution.py:512
  131.7 1.5 collective-permute-start.19
  133.2 6.2 %all-to-all-done.refs_0_ = bf16[8,64,128]{2,1,0:T(8,128)(2,1)} async-done(((bf16[8,64,128]{2,1,0:T(8,128)(2,1)}), bf16[8,64,128]{2,1,0:T(8,128)(2,1)}, u32[]{:S(2)}, u32[]{:S(2)}) %all-to-all-start) | async-done | bytes 131104 | tf_op jit(solution)/shard_map/all_to_all | solution.py:512
  139.5 1.5 collective-permute-start.11
  141.0 4.4 %lowrank_hid.1.refs_0_ = f32[128,512]{1,0:T(8,128)} custom-call(s32[3]{0:T(128)S(1)} %pad_add_fusion.at_ref, s32[128,8]{1,0:T(8,128)S(1)} %copy.13.index_ref.index_all_ref, bf16[1024,768]{1,0:T(8,128)(2,1)S(1)} %bitcast.15, bf16[256,768]{1,0:T(8,128)(2,1)} %bitcast.7.rest_0_, bf16[256,768]{1,0:T(8,128)(2,1)} %bitcast.8.rest_1_), custom_call_target="tpu_custom_call" | custom-call | flops 1 | bytes 1 | tf_op jit(solution)/shard_map/lowrank_hid/pallas_call | solution.py:34
  145.9 1.5 collective-permute-start.16
  147.5 1.3 collective-permute-done.11.refs_1_
  148.9 1.6 low_dense.1.low_ref
  150.5 3.5 %first_grad.1 = (f32[8,32,768]{2,1,0:T(8,128)S(1)}, bf16[8,32,768]{2,1,0:T(8,128)(2,1)S(1)}) custom-call(s32[3]{0:T(128)S(1)} %pad_add_fusion.at_ref, s32[128,8]{1,0:T(8,128)S(1)} %copy.13.index_ref.index_all_ref, bf16[128,8]{1,0:T(8,128)(2,1)S(1)} %copy.15.prob_ref, f32[128,512]{1,0:T(8,128)S(1)} %low_dense.1.low_ref, bf16[1024,768]{1,0:T(8,128)(2,1)S(1)} %bitcast.16), custom_call_target="tpu_custom_call" | custom-call | flops 1 | bytes 1 | tf_op jit(solution)/shard_map/first_grad/pallas_call | solution.py:34
  154.7 3.0 %collective-permute-start.15 = (bf16[160,768]{1,0:T(8,128)(2,1)}, bf16[160,768]{1,0:T(8,128)(2,1)S(1)}, u32[]{:S(2)}, u32[]{:S(2)}) collective-permute-start(bf16[160,768]{1,0:T(8,128)(2,1)} %copy-done.42), channel_id=1, source_target_pairs={{0,12},{4,8},{8,4},{12,0},{16,28},{20,24},{24,20},{28,16},{1,13},{... | collective-permute-start | bytes 737288 | tf_op jit(solution)/shard_map/ppermute | solution.py:506
  158.3 2.0 scaled_hid.1
  160.3 13.5 %all_to_all.15.scaled_ref = bf16[8,64,128]{2,1,0:T(8,128)(2,1)S(1)} all-to-all(bf16[8,64,128]{2,1,0:T(8,128)(2,1)S(1)} %scaled_hid.1), channel_id=1, replica_groups=mesh['grp'=1,'ep'=8,'rep'=2,'sub'=2] {'ep'}, dimensions={0} | all-to-all | bytes 262144 | tf_op jit(solution)/shard_map/all_to_all | solution.py:512
  173.8 1.1 copy-done.2
  174.9 1.1 copy-done.4
  176.0 1.1 copy-done.6
  177.0 1.1 copy-done.8
  178.1 1.1 copy-done.10
  179.2 3.7 %second_grad.1 = (f32[32,2048]{1,0:T(8,128)S(1)}, f32[32,2048]{1,0:T(8,128)}) custom-call(s32[3]{0:T(128)S(1)} %pad_add_fusion.at_ref, bf16[8,64,128]{2,1,0:T(8,128)(2,1)S(1)} %all_to_all.15.scaled_ref, bf16[128,2304]{1,0:T(8,128)(2,1)S(1)} %pack_block.1.rest_0_.refs_4_.refs_0_, bf16[128,2304]{1,0:T(8,128)(2,1)S(1)} %copy-done.10, ...), custom_call_target="tpu_custom_call" | custom-call | flops 1 | bytes 1 | tf_op jit(solution)/shard_map/second_grad/pallas_call | solution.py:34
  182.9 2.5 share_sum.7
  185.3 2.5 share_sum.6
  188.5 1.6 collective-permute-start.20
  190.8 2.2 collective-permute-start.21
  193.8 3.8 %collective-permute-start.18 = (bf16[160,768]{1,0:T(8,128)(2,1)}, bf16[160,768]{1,0:T(8,128)(2,1)S(1)}, u32[]{:S(2)}, u32[]{:S(2)}) collective-permute-start(bf16[160,768]{1,0:T(8,128)(2,1)} %get-tuple-element.53), channel_id=1, source_target_pairs={{0,20},{4,16},{8,28},{12,24},{16,4},{20,0},{24,12},{28,8},{1,21},{... | collective-permute-start | bytes 737288 | tf_op jit(solution)/shard_map/ppermute | solution.py:506
  197.6 1.3 first_sum.1
  198.9 4.1 %all-to-all-start.1 = ((bf16[8,32,768]{2,1,0:T(8,128)(2,1)}), bf16[8,32,768]{2,1,0:T(8,128)(2,1)}, u32[]{:S(2)}, u32[]{:S(2)}) async-start(bf16[8,32,768]{2,1,0:T(8,128)(2,1)} %first_sum.1), calls=%async_computation.1 | async-start | bytes 786432 | tf_op jit(solution)/shard_map/all_to_all | solution.py:512
  203.8 0.9 collective-permute-done.21.rest_9_
  205.4 28.1 %collective-permute-done.17.rest_6_ = bf16[160,768]{1,0:T(8,128)(2,1)S(1)} collective-permute-done((bf16[160,768]{1,0:T(8,128)(2,1)}, bf16[160,768]{1,0:T(8,128)(2,1)S(1)}, u32[]{:S(2)}, u32[]{:S(2)}) %collective-permute-start.17) | collective-permute-done | bytes 245792 | tf_op jit(solution)/shard_map/ppermute | solution.py:506
  234.1 5.3 %collective-permute-done.18.rest_7_ = bf16[160,768]{1,0:T(8,128)(2,1)S(1)} collective-permute-done((bf16[160,768]{1,0:T(8,128)(2,1)}, bf16[160,768]{1,0:T(8,128)(2,1)S(1)}, u32[]{:S(2)}, u32[]{:S(2)}) %collective-permute-start.18) | collective-permute-done | bytes 245792 | tf_op jit(solution)/shard_map/ppermute | solution.py:506
  240.1 0.9 copy-done.12
  241.1 0.9 copy-done.16
  242.0 0.9 copy-done.26
  243.0 0.9 copy-done.28
  243.9 0.9 copy-done.30
  244.8 0.9 copy-done.32
  245.8 0.9 copy-done.34
  246.7 0.9 copy-done.36
  247.7 0.9 copy-done.38
  248.6 7.8 %finish.1 = (bf16[1024,768]{1,0:T(8,128)(2,1)}, f32[128,8]{1,0:T(8,128)S(1)}) custom-call(s32[3]{0:T(128)S(1)} %pad_add_fusion.at_ref, s32[128,8]{1,0:T(8,128)S(1)} %copy.13.index_ref.index_all_ref, s32[128,8]{1,0:T(8,128)S(1)} %copy.13.index_ref.index_all_ref, bf16[128,8]{1,0:T(8,128)(2,1)S(1)} %copy.15.prob_ref, f32[128,512]{1,0:T(8,128)S(1)} %copy-done.12, ...), custom_call_target="tpu_custom_call" | custom-call | flops 1 | bytes 1 | tf_op jit(solution)/shard_map/finish/pallas_call | solution.py:34
  256.4 1.5 collective-permute-start.22
  257.9 2.8 %collective-permute-done.22 = f32[128,8]{1,0:T(8,128)S(1)} collective-permute-done((f32[128,8]{1,0:T(8,128)S(1)}, f32[128,8]{1,0:T(8,128)S(1)}, u32[]{:S(2)}, u32[]{:S(2)}) %collective-permute-start.22) | collective-permute-done | bytes 4128 | tf_op jit(solution)/shard_map/ppermute | solution.py:500
  261.4 1.7 add_bitcast_fusion
  263.1 1.7 convert_reduce_fusion
  (106 shorter events, 11.0 us)
Async XLA Ops:
  0.6 64.8 %collective-permute-start.2 = (bf16[1536,2048]{1,0:T(8,128)(2,1)}, bf16[1536,2048]{1,0:T(8,128)(2,1)}, u32[]{:S(2)}, u32[]{:S(2)}) collective-permute-start(bf16[1536,2048]{1,0:T(8,128)(2,1)} %bitcast.24), channel_id=1, source_target_pairs={{0,1},{1,0},{2,3},{3,2},{4,5},{5,4},{6,7},{7,6},{8,9},{9,8},{10,11... | collective-permute-start | bytes 18874376 | tf_op jit(solution)/shard_map/ppermute | solution.py:509
  3.0 1.0 copy-start.17
  4.8 29.2 %collective-permute-start.3 = (bf16[128,2304]{1,0:T(8,128)(2,1)S(1)}, bf16[128,2304]{1,0:T(8,128)(2,1)S(1)}, u32[]{:S(2)}, u32[]{:S(2)}) collective-permute-start(bf16[128,2304]{1,0:T(8,128)(2,1)S(1)} %pack_block.1.rest_0_.refs_4_.refs_0_), channel_id=1, source_target_pairs={{0,8},{4,12},{8,0},{12,4},{16,24},{20,28},{24,16},{28,20},{1,9},{5... | collective-permute-start | bytes 1769480 | tf_op jit(solution)/shard_map/ppermute | solution.py:506
  7.4 29.0 %collective-permute-start.4 = (bf16[128,2304]{1,0:T(8,128)(2,1)S(1)}, bf16[128,2304]{1,0:T(8,128)(2,1)S(1)}, u32[]{:S(2)}, u32[]{:S(2)}) collective-permute-start(bf16[128,2304]{1,0:T(8,128)(2,1)S(1)} %pack_block.1.rest_0_.refs_4_.refs_0_), channel_id=1, source_target_pairs={{0,16},{4,20},{8,24},{12,28},{16,0},{20,4},{24,8},{28,12},{1,17},{... | collective-permute-start | bytes 1769480 | tf_op jit(solution)/shard_map/ppermute | solution.py:506
  33.9 91.9 %copy-start.5 = (bf16[128,2304]{1,0:T(8,128)(2,1)}, bf16[128,2304]{1,0:T(8,128)(2,1)S(1)}, u32[]{:S(2)}) copy-start(bf16[128,2304]{1,0:T(8,128)(2,1)S(1)} %collective-permute-done.3.rest_0_.refs_6_.refs_2_) | copy-start | bytes 1769476
  33.9 15.1 %collective-permute-start.5 = (bf16[128,2304]{1,0:T(8,128)(2,1)S(1)}, bf16[128,2304]{1,0:T(8,128)(2,1)S(1)}, u32[]{:S(2)}, u32[]{:S(2)}) collective-permute-start(bf16[128,2304]{1,0:T(8,128)(2,1)S(1)} %collective-permute-done.3.rest_0_.refs_6_.refs_2_), channel_id=1, source_target_pairs={{0,4},{4,0},{8,12},{12,8},{16,20},{20,16},{24,28},{28,24},{1,5},{5... | collective-permute-start | bytes 1769480 | tf_op jit(solution)/shard_map/ppermute | solution.py:506
  49.1 76.8 %copy-start.7 = (bf16[128,2304]{1,0:T(8,128)(2,1)}, bf16[128,2304]{1,0:T(8,128)(2,1)S(1)}, u32[]{:S(2)}) copy-start(bf16[128,2304]{1,0:T(8,128)(2,1)S(1)} %collective-permute-done.5.rest_1_.refs_7_.refs_3_) | copy-start | bytes 1769476
  49.1 14.3 %collective-permute-start.8 = (bf16[128,2304]{1,0:T(8,128)(2,1)S(1)}, bf16[128,2304]{1,0:T(8,128)(2,1)S(1)}, u32[]{:S(2)}, u32[]{:S(2)}) collective-permute-start(bf16[128,2304]{1,0:T(8,128)(2,1)S(1)} %collective-permute-done.4.rest_0_.refs_8_.refs_4_), channel_id=1, source_target_pairs={{0,8},{4,12},{8,0},{12,4},{16,24},{20,28},{24,16},{28,20},{1,9},{5... | collective-permute-start | bytes 1769480 | tf_op jit(solution)/shard_map/ppermute | solution.py:506
  49.1 32.1 %collective-permute-start = (bf16[128,2304]{1,0:T(8,128)(2,1)S(1)}, bf16[128,2304]{1,0:T(8,128)(2,1)S(1)}, u32[]{:S(2)}, u32[]{:S(2)}) collective-permute-start(bf16[128,2304]{1,0:T(8,128)(2,1)S(1)} %pack_block.1.rest_0_.refs_4_.refs_0_), channel_id=1, source_target_pairs={{0,4},{4,0},{8,12},{12,8},{16,20},{20,16},{24,28},{28,24},{1,5},{5... | collective-permute-start | bytes 1769480 | tf_op jit(solution)/shard_map/ppermute | solution.py:506
  50.6 14.8 %collective-permute-start.1 = (bf16[32,2048]{1,0:T(8,128)(2,1)}, bf16[32,2048]{1,0:T(8,128)(2,1)S(1)}, u32[]{:S(2)}, u32[]{:S(2)}) collective-permute-start(bf16[32,2048]{1,0:T(8,128)(2,1)} %bitcast.18), channel_id=1, source_target_pairs={{0,1},{1,0},{2,3},{3,2},{4,5},{5,4},{6,7},{7,6},{8,9},{9,8},{10,11... | collective-permute-start | bytes 393224 | tf_op jit(solution)/shard_map/ppermute | solution.py:509
  63.4 33.6 %collective-permute-start.9 = (bf16[128,2304]{1,0:T(8,128)(2,1)S(1)}, bf16[128,2304]{1,0:T(8,128)(2,1)S(1)}, u32[]{:S(2)}, u32[]{:S(2)}) collective-permute-start(bf16[128,2304]{1,0:T(8,128)(2,1)S(1)} %collective-permute-done.8.rest_0_.refs_10_.refs_6_), channel_id=1, source_target_pairs={{0,4},{4,0},{8,12},{12,8},{16,20},{20,16},{24,28},{28,24},{1,5},{5... | collective-permute-start | bytes 1769480 | tf_op jit(solution)/shard_map/ppermute | solution.py:506
  64.6 47.4 %collective-permute-start.6 = (bf16[128,2304]{1,0:T(8,128)(2,1)S(1)}, bf16[128,2304]{1,0:T(8,128)(2,1)S(1)}, u32[]{:S(2)}, u32[]{:S(2)}) collective-permute-start(bf16[128,2304]{1,0:T(8,128)(2,1)S(1)} %collective-permute-done.4.rest_0_.refs_8_.refs_4_), channel_id=1, source_target_pairs={{0,4},{4,0},{8,12},{12,8},{16,20},{20,16},{24,28},{28,24},{1,5},{5... | collective-permute-start | bytes 1769480 | tf_op jit(solution)/shard_map/ppermute | solution.py:506
  65.4 0.9 copy-start.13
  79.9 17.1 %copy-start.14 = (bf16[1,32,2048]{2,1,0:T(8,128)(2,1)S(1)}, bf16[1,32,2048]{2,1,0:T(8,128)(2,1)}, u32[]{:S(2)}) copy-start(bf16[1,32,2048]{2,1,0:T(8,128)(2,1)} %param.13) | copy-start | bytes 393220
  79.9 15.8 %collective-permute-start.10 = (bf16[320,768]{1,0:T(8,128)(2,1)S(1)}, bf16[320,768]{1,0:T(8,128)(2,1)S(1)}, u32[]{:S(2)}, u32[]{:S(2)}) collective-permute-start(bf16[320,768]{1,0:T(8,128)(2,1)S(1)} %get-tuple-element.43), channel_id=1, source_target_pairs={{0,2},{2,0},{1,3},{3,1},{4,6},{6,4},{5,7},{7,5},{8,10},{10,8},{9,1... | collective-permute-start | bytes 1474568 | tf_op jit(solution)/shard_map/ppermute | solution.py:500
  81.2 44.7 %copy-start.9 = (bf16[128,2304]{1,0:T(8,128)(2,1)}, bf16[128,2304]{1,0:T(8,128)(2,1)S(1)}, u32[]{:S(2)}) copy-start(bf16[128,2304]{1,0:T(8,128)(2,1)S(1)} %collective-permute-done.rest_1_.refs_5_.refs_1_) | copy-start | bytes 1769476
  94.8 15.8 %collective-permute-start.7 = (bf16[320,768]{1,0:T(8,128)(2,1)S(1)}, bf16[320,768]{1,0:T(8,128)(2,1)S(1)}, u32[]{:S(2)}, u32[]{:S(2)}) collective-permute-start(bf16[320,768]{1,0:T(8,128)(2,1)S(1)} %get-tuple-element.39), channel_id=1, source_target_pairs={{0,2},{2,0},{1,3},{3,1},{4,6},{6,4},{5,7},{7,5},{8,10},{10,8},{9,1... | collective-permute-start | bytes 1474568 | tf_op jit(solution)/shard_map/ppermute | solution.py:500
  97.0 13.6 %copy-start.24 = (bf16[160,768]{1,0:T(8,128)(2,1)}, bf16[160,768]{1,0:T(8,128)(2,1)S(1)}, u32[]{:S(2)}) copy-start(bf16[160,768]{1,0:T(8,128)(2,1)S(1)} %get-tuple-element.44.rest_6_) | copy-start | bytes 737284
  97.0 28.9 %copy-start.1 = (bf16[128,2304]{1,0:T(8,128)(2,1)}, bf16[128,2304]{1,0:T(8,128)(2,1)S(1)}, u32[]{:S(2)}) copy-start(bf16[128,2304]{1,0:T(8,128)(2,1)S(1)} %collective-permute-done.9.rest_1_.refs_11_.refs_7_) | copy-start | bytes 1769476
  110.6 1.4 copy-start.18
  110.6 15.2 %copy-start.40 = (bf16[320,768]{1,0:T(8,128)(2,1)}, bf16[320,768]{1,0:T(8,128)(2,1)S(1)}, u32[]{:S(2)}) copy-start(bf16[320,768]{1,0:T(8,128)(2,1)S(1)} %get-tuple-element.55) | copy-start | bytes 1474564
  112.0 13.8 %copy-start.15 = (bf16[160,768]{1,0:T(8,128)(2,1)}, bf16[160,768]{1,0:T(8,128)(2,1)S(1)}, u32[]{:S(2)}) copy-start(bf16[160,768]{1,0:T(8,128)(2,1)S(1)} %get-tuple-element.40.rest_6_.rest_2_) | copy-start | bytes 737284
  112.0 13.9 %copy-start.3 = (bf16[128,2304]{1,0:T(8,128)(2,1)}, bf16[128,2304]{1,0:T(8,128)(2,1)S(1)}, u32[]{:S(2)}) copy-start(bf16[128,2304]{1,0:T(8,128)(2,1)S(1)} %collective-permute-done.6.rest_1_.refs_9_.refs_5_) | copy-start | bytes 1769476
  112.0 29.0 %copy-start = (bf16[128,8,768]{2,1,0:T(8,128)(2,1)S(1)}, bf16[128,8,768]{2,1,0:T(8,128)(2,1)}, u32[]{:S(2)}) copy-start(bf16[128,8,768]{2,1,0:T(8,128)(2,1)} %param.8) | copy-start | bytes 4718596
  125.8 1.5 copy-start.20
  125.8 1.5 copy-start.39
  125.8 21.6 %copy-start.43 = (bf16[128,8]{0,1:T(8,128)(2,1)S(1)}, bf16[128,8]{0,1:T(8,128)(2,1)}, u32[]{:S(2)}) copy-start(bf16[128,8]{0,1:T(8,128)(2,1)} %param.10) | copy-start | bytes 6148
  127.3 13.7 %collective-permute-start.12 = (bf16[8,32,768]{2,1,0:T(8,128)(2,1)}, bf16[8,32,768]{2,1,0:T(8,128)(2,1)}, u32[]{:S(2)}, u32[]{:S(2)}) collective-permute-start(bf16[8,32,768]{2,1,0:T(8,128)(2,1)} %get-tuple-element.47), channel_id=1, source_target_pairs={{0,1},{1,0},{2,3},{3,2},{4,5},{5,4},{6,7},{7,6},{8,9},{9,8},{10,11... | collective-permute-start | bytes 1179656 | tf_op jit(solution)/shard_map/ppermute | solution.py:509
  127.3 12.2 %all-to-all-start = ((bf16[8,64,128]{2,1,0:T(8,128)(2,1)}), bf16[8,64,128]{2,1,0:T(8,128)(2,1)}, u32[]{:S(2)}, u32[]{:S(2)}) async-start(bf16[8,64,128]{2,1,0:T(8,128)(2,1)} %get-tuple-element.46), calls=%async_computation | async-start | bytes 262144 | tf_op jit(solution)/shard_map/all_to_all | solution.py:512
  131.7 26.0 %collective-permute-start.19 = (bf16[320,768]{1,0:T(8,128)(2,1)}, bf16[320,768]{1,0:T(8,128)(2,1)}, u32[]{:S(2)}, u32[]{:S(2)}) collective-permute-start(bf16[320,768]{1,0:T(8,128)(2,1)} %copy-done.40), channel_id=1, source_target_pairs={{0,2},{2,0},{1,3},{3,1},{4,6},{6,4},{5,7},{7,5},{8,10},{10,8},{9,1... | collective-permute-start | bytes 1474568 | tf_op jit(solution)/shard_map/ppermute | solution.py:500
  139.5 9.4 %collective-permute-start.11 = (bf16[8,64,128]{2,1,0:T(8,128)(2,1)}, bf16[8,64,128]{2,1,0:T(8,128)(2,1)}, u32[]{:S(2)}, u32[]{:S(2)}) collective-permute-start(bf16[8,64,128]{2,1,0:T(8,128)(2,1)} %all-to-all-done.refs_0_), channel_id=1, source_target_pairs={{0,2},{2,0},{1,3},{3,1},{4,6},{6,4},{5,7},{7,5},{8,10},{10,8},{9,1... | collective-permute-start | bytes 393224 | tf_op jit(solution)/shard_map/ppermute | solution.py:500
  145.4 12.9 %collective-permute-start.24 = (f32[128,512]{1,0:T(8,128)}, f32[128,512]{1,0:T(8,128)}, u32[]{:S(2)}, u32[]{:S(2)}) collective-permute-start(f32[128,512]{1,0:T(8,128)} %lowrank_hid.1.refs_0_), channel_id=1, source_target_pairs={{0,2},{2,0},{1,3},{3,1},{4,6},{6,4},{5,7},{7,5},{8,10},{10,8},{9,1... | collective-permute-start | bytes 786440 | tf_op jit(solution)/shard_map/ppermute | solution.py:500
  145.9 36.9 %collective-permute-start.16 = (bf16[320,768]{1,0:T(8,128)(2,1)}, bf16[320,768]{1,0:T(8,128)(2,1)}, u32[]{:S(2)}, u32[]{:S(2)}) collective-permute-start(bf16[320,768]{1,0:T(8,128)(2,1)} %copy-done.39), channel_id=1, source_target_pairs={{0,2},{2,0},{1,3},{3,1},{4,6},{6,4},{5,7},{7,5},{8,10},{10,8},{9,1... | collective-permute-start | bytes 1474568 | tf_op jit(solution)/shard_map/ppermute | solution.py:500
  147.5 35.3 %copy-start.19 = (bf16[320,768]{1,0:T(8,128)(2,1)S(1)}, bf16[320,768]{1,0:T(8,128)(2,1)}, u32[]{:S(2)}) copy-start(bf16[320,768]{1,0:T(8,128)(2,1)} %copy-done.18) | copy-start | bytes 1474564
  147.5 37.8 %copy-start.21 = (bf16[320,768]{1,0:T(8,128)(2,1)S(1)}, bf16[320,768]{1,0:T(8,128)(2,1)}, u32[]{:S(2)}) copy-start(bf16[320,768]{1,0:T(8,128)(2,1)} %copy-done.20) | copy-start | bytes 1474564
  154.7 39.0 %collective-permute-start.23 = (bf16[8,32,768]{2,1,0:T(8,128)(2,1)S(1)}, bf16[8,32,768]{2,1,0:T(8,128)(2,1)S(1)}, u32[]{:S(2)}, u32[]{:S(2)}) collective-permute-start(bf16[8,32,768]{2,1,0:T(8,128)(2,1)S(1)} %get-tuple-element.61), channel_id=1, source_target_pairs={{0,1},{1,0},{2,3},{3,2},{4,5},{5,4},{6,7},{7,6},{8,9},{9,8},{10,11... | collective-permute-start | bytes 1179656 | tf_op jit(solution)/shard_map/ppermute | solution.py:509
  154.7 33.1 %collective-permute-start.15 = (bf16[160,768]{1,0:T(8,128)(2,1)}, bf16[160,768]{1,0:T(8,128)(2,1)S(1)}, u32[]{:S(2)}, u32[]{:S(2)}) collective-permute-start(bf16[160,768]{1,0:T(8,128)(2,1)} %copy-done.42), channel_id=1, source_target_pairs={{0,12},{4,8},{8,4},{12,0},{16,28},{20,24},{24,20},{28,16},{1,13},{... | collective-permute-start | bytes 737288 | tf_op jit(solution)/shard_map/ppermute | solution.py:506
  157.7 32.4 %collective-permute-start.14 = (bf16[160,768]{1,0:T(8,128)(2,1)}, bf16[160,768]{1,0:T(8,128)(2,1)S(1)}, u32[]{:S(2)}, u32[]{:S(2)}) collective-permute-start(bf16[160,768]{1,0:T(8,128)(2,1)} %copy-done.24), channel_id=1, source_target_pairs={{0,8},{4,12},{8,0},{12,4},{16,24},{20,28},{24,16},{28,20},{1,9},{5... | collective-permute-start | bytes 737288 | tf_op jit(solution)/shard_map/ppermute | solution.py:506
  158.2 34.8 %collective-permute-start.13 = (bf16[160,768]{1,0:T(8,128)(2,1)}, bf16[160,768]{1,0:T(8,128)(2,1)S(1)}, u32[]{:S(2)}, u32[]{:S(2)}) collective-permute-start(bf16[160,768]{1,0:T(8,128)(2,1)} %copy-done.41), channel_id=1, source_target_pairs={{0,4},{4,0},{8,12},{12,8},{16,20},{20,16},{24,28},{28,24},{1,5},{5... | collective-permute-start | bytes 737288 | tf_op jit(solution)/shard_map/ppermute | solution.py:506
  173.8 1.1 copy-start.2
  174.9 1.1 copy-start.4
  176.0 1.1 copy-start.6
  177.0 1.1 copy-start.8
  178.1 1.1 copy-start.10
  182.8 10.9 %copy-start.22 = (f32[32,2048]{1,0:T(8,128)}, f32[32,2048]{1,0:T(8,128)S(1)}, u32[]{:S(2)}) copy-start(f32[32,2048]{1,0:T(8,128)S(1)} %get-tuple-element.62) | copy-start | bytes 786436
  182.8 78.5 %collective-permute-start.25 = (f32[32,2048]{1,0:T(8,128)}, f32[32,2048]{1,0:T(8,128)}, u32[]{:S(2)}, u32[]{:S(2)}) collective-permute-start(f32[32,2048]{1,0:T(8,128)} %get-tuple-element.63), channel_id=1, source_target_pairs={{0,1},{1,0},{2,3},{3,2},{4,5},{5,4},{6,7},{7,6},{8,9},{9,8},{10,11... | collective-permute-start | bytes 786440 | tf_op jit(solution)/shard_map/ppermute | solution.py:509
  188.5 14.6 %collective-permute-start.20 = (bf16[160,768]{1,0:T(8,128)(2,1)}, bf16[160,768]{1,0:T(8,128)(2,1)S(1)}, u32[]{:S(2)}, u32[]{:S(2)}) collective-permute-start(bf16[160,768]{1,0:T(8,128)(2,1)} %get-tuple-element.56), channel_id=1, source_target_pairs={{0,24},{4,28},{8,16},{12,20},{16,8},{20,12},{24,0},{28,4},{1,25},{... | collective-permute-start | bytes 737288 | tf_op jit(solution)/shard_map/ppermute | solution.py:506
  190.8 13.9 %collective-permute-start.21 = (bf16[160,768]{1,0:T(8,128)(2,1)}, bf16[160,768]{1,0:T(8,128)(2,1)S(1)}, u32[]{:S(2)}, u32[]{:S(2)}) collective-permute-start(bf16[160,768]{1,0:T(8,128)(2,1)} %get-tuple-element.57), channel_id=1, source_target_pairs={{0,28},{4,24},{8,20},{12,16},{16,12},{20,8},{24,4},{28,0},{1,29},{... | collective-permute-start | bytes 737288 | tf_op jit(solution)/shard_map/ppermute | solution.py:506
  193.7 39.7 %collective-permute-start.17 = (bf16[160,768]{1,0:T(8,128)(2,1)}, bf16[160,768]{1,0:T(8,128)(2,1)S(1)}, u32[]{:S(2)}, u32[]{:S(2)}) collective-permute-start(bf16[160,768]{1,0:T(8,128)(2,1)} %get-tuple-element.52), channel_id=1, source_target_pairs={{0,16},{4,20},{8,24},{12,28},{16,0},{20,4},{24,8},{28,12},{1,17},{... | collective-permute-start | bytes 737288 | tf_op jit(solution)/shard_map/ppermute | solution.py:506
  193.7 67.6 %copy-start.23 = (f32[32,2048]{1,0:T(8,128)S(1)}, f32[32,2048]{1,0:T(8,128)}, u32[]{:S(2)}) copy-start(f32[32,2048]{1,0:T(8,128)} %copy-done.22) | copy-start | bytes 786436
  193.8 45.6 %collective-permute-start.18 = (bf16[160,768]{1,0:T(8,128)(2,1)}, bf16[160,768]{1,0:T(8,128)(2,1)S(1)}, u32[]{:S(2)}, u32[]{:S(2)}) collective-permute-start(bf16[160,768]{1,0:T(8,128)(2,1)} %get-tuple-element.53), channel_id=1, source_target_pairs={{0,20},{4,16},{8,28},{12,24},{16,4},{20,0},{24,12},{28,8},{1,21},{... | collective-permute-start | bytes 737288 | tf_op jit(solution)/shard_map/ppermute | solution.py:506
  198.9 64.2 %all-to-all-start.1 = ((bf16[8,32,768]{2,1,0:T(8,128)(2,1)}), bf16[8,32,768]{2,1,0:T(8,128)(2,1)}, u32[]{:S(2)}, u32[]{:S(2)}) async-start(bf16[8,32,768]{2,1,0:T(8,128)(2,1)} %first_sum.1), calls=%async_computation.1 | async-start | bytes 786432 | tf_op jit(solution)/shard_map/all_to_all | solution.py:512
  203.0 0.7 copy-start.31
  204.6 0.7 copy-start.33
  240.1 0.9 copy-start.12
  241.1 0.9 copy-start.16
  242.0 0.9 copy-start.26
  243.0 0.9 copy-start.28
  243.9 0.9 copy-start.30
  244.8 0.9 copy-start.32
  245.8 0.9 copy-start.34
  246.7 0.9 copy-start.36
  247.7 0.9 copy-start.38
  256.4 4.3 %collective-permute-start.22 = (f32[128,8]{1,0:T(8,128)S(1)}, f32[128,8]{1,0:T(8,128)S(1)}, u32[]{:S(2)}, u32[]{:S(2)}) collective-permute-start(f32[128,8]{1,0:T(8,128)S(1)} %get-tuple-element.59), channel_id=1, source_target_pairs={{0,2},{2,0},{1,3},{3,1},{4,6},{6,4},{5,7},{7,5},{8,10},{10,8},{9,1... | collective-permute-start | bytes 12296 | tf_op jit(solution)/shard_map/ppermute | solution.py:500
  (8 other events, 5.6 us)

commit v5 on v4

--- a/solution.py
+++ b/solution.py
@@ -8,18 +8,23 @@
 from jax.sharding import PartitionSpec as P
 
 adapter_scale = 2.0
+CHUNKS = 3
 BF16 = jnp.bfloat16
 F32 = jnp.float32
 NT = (((1,), (1,)), ((), ()))
 TN = (((0,), (0,)), ((), ()))
 NN = (((1,), (0,)), ((), ()))
-PARAMS = pltpu.CompilerParams(vmem_limit_bytes=20 * 2**20)
+PARAMS = pltpu.CompilerParams(vmem_limit_bytes=40 * 2**20)
 SMALL = pl.CostEstimate(flops=1, bytes_accessed=1, transcendentals=0)
 ANY = pl.BlockSpec(memory_space=pl.ANY)
 
 
 def dot(a, b, dims):
     return lax.dot_general(a, b, dims, preferred_element_type=F32)
+
+
+def in_hbm(x):
+    return pltpu.with_memory_space_constraint(x, pltpu.HBM)
 
 
 def iota(shape, axis):
@@ -48,7 +53,7 @@
 
 
 def relative(at_ref, index, groups):
-    o = lax.bitwise_xor(lax.shift_right_logical(index, 1), at_ref[1])
+    o = lax.shift_right_logical(index, 1)
     q = lax.bitwise_xor(lax.bitwise_and(index, 1), at_ref[2])
     return q * groups + o
 
@@ -106,131 +111,138 @@
     )[0]
 
 
-def expert_rows_kernel(slots, tiles, shares, batch, feats, route_row, at_ref, *rest):
-    grads, seconds, weights = rest[:batch], rest[batch : batch + 2], rest[batch + 2 : batch + 4]
-    outs, low_ref, rows_ref = rest[-2 - shares : -2], rest[-2], rest[-1]
-    step = pl.program_id(0)
-
-    @pl.when(step == 0)
-    def _():
-        toks = grads[0].shape[0]
-        before = jnp.where(iota((toks, toks), 0) < iota((toks, toks), 1), 1.0, 0.0).astype(BF16)
-        slot = iota((slots, toks), 0).astype(F32)
-        second = jnp.concatenate([ref[...] for ref in seconds], axis=0)
-        for k, grad_ref in enumerate(grads):
-            routes = grad_ref[pl.ds(route_row, 16), pl.ds(feats, toks)].astype(F32)
-            picks = []
-            for q in range(2):
-                expert = at_ref[1] * 2 + lax.bitwise_xor(at_ref[2], q)
-                hits = jnp.where(routes == expert.astype(F32), 1.0, 0.0)
-                mine = jnp.max(hits, axis=0, keepdims=True)
-                pos = dot(jnp.broadcast_to(mine, (16, toks)).astype(BF16), before, NN)[:1]
-                picks.append(jnp.where((slot == pos) & (mine > 0.0), 1.0, 0.0).astype(BF16))
-            grad = grad_ref[:, pl.ds(0, feats)]
-            rows = dot(jnp.concatenate(picks, axis=0), grad, NN).astype(BF16)
-            for q in range(2):
-                rows_ref[q, pl.ds(k * slots, slots), :] = rows[q * slots : (q + 1) * slots]
-            low_ref[k] = dot(second, grad, NT).astype(BF16)
-
-    turn = step // tiles
-    tile = weights[0].shape[0]
-    column = pl.ds(pl.multiple_of(lax.rem(step, tiles) * tile, 128), tile)
+def weight_copies(chunk, chunks, at_ref, downs, tiles_ref, sems):
+    _, shares, units, _ = tiles_ref.shape
+    copies = []
     for q in range(2):
-
-        @pl.when(lax.rem(turn, 2) == q)
-        def _():
-            value = dot(rows_ref[q], weights[q][...], NT).astype(BF16)
-            for k, out_ref in enumerate(outs):
-
-                @pl.when(turn // 2 == k)
-                def _():
-                    out_ref[pl.ds(q * batch * slots, batch * slots), column] = value
-
-
-def expert_rows_call(at, grads, seconds, downs, shares, slots, after):
-    batch, (toks, wide) = len(grads), grads[0].shape
+        for k in range(shares):
+            share = lax.rem(at_ref[0] + k + 1, shares)
+            row = pl.multiple_of((share * chunks + chunk) * units, units)
+            copies.append(
+                pltpu.make_async_copy(
+                    downs[q].at[pl.ds(row, units), :], tiles_ref.at[q, k], sems.at[q * shares + k]
+                )
+            )
+    return copies
+
+
+def chunk_product(copies, rows_ref, tiles_ref, outs):
+    shares = len(outs)
+    groups, both, units = outs[0].shape
+    slots = both // 2
+    for q in range(2):
+        for k in range(shares):
+            copies[q * shares + k].wait()
+            value = dot(rows_ref[q], tiles_ref[q, k], NT).astype(BF16)
+            outs[k][:, pl.ds(q * slots, slots), :] = value.reshape(groups, slots, units)
+
+
+def first_chunk_kernel(chunks, route_row, at_ref, grad_ref, *rest):
+    seconds, downs = rest[:2], rest[2:4]
+    *outs, rows_ref, low_ref, block_ref, tiles_ref, block_sems, sems = rest[4:]
+    groups, toks, wide = grad_ref.shape
+    slots = outs[0].shape[1] // 2
+    feats = rows_ref.shape[2]
+    copies = weight_copies(0, chunks, at_ref, downs, tiles_ref, sems)
+    blocks = [
+        pltpu.make_async_copy(grad_ref.at[j], block_ref.at[j], block_sems.at[j])
+        for j in range(groups)
+    ]
+    for copy in blocks + copies:
+        copy.start()
+    before = jnp.where(iota((toks, toks), 0) < iota((toks, toks), 1), 1.0, 0.0).astype(BF16)
+    slot = iota((slots, toks), 0).astype(F32)
+    second = jnp.concatenate([ref[...] for ref in seconds], axis=0)
+    for j in range(groups):
+        blocks[j].wait()
+        routes = block_ref[j, pl.ds(route_row, 16), pl.ds(feats, toks)].astype(F32)
+        picks = []
+        for q in range(2):
+            expert = at_ref[1] * 2 + lax.bitwise_xor(at_ref[2], q)
+            hits = jnp.where(routes == expert.astype(F32), 1.0, 0.0)
+            mine = jnp.max(hits, axis=0, keepdims=True)
+            pos = dot(jnp.broadcast_to(mine, (16, toks)).astype(BF16), before, NN)[:1]
+            picks.append(jnp.where((slot == pos) & (mine > 0.0), 1.0, 0.0).astype(BF16))
+        grad = block_ref[j, :, pl.ds(0, feats)]
+        rows = dot(jnp.concatenate(picks, axis=0), grad, NN).astype(BF16)
+        for q in range(2):
+            rows_ref[q, pl.ds(j * slots, slots), :] = rows[q * slots : (q + 1) * slots]
+        low_ref[j] = dot(second, grad, NT).astype(BF16)
+    chunk_product(copies, rows_ref, tiles_ref, outs)
+
+
+def next_chunk_kernel(chunk, chunks, at_ref, rows_ref, *rest):
+    downs = rest[:2]
+    *outs, tiles_ref, sems = rest[2:]
+    copies = weight_copies(chunk, chunks, at_ref, downs, tiles_ref, sems)
+    for copy in copies:
+        copy.start()
+    chunk_product(copies, rows_ref, tiles_ref, outs)
+
+
+SMEM = pl.BlockSpec(memory_space=pltpu.SMEM)
+VMEM = pl.BlockSpec(memory_space=pltpu.VMEM)
+
+
+def chunk_call(at, chunk, chunks, source, seconds, downs, shares, slots):
     rank, feats = seconds[0].shape
-    units = downs[0].shape[0] // shares
-    tiles = 3
-    tile = units // tiles
-    rows = 2 * batch * slots
-
-    def weight_at(q, i, at):
-        share = lax.rem(at[0] + i // (2 * tiles) + 1, shares)
-        turn = lax.rem(i // tiles, 2)
-        idle = (tiles - 1) * (1 - q)
-        return (share * tiles + jnp.where(turn == q, lax.rem(i, tiles), idle), 0)
-
-    return call(
-        functools.partial(expert_rows_kernel, slots, tiles, shares, batch, feats, 3 * rank),
-        "expert_rows",
-        at,
-        [*grads, *seconds, *downs, *after],
-        [whole((toks, wide))] * batch
-        + [whole((rank, feats))] * 2
-        + [pl.BlockSpec((tile, feats), functools.partial(weight_at, q)) for q in range(2)]
+    units = downs[0].shape[0] // shares // chunks
+    if chunk == 0:
+        groups, toks, wide = source.shape
+        kernel = functools.partial(first_chunk_kernel, chunks, 3 * rank)
+        arrays = [at, in_hbm(source), *seconds, in_hbm(downs[0]), downs[1]]
+        in_specs = [SMEM, ANY, VMEM, VMEM, ANY, ANY]
+        extra_outs = [
+            jax.ShapeDtypeStruct((2, groups * slots, feats), BF16),
+            jax.ShapeDtypeStruct((groups, 2 * rank, toks), BF16),
+        ]
+        extra_scratch = [pltpu.VMEM((groups, toks, wide), BF16)]
+        extra_sems = [pltpu.SemaphoreType.DMA((groups,))]
+    else:
+        groups = source.shape[1] // slots
+        kernel = functools.partial(next_chunk_kernel, chunk, chunks)
+        arrays = [at, source, in_hbm(downs[0]), downs[1]]
+        in_specs = [SMEM, VMEM, ANY, ANY]
+        extra_outs, extra_scratch, extra_sems = [], [], []
+    outs = [jax.ShapeDtypeStruct((groups, 2 * slots, units), BF16)] * shares + extra_outs
+    return pl.pallas_call(
+        kernel,
+        in_specs=in_specs,
+        out_specs=[VMEM] * len(outs),
+        out_shape=outs,
+        scratch_shapes=extra_scratch
+        + [pltpu.VMEM((2, shares, units, feats), BF16)]
+        + extra_sems
+        + [pltpu.SemaphoreType.DMA((2 * shares,))],
+        compiler_params=PARAMS,
+        cost_estimate=SMALL,
+        name="chunk_product",
+    )(*arrays)
+
+
+def collect_kernel(at_ref, extra_ref, *rest):
+    first_ref = rest[-1]
+    groups, rank, units = first_ref.shape
+    wide = units // 3
+    for o in range(groups):
+        for k in range(3):
+            first_ref[o, :, pl.ds(k * wide, wide)] = extra_ref[o, pl.ds(k * rank, rank), :]
+
+
+def collect_call(at, grads, rank, feats, after):
+    groups, toks, wide = grads.shape
+    extra = wide - feats
+    shape = (groups, rank, 3 * extra)
+    return call(
+        collect_kernel,
+        "collect_first",
+        at,
+        [in_hbm(grads), *after],
+        [pl.BlockSpec((groups, toks, extra), lambda i, at: (0, 0, feats // extra))]
         + [ANY] * len(after),
-        [((rows, units), BF16)] * shares + [((batch, 2 * rank, toks), BF16)],
-        [whole((rows, units))] * shares + [whole((batch, 2 * rank, toks))],
-        grid=(shares * 2 * tiles,),
-        scratch=[pltpu.VMEM((2, batch * slots, feats), BF16)],
-    )
-
-
-def share_sum_kernel(parts, slots, at_ref, *refs):
-    outs = refs[parts:]
-    for k, out_ref in enumerate(outs):
-        for q in range(2):
-            at = pl.ds((q * len(outs) + k) * slots, slots)
-            total = refs[0][at, :].astype(F32)
-            for part in refs[1:parts]:
-                total = total + part[at, :].astype(F32)
-            out_ref[pl.ds(q * slots, slots), :] = total.astype(BF16)
-
-
-def share_sum_call(at, parts, batch, slots):
-    rows, units = parts[0].shape
-    shape = (2 * slots, units)
-    return call(
-        functools.partial(share_sum_kernel, len(parts), slots),
-        "share_sum",
-        at,
-        parts,
-        [whole((rows, units))] * len(parts),
-        [(shape, BF16)] * batch,
-        [whole(shape)] * batch,
-    )
-
-
-def collect_kernel(parts, at_ref, *refs):
-    low_ref, first_ref = refs[-2:]
-    rank = first_ref.shape[1]
-    o = 0
-    for ref in refs[:parts]:
-        for k in range(ref.shape[0]):
-            low_ref[lax.bitwise_xor(at_ref[1], o)] = ref[k]
-            o += 1
-    for o, ref in enumerate(refs[parts:-2]):
-        wide = ref.shape[1]
-        for k in range(3):
-            first_ref[o, :, pl.ds(k * wide, wide)] = ref[pl.ds(k * rank, rank), :]
-
-
-def collect_call(at, lows, grads, feats):
-    groups, (toks, wide) = len(grads), grads[0].shape
-    rank = lows[0].shape[1] // 2
-    extra = wide - feats
-    low_shape, first_shape = (groups, 2 * rank, toks), (groups, rank, 3 * extra)
-    return call(
-        functools.partial(collect_kernel, len(lows)),
-        "collect_blocks",
-        at,
-        [*lows, *grads],
-        [whole(b.shape) for b in lows]
-        + [pl.BlockSpec((toks, extra), lambda i, at: (0, feats // extra))] * groups,
-        [(low_shape, BF16), (first_shape, BF16)],
-        [whole(low_shape), whole(first_shape)],
-    )
+        [(shape, BF16)],
+        [whole(shape)],
+    )[0]
 
 
 def low_dense_kernel(at_ref, *refs):
@@ -238,9 +250,9 @@
     groups, both, _ = refs[0].shape
     rank = both // 2
     for o in range(groups):
-        total = refs[0][lax.bitwise_xor(at_ref[1], o)].astype(F32)
+        total = refs[0][o].astype(F32)
         for ref in refs[1:-2]:
-            total = total + ref[lax.bitwise_xor(at_ref[1], o)].astype(F32)
+            total = total + ref[o].astype(F32)
         for q in range(2):
             at = pl.ds((q * groups + o) * rank, rank)
             sum_ref[at, :] = total[q * rank : (q + 1) * rank]
@@ -280,7 +292,7 @@
         functools.partial(lowrank_hid_kernel, groups),
         "lowrank_hid",
         at,
-        [index, hid, *firsts],
+        [index, in_hbm(hid), *firsts],
         [
             pl.BlockSpec((toks // steps, top), lambda i, at: (i, 0)),
             pl.BlockSpec((pairs // steps, units), lambda i, at: (i, 0)),
@@ -307,7 +319,7 @@
     for o in range(groups):
         for q in range(2):
             at = (q * groups + o) * rank
-            out_ref[lax.bitwise_xor(at_ref[1], o), pl.ds(q * rank, rank), :] = scaled[at : at + rank]
+            out_ref[o, pl.ds(q * rank, rank), :] = scaled[at : at + rank]
 
 
 def scaled_hid_call(at, index, prob, parts, groups):
@@ -325,12 +337,11 @@
     )[0]
 
 
-def second_grad_kernel(at_ref, scaled_ref, *refs):
-    grads, outs = refs[:-2], refs[-2:]
+def second_grad_kernel(at_ref, scaled_ref, grad_ref, *outs):
     rank, tile = outs[0].shape
     total = jnp.zeros((2 * rank, tile), F32)
-    for o, grad_ref in enumerate(grads):
-        total = total + dot(scaled_ref[lax.bitwise_xor(at_ref[1], o)], grad_ref[...], NN)
+    for o in range(scaled_ref.shape[0]):
+        total = total + dot(scaled_ref[o], grad_ref[o], NN)
     for q, out_ref in enumerate(outs):
         out_ref[...] = adapter_scale * total[q * rank : (q + 1) * rank]
 
@@ -344,8 +355,8 @@
         second_grad_kernel,
         "second_grad",
         at,
-        [scaled, *grads],
-        [whole(scaled.shape)] + [pl.BlockSpec((toks, tile), lambda i, at: (0, i))] * groups,
+        [scaled, in_hbm(grads)],
+        [whole(scaled.shape), pl.BlockSpec((groups, toks, tile), lambda i, at: (0, 0, i))],
         [((both // 2, feats), F32)] * 2,
         [block] * 2,
         grid=(steps,),
@@ -387,7 +398,7 @@
         functools.partial(first_grad_kernel, groups, steps),
         "first_grad",
         at,
-        [index, prob, low, hid],
+        [index, prob, low, in_hbm(hid)],
         [
             pl.BlockSpec((toks // steps, top), lambda i, at: (i, 0)),
             pl.BlockSpec((toks // steps, top), lambda i, at: (i, 0)),
@@ -404,7 +415,7 @@
 def first_sum_kernel(at_ref, keep_ref, got_ref, out_ref):
     for o in range(keep_ref.shape[0]):
         total = keep_ref[o] + got_ref[o].astype(F32)
-        out_ref[lax.bitwise_xor(at_ref[1], o)] = total.astype(BF16)
+        out_ref[o] = total.astype(BF16)
 
 
 def first_sum_call(at, keep, got):
@@ -420,19 +431,24 @@
     )[0]
 
 
-def finish_kernel(count, slots, at_ref, index_all_ref, index_ref, prob_ref, low_ref, hid_ref, *rest):
-    firsts, back = rest[:2], rest[2 : 2 + count]
-    out_ref, sum_ref, all_ref, place_ref = rest[2 + count :]
+def finish_kernel(chunks, at_ref, index_all_ref, index_ref, prob_ref, low_ref, hid_ref, *rest):
+    firsts, back = rest[:2], rest[2 : 2 + chunks]
+    out_ref, sum_ref, all_ref, place_ref = rest[2 + chunks :]
     top = index_ref.shape[1]
     toks = index_all_ref.shape[0]
-    experts = 2 * count
+    groups, both, units = back[0].shape
+    slots = both // 2
+    experts = 2 * groups
 
     @pl.when(pl.program_id(0) == 0)
     def _():
-        for o, ref in enumerate(back):
-            for q in range(2):
-                all_ref[pl.ds((q * count + o) * slots, slots), :] = ref[pl.ds(q * slots, slots), :]
-        experts_all = relative(at_ref, index_all_ref[...], count)
+        for c, ref in enumerate(back):
+            for o in range(groups):
+                for q in range(2):
+                    all_ref[pl.ds((q * groups + o) * slots, slots), pl.ds(c * units, units)] = ref[
+                        o, pl.ds(q * slots, slots), :
+                    ]
+        experts_all = relative(at_ref, index_all_ref[...], groups)
         hit = jnp.zeros((toks, experts), F32)
         for k in range(top):
             hit = jnp.where(iota((toks, experts), 1) == experts_all[:, k : k + 1], 1.0, hit)
@@ -441,7 +457,7 @@
 
     pairs = hid_ref.shape[0]
     some = index_ref.shape[0]
-    column = pair_column(relative(at_ref, index_ref[...], count).astype(F32))
+    column = pair_column(relative(at_ref, index_ref[...], groups).astype(F32))
     place = spread_pairs(place_ref[pl.ds(pl.program_id(0) * some, some), :], top)
     mine = iota((pairs, experts), 1) == column.astype(jnp.int32)
     target = column * slots + jnp.sum(jnp.where(mine, place, 0.0), axis=1, keepdims=True)
@@ -463,25 +479,24 @@
 def finish_call(at, index, prob, low, hid, firsts, back):
     (toks, top), (pairs, units) = index.shape, hid.shape
     width = low.shape[1]
-    both = back[0].shape[0]
+    groups, both, _ = back[0].shape
     steps = 4
-    count = len(back)
 
     def rows(n, columns):
         return pl.BlockSpec((n // steps, columns), lambda i, at: (i, 0))
 
     return call(
-        functools.partial(finish_kernel, count, both // 2),
+        functools.partial(finish_kernel, len(back)),
         "finish",
         at,
-        [index, index, prob, low, hid, *firsts, *back],
+        [index, index, prob, low, in_hbm(hid), *firsts, *back],
         [whole(index.shape), rows(toks, top), rows(toks, top), rows(toks, width), rows(pairs, units)]
         + [whole(firsts[0].shape)] * 2
-        + [whole((both, units))] * count,
+        + [whole(back[0].shape)] * len(back),
         [((pairs, units), BF16), ((toks, top), F32)],
         [rows(pairs, units), rows(toks, top)],
         grid=(steps,),
-        scratch=[pltpu.VMEM((count * both, units), BF16), pltpu.VMEM((toks, 2 * count), F32)],
+        scratch=[pltpu.VMEM((groups * both, units), BF16), pltpu.VMEM((toks, 2 * groups), F32)],
     )
 
 
@@ -502,42 +517,36 @@
     def all_shares(x):
         return [x] + [turn(x, k) for k in range(1, shares)]
 
-    def flip(x, mask):
-        return lax.ppermute(x, "ep", [(i, i ^ mask) for i in range(groups)])
-
     def swap(x):
         return lax.ppermute(x, "sub", [(0, 1), (1, 0)])
 
     def exchange(x):
         return lax.all_to_all(x, "ep", split_axis=0, concat_axis=0, tiled=True)
 
-    blocks = [pack_call(at, grad, first[0], index)]
-    for o in range(1, groups):
-        last = o & -o
-        blocks.append(flip(blocks[o ^ last], last))
-        if last == o and o >= 4:
-            blocks[o], blocks[o - 1] = lax.optimization_barrier((blocks[o], blocks[o - 1]))
-    downs = [pltpu.with_memory_space_constraint(down[0], pltpu.HBM), swap(down[0])]
+    grads = lax.all_gather(pack_call(at, grad, first[0], index), "ep")
+    downs = [down[0], swap(down[0])]
     seconds = [second[0], swap(second[0])]
 
-    back, lows, after = [], [], [[], []]
-    for o in range(0, groups, 2):
-        *give, keep, low = expert_rows_call(
-            at, blocks[o : o + 2], seconds, downs, shares, slots, after[-2]
+    back = []
+    for c in range(CHUNKS):
+        *give, keep = chunk_call(
+            at, c, CHUNKS, rows if c else grads, seconds, downs, shares, slots
         )
-        parts = [keep] + [turn(x, k + 1) for k, x in enumerate(give)]
-        sums = share_sum_call(at, parts, 2, slots)
-        back += [flip(rows, o + k) if o + k else rows for k, rows in enumerate(sums)]
-        lows.append(low)
-        after.append(sums[:1])
+        if c == 0:
+            rows, low_grad = give[-1], keep
+            *give, keep = give[:-1]
+        total = keep.astype(F32)
+        for k, x in enumerate(give):
+            total = total + turn(x, k + 1).astype(F32)
+        back.append(exchange(total.astype(BF16)))
 
     hid = hidden.reshape(pairs, units)
-    low_grad, first_own = collect_call(at, lows, blocks, feats)
+    first_own = collect_call(at, grads, rank, feats, [low_grad])
     firsts = [x.reshape(groups * rank, units) for x in (first_own, swap(first_own))]
 
     low_hid = all_shares(lowrank_hid_call(at, index, hid, firsts, groups))
     scaled_hid = exchange(scaled_hid_call(at, index, weight, low_hid, groups))
-    second_keep, second_give = second_grad_call(at, scaled_hid, blocks, feats)
+    second_keep, second_give = second_grad_call(at, scaled_hid, grads, feats)
     second_grad = second_keep + swap(second_give)
 
     low_grad = low_dense_call(at, all_shares(exchange(low_grad)))

time: 267 us -> 263 us (0.985)
  the two profiles are of different devices: /device:TPU:0 before, /device:TPU:8 now
where the time goes in v5:
time: 263 us; the launch traced here: 260 us
  waiting for transfers between devices  122 us (46%)
  Pallas kernels  58.6 us (22%)
  starting transfers between devices  42.7 us (16%)
  local copies, waits for them, and re-layouts  16.1 us (6%)
  between operations  14.2 us (5%)
  other arithmetic  6.53 us (2%)
    all_gather x1, waiting for transfers between devices, body(): grads = lax.all_gather(pack_call(at, grad, first[0], index), 'ep')  66.9 us
    ppermute x6, waiting for transfers between devices, turn(): lax.ppermute(x, 'rep', [(r, (r + offset) % shares) for r in range(shares)])  41 us
    all_to_all x6, starting transfers between devices, exchange(): return lax.all_to_all(x, 'ep', split_axis=0, concat_axis=0, tiled=True)  33.3 us
    pallas_call x3, Pallas kernels, chunk_call(): pl.pallas_call(kernel, in_specs=in_specs, out_specs=[VMEM] * len(outs), o...  29.9 us
    pallas_call x9, Pallas kernels, call(): pl.pallas_call(kernel, grid_spec=pltpu.PrefetchScalarGridSpec(num_scalar_...  28.7 us
    unnamed x40, local copies, waits for them, and re-layouts  16.1 us
    ppermute x5, waiting for transfers between devices, swap(): return lax.ppermute(x, 'sub', [(0, 1), (1, 0)])  10.1 us
    ppermute x6, starting transfers between devices, turn(): lax.ppermute(x, 'rep', [(r, (r + offset) % shares) for r in range(shares)])  8.14 us
  transfers between devices with their start and end apart: 18, of which 9 were waited for; matrix products, arithmetic and copies ran while one was open for 3% of the time, Pallas kernels for 16%

profile of v5, /device:TPU:8, one launch (start us, length us, event | category | flops | bytes accessed | tf_op | source)
XLA Modules:
  0.0 260.4 jit_solution(18362552777013460901)
XLA Ops:
  7.2 0.0 all-gather.3.cloned.1.call-start
  7.2 0.8 copy.13.index_ref.index_all_ref
  8.0 1.0 copy.11
  9.0 0.1 pad_add_fusion.at_ref
  9.1 1.0 copy-done.14
  10.1 1.6 pack_block.1
  11.7 0.0 all-gather.3.cloned.1.call-update
  11.7 0.1 collective-permute-start.1
  11.8 0.5 collective-permute-start
  12.3 5.7 %collective-permute-done.rest_1_ = bf16[32,2048]{1,0:T(8,128)(2,1)S(1)} collective-permute-done((bf16[32,2048]{1,0:T(8,128)(2,1)S(1)}, bf16[32,2048]{1,0:T(8,128)(2,1)S(1)}, u32[]{:S(2)}, u32[]{:S(2)}) %collective-permute-start) | collective-permute-done | bytes 131104 | tf_op jit(solution)/shard_map/ppermute | solution.py:521
  18.0 4.3 %collective-permute-done.1.rest_3_.rest_1_ = bf16[1536,2048]{1,0:T(8,128)(2,1)S(1)} collective-permute-done((bf16[1536,2048]{1,0:T(8,128)(2,1)}, bf16[1536,2048]{1,0:T(8,128)(2,1)S(1)}, u32[]{:S(2)}, u32[]{:S(2)}) %collective-permute-start.1) | collective-permute-done | bytes 6291488 | tf_op jit(solution)/shard_map/ppermute | solution.py:521
  22.3 2.7 %copy-done = bf16[1536,2048]{1,0:T(8,128)(2,1)} copy-done((bf16[1536,2048]{1,0:T(8,128)(2,1)}, bf16[1536,2048]{1,0:T(8,128)(2,1)S(1)}, u32[]{:S(2)}) %copy-start) | copy-done | bytes 6291480
  25.0 66.9 %all-gather.3.cloned.1.call-done = bf16[1024,2304]{1,0:T(8,128)(2,1)} async-done(((bf16[128,2304]{1,0:T(8,128)(2,1)}), bf16[1024,2304]{1,0:T(8,128)(2,1)}) %all-gather.3.cloned.1.call-update) | async-done | bytes 4718608 | tf_op jit(solution)/shard_map/all_gather | solution.py:526
  91.9 2.8 %copy-done.1 = bf16[1536,2048]{1,0:T(8,128)(2,1)S(1)} copy-done((bf16[1536,2048]{1,0:T(8,128)(2,1)S(1)}, bf16[1536,2048]{1,0:T(8,128)(2,1)}, u32[]{:S(2)}) %copy-start.1) | copy-done | bytes 6291480
  94.7 14.0 %chunk_product.3 = (bf16[8,160,256]{2,1,0:T(8,128)(2,1)S(1)}, bf16[8,160,256]{2,1,0:T(8,128)(2,1)S(1)}, bf16[2,640,2048]{2,1,0:T(8,128)(2,1)S(1)}, bf16[8,64,128]{2,1,0:T(8,128)(2,1)}) custom-call(s32[3]{0:T(128)S(1)} %pad_add_fusion.at_ref, bf16[8,128,2304]{2,1,0:T(8,128)(2,1)} %bitcast.27, bf16[32,2048]{1,0:T(8,128)(2,1)S(1)} %bitcast.22, ...), custom_call_target="tpu_custom_call" | custom-call | flops 1 | bytes 1 | tf_op jit(solution)/shard_map/chunk_product/pallas_call | solution.py:208
  108.7 0.0 copy-start.10
  108.7 0.8 copy-done.10
  109.5 2.0 collect_first.1
  111.6 0.1 collective-permute-start.3
  111.6 0.2 copy-done.4
  111.8 8.0 %chunk_product.5 = (bf16[8,160,256]{2,1,0:T(8,128)(2,1)S(1)}, bf16[8,160,256]{2,1,0:T(8,128)(2,1)S(1)}) custom-call(s32[3]{0:T(128)S(1)} %pad_add_fusion.at_ref, bf16[2,640,2048]{2,1,0:T(8,128)(2,1)S(1)} %get-tuple-element.21.rows_ref, bf16[1536,2048]{1,0:T(8,128)(2,1)} %bitcast.25, bf16[1536,2048]{1,0:T(8,128)(2,1)S(1)} %copy-done.2), custom_call_target="tpu_custom_call" | custom-call | flops 1 | bytes 1 | tf_op jit(solution)/shard_map/chunk_product/pallas_call | solution.py:208
  119.8 1.5 collective-permute-start.6
  121.4 0.0 collective-permute-done.3
  121.4 4.1 %lowrank_hid.1.refs_0_ = f32[128,512]{1,0:T(8,128)S(1)} custom-call(s32[3]{0:T(128)S(1)} %pad_add_fusion.at_ref, s32[128,8]{1,0:T(8,128)S(1)} %copy.13.index_ref.index_all_ref, bf16[1024,768]{1,0:T(8,128)(2,1)} %bitcast.30, bf16[256,768]{1,0:T(8,128)(2,1)S(1)} %bitcast.16, bf16[256,768]{1,0:T(8,128)(2,1)S(1)} %bitcast.18), custom_call_target="tpu_custom_call" | custom-call | flops 1 | bytes 1 | tf_op jit(solution)/shard_map/lowrank_hid/pallas_call | solution.py:39
  125.5 0.6 collective-permute-start.9
  126.1 4.9 %all-to-all-start = ((bf16[8,64,128]{2,1,0:T(8,128)(2,1)}), bf16[8,64,128]{2,1,0:T(8,128)(2,1)S(1)}, u32[]{:S(2)}, u32[]{:S(2)}) async-start(bf16[8,64,128]{2,1,0:T(8,128)(2,1)} %get-tuple-element.18.rest_0_), calls=%async_computation | async-start | bytes 262144 | tf_op jit(solution)/shard_map/all_to_all | solution.py:524
  131.0 0.1 copy.15.prob_ref
  131.1 11.3 %collective-permute-done.9.refs_1_ = f32[128,512]{1,0:T(8,128)S(1)} collective-permute-done((f32[128,512]{1,0:T(8,128)S(1)}, f32[128,512]{1,0:T(8,128)S(1)}, u32[]{:S(2)}, u32[]{:S(2)}) %collective-permute-start.9) | collective-permute-done | bytes 262176 | tf_op jit(solution)/shard_map/ppermute | solution.py:515
  142.5 1.6 scaled_hid.1
  144.1 4.8 %all-to-all-start.5 = ((bf16[8,64,128]{2,1,0:T(8,128)(2,1)}), bf16[8,64,128]{2,1,0:T(8,128)(2,1)S(1)}, u32[]{:S(2)}, u32[]{:S(2)}) async-start(bf16[8,64,128]{2,1,0:T(8,128)(2,1)} %scaled_hid.1), calls=%async_computation.5 | async-start | bytes 262144 | tf_op jit(solution)/shard_map/all_to_all | solution.py:524
  148.9 1.0 add_convert_fusion
  149.9 4.2 %all-to-all-done.5.scaled_ref = bf16[8,64,128]{2,1,0:T(8,128)(2,1)S(1)} async-done(((bf16[8,64,128]{2,1,0:T(8,128)(2,1)}), bf16[8,64,128]{2,1,0:T(8,128)(2,1)S(1)}, u32[]{:S(2)}, u32[]{:S(2)}) %all-to-all-start.5) | async-done | bytes 131104 | tf_op jit(solution)/shard_map/all_to_all | solution.py:524
  154.1 5.6 %all-to-all-start.3 = ((bf16[8,160,256]{2,1,0:T(8,128)(2,1)}), bf16[8,160,256]{2,1,0:T(8,128)(2,1)S(1)}, u32[]{:S(2)}, u32[]{:S(2)}) async-start(bf16[8,160,256]{2,1,0:T(8,128)(2,1)} %add_convert_fusion), calls=%async_computation.3 | async-start | bytes 1310720 | tf_op jit(solution)/shard_map/all_to_all | solution.py:524
  159.7 2.8 %copy-done.3 = bf16[1536,2048]{1,0:T(8,128)(2,1)S(1)} copy-done((bf16[1536,2048]{1,0:T(8,128)(2,1)S(1)}, bf16[1536,2048]{1,0:T(8,128)(2,1)}, u32[]{:S(2)}) %copy-start.3) | copy-done | bytes 6291480
  162.5 2.5 copy-done.5
  164.9 8.0 %chunk_product.4 = (bf16[8,160,256]{2,1,0:T(8,128)(2,1)S(1)}, bf16[8,160,256]{2,1,0:T(8,128)(2,1)S(1)}) custom-call(s32[3]{0:T(128)S(1)} %pad_add_fusion.at_ref, bf16[2,640,2048]{2,1,0:T(8,128)(2,1)S(1)} %copy-done.5, bf16[1536,2048]{1,0:T(8,128)(2,1)} %bitcast.26, bf16[1536,2048]{1,0:T(8,128)(2,1)S(1)} %copy-done.3), custom_call_target="tpu_custom_call" | custom-call | flops 1 | bytes 1 | tf_op jit(solution)/shard_map/chunk_product/pallas_call | solution.py:208
  172.9 1.5 collective-permute-start.5
  174.5 13.3 %collective-permute-done.5 = bf16[8,160,256]{2,1,0:T(8,128)(2,1)S(1)} collective-permute-done((bf16[8,160,256]{2,1,0:T(8,128)(2,1)S(1)}, bf16[8,160,256]{2,1,0:T(8,128)(2,1)S(1)}, u32[]{:S(2)}, u32[]{:S(2)}) %collective-permute-start.5) | collective-permute-done | bytes 655392 | tf_op jit(solution)/shard_map/ppermute | solution.py:515
  187.8 1.0 add_convert_fusion.1
  188.8 6.0 %all-to-all-start.2 = ((bf16[8,160,256]{2,1,0:T(8,128)(2,1)}), bf16[8,160,256]{2,1,0:T(8,128)(2,1)S(1)}, u32[]{:S(2)}, u32[]{:S(2)}) async-start(bf16[8,160,256]{2,1,0:T(8,128)(2,1)} %add_convert_fusion.1), calls=%async_computation.2 | async-start | bytes 1310720 | tf_op jit(solution)/shard_map/all_to_all | solution.py:524
  194.8 1.5 collective-permute-start.4
  196.3 11.8 %collective-permute-done.4 = bf16[8,160,256]{2,1,0:T(8,128)(2,1)S(1)} collective-permute-done((bf16[8,160,256]{2,1,0:T(8,128)(2,1)S(1)}, bf16[8,160,256]{2,1,0:T(8,128)(2,1)S(1)}, u32[]{:S(2)}, u32[]{:S(2)}) %collective-permute-start.4) | collective-permute-done | bytes 655392 | tf_op jit(solution)/shard_map/ppermute | solution.py:515
  208.2 1.0 add_convert_fusion.2
  209.2 6.0 %all-to-all-start.1 = ((bf16[8,160,256]{2,1,0:T(8,128)(2,1)}), bf16[8,160,256]{2,1,0:T(8,128)(2,1)S(1)}, u32[]{:S(2)}, u32[]{:S(2)}) async-start(bf16[8,160,256]{2,1,0:T(8,128)(2,1)} %add_convert_fusion.2), calls=%async_computation.1 | async-start | bytes 1310720 | tf_op jit(solution)/shard_map/all_to_all | solution.py:524
  215.2 1.5 collective-permute-start.2
  216.7 3.5 %collective-permute-done.2.refs_1_ = bf16[8,64,128]{2,1,0:T(8,128)(2,1)S(1)} collective-permute-done((bf16[8,64,128]{2,1,0:T(8,128)(2,1)S(1)}, bf16[8,64,128]{2,1,0:T(8,128)(2,1)S(1)}, u32[]{:S(2)}, u32[]{:S(2)}) %collective-permute-start.2) | collective-permute-done | bytes 131104 | tf_op jit(solution)/shard_map/ppermute | solution.py:515
  220.2 0.7 low_dense.1.low_ref
  220.8 4.8 %first_grad.1 = (f32[8,32,768]{2,1,0:T(8,128)S(1)}, bf16[8,32,768]{2,1,0:T(8,128)(2,1)S(1)}) custom-call(s32[3]{0:T(128)S(1)} %pad_add_fusion.at_ref, s32[128,8]{1,0:T(8,128)S(1)} %copy.13.index_ref.index_all_ref, bf16[128,8]{1,0:T(8,128)(2,1)S(1)} %copy.15.prob_ref, f32[128,512]{1,0:T(8,128)S(1)} %low_dense.1.low_ref, bf16[1024,768]{1,0:T(8,128)(2,1)} %bitcast.31), custom_call_target="tpu_custom_call" | custom-call | flops 1 | bytes 1 | tf_op jit(solution)/shard_map/first_grad/pallas_call | solution.py:39
  225.6 0.1 collective-permute-start.8
  225.7 4.9 %second_grad.1 = (f32[32,2048]{1,0:T(8,128)S(1)}, f32[32,2048]{1,0:T(8,128)}) custom-call(s32[3]{0:T(128)S(1)} %pad_add_fusion.at_ref, bf16[8,64,128]{2,1,0:T(8,128)(2,1)S(1)} %all-to-all-done.5.scaled_ref, bf16[8,128,2304]{2,1,0:T(8,128)(2,1)} %bitcast.29), custom_call_target="tpu_custom_call" | custom-call | flops 1 | bytes 1 | tf_op jit(solution)/shard_map/second_grad/pallas_call | solution.py:39
  230.6 0.7 copy-done.15
  231.3 0.5 collective-permute-start.10
  231.8 0.0 collective-permute-done.8.got_ref
  231.9 1.4 first_sum.1
  233.2 0.0 all-to-all-done.1.rest_2_
  233.2 6.0 %all-to-all-start.4 = ((bf16[8,32,768]{2,1,0:T(8,128)(2,1)}), bf16[8,32,768]{2,1,0:T(8,128)(2,1)}, u32[]{:S(2)}, u32[]{:S(2)}) async-start(bf16[8,32,768]{2,1,0:T(8,128)(2,1)} %first_sum.1), calls=%async_computation.4 | async-start | bytes 786432 | tf_op jit(solution)/shard_map/all_to_all | solution.py:524
  239.2 0.0 collective-permute-done.10
  239.2 1.7 add_bitcast_fusion
  240.9 7.7 %finish.1 = (bf16[1024,768]{1,0:T(8,128)(2,1)}, f32[128,8]{1,0:T(8,128)S(1)}) custom-call(s32[3]{0:T(128)S(1)} %pad_add_fusion.at_ref, s32[128,8]{1,0:T(8,128)S(1)} %copy.13.index_ref.index_all_ref, s32[128,8]{1,0:T(8,128)S(1)} %copy.13.index_ref.index_all_ref, bf16[128,8]{1,0:T(8,128)(2,1)S(1)} %copy.15.prob_ref, f32[128,512]{1,0:T(8,128)S(1)} %low_dense.1.low_ref, ...), custom_call_target="tpu_custom_call" | custom-call | flops 1 | bytes 1 | tf_op jit(solution)/shard_map/finish/pallas_call | solution.py:39
  248.6 1.5 collective-permute-start.7
  250.1 0.0 all-to-all-done.4
  250.1 1.7 convert_reduce_fusion
  251.8 1.1 collective-permute-done.7
  252.9 0.7 copy.21
  (32 shorter events, 0.1 us)
Async XLA Ops:
  7.2 4.6 %copy-start.16 = (bf16[1,32,2048]{2,1,0:T(8,128)(2,1)S(1)}, bf16[1,32,2048]{2,1,0:T(8,128)(2,1)}, u32[]{:S(2)}) copy-start(bf16[1,32,2048]{2,1,0:T(8,128)(2,1)} %param.13) | copy-start | bytes 393220
  7.2 84.8 %all-gather.3.cloned.1.call-start = ((), (), s32[]{:S(2)}) async-start(), calls=%async_computation.6 | async-start | bytes 5308416 | tf_op jit(solution)/shard_map/all_gather | solution.py:526
  9.1 1.0 copy-start.14
  11.7 10.6 %collective-permute-start.1 = (bf16[1536,2048]{1,0:T(8,128)(2,1)}, bf16[1536,2048]{1,0:T(8,128)(2,1)S(1)}, u32[]{:S(2)}, u32[]{:S(2)}) collective-permute-start(bf16[1536,2048]{1,0:T(8,128)(2,1)} %bitcast.23), channel_id=1, source_target_pairs={{0,1},{1,0},{2,3},{3,2},{4,5},{5,4},{6,7},{7,6},{8,9},{9,8},{10,11... | collective-permute-start | bytes 18874376 | tf_op jit(solution)/shard_map/ppermute | solution.py:521
  11.8 6.2 %collective-permute-start = (bf16[32,2048]{1,0:T(8,128)(2,1)S(1)}, bf16[32,2048]{1,0:T(8,128)(2,1)S(1)}, u32[]{:S(2)}, u32[]{:S(2)}) collective-permute-start(bf16[32,2048]{1,0:T(8,128)(2,1)S(1)} %bitcast.21), channel_id=1, source_target_pairs={{0,1},{1,0},{2,3},{3,2},{4,5},{5,4},{6,7},{7,6},{8,9},{9,8},{10,11... | collective-permute-start | bytes 393224 | tf_op jit(solution)/shard_map/ppermute | solution.py:521
  22.3 2.7 %copy-start = (bf16[1536,2048]{1,0:T(8,128)(2,1)}, bf16[1536,2048]{1,0:T(8,128)(2,1)S(1)}, u32[]{:S(2)}) copy-start(bf16[1536,2048]{1,0:T(8,128)(2,1)S(1)} %collective-permute-done.1.rest_3_.rest_1_) | copy-start | bytes 18874372
  91.9 2.8 %copy-start.1 = (bf16[1536,2048]{1,0:T(8,128)(2,1)S(1)}, bf16[1536,2048]{1,0:T(8,128)(2,1)}, u32[]{:S(2)}) copy-start(bf16[1536,2048]{1,0:T(8,128)(2,1)} %copy-done) | copy-start | bytes 18874372
  94.7 17.1 %copy-start.2 = (bf16[1536,2048]{1,0:T(8,128)(2,1)S(1)}, bf16[1536,2048]{1,0:T(8,128)(2,1)}, u32[]{:S(2)}) copy-start(bf16[1536,2048]{1,0:T(8,128)(2,1)} %copy-done) | copy-start | bytes 18874372
  108.7 0.8 copy-start.10
  109.5 2.3 copy-start.4
  111.6 9.8 %copy-start.6 = (bf16[8,32,768]{2,1,0:T(8,128)(2,1)}, bf16[8,32,768]{2,1,0:T(8,128)(2,1)S(1)}, u32[]{:S(2)}) copy-start(bf16[8,32,768]{2,1,0:T(8,128)(2,1)S(1)} %collect_first.1) | copy-start | bytes 1179652
  111.6 9.8 %collective-permute-start.3 = (bf16[8,32,768]{2,1,0:T(8,128)(2,1)S(1)}, bf16[8,32,768]{2,1,0:T(8,128)(2,1)S(1)}, u32[]{:S(2)}, u32[]{:S(2)}) collective-permute-start(bf16[8,32,768]{2,1,0:T(8,128)(2,1)S(1)} %collect_first.1), channel_id=1, source_target_pairs={{0,1},{1,0},{2,3},{3,2},{4,5},{5,4},{6,7},{7,6},{8,9},{9,8},{10,11... | collective-permute-start | bytes 1179656 | tf_op jit(solution)/shard_map/ppermute | solution.py:521
  119.8 5.7 %copy-start.12 = (bf16[8,160,256]{2,1,0:T(8,128)(2,1)}, bf16[8,160,256]{2,1,0:T(8,128)(2,1)S(1)}, u32[]{:S(2)}) copy-start(bf16[8,160,256]{2,1,0:T(8,128)(2,1)S(1)} %get-tuple-element.24) | copy-start | bytes 1966084
  119.8 29.0 %collective-permute-start.6 = (bf16[8,160,256]{2,1,0:T(8,128)(2,1)S(1)}, bf16[8,160,256]{2,1,0:T(8,128)(2,1)S(1)}, u32[]{:S(2)}, u32[]{:S(2)}) collective-permute-start(bf16[8,160,256]{2,1,0:T(8,128)(2,1)S(1)} %get-tuple-element.25), channel_id=1, source_target_pairs={{0,2},{2,0},{1,3},{3,1},{4,6},{6,4},{5,7},{7,5},{8,10},{10,8},{9,1... | collective-permute-start | bytes 1966088 | tf_op jit(solution)/shard_map/ppermute | solution.py:515
  121.4 4.1 %copy-start.8 = (bf16[8,32,768]{2,1,0:T(8,128)(2,1)}, bf16[8,32,768]{2,1,0:T(8,128)(2,1)S(1)}, u32[]{:S(2)}) copy-start(bf16[8,32,768]{2,1,0:T(8,128)(2,1)S(1)} %collective-permute-done.3) | copy-start | bytes 1179652
  121.4 9.6 %copy-start.17 = (bf16[128,8]{0,1:T(8,128)(2,1)S(1)}, bf16[128,8]{0,1:T(8,128)(2,1)}, u32[]{:S(2)}) copy-start(bf16[128,8]{0,1:T(8,128)(2,1)} %param.10) | copy-start | bytes 6148
  125.5 17.0 %collective-permute-start.9 = (f32[128,512]{1,0:T(8,128)S(1)}, f32[128,512]{1,0:T(8,128)S(1)}, u32[]{:S(2)}, u32[]{:S(2)}) collective-permute-start(f32[128,512]{1,0:T(8,128)S(1)} %lowrank_hid.1.refs_0_), channel_id=1, source_target_pairs={{0,2},{2,0},{1,3},{3,1},{4,6},{6,4},{5,7},{7,5},{8,10},{10,8},{9,1... | collective-permute-start | bytes 786440 | tf_op jit(solution)/shard_map/ppermute | solution.py:515
  126.1 22.7 %copy-start.13 = (bf16[8,160,256]{2,1,0:T(8,128)(2,1)S(1)}, bf16[8,160,256]{2,1,0:T(8,128)(2,1)}, u32[]{:S(2)}) copy-start(bf16[8,160,256]{2,1,0:T(8,128)(2,1)} %copy-done.12) | copy-start | bytes 1966084
  126.1 18.0 %all-to-all-start = ((bf16[8,64,128]{2,1,0:T(8,128)(2,1)}), bf16[8,64,128]{2,1,0:T(8,128)(2,1)S(1)}, u32[]{:S(2)}, u32[]{:S(2)}) async-start(bf16[8,64,128]{2,1,0:T(8,128)(2,1)} %get-tuple-element.18.rest_0_), calls=%async_computation | async-start | bytes 262144 | tf_op jit(solution)/shard_map/all_to_all | solution.py:524
  144.1 10.0 %all-to-all-start.5 = ((bf16[8,64,128]{2,1,0:T(8,128)(2,1)}), bf16[8,64,128]{2,1,0:T(8,128)(2,1)S(1)}, u32[]{:S(2)}, u32[]{:S(2)}) async-start(bf16[8,64,128]{2,1,0:T(8,128)(2,1)} %scaled_hid.1), calls=%async_computation.5 | async-start | bytes 262144 | tf_op jit(solution)/shard_map/all_to_all | solution.py:524
  154.1 34.8 %all-to-all-start.3 = ((bf16[8,160,256]{2,1,0:T(8,128)(2,1)}), bf16[8,160,256]{2,1,0:T(8,128)(2,1)S(1)}, u32[]{:S(2)}, u32[]{:S(2)}) async-start(bf16[8,160,256]{2,1,0:T(8,128)(2,1)} %add_convert_fusion), calls=%async_computation.3 | async-start | bytes 1310720 | tf_op jit(solution)/shard_map/all_to_all | solution.py:524
  159.7 2.8 %copy-start.3 = (bf16[1536,2048]{1,0:T(8,128)(2,1)S(1)}, bf16[1536,2048]{1,0:T(8,128)(2,1)}, u32[]{:S(2)}) copy-start(bf16[1536,2048]{1,0:T(8,128)(2,1)} %copy-done) | copy-start | bytes 18874372
  162.5 2.5 copy-start.5
  172.9 14.9 %collective-permute-start.5 = (bf16[8,160,256]{2,1,0:T(8,128)(2,1)S(1)}, bf16[8,160,256]{2,1,0:T(8,128)(2,1)S(1)}, u32[]{:S(2)}, u32[]{:S(2)}) collective-permute-start(bf16[8,160,256]{2,1,0:T(8,128)(2,1)S(1)} %get-tuple-element.23), channel_id=1, source_target_pairs={{0,2},{2,0},{1,3},{3,1},{4,6},{6,4},{5,7},{7,5},{8,10},{10,8},{9,1... | collective-permute-start | bytes 1966088 | tf_op jit(solution)/shard_map/ppermute | solution.py:515
  187.8 20.4 %copy-start.11 = (bf16[8,160,256]{2,1,0:T(8,128)(2,1)S(1)}, bf16[8,160,256]{2,1,0:T(8,128)(2,1)}, u32[]{:S(2)}) copy-start(bf16[8,160,256]{2,1,0:T(8,128)(2,1)} %copy-done.10) | copy-start | bytes 1966084
  188.8 20.4 %all-to-all-start.2 = ((bf16[8,160,256]{2,1,0:T(8,128)(2,1)}), bf16[8,160,256]{2,1,0:T(8,128)(2,1)S(1)}, u32[]{:S(2)}, u32[]{:S(2)}) async-start(bf16[8,160,256]{2,1,0:T(8,128)(2,1)} %add_convert_fusion.1), calls=%async_computation.2 | async-start | bytes 1310720 | tf_op jit(solution)/shard_map/all_to_all | solution.py:524
  194.8 13.3 %collective-permute-start.4 = (bf16[8,160,256]{2,1,0:T(8,128)(2,1)S(1)}, bf16[8,160,256]{2,1,0:T(8,128)(2,1)S(1)}, u32[]{:S(2)}, u32[]{:S(2)}) collective-permute-start(bf16[8,160,256]{2,1,0:T(8,128)(2,1)S(1)} %get-tuple-element.20), channel_id=1, source_target_pairs={{0,2},{2,0},{1,3},{3,1},{4,6},{6,4},{5,7},{7,5},{8,10},{10,8},{9,1... | collective-permute-start | bytes 1966088 | tf_op jit(solution)/shard_map/ppermute | solution.py:515
  209.2 24.0 %all-to-all-start.1 = ((bf16[8,160,256]{2,1,0:T(8,128)(2,1)}), bf16[8,160,256]{2,1,0:T(8,128)(2,1)S(1)}, u32[]{:S(2)}, u32[]{:S(2)}) async-start(bf16[8,160,256]{2,1,0:T(8,128)(2,1)} %add_convert_fusion.2), calls=%async_computation.1 | async-start | bytes 1310720 | tf_op jit(solution)/shard_map/all_to_all | solution.py:524
  215.2 5.0 %collective-permute-start.2 = (bf16[8,64,128]{2,1,0:T(8,128)(2,1)S(1)}, bf16[8,64,128]{2,1,0:T(8,128)(2,1)S(1)}, u32[]{:S(2)}, u32[]{:S(2)}) collective-permute-start(bf16[8,64,128]{2,1,0:T(8,128)(2,1)S(1)} %all-to-all-done.refs_0_), channel_id=1, source_target_pairs={{0,2},{2,0},{1,3},{3,1},{4,6},{6,4},{5,7},{7,5},{8,10},{10,8},{9,1... | collective-permute-start | bytes 393224 | tf_op jit(solution)/shard_map/ppermute | solution.py:515
  225.6 6.2 %collective-permute-start.8 = (bf16[8,32,768]{2,1,0:T(8,128)(2,1)S(1)}, bf16[8,32,768]{2,1,0:T(8,128)(2,1)S(1)}, u32[]{:S(2)}, u32[]{:S(2)}) collective-permute-start(bf16[8,32,768]{2,1,0:T(8,128)(2,1)S(1)} %get-tuple-element.29), channel_id=1, source_target_pairs={{0,1},{1,0},{2,3},{3,2},{4,5},{5,4},{6,7},{7,6},{8,9},{9,8},{10,11... | collective-permute-start | bytes 1179656 | tf_op jit(solution)/shard_map/ppermute | solution.py:521
  230.6 0.7 copy-start.15
  231.3 7.9 %collective-permute-start.10 = (f32[32,2048]{1,0:T(8,128)}, f32[32,2048]{1,0:T(8,128)S(1)}, u32[]{:S(2)}, u32[]{:S(2)}) collective-permute-start(f32[32,2048]{1,0:T(8,128)} %get-tuple-element.31), channel_id=1, source_target_pairs={{0,1},{1,0},{2,3},{3,2},{4,5},{5,4},{6,7},{7,6},{8,9},{9,8},{10,11... | collective-permute-start | bytes 786440 | tf_op jit(solution)/shard_map/ppermute | solution.py:521
  231.9 9.1 %copy-start.7 = (bf16[8,32,768]{2,1,0:T(8,128)(2,1)S(1)}, bf16[8,32,768]{2,1,0:T(8,128)(2,1)}, u32[]{:S(2)}) copy-start(bf16[8,32,768]{2,1,0:T(8,128)(2,1)} %copy-done.6) | copy-start | bytes 1179652
  231.9 9.1 %copy-start.9 = (bf16[8,32,768]{2,1,0:T(8,128)(2,1)S(1)}, bf16[8,32,768]{2,1,0:T(8,128)(2,1)}, u32[]{:S(2)}) copy-start(bf16[8,32,768]{2,1,0:T(8,128)(2,1)} %copy-done.8) | copy-start | bytes 1179652
  233.2 16.9 %all-to-all-start.4 = ((bf16[8,32,768]{2,1,0:T(8,128)(2,1)}), bf16[8,32,768]{2,1,0:T(8,128)(2,1)}, u32[]{:S(2)}, u32[]{:S(2)}) async-start(bf16[8,32,768]{2,1,0:T(8,128)(2,1)} %first_sum.1), calls=%async_computation.4 | async-start | bytes 786432 | tf_op jit(solution)/shard_map/all_to_all | solution.py:524
  248.6 4.3 %collective-permute-start.7 = (f32[128,8]{1,0:T(8,128)S(1)}, f32[128,8]{1,0:T(8,128)S(1)}, u32[]{:S(2)}, u32[]{:S(2)}) collective-permute-start(f32[128,8]{1,0:T(8,128)S(1)} %get-tuple-element.27), channel_id=1, source_target_pairs={{0,2},{2,0},{1,3},{3,1},{4,6},{6,4},{5,7},{7,5},{8,10},{10,8},{9,1... | collective-permute-start | bytes 12296 | tf_op jit(solution)/shard_map/ppermute | solution.py:515
Sparse Core Ops, SparseCore 0:
  11.8 80.0 all-gather.2

commit v6 on v4

--- a/solution.py
+++ b/solution.py
@@ -13,9 +13,10 @@
 NT = (((1,), (1,)), ((), ()))
 TN = (((0,), (0,)), ((), ()))
 NN = (((1,), (0,)), ((), ()))
-PARAMS = pltpu.CompilerParams(vmem_limit_bytes=20 * 2**20)
 SMALL = pl.CostEstimate(flops=1, bytes_accessed=1, transcendentals=0)
+LONG = pl.CostEstimate(flops=1, bytes_accessed=2 * 10**7, transcendentals=0)
 ANY = pl.BlockSpec(memory_space=pl.ANY)
+SMEM = pl.BlockSpec(memory_space=pltpu.SMEM)
 
 
 def dot(a, b, dims):
@@ -30,21 +31,39 @@
     return pl.BlockSpec(shape, lambda *_: (0,) * len(shape))
 
 
-def call(kernel, name, at, arrays, in_specs, outs, out_specs, grid=(1,), scratch=()):
-    return pl.pallas_call(
-        kernel,
-        grid_spec=pltpu.PrefetchScalarGridSpec(
-            num_scalar_prefetch=1,
+def in_hbm(x):
+    return pltpu.with_memory_space_constraint(x, pltpu.HBM)
+
+
+class Order:
+    def __init__(self, at):
+        self.at, self.last = at, []
+
+    def wait(self, arrays):
+        self.last = self.last + list(arrays)
+
+    def call(self, kernel, name, arrays, in_specs, outs, out_specs, grid=(1,), scratch=(), mib=16, cost=SMALL, **more):
+        count, last = 1 + len(arrays), len(self.last)
+
+        def ordered(*refs):
+            here = count + last + len(outs)
+            kernel(*refs[:count], *refs[count + last : here], *refs[here + 1 :])
+
+        *result, token = pl.pallas_call(
+            ordered,
             grid=grid,
-            in_specs=in_specs,
-            out_specs=out_specs,
+            in_specs=[SMEM, *in_specs] + [ANY] * last,
+            out_specs=[*out_specs, ANY],
             scratch_shapes=scratch,
-        ),
-        out_shape=[jax.ShapeDtypeStruct(*o) for o in outs],
-        compiler_params=PARAMS,
-        cost_estimate=SMALL,
-        name=name,
-    )(at, *arrays)
+            out_shape=[jax.ShapeDtypeStruct(*o) if isinstance(o, tuple) else o for o in outs]
+            + [pltpu.HBM((8, 128), F32)],
+            compiler_params=pltpu.CompilerParams(vmem_limit_bytes=mib * 2**20),
+            cost_estimate=cost,
+            name=name,
+            **more,
+        )(self.at, *arrays, *self.last)
+        self.last = [in_hbm(token)]
+        return result
 
 
 def relative(at_ref, index, groups):
@@ -91,14 +110,13 @@
     out_ref[pl.ds(3 * rank, 16), pl.ds(feats, toks)] = routes.astype(BF16)
 
 
-def pack_call(at, grad, first, index):
+def pack_call(order, grad, first, index):
     (toks, feats), (units, rank) = grad.shape, first.shape
     extra = units // 3
     shape = (toks, feats + extra)
-    return call(
+    return order.call(
         functools.partial(pack_kernel, rank),
         "pack_block",
-        at,
         [grad, first, index],
         [whole(grad.shape), whole(first.shape), whole(index.shape)],
         [(shape, BF16)],
@@ -106,75 +124,94 @@
     )[0]
 
 
-def expert_rows_kernel(slots, tiles, shares, batch, feats, route_row, at_ref, *rest):
-    grads, seconds, weights = rest[:batch], rest[batch : batch + 2], rest[batch + 2 : batch + 4]
-    outs, low_ref, rows_ref = rest[-2 - shares : -2], rest[-2], rest[-1]
-    step = pl.program_id(0)
-
-    @pl.when(step == 0)
-    def _():
-        toks = grads[0].shape[0]
-        before = jnp.where(iota((toks, toks), 0) < iota((toks, toks), 1), 1.0, 0.0).astype(BF16)
-        slot = iota((slots, toks), 0).astype(F32)
-        second = jnp.concatenate([ref[...] for ref in seconds], axis=0)
-        for k, grad_ref in enumerate(grads):
-            routes = grad_ref[pl.ds(route_row, 16), pl.ds(feats, toks)].astype(F32)
-            picks = []
-            for q in range(2):
-                expert = at_ref[1] * 2 + lax.bitwise_xor(at_ref[2], q)
-                hits = jnp.where(routes == expert.astype(F32), 1.0, 0.0)
-                mine = jnp.max(hits, axis=0, keepdims=True)
-                pos = dot(jnp.broadcast_to(mine, (16, toks)).astype(BF16), before, NN)[:1]
-                picks.append(jnp.where((slot == pos) & (mine > 0.0), 1.0, 0.0).astype(BF16))
-            grad = grad_ref[:, pl.ds(0, feats)]
-            rows = dot(jnp.concatenate(picks, axis=0), grad, NN).astype(BF16)
-            for q in range(2):
-                rows_ref[q, pl.ds(k * slots, slots), :] = rows[q * slots : (q + 1) * slots]
-            low_ref[k] = dot(second, grad, NT).astype(BF16)
-
-    turn = step // tiles
-    tile = weights[0].shape[0]
-    column = pl.ds(pl.multiple_of(lax.rem(step, tiles) * tile, 128), tile)
-    for q in range(2):
-
-        @pl.when(lax.rem(turn, 2) == q)
-        def _():
-            value = dot(rows_ref[q], weights[q][...], NT).astype(BF16)
-            for k, out_ref in enumerate(outs):
-
-                @pl.when(turn // 2 == k)
-                def _():
-                    out_ref[pl.ds(q * batch * slots, batch * slots), column] = value
-
-
-def expert_rows_call(at, grads, seconds, downs, shares, slots, after):
+def expert_rows_kernel(slots, tiles, shares, batch, route_row, at_ref, *rest):
+    grads, seconds, downs = rest[:batch], rest[batch : batch + 2], rest[batch + 2 : batch + 4]
+    *outs, low_ref = rest[batch + 4 : batch + 5 + shares]
+    block_ref, rows_ref, tiles_ref, block_sems, sems = rest[batch + 5 + shares :]
+    tile = tiles_ref.shape[1]
+    feats = rows_ref.shape[2]
+    toks = block_ref.shape[1]
+    blocks = [
+        pltpu.make_async_copy(ref, block_ref.at[k], block_sems.at[k]) for k, ref in enumerate(grads)
+    ]
+    parts = [(k, q, t) for k in range(shares) for q in range(2) for t in range(tiles)]
+    weights = []
+    for n, (k, q, t) in enumerate(parts):
+        share = lax.rem(at_ref[0] + k + 1, shares)
+        row = pl.multiple_of((share * tiles + t) * tile, tile)
+        weights.append(
+            pltpu.make_async_copy(downs[q].at[pl.ds(row, tile), :], tiles_ref.at[n], sems.at[n])
+        )
+    for copy in blocks + weights:
+        copy.start()
+
+    before = jnp.where(iota((toks, toks), 0) < iota((toks, toks), 1), 1.0, 0.0).astype(BF16)
+    slot = iota((slots, toks), 0).astype(F32)
+    second = jnp.concatenate([ref[...] for ref in seconds], axis=0)
+    for k in range(batch):
+        blocks[k].wait()
+        routes = block_ref[k, pl.ds(route_row, 16), pl.ds(feats, toks)].astype(F32)
+        picks = []
+        for q in range(2):
+            expert = at_ref[1] * 2 + lax.bitwise_xor(at_ref[2], q)
+            hits = jnp.where(routes == expert.astype(F32), 1.0, 0.0)
+            mine = jnp.max(hits, axis=0, keepdims=True)
+            pos = dot(jnp.broadcast_to(mine, (16, toks)).astype(BF16), before, NN)[:1]
+            picks.append(jnp.where((slot == pos) & (mine > 0.0), 1.0, 0.0).astype(BF16))
+        grad = block_ref[k, :, pl.ds(0, feats)]
+        rows = dot(jnp.concatenate(picks, axis=0), grad, NN).astype(BF16)
+        for q in range(2):
+            rows_ref[q, pl.ds(k * slots, slots), :] = rows[q * slots : (q + 1) * slots]
+        low_ref[k] = dot(second, grad, NT).astype(BF16)
+
+    for n, (k, q, t) in enumerate(parts):
+        weights[n].wait()
+        value = dot(rows_ref[q], tiles_ref[n], NT).astype(BF16)
+        outs[k][pl.ds(q * batch * slots, batch * slots), pl.ds(t * tile, tile)] = value
+
+
+def expert_rows_call(order, grads, seconds, downs, shares, slots):
     batch, (toks, wide) = len(grads), grads[0].shape
     rank, feats = seconds[0].shape
     units = downs[0].shape[0] // shares
     tiles = 3
     tile = units // tiles
     rows = 2 * batch * slots
-
-    def weight_at(q, i, at):
-        share = lax.rem(at[0] + i // (2 * tiles) + 1, shares)
-        turn = lax.rem(i // tiles, 2)
-        idle = (tiles - 1) * (1 - q)
-        return (share * tiles + jnp.where(turn == q, lax.rem(i, tiles), idle), 0)
-
-    return call(
-        functools.partial(expert_rows_kernel, slots, tiles, shares, batch, feats, 3 * rank),
+    count = shares * 2 * tiles
+    low_shape = (batch, 2 * rank, toks)
+    return order.call(
+        functools.partial(expert_rows_kernel, slots, tiles, shares, batch, 3 * rank),
         "expert_rows",
-        at,
-        [*grads, *seconds, *downs, *after],
-        [whole((toks, wide))] * batch
-        + [whole((rank, feats))] * 2
-        + [pl.BlockSpec((tile, feats), functools.partial(weight_at, q)) for q in range(2)]
-        + [ANY] * len(after),
-        [((rows, units), BF16)] * shares + [((batch, 2 * rank, toks), BF16)],
-        [whole((rows, units))] * shares + [whole((batch, 2 * rank, toks))],
-        grid=(shares * 2 * tiles,),
-        scratch=[pltpu.VMEM((2, batch * slots, feats), BF16)],
-    )
+        [*grads, *seconds, *[in_hbm(x) for x in downs]],
+        [ANY] * batch + [whole((rank, feats))] * 2 + [ANY] * 2,
+        [((rows, units), BF16)] * (shares - 1)
+        + [pltpu.HBM((rows, units), BF16), pltpu.HBM(low_shape, BF16)],
+        [whole((rows, units))] * shares + [whole(low_shape)],
+        scratch=[
+            pltpu.VMEM((batch, toks, wide), BF16),
+            pltpu.VMEM((2, batch * slots, feats), BF16),
+            pltpu.VMEM((count, tile, feats), BF16),
+            pltpu.SemaphoreType.DMA((batch,)),
+            pltpu.SemaphoreType.DMA((count,)),
+        ],
+        mib=28,
+    )
+
+
+def gate_kernel(at_ref, block_ref, out_ref):
+    pass
+
+
+def gate_call(order, block):
+    return order.call(
+        gate_kernel,
+        "gate",
+        [block],
+        [ANY],
+        [(block.shape, block.dtype)],
+        [ANY],
+        input_output_aliases={1: 0},
+    )[0]
 
 
 def share_sum_kernel(parts, slots, at_ref, *refs):
@@ -188,13 +225,12 @@
             out_ref[pl.ds(q * slots, slots), :] = total.astype(BF16)
 
 
-def share_sum_call(at, parts, batch, slots):
+def share_sum_call(order, parts, batch, slots):
     rows, units = parts[0].shape
     shape = (2 * slots, units)
-    return call(
+    return order.call(
         functools.partial(share_sum_kernel, len(parts), slots),
         "share_sum",
-        at,
         parts,
         [whole((rows, units))] * len(parts),
         [(shape, BF16)] * batch,
@@ -202,32 +238,32 @@
     )
 
 
-def collect_kernel(parts, at_ref, *refs):
+def collect_kernel(places, at_ref, *refs):
     low_ref, first_ref = refs[-2:]
     rank = first_ref.shape[1]
-    o = 0
-    for ref in refs[:parts]:
+    at = 0
+    lows = len(refs) - 2 - len(places)
+    for ref in refs[:lows]:
         for k in range(ref.shape[0]):
-            low_ref[lax.bitwise_xor(at_ref[1], o)] = ref[k]
-            o += 1
-    for o, ref in enumerate(refs[parts:-2]):
+            low_ref[lax.bitwise_xor(at_ref[1], places[at])] = ref[k]
+            at += 1
+    for o, ref in zip(places, refs[lows:-2]):
         wide = ref.shape[1]
         for k in range(3):
             first_ref[o, :, pl.ds(k * wide, wide)] = ref[pl.ds(k * rank, rank), :]
 
 
-def collect_call(at, lows, grads, feats):
+def collect_call(order, places, lows, grads, feats):
     groups, (toks, wide) = len(grads), grads[0].shape
     rank = lows[0].shape[1] // 2
     extra = wide - feats
     low_shape, first_shape = (groups, 2 * rank, toks), (groups, rank, 3 * extra)
-    return call(
-        functools.partial(collect_kernel, len(lows)),
+    return order.call(
+        functools.partial(collect_kernel, places),
         "collect_blocks",
-        at,
-        [*lows, *grads],
+        [*lows, *[in_hbm(x) for x in grads]],
         [whole(b.shape) for b in lows]
-        + [pl.BlockSpec((toks, extra), lambda i, at: (0, feats // extra))] * groups,
+        + [pl.BlockSpec((toks, extra), lambda i: (0, feats // extra))] * groups,
         [(low_shape, BF16), (first_shape, BF16)],
         [whole(low_shape), whole(first_shape)],
     )
@@ -247,13 +283,12 @@
     out_ref[...] = sum_ref[...].T
 
 
-def low_dense_call(at, parts):
+def low_dense_call(order, parts):
     groups, both, toks = parts[0].shape
     shape = (toks, groups * both)
-    return call(
+    return order.call(
         low_dense_kernel,
         "low_dense",
-        at,
         parts,
         [whole(parts[0].shape)] * len(parts),
         [(shape, F32)],
@@ -272,22 +307,21 @@
     out_ref[...] = wide.reshape(wide.shape[0] // top, top, wide.shape[1]).sum(axis=1)
 
 
-def lowrank_hid_call(at, index, hid, firsts, groups):
+def lowrank_hid_call(order, index, hid, firsts, groups):
     (toks, top), (pairs, units) = index.shape, hid.shape
     half = firsts[0].shape[0]
     steps = 4
-    return call(
+    return order.call(
         functools.partial(lowrank_hid_kernel, groups),
         "lowrank_hid",
-        at,
-        [index, hid, *firsts],
+        [index, in_hbm(hid), *firsts],
         [
-            pl.BlockSpec((toks // steps, top), lambda i, at: (i, 0)),
-            pl.BlockSpec((pairs // steps, units), lambda i, at: (i, 0)),
+            pl.BlockSpec((toks // steps, top), lambda i: (i, 0)),
+            pl.BlockSpec((pairs // steps, units), lambda i: (i, 0)),
         ]
         + [whole((half, units))] * 2,
         [((toks, 2 * half), F32)],
-        [pl.BlockSpec((toks // steps, 2 * half), lambda i, at: (i, 0))],
+        [pl.BlockSpec((toks // steps, 2 * half), lambda i: (i, 0))],
         grid=(steps,),
     )[0]
 
@@ -310,14 +344,13 @@
             out_ref[lax.bitwise_xor(at_ref[1], o), pl.ds(q * rank, rank), :] = scaled[at : at + rank]
 
 
-def scaled_hid_call(at, index, prob, parts, groups):
+def scaled_hid_call(order, index, prob, parts, groups):
     toks, width = parts[0].shape
     rank = width // groups // 2
     shape = (groups, 2 * rank, toks)
-    return call(
+    return order.call(
         functools.partial(scaled_hid_kernel, groups, rank),
         "scaled_hid",
-        at,
         [index, prob, *parts],
         [whole(index.shape), whole(prob.shape)] + [whole((toks, width))] * len(parts),
         [(shape, BF16)],
@@ -325,30 +358,30 @@
     )[0]
 
 
-def second_grad_kernel(at_ref, scaled_ref, *refs):
+def second_grad_kernel(places, at_ref, scaled_ref, *refs):
     grads, outs = refs[:-2], refs[-2:]
     rank, tile = outs[0].shape
     total = jnp.zeros((2 * rank, tile), F32)
-    for o, grad_ref in enumerate(grads):
+    for o, grad_ref in zip(places, grads):
         total = total + dot(scaled_ref[lax.bitwise_xor(at_ref[1], o)], grad_ref[...], NN)
     for q, out_ref in enumerate(outs):
         out_ref[...] = adapter_scale * total[q * rank : (q + 1) * rank]
 
 
-def second_grad_call(at, scaled, grads, feats):
+def second_grad_call(order, places, scaled, grads, feats):
     groups, both, toks = scaled.shape
     steps = 4
     tile = feats // steps
-    block = pl.BlockSpec((both // 2, tile), lambda i, at: (0, i))
-    return call(
-        second_grad_kernel,
+    block = pl.BlockSpec((both // 2, tile), lambda i: (0, i))
+    return order.call(
+        functools.partial(second_grad_kernel, places),
         "second_grad",
-        at,
-        [scaled, *grads],
-        [whole(scaled.shape)] + [pl.BlockSpec((toks, tile), lambda i, at: (0, i))] * groups,
+        [scaled, *[in_hbm(x) for x in grads]],
+        [whole(scaled.shape)] + [pl.BlockSpec((toks, tile), lambda i: (0, i))] * groups,
         [((both // 2, feats), F32)] * 2,
         [block] * 2,
         grid=(steps,),
+        cost=LONG,
     )
 
 
@@ -378,21 +411,20 @@
             out_ref[...] = half.reshape(out_ref.shape).astype(out_ref.dtype)
 
 
-def first_grad_call(at, index, prob, low, hid, groups):
+def first_grad_call(order, index, prob, low, hid, groups):
     (toks, top), (pairs, units) = index.shape, hid.shape
     width = low.shape[1]
     steps = 4
     shape = (groups, width // groups // 2, units)
-    return call(
+    return order.call(
         functools.partial(first_grad_kernel, groups, steps),
         "first_grad",
-        at,
-        [index, prob, low, hid],
+        [index, prob, low, in_hbm(hid)],
         [
-            pl.BlockSpec((toks // steps, top), lambda i, at: (i, 0)),
-            pl.BlockSpec((toks // steps, top), lambda i, at: (i, 0)),
-            pl.BlockSpec((toks // steps, width), lambda i, at: (i, 0)),
-            pl.BlockSpec((pairs // steps, units), lambda i, at: (i, 0)),
+            pl.BlockSpec((toks // steps, top), lambda i: (i, 0)),
+            pl.BlockSpec((toks // steps, top), lambda i: (i, 0)),
+            pl.BlockSpec((toks // steps, width), lambda i: (i, 0)),
+            pl.BlockSpec((pairs // steps, units), lambda i: (i, 0)),
         ],
         [(shape, F32), (shape, BF16)],
         [whole(shape)] * 2,
@@ -407,12 +439,11 @@
         out_ref[lax.bitwise_xor(at_ref[1], o)] = total.astype(BF16)
 
 
-def first_sum_call(at, keep, got):
+def first_sum_call(order, keep, got):
     shape = keep.shape
-    return call(
+    return order.call(
         first_sum_kernel,
         "first_sum",
-        at,
         [keep, got],
         [whole(shape)] * 2,
         [(shape, BF16)],
@@ -460,7 +491,7 @@
     sum_ref[...] = sums.reshape(some, top, top).sum(axis=1)
 
 
-def finish_call(at, index, prob, low, hid, firsts, back):
+def finish_call(order, index, prob, low, hid, firsts, back):
     (toks, top), (pairs, units) = index.shape, hid.shape
     width = low.shape[1]
     both = back[0].shape[0]
@@ -468,13 +499,12 @@
     count = len(back)
 
     def rows(n, columns):
-        return pl.BlockSpec((n // steps, columns), lambda i, at: (i, 0))
-
-    return call(
+        return pl.BlockSpec((n // steps, columns), lambda i: (i, 0))
+
+    return order.call(
         functools.partial(finish_kernel, count, both // 2),
         "finish",
-        at,
-        [index, index, prob, low, hid, *firsts, *back],
+        [index, index, prob, low, in_hbm(hid), *firsts, *[in_hbm(x) for x in back]],
         [whole(index.shape), rows(toks, top), rows(toks, top), rows(toks, width), rows(pairs, units)]
         + [whole(firsts[0].shape)] * 2
         + [whole((both, units))] * count,
@@ -495,6 +525,7 @@
     slots = -(-cap // 16) * 16
     pairs = toks * top
     at = jnp.stack([lax.axis_index(name).astype(jnp.int32) for name in ("rep", "ep", "sub")])
+    order = Order(at)
 
     def turn(x, offset):
         return lax.ppermute(x, "rep", [(r, (r + offset) % shares) for r in range(shares)])
@@ -511,41 +542,67 @@
     def exchange(x):
         return lax.all_to_all(x, "ep", split_axis=0, concat_axis=0, tiled=True)
 
-    blocks = [pack_call(at, grad, first[0], index)]
-    for o in range(1, groups):
-        last = o & -o
-        blocks.append(flip(blocks[o ^ last], last))
-        if last == o and o >= 4:
-            blocks[o], blocks[o - 1] = lax.optimization_barrier((blocks[o], blocks[o - 1]))
-    downs = [pltpu.with_memory_space_constraint(down[0], pltpu.HBM), swap(down[0])]
+    blocks = {0: pack_call(order, grad, first[0], index)}
+
+    def fetch(o):
+        if o not in blocks:
+            last = o & -o
+            blocks[o] = flip(fetch(o ^ last), last)
+        return blocks[o]
+
+    downs = [down[0], swap(down[0])]
     seconds = [second[0], swap(second[0])]
 
-    back, lows, after = [], [], [[], []]
-    for o in range(0, groups, 2):
+    if groups == 8:
+        batches, gates = [(0, 2), (1, 4), (3, 6), (5, 7)], {1: 4, 2: 6}
+    else:
+        batches, gates = [(o, o + 1) for o in range(0, groups, 2)], {}
+    places = [o for batch in batches for o in batch]
+    back, lows, waiting = {}, [], []
+
+    def arrived(i):
+        order.wait([back[o] for o in batches[i] if o])
+
+    def send_back(batch, parts):
+        for o, rows in zip(batch, share_sum_call(order, parts, 2, slots)):
+            back[o] = flip(rows, o) if o else rows
+
+    for i, batch in enumerate(batches):
+        if i in gates:
+            blocks[gates[i]] = gate_call(order, fetch(gates[i]))
         *give, keep, low = expert_rows_call(
-            at, blocks[o : o + 2], seconds, downs, shares, slots, after[-2]
+            order, [fetch(o) for o in batch], seconds, downs, shares, slots
         )
-        parts = [keep] + [turn(x, k + 1) for k, x in enumerate(give)]
-        sums = share_sum_call(at, parts, 2, slots)
-        back += [flip(rows, o + k) if o + k else rows for k, rows in enumerate(sums)]
         lows.append(low)
-        after.append(sums[:1])
+        if i > 1:
+            arrived(i - 2)
+        if i > 0:
+            send_back(*waiting)
+        waiting = (batch, [keep] + [turn(x, k + 1) for k, x in enumerate(give)])
 
     hid = hidden.reshape(pairs, units)
-    low_grad, first_own = collect_call(at, lows, blocks, feats)
+    grads = [blocks[o] for o in places]
+
+    low_grad, first_own = collect_call(order, places, lows, grads, feats)
     firsts = [x.reshape(groups * rank, units) for x in (first_own, swap(first_own))]
-
-    low_hid = all_shares(lowrank_hid_call(at, index, hid, firsts, groups))
-    scaled_hid = exchange(scaled_hid_call(at, index, weight, low_hid, groups))
-    second_keep, second_give = second_grad_call(at, scaled_hid, blocks, feats)
+    low_hid = all_shares(lowrank_hid_call(order, index, hid, firsts, groups))
+    low_grad = all_shares(exchange(low_grad))
+    send_back(*waiting)
+
+    arrived(len(batches) - 2)
+    scaled_hid = exchange(scaled_hid_call(order, index, weight, low_hid, groups))
+
+    low_grad = low_dense_call(order, low_grad)
+    first_keep, first_give = first_grad_call(order, index, weight, low_grad, hid, groups)
+    first_part = exchange(first_sum_call(order, first_keep, swap(first_give)))
+    first_grad = jnp.sum(first_part.astype(F32), axis=0)
+    order.wait([back[batches[-1][0]]])
+    second_keep, second_give = second_grad_call(order, places, scaled_hid, grads, feats)
     second_grad = second_keep + swap(second_give)
 
-    low_grad = low_dense_call(at, all_shares(exchange(low_grad)))
-    first_keep, first_give = first_grad_call(at, index, weight, low_grad, hid, groups)
-    first_part = exchange(first_sum_call(at, first_keep, swap(first_give)))
-    first_grad = jnp.sum(first_part.astype(F32), axis=0)
-
-    grad_hidden, sums = finish_call(at, index, weight, low_grad, hid, firsts, back)
+    order.wait([first_part])
+    back = [back[o] for o in range(groups)]
+    grad_hidden, sums = finish_call(order, index, weight, low_grad, hid, firsts, back)
     sums = sums + turn(sums, 1) if shares == 2 else lax.psum(sums, "rep")
     return (
         grad_hidden.reshape(toks, top, units),

time: 267 us -> 201 us (0.75)
  the two profiles are of different devices: /device:TPU:0 before, /device:TPU:8 now
where the time goes in v6:
time: 201 us; the launch traced here: 200 us
  Pallas kernels  78.1 us (39%)
  waiting for transfers between devices  66.2 us (33%)
  starting transfers between devices  47 us (23%)
  local copies, waits for them, and re-layouts  6.33 us (3%)
    pallas_call x19, Pallas kernels, call(): pl.pallas_call(ordered, grid=grid, in_specs=[SMEM, *in_specs] + [ANY] * l...  78.1 us
    ppermute x14, waiting for transfers between devices, flip(): return lax.ppermute(x, 'ep', [(i, i ^ mask) for i in range(groups)])  59.6 us
    ppermute x14, starting transfers between devices, flip(): return lax.ppermute(x, 'ep', [(i, i ^ mask) for i in range(groups)])  23.1 us
    all_to_all x3, starting transfers between devices, exchange(): return lax.all_to_all(x, 'ep', split_axis=0, concat_axis=0, tiled=True)  14.8 us
    ppermute x7, starting transfers between devices, turn(): lax.ppermute(x, 'rep', [(r, (r + offset) % shares) for r in range(shares)])  8.85 us
    unnamed x66, local copies, waits for them, and re-layouts  6.33 us
  transfers between devices with their start and end apart: 29, of which 9 were waited for; matrix products, arithmetic and copies ran while one was open for 2% of the time, Pallas kernels for 29%

profile of v6, /device:TPU:8, one launch (start us, length us, event | category | flops | bytes accessed | tf_op | source)
XLA Modules:
  0.0 200.2 jit_solution(3585580487393291737)
XLA Ops:
  0.7 0.8 copy.20.refs_3_.refs_1_.refs_2_
  1.5 1.0 copy.13
  2.5 0.1 pad_add_fusion.refs_0_
  2.6 1.0 copy-done.18
  3.6 0.8 pack_block.1
  4.5 3.0 %collective-permute-start.4 = (bf16[128,2304]{1,0:T(8,128)(2,1)S(1)}, bf16[128,2304]{1,0:T(8,128)(2,1)S(1)}, u32[]{:S(2)}, u32[]{:S(2)}) collective-permute-start(bf16[128,2304]{1,0:T(8,128)(2,1)S(1)} %get-tuple-element.57.refs_1_.refs_5_.refs_2_), channel_id=1, source_target_pairs={{0,16},{4,20},{8,24},{12,28},{16,0},{20,4},{24,8},{28,12},{1,17},{... | collective-permute-start | bytes 1769480 | tf_op jit(solution)/shard_map/ppermute | solution.py:537
  7.5 1.5 collective-permute-start.3
  9.0 2.2 %collective-permute-done.1.refs_4_ = bf16[32,2048]{1,0:T(8,128)(2,1)S(1)} collective-permute-done((bf16[32,2048]{1,0:T(8,128)(2,1)}, bf16[32,2048]{1,0:T(8,128)(2,1)S(1)}, u32[]{:S(2)}, u32[]{:S(2)}) %collective-permute-start.1) | collective-permute-done | bytes 131104 | tf_op jit(solution)/shard_map/ppermute | solution.py:540
  11.3 19.3 %collective-permute-done.refs_2_.refs_6_.refs_3_ = bf16[128,2304]{1,0:T(8,128)(2,1)S(1)} collective-permute-done((bf16[128,2304]{1,0:T(8,128)(2,1)S(1)}, bf16[128,2304]{1,0:T(8,128)(2,1)S(1)}, u32[]{:S(2)}, u32[]{:S(2)}) %collective-permute-start) | collective-permute-done | bytes 589856 | tf_op jit(solution)/shard_map/ppermute | solution.py:537
  30.5 1.0 copy-done.10
  31.6 11.5 %expert_rows.4 = (bf16[320,768]{1,0:T(8,128)(2,1)S(1)}, bf16[320,768]{1,0:T(8,128)(2,1)}, bf16[2,64,128]{2,1,0:T(8,128)(2,1)}, f32[8,128]{1,0:T(8,128)}) custom-call(s32[3]{0:T(128)S(1)} %pad_add_fusion.refs_0_, bf16[128,2304]{1,0:T(8,128)(2,1)S(1)} %get-tuple-element.57.refs_1_.refs_5_.refs_2_, ...), custom_call_target="tpu_custom_call" | custom-call | flops 1 | bytes 1 | tf_op jit(solution)/shard_map/expert_rows/pallas_call | solution.py:52
  43.1 0.5 gate.2
  43.7 2.5 %collective-permute-start.6 = (bf16[128,2304]{1,0:T(8,128)(2,1)S(1)}, bf16[128,2304]{1,0:T(8,128)(2,1)S(1)}, u32[]{:S(2)}, u32[]{:S(2)}) collective-permute-start(bf16[128,2304]{1,0:T(8,128)(2,1)S(1)} %get-tuple-element.61.refs_2_.refs_8_.refs_5_), channel_id=1, source_target_pairs={{0,8},{4,12},{8,0},{12,4},{16,24},{20,28},{24,16},{28,20},{1,9},{5... | collective-permute-start | bytes 1769480 | tf_op jit(solution)/shard_map/ppermute | solution.py:537
  46.2 1.7 collective-permute-start.7
  47.9 1.5 collective-permute-start.5
  49.4 11.6 %expert_rows.5 = (bf16[320,768]{1,0:T(8,128)(2,1)S(1)}, bf16[320,768]{1,0:T(8,128)(2,1)}, bf16[2,64,128]{2,1,0:T(8,128)(2,1)}, f32[8,128]{1,0:T(8,128)}) custom-call(s32[3]{0:T(128)S(1)} %pad_add_fusion.refs_0_, bf16[128,2304]{1,0:T(8,128)(2,1)S(1)} %collective-permute-done.3.refs_1_.refs_7_.refs_4_, ...), custom_call_target="tpu_custom_call" | custom-call | flops 1 | bytes 1 | tf_op jit(solution)/shard_map/expert_rows/pallas_call | solution.py:52
  61.0 0.6 collective-permute-start.10
  61.6 0.3 collective-permute-start.8
  62.0 0.7 share_sum.4
  62.6 0.5 gate.3
  63.2 0.1 copy-done.23
  63.3 1.7 collective-permute-start.9
  65.0 0.1 collective-permute-start.11
  65.1 11.8 %expert_rows.6 = (bf16[320,768]{1,0:T(8,128)(2,1)S(1)}, bf16[320,768]{1,0:T(8,128)(2,1)}, bf16[2,64,128]{2,1,0:T(8,128)(2,1)}, f32[8,128]{1,0:T(8,128)}) custom-call(s32[3]{0:T(128)S(1)} %pad_add_fusion.refs_0_, bf16[128,2304]{1,0:T(8,128)(2,1)S(1)} %collective-permute-done.5.refs_1_.refs_9_.refs_6_, ...), custom_call_target="tpu_custom_call" | custom-call | flops 1 | bytes 1 | tf_op jit(solution)/shard_map/expert_rows/pallas_call | solution.py:52
  76.9 1.5 collective-permute-start.12
  78.4 0.7 share_sum.5
  79.1 0.6 collective-permute-start.13
  79.7 3.0 %collective-permute-start.14 = (bf16[160,768]{1,0:T(8,128)(2,1)S(1)}, bf16[160,768]{1,0:T(8,128)(2,1)S(1)}, u32[]{:S(2)}, u32[]{:S(2)}) collective-permute-start(bf16[160,768]{1,0:T(8,128)(2,1)S(1)} %get-tuple-element.81), channel_id=1, source_target_pairs={{0,16},{4,20},{8,24},{12,28},{16,0},{20,4},{24,8},{28,12},{1,17},{... | collective-permute-start | bytes 737288 | tf_op jit(solution)/shard_map/ppermute | solution.py:537
  82.7 7.9 %collective-permute-done.9.refs_2_.refs_12_.refs_9_ = bf16[128,2304]{1,0:T(8,128)(2,1)S(1)} collective-permute-done((bf16[128,2304]{1,0:T(8,128)(2,1)S(1)}, bf16[128,2304]{1,0:T(8,128)(2,1)S(1)}, u32[]{:S(2)}, u32[]{:S(2)}) %collective-permute-start.9) | collective-permute-done | bytes 589856 | tf_op jit(solution)/shard_map/ppermute | solution.py:537
  90.5 11.5 %expert_rows.7 = (bf16[320,768]{1,0:T(8,128)(2,1)}, bf16[320,768]{1,0:T(8,128)(2,1)}, bf16[2,64,128]{2,1,0:T(8,128)(2,1)}, f32[8,128]{1,0:T(8,128)}) custom-call(s32[3]{0:T(128)S(1)} %pad_add_fusion.refs_0_, bf16[128,2304]{1,0:T(8,128)(2,1)S(1)} %collective-permute-done.8.refs_1_.refs_11_.refs_8_, ...), custom_call_target="tpu_custom_call" | custom-call | flops 1 | bytes 1 | tf_op jit(solution)/shard_map/expert_rows/pallas_call | solution.py:52
  102.2 1.3 share_sum.6
  103.5 0.7 copy-done.27
  104.3 1.7 collect_blocks.1
  106.0 1.5 collective-permute-start.18
  107.5 4.3 %all-to-all-start = ((bf16[8,64,128]{2,1,0:T(8,128)(2,1)}), bf16[8,64,128]{2,1,0:T(8,128)(2,1)S(1)}, u32[]{:S(2)}, u32[]{:S(2)}) async-start(bf16[8,64,128]{2,1,0:T(8,128)(2,1)} %get-tuple-element.83), calls=%async_computation | async-start | bytes 262144 | tf_op jit(solution)/shard_map/all_to_all | solution.py:543
  111.8 3.6 %lowrank_hid.1 = (f32[128,512]{1,0:T(8,128)S(1)}, f32[8,128]{1,0:T(8,128)}) custom-call(s32[3]{0:T(128)S(1)} %pad_add_fusion.refs_0_, s32[128,8]{1,0:T(8,128)S(1)} %copy-done.9, bf16[1024,768]{1,0:T(8,128)(2,1)} %bitcast.30, bf16[256,768]{1,0:T(8,128)(2,1)S(1)} %bitcast.20, bf16[256,768]{1,0:T(8,128)(2,1)S(1)} %bitcast.22, f32[8,128]{1,0:T(8,128)} %get-tuple-element.85.refs_5_), custom_call_target="tpu_custom_call" | custom-call | flops 1 | bytes 1 | tf_op jit(solution)/shard_map/lowrank_hid/pallas_call | solution.py:52
  115.4 0.6 collective-permute-start.17
  116.0 1.5 collective-permute-start.19
  117.5 2.4 %collective-permute-start.20 = (bf16[160,768]{1,0:T(8,128)(2,1)S(1)}, bf16[160,768]{1,0:T(8,128)(2,1)S(1)}, u32[]{:S(2)}, u32[]{:S(2)}) collective-permute-start(bf16[160,768]{1,0:T(8,128)(2,1)S(1)} %get-tuple-element.92), channel_id=1, source_target_pairs={{0,24},{4,28},{8,16},{12,20},{16,8},{20,12},{24,0},{28,4},{1,25},{... | collective-permute-start | bytes 737288 | tf_op jit(solution)/shard_map/ppermute | solution.py:537
  119.8 1.5 collective-permute-start.15
  121.3 0.1 copy.22.refs_2_.refs_3_
  121.5 1.8 share_sum.7
  123.2 2.8 %collective-permute-done.19.refs_6_.refs_11_ = bf16[160,768]{1,0:T(8,128)(2,1)S(1)} collective-permute-done((bf16[160,768]{1,0:T(8,128)(2,1)}, bf16[160,768]{1,0:T(8,128)(2,1)S(1)}, u32[]{:S(2)}, u32[]{:S(2)}) %collective-permute-start.19) | collective-permute-done | bytes 245792 | tf_op jit(solution)/shard_map/ppermute | solution.py:537
  126.0 3.6 %collective-permute-done.20.refs_7_.refs_14_ = bf16[160,768]{1,0:T(8,128)(2,1)S(1)} collective-permute-done((bf16[160,768]{1,0:T(8,128)(2,1)S(1)}, bf16[160,768]{1,0:T(8,128)(2,1)S(1)}, u32[]{:S(2)}, u32[]{:S(2)}) %collective-permute-start.20) | collective-permute-done | bytes 245792 | tf_op jit(solution)/shard_map/ppermute | solution.py:537
  129.6 1.6 scaled_hid.1
  131.2 0.7 low_dense.1
  131.9 5.0 %first_grad.1 = (f32[8,32,768]{2,1,0:T(8,128)S(1)}, bf16[8,32,768]{2,1,0:T(8,128)(2,1)}, f32[8,128]{1,0:T(8,128)}) custom-call(s32[3]{0:T(128)S(1)} %pad_add_fusion.refs_0_, s32[128,8]{1,0:T(8,128)S(1)} %copy-done.9, bf16[128,8]{1,0:T(8,128)(2,1)S(1)} %copy.22.refs_2_.refs_3_, f32[128,512]{1,0:T(8,128)S(1)} %get-tuple-element.94.refs_3_.refs_4_, ...), custom_call_target="tpu_custom_call" | custom-call | flops 1 | bytes 1 | tf_op jit(solution)/shard_map/first_grad/pallas_call | solution.py:52
  136.9 2.6 %collective-permute-start.21 = (bf16[160,768]{1,0:T(8,128)(2,1)}, bf16[160,768]{1,0:T(8,128)(2,1)S(1)}, u32[]{:S(2)}, u32[]{:S(2)}) collective-permute-start(bf16[160,768]{1,0:T(8,128)(2,1)} %get-tuple-element.96), channel_id=1, source_target_pairs={{0,20},{4,16},{8,28},{12,24},{16,4},{20,0},{24,12},{28,8},{1,21},{... | collective-permute-start | bytes 737288 | tf_op jit(solution)/shard_map/ppermute | solution.py:537
  139.5 5.0 %all-to-all-start.1 = ((bf16[8,64,128]{2,1,0:T(8,128)(2,1)}), bf16[8,64,128]{2,1,0:T(8,128)(2,1)S(1)}, u32[]{:S(2)}, u32[]{:S(2)}) async-start(bf16[8,64,128]{2,1,0:T(8,128)(2,1)} %get-tuple-element.98), calls=%async_computation.1 | async-start | bytes 262144 | tf_op jit(solution)/shard_map/all_to_all | solution.py:543
  144.5 1.4 first_sum.1
  145.9 6.9 %collective-permute-done.21.refs_11_.refs_13_ = bf16[160,768]{1,0:T(8,128)(2,1)S(1)} collective-permute-done((bf16[160,768]{1,0:T(8,128)(2,1)}, bf16[160,768]{1,0:T(8,128)(2,1)S(1)}, u32[]{:S(2)}, u32[]{:S(2)}) %collective-permute-start.21) | collective-permute-done | bytes 245792 | tf_op jit(solution)/shard_map/ppermute | solution.py:537
  152.8 2.3 %all-to-all-done.1.refs_1_ = bf16[8,64,128]{2,1,0:T(8,128)(2,1)S(1)} async-done(((bf16[8,64,128]{2,1,0:T(8,128)(2,1)}), bf16[8,64,128]{2,1,0:T(8,128)(2,1)S(1)}, u32[]{:S(2)}, u32[]{:S(2)}) %all-to-all-start.1) | async-done | bytes 131104 | tf_op jit(solution)/shard_map/all_to_all | solution.py:543
  155.1 3.7 %second_grad.1 = (f32[32,2048]{1,0:T(8,128)S(1)}, f32[32,2048]{1,0:T(8,128)S(1)}, f32[8,128]{1,0:T(8,128)}) custom-call(s32[3]{0:T(128)S(1)} %pad_add_fusion.refs_0_, bf16[8,64,128]{2,1,0:T(8,128)(2,1)S(1)} %all-to-all-done.1.refs_1_, bf16[128,2304]{1,0:T(8,128)(2,1)} %copy-done.2, bf16[128,2304]{1,0:T(8,128)(2,1)} %copy-done.3, ...), custom_call_target="tpu_custom_call" | custom-call | flops 1 | bytes 20000000 | tf_op jit(solution)/shard_map/second_grad/pallas_call | solution.py:52
  158.8 0.1 collective-permute-start.25
  158.9 5.5 %all-to-all-start.2 = ((bf16[8,32,768]{2,1,0:T(8,128)(2,1)}), bf16[8,32,768]{2,1,0:T(8,128)(2,1)S(1)}, u32[]{:S(2)}, u32[]{:S(2)}) async-start(bf16[8,32,768]{2,1,0:T(8,128)(2,1)} %get-tuple-element.105), calls=%async_computation.2 | async-start | bytes 786432 | tf_op jit(solution)/shard_map/all_to_all | solution.py:543
  164.4 2.4 %collective-permute-start.22 = (bf16[160,768]{1,0:T(8,128)(2,1)}, bf16[160,768]{1,0:T(8,128)(2,1)S(1)}, u32[]{:S(2)}, u32[]{:S(2)}) collective-permute-start(bf16[160,768]{1,0:T(8,128)(2,1)} %copy-done.28), channel_id=1, source_target_pairs={{0,28},{4,24},{8,20},{12,16},{16,12},{20,8},{24,4},{28,0},{1,29},{... | collective-permute-start | bytes 737288 | tf_op jit(solution)/shard_map/ppermute | solution.py:537
  166.8 0.7 add_bitcast_fusion
  167.5 19.2 %collective-permute-done.22.refs_15_ = bf16[160,768]{1,0:T(8,128)(2,1)S(1)} collective-permute-done((bf16[160,768]{1,0:T(8,128)(2,1)}, bf16[160,768]{1,0:T(8,128)(2,1)S(1)}, u32[]{:S(2)}, u32[]{:S(2)}) %collective-permute-start.22) | collective-permute-done | bytes 245792 | tf_op jit(solution)/shard_map/ppermute | solution.py:537
  186.7 0.7 copy-done.29
  187.4 7.9 %finish.1 = (bf16[1024,768]{1,0:T(8,128)(2,1)}, f32[128,8]{1,0:T(8,128)S(1)}, f32[8,128]{1,0:T(8,128)}) custom-call(s32[3]{0:T(128)S(1)} %pad_add_fusion.refs_0_, s32[128,8]{1,0:T(8,128)S(1)} %copy-done.9, s32[128,8]{1,0:T(8,128)S(1)} %copy-done.9, bf16[128,8]{1,0:T(8,128)(2,1)S(1)} %copy.22.refs_2_.refs_3_, ...), custom_call_target="tpu_custom_call" | custom-call | flops 1 | bytes 1 | tf_op jit(solution)/shard_map/finish/pallas_call | solution.py:52
  195.3 1.5 collective-permute-start.24
  196.8 0.7 convert_reduce_fusion
  197.5 2.1 %collective-permute-done.24 = f32[128,8]{1,0:T(8,128)S(1)} collective-permute-done((f32[128,8]{1,0:T(8,128)S(1)}, f32[128,8]{1,0:T(8,128)S(1)}, u32[]{:S(2)}, u32[]{:S(2)}) %collective-permute-start.24) | collective-permute-done | bytes 4128 | tf_op jit(solution)/shard_map/ppermute | solution.py:531
  199.6 0.7 copy.23
  (83 shorter events, 0.3 us)
Async XLA Ops:
  0.6 29.9 %collective-permute-start.2 = (bf16[1536,2048]{1,0:T(8,128)(2,1)}, bf16[1536,2048]{1,0:T(8,128)(2,1)}, u32[]{:S(2)}, u32[]{:S(2)}) collective-permute-start(bf16[1536,2048]{1,0:T(8,128)(2,1)} %bitcast.25), channel_id=1, source_target_pairs={{0,1},{1,0},{2,3},{3,2},{4,5},{5,4},{6,7},{7,6},{8,9},{9,8},{10,11... | collective-permute-start | bytes 18874376 | tf_op jit(solution)/shard_map/ppermute | solution.py:540
  1.5 41.6 %copy-start.8 = (s32[128,8]{1,0:T(8,128)}, s32[128,8]{1,0:T(8,128)S(1)}, u32[]{:S(2)}) copy-start(s32[128,8]{1,0:T(8,128)S(1)} %copy.20.refs_3_.refs_1_.refs_2_) | copy-start | bytes 12292
  2.6 1.0 copy-start.18
  4.4 38.7 %copy-start.2 = (bf16[128,2304]{1,0:T(8,128)(2,1)}, bf16[128,2304]{1,0:T(8,128)(2,1)S(1)}, u32[]{:S(2)}) copy-start(bf16[128,2304]{1,0:T(8,128)(2,1)S(1)} %get-tuple-element.57.refs_1_.refs_5_.refs_2_) | copy-start | bytes 1769476
  4.4 26.1 %collective-permute-start = (bf16[128,2304]{1,0:T(8,128)(2,1)S(1)}, bf16[128,2304]{1,0:T(8,128)(2,1)S(1)}, u32[]{:S(2)}, u32[]{:S(2)}) collective-permute-start(bf16[128,2304]{1,0:T(8,128)(2,1)S(1)} %get-tuple-element.57.refs_1_.refs_5_.refs_2_), channel_id=1, source_target_pairs={{0,8},{4,12},{8,0},{12,4},{16,24},{20,28},{24,16},{28,20},{1,9},{5... | collective-permute-start | bytes 1769480 | tf_op jit(solution)/shard_map/ppermute | solution.py:537
  4.5 38.6 %collective-permute-start.4 = (bf16[128,2304]{1,0:T(8,128)(2,1)S(1)}, bf16[128,2304]{1,0:T(8,128)(2,1)S(1)}, u32[]{:S(2)}, u32[]{:S(2)}) collective-permute-start(bf16[128,2304]{1,0:T(8,128)(2,1)S(1)} %get-tuple-element.57.refs_1_.refs_5_.refs_2_), channel_id=1, source_target_pairs={{0,16},{4,20},{8,24},{12,28},{16,0},{20,4},{24,8},{28,12},{1,17},{... | collective-permute-start | bytes 1769480 | tf_op jit(solution)/shard_map/ppermute | solution.py:537
  7.5 41.9 %collective-permute-start.3 = (bf16[128,2304]{1,0:T(8,128)(2,1)S(1)}, bf16[128,2304]{1,0:T(8,128)(2,1)S(1)}, u32[]{:S(2)}, u32[]{:S(2)}) collective-permute-start(bf16[128,2304]{1,0:T(8,128)(2,1)S(1)} %get-tuple-element.57.refs_1_.refs_5_.refs_2_), channel_id=1, source_target_pairs={{0,4},{4,0},{8,12},{12,8},{16,20},{20,16},{24,28},{28,24},{1,5},{5... | collective-permute-start | bytes 1769480 | tf_op jit(solution)/shard_map/ppermute | solution.py:537
  9.0 2.2 %collective-permute-start.1 = (bf16[32,2048]{1,0:T(8,128)(2,1)}, bf16[32,2048]{1,0:T(8,128)(2,1)S(1)}, u32[]{:S(2)}, u32[]{:S(2)}) collective-permute-start(bf16[32,2048]{1,0:T(8,128)(2,1)} %bitcast.15), channel_id=1, source_target_pairs={{0,1},{1,0},{2,3},{3,2},{4,5},{5,4},{6,7},{7,6},{8,9},{9,8},{10,11... | collective-permute-start | bytes 393224 | tf_op jit(solution)/shard_map/ppermute | solution.py:540
  30.5 17.4 %copy-start.3 = (bf16[128,2304]{1,0:T(8,128)(2,1)}, bf16[128,2304]{1,0:T(8,128)(2,1)S(1)}, u32[]{:S(2)}) copy-start(bf16[128,2304]{1,0:T(8,128)(2,1)S(1)} %collective-permute-done.refs_2_.refs_6_.refs_3_) | copy-start | bytes 1769476
  30.5 1.0 copy-start.10
  31.6 17.9 %copy-start.11 = (bf16[1,32,2048]{2,1,0:T(8,128)(2,1)S(1)}, bf16[1,32,2048]{2,1,0:T(8,128)(2,1)}, u32[]{:S(2)}) copy-start(bf16[1,32,2048]{2,1,0:T(8,128)(2,1)} %param.13) | copy-start | bytes 393220
  43.7 17.9 %copy-start.1 = (bf16[128,2304]{1,0:T(8,128)(2,1)}, bf16[128,2304]{1,0:T(8,128)(2,1)S(1)}, u32[]{:S(2)}) copy-start(bf16[128,2304]{1,0:T(8,128)(2,1)S(1)} %get-tuple-element.61.refs_2_.refs_8_.refs_5_) | copy-start | bytes 1769476
  43.7 18.9 %collective-permute-start.6 = (bf16[128,2304]{1,0:T(8,128)(2,1)S(1)}, bf16[128,2304]{1,0:T(8,128)(2,1)S(1)}, u32[]{:S(2)}, u32[]{:S(2)}) collective-permute-start(bf16[128,2304]{1,0:T(8,128)(2,1)S(1)} %get-tuple-element.61.refs_2_.refs_8_.refs_5_), channel_id=1, source_target_pairs={{0,8},{4,12},{8,0},{12,4},{16,24},{20,28},{24,16},{28,20},{1,9},{5... | collective-permute-start | bytes 1769480 | tf_op jit(solution)/shard_map/ppermute | solution.py:537
  46.2 15.7 %collective-permute-start.7 = (bf16[320,768]{1,0:T(8,128)(2,1)S(1)}, bf16[320,768]{1,0:T(8,128)(2,1)S(1)}, u32[]{:S(2)}, u32[]{:S(2)}) collective-permute-start(bf16[320,768]{1,0:T(8,128)(2,1)S(1)} %get-tuple-element.65), channel_id=1, source_target_pairs={{0,2},{2,0},{1,3},{3,1},{4,6},{6,4},{5,7},{7,5},{8,10},{10,8},{9,1... | collective-permute-start | bytes 1474568 | tf_op jit(solution)/shard_map/ppermute | solution.py:531
  47.9 17.2 %collective-permute-start.5 = (bf16[128,2304]{1,0:T(8,128)(2,1)S(1)}, bf16[128,2304]{1,0:T(8,128)(2,1)S(1)}, u32[]{:S(2)}, u32[]{:S(2)}) collective-permute-start(bf16[128,2304]{1,0:T(8,128)(2,1)S(1)} %collective-permute-done.refs_2_.refs_6_.refs_3_), channel_id=1, source_target_pairs={{0,4},{4,0},{8,12},{12,8},{16,20},{20,16},{24,28},{28,24},{1,5},{5... | collective-permute-start | bytes 1769480 | tf_op jit(solution)/shard_map/ppermute | solution.py:537
  49.4 11.6 %copy-start.4 = (bf16[128,2304]{1,0:T(8,128)(2,1)}, bf16[128,2304]{1,0:T(8,128)(2,1)S(1)}, u32[]{:S(2)}) copy-start(bf16[128,2304]{1,0:T(8,128)(2,1)S(1)} %collective-permute-done.3.refs_1_.refs_7_.refs_4_) | copy-start | bytes 1769476
  49.4 12.5 %copy-start.20 = (bf16[320,768]{1,0:T(8,128)(2,1)S(1)}, bf16[320,768]{1,0:T(8,128)(2,1)}, u32[]{:S(2)}) copy-start(bf16[320,768]{1,0:T(8,128)(2,1)} %get-tuple-element.64.refs_1_) | copy-start | bytes 1474564
  61.0 17.4 %collective-permute-start.10 = (bf16[320,768]{1,0:T(8,128)(2,1)S(1)}, bf16[320,768]{1,0:T(8,128)(2,1)S(1)}, u32[]{:S(2)}, u32[]{:S(2)}) collective-permute-start(bf16[320,768]{1,0:T(8,128)(2,1)S(1)} %get-tuple-element.72), channel_id=1, source_target_pairs={{0,2},{2,0},{1,3},{3,1},{4,6},{6,4},{5,7},{7,5},{8,10},{10,8},{9,1... | collective-permute-start | bytes 1474568 | tf_op jit(solution)/shard_map/ppermute | solution.py:531
  61.6 21.0 %collective-permute-start.8 = (bf16[128,2304]{1,0:T(8,128)(2,1)S(1)}, bf16[128,2304]{1,0:T(8,128)(2,1)S(1)}, u32[]{:S(2)}, u32[]{:S(2)}) collective-permute-start(bf16[128,2304]{1,0:T(8,128)(2,1)S(1)} %get-tuple-element.61.refs_2_.refs_8_.refs_5_), channel_id=1, source_target_pairs={{0,4},{4,0},{8,12},{12,8},{16,20},{20,16},{24,28},{28,24},{1,5},{5... | collective-permute-start | bytes 1769480 | tf_op jit(solution)/shard_map/ppermute | solution.py:537
  62.6 0.7 copy-start.23
  63.3 13.5 %copy-start = (bf16[128,2304]{1,0:T(8,128)(2,1)}, bf16[128,2304]{1,0:T(8,128)(2,1)S(1)}, u32[]{:S(2)}) copy-start(bf16[128,2304]{1,0:T(8,128)(2,1)S(1)} %get-tuple-element.68.refs_2_.refs_10_.refs_7_) | copy-start | bytes 1769476
  63.3 27.2 %collective-permute-start.9 = (bf16[128,2304]{1,0:T(8,128)(2,1)S(1)}, bf16[128,2304]{1,0:T(8,128)(2,1)S(1)}, u32[]{:S(2)}, u32[]{:S(2)}) collective-permute-start(bf16[128,2304]{1,0:T(8,128)(2,1)S(1)} %get-tuple-element.68.refs_2_.refs_10_.refs_7_), channel_id=1, source_target_pairs={{0,4},{4,0},{8,12},{12,8},{16,20},{20,16},{24,28},{28,24},{1,5},{5... | collective-permute-start | bytes 1769480 | tf_op jit(solution)/shard_map/ppermute | solution.py:537
  65.0 13.4 %collective-permute-start.11 = (bf16[160,768]{1,0:T(8,128)(2,1)S(1)}, bf16[160,768]{1,0:T(8,128)(2,1)S(1)}, u32[]{:S(2)}, u32[]{:S(2)}) collective-permute-start(bf16[160,768]{1,0:T(8,128)(2,1)S(1)} %get-tuple-element.74), channel_id=1, source_target_pairs={{0,8},{4,12},{8,0},{12,4},{16,24},{20,28},{24,16},{28,20},{1,9},{5... | collective-permute-start | bytes 737288 | tf_op jit(solution)/shard_map/ppermute | solution.py:537
  65.1 11.8 %copy-start.5 = (bf16[128,2304]{1,0:T(8,128)(2,1)}, bf16[128,2304]{1,0:T(8,128)(2,1)S(1)}, u32[]{:S(2)}) copy-start(bf16[128,2304]{1,0:T(8,128)(2,1)S(1)} %collective-permute-done.5.refs_1_.refs_9_.refs_6_) | copy-start | bytes 1769476
  65.1 13.3 %copy-start.21 = (bf16[320,768]{1,0:T(8,128)(2,1)S(1)}, bf16[320,768]{1,0:T(8,128)(2,1)}, u32[]{:S(2)}) copy-start(bf16[320,768]{1,0:T(8,128)(2,1)} %get-tuple-element.71.refs_1_) | copy-start | bytes 1474564
  76.9 25.3 %collective-permute-start.12 = (bf16[320,768]{1,0:T(8,128)(2,1)S(1)}, bf16[320,768]{1,0:T(8,128)(2,1)S(1)}, u32[]{:S(2)}, u32[]{:S(2)}) collective-permute-start(bf16[320,768]{1,0:T(8,128)(2,1)S(1)} %get-tuple-element.78), channel_id=1, source_target_pairs={{0,2},{2,0},{1,3},{3,1},{4,6},{6,4},{5,7},{7,5},{8,10},{10,8},{9,1... | collective-permute-start | bytes 1474568 | tf_op jit(solution)/shard_map/ppermute | solution.py:531
  78.4 23.7 %copy-start.12 = (bf16[160,768]{1,0:T(8,128)(2,1)}, bf16[160,768]{1,0:T(8,128)(2,1)S(1)}, u32[]{:S(2)}) copy-start(bf16[160,768]{1,0:T(8,128)(2,1)S(1)} %collective-permute-done.11.refs_4_.refs_10_) | copy-start | bytes 737284
  79.1 23.1 %collective-permute-start.13 = (bf16[160,768]{1,0:T(8,128)(2,1)S(1)}, bf16[160,768]{1,0:T(8,128)(2,1)S(1)}, u32[]{:S(2)}, u32[]{:S(2)}) collective-permute-start(bf16[160,768]{1,0:T(8,128)(2,1)S(1)} %get-tuple-element.80), channel_id=1, source_target_pairs={{0,4},{4,0},{8,12},{12,8},{16,20},{20,16},{24,28},{28,24},{1,5},{5... | collective-permute-start | bytes 737288 | tf_op jit(solution)/shard_map/ppermute | solution.py:537
  79.7 22.5 %collective-permute-start.14 = (bf16[160,768]{1,0:T(8,128)(2,1)S(1)}, bf16[160,768]{1,0:T(8,128)(2,1)S(1)}, u32[]{:S(2)}, u32[]{:S(2)}) collective-permute-start(bf16[160,768]{1,0:T(8,128)(2,1)S(1)} %get-tuple-element.81), channel_id=1, source_target_pairs={{0,16},{4,20},{8,24},{12,28},{16,0},{20,4},{24,8},{28,12},{1,17},{... | collective-permute-start | bytes 737288 | tf_op jit(solution)/shard_map/ppermute | solution.py:537
  82.7 19.4 %copy-start.6 = (bf16[128,2304]{1,0:T(8,128)(2,1)}, bf16[128,2304]{1,0:T(8,128)(2,1)S(1)}, u32[]{:S(2)}) copy-start(bf16[128,2304]{1,0:T(8,128)(2,1)S(1)} %collective-permute-done.8.refs_1_.refs_11_.refs_8_) | copy-start | bytes 1769476
  90.5 11.6 %copy-start.7 = (bf16[128,2304]{1,0:T(8,128)(2,1)}, bf16[128,2304]{1,0:T(8,128)(2,1)S(1)}, u32[]{:S(2)}) copy-start(bf16[128,2304]{1,0:T(8,128)(2,1)S(1)} %collective-permute-done.9.refs_2_.refs_12_.refs_9_) | copy-start | bytes 1769476
  90.5 11.7 %copy-start.22 = (bf16[320,768]{1,0:T(8,128)(2,1)S(1)}, bf16[320,768]{1,0:T(8,128)(2,1)}, u32[]{:S(2)}) copy-start(bf16[320,768]{1,0:T(8,128)(2,1)} %get-tuple-element.77.refs_1_) | copy-start | bytes 1474564
  90.5 13.0 %copy-start.24 = (bf16[2,64,128]{2,1,0:T(8,128)(2,1)S(1)}, bf16[2,64,128]{2,1,0:T(8,128)(2,1)}, u32[]{:S(2)}) copy-start(bf16[2,64,128]{2,1,0:T(8,128)(2,1)} %get-tuple-element.59.refs_1_) | copy-start | bytes 98308
  90.5 13.0 %copy-start.25 = (bf16[2,64,128]{2,1,0:T(8,128)(2,1)S(1)}, bf16[2,64,128]{2,1,0:T(8,128)(2,1)}, u32[]{:S(2)}) copy-start(bf16[2,64,128]{2,1,0:T(8,128)(2,1)} %get-tuple-element.63.refs_2_) | copy-start | bytes 98308
  90.5 13.0 %copy-start.26 = (bf16[2,64,128]{2,1,0:T(8,128)(2,1)S(1)}, bf16[2,64,128]{2,1,0:T(8,128)(2,1)}, u32[]{:S(2)}) copy-start(bf16[2,64,128]{2,1,0:T(8,128)(2,1)} %get-tuple-element.70.refs_3_) | copy-start | bytes 98308
  102.1 9.7 %copy-start.9 = (s32[128,8]{1,0:T(8,128)S(1)}, s32[128,8]{1,0:T(8,128)}, u32[]{:S(2)}) copy-start(s32[128,8]{1,0:T(8,128)} %copy-done.8) | copy-start | bytes 12292
  102.1 19.2 %copy-start.30 = (bf16[128,8]{0,1:T(8,128)(2,1)S(1)}, bf16[128,8]{0,1:T(8,128)(2,1)}, u32[]{:S(2)}) copy-start(bf16[128,8]{0,1:T(8,128)(2,1)} %param.10) | copy-start | bytes 6148
  102.1 19.3 %copy-start.19 = (bf16[320,768]{1,0:T(8,128)(2,1)S(1)}, bf16[320,768]{1,0:T(8,128)(2,1)}, u32[]{:S(2)}) copy-start(bf16[320,768]{1,0:T(8,128)(2,1)} %get-tuple-element.87.refs_1_) | copy-start | bytes 1474564
  102.2 34.8 %copy-start.13 = (bf16[160,768]{1,0:T(8,128)(2,1)}, bf16[160,768]{1,0:T(8,128)(2,1)S(1)}, u32[]{:S(2)}) copy-start(bf16[160,768]{1,0:T(8,128)(2,1)S(1)} %collective-permute-done.13.refs_4_.refs_9_) | copy-start | bytes 737284
  102.2 34.7 %copy-start.14 = (bf16[160,768]{1,0:T(8,128)(2,1)}, bf16[160,768]{1,0:T(8,128)(2,1)S(1)}, u32[]{:S(2)}) copy-start(bf16[160,768]{1,0:T(8,128)(2,1)S(1)} %collective-permute-done.14.refs_5_.refs_12_) | copy-start | bytes 737284
  103.5 0.8 copy-start.27
  106.0 5.8 %collective-permute-start.16 = (bf16[8,32,768]{2,1,0:T(8,128)(2,1)S(1)}, bf16[8,32,768]{2,1,0:T(8,128)(2,1)S(1)}, u32[]{:S(2)}, u32[]{:S(2)}) collective-permute-start(bf16[8,32,768]{2,1,0:T(8,128)(2,1)S(1)} %get-tuple-element.84), channel_id=1, source_target_pairs={{0,1},{1,0},{2,3},{3,2},{4,5},{5,4},{6,7},{7,6},{8,9},{9,8},{10,11... | collective-permute-start | bytes 1179656 | tf_op jit(solution)/shard_map/ppermute | solution.py:540
  106.0 15.4 %collective-permute-start.18 = (bf16[320,768]{1,0:T(8,128)(2,1)}, bf16[320,768]{1,0:T(8,128)(2,1)}, u32[]{:S(2)}, u32[]{:S(2)}) collective-permute-start(bf16[320,768]{1,0:T(8,128)(2,1)} %get-tuple-element.88), channel_id=1, source_target_pairs={{0,2},{2,0},{1,3},{3,1},{4,6},{6,4},{5,7},{7,5},{8,10},{10,8},{9,1... | collective-permute-start | bytes 1474568 | tf_op jit(solution)/shard_map/ppermute | solution.py:531
  107.5 12.3 %all-to-all-start = ((bf16[8,64,128]{2,1,0:T(8,128)(2,1)}), bf16[8,64,128]{2,1,0:T(8,128)(2,1)S(1)}, u32[]{:S(2)}, u32[]{:S(2)}) async-start(bf16[8,64,128]{2,1,0:T(8,128)(2,1)} %get-tuple-element.83), calls=%async_computation | async-start | bytes 262144 | tf_op jit(solution)/shard_map/all_to_all | solution.py:543
  115.4 14.2 %collective-permute-start.17 = (f32[128,512]{1,0:T(8,128)S(1)}, f32[128,512]{1,0:T(8,128)S(1)}, u32[]{:S(2)}, u32[]{:S(2)}) collective-permute-start(f32[128,512]{1,0:T(8,128)S(1)} %get-tuple-element.86.refs_3_), channel_id=1, source_target_pairs={{0,2},{2,0},{1,3},{3,1},{4,6},{6,4},{5,7},{7,5},{8,10},{10,8},{9,1... | collective-permute-start | bytes 786440 | tf_op jit(solution)/shard_map/ppermute | solution.py:531
  116.0 10.0 %collective-permute-start.19 = (bf16[160,768]{1,0:T(8,128)(2,1)}, bf16[160,768]{1,0:T(8,128)(2,1)S(1)}, u32[]{:S(2)}, u32[]{:S(2)}) collective-permute-start(bf16[160,768]{1,0:T(8,128)(2,1)} %get-tuple-element.91), channel_id=1, source_target_pairs={{0,12},{4,8},{8,4},{12,0},{16,28},{20,24},{24,20},{28,16},{1,13},{... | collective-permute-start | bytes 737288 | tf_op jit(solution)/shard_map/ppermute | solution.py:537
  117.5 12.1 %collective-permute-start.20 = (bf16[160,768]{1,0:T(8,128)(2,1)S(1)}, bf16[160,768]{1,0:T(8,128)(2,1)S(1)}, u32[]{:S(2)}, u32[]{:S(2)}) collective-permute-start(bf16[160,768]{1,0:T(8,128)(2,1)S(1)} %get-tuple-element.92), channel_id=1, source_target_pairs={{0,24},{4,28},{8,16},{12,20},{16,8},{20,12},{24,0},{28,4},{1,25},{... | collective-permute-start | bytes 737288 | tf_op jit(solution)/shard_map/ppermute | solution.py:537
  119.8 11.4 %collective-permute-start.15 = (bf16[8,64,128]{2,1,0:T(8,128)(2,1)S(1)}, bf16[8,64,128]{2,1,0:T(8,128)(2,1)S(1)}, u32[]{:S(2)}, u32[]{:S(2)}) collective-permute-start(bf16[8,64,128]{2,1,0:T(8,128)(2,1)S(1)} %all-to-all-done.refs_1_), channel_id=1, source_target_pairs={{0,2},{2,0},{1,3},{3,1},{4,6},{6,4},{5,7},{7,5},{8,10},{10,8},{9,1... | collective-permute-start | bytes 393224 | tf_op jit(solution)/shard_map/ppermute | solution.py:531
  123.2 13.7 %copy-start.28 = (bf16[160,768]{1,0:T(8,128)(2,1)}, bf16[160,768]{1,0:T(8,128)(2,1)S(1)}, u32[]{:S(2)}) copy-start(bf16[160,768]{1,0:T(8,128)(2,1)S(1)} %get-tuple-element.97) | copy-start | bytes 737284
  126.0 61.4 %copy-start.15 = (bf16[160,768]{1,0:T(8,128)(2,1)}, bf16[160,768]{1,0:T(8,128)(2,1)S(1)}, u32[]{:S(2)}) copy-start(bf16[160,768]{1,0:T(8,128)(2,1)S(1)} %collective-permute-done.19.refs_6_.refs_11_) | copy-start | bytes 737284
  129.6 57.8 %copy-start.16 = (bf16[160,768]{1,0:T(8,128)(2,1)}, bf16[160,768]{1,0:T(8,128)(2,1)S(1)}, u32[]{:S(2)}) copy-start(bf16[160,768]{1,0:T(8,128)(2,1)S(1)} %collective-permute-done.20.refs_7_.refs_14_) | copy-start | bytes 737284
  136.9 7.6 %collective-permute-start.23 = (bf16[8,32,768]{2,1,0:T(8,128)(2,1)}, bf16[8,32,768]{2,1,0:T(8,128)(2,1)S(1)}, u32[]{:S(2)}, u32[]{:S(2)}) collective-permute-start(bf16[8,32,768]{2,1,0:T(8,128)(2,1)} %get-tuple-element.101), channel_id=1, source_target_pairs={{0,1},{1,0},{2,3},{3,2},{4,5},{5,4},{6,7},{7,6},{8,9},{9,8},{10,11... | collective-permute-start | bytes 1179656 | tf_op jit(solution)/shard_map/ppermute | solution.py:540
  136.9 15.8 %collective-permute-start.21 = (bf16[160,768]{1,0:T(8,128)(2,1)}, bf16[160,768]{1,0:T(8,128)(2,1)S(1)}, u32[]{:S(2)}, u32[]{:S(2)}) collective-permute-start(bf16[160,768]{1,0:T(8,128)(2,1)} %get-tuple-element.96), channel_id=1, source_target_pairs={{0,20},{4,16},{8,28},{12,24},{16,4},{20,0},{24,12},{28,8},{1,21},{... | collective-permute-start | bytes 737288 | tf_op jit(solution)/shard_map/ppermute | solution.py:537
  139.5 15.6 %all-to-all-start.1 = ((bf16[8,64,128]{2,1,0:T(8,128)(2,1)}), bf16[8,64,128]{2,1,0:T(8,128)(2,1)S(1)}, u32[]{:S(2)}, u32[]{:S(2)}) async-start(bf16[8,64,128]{2,1,0:T(8,128)(2,1)} %get-tuple-element.98), calls=%async_computation.1 | async-start | bytes 262144 | tf_op jit(solution)/shard_map/all_to_all | solution.py:543
  152.8 34.6 %copy-start.17 = (bf16[160,768]{1,0:T(8,128)(2,1)}, bf16[160,768]{1,0:T(8,128)(2,1)S(1)}, u32[]{:S(2)}) copy-start(bf16[160,768]{1,0:T(8,128)(2,1)S(1)} %collective-permute-done.21.refs_11_.refs_13_) | copy-start | bytes 737284
  158.8 8.0 %collective-permute-start.25 = (f32[32,2048]{1,0:T(8,128)S(1)}, f32[32,2048]{1,0:T(8,128)S(1)}, u32[]{:S(2)}, u32[]{:S(2)}) collective-permute-start(f32[32,2048]{1,0:T(8,128)S(1)} %get-tuple-element.109), channel_id=1, source_target_pairs={{0,1},{1,0},{2,3},{3,2},{4,5},{5,4},{6,7},{7,6},{8,9},{9,8},{10,11... | collective-permute-start | bytes 786440 | tf_op jit(solution)/shard_map/ppermute | solution.py:540
  158.9 27.9 %all-to-all-start.2 = ((bf16[8,32,768]{2,1,0:T(8,128)(2,1)}), bf16[8,32,768]{2,1,0:T(8,128)(2,1)S(1)}, u32[]{:S(2)}, u32[]{:S(2)}) async-start(bf16[8,32,768]{2,1,0:T(8,128)(2,1)} %get-tuple-element.105), calls=%async_computation.2 | async-start | bytes 786432 | tf_op jit(solution)/shard_map/all_to_all | solution.py:543
  164.4 22.3 %collective-permute-start.22 = (bf16[160,768]{1,0:T(8,128)(2,1)}, bf16[160,768]{1,0:T(8,128)(2,1)S(1)}, u32[]{:S(2)}, u32[]{:S(2)}) collective-permute-start(bf16[160,768]{1,0:T(8,128)(2,1)} %copy-done.28), channel_id=1, source_target_pairs={{0,28},{4,24},{8,20},{12,16},{16,12},{20,8},{24,4},{28,0},{1,29},{... | collective-permute-start | bytes 737288 | tf_op jit(solution)/shard_map/ppermute | solution.py:537
  186.7 0.7 copy-start.29
  195.3 4.3 %collective-permute-start.24 = (f32[128,8]{1,0:T(8,128)S(1)}, f32[128,8]{1,0:T(8,128)S(1)}, u32[]{:S(2)}, u32[]{:S(2)}) collective-permute-start(f32[128,8]{1,0:T(8,128)S(1)} %get-tuple-element.107), channel_id=1, source_target_pairs={{0,2},{2,0},{1,3},{3,1},{4,6},{6,4},{5,7},{7,5},{8,10},{10,8},{9,1... | collective-permute-start | bytes 12296 | tf_op jit(solution)/shard_map/ppermute | solution.py:531

commit v7 on v6

--- a/solution.py
+++ b/solution.py
@@ -14,7 +14,6 @@
 TN = (((0,), (0,)), ((), ()))
 NN = (((1,), (0,)), ((), ()))
 SMALL = pl.CostEstimate(flops=1, bytes_accessed=1, transcendentals=0)
-LONG = pl.CostEstimate(flops=1, bytes_accessed=2 * 10**7, transcendentals=0)
 ANY = pl.BlockSpec(memory_space=pl.ANY)
 SMEM = pl.BlockSpec(memory_space=pltpu.SMEM)
 
@@ -127,9 +126,9 @@
 def expert_rows_kernel(slots, tiles, shares, batch, route_row, at_ref, *rest):
     grads, seconds, downs = rest[:batch], rest[batch : batch + 2], rest[batch + 2 : batch + 4]
     *outs, low_ref = rest[batch + 4 : batch + 5 + shares]
-    block_ref, rows_ref, tiles_ref, block_sems, sems = rest[batch + 5 + shares :]
+    block_ref, turned_ref, tiles_ref, block_sems, sems = rest[batch + 5 + shares :]
     tile = tiles_ref.shape[1]
-    feats = rows_ref.shape[2]
+    feats = turned_ref.shape[1]
     toks = block_ref.shape[1]
     blocks = [
         pltpu.make_async_copy(ref, block_ref.at[k], block_sems.at[k]) for k, ref in enumerate(grads)
@@ -146,28 +145,33 @@
         copy.start()
 
     before = jnp.where(iota((toks, toks), 0) < iota((toks, toks), 1), 1.0, 0.0).astype(BF16)
-    slot = iota((slots, toks), 0).astype(F32)
+    columns = turned_ref.shape[2]
+    slot = iota((columns, batch * toks), 0).astype(F32)
     second = jnp.concatenate([ref[...] for ref in seconds], axis=0)
+    routes = []
     for k in range(batch):
         blocks[k].wait()
-        routes = block_ref[k, pl.ds(route_row, 16), pl.ds(feats, toks)].astype(F32)
-        picks = []
-        for q in range(2):
-            expert = at_ref[1] * 2 + lax.bitwise_xor(at_ref[2], q)
-            hits = jnp.where(routes == expert.astype(F32), 1.0, 0.0)
+        routes.append(block_ref[k, pl.ds(route_row, 16), pl.ds(feats, toks)].astype(F32))
+    grad = block_ref[:, :, pl.ds(0, feats)].reshape(batch * toks, feats)
+    for q in range(2):
+        expert = at_ref[1] * 2 + lax.bitwise_xor(at_ref[2], q)
+        targets = []
+        for k in range(batch):
+            hits = jnp.where(routes[k] == expert.astype(F32), 1.0, 0.0)
             mine = jnp.max(hits, axis=0, keepdims=True)
             pos = dot(jnp.broadcast_to(mine, (16, toks)).astype(BF16), before, NN)[:1]
-            picks.append(jnp.where((slot == pos) & (mine > 0.0), 1.0, 0.0).astype(BF16))
-        grad = block_ref[k, :, pl.ds(0, feats)]
-        rows = dot(jnp.concatenate(picks, axis=0), grad, NN).astype(BF16)
-        for q in range(2):
-            rows_ref[q, pl.ds(k * slots, slots), :] = rows[q * slots : (q + 1) * slots]
-        low_ref[k] = dot(second, grad, NT).astype(BF16)
-
+            targets.append(jnp.where(mine > 0.0, pos + float(k * slots), -1.0))
+        pick = jnp.where(slot == jnp.concatenate(targets, axis=1), 1.0, 0.0)
+        turned_ref[q] = dot(grad, pick.T.astype(BF16), TN).astype(BF16)
+    low = dot(second, grad, NT).astype(BF16)
+    for k in range(batch):
+        low_ref[k] = low[:, k * toks : (k + 1) * toks]
+
+    rows = batch * slots
     for n, (k, q, t) in enumerate(parts):
         weights[n].wait()
-        value = dot(rows_ref[q], tiles_ref[n], NT).astype(BF16)
-        outs[k][pl.ds(q * batch * slots, batch * slots), pl.ds(t * tile, tile)] = value
+        value = dot(tiles_ref[n], turned_ref[q], NN)
+        outs[k][pl.ds(q * rows, rows), pl.ds(t * tile, tile)] = value.T[:rows].astype(BF16)
 
 
 def expert_rows_call(order, grads, seconds, downs, shares, slots):
@@ -189,29 +193,13 @@
         [whole((rows, units))] * shares + [whole(low_shape)],
         scratch=[
             pltpu.VMEM((batch, toks, wide), BF16),
-            pltpu.VMEM((2, batch * slots, feats), BF16),
+            pltpu.VMEM((2, feats, -(-batch * slots // 128) * 128), BF16),
             pltpu.VMEM((count, tile, feats), BF16),
             pltpu.SemaphoreType.DMA((batch,)),
             pltpu.SemaphoreType.DMA((count,)),
         ],
         mib=28,
     )
-
-
-def gate_kernel(at_ref, block_ref, out_ref):
-    pass
-
-
-def gate_call(order, block):
-    return order.call(
-        gate_kernel,
-        "gate",
-        [block],
-        [ANY],
-        [(block.shape, block.dtype)],
-        [ANY],
-        input_output_aliases={1: 0},
-    )[0]
 
 
 def share_sum_kernel(parts, slots, at_ref, *refs):
@@ -381,15 +369,14 @@
         [((both // 2, feats), F32)] * 2,
         [block] * 2,
         grid=(steps,),
-        cost=LONG,
     )
 
 
 def first_grad_kernel(groups, steps, at_ref, index_ref, prob_ref, low_ref, hid_ref, *rest):
-    keep_ref, give_ref, sum_ref = rest
+    out_ref, sum_ref = rest
     step = pl.program_id(0)
     top = index_ref.shape[1]
-    rank = keep_ref.shape[1]
+    rank = out_ref.shape[1]
     low = spread_pairs(low_ref[...], top)
     column = pair_column(relative(at_ref, index_ref[...], groups).astype(F32))
     keep = expert_mask(column, low.shape[1], rank)
@@ -406,16 +393,18 @@
 
     @pl.when(step == steps - 1)
     def _():
-        for q, out_ref in enumerate((keep_ref, give_ref)):
-            half = sum_ref[pl.ds(q * groups * rank, groups * rank), :]
-            out_ref[...] = half.reshape(out_ref.shape).astype(out_ref.dtype)
+        for o in range(groups):
+            for q in range(2):
+                expert = 2 * lax.bitwise_xor(at_ref[1], o) + lax.bitwise_xor(at_ref[2], q)
+                rows = sum_ref[pl.ds((q * groups + o) * rank, rank), :]
+                out_ref[expert] = rows.astype(BF16)
 
 
 def first_grad_call(order, index, prob, low, hid, groups):
     (toks, top), (pairs, units) = index.shape, hid.shape
     width = low.shape[1]
     steps = 4
-    shape = (groups, width // groups // 2, units)
+    shape = (2 * groups, width // groups // 2, units)
     return order.call(
         functools.partial(first_grad_kernel, groups, steps),
         "first_grad",
@@ -426,28 +415,10 @@
             pl.BlockSpec((toks // steps, width), lambda i: (i, 0)),
             pl.BlockSpec((pairs // steps, units), lambda i: (i, 0)),
         ],
-        [(shape, F32), (shape, BF16)],
-        [whole(shape)] * 2,
+        [(shape, BF16)],
+        [whole(shape)],
         grid=(steps,),
         scratch=[pltpu.VMEM((width, units), F32)],
-    )
-
-
-def first_sum_kernel(at_ref, keep_ref, got_ref, out_ref):
-    for o in range(keep_ref.shape[0]):
-        total = keep_ref[o] + got_ref[o].astype(F32)
-        out_ref[lax.bitwise_xor(at_ref[1], o)] = total.astype(BF16)
-
-
-def first_sum_call(order, keep, got):
-    shape = keep.shape
-    return order.call(
-        first_sum_kernel,
-        "first_sum",
-        [keep, got],
-        [whole(shape)] * 2,
-        [(shape, BF16)],
-        [whole(shape)],
     )[0]
 
 
@@ -539,8 +510,8 @@
     def swap(x):
         return lax.ppermute(x, "sub", [(0, 1), (1, 0)])
 
-    def exchange(x):
-        return lax.all_to_all(x, "ep", split_axis=0, concat_axis=0, tiled=True)
+    def exchange(x, axes="ep"):
+        return lax.all_to_all(x, axes, split_axis=0, concat_axis=0, tiled=True)
 
     blocks = {0: pack_call(order, grad, first[0], index)}
 
@@ -554,9 +525,9 @@
     seconds = [second[0], swap(second[0])]
 
     if groups == 8:
-        batches, gates = [(0, 2), (1, 4), (3, 6), (5, 7)], {1: 4, 2: 6}
+        batches = [(0, 1), (2, 4), (3, 6), (5, 7)]
     else:
-        batches, gates = [(o, o + 1) for o in range(0, groups, 2)], {}
+        batches = [(o, o + 1) for o in range(0, groups, 2)]
     places = [o for batch in batches for o in batch]
     back, lows, waiting = {}, [], []
 
@@ -568,13 +539,11 @@
             back[o] = flip(rows, o) if o else rows
 
     for i, batch in enumerate(batches):
-        if i in gates:
-            blocks[gates[i]] = gate_call(order, fetch(gates[i]))
         *give, keep, low = expert_rows_call(
             order, [fetch(o) for o in batch], seconds, downs, shares, slots
         )
         lows.append(low)
-        if i > 1:
+        if 1 < i < len(batches) - 1:
             arrived(i - 2)
         if i > 0:
             send_back(*waiting)
@@ -585,22 +554,20 @@
 
     low_grad, first_own = collect_call(order, places, lows, grads, feats)
     firsts = [x.reshape(groups * rank, units) for x in (first_own, swap(first_own))]
+    low_grad = all_shares(exchange(low_grad))
     low_hid = all_shares(lowrank_hid_call(order, index, hid, firsts, groups))
-    low_grad = all_shares(exchange(low_grad))
     send_back(*waiting)
 
+    arrived(len(batches) - 3)
     arrived(len(batches) - 2)
     scaled_hid = exchange(scaled_hid_call(order, index, weight, low_hid, groups))
 
     low_grad = low_dense_call(order, low_grad)
-    first_keep, first_give = first_grad_call(order, index, weight, low_grad, hid, groups)
-    first_part = exchange(first_sum_call(order, first_keep, swap(first_give)))
-    first_grad = jnp.sum(first_part.astype(F32), axis=0)
-    order.wait([back[batches[-1][0]]])
+    first_part = first_grad_call(order, index, weight, low_grad, hid, groups)
+    first_grad = jnp.sum(exchange(first_part, ("ep", "sub")).astype(F32), axis=0)
     second_keep, second_give = second_grad_call(order, places, scaled_hid, grads, feats)
     second_grad = second_keep + swap(second_give)
 
-    order.wait([first_part])
     back = [back[o] for o in range(groups)]
     grad_hidden, sums = finish_call(order, index, weight, low_grad, hid, firsts, back)
     sums = sums + turn(sums, 1) if shares == 2 else lax.psum(sums, "rep")

time: 201 us -> 224 us (1.11)
  waiting for transfers between devices: 66.2 us -> 86.2 us
    ppermute x14, waiting for transfers between devices: 59.6 us -> 76.3 us  [flip(): return lax.ppermute(x, 'ep', [(i, i ^ mask) for i in range(groups)])]
    ppermute x7, waiting for transfers between devices: 2.1 us -> 8.17 us  [turn(): lax.ppermute(x, 'rep', [(r, (r + offset) % shares) for r in range(shares)])]
    all_to_all x3, starting transfers between devices: 14.8 us -> 18.6 us  [exchange(): return lax.all_to_all(x, axes, split_axis=0, concat_axis=0, tiled=True)]
    ppermute x14, starting transfers between devices: 23.1 us -> 19.8 us  [flip(): return lax.ppermute(x, 'ep', [(i, i ^ mask) for i in range(groups)])]
    all_to_all x3, waiting for transfers between devices: 2.31 us -> 0.01 us  [exchange(): return lax.all_to_all(x, axes, split_axis=0, concat_axis=0, tiled=True)]
    unnamed x66 -> x70, local copies, waits for them, and re-layouts: 6.33 us -> 8.25 us
    pallas_call x19 -> x16, Pallas kernels: 78.1 us -> 79.4 us  [call(): pl.pallas_call(ordered, grid=grid, in_specs=[SMEM, *in_specs] + [ANY] * l...]
  transfers between devices with their start and end apart: 29 -> 28, of which waited for: 9 -> 10; matrix products, arithmetic and copies ran while one was open for 2% -> 2% of each run, Pallas kernels for 29% -> 36%
where the time goes in v7:
time: 224 us; the launch traced here: 223 us
  waiting for transfers between devices  86.2 us (38%)
  Pallas kernels  79.4 us (35%)
  starting transfers between devices  45.6 us (20%)
  local copies, waits for them, and re-layouts  8.25 us (4%)
  other arithmetic  2.52 us (1%)
    pallas_call x16, Pallas kernels, call(): pl.pallas_call(ordered, grid=grid, in_specs=[SMEM, *in_specs] + [ANY] * l...  79.4 us
    ppermute x14, waiting for transfers between devices, flip(): return lax.ppermute(x, 'ep', [(i, i ^ mask) for i in range(groups)])  76.3 us
    ppermute x14, starting transfers between devices, flip(): return lax.ppermute(x, 'ep', [(i, i ^ mask) for i in range(groups)])  19.8 us
    all_to_all x3, starting transfers between devices, exchange(): return lax.all_to_all(x, axes, split_axis=0, concat_axis=0, tiled=True)  18.6 us
    unnamed x70, local copies, waits for them, and re-layouts  8.25 us
    ppermute x7, waiting for transfers between devices, turn(): lax.ppermute(x, 'rep', [(r, (r + offset) % shares) for r in range(shares)])  8.17 us
    ppermute x7, starting transfers between devices, turn(): lax.ppermute(x, 'rep', [(r, (r + offset) % shares) for r in range(shares)])  6.94 us
  transfers between devices with their start and end apart: 28, of which 10 were waited for; matrix products, arithmetic and copies ran while one was open for 2% of the time, Pallas kernels for 36%

profile of v7, /device:TPU:8, one launch (start us, length us, event | category | flops | bytes accessed | tf_op | source)
XLA Modules:
  0.0 223.0 jit_solution(1596783284201062618)
XLA Ops:
  0.7 0.8 copy.18.refs_3_.refs_1_.refs_2_
  1.5 1.0 copy.11
  2.5 0.1 pad_add_fusion.refs_0_
  2.6 1.0 copy-done.16
  3.6 0.8 pack_block.1
  4.4 2.7 %collective-permute-start.4 = (bf16[128,2304]{1,0:T(8,128)(2,1)S(1)}, bf16[128,2304]{1,0:T(8,128)(2,1)S(1)}, u32[]{:S(2)}, u32[]{:S(2)}) collective-permute-start(bf16[128,2304]{1,0:T(8,128)(2,1)S(1)} %get-tuple-element.50.refs_1_.refs_5_.refs_2_), channel_id=1, source_target_pairs={{0,16},{4,20},{8,24},{12,28},{16,0},{20,4},{24,8},{28,12},{1,17},{... | collective-permute-start | bytes 1769480 | tf_op jit(solution)/shard_map/ppermute | solution.py:508
  7.1 0.4 collective-permute-start.3
  7.5 1.5 collective-permute-start
  9.0 23.8 %collective-permute-done.4.refs_2_.refs_8_.refs_5_ = bf16[128,2304]{1,0:T(8,128)(2,1)S(1)} collective-permute-done((bf16[128,2304]{1,0:T(8,128)(2,1)S(1)}, bf16[128,2304]{1,0:T(8,128)(2,1)S(1)}, u32[]{:S(2)}, u32[]{:S(2)}) %collective-permute-start.4) | collective-permute-done | bytes 589856 | tf_op jit(solution)/shard_map/ppermute | solution.py:508
  32.9 1.4 collective-permute-start.6
  34.3 1.6 collective-permute-start.5
  35.9 1.0 copy-done.10
  37.0 12.3 %expert_rows.4 = (bf16[320,768]{1,0:T(8,128)(2,1)S(1)}, bf16[320,768]{1,0:T(8,128)(2,1)}, bf16[2,64,128]{2,1,0:T(8,128)(2,1)}, f32[8,128]{1,0:T(8,128)}) custom-call(s32[3]{0:T(128)S(1)} %pad_add_fusion.refs_0_, bf16[128,2304]{1,0:T(8,128)(2,1)S(1)} %get-tuple-element.50.refs_1_.refs_5_.refs_2_, ...), custom_call_target="tpu_custom_call" | custom-call | flops 1 | bytes 1 | tf_op jit(solution)/shard_map/expert_rows/pallas_call | solution.py:51
  49.3 1.6 collective-permute-start.7
  50.8 1.5 collective-permute-start.8
  52.3 0.6 collective-permute-start.9
  52.9 12.5 %expert_rows.5 = (bf16[320,768]{1,0:T(8,128)(2,1)S(1)}, bf16[320,768]{1,0:T(8,128)(2,1)}, bf16[2,64,128]{2,1,0:T(8,128)(2,1)}, f32[8,128]{1,0:T(8,128)}) custom-call(s32[3]{0:T(128)S(1)} %pad_add_fusion.refs_0_, bf16[128,2304]{1,0:T(8,128)(2,1)S(1)} %collective-permute-done.3.refs_1_.refs_7_.refs_4_, ...), custom_call_target="tpu_custom_call" | custom-call | flops 1 | bytes 1 | tf_op jit(solution)/shard_map/expert_rows/pallas_call | solution.py:51
  65.3 0.6 collective-permute-start.10
  66.0 0.7 share_sum.4
  66.6 0.7 copy-done.21
  67.3 12.5 %expert_rows.6 = (bf16[320,768]{1,0:T(8,128)(2,1)S(1)}, bf16[320,768]{1,0:T(8,128)(2,1)}, bf16[2,64,128]{2,1,0:T(8,128)(2,1)}, f32[8,128]{1,0:T(8,128)}) custom-call(s32[3]{0:T(128)S(1)} %pad_add_fusion.refs_0_, bf16[128,2304]{1,0:T(8,128)(2,1)S(1)} %collective-permute-done.5.refs_1_.refs_9_.refs_6_, ...), custom_call_target="tpu_custom_call" | custom-call | flops 1 | bytes 1 | tf_op jit(solution)/shard_map/expert_rows/pallas_call | solution.py:51
  79.9 1.6 collective-permute-start.12
  81.4 1.5 collective-permute-start.11
  82.9 5.1 %collective-permute-done.11.refs_4_.refs_9_ = bf16[160,768]{1,0:T(8,128)(2,1)S(1)} collective-permute-done((bf16[160,768]{1,0:T(8,128)(2,1)S(1)}, bf16[160,768]{1,0:T(8,128)(2,1)S(1)}, u32[]{:S(2)}, u32[]{:S(2)}) %collective-permute-start.11) | collective-permute-done | bytes 245792 | tf_op jit(solution)/shard_map/ppermute | solution.py:508
  88.0 1.4 share_sum.5
  89.5 12.5 %expert_rows.7 = (bf16[320,768]{1,0:T(8,128)(2,1)S(1)}, bf16[320,768]{1,0:T(8,128)(2,1)}, bf16[2,64,128]{2,1,0:T(8,128)(2,1)}, f32[8,128]{1,0:T(8,128)}) custom-call(s32[3]{0:T(128)S(1)} %pad_add_fusion.refs_0_, bf16[128,2304]{1,0:T(8,128)(2,1)S(1)} %collective-permute-done.8.refs_1_.refs_11_.refs_8_, ...), custom_call_target="tpu_custom_call" | custom-call | flops 1 | bytes 1 | tf_op jit(solution)/shard_map/expert_rows/pallas_call | solution.py:51
  102.0 0.6 collective-permute-start.16
  102.6 1.4 share_sum.6
  104.0 0.7 copy-done.25
  104.8 1.8 collect_blocks.1
  106.6 1.7 collective-permute-done.14
  108.3 3.5 %lowrank_hid.1 = (f32[128,512]{1,0:T(8,128)S(1)}, f32[8,128]{1,0:T(8,128)}) custom-call(s32[3]{0:T(128)S(1)} %pad_add_fusion.refs_0_, s32[128,8]{1,0:T(8,128)S(1)} %copy-done.9, bf16[1024,768]{1,0:T(8,128)(2,1)} %bitcast.30, bf16[256,768]{1,0:T(8,128)(2,1)S(1)} %bitcast.20, bf16[256,768]{1,0:T(8,128)(2,1)S(1)} %bitcast.22, f32[8,128]{1,0:T(8,128)} %get-tuple-element.72.refs_5_), custom_call_target="tpu_custom_call" | custom-call | flops 1 | bytes 1 | tf_op jit(solution)/shard_map/lowrank_hid/pallas_call | solution.py:51
  111.8 1.6 collective-permute-start.15
  113.4 0.6 collective-permute-start.17
  114.0 3.4 %collective-permute-start.18 = (bf16[160,768]{1,0:T(8,128)(2,1)}, bf16[160,768]{1,0:T(8,128)(2,1)S(1)}, u32[]{:S(2)}, u32[]{:S(2)}) collective-permute-start(bf16[160,768]{1,0:T(8,128)(2,1)} %get-tuple-element.79), channel_id=1, source_target_pairs={{0,16},{4,20},{8,24},{12,28},{16,0},{20,4},{24,8},{28,12},{1,17},{... | collective-permute-start | bytes 737288 | tf_op jit(solution)/shard_map/ppermute | solution.py:508
  117.3 0.9 collective-permute-start.19
  118.2 0.6 collective-permute-start.20
  118.8 6.6 %all-to-all-start = ((bf16[8,64,128]{2,1,0:T(8,128)(2,1)}), bf16[8,64,128]{2,1,0:T(8,128)(2,1)S(1)}, u32[]{:S(2)}, u32[]{:S(2)}) async-start(bf16[8,64,128]{2,1,0:T(8,128)(2,1)} %get-tuple-element.70), calls=%async_computation | async-start | bytes 262144 | tf_op jit(solution)/shard_map/all_to_all | solution.py:514
  125.4 0.1 copy.20.refs_2_.refs_3_
  125.5 0.7 share_sum.7
  126.2 0.7 copy-done.26
  126.9 0.7 copy-done.28
  127.5 2.1 collective-permute-done.18.refs_7_.refs_12_
  129.7 4.3 %collective-permute-done.19.refs_8_.refs_11_ = bf16[160,768]{1,0:T(8,128)(2,1)S(1)} collective-permute-done((bf16[160,768]{1,0:T(8,128)(2,1)}, bf16[160,768]{1,0:T(8,128)(2,1)S(1)}, u32[]{:S(2)}, u32[]{:S(2)}) %collective-permute-start.19) | collective-permute-done | bytes 245792 | tf_op jit(solution)/shard_map/ppermute | solution.py:508
  134.0 6.6 %collective-permute-done.20.refs_9_.refs_14_ = bf16[160,768]{1,0:T(8,128)(2,1)S(1)} collective-permute-done((bf16[160,768]{1,0:T(8,128)(2,1)}, bf16[160,768]{1,0:T(8,128)(2,1)S(1)}, u32[]{:S(2)}, u32[]{:S(2)}) %collective-permute-start.20) | collective-permute-done | bytes 245792 | tf_op jit(solution)/shard_map/ppermute | solution.py:508
  140.6 2.1 scaled_hid.1
  142.7 6.0 %all-to-all-start.1 = ((bf16[8,64,128]{2,1,0:T(8,128)(2,1)}), bf16[8,64,128]{2,1,0:T(8,128)(2,1)S(1)}, u32[]{:S(2)}, u32[]{:S(2)}) async-start(bf16[8,64,128]{2,1,0:T(8,128)(2,1)} %get-tuple-element.87), calls=%async_computation.1 | async-start | bytes 262144 | tf_op jit(solution)/shard_map/all_to_all | solution.py:514
  148.7 0.5 collective-permute-start.13
  149.2 4.4 %collective-permute-done.13.refs_2_ = bf16[8,64,128]{2,1,0:T(8,128)(2,1)S(1)} collective-permute-done((bf16[8,64,128]{2,1,0:T(8,128)(2,1)S(1)}, bf16[8,64,128]{2,1,0:T(8,128)(2,1)S(1)}, u32[]{:S(2)}, u32[]{:S(2)}) %collective-permute-start.13) | collective-permute-done | bytes 131104 | tf_op jit(solution)/shard_map/ppermute | solution.py:502
  153.7 0.7 low_dense.1
  154.3 5.2 %first_grad.1 = (bf16[16,32,768]{2,1,0:T(8,128)(2,1)}, f32[8,128]{1,0:T(8,128)}) custom-call(s32[3]{0:T(128)S(1)} %pad_add_fusion.refs_0_, s32[128,8]{1,0:T(8,128)S(1)} %copy-done.9, bf16[128,8]{1,0:T(8,128)(2,1)S(1)} %copy.20.refs_2_.refs_3_, f32[128,512]{1,0:T(8,128)S(1)} %get-tuple-element.83.refs_3_.refs_4_, bf16[1024,768]{1,0:T(8,128)(2,1)} %bitcast.31, ...), custom_call_target="tpu_custom_call" | custom-call | flops 1 | bytes 1 | tf_op jit(solution)/shard_map/first_grad/pallas_call | solution.py:51
  159.5 6.0 %all-to-all-start.2 = ((bf16[16,32,768]{2,1,0:T(8,128)(2,1)}), bf16[16,32,768]{2,1,0:T(8,128)(2,1)S(1)}, u32[]{:S(2)}, u32[]{:S(2)}) async-start(bf16[16,32,768]{2,1,0:T(8,128)(2,1)} %get-tuple-element.93), calls=%async_computation.2 | async-start | bytes 1572864 | tf_op jit(solution)/shard_map/all_to_all | solution.py:514
  165.6 3.7 %second_grad.1 = (f32[32,2048]{1,0:T(8,128)S(1)}, f32[32,2048]{1,0:T(8,128)S(1)}, f32[8,128]{1,0:T(8,128)}) custom-call(s32[3]{0:T(128)S(1)} %pad_add_fusion.refs_0_, bf16[8,64,128]{2,1,0:T(8,128)(2,1)S(1)} %all-to-all-done.1.refs_1_, bf16[128,2304]{1,0:T(8,128)(2,1)} %copy-done, bf16[128,2304]{1,0:T(8,128)(2,1)} %copy-done.3, bf16[128,2304]{1,0:T(8,128)(2,1)} %copy-done.2, ...), custom_call_target="tpu_custom_call" | custom-call | flops 1 | bytes 1 | tf_op jit(solution)/shard_map/second_grad/pallas_call | solution.py:51
  169.3 0.2 collective-permute-start.24
  169.5 3.3 %collective-permute-start.21 = (bf16[160,768]{1,0:T(8,128)(2,1)S(1)}, bf16[160,768]{1,0:T(8,128)(2,1)S(1)}, u32[]{:S(2)}, u32[]{:S(2)}) collective-permute-start(bf16[160,768]{1,0:T(8,128)(2,1)S(1)} %copy-done.29), channel_id=1, source_target_pairs={{0,20},{4,16},{8,28},{12,24},{16,4},{20,0},{24,12},{28,8},{1,21},{... | collective-permute-start | bytes 737288 | tf_op jit(solution)/shard_map/ppermute | solution.py:508
  172.8 26.7 %collective-permute-done.21.refs_13_ = bf16[160,768]{1,0:T(8,128)(2,1)S(1)} collective-permute-done((bf16[160,768]{1,0:T(8,128)(2,1)S(1)}, bf16[160,768]{1,0:T(8,128)(2,1)S(1)}, u32[]{:S(2)}, u32[]{:S(2)}) %collective-permute-start.21) | collective-permute-done | bytes 245792 | tf_op jit(solution)/shard_map/ppermute | solution.py:508
  199.5 7.6 %collective-permute-done.22.refs_15_ = bf16[160,768]{1,0:T(8,128)(2,1)S(1)} collective-permute-done((bf16[160,768]{1,0:T(8,128)(2,1)S(1)}, bf16[160,768]{1,0:T(8,128)(2,1)S(1)}, u32[]{:S(2)}, u32[]{:S(2)}) %collective-permute-start.22) | collective-permute-done | bytes 245792 | tf_op jit(solution)/shard_map/ppermute | solution.py:508
  207.1 0.7 copy-done.31
  207.8 7.8 %finish.1 = (bf16[1024,768]{1,0:T(8,128)(2,1)}, f32[128,8]{1,0:T(8,128)S(1)}, f32[8,128]{1,0:T(8,128)}) custom-call(s32[3]{0:T(128)S(1)} %pad_add_fusion.refs_0_, s32[128,8]{1,0:T(8,128)S(1)} %copy-done.9, s32[128,8]{1,0:T(8,128)S(1)} %copy-done.9, bf16[128,8]{1,0:T(8,128)(2,1)S(1)} %copy.20.refs_2_.refs_3_, ...), custom_call_target="tpu_custom_call" | custom-call | flops 1 | bytes 1 | tf_op jit(solution)/shard_map/finish/pallas_call | solution.py:51
  215.6 0.5 collective-permute-start.23
  216.1 3.7 %collective-permute-done.23 = f32[128,8]{1,0:T(8,128)S(1)} collective-permute-done((f32[128,8]{1,0:T(8,128)S(1)}, f32[128,8]{1,0:T(8,128)S(1)}, u32[]{:S(2)}, u32[]{:S(2)}) %collective-permute-start.23) | collective-permute-done | bytes 4128 | tf_op jit(solution)/shard_map/ppermute | solution.py:502
  219.9 0.7 copy.21
  220.5 1.7 add_bitcast_fusion
  222.2 0.7 convert_reduce_fusion
  (82 shorter events, 0.3 us)
Async XLA Ops:
  0.6 35.3 %collective-permute-start.2 = (bf16[1536,2048]{1,0:T(8,128)(2,1)}, bf16[1536,2048]{1,0:T(8,128)(2,1)}, u32[]{:S(2)}, u32[]{:S(2)}) collective-permute-start(bf16[1536,2048]{1,0:T(8,128)(2,1)} %bitcast.25), channel_id=1, source_target_pairs={{0,1},{1,0},{2,3},{3,2},{4,5},{5,4},{6,7},{7,6},{8,9},{9,8},{10,11... | collective-permute-start | bytes 18874376 | tf_op jit(solution)/shard_map/ppermute | solution.py:511
  1.5 2.9 %copy-start.8 = (s32[128,8]{1,0:T(8,128)}, s32[128,8]{1,0:T(8,128)S(1)}, u32[]{:S(2)}) copy-start(s32[128,8]{1,0:T(8,128)S(1)} %copy.18.refs_3_.refs_1_.refs_2_) | copy-start | bytes 12292
  2.6 1.0 copy-start.16
  4.4 44.8 %copy-start = (bf16[128,2304]{1,0:T(8,128)(2,1)}, bf16[128,2304]{1,0:T(8,128)(2,1)S(1)}, u32[]{:S(2)}) copy-start(bf16[128,2304]{1,0:T(8,128)(2,1)S(1)} %get-tuple-element.50.refs_1_.refs_5_.refs_2_) | copy-start | bytes 1769476
  4.4 28.4 %collective-permute-start.4 = (bf16[128,2304]{1,0:T(8,128)(2,1)S(1)}, bf16[128,2304]{1,0:T(8,128)(2,1)S(1)}, u32[]{:S(2)}, u32[]{:S(2)}) collective-permute-start(bf16[128,2304]{1,0:T(8,128)(2,1)S(1)} %get-tuple-element.50.refs_1_.refs_5_.refs_2_), channel_id=1, source_target_pairs={{0,16},{4,20},{8,24},{12,28},{16,0},{20,4},{24,8},{28,12},{1,17},{... | collective-permute-start | bytes 1769480 | tf_op jit(solution)/shard_map/ppermute | solution.py:508
  7.1 27.2 %collective-permute-start.3 = (bf16[128,2304]{1,0:T(8,128)(2,1)S(1)}, bf16[128,2304]{1,0:T(8,128)(2,1)S(1)}, u32[]{:S(2)}, u32[]{:S(2)}) collective-permute-start(bf16[128,2304]{1,0:T(8,128)(2,1)S(1)} %get-tuple-element.50.refs_1_.refs_5_.refs_2_), channel_id=1, source_target_pairs={{0,8},{4,12},{8,0},{12,4},{16,24},{20,28},{24,16},{28,20},{1,9},{5... | collective-permute-start | bytes 1769480 | tf_op jit(solution)/shard_map/ppermute | solution.py:508
  7.5 28.4 %collective-permute-start = (bf16[128,2304]{1,0:T(8,128)(2,1)S(1)}, bf16[128,2304]{1,0:T(8,128)(2,1)S(1)}, u32[]{:S(2)}, u32[]{:S(2)}) collective-permute-start(bf16[128,2304]{1,0:T(8,128)(2,1)S(1)} %get-tuple-element.50.refs_1_.refs_5_.refs_2_), channel_id=1, source_target_pairs={{0,4},{4,0},{8,12},{12,8},{16,20},{20,16},{24,28},{28,24},{1,5},{5... | collective-permute-start | bytes 1769480 | tf_op jit(solution)/shard_map/ppermute | solution.py:508
  32.9 20.0 %copy-start.1 = (bf16[128,2304]{1,0:T(8,128)(2,1)}, bf16[128,2304]{1,0:T(8,128)(2,1)S(1)}, u32[]{:S(2)}) copy-start(bf16[128,2304]{1,0:T(8,128)(2,1)S(1)} %collective-permute-done.4.refs_2_.refs_8_.refs_5_) | copy-start | bytes 1769476
  32.9 19.4 %collective-permute-start.6 = (bf16[128,2304]{1,0:T(8,128)(2,1)S(1)}, bf16[128,2304]{1,0:T(8,128)(2,1)S(1)}, u32[]{:S(2)}, u32[]{:S(2)}) collective-permute-start(bf16[128,2304]{1,0:T(8,128)(2,1)S(1)} %collective-permute-done.4.refs_2_.refs_8_.refs_5_), channel_id=1, source_target_pairs={{0,8},{4,12},{8,0},{12,4},{16,24},{20,28},{24,16},{28,20},{1,9},{5... | collective-permute-start | bytes 1769480 | tf_op jit(solution)/shard_map/ppermute | solution.py:508
  34.2 1.6 collective-permute-start.1
  34.3 18.6 %copy-start.2 = (bf16[128,2304]{1,0:T(8,128)(2,1)}, bf16[128,2304]{1,0:T(8,128)(2,1)S(1)}, u32[]{:S(2)}) copy-start(bf16[128,2304]{1,0:T(8,128)(2,1)S(1)} %collective-permute-done.3.refs_1_.refs_7_.refs_4_) | copy-start | bytes 1769476
  34.3 33.1 %collective-permute-start.5 = (bf16[128,2304]{1,0:T(8,128)(2,1)S(1)}, bf16[128,2304]{1,0:T(8,128)(2,1)S(1)}, u32[]{:S(2)}, u32[]{:S(2)}) collective-permute-start(bf16[128,2304]{1,0:T(8,128)(2,1)S(1)} %collective-permute-done.3.refs_1_.refs_7_.refs_4_), channel_id=1, source_target_pairs={{0,4},{4,0},{8,12},{12,8},{16,20},{20,16},{24,28},{28,24},{1,5},{5... | collective-permute-start | bytes 1769480 | tf_op jit(solution)/shard_map/ppermute | solution.py:508
  35.9 13.4 %copy-start.3 = (bf16[128,2304]{1,0:T(8,128)(2,1)}, bf16[128,2304]{1,0:T(8,128)(2,1)S(1)}, u32[]{:S(2)}) copy-start(bf16[128,2304]{1,0:T(8,128)(2,1)S(1)} %collective-permute-done.refs_2_.refs_6_.refs_3_) | copy-start | bytes 1769476
  35.9 1.0 copy-start.10
  49.3 16.7 %collective-permute-start.7 = (bf16[320,768]{1,0:T(8,128)(2,1)S(1)}, bf16[320,768]{1,0:T(8,128)(2,1)S(1)}, u32[]{:S(2)}, u32[]{:S(2)}) collective-permute-start(bf16[320,768]{1,0:T(8,128)(2,1)S(1)} %get-tuple-element.56), channel_id=1, source_target_pairs={{0,2},{2,0},{1,3},{3,1},{4,6},{6,4},{5,7},{7,5},{8,10},{10,8},{9,1... | collective-permute-start | bytes 1474568 | tf_op jit(solution)/shard_map/ppermute | solution.py:502
  50.8 38.6 %collective-permute-start.8 = (bf16[128,2304]{1,0:T(8,128)(2,1)S(1)}, bf16[128,2304]{1,0:T(8,128)(2,1)S(1)}, u32[]{:S(2)}, u32[]{:S(2)}) collective-permute-start(bf16[128,2304]{1,0:T(8,128)(2,1)S(1)} %collective-permute-done.4.refs_2_.refs_8_.refs_5_), channel_id=1, source_target_pairs={{0,4},{4,0},{8,12},{12,8},{16,20},{20,16},{24,28},{28,24},{1,5},{5... | collective-permute-start | bytes 1769480 | tf_op jit(solution)/shard_map/ppermute | solution.py:508
  52.3 15.0 %copy-start.4 = (bf16[128,2304]{1,0:T(8,128)(2,1)}, bf16[128,2304]{1,0:T(8,128)(2,1)S(1)}, u32[]{:S(2)}) copy-start(bf16[128,2304]{1,0:T(8,128)(2,1)S(1)} %collective-permute-done.6.refs_2_.refs_10_.refs_7_) | copy-start | bytes 1769476
  52.3 37.1 %collective-permute-start.9 = (bf16[128,2304]{1,0:T(8,128)(2,1)S(1)}, bf16[128,2304]{1,0:T(8,128)(2,1)S(1)}, u32[]{:S(2)}, u32[]{:S(2)}) collective-permute-start(bf16[128,2304]{1,0:T(8,128)(2,1)S(1)} %collective-permute-done.6.refs_2_.refs_10_.refs_7_), channel_id=1, source_target_pairs={{0,4},{4,0},{8,12},{12,8},{16,20},{20,16},{24,28},{28,24},{1,5},{5... | collective-permute-start | bytes 1769480 | tf_op jit(solution)/shard_map/ppermute | solution.py:508
  52.9 13.1 %copy-start.19 = (bf16[320,768]{1,0:T(8,128)(2,1)S(1)}, bf16[320,768]{1,0:T(8,128)(2,1)}, u32[]{:S(2)}) copy-start(bf16[320,768]{1,0:T(8,128)(2,1)} %get-tuple-element.55.refs_1_) | copy-start | bytes 1474564
  65.3 17.5 %collective-permute-start.10 = (bf16[320,768]{1,0:T(8,128)(2,1)S(1)}, bf16[320,768]{1,0:T(8,128)(2,1)S(1)}, u32[]{:S(2)}, u32[]{:S(2)}) collective-permute-start(bf16[320,768]{1,0:T(8,128)(2,1)S(1)} %get-tuple-element.61), channel_id=1, source_target_pairs={{0,2},{2,0},{1,3},{3,1},{4,6},{6,4},{5,7},{7,5},{8,10},{10,8},{9,1... | collective-permute-start | bytes 1474568 | tf_op jit(solution)/shard_map/ppermute | solution.py:502
  66.6 0.7 copy-start.21
  67.3 12.5 %copy-start.5 = (bf16[128,2304]{1,0:T(8,128)(2,1)}, bf16[128,2304]{1,0:T(8,128)(2,1)S(1)}, u32[]{:S(2)}) copy-start(bf16[128,2304]{1,0:T(8,128)(2,1)S(1)} %collective-permute-done.5.refs_1_.refs_9_.refs_6_) | copy-start | bytes 1769476
  67.3 20.7 %copy-start.20 = (bf16[320,768]{1,0:T(8,128)(2,1)S(1)}, bf16[320,768]{1,0:T(8,128)(2,1)}, u32[]{:S(2)}) copy-start(bf16[320,768]{1,0:T(8,128)(2,1)} %get-tuple-element.60.refs_1_) | copy-start | bytes 1474564
  79.9 22.8 %collective-permute-start.12 = (bf16[320,768]{1,0:T(8,128)(2,1)S(1)}, bf16[320,768]{1,0:T(8,128)(2,1)S(1)}, u32[]{:S(2)}, u32[]{:S(2)}) collective-permute-start(bf16[320,768]{1,0:T(8,128)(2,1)S(1)} %get-tuple-element.67), channel_id=1, source_target_pairs={{0,2},{2,0},{1,3},{3,1},{4,6},{6,4},{5,7},{7,5},{8,10},{10,8},{9,1... | collective-permute-start | bytes 1474568 | tf_op jit(solution)/shard_map/ppermute | solution.py:502
  81.4 6.6 %collective-permute-start.11 = (bf16[160,768]{1,0:T(8,128)(2,1)S(1)}, bf16[160,768]{1,0:T(8,128)(2,1)S(1)}, u32[]{:S(2)}, u32[]{:S(2)}) collective-permute-start(bf16[160,768]{1,0:T(8,128)(2,1)S(1)} %get-tuple-element.63), channel_id=1, source_target_pairs={{0,4},{4,0},{8,12},{12,8},{16,20},{20,16},{24,28},{28,24},{1,5},{5... | collective-permute-start | bytes 737288 | tf_op jit(solution)/shard_map/ppermute | solution.py:508
  88.0 14.0 %copy-start.11 = (bf16[160,768]{1,0:T(8,128)(2,1)}, bf16[160,768]{1,0:T(8,128)(2,1)S(1)}, u32[]{:S(2)}) copy-start(bf16[160,768]{1,0:T(8,128)(2,1)S(1)} %collective-permute-done.11.refs_4_.refs_9_) | copy-start | bytes 737284
  89.4 12.6 %copy-start.6 = (bf16[128,2304]{1,0:T(8,128)(2,1)}, bf16[128,2304]{1,0:T(8,128)(2,1)S(1)}, u32[]{:S(2)}) copy-start(bf16[128,2304]{1,0:T(8,128)(2,1)S(1)} %collective-permute-done.8.refs_1_.refs_11_.refs_8_) | copy-start | bytes 1769476
  89.4 12.6 %copy-start.7 = (bf16[128,2304]{1,0:T(8,128)(2,1)}, bf16[128,2304]{1,0:T(8,128)(2,1)S(1)}, u32[]{:S(2)}) copy-start(bf16[128,2304]{1,0:T(8,128)(2,1)S(1)} %collective-permute-done.9.refs_2_.refs_12_.refs_9_) | copy-start | bytes 1769476
  89.4 13.2 %copy-start.18 = (bf16[320,768]{1,0:T(8,128)(2,1)S(1)}, bf16[320,768]{1,0:T(8,128)(2,1)}, u32[]{:S(2)}) copy-start(bf16[320,768]{1,0:T(8,128)(2,1)} %get-tuple-element.66.refs_1_) | copy-start | bytes 1474564
  89.5 14.6 %copy-start.22 = (bf16[2,64,128]{2,1,0:T(8,128)(2,1)S(1)}, bf16[2,64,128]{2,1,0:T(8,128)(2,1)}, u32[]{:S(2)}) copy-start(bf16[2,64,128]{2,1,0:T(8,128)(2,1)} %get-tuple-element.52.refs_1_) | copy-start | bytes 98308
  89.5 14.6 %copy-start.23 = (bf16[2,64,128]{2,1,0:T(8,128)(2,1)S(1)}, bf16[2,64,128]{2,1,0:T(8,128)(2,1)}, u32[]{:S(2)}) copy-start(bf16[2,64,128]{2,1,0:T(8,128)(2,1)} %get-tuple-element.54.refs_2_) | copy-start | bytes 98308
  89.5 14.5 %copy-start.24 = (bf16[2,64,128]{2,1,0:T(8,128)(2,1)S(1)}, bf16[2,64,128]{2,1,0:T(8,128)(2,1)}, u32[]{:S(2)}) copy-start(bf16[2,64,128]{2,1,0:T(8,128)(2,1)} %get-tuple-element.59.refs_3_) | copy-start | bytes 98308
  102.0 16.2 %collective-permute-start.16 = (bf16[320,768]{1,0:T(8,128)(2,1)S(1)}, bf16[320,768]{1,0:T(8,128)(2,1)S(1)}, u32[]{:S(2)}, u32[]{:S(2)}) collective-permute-start(bf16[320,768]{1,0:T(8,128)(2,1)S(1)} %get-tuple-element.75), channel_id=1, source_target_pairs={{0,2},{2,0},{1,3},{3,1},{4,6},{6,4},{5,7},{7,5},{8,10},{10,8},{9,1... | collective-permute-start | bytes 1474568 | tf_op jit(solution)/shard_map/ppermute | solution.py:502
  104.0 0.8 copy-start.25
  104.8 3.5 %copy-start.9 = (s32[128,8]{1,0:T(8,128)S(1)}, s32[128,8]{1,0:T(8,128)}, u32[]{:S(2)}) copy-start(s32[128,8]{1,0:T(8,128)} %copy-done.8) | copy-start | bytes 12292
  106.6 18.8 %copy-start.32 = (bf16[128,8]{0,1:T(8,128)(2,1)S(1)}, bf16[128,8]{0,1:T(8,128)(2,1)}, u32[]{:S(2)}) copy-start(bf16[128,8]{0,1:T(8,128)(2,1)} %param.10) | copy-start | bytes 6148
  106.6 18.9 %copy-start.17 = (bf16[320,768]{1,0:T(8,128)(2,1)S(1)}, bf16[320,768]{1,0:T(8,128)(2,1)}, u32[]{:S(2)}) copy-start(bf16[320,768]{1,0:T(8,128)(2,1)} %get-tuple-element.74.refs_1_) | copy-start | bytes 1474564
  106.6 1.7 collective-permute-start.14
  111.8 28.7 %collective-permute-start.15 = (f32[128,512]{1,0:T(8,128)S(1)}, f32[128,512]{1,0:T(8,128)}, u32[]{:S(2)}, u32[]{:S(2)}) collective-permute-start(f32[128,512]{1,0:T(8,128)S(1)} %get-tuple-element.73.refs_3_), channel_id=1, source_target_pairs={{0,2},{2,0},{1,3},{3,1},{4,6},{6,4},{5,7},{7,5},{8,10},{10,8},{9,1... | collective-permute-start | bytes 786440 | tf_op jit(solution)/shard_map/ppermute | solution.py:502
  113.4 14.1 %collective-permute-start.17 = (bf16[160,768]{1,0:T(8,128)(2,1)}, bf16[160,768]{1,0:T(8,128)(2,1)S(1)}, u32[]{:S(2)}, u32[]{:S(2)}) collective-permute-start(bf16[160,768]{1,0:T(8,128)(2,1)} %get-tuple-element.78), channel_id=1, source_target_pairs={{0,8},{4,12},{8,0},{12,4},{16,24},{20,28},{24,16},{28,20},{1,9},{5... | collective-permute-start | bytes 737288 | tf_op jit(solution)/shard_map/ppermute | solution.py:508
  114.0 15.7 %collective-permute-start.18 = (bf16[160,768]{1,0:T(8,128)(2,1)}, bf16[160,768]{1,0:T(8,128)(2,1)S(1)}, u32[]{:S(2)}, u32[]{:S(2)}) collective-permute-start(bf16[160,768]{1,0:T(8,128)(2,1)} %get-tuple-element.79), channel_id=1, source_target_pairs={{0,16},{4,20},{8,24},{12,28},{16,0},{20,4},{24,8},{28,12},{1,17},{... | collective-permute-start | bytes 737288 | tf_op jit(solution)/shard_map/ppermute | solution.py:508
  117.3 16.6 %collective-permute-start.19 = (bf16[160,768]{1,0:T(8,128)(2,1)}, bf16[160,768]{1,0:T(8,128)(2,1)S(1)}, u32[]{:S(2)}, u32[]{:S(2)}) collective-permute-start(bf16[160,768]{1,0:T(8,128)(2,1)} %get-tuple-element.80), channel_id=1, source_target_pairs={{0,12},{4,8},{8,4},{12,0},{16,28},{20,24},{24,20},{28,16},{1,13},{... | collective-permute-start | bytes 737288 | tf_op jit(solution)/shard_map/ppermute | solution.py:508
  118.2 22.3 %collective-permute-start.20 = (bf16[160,768]{1,0:T(8,128)(2,1)}, bf16[160,768]{1,0:T(8,128)(2,1)S(1)}, u32[]{:S(2)}, u32[]{:S(2)}) collective-permute-start(bf16[160,768]{1,0:T(8,128)(2,1)} %get-tuple-element.81), channel_id=1, source_target_pairs={{0,24},{4,28},{8,16},{12,20},{16,8},{20,12},{24,0},{28,4},{1,25},{... | collective-permute-start | bytes 737288 | tf_op jit(solution)/shard_map/ppermute | solution.py:508
  118.8 23.9 %all-to-all-start = ((bf16[8,64,128]{2,1,0:T(8,128)(2,1)}), bf16[8,64,128]{2,1,0:T(8,128)(2,1)S(1)}, u32[]{:S(2)}, u32[]{:S(2)}) async-start(bf16[8,64,128]{2,1,0:T(8,128)(2,1)} %get-tuple-element.70), calls=%async_computation | async-start | bytes 262144 | tf_op jit(solution)/shard_map/all_to_all | solution.py:514
  126.2 0.7 copy-start.26
  126.9 0.7 copy-start.28
  127.5 32.0 %copy-start.12 = (bf16[160,768]{1,0:T(8,128)(2,1)}, bf16[160,768]{1,0:T(8,128)(2,1)S(1)}, u32[]{:S(2)}) copy-start(bf16[160,768]{1,0:T(8,128)(2,1)S(1)} %collective-permute-done.17.refs_6_.refs_10_) | copy-start | bytes 737284
  129.7 29.8 %copy-start.13 = (bf16[160,768]{1,0:T(8,128)(2,1)}, bf16[160,768]{1,0:T(8,128)(2,1)S(1)}, u32[]{:S(2)}) copy-start(bf16[160,768]{1,0:T(8,128)(2,1)S(1)} %collective-permute-done.18.refs_7_.refs_12_) | copy-start | bytes 737284
  133.9 25.6 %copy-start.14 = (bf16[160,768]{1,0:T(8,128)(2,1)}, bf16[160,768]{1,0:T(8,128)(2,1)S(1)}, u32[]{:S(2)}) copy-start(bf16[160,768]{1,0:T(8,128)(2,1)S(1)} %collective-permute-done.19.refs_8_.refs_11_) | copy-start | bytes 737284
  140.6 19.0 %copy-start.15 = (bf16[160,768]{1,0:T(8,128)(2,1)}, bf16[160,768]{1,0:T(8,128)(2,1)S(1)}, u32[]{:S(2)}) copy-start(bf16[160,768]{1,0:T(8,128)(2,1)S(1)} %collective-permute-done.20.refs_9_.refs_14_) | copy-start | bytes 737284
  142.7 16.8 %all-to-all-start.1 = ((bf16[8,64,128]{2,1,0:T(8,128)(2,1)}), bf16[8,64,128]{2,1,0:T(8,128)(2,1)S(1)}, u32[]{:S(2)}, u32[]{:S(2)}) async-start(bf16[8,64,128]{2,1,0:T(8,128)(2,1)} %get-tuple-element.87), calls=%async_computation.1 | async-start | bytes 262144 | tf_op jit(solution)/shard_map/all_to_all | solution.py:514
  148.7 5.0 %collective-permute-start.13 = (bf16[8,64,128]{2,1,0:T(8,128)(2,1)S(1)}, bf16[8,64,128]{2,1,0:T(8,128)(2,1)S(1)}, u32[]{:S(2)}, u32[]{:S(2)}) collective-permute-start(bf16[8,64,128]{2,1,0:T(8,128)(2,1)S(1)} %all-to-all-done.refs_1_), channel_id=1, source_target_pairs={{0,2},{2,0},{1,3},{3,1},{4,6},{6,4},{5,7},{7,5},{8,10},{10,8},{9,1... | collective-permute-start | bytes 393224 | tf_op jit(solution)/shard_map/ppermute | solution.py:502
  159.5 62.7 %all-to-all-start.2 = ((bf16[16,32,768]{2,1,0:T(8,128)(2,1)}), bf16[16,32,768]{2,1,0:T(8,128)(2,1)S(1)}, u32[]{:S(2)}, u32[]{:S(2)}) async-start(bf16[16,32,768]{2,1,0:T(8,128)(2,1)} %get-tuple-element.93), calls=%async_computation.2 | async-start | bytes 1572864 | tf_op jit(solution)/shard_map/all_to_all | solution.py:514
  165.6 4.0 %copy-start.29 = (bf16[160,768]{1,0:T(8,128)(2,1)S(1)}, bf16[160,768]{1,0:T(8,128)(2,1)}, u32[]{:S(2)}) copy-start(bf16[160,768]{1,0:T(8,128)(2,1)} %copy-done.28) | copy-start | bytes 737284
  165.6 7.3 %copy-start.27 = (bf16[160,768]{1,0:T(8,128)(2,1)S(1)}, bf16[160,768]{1,0:T(8,128)(2,1)}, u32[]{:S(2)}) copy-start(bf16[160,768]{1,0:T(8,128)(2,1)} %copy-done.26) | copy-start | bytes 737284
  169.3 51.2 %collective-permute-start.24 = (f32[32,2048]{1,0:T(8,128)S(1)}, f32[32,2048]{1,0:T(8,128)}, u32[]{:S(2)}, u32[]{:S(2)}) collective-permute-start(f32[32,2048]{1,0:T(8,128)S(1)} %get-tuple-element.95), channel_id=1, source_target_pairs={{0,1},{1,0},{2,3},{3,2},{4,5},{5,4},{6,7},{7,6},{8,9},{9,8},{10,11... | collective-permute-start | bytes 786440 | tf_op jit(solution)/shard_map/ppermute | solution.py:511
  169.5 29.9 %collective-permute-start.21 = (bf16[160,768]{1,0:T(8,128)(2,1)S(1)}, bf16[160,768]{1,0:T(8,128)(2,1)S(1)}, u32[]{:S(2)}, u32[]{:S(2)}) collective-permute-start(bf16[160,768]{1,0:T(8,128)(2,1)S(1)} %copy-done.29), channel_id=1, source_target_pairs={{0,20},{4,16},{8,28},{12,24},{16,4},{20,0},{24,12},{28,8},{1,21},{... | collective-permute-start | bytes 737288 | tf_op jit(solution)/shard_map/ppermute | solution.py:508
  172.8 34.3 %collective-permute-start.22 = (bf16[160,768]{1,0:T(8,128)(2,1)S(1)}, bf16[160,768]{1,0:T(8,128)(2,1)S(1)}, u32[]{:S(2)}, u32[]{:S(2)}) collective-permute-start(bf16[160,768]{1,0:T(8,128)(2,1)S(1)} %copy-done.27), channel_id=1, source_target_pairs={{0,28},{4,24},{8,20},{12,16},{16,12},{20,8},{24,4},{28,0},{1,29},{... | collective-permute-start | bytes 737288 | tf_op jit(solution)/shard_map/ppermute | solution.py:508
  199.5 7.6 %copy-start.30 = (bf16[160,768]{1,0:T(8,128)(2,1)}, bf16[160,768]{1,0:T(8,128)(2,1)S(1)}, u32[]{:S(2)}) copy-start(bf16[160,768]{1,0:T(8,128)(2,1)S(1)} %collective-permute-done.21.refs_13_) | copy-start | bytes 737284
  207.1 0.7 copy-start.31
  215.6 4.3 %collective-permute-start.23 = (f32[128,8]{1,0:T(8,128)S(1)}, f32[128,8]{1,0:T(8,128)S(1)}, u32[]{:S(2)}, u32[]{:S(2)}) collective-permute-start(f32[128,8]{1,0:T(8,128)S(1)} %get-tuple-element.92), channel_id=1, source_target_pairs={{0,2},{2,0},{1,3},{3,1},{4,6},{6,4},{5,7},{7,5},{8,10},{10,8},{9,1... | collective-permute-start | bytes 12296 | tf_op jit(solution)/shard_map/ppermute | solution.py:502

commit v8 on v7

--- a/solution.py
+++ b/solution.py
@@ -16,6 +16,7 @@
 SMALL = pl.CostEstimate(flops=1, bytes_accessed=1, transcendentals=0)
 ANY = pl.BlockSpec(memory_space=pl.ANY)
 SMEM = pl.BlockSpec(memory_space=pltpu.SMEM)
+VMEM = pl.BlockSpec(memory_space=pltpu.VMEM)
 
 
 def dot(a, b, dims):
@@ -123,25 +124,45 @@
     )[0]
 
 
+def load_kernel(at_ref, down_ref, out_ref, sems):
+    parts = sems.shape[0]
+    rows = down_ref.shape[0] // parts
+    copies = [
+        pltpu.make_async_copy(
+            down_ref.at[pl.ds(k * rows, rows), :], out_ref.at[pl.ds(k * rows, rows), :], sems.at[k]
+        )
+        for k in range(parts)
+    ]
+    for copy in copies:
+        copy.start()
+    for copy in copies:
+        copy.wait()
+
+
+def load_call(order, down):
+    return order.call(
+        load_kernel,
+        "load_matrix",
+        [in_hbm(down)],
+        [ANY],
+        [pltpu.VMEM(down.shape, down.dtype)],
+        [VMEM],
+        grid=(),
+        scratch=[pltpu.SemaphoreType.DMA((4,))],
+    )[0]
+
+
 def expert_rows_kernel(slots, tiles, shares, batch, route_row, at_ref, *rest):
     grads, seconds, downs = rest[:batch], rest[batch : batch + 2], rest[batch + 2 : batch + 4]
     *outs, low_ref = rest[batch + 4 : batch + 5 + shares]
-    block_ref, turned_ref, tiles_ref, block_sems, sems = rest[batch + 5 + shares :]
-    tile = tiles_ref.shape[1]
+    block_ref, turned_ref, block_sems = rest[batch + 5 + shares :]
+    tile = downs[0].shape[0] // shares // tiles
     feats = turned_ref.shape[1]
     toks = block_ref.shape[1]
     blocks = [
         pltpu.make_async_copy(ref, block_ref.at[k], block_sems.at[k]) for k, ref in enumerate(grads)
     ]
-    parts = [(k, q, t) for k in range(shares) for q in range(2) for t in range(tiles)]
-    weights = []
-    for n, (k, q, t) in enumerate(parts):
-        share = lax.rem(at_ref[0] + k + 1, shares)
-        row = pl.multiple_of((share * tiles + t) * tile, tile)
-        weights.append(
-            pltpu.make_async_copy(downs[q].at[pl.ds(row, tile), :], tiles_ref.at[n], sems.at[n])
-        )
-    for copy in blocks + weights:
+    for copy in blocks:
         copy.start()
 
     before = jnp.where(iota((toks, toks), 0) < iota((toks, toks), 1), 1.0, 0.0).astype(BF16)
@@ -168,37 +189,33 @@
         low_ref[k] = low[:, k * toks : (k + 1) * toks]
 
     rows = batch * slots
-    for n, (k, q, t) in enumerate(parts):
-        weights[n].wait()
-        value = dot(tiles_ref[n], turned_ref[q], NN)
-        outs[k][pl.ds(q * rows, rows), pl.ds(t * tile, tile)] = value.T[:rows].astype(BF16)
+    for k in range(shares):
+        share = lax.rem(at_ref[0] + k + 1, shares)
+        for q in range(2):
+            for t in range(tiles):
+                row = pl.multiple_of((share * tiles + t) * tile, tile)
+                value = dot(downs[q][pl.ds(row, tile), :], turned_ref[q], NN)
+                outs[k][pl.ds(q * rows, rows), pl.ds(t * tile, tile)] = value.T[:rows].astype(BF16)
 
 
 def expert_rows_call(order, grads, seconds, downs, shares, slots):
     batch, (toks, wide) = len(grads), grads[0].shape
     rank, feats = seconds[0].shape
     units = downs[0].shape[0] // shares
-    tiles = 3
-    tile = units // tiles
     rows = 2 * batch * slots
-    count = shares * 2 * tiles
-    low_shape = (batch, 2 * rank, toks)
-    return order.call(
-        functools.partial(expert_rows_kernel, slots, tiles, shares, batch, 3 * rank),
+    return order.call(
+        functools.partial(expert_rows_kernel, slots, 3, shares, batch, 3 * rank),
         "expert_rows",
-        [*grads, *seconds, *[in_hbm(x) for x in downs]],
-        [ANY] * batch + [whole((rank, feats))] * 2 + [ANY] * 2,
-        [((rows, units), BF16)] * (shares - 1)
-        + [pltpu.HBM((rows, units), BF16), pltpu.HBM(low_shape, BF16)],
-        [whole((rows, units))] * shares + [whole(low_shape)],
+        [*grads, *seconds, *[pltpu.with_memory_space_constraint(x, pltpu.VMEM) for x in downs]],
+        [ANY] * batch + [VMEM] * 4,
+        [((rows, units), BF16)] * shares + [((batch, 2 * rank, toks), BF16)],
+        [VMEM] * (shares + 1),
+        grid=(),
         scratch=[
             pltpu.VMEM((batch, toks, wide), BF16),
             pltpu.VMEM((2, feats, -(-batch * slots // 128) * 128), BF16),
-            pltpu.VMEM((count, tile, feats), BF16),
             pltpu.SemaphoreType.DMA((batch,)),
-            pltpu.SemaphoreType.DMA((count,)),
         ],
-        mib=28,
     )
 
 
@@ -521,7 +538,7 @@
             blocks[o] = flip(fetch(o ^ last), last)
         return blocks[o]
 
-    downs = [down[0], swap(down[0])]
+    downs = [load_call(order, down[0]), swap(down[0])]
     seconds = [second[0], swap(second[0])]
 
     if groups == 8:
@@ -543,7 +560,7 @@
             order, [fetch(o) for o in batch], seconds, downs, shares, slots
         )
         lows.append(low)
-        if 1 < i < len(batches) - 1:
+        if i > 1:
             arrived(i - 2)
         if i > 0:
             send_back(*waiting)
@@ -555,22 +572,22 @@
     low_grad, first_own = collect_call(order, places, lows, grads, feats)
     firsts = [x.reshape(groups * rank, units) for x in (first_own, swap(first_own))]
     low_grad = all_shares(exchange(low_grad))
+    arrived(len(batches) - 2)
+    send_back(*waiting)
     low_hid = all_shares(lowrank_hid_call(order, index, hid, firsts, groups))
-    send_back(*waiting)
-
-    arrived(len(batches) - 3)
-    arrived(len(batches) - 2)
-    scaled_hid = exchange(scaled_hid_call(order, index, weight, low_hid, groups))
 
     low_grad = low_dense_call(order, low_grad)
     first_part = first_grad_call(order, index, weight, low_grad, hid, groups)
-    first_grad = jnp.sum(exchange(first_part, ("ep", "sub")).astype(F32), axis=0)
-    second_keep, second_give = second_grad_call(order, places, scaled_hid, grads, feats)
-    second_grad = second_keep + swap(second_give)
-
+    first_part = exchange(first_part, ("ep", "sub"))
+    first_grad = jnp.sum(first_part.astype(F32), axis=0)
+
+    scaled_hid = exchange(scaled_hid_call(order, index, weight, low_hid, groups))
     back = [back[o] for o in range(groups)]
     grad_hidden, sums = finish_call(order, index, weight, low_grad, hid, firsts, back)
     sums = sums + turn(sums, 1) if shares == 2 else lax.psum(sums, "rep")
+    order.wait([first_part])
+    second_keep, second_give = second_grad_call(order, places, scaled_hid, grads, feats)
+    second_grad = second_keep + swap(second_give)
     return (
         grad_hidden.reshape(toks, top, units),
         sums,

time: 224 us -> 223 us (level)
  Pallas kernels: 79.4 us -> 63.4 us
  blocking collectives: 0 us -> 12.3 us
  waiting for transfers between devices: 86.2 us -> 96.2 us
  starting transfers between devices: 45.6 us -> 41.2 us
  local copies, waits for them, and re-layouts: 8.25 us -> 5.93 us
    pallas_call x16 -> x17, Pallas kernels: 79.4 us -> 63.4 us  [call(): pl.pallas_call(ordered, grid=grid, in_specs=[SMEM, *in_specs] + [ANY] * l...]
    all_to_all x0 -> x1, blocking collectives: none -> 12.3 us  [exchange(): return lax.all_to_all(x, axes, split_axis=0, concat_axis=0, tiled=True)]
    ppermute x14, waiting for transfers between devices: 76.3 us -> 84.8 us  [flip(): return lax.ppermute(x, 'ep', [(i, i ^ mask) for i in range(groups)])]
    all_to_all x3 -> x2, starting transfers between devices: 18.6 us -> 11.3 us  [exchange(): return lax.all_to_all(x, axes, split_axis=0, concat_axis=0, tiled=True)]
    ppermute x7, waiting for transfers between devices: 8.17 us -> 11.4 us  [turn(): lax.ppermute(x, 'rep', [(r, (r + offset) % shares) for r in range(shares)])]
    ppermute x7, starting transfers between devices: 6.94 us -> 10 us  [turn(): lax.ppermute(x, 'rep', [(r, (r + offset) % shares) for r in range(shares)])]
    unnamed x70 -> x48, local copies, waits for them, and re-layouts: 8.25 us -> 5.93 us
  transfers between devices with their start and end apart: 28 -> 27, of which waited for: 10 -> 9; matrix products, arithmetic and copies ran while one was open for 2% -> 2% of each run, Pallas kernels for 36% -> 27%
where the time goes in v8:
time: 223 us; the launch traced here: 222 us
  waiting for transfers between devices  96.2 us (43%)
  Pallas kernels  63.4 us (28%)
  starting transfers between devices  41.2 us (18%)
  blocking collectives  12.3 us (6%)
  local copies, waits for them, and re-layouts  5.93 us (3%)
    ppermute x14, waiting for transfers between devices, flip(): return lax.ppermute(x, 'ep', [(i, i ^ mask) for i in range(groups)])  84.8 us
    pallas_call x17, Pallas kernels, call(): pl.pallas_call(ordered, grid=grid, in_specs=[SMEM, *in_specs] + [ANY] * l...  63.4 us
    ppermute x14, starting transfers between devices, flip(): return lax.ppermute(x, 'ep', [(i, i ^ mask) for i in range(groups)])  19.8 us
    all_to_all x1, blocking collectives, exchange(): return lax.all_to_all(x, axes, split_axis=0, concat_axis=0, tiled=True)  12.3 us
    ppermute x7, waiting for transfers between devices, turn(): lax.ppermute(x, 'rep', [(r, (r + offset) % shares) for r in range(shares)])  11.4 us
    all_to_all x2, starting transfers between devices, exchange(): return lax.all_to_all(x, axes, split_axis=0, concat_axis=0, tiled=True)  11.3 us
    ppermute x7, starting transfers between devices, turn(): lax.ppermute(x, 'rep', [(r, (r + offset) % shares) for r in range(shares)])  10 us
    unnamed x48, local copies, waits for them, and re-layouts  5.93 us
  transfers between devices with their start and end apart: 27, of which 9 were waited for; matrix products, arithmetic and copies ran while one was open for 2% of the time, Pallas kernels for 27%

profile of v8, /device:TPU:8, one launch (start us, length us, event | category | flops | bytes accessed | tf_op | source)
XLA Modules:
  0.0 221.6 jit_solution(5518111536482244246)
XLA Ops:
  0.6 0.0 copy-start.8
  0.6 0.1 collective-permute-start.2
  0.7 0.8 copy.18.refs_3_.refs_1_.refs_2_
  1.5 1.0 copy.11
  2.5 0.1 pad_add_fusion.refs_0_
  2.6 1.0 copy-done.15
  3.6 0.8 pack_block.1
  4.4 2.7 %collective-permute-start.4 = (bf16[128,2304]{1,0:T(8,128)(2,1)S(1)}, bf16[128,2304]{1,0:T(8,128)(2,1)S(1)}, u32[]{:S(2)}, u32[]{:S(2)}) collective-permute-start(bf16[128,2304]{1,0:T(8,128)(2,1)S(1)} %get-tuple-element.52.refs_1_.refs_5_.refs_2_), channel_id=1, source_target_pairs={{0,16},{4,20},{8,24},{12,28},{16,0},{20,4},{24,8},{28,12},{1,17},{... | collective-permute-start | bytes 1769480 | tf_op jit(solution)/shard_map/ppermute | solution.py:525
  7.0 0.4 collective-permute-start.3
  7.5 1.5 collective-permute-start
  9.0 23.8 %collective-permute-done.4.refs_2_.refs_8_.refs_5_ = bf16[128,2304]{1,0:T(8,128)(2,1)S(1)} collective-permute-done((bf16[128,2304]{1,0:T(8,128)(2,1)S(1)}, bf16[128,2304]{1,0:T(8,128)(2,1)S(1)}, u32[]{:S(2)}, u32[]{:S(2)}) %collective-permute-start.4) | collective-permute-done | bytes 589856 | tf_op jit(solution)/shard_map/ppermute | solution.py:525
  32.8 1.4 collective-permute-start.6
  34.2 1.6 collective-permute-start.5
  35.9 3.4 %load_matrix.1 = (bf16[1536,2048]{1,0:T(8,128)(2,1)S(1)}, f32[8,128]{1,0:T(8,128)}) custom-call(s32[3]{0:T(128)S(1)} %pad_add_fusion.refs_0_, bf16[1536,2048]{1,0:T(8,128)(2,1)} %bitcast.29, f32[8,128]{1,0:T(8,128)} %get-tuple-element.53.refs_2_), custom_call_target="tpu_custom_call" | custom-call | flops 1 | bytes 1 | tf_op jit(solution)/shard_map/load_matrix/pallas_call | solution.py:52
  39.3 8.1 %expert_rows.4 = (bf16[320,768]{1,0:T(8,128)(2,1)S(1)}, bf16[320,768]{1,0:T(8,128)(2,1)S(1)}, bf16[2,64,128]{2,1,0:T(8,128)(2,1)S(1)}, f32[8,128]{1,0:T(8,128)}) custom-call(s32[3]{0:T(128)S(1)} %pad_add_fusion.refs_0_, bf16[128,2304]{1,0:T(8,128)(2,1)S(1)} %get-tuple-element.52.refs_1_.refs_5_.refs_2_, ...), custom_call_target="tpu_custom_call" | custom-call | flops 1 | bytes 1 | tf_op jit(solution)/shard_map/expert_rows/pallas_call | solution.py:52
  47.4 1.6 collective-permute-start.7
  49.0 7.9 %expert_rows.5 = (bf16[320,768]{1,0:T(8,128)(2,1)S(1)}, bf16[320,768]{1,0:T(8,128)(2,1)S(1)}, bf16[2,64,128]{2,1,0:T(8,128)(2,1)S(1)}, f32[8,128]{1,0:T(8,128)}) custom-call(s32[3]{0:T(128)S(1)} %pad_add_fusion.refs_0_, bf16[128,2304]{1,0:T(8,128)(2,1)S(1)} %collective-permute-done.3.refs_1_.refs_7_.refs_4_, ...), custom_call_target="tpu_custom_call" | custom-call | flops 1 | bytes 1 | tf_op jit(solution)/shard_map/expert_rows/pallas_call | solution.py:52
  56.9 0.6 collective-permute-start.10
  57.5 0.5 collective-permute-start.8
  57.9 1.6 collective-permute-start.9
  59.5 2.1 collective-permute-done.7.refs_2_
  61.5 0.7 share_sum.4
  62.2 0.7 copy-done.16
  62.9 0.5 collective-permute-start.11
  63.4 8.3 %expert_rows.6 = (bf16[320,768]{1,0:T(8,128)(2,1)S(1)}, bf16[320,768]{1,0:T(8,128)(2,1)S(1)}, bf16[2,64,128]{2,1,0:T(8,128)(2,1)S(1)}, f32[8,128]{1,0:T(8,128)}) custom-call(s32[3]{0:T(128)S(1)} %pad_add_fusion.refs_0_, bf16[128,2304]{1,0:T(8,128)(2,1)S(1)} %collective-permute-done.5.refs_1_.refs_9_.refs_6_, ...), custom_call_target="tpu_custom_call" | custom-call | flops 1 | bytes 1 | tf_op jit(solution)/shard_map/expert_rows/pallas_call | solution.py:52
  71.7 1.6 collective-permute-start.12
  73.3 16.9 %collective-permute-done.11.refs_4_.refs_9_ = bf16[160,768]{1,0:T(8,128)(2,1)S(1)} collective-permute-done((bf16[160,768]{1,0:T(8,128)(2,1)S(1)}, bf16[160,768]{1,0:T(8,128)(2,1)S(1)}, u32[]{:S(2)}, u32[]{:S(2)}) %collective-permute-start.11) | collective-permute-done | bytes 245792 | tf_op jit(solution)/shard_map/ppermute | solution.py:525
  90.2 0.7 share_sum.5
  90.9 0.7 collective-permute-start.13
  91.5 3.4 %collective-permute-start.14 = (bf16[160,768]{1,0:T(8,128)(2,1)S(1)}, bf16[160,768]{1,0:T(8,128)(2,1)S(1)}, u32[]{:S(2)}, u32[]{:S(2)}) collective-permute-start(bf16[160,768]{1,0:T(8,128)(2,1)S(1)} %get-tuple-element.74), channel_id=1, source_target_pairs={{0,16},{4,20},{8,24},{12,28},{16,0},{20,4},{24,8},{28,12},{1,17},{... | collective-permute-start | bytes 737288 | tf_op jit(solution)/shard_map/ppermute | solution.py:525
  94.9 9.0 %expert_rows.7 = (bf16[320,768]{1,0:T(8,128)(2,1)}, bf16[320,768]{1,0:T(8,128)(2,1)S(1)}, bf16[2,64,128]{2,1,0:T(8,128)(2,1)S(1)}, f32[8,128]{1,0:T(8,128)}) custom-call(s32[3]{0:T(128)S(1)} %pad_add_fusion.refs_0_, bf16[128,2304]{1,0:T(8,128)(2,1)S(1)} %collective-permute-done.8.refs_1_.refs_11_.refs_8_, ...), custom_call_target="tpu_custom_call" | custom-call | flops 1 | bytes 1 | tf_op jit(solution)/shard_map/expert_rows/pallas_call | solution.py:52
  103.9 0.0 copy-start.21
  103.9 1.6 collective-permute-start.17
  105.5 1.3 share_sum.6
  106.8 1.7 collect_blocks.1
  108.5 0.0 collective-permute-start.18
  108.6 2.3 %collective-permute-start.19 = (bf16[160,768]{1,0:T(8,128)(2,1)S(1)}, bf16[160,768]{1,0:T(8,128)(2,1)S(1)}, u32[]{:S(2)}, u32[]{:S(2)}) collective-permute-start(bf16[160,768]{1,0:T(8,128)(2,1)S(1)} %get-tuple-element.82), channel_id=1, source_target_pairs={{0,24},{4,28},{8,16},{12,20},{16,8},{20,12},{24,0},{28,4},{1,25},{... | collective-permute-start | bytes 737288 | tf_op jit(solution)/shard_map/ppermute | solution.py:525
  110.9 5.7 %all-to-all-start = ((bf16[8,64,128]{2,1,0:T(8,128)(2,1)}), bf16[8,64,128]{2,1,0:T(8,128)(2,1)S(1)}, u32[]{:S(2)}, u32[]{:S(2)}) async-start(bf16[8,64,128]{2,1,0:T(8,128)(2,1)} %get-tuple-element.76), calls=%async_computation | async-start | bytes 262144 | tf_op jit(solution)/shard_map/all_to_all | solution.py:531
  116.6 1.8 collective-permute-done.18.refs_4_.refs_11_
  118.4 4.0 %collective-permute-done.19.refs_5_.refs_14_ = bf16[160,768]{1,0:T(8,128)(2,1)S(1)} collective-permute-done((bf16[160,768]{1,0:T(8,128)(2,1)S(1)}, bf16[160,768]{1,0:T(8,128)(2,1)S(1)}, u32[]{:S(2)}, u32[]{:S(2)}) %collective-permute-start.19) | collective-permute-done | bytes 245792 | tf_op jit(solution)/shard_map/ppermute | solution.py:525
  122.4 0.7 share_sum.7
  123.1 3.7 %lowrank_hid.1 = (f32[128,512]{1,0:T(8,128)S(1)}, f32[8,128]{1,0:T(8,128)}) custom-call(s32[3]{0:T(128)S(1)} %pad_add_fusion.refs_0_, s32[128,8]{1,0:T(8,128)S(1)} %copy.18.refs_3_.refs_1_.refs_2_, bf16[1024,768]{1,0:T(8,128)(2,1)} %bitcast.25, bf16[256,768]{1,0:T(8,128)(2,1)S(1)} %bitcast.20, bf16[256,768]{1,0:T(8,128)(2,1)S(1)} %bitcast.22, ...), custom_call_target="tpu_custom_call" | custom-call | flops 1 | bytes 1 | tf_op jit(solution)/shard_map/lowrank_hid/pallas_call | solution.py:52
  126.8 3.0 %collective-permute-start.22 = (f32[128,512]{1,0:T(8,128)S(1)}, f32[128,512]{1,0:T(8,128)S(1)}, u32[]{:S(2)}, u32[]{:S(2)}) collective-permute-start(f32[128,512]{1,0:T(8,128)S(1)} %get-tuple-element.89.refs_3_), channel_id=1, source_target_pairs={{0,2},{2,0},{1,3},{3,1},{4,6},{6,4},{5,7},{7,5},{8,10},{10,8},{9,1... | collective-permute-start | bytes 786440 | tf_op jit(solution)/shard_map/ppermute | solution.py:519
  129.8 0.1 collective-permute-start.15
  129.9 0.1 copy.20.refs_2_.refs_3_
  130.0 6.3 %collective-permute-done.15.refs_2_ = bf16[8,64,128]{2,1,0:T(8,128)(2,1)S(1)} collective-permute-done((bf16[8,64,128]{2,1,0:T(8,128)(2,1)S(1)}, bf16[8,64,128]{2,1,0:T(8,128)(2,1)S(1)}, u32[]{:S(2)}, u32[]{:S(2)}) %collective-permute-start.15) | collective-permute-done | bytes 131104 | tf_op jit(solution)/shard_map/ppermute | solution.py:519
  136.4 0.7 low_dense.1
  137.1 4.3 %first_grad.1 = (bf16[16,32,768]{2,1,0:T(8,128)(2,1)S(1)}, f32[8,128]{1,0:T(8,128)}) custom-call(s32[3]{0:T(128)S(1)} %pad_add_fusion.refs_0_, s32[128,8]{1,0:T(8,128)S(1)} %copy.18.refs_3_.refs_1_.refs_2_, bf16[128,8]{1,0:T(8,128)(2,1)S(1)} %copy.20.refs_2_.refs_3_, f32[128,512]{1,0:T(8,128)S(1)} %get-tuple-element.85.refs_3_.refs_4_, ...), custom_call_target="tpu_custom_call" | custom-call | flops 1 | bytes 1 | tf_op jit(solution)/shard_map/first_grad/pallas_call | solution.py:52
  141.4 0.9 copy-done.14
  142.3 1.0 scaled_hid.1
  143.2 12.3 %all_to_all.15.refs_1_ = bf16[8,64,128]{2,1,0:T(8,128)(2,1)S(1)} all-to-all(bf16[8,64,128]{2,1,0:T(8,128)(2,1)S(1)} %get-tuple-element.96), channel_id=1, replica_groups=mesh['grp'=1,'ep'=8,'rep'=2,'sub'=2] {'ep'}, dimensions={0} | all-to-all | bytes 262144 | tf_op jit(solution)/shard_map/all_to_all | solution.py:531
  155.5 5.6 %all-to-all-start.1 = ((bf16[16,32,768]{2,1,0:T(8,128)(2,1)}), bf16[16,32,768]{2,1,0:T(8,128)(2,1)S(1)}, u32[]{:S(2)}, u32[]{:S(2)}) async-start(bf16[16,32,768]{2,1,0:T(8,128)(2,1)} %copy-done.14), calls=%async_computation.1 | async-start | bytes 1572864 | tf_op jit(solution)/shard_map/all_to_all | solution.py:531
  161.1 3.3 %collective-permute-start.20 = (bf16[160,768]{1,0:T(8,128)(2,1)}, bf16[160,768]{1,0:T(8,128)(2,1)S(1)}, u32[]{:S(2)}, u32[]{:S(2)}) collective-permute-start(bf16[160,768]{1,0:T(8,128)(2,1)} %copy-done.18), channel_id=1, source_target_pairs={{0,20},{4,16},{8,28},{12,24},{16,4},{20,0},{24,12},{28,8},{1,21},{... | collective-permute-start | bytes 737288 | tf_op jit(solution)/shard_map/ppermute | solution.py:525
  164.5 30.7 %collective-permute-done.20.refs_13_ = bf16[160,768]{1,0:T(8,128)(2,1)S(1)} collective-permute-done((bf16[160,768]{1,0:T(8,128)(2,1)}, bf16[160,768]{1,0:T(8,128)(2,1)S(1)}, u32[]{:S(2)}, u32[]{:S(2)}) %collective-permute-start.20) | collective-permute-done | bytes 245792 | tf_op jit(solution)/shard_map/ppermute | solution.py:525
  195.1 7.5 %collective-permute-done.21.refs_15_ = bf16[160,768]{1,0:T(8,128)(2,1)S(1)} collective-permute-done((bf16[160,768]{1,0:T(8,128)(2,1)}, bf16[160,768]{1,0:T(8,128)(2,1)S(1)}, u32[]{:S(2)}, u32[]{:S(2)}) %collective-permute-start.21) | collective-permute-done | bytes 245792 | tf_op jit(solution)/shard_map/ppermute | solution.py:525
  202.7 0.7 copy-done.20
  203.4 7.8 %finish.1 = (bf16[1024,768]{1,0:T(8,128)(2,1)}, f32[128,8]{1,0:T(8,128)S(1)}, f32[8,128]{1,0:T(8,128)}) custom-call(s32[3]{0:T(128)S(1)} %pad_add_fusion.refs_0_, s32[128,8]{1,0:T(8,128)S(1)} %copy.18.refs_3_.refs_1_.refs_2_, s32[128,8]{1,0:T(8,128)S(1)} %copy.18.refs_3_.refs_1_.refs_2_, bf16[128,8]{1,0:T(8,128)(2,1)S(1)} %copy.20.refs_2_.refs_3_, ...), custom_call_target="tpu_custom_call" | custom-call | flops 1 | bytes 1 | tf_op jit(solution)/shard_map/finish/pallas_call | solution.py:52
  211.2 3.7 %second_grad.1 = (f32[32,2048]{1,0:T(8,128)S(1)}, f32[32,2048]{1,0:T(8,128)S(1)}, f32[8,128]{1,0:T(8,128)}) custom-call(s32[3]{0:T(128)S(1)} %pad_add_fusion.refs_0_, bf16[8,64,128]{2,1,0:T(8,128)(2,1)S(1)} %all_to_all.15.refs_1_, bf16[128,2304]{1,0:T(8,128)(2,1)} %copy-done, bf16[128,2304]{1,0:T(8,128)(2,1)} %copy-done.3, bf16[128,2304]{1,0:T(8,128)(2,1)} %copy-done.2, ...), custom_call_target="tpu_custom_call" | custom-call | flops 1 | bytes 1 | tf_op jit(solution)/shard_map/second_grad/pallas_call | solution.py:52
  214.9 0.1 collective-permute-start.24
  215.0 1.6 collective-permute-start.23
  216.5 2.9 %collective-permute-done.23 = f32[128,8]{1,0:T(8,128)S(1)} collective-permute-done((f32[128,8]{1,0:T(8,128)S(1)}, f32[128,8]{1,0:T(8,128)S(1)}, u32[]{:S(2)}, u32[]{:S(2)}) %collective-permute-start.23) | collective-permute-done | bytes 4128 | tf_op jit(solution)/shard_map/ppermute | solution.py:519
  219.5 0.7 copy.21
  220.1 0.7 convert_reduce_fusion
  220.9 0.7 add_bitcast_fusion
  (60 shorter events, 0.1 us)
Async XLA Ops:
  0.6 38.7 %copy-start.8 = (bf16[1,32,2048]{2,1,0:T(8,128)(2,1)S(1)}, bf16[1,32,2048]{2,1,0:T(8,128)(2,1)}, u32[]{:S(2)}) copy-start(bf16[1,32,2048]{2,1,0:T(8,128)(2,1)} %param.13) | copy-start | bytes 393220
  0.6 38.7 %collective-permute-start.2 = (bf16[1536,2048]{1,0:T(8,128)(2,1)}, bf16[1536,2048]{1,0:T(8,128)(2,1)}, u32[]{:S(2)}, u32[]{:S(2)}) collective-permute-start(bf16[1536,2048]{1,0:T(8,128)(2,1)} %bitcast.28), channel_id=1, source_target_pairs={{0,1},{1,0},{2,3},{3,2},{4,5},{5,4},{6,7},{7,6},{8,9},{9,8},{10,11... | collective-permute-start | bytes 18874376 | tf_op jit(solution)/shard_map/ppermute | solution.py:528
  2.6 1.0 copy-start.15
  4.4 43.0 %copy-start = (bf16[128,2304]{1,0:T(8,128)(2,1)}, bf16[128,2304]{1,0:T(8,128)(2,1)S(1)}, u32[]{:S(2)}) copy-start(bf16[128,2304]{1,0:T(8,128)(2,1)S(1)} %get-tuple-element.52.refs_1_.refs_5_.refs_2_) | copy-start | bytes 1769476
  4.4 28.4 %collective-permute-start.4 = (bf16[128,2304]{1,0:T(8,128)(2,1)S(1)}, bf16[128,2304]{1,0:T(8,128)(2,1)S(1)}, u32[]{:S(2)}, u32[]{:S(2)}) collective-permute-start(bf16[128,2304]{1,0:T(8,128)(2,1)S(1)} %get-tuple-element.52.refs_1_.refs_5_.refs_2_), channel_id=1, source_target_pairs={{0,16},{4,20},{8,24},{12,28},{16,0},{20,4},{24,8},{28,12},{1,17},{... | collective-permute-start | bytes 1769480 | tf_op jit(solution)/shard_map/ppermute | solution.py:525
  7.0 27.2 %collective-permute-start.3 = (bf16[128,2304]{1,0:T(8,128)(2,1)S(1)}, bf16[128,2304]{1,0:T(8,128)(2,1)S(1)}, u32[]{:S(2)}, u32[]{:S(2)}) collective-permute-start(bf16[128,2304]{1,0:T(8,128)(2,1)S(1)} %get-tuple-element.52.refs_1_.refs_5_.refs_2_), channel_id=1, source_target_pairs={{0,8},{4,12},{8,0},{12,4},{16,24},{20,28},{24,16},{28,20},{1,9},{5... | collective-permute-start | bytes 1769480 | tf_op jit(solution)/shard_map/ppermute | solution.py:525
  7.5 31.8 %collective-permute-start = (bf16[128,2304]{1,0:T(8,128)(2,1)S(1)}, bf16[128,2304]{1,0:T(8,128)(2,1)S(1)}, u32[]{:S(2)}, u32[]{:S(2)}) collective-permute-start(bf16[128,2304]{1,0:T(8,128)(2,1)S(1)} %get-tuple-element.52.refs_1_.refs_5_.refs_2_), channel_id=1, source_target_pairs={{0,4},{4,0},{8,12},{12,8},{16,20},{20,16},{24,28},{28,24},{1,5},{5... | collective-permute-start | bytes 1769480 | tf_op jit(solution)/shard_map/ppermute | solution.py:525
  32.8 24.6 %copy-start.1 = (bf16[128,2304]{1,0:T(8,128)(2,1)}, bf16[128,2304]{1,0:T(8,128)(2,1)S(1)}, u32[]{:S(2)}) copy-start(bf16[128,2304]{1,0:T(8,128)(2,1)S(1)} %collective-permute-done.4.refs_2_.refs_8_.refs_5_) | copy-start | bytes 1769476
  32.8 25.1 %collective-permute-start.6 = (bf16[128,2304]{1,0:T(8,128)(2,1)S(1)}, bf16[128,2304]{1,0:T(8,128)(2,1)S(1)}, u32[]{:S(2)}, u32[]{:S(2)}) collective-permute-start(bf16[128,2304]{1,0:T(8,128)(2,1)S(1)} %collective-permute-done.4.refs_2_.refs_8_.refs_5_), channel_id=1, source_target_pairs={{0,8},{4,12},{8,0},{12,4},{16,24},{20,28},{24,16},{28,20},{1,9},{5... | collective-permute-start | bytes 1769480 | tf_op jit(solution)/shard_map/ppermute | solution.py:525
  34.2 5.1 %collective-permute-start.1 = (bf16[32,2048]{1,0:T(8,128)(2,1)}, bf16[32,2048]{1,0:T(8,128)(2,1)S(1)}, u32[]{:S(2)}, u32[]{:S(2)}) collective-permute-start(bf16[32,2048]{1,0:T(8,128)(2,1)} %bitcast.15), channel_id=1, source_target_pairs={{0,1},{1,0},{2,3},{3,2},{4,5},{5,4},{6,7},{7,6},{8,9},{9,8},{10,11... | collective-permute-start | bytes 393224 | tf_op jit(solution)/shard_map/ppermute | solution.py:528
  34.2 14.8 %copy-start.2 = (bf16[128,2304]{1,0:T(8,128)(2,1)}, bf16[128,2304]{1,0:T(8,128)(2,1)S(1)}, u32[]{:S(2)}) copy-start(bf16[128,2304]{1,0:T(8,128)(2,1)S(1)} %collective-permute-done.3.refs_1_.refs_7_.refs_4_) | copy-start | bytes 1769476
  34.2 29.2 %collective-permute-start.5 = (bf16[128,2304]{1,0:T(8,128)(2,1)S(1)}, bf16[128,2304]{1,0:T(8,128)(2,1)S(1)}, u32[]{:S(2)}, u32[]{:S(2)}) collective-permute-start(bf16[128,2304]{1,0:T(8,128)(2,1)S(1)} %collective-permute-done.3.refs_1_.refs_7_.refs_4_), channel_id=1, source_target_pairs={{0,4},{4,0},{8,12},{12,8},{16,20},{20,16},{24,28},{28,24},{1,5},{5... | collective-permute-start | bytes 1769480 | tf_op jit(solution)/shard_map/ppermute | solution.py:525
  39.3 8.1 %copy-start.3 = (bf16[128,2304]{1,0:T(8,128)(2,1)}, bf16[128,2304]{1,0:T(8,128)(2,1)S(1)}, u32[]{:S(2)}) copy-start(bf16[128,2304]{1,0:T(8,128)(2,1)S(1)} %collective-permute-done.refs_2_.refs_6_.refs_3_) | copy-start | bytes 1769476
  47.4 14.1 %collective-permute-start.7 = (bf16[320,768]{1,0:T(8,128)(2,1)S(1)}, bf16[320,768]{1,0:T(8,128)(2,1)S(1)}, u32[]{:S(2)}, u32[]{:S(2)}) collective-permute-start(bf16[320,768]{1,0:T(8,128)(2,1)S(1)} %get-tuple-element.60), channel_id=1, source_target_pairs={{0,2},{2,0},{1,3},{3,1},{4,6},{6,4},{5,7},{7,5},{8,10},{10,8},{9,1... | collective-permute-start | bytes 1474568 | tf_op jit(solution)/shard_map/ppermute | solution.py:519
  56.9 16.4 %collective-permute-start.10 = (bf16[320,768]{1,0:T(8,128)(2,1)S(1)}, bf16[320,768]{1,0:T(8,128)(2,1)S(1)}, u32[]{:S(2)}, u32[]{:S(2)}) collective-permute-start(bf16[320,768]{1,0:T(8,128)(2,1)S(1)} %get-tuple-element.65), channel_id=1, source_target_pairs={{0,2},{2,0},{1,3},{3,1},{4,6},{6,4},{5,7},{7,5},{8,10},{10,8},{9,1... | collective-permute-start | bytes 1474568 | tf_op jit(solution)/shard_map/ppermute | solution.py:519
  57.5 37.4 %collective-permute-start.8 = (bf16[128,2304]{1,0:T(8,128)(2,1)S(1)}, bf16[128,2304]{1,0:T(8,128)(2,1)S(1)}, u32[]{:S(2)}, u32[]{:S(2)}) collective-permute-start(bf16[128,2304]{1,0:T(8,128)(2,1)S(1)} %collective-permute-done.4.refs_2_.refs_8_.refs_5_), channel_id=1, source_target_pairs={{0,4},{4,0},{8,12},{12,8},{16,20},{20,16},{24,28},{28,24},{1,5},{5... | collective-permute-start | bytes 1769480 | tf_op jit(solution)/shard_map/ppermute | solution.py:525
  57.9 13.7 %copy-start.4 = (bf16[128,2304]{1,0:T(8,128)(2,1)}, bf16[128,2304]{1,0:T(8,128)(2,1)S(1)}, u32[]{:S(2)}) copy-start(bf16[128,2304]{1,0:T(8,128)(2,1)S(1)} %collective-permute-done.6.refs_2_.refs_10_.refs_7_) | copy-start | bytes 1769476
  57.9 37.0 %collective-permute-start.9 = (bf16[128,2304]{1,0:T(8,128)(2,1)S(1)}, bf16[128,2304]{1,0:T(8,128)(2,1)S(1)}, u32[]{:S(2)}, u32[]{:S(2)}) collective-permute-start(bf16[128,2304]{1,0:T(8,128)(2,1)S(1)} %collective-permute-done.6.refs_2_.refs_10_.refs_7_), channel_id=1, source_target_pairs={{0,4},{4,0},{8,12},{12,8},{16,20},{20,16},{24,28},{28,24},{1,5},{5... | collective-permute-start | bytes 1769480 | tf_op jit(solution)/shard_map/ppermute | solution.py:525
  62.2 0.7 copy-start.16
  62.9 27.3 %collective-permute-start.11 = (bf16[160,768]{1,0:T(8,128)(2,1)S(1)}, bf16[160,768]{1,0:T(8,128)(2,1)S(1)}, u32[]{:S(2)}, u32[]{:S(2)}) collective-permute-start(bf16[160,768]{1,0:T(8,128)(2,1)S(1)} %get-tuple-element.67), channel_id=1, source_target_pairs={{0,4},{4,0},{8,12},{12,8},{16,20},{20,16},{24,28},{28,24},{1,5},{5... | collective-permute-start | bytes 737288 | tf_op jit(solution)/shard_map/ppermute | solution.py:525
  63.4 8.3 %copy-start.5 = (bf16[128,2304]{1,0:T(8,128)(2,1)}, bf16[128,2304]{1,0:T(8,128)(2,1)S(1)}, u32[]{:S(2)}) copy-start(bf16[128,2304]{1,0:T(8,128)(2,1)S(1)} %collective-permute-done.5.refs_1_.refs_9_.refs_6_) | copy-start | bytes 1769476
  71.7 33.8 %collective-permute-start.12 = (bf16[320,768]{1,0:T(8,128)(2,1)S(1)}, bf16[320,768]{1,0:T(8,128)(2,1)S(1)}, u32[]{:S(2)}, u32[]{:S(2)}) collective-permute-start(bf16[320,768]{1,0:T(8,128)(2,1)S(1)} %get-tuple-element.71), channel_id=1, source_target_pairs={{0,2},{2,0},{1,3},{3,1},{4,6},{6,4},{5,7},{7,5},{8,10},{10,8},{9,1... | collective-permute-start | bytes 1474568 | tf_op jit(solution)/shard_map/ppermute | solution.py:519
  90.2 13.7 %copy-start.9 = (bf16[160,768]{1,0:T(8,128)(2,1)}, bf16[160,768]{1,0:T(8,128)(2,1)S(1)}, u32[]{:S(2)}) copy-start(bf16[160,768]{1,0:T(8,128)(2,1)S(1)} %collective-permute-done.11.refs_4_.refs_9_) | copy-start | bytes 737284
  90.9 14.6 %collective-permute-start.13 = (bf16[160,768]{1,0:T(8,128)(2,1)S(1)}, bf16[160,768]{1,0:T(8,128)(2,1)S(1)}, u32[]{:S(2)}, u32[]{:S(2)}) collective-permute-start(bf16[160,768]{1,0:T(8,128)(2,1)S(1)} %get-tuple-element.73), channel_id=1, source_target_pairs={{0,8},{4,12},{8,0},{12,4},{16,24},{20,28},{24,16},{28,20},{1,9},{5... | collective-permute-start | bytes 737288 | tf_op jit(solution)/shard_map/ppermute | solution.py:525
  91.5 14.0 %collective-permute-start.14 = (bf16[160,768]{1,0:T(8,128)(2,1)S(1)}, bf16[160,768]{1,0:T(8,128)(2,1)S(1)}, u32[]{:S(2)}, u32[]{:S(2)}) collective-permute-start(bf16[160,768]{1,0:T(8,128)(2,1)S(1)} %get-tuple-element.74), channel_id=1, source_target_pairs={{0,16},{4,20},{8,24},{12,28},{16,0},{20,4},{24,8},{28,12},{1,17},{... | collective-permute-start | bytes 737288 | tf_op jit(solution)/shard_map/ppermute | solution.py:525
  94.9 9.0 %copy-start.6 = (bf16[128,2304]{1,0:T(8,128)(2,1)}, bf16[128,2304]{1,0:T(8,128)(2,1)S(1)}, u32[]{:S(2)}) copy-start(bf16[128,2304]{1,0:T(8,128)(2,1)S(1)} %collective-permute-done.8.refs_1_.refs_11_.refs_8_) | copy-start | bytes 1769476
  94.9 9.0 %copy-start.7 = (bf16[128,2304]{1,0:T(8,128)(2,1)}, bf16[128,2304]{1,0:T(8,128)(2,1)S(1)}, u32[]{:S(2)}) copy-start(bf16[128,2304]{1,0:T(8,128)(2,1)S(1)} %collective-permute-done.9.refs_2_.refs_12_.refs_9_) | copy-start | bytes 1769476
  103.9 26.0 %copy-start.21 = (bf16[128,8]{0,1:T(8,128)(2,1)S(1)}, bf16[128,8]{0,1:T(8,128)(2,1)}, u32[]{:S(2)}) copy-start(bf16[128,8]{0,1:T(8,128)(2,1)} %param.10) | copy-start | bytes 6148
  103.9 12.7 %collective-permute-start.17 = (bf16[320,768]{1,0:T(8,128)(2,1)}, bf16[320,768]{1,0:T(8,128)(2,1)S(1)}, u32[]{:S(2)}, u32[]{:S(2)}) collective-permute-start(bf16[320,768]{1,0:T(8,128)(2,1)} %get-tuple-element.79), channel_id=1, source_target_pairs={{0,2},{2,0},{1,3},{3,1},{4,6},{6,4},{5,7},{7,5},{8,10},{10,8},{9,1... | collective-permute-start | bytes 1474568 | tf_op jit(solution)/shard_map/ppermute | solution.py:519
  105.5 35.9 %copy-start.10 = (bf16[160,768]{1,0:T(8,128)(2,1)}, bf16[160,768]{1,0:T(8,128)(2,1)S(1)}, u32[]{:S(2)}) copy-start(bf16[160,768]{1,0:T(8,128)(2,1)S(1)} %collective-permute-done.13.refs_4_.refs_10_) | copy-start | bytes 737284
  105.5 35.9 %copy-start.11 = (bf16[160,768]{1,0:T(8,128)(2,1)}, bf16[160,768]{1,0:T(8,128)(2,1)S(1)}, u32[]{:S(2)}) copy-start(bf16[160,768]{1,0:T(8,128)(2,1)S(1)} %collective-permute-done.14.refs_5_.refs_12_) | copy-start | bytes 737284
  108.5 14.5 %collective-permute-start.16 = (bf16[8,32,768]{2,1,0:T(8,128)(2,1)S(1)}, bf16[8,32,768]{2,1,0:T(8,128)(2,1)S(1)}, u32[]{:S(2)}, u32[]{:S(2)}) collective-permute-start(bf16[8,32,768]{2,1,0:T(8,128)(2,1)S(1)} %get-tuple-element.77), channel_id=1, source_target_pairs={{0,1},{1,0},{2,3},{3,2},{4,5},{5,4},{6,7},{7,6},{8,9},{9,8},{10,11... | collective-permute-start | bytes 1179656 | tf_op jit(solution)/shard_map/ppermute | solution.py:528
  108.5 9.9 %collective-permute-start.18 = (bf16[160,768]{1,0:T(8,128)(2,1)}, bf16[160,768]{1,0:T(8,128)(2,1)S(1)}, u32[]{:S(2)}, u32[]{:S(2)}) collective-permute-start(bf16[160,768]{1,0:T(8,128)(2,1)} %get-tuple-element.81), channel_id=1, source_target_pairs={{0,12},{4,8},{8,4},{12,0},{16,28},{20,24},{24,20},{28,16},{1,13},{... | collective-permute-start | bytes 737288 | tf_op jit(solution)/shard_map/ppermute | solution.py:525
  108.6 13.8 %collective-permute-start.19 = (bf16[160,768]{1,0:T(8,128)(2,1)S(1)}, bf16[160,768]{1,0:T(8,128)(2,1)S(1)}, u32[]{:S(2)}, u32[]{:S(2)}) collective-permute-start(bf16[160,768]{1,0:T(8,128)(2,1)S(1)} %get-tuple-element.82), channel_id=1, source_target_pairs={{0,24},{4,28},{8,16},{12,20},{16,8},{20,12},{24,0},{28,4},{1,25},{... | collective-permute-start | bytes 737288 | tf_op jit(solution)/shard_map/ppermute | solution.py:525
  110.9 19.0 %all-to-all-start = ((bf16[8,64,128]{2,1,0:T(8,128)(2,1)}), bf16[8,64,128]{2,1,0:T(8,128)(2,1)S(1)}, u32[]{:S(2)}, u32[]{:S(2)}) async-start(bf16[8,64,128]{2,1,0:T(8,128)(2,1)} %get-tuple-element.76), calls=%async_computation | async-start | bytes 262144 | tf_op jit(solution)/shard_map/all_to_all | solution.py:531
  118.4 84.3 %copy-start.12 = (bf16[160,768]{1,0:T(8,128)(2,1)}, bf16[160,768]{1,0:T(8,128)(2,1)S(1)}, u32[]{:S(2)}) copy-start(bf16[160,768]{1,0:T(8,128)(2,1)S(1)} %collective-permute-done.18.refs_4_.refs_11_) | copy-start | bytes 737284
  122.4 80.3 %copy-start.13 = (bf16[160,768]{1,0:T(8,128)(2,1)}, bf16[160,768]{1,0:T(8,128)(2,1)S(1)}, u32[]{:S(2)}) copy-start(bf16[160,768]{1,0:T(8,128)(2,1)S(1)} %collective-permute-done.19.refs_5_.refs_14_) | copy-start | bytes 737284
  123.0 3.8 %copy-start.18 = (bf16[160,768]{1,0:T(8,128)(2,1)}, bf16[160,768]{1,0:T(8,128)(2,1)S(1)}, u32[]{:S(2)}) copy-start(bf16[160,768]{1,0:T(8,128)(2,1)S(1)} %get-tuple-element.87) | copy-start | bytes 737284
  123.0 13.3 %copy-start.17 = (bf16[160,768]{1,0:T(8,128)(2,1)}, bf16[160,768]{1,0:T(8,128)(2,1)S(1)}, u32[]{:S(2)}) copy-start(bf16[160,768]{1,0:T(8,128)(2,1)S(1)} %get-tuple-element.88) | copy-start | bytes 737284
  126.8 15.5 %collective-permute-start.22 = (f32[128,512]{1,0:T(8,128)S(1)}, f32[128,512]{1,0:T(8,128)S(1)}, u32[]{:S(2)}, u32[]{:S(2)}) collective-permute-start(f32[128,512]{1,0:T(8,128)S(1)} %get-tuple-element.89.refs_3_), channel_id=1, source_target_pairs={{0,2},{2,0},{1,3},{3,1},{4,6},{6,4},{5,7},{7,5},{8,10},{10,8},{9,1... | collective-permute-start | bytes 786440 | tf_op jit(solution)/shard_map/ppermute | solution.py:519
  129.8 6.6 %collective-permute-start.15 = (bf16[8,64,128]{2,1,0:T(8,128)(2,1)S(1)}, bf16[8,64,128]{2,1,0:T(8,128)(2,1)S(1)}, u32[]{:S(2)}, u32[]{:S(2)}) collective-permute-start(bf16[8,64,128]{2,1,0:T(8,128)(2,1)S(1)} %all-to-all-done.refs_1_), channel_id=1, source_target_pairs={{0,2},{2,0},{1,3},{3,1},{4,6},{6,4},{5,7},{7,5},{8,10},{10,8},{9,1... | collective-permute-start | bytes 393224 | tf_op jit(solution)/shard_map/ppermute | solution.py:519
  141.3 0.9 copy-start.14
  155.5 55.6 %all-to-all-start.1 = ((bf16[16,32,768]{2,1,0:T(8,128)(2,1)}), bf16[16,32,768]{2,1,0:T(8,128)(2,1)S(1)}, u32[]{:S(2)}, u32[]{:S(2)}) async-start(bf16[16,32,768]{2,1,0:T(8,128)(2,1)} %copy-done.14), calls=%async_computation.1 | async-start | bytes 1572864 | tf_op jit(solution)/shard_map/all_to_all | solution.py:531
  161.1 34.0 %collective-permute-start.20 = (bf16[160,768]{1,0:T(8,128)(2,1)}, bf16[160,768]{1,0:T(8,128)(2,1)S(1)}, u32[]{:S(2)}, u32[]{:S(2)}) collective-permute-start(bf16[160,768]{1,0:T(8,128)(2,1)} %copy-done.18), channel_id=1, source_target_pairs={{0,20},{4,16},{8,28},{12,24},{16,4},{20,0},{24,12},{28,8},{1,21},{... | collective-permute-start | bytes 737288 | tf_op jit(solution)/shard_map/ppermute | solution.py:525
  164.5 38.2 %collective-permute-start.21 = (bf16[160,768]{1,0:T(8,128)(2,1)}, bf16[160,768]{1,0:T(8,128)(2,1)S(1)}, u32[]{:S(2)}, u32[]{:S(2)}) collective-permute-start(bf16[160,768]{1,0:T(8,128)(2,1)} %copy-done.17), channel_id=1, source_target_pairs={{0,28},{4,24},{8,20},{12,16},{16,12},{20,8},{24,4},{28,0},{1,29},{... | collective-permute-start | bytes 737288 | tf_op jit(solution)/shard_map/ppermute | solution.py:525
  195.1 7.6 %copy-start.19 = (bf16[160,768]{1,0:T(8,128)(2,1)}, bf16[160,768]{1,0:T(8,128)(2,1)S(1)}, u32[]{:S(2)}) copy-start(bf16[160,768]{1,0:T(8,128)(2,1)S(1)} %collective-permute-done.20.refs_13_) | copy-start | bytes 737284
  202.7 0.7 copy-start.20
  214.9 6.0 %collective-permute-start.24 = (f32[32,2048]{1,0:T(8,128)S(1)}, f32[32,2048]{1,0:T(8,128)S(1)}, u32[]{:S(2)}, u32[]{:S(2)}) collective-permute-start(f32[32,2048]{1,0:T(8,128)S(1)} %get-tuple-element.99), channel_id=1, source_target_pairs={{0,1},{1,0},{2,3},{3,2},{4,5},{5,4},{6,7},{7,6},{8,9},{9,8},{10,11... | collective-permute-start | bytes 786440 | tf_op jit(solution)/shard_map/ppermute | solution.py:528
  215.0 4.5 %collective-permute-start.23 = (f32[128,8]{1,0:T(8,128)S(1)}, f32[128,8]{1,0:T(8,128)S(1)}, u32[]{:S(2)}, u32[]{:S(2)}) collective-permute-start(f32[128,8]{1,0:T(8,128)S(1)} %get-tuple-element.94), channel_id=1, source_target_pairs={{0,2},{2,0},{1,3},{3,1},{4,6},{6,4},{5,7},{7,5},{8,10},{10,8},{9,1... | collective-permute-start | bytes 12296 | tf_op jit(solution)/shard_map/ppermute | solution.py:519

commit v9 on v8

--- a/solution.py
+++ b/solution.py
@@ -14,6 +14,7 @@
 TN = (((0,), (0,)), ((), ()))
 NN = (((1,), (0,)), ((), ()))
 SMALL = pl.CostEstimate(flops=1, bytes_accessed=1, transcendentals=0)
+LONG = pl.CostEstimate(flops=1, bytes_accessed=2 * 10**7, transcendentals=0)
 ANY = pl.BlockSpec(memory_space=pl.ANY)
 SMEM = pl.BlockSpec(memory_space=pltpu.SMEM)
 VMEM = pl.BlockSpec(memory_space=pltpu.VMEM)
@@ -91,40 +92,37 @@
     return iota((column.shape[0], width), 1) // rank == column.astype(jnp.int32)
 
 
-def pack_kernel(rank, at_ref, grad_ref, first_ref, index_ref, out_ref):
+def pack_kernel(at_ref, grad_ref, first_ref, index_ref, out_ref):
     toks, feats = grad_ref.shape
+    rank = first_ref.shape[0]
     extra = out_ref.shape[1] - feats
     out_ref[:, pl.ds(0, feats)] = grad_ref[...]
-    same = jnp.where(iota((rank, rank), 0) == iota((rank, rank), 1), 1.0, 0.0).astype(BF16)
-    factor = dot(same, first_ref[...], NT).astype(BF16)
     for k in range(3):
-        piece = factor[:, k * extra : (k + 1) * extra]
+        piece = first_ref[:, pl.ds(k * extra, extra)]
         out_ref[pl.ds(k * rank, rank), pl.ds(feats, extra)] = piece
-    top = index_ref.shape[1]
+    top = index_ref.shape[0]
     out_ref[pl.ds(3 * rank, toks - 3 * rank), pl.ds(feats, extra)] = jnp.full(
         (toks - 3 * rank, extra), -1.0, BF16
     )
-    turn = jnp.where(iota((16, top), 0) == iota((16, top), 1), 1.0, 0.0).astype(BF16)
-    routes = dot(turn, index_ref[...].astype(F32).astype(BF16), NT)
-    routes = jnp.where(iota((16, toks), 0) < top, routes, -1.0)
+    routes = index_ref[...].astype(F32)
+    routes = jnp.concatenate([routes, jnp.full((16 - top, toks), -1.0, F32)], axis=0)
     out_ref[pl.ds(3 * rank, 16), pl.ds(feats, toks)] = routes.astype(BF16)
 
 
 def pack_call(order, grad, first, index):
-    (toks, feats), (units, rank) = grad.shape, first.shape
-    extra = units // 3
-    shape = (toks, feats + extra)
-    return order.call(
-        functools.partial(pack_kernel, rank),
+    (toks, feats), (rank, units) = grad.shape, first.shape
+    shape = (toks, feats + units // 3)
+    return order.call(
+        pack_kernel,
         "pack_block",
-        [grad, first, index],
+        [in_hbm(grad), first, index],
         [whole(grad.shape), whole(first.shape), whole(index.shape)],
         [(shape, BF16)],
         [whole(shape)],
     )[0]
 
 
-def load_kernel(at_ref, down_ref, out_ref, sems):
+def load_kernel(at_ref, down_ref, second_ref, out_ref, same_ref, sems):
     parts = sems.shape[0]
     rows = down_ref.shape[0] // parts
     copies = [
@@ -135,21 +133,22 @@
     ]
     for copy in copies:
         copy.start()
+    same_ref[...] = second_ref[...]
     for copy in copies:
         copy.wait()
 
 
-def load_call(order, down):
+def load_call(order, down, second):
     return order.call(
         load_kernel,
         "load_matrix",
-        [in_hbm(down)],
-        [ANY],
-        [pltpu.VMEM(down.shape, down.dtype)],
-        [VMEM],
+        [in_hbm(down), second],
+        [ANY, VMEM],
+        [pltpu.VMEM(down.shape, down.dtype), (second.shape, second.dtype)],
+        [VMEM, VMEM],
         grid=(),
         scratch=[pltpu.SemaphoreType.DMA((4,))],
-    )[0]
+    )
 
 
 def expert_rows_kernel(slots, tiles, shares, batch, route_row, at_ref, *rest):
@@ -499,6 +498,7 @@
         [((pairs, units), BF16), ((toks, top), F32)],
         [rows(pairs, units), rows(toks, top)],
         grid=(steps,),
+        cost=LONG,
         scratch=[pltpu.VMEM((count * both, units), BF16), pltpu.VMEM((toks, 2 * count), F32)],
     )
 
@@ -530,7 +530,7 @@
     def exchange(x, axes="ep"):
         return lax.all_to_all(x, axes, split_axis=0, concat_axis=0, tiled=True)
 
-    blocks = {0: pack_call(order, grad, first[0], index)}
+    blocks = {0: pack_call(order, grad, first[0].T, index.T)}
 
     def fetch(o):
         if o not in blocks:
@@ -538,11 +538,12 @@
             blocks[o] = flip(fetch(o ^ last), last)
         return blocks[o]
 
-    downs = [load_call(order, down[0]), swap(down[0])]
-    seconds = [second[0], swap(second[0])]
+    own_down, own_second = load_call(order, down[0], second[0])
+    downs = [own_down, swap(down[0])]
+    seconds = [own_second, swap(own_second)]
 
     if groups == 8:
-        batches = [(0, 1), (2, 4), (3, 6), (5, 7)]
+        batches = [(0, 1), (2, 4), (6, 5), (3, 7)]
     else:
         batches = [(o, o + 1) for o in range(0, groups, 2)]
     places = [o for batch in batches for o in batch]
@@ -553,15 +554,19 @@
 
     def send_back(batch, parts):
         for o, rows in zip(batch, share_sum_call(order, parts, 2, slots)):
-            back[o] = flip(rows, o) if o else rows
+            if batch == batches[-1] and o > 1 and o % 2:
+                back[o] = flip(flip(rows, 1), o - 1)
+            else:
+                back[o] = flip(rows, o) if o else rows
 
     for i, batch in enumerate(batches):
         *give, keep, low = expert_rows_call(
             order, [fetch(o) for o in batch], seconds, downs, shares, slots
         )
         lows.append(low)
-        if i > 1:
-            arrived(i - 2)
+        if i > 1 and i == len(batches) - 1:
+            for j in range(i - 1):
+                arrived(j)
         if i > 0:
             send_back(*waiting)
         waiting = (batch, [keep] + [turn(x, k + 1) for k, x in enumerate(give)])
@@ -572,11 +577,11 @@
     low_grad, first_own = collect_call(order, places, lows, grads, feats)
     firsts = [x.reshape(groups * rank, units) for x in (first_own, swap(first_own))]
     low_grad = all_shares(exchange(low_grad))
+    send_back(*waiting)
+
+    low_grad = low_dense_call(order, low_grad)
     arrived(len(batches) - 2)
-    send_back(*waiting)
     low_hid = all_shares(lowrank_hid_call(order, index, hid, firsts, groups))
-
-    low_grad = low_dense_call(order, low_grad)
     first_part = first_grad_call(order, index, weight, low_grad, hid, groups)
     first_part = exchange(first_part, ("ep", "sub"))
     first_grad = jnp.sum(first_part.astype(F32), axis=0)

time: 223 us -> 208 us (0.933)
  waiting for transfers between devices: 96.2 us -> 85.6 us
  blocking collectives: 12.3 us -> 9.38 us
    ppermute x14 -> x16, waiting for transfers between devices: 84.8 us -> 59.4 us  [flip(): return lax.ppermute(x, 'ep', [(i, i ^ mask) for i in range(groups)])]
    all_to_all x2, waiting for transfers between devices: 0.01 us -> 13.8 us  [exchange(): return lax.all_to_all(x, axes, split_axis=0, concat_axis=0, tiled=True)]
    ppermute x7, starting transfers between devices: 10 us -> 6.99 us  [turn(): lax.ppermute(x, 'rep', [(r, (r + offset) % shares) for r in range(shares)])]
    all_to_all x1, blocking collectives: 12.3 us -> 9.38 us  [exchange(): return lax.all_to_all(x, axes, split_axis=0, concat_axis=0, tiled=True)]
    ppermute x14 -> x16, starting transfers between devices: 19.8 us -> 21.1 us  [flip(): return lax.ppermute(x, 'ep', [(i, i ^ mask) for i in range(groups)])]
    unnamed x48 -> x53, local copies, waits for them, and re-layouts: 5.93 us -> 6.31 us
  transfers between devices with their start and end apart: 27 -> 29, of which waited for: 9 -> 12; matrix products, arithmetic and copies ran while one was open for 2% -> 1% of each run, Pallas kernels for 27% -> 27%
where the time goes in v9:
time: 208 us
  waiting for transfers between devices  85.6 us (41%)
  Pallas kernels  63.6 us (31%)
  starting transfers between devices  40.1 us (19%)
  blocking collectives  9.38 us (5%)
  local copies, waits for them, and re-layouts  6.31 us (3%)
    pallas_call x17, Pallas kernels, call(): pl.pallas_call(ordered, grid=grid, in_specs=[SMEM, *in_specs] + [ANY] * l...  63.6 us
    ppermute x16, waiting for transfers between devices, flip(): return lax.ppermute(x, 'ep', [(i, i ^ mask) for i in range(groups)])  59.4 us
    ppermute x16, starting transfers between devices, flip(): return lax.ppermute(x, 'ep', [(i, i ^ mask) for i in range(groups)])  21.1 us
    all_to_all x2, waiting for transfers between devices, exchange(): return lax.all_to_all(x, axes, split_axis=0, concat_axis=0, tiled=True)  13.8 us
    all_to_all x2, starting transfers between devices, exchange(): return lax.all_to_all(x, axes, split_axis=0, concat_axis=0, tiled=True)  11.8 us
    ppermute x7, waiting for transfers between devices, turn(): lax.ppermute(x, 'rep', [(r, (r + offset) % shares) for r in range(shares)])  11.1 us
    all_to_all x1, blocking collectives, exchange(): return lax.all_to_all(x, axes, split_axis=0, concat_axis=0, tiled=True)  9.38 us
    ppermute x7, starting transfers between devices, turn(): lax.ppermute(x, 'rep', [(r, (r + offset) % shares) for r in range(shares)])  6.99 us
  transfers between devices with their start and end apart: 29, of which 12 were waited for; matrix products, arithmetic and copies ran while one was open for 1% of the time, Pallas kernels for 27%

profile of v9, /device:TPU:8, one launch (start us, length us, event | category | flops | bytes accessed | tf_op | source)
XLA Modules:
  0.0 207.5 jit_solution(13180789081845703042)
XLA Ops:
  0.8 0.8 copy-done.16
  1.6 0.7 copy-done.17
  2.3 1.1 pack_block.1
  3.4 2.7 %collective-permute-start.4 = (bf16[128,2304]{1,0:T(8,128)(2,1)S(1)}, bf16[128,2304]{1,0:T(8,128)(2,1)S(1)}, u32[]{:S(2)}, u32[]{:S(2)}) collective-permute-start(bf16[128,2304]{1,0:T(8,128)(2,1)S(1)} %get-tuple-element.53.refs_1_.refs_5_.refs_2_), channel_id=1, source_target_pairs={{0,16},{4,20},{8,24},{12,28},{16,0},{20,4},{24,8},{28,12},{1,17},{... | collective-permute-start | bytes 1769480 | tf_op jit(solution)/shard_map/ppermute | solution.py:525
  6.0 1.5 collective-permute-start
  7.6 0.4 collective-permute-start.3
  8.0 23.9 %collective-permute-done.4.refs_2_.refs_8_.refs_5_ = bf16[128,2304]{1,0:T(8,128)(2,1)S(1)} collective-permute-done((bf16[128,2304]{1,0:T(8,128)(2,1)S(1)}, bf16[128,2304]{1,0:T(8,128)(2,1)S(1)}, u32[]{:S(2)}, u32[]{:S(2)}) %collective-permute-start.4) | collective-permute-done | bytes 589856 | tf_op jit(solution)/shard_map/ppermute | solution.py:525
  31.9 1.3 collective-permute-start.5
  33.2 0.9 copy-done.15
  34.1 3.4 %load_matrix.1 = (bf16[1536,2048]{1,0:T(8,128)(2,1)S(1)}, bf16[32,2048]{1,0:T(8,128)(2,1)S(1)}, f32[8,128]{1,0:T(8,128)}) custom-call(s32[3]{0:T(128)S(1)} %pad_add_fusion.refs_0_, bf16[1536,2048]{1,0:T(8,128)(2,1)} %bitcast.29, bf16[32,2048]{1,0:T(8,128)(2,1)S(1)} %bitcast.22, f32[8,128]{1,0:T(8,128)} %get-tuple-element.54.refs_3_), custom_call_target="tpu_custom_call" | custom-call | flops 1 | bytes 1 | tf_op jit(solution)/shard_map/load_matrix/pallas_call | solution.py:53
  37.6 1.3 collective-permute-done.1.refs_4_
  39.0 1.6 collective-permute-start.6
  40.5 8.1 %expert_rows.4 = (bf16[320,768]{1,0:T(8,128)(2,1)S(1)}, bf16[320,768]{1,0:T(8,128)(2,1)S(1)}, bf16[2,64,128]{2,1,0:T(8,128)(2,1)S(1)}, f32[8,128]{1,0:T(8,128)}) custom-call(s32[3]{0:T(128)S(1)} %pad_add_fusion.refs_0_, bf16[128,2304]{1,0:T(8,128)(2,1)S(1)} %get-tuple-element.53.refs_1_.refs_5_.refs_2_, ...), custom_call_target="tpu_custom_call" | custom-call | flops 1 | bytes 1 | tf_op jit(solution)/shard_map/expert_rows/pallas_call | solution.py:53
  48.7 1.6 collective-permute-start.7
  50.2 0.5 collective-permute-start.8
  50.7 7.9 %expert_rows.5 = (bf16[320,768]{1,0:T(8,128)(2,1)S(1)}, bf16[320,768]{1,0:T(8,128)(2,1)S(1)}, bf16[2,64,128]{2,1,0:T(8,128)(2,1)S(1)}, f32[8,128]{1,0:T(8,128)}) custom-call(s32[3]{0:T(128)S(1)} %pad_add_fusion.refs_0_, bf16[128,2304]{1,0:T(8,128)(2,1)S(1)} %collective-permute-done.3.refs_1_.refs_7_.refs_4_, ...), custom_call_target="tpu_custom_call" | custom-call | flops 1 | bytes 1 | tf_op jit(solution)/shard_map/expert_rows/pallas_call | solution.py:53
  58.6 0.6 collective-permute-start.10
  59.2 1.6 collective-permute-start.9
  60.7 2.1 %collective-permute-done.7.refs_2_ = bf16[320,768]{1,0:T(8,128)(2,1)S(1)} collective-permute-done((bf16[320,768]{1,0:T(8,128)(2,1)S(1)}, bf16[320,768]{1,0:T(8,128)(2,1)S(1)}, u32[]{:S(2)}, u32[]{:S(2)}) %collective-permute-start.7) | collective-permute-done | bytes 491552 | tf_op jit(solution)/shard_map/ppermute | solution.py:519
  62.8 0.7 share_sum.4
  63.5 0.7 copy-done.14
  64.2 8.3 %expert_rows.6 = (bf16[320,768]{1,0:T(8,128)(2,1)S(1)}, bf16[320,768]{1,0:T(8,128)(2,1)S(1)}, bf16[2,64,128]{2,1,0:T(8,128)(2,1)S(1)}, f32[8,128]{1,0:T(8,128)}) custom-call(s32[3]{0:T(128)S(1)} %pad_add_fusion.refs_0_, bf16[128,2304]{1,0:T(8,128)(2,1)S(1)} %collective-permute-done.5.refs_1_.refs_9_.refs_6_, ...), custom_call_target="tpu_custom_call" | custom-call | flops 1 | bytes 1 | tf_op jit(solution)/shard_map/expert_rows/pallas_call | solution.py:53
  72.5 1.6 collective-permute-start.11
  74.0 0.7 share_sum.5
  74.7 0.7 collective-permute-start.13
  75.3 3.3 %collective-permute-start.14 = (bf16[160,768]{1,0:T(8,128)(2,1)S(1)}, bf16[160,768]{1,0:T(8,128)(2,1)S(1)}, u32[]{:S(2)}, u32[]{:S(2)}) collective-permute-start(bf16[160,768]{1,0:T(8,128)(2,1)S(1)} %get-tuple-element.76), channel_id=1, source_target_pairs={{0,16},{4,20},{8,24},{12,28},{16,0},{20,4},{24,8},{28,12},{1,17},{... | collective-permute-start | bytes 737288 | tf_op jit(solution)/shard_map/ppermute | solution.py:525
  78.7 0.6 collective-permute-start.12
  79.3 1.1 collective-permute-done.9.refs_2_.refs_12_.refs_9_
  80.4 8.7 %expert_rows.7 = (bf16[320,768]{1,0:T(8,128)(2,1)}, bf16[320,768]{1,0:T(8,128)(2,1)S(1)}, bf16[2,64,128]{2,1,0:T(8,128)(2,1)S(1)}, f32[8,128]{1,0:T(8,128)}) custom-call(s32[3]{0:T(128)S(1)} %pad_add_fusion.refs_0_, bf16[128,2304]{1,0:T(8,128)(2,1)S(1)} %collective-permute-done.8.refs_1_.refs_11_.refs_8_, ...), custom_call_target="tpu_custom_call" | custom-call | flops 1 | bytes 1 | tf_op jit(solution)/shard_map/expert_rows/pallas_call | solution.py:53
  89.2 1.6 collective-permute-start.16
  90.9 1.4 share_sum.6
  92.2 1.7 collect_blocks.1
  94.0 6.2 %all-to-all-start = ((bf16[8,64,128]{2,1,0:T(8,128)(2,1)}), bf16[8,64,128]{2,1,0:T(8,128)(2,1)S(1)}, u32[]{:S(2)}, u32[]{:S(2)}) async-start(bf16[8,64,128]{2,1,0:T(8,128)(2,1)} %get-tuple-element.78), calls=%async_computation | async-start | bytes 262144 | tf_op jit(solution)/shard_map/all_to_all | solution.py:531
  100.2 3.3 %collective-permute-start.20 = (bf16[160,768]{1,0:T(8,128)(2,1)}, bf16[160,768]{1,0:T(8,128)(2,1)S(1)}, u32[]{:S(2)}, u32[]{:S(2)}) collective-permute-start(bf16[160,768]{1,0:T(8,128)(2,1)} %get-tuple-element.87), channel_id=1, source_target_pairs={{0,20},{4,16},{8,28},{12,24},{16,4},{20,0},{24,12},{28,8},{1,21},{... | collective-permute-start | bytes 737288 | tf_op jit(solution)/shard_map/ppermute | solution.py:525
  103.5 13.8 %all-to-all-done.refs_1_ = bf16[8,64,128]{2,1,0:T(8,128)(2,1)S(1)} async-done(((bf16[8,64,128]{2,1,0:T(8,128)(2,1)}), bf16[8,64,128]{2,1,0:T(8,128)(2,1)S(1)}, u32[]{:S(2)}, u32[]{:S(2)}) %all-to-all-start) | async-done | bytes 131104 | tf_op jit(solution)/shard_map/all_to_all | solution.py:531
  117.3 0.5 collective-permute-start.15
  117.9 0.7 share_sum.7
  118.6 0.7 copy-done.19
  119.3 3.0 %collective-permute-done.15.refs_2_ = bf16[8,64,128]{2,1,0:T(8,128)(2,1)S(1)} collective-permute-done((bf16[8,64,128]{2,1,0:T(8,128)(2,1)S(1)}, bf16[8,64,128]{2,1,0:T(8,128)(2,1)S(1)}, u32[]{:S(2)}, u32[]{:S(2)}) %collective-permute-start.15) | collective-permute-done | bytes 131104 | tf_op jit(solution)/shard_map/ppermute | solution.py:519
  122.2 0.7 low_dense.1
  122.9 3.6 %collective-permute-done.21.refs_6_.refs_14_ = bf16[160,768]{1,0:T(8,128)(2,1)S(1)} collective-permute-done((bf16[160,768]{1,0:T(8,128)(2,1)}, bf16[160,768]{1,0:T(8,128)(2,1)S(1)}, u32[]{:S(2)}, u32[]{:S(2)}) %collective-permute-start.21) | collective-permute-done | bytes 245792 | tf_op jit(solution)/shard_map/ppermute | solution.py:525
  126.6 3.6 %lowrank_hid.1 = (f32[128,512]{1,0:T(8,128)S(1)}, f32[8,128]{1,0:T(8,128)}) custom-call(s32[3]{0:T(128)S(1)} %pad_add_fusion.refs_0_, s32[128,8]{1,0:T(8,128)S(1)} %copy.16.refs_1_.refs_2_, bf16[1024,768]{1,0:T(8,128)(2,1)} %bitcast.25, bf16[256,768]{1,0:T(8,128)(2,1)S(1)} %bitcast.18, bf16[256,768]{1,0:T(8,128)(2,1)S(1)} %bitcast.20, ...), custom_call_target="tpu_custom_call" | custom-call | flops 1 | bytes 1 | tf_op jit(solution)/shard_map/lowrank_hid/pallas_call | solution.py:53
  130.2 0.6 collective-permute-start.24
  130.8 0.1 copy.18.refs_2_.refs_3_
  131.0 4.2 %first_grad.1 = (bf16[16,32,768]{2,1,0:T(8,128)(2,1)S(1)}, f32[8,128]{1,0:T(8,128)}) custom-call(s32[3]{0:T(128)S(1)} %pad_add_fusion.refs_0_, s32[128,8]{1,0:T(8,128)S(1)} %copy.16.refs_1_.refs_2_, bf16[128,8]{1,0:T(8,128)(2,1)S(1)} %copy.18.refs_2_.refs_3_, f32[128,512]{1,0:T(8,128)S(1)} %get-tuple-element.83.refs_3_.refs_4_, bf16[1024,768]{1,0:T(8,128)(2,1)} %bitcast.26, ...), custom_call_target="tpu_custom_call" | custom-call | flops 1 | bytes 1 | tf_op jit(solution)/shard_map/first_grad/pallas_call | solution.py:53
  135.2 0.9 copy-done.13
  136.1 2.1 %collective-permute-done.24.refs_4_ = f32[128,512]{1,0:T(8,128)S(1)} collective-permute-done((f32[128,512]{1,0:T(8,128)S(1)}, f32[128,512]{1,0:T(8,128)S(1)}, u32[]{:S(2)}, u32[]{:S(2)}) %collective-permute-start.24) | collective-permute-done | bytes 262176 | tf_op jit(solution)/shard_map/ppermute | solution.py:519
  138.3 1.0 scaled_hid.1
  139.2 9.4 %all_to_all.15.refs_1_ = bf16[8,64,128]{2,1,0:T(8,128)(2,1)S(1)} all-to-all(bf16[8,64,128]{2,1,0:T(8,128)(2,1)S(1)} %get-tuple-element.98), channel_id=1, replica_groups=mesh['grp'=1,'ep'=8,'rep'=2,'sub'=2] {'ep'}, dimensions={0} | all-to-all | bytes 262144 | tf_op jit(solution)/shard_map/all_to_all | solution.py:531
  148.6 5.6 %all-to-all-start.1 = ((bf16[16,32,768]{2,1,0:T(8,128)(2,1)}), bf16[16,32,768]{2,1,0:T(8,128)(2,1)S(1)}, u32[]{:S(2)}, u32[]{:S(2)}) async-start(bf16[16,32,768]{2,1,0:T(8,128)(2,1)} %copy-done.13), calls=%async_computation.1 | async-start | bytes 1572864 | tf_op jit(solution)/shard_map/all_to_all | solution.py:531
  154.2 1.5 collective-permute-start.18
  155.7 0.5 collective-permute-start.22
  156.3 13.7 %collective-permute-done.18 = bf16[160,768]{1,0:T(8,128)(2,1)S(1)} collective-permute-done((bf16[160,768]{1,0:T(8,128)(2,1)}, bf16[160,768]{1,0:T(8,128)(2,1)S(1)}, u32[]{:S(2)}, u32[]{:S(2)}) %collective-permute-start.18) | collective-permute-done | bytes 245792 | tf_op jit(solution)/shard_map/ppermute | solution.py:525
  170.0 5.8 %collective-permute-done.22 = bf16[160,768]{1,0:T(8,128)(2,1)S(1)} collective-permute-done((bf16[160,768]{1,0:T(8,128)(2,1)S(1)}, bf16[160,768]{1,0:T(8,128)(2,1)S(1)}, u32[]{:S(2)}, u32[]{:S(2)}) %collective-permute-start.22) | collective-permute-done | bytes 245792 | tf_op jit(solution)/shard_map/ppermute | solution.py:525
  175.8 1.5 collective-permute-start.23
  177.3 11.3 %collective-permute-done.23.refs_15_ = bf16[160,768]{1,0:T(8,128)(2,1)S(1)} collective-permute-done((bf16[160,768]{1,0:T(8,128)(2,1)S(1)}, bf16[160,768]{1,0:T(8,128)(2,1)S(1)}, u32[]{:S(2)}, u32[]{:S(2)}) %collective-permute-start.23) | collective-permute-done | bytes 245792 | tf_op jit(solution)/shard_map/ppermute | solution.py:525
  188.6 0.7 copy-done.23
  189.3 7.8 %finish.1 = (bf16[1024,768]{1,0:T(8,128)(2,1)}, f32[128,8]{1,0:T(8,128)S(1)}, f32[8,128]{1,0:T(8,128)}) custom-call(s32[3]{0:T(128)S(1)} %pad_add_fusion.refs_0_, s32[128,8]{1,0:T(8,128)S(1)} %copy.16.refs_1_.refs_2_, s32[128,8]{1,0:T(8,128)S(1)} %copy.16.refs_1_.refs_2_, bf16[128,8]{1,0:T(8,128)(2,1)S(1)} %copy.18.refs_2_.refs_3_, ...), custom_call_target="tpu_custom_call" | custom-call | flops 1 | bytes 20000000 | tf_op jit(solution)/shard_map/finish/pallas_call | solution.py:53
  197.1 3.7 %second_grad.1 = (f32[32,2048]{1,0:T(8,128)S(1)}, f32[32,2048]{1,0:T(8,128)S(1)}, f32[8,128]{1,0:T(8,128)}) custom-call(s32[3]{0:T(128)S(1)} %pad_add_fusion.refs_0_, bf16[8,64,128]{2,1,0:T(8,128)(2,1)S(1)} %all_to_all.15.refs_1_, bf16[128,2304]{1,0:T(8,128)(2,1)} %copy-done, bf16[128,2304]{1,0:T(8,128)(2,1)} %copy-done.2, bf16[128,2304]{1,0:T(8,128)(2,1)} %copy-done.3, ...), custom_call_target="tpu_custom_call" | custom-call | flops 1 | bytes 1 | tf_op jit(solution)/shard_map/second_grad/pallas_call | solution.py:53
  200.9 0.6 collective-permute-start.25
  201.5 3.9 %collective-permute-done.25 = f32[128,8]{1,0:T(8,128)S(1)} collective-permute-done((f32[128,8]{1,0:T(8,128)S(1)}, f32[128,8]{1,0:T(8,128)S(1)}, u32[]{:S(2)}, u32[]{:S(2)}) %collective-permute-start.25) | collective-permute-done | bytes 4128 | tf_op jit(solution)/shard_map/ppermute | solution.py:519
  205.4 0.7 copy.19
  206.0 0.7 convert_reduce_fusion
  206.8 0.7 add_bitcast_fusion
  (69 shorter events, 0.5 us)
Async XLA Ops:
  0.6 39.9 %collective-permute-start.2 = (bf16[1536,2048]{1,0:T(8,128)(2,1)}, bf16[1536,2048]{1,0:T(8,128)(2,1)}, u32[]{:S(2)}, u32[]{:S(2)}) collective-permute-start(bf16[1536,2048]{1,0:T(8,128)(2,1)} %bitcast.28), channel_id=1, source_target_pairs={{0,1},{1,0},{2,3},{3,2},{4,5},{5,4},{6,7},{7,6},{8,9},{9,8},{10,11... | collective-permute-start | bytes 18874376 | tf_op jit(solution)/shard_map/ppermute | solution.py:528
  0.8 0.8 copy-start.16
  1.6 0.7 copy-start.17
  3.4 45.3 %copy-start = (bf16[128,2304]{1,0:T(8,128)(2,1)}, bf16[128,2304]{1,0:T(8,128)(2,1)S(1)}, u32[]{:S(2)}) copy-start(bf16[128,2304]{1,0:T(8,128)(2,1)S(1)} %get-tuple-element.53.refs_1_.refs_5_.refs_2_) | copy-start | bytes 1769476
  3.4 28.5 %collective-permute-start.4 = (bf16[128,2304]{1,0:T(8,128)(2,1)S(1)}, bf16[128,2304]{1,0:T(8,128)(2,1)S(1)}, u32[]{:S(2)}, u32[]{:S(2)}) collective-permute-start(bf16[128,2304]{1,0:T(8,128)(2,1)S(1)} %get-tuple-element.53.refs_1_.refs_5_.refs_2_), channel_id=1, source_target_pairs={{0,16},{4,20},{8,24},{12,28},{16,0},{20,4},{24,8},{28,12},{1,17},{... | collective-permute-start | bytes 1769480 | tf_op jit(solution)/shard_map/ppermute | solution.py:525
  6.0 34.5 %collective-permute-start = (bf16[128,2304]{1,0:T(8,128)(2,1)S(1)}, bf16[128,2304]{1,0:T(8,128)(2,1)S(1)}, u32[]{:S(2)}, u32[]{:S(2)}) collective-permute-start(bf16[128,2304]{1,0:T(8,128)(2,1)S(1)} %get-tuple-element.53.refs_1_.refs_5_.refs_2_), channel_id=1, source_target_pairs={{0,4},{4,0},{8,12},{12,8},{16,20},{20,16},{24,28},{28,24},{1,5},{5... | collective-permute-start | bytes 1769480 | tf_op jit(solution)/shard_map/ppermute | solution.py:525
  7.6 42.6 %collective-permute-start.3 = (bf16[128,2304]{1,0:T(8,128)(2,1)S(1)}, bf16[128,2304]{1,0:T(8,128)(2,1)S(1)}, u32[]{:S(2)}, u32[]{:S(2)}) collective-permute-start(bf16[128,2304]{1,0:T(8,128)(2,1)S(1)} %get-tuple-element.53.refs_1_.refs_5_.refs_2_), channel_id=1, source_target_pairs={{0,8},{4,12},{8,0},{12,4},{16,24},{20,28},{24,16},{28,20},{1,9},{5... | collective-permute-start | bytes 1769480 | tf_op jit(solution)/shard_map/ppermute | solution.py:525
  31.9 18.8 %copy-start.1 = (bf16[128,2304]{1,0:T(8,128)(2,1)}, bf16[128,2304]{1,0:T(8,128)(2,1)S(1)}, u32[]{:S(2)}) copy-start(bf16[128,2304]{1,0:T(8,128)(2,1)S(1)} %collective-permute-done.4.refs_2_.refs_8_.refs_5_) | copy-start | bytes 1769476
  31.9 27.3 %collective-permute-start.5 = (bf16[128,2304]{1,0:T(8,128)(2,1)S(1)}, bf16[128,2304]{1,0:T(8,128)(2,1)S(1)}, u32[]{:S(2)}, u32[]{:S(2)}) collective-permute-start(bf16[128,2304]{1,0:T(8,128)(2,1)S(1)} %collective-permute-done.4.refs_2_.refs_8_.refs_5_), channel_id=1, source_target_pairs={{0,8},{4,12},{8,0},{12,4},{16,24},{20,28},{24,16},{28,20},{1,9},{5... | collective-permute-start | bytes 1769480 | tf_op jit(solution)/shard_map/ppermute | solution.py:525
  33.2 0.9 copy-start.15
  37.5 1.4 collective-permute-start.1
  39.0 25.2 %collective-permute-start.6 = (bf16[128,2304]{1,0:T(8,128)(2,1)S(1)}, bf16[128,2304]{1,0:T(8,128)(2,1)S(1)}, u32[]{:S(2)}, u32[]{:S(2)}) collective-permute-start(bf16[128,2304]{1,0:T(8,128)(2,1)S(1)} %collective-permute-done.4.refs_2_.refs_8_.refs_5_), channel_id=1, source_target_pairs={{0,4},{4,0},{8,12},{12,8},{16,20},{20,16},{24,28},{28,24},{1,5},{5... | collective-permute-start | bytes 1769480 | tf_op jit(solution)/shard_map/ppermute | solution.py:525
  40.5 8.1 %copy-start.2 = (bf16[128,2304]{1,0:T(8,128)(2,1)}, bf16[128,2304]{1,0:T(8,128)(2,1)S(1)}, u32[]{:S(2)}) copy-start(bf16[128,2304]{1,0:T(8,128)(2,1)S(1)} %collective-permute-done.refs_2_.refs_6_.refs_3_) | copy-start | bytes 1769476
  48.7 14.2 %collective-permute-start.7 = (bf16[320,768]{1,0:T(8,128)(2,1)S(1)}, bf16[320,768]{1,0:T(8,128)(2,1)S(1)}, u32[]{:S(2)}, u32[]{:S(2)}) collective-permute-start(bf16[320,768]{1,0:T(8,128)(2,1)S(1)} %get-tuple-element.62), channel_id=1, source_target_pairs={{0,2},{2,0},{1,3},{3,1},{4,6},{6,4},{5,7},{7,5},{8,10},{10,8},{9,1... | collective-permute-start | bytes 1474568 | tf_op jit(solution)/shard_map/ppermute | solution.py:519
  50.2 8.4 %copy-start.3 = (bf16[128,2304]{1,0:T(8,128)(2,1)}, bf16[128,2304]{1,0:T(8,128)(2,1)S(1)}, u32[]{:S(2)}) copy-start(bf16[128,2304]{1,0:T(8,128)(2,1)S(1)} %collective-permute-done.3.refs_1_.refs_7_.refs_4_) | copy-start | bytes 1769476
  50.2 28.5 %collective-permute-start.8 = (bf16[128,2304]{1,0:T(8,128)(2,1)S(1)}, bf16[128,2304]{1,0:T(8,128)(2,1)S(1)}, u32[]{:S(2)}, u32[]{:S(2)}) collective-permute-start(bf16[128,2304]{1,0:T(8,128)(2,1)S(1)} %collective-permute-done.3.refs_1_.refs_7_.refs_4_), channel_id=1, source_target_pairs={{0,4},{4,0},{8,12},{12,8},{16,20},{20,16},{24,28},{28,24},{1,5},{5... | collective-permute-start | bytes 1769480 | tf_op jit(solution)/shard_map/ppermute | solution.py:525
  58.6 15.4 %collective-permute-start.10 = (bf16[320,768]{1,0:T(8,128)(2,1)S(1)}, bf16[320,768]{1,0:T(8,128)(2,1)S(1)}, u32[]{:S(2)}, u32[]{:S(2)}) collective-permute-start(bf16[320,768]{1,0:T(8,128)(2,1)S(1)} %get-tuple-element.67), channel_id=1, source_target_pairs={{0,2},{2,0},{1,3},{3,1},{4,6},{6,4},{5,7},{7,5},{8,10},{10,8},{9,1... | collective-permute-start | bytes 1474568 | tf_op jit(solution)/shard_map/ppermute | solution.py:519
  59.2 13.3 %copy-start.4 = (bf16[128,2304]{1,0:T(8,128)(2,1)}, bf16[128,2304]{1,0:T(8,128)(2,1)S(1)}, u32[]{:S(2)}) copy-start(bf16[128,2304]{1,0:T(8,128)(2,1)S(1)} %collective-permute-done.5.refs_1_.refs_9_.refs_6_) | copy-start | bytes 1769476
  59.2 21.2 %collective-permute-start.9 = (bf16[128,2304]{1,0:T(8,128)(2,1)S(1)}, bf16[128,2304]{1,0:T(8,128)(2,1)S(1)}, u32[]{:S(2)}, u32[]{:S(2)}) collective-permute-start(bf16[128,2304]{1,0:T(8,128)(2,1)S(1)} %collective-permute-done.5.refs_1_.refs_9_.refs_6_), channel_id=1, source_target_pairs={{0,4},{4,0},{8,12},{12,8},{16,20},{20,16},{24,28},{28,24},{1,5},{5... | collective-permute-start | bytes 1769480 | tf_op jit(solution)/shard_map/ppermute | solution.py:525
  63.5 0.7 copy-start.14
  64.2 8.3 %copy-start.5 = (bf16[128,2304]{1,0:T(8,128)(2,1)}, bf16[128,2304]{1,0:T(8,128)(2,1)S(1)}, u32[]{:S(2)}) copy-start(bf16[128,2304]{1,0:T(8,128)(2,1)S(1)} %collective-permute-done.6.refs_2_.refs_10_.refs_7_) | copy-start | bytes 1769476
  72.5 18.4 %collective-permute-start.11 = (bf16[320,768]{1,0:T(8,128)(2,1)S(1)}, bf16[320,768]{1,0:T(8,128)(2,1)S(1)}, u32[]{:S(2)}, u32[]{:S(2)}) collective-permute-start(bf16[320,768]{1,0:T(8,128)(2,1)S(1)} %get-tuple-element.72), channel_id=1, source_target_pairs={{0,2},{2,0},{1,3},{3,1},{4,6},{6,4},{5,7},{7,5},{8,10},{10,8},{9,1... | collective-permute-start | bytes 1474568 | tf_op jit(solution)/shard_map/ppermute | solution.py:519
  74.7 16.1 %collective-permute-start.13 = (bf16[160,768]{1,0:T(8,128)(2,1)S(1)}, bf16[160,768]{1,0:T(8,128)(2,1)S(1)}, u32[]{:S(2)}, u32[]{:S(2)}) collective-permute-start(bf16[160,768]{1,0:T(8,128)(2,1)S(1)} %get-tuple-element.75), channel_id=1, source_target_pairs={{0,8},{4,12},{8,0},{12,4},{16,24},{20,28},{24,16},{28,20},{1,9},{5... | collective-permute-start | bytes 737288 | tf_op jit(solution)/shard_map/ppermute | solution.py:525
  75.3 15.5 %collective-permute-start.14 = (bf16[160,768]{1,0:T(8,128)(2,1)S(1)}, bf16[160,768]{1,0:T(8,128)(2,1)S(1)}, u32[]{:S(2)}, u32[]{:S(2)}) collective-permute-start(bf16[160,768]{1,0:T(8,128)(2,1)S(1)} %get-tuple-element.76), channel_id=1, source_target_pairs={{0,16},{4,20},{8,24},{12,28},{16,0},{20,4},{24,8},{28,12},{1,17},{... | collective-permute-start | bytes 737288 | tf_op jit(solution)/shard_map/ppermute | solution.py:525
  78.7 10.5 %copy-start.6 = (bf16[128,2304]{1,0:T(8,128)(2,1)}, bf16[128,2304]{1,0:T(8,128)(2,1)S(1)}, u32[]{:S(2)}) copy-start(bf16[128,2304]{1,0:T(8,128)(2,1)S(1)} %collective-permute-done.8.refs_1_.refs_11_.refs_8_) | copy-start | bytes 1769476
  78.7 12.1 %collective-permute-start.12 = (bf16[160,768]{1,0:T(8,128)(2,1)S(1)}, bf16[160,768]{1,0:T(8,128)(2,1)S(1)}, u32[]{:S(2)}, u32[]{:S(2)}) collective-permute-start(bf16[160,768]{1,0:T(8,128)(2,1)S(1)} %get-tuple-element.74), channel_id=1, source_target_pairs={{0,4},{4,0},{8,12},{12,8},{16,20},{20,16},{24,28},{28,24},{1,5},{5... | collective-permute-start | bytes 737288 | tf_op jit(solution)/shard_map/ppermute | solution.py:525
  80.4 8.8 %copy-start.7 = (bf16[128,2304]{1,0:T(8,128)(2,1)}, bf16[128,2304]{1,0:T(8,128)(2,1)S(1)}, u32[]{:S(2)}) copy-start(bf16[128,2304]{1,0:T(8,128)(2,1)S(1)} %collective-permute-done.9.refs_2_.refs_12_.refs_9_) | copy-start | bytes 1769476
  89.2 28.6 %copy-start.18 = (s32[128,8]{0,1:T(8,128)S(1)}, s32[128,8]{0,1:T(8,128)}, u32[]{:S(2)}) copy-start(s32[128,8]{0,1:T(8,128)} %param.9) | copy-start | bytes 12292
  89.2 41.6 %copy-start.24 = (bf16[128,8]{0,1:T(8,128)(2,1)S(1)}, bf16[128,8]{0,1:T(8,128)(2,1)}, u32[]{:S(2)}) copy-start(bf16[128,8]{0,1:T(8,128)(2,1)} %param.10) | copy-start | bytes 6148
  89.2 28.7 %collective-permute-start.16 = (bf16[320,768]{1,0:T(8,128)(2,1)}, bf16[320,768]{1,0:T(8,128)(2,1)S(1)}, u32[]{:S(2)}, u32[]{:S(2)}) collective-permute-start(bf16[320,768]{1,0:T(8,128)(2,1)} %get-tuple-element.80), channel_id=1, source_target_pairs={{0,2},{2,0},{1,3},{3,1},{4,6},{6,4},{5,7},{7,5},{8,10},{10,8},{9,1... | collective-permute-start | bytes 1474568 | tf_op jit(solution)/shard_map/ppermute | solution.py:519
  90.8 44.4 %copy-start.8 = (bf16[160,768]{1,0:T(8,128)(2,1)}, bf16[160,768]{1,0:T(8,128)(2,1)S(1)}, u32[]{:S(2)}) copy-start(bf16[160,768]{1,0:T(8,128)(2,1)S(1)} %collective-permute-done.13.refs_5_.refs_10_) | copy-start | bytes 737284
  90.8 3.2 %copy-start.9 = (bf16[160,768]{1,0:T(8,128)(2,1)}, bf16[160,768]{1,0:T(8,128)(2,1)S(1)}, u32[]{:S(2)}) copy-start(bf16[160,768]{1,0:T(8,128)(2,1)S(1)} %collective-permute-done.14.refs_6_.refs_12_) | copy-start | bytes 737284
  90.8 44.4 %copy-start.10 = (bf16[160,768]{1,0:T(8,128)(2,1)}, bf16[160,768]{1,0:T(8,128)(2,1)S(1)}, u32[]{:S(2)}) copy-start(bf16[160,768]{1,0:T(8,128)(2,1)S(1)} %collective-permute-done.12.refs_4_.refs_9_) | copy-start | bytes 737284
  94.0 32.6 %collective-permute-start.17 = (bf16[8,32,768]{2,1,0:T(8,128)(2,1)S(1)}, bf16[8,32,768]{2,1,0:T(8,128)(2,1)S(1)}, u32[]{:S(2)}, u32[]{:S(2)}) collective-permute-start(bf16[8,32,768]{2,1,0:T(8,128)(2,1)S(1)} %get-tuple-element.84), channel_id=1, source_target_pairs={{0,1},{1,0},{2,3},{3,2},{4,5},{5,4},{6,7},{7,6},{8,9},{9,8},{10,11... | collective-permute-start | bytes 1179656 | tf_op jit(solution)/shard_map/ppermute | solution.py:528
  94.0 23.2 %all-to-all-start = ((bf16[8,64,128]{2,1,0:T(8,128)(2,1)}), bf16[8,64,128]{2,1,0:T(8,128)(2,1)S(1)}, u32[]{:S(2)}, u32[]{:S(2)}) async-start(bf16[8,64,128]{2,1,0:T(8,128)(2,1)} %get-tuple-element.78), calls=%async_computation | async-start | bytes 262144 | tf_op jit(solution)/shard_map/all_to_all | solution.py:531
  100.2 22.7 %collective-permute-start.20 = (bf16[160,768]{1,0:T(8,128)(2,1)}, bf16[160,768]{1,0:T(8,128)(2,1)S(1)}, u32[]{:S(2)}, u32[]{:S(2)}) collective-permute-start(bf16[160,768]{1,0:T(8,128)(2,1)} %get-tuple-element.87), channel_id=1, source_target_pairs={{0,20},{4,16},{8,28},{12,24},{16,4},{20,0},{24,12},{28,8},{1,21},{... | collective-permute-start | bytes 737288 | tf_op jit(solution)/shard_map/ppermute | solution.py:525
  103.5 23.1 %collective-permute-start.21 = (bf16[160,768]{1,0:T(8,128)(2,1)}, bf16[160,768]{1,0:T(8,128)(2,1)S(1)}, u32[]{:S(2)}, u32[]{:S(2)}) collective-permute-start(bf16[160,768]{1,0:T(8,128)(2,1)} %get-tuple-element.88), channel_id=1, source_target_pairs={{0,24},{4,28},{8,16},{12,20},{16,8},{20,12},{24,0},{28,4},{1,25},{... | collective-permute-start | bytes 737288 | tf_op jit(solution)/shard_map/ppermute | solution.py:525
  117.3 5.0 %collective-permute-start.15 = (bf16[8,64,128]{2,1,0:T(8,128)(2,1)S(1)}, bf16[8,64,128]{2,1,0:T(8,128)(2,1)S(1)}, u32[]{:S(2)}, u32[]{:S(2)}) collective-permute-start(bf16[8,64,128]{2,1,0:T(8,128)(2,1)S(1)} %all-to-all-done.refs_1_), channel_id=1, source_target_pairs={{0,2},{2,0},{1,3},{3,1},{4,6},{6,4},{5,7},{7,5},{8,10},{10,8},{9,1... | collective-permute-start | bytes 393224 | tf_op jit(solution)/shard_map/ppermute | solution.py:519
  118.6 0.7 copy-start.19
  119.3 11.0 %copy-start.21 = (bf16[160,768]{1,0:T(8,128)(2,1)}, bf16[160,768]{1,0:T(8,128)(2,1)S(1)}, u32[]{:S(2)}) copy-start(bf16[160,768]{1,0:T(8,128)(2,1)S(1)} %get-tuple-element.86) | copy-start | bytes 737284
  122.2 33.5 %copy-start.20 = (bf16[160,768]{1,0:T(8,128)(2,1)S(1)}, bf16[160,768]{1,0:T(8,128)(2,1)}, u32[]{:S(2)}) copy-start(bf16[160,768]{1,0:T(8,128)(2,1)} %copy-done.19) | copy-start | bytes 737284
  122.9 65.7 %copy-start.11 = (bf16[160,768]{1,0:T(8,128)(2,1)}, bf16[160,768]{1,0:T(8,128)(2,1)S(1)}, u32[]{:S(2)}) copy-start(bf16[160,768]{1,0:T(8,128)(2,1)S(1)} %collective-permute-done.20.refs_7_.refs_13_) | copy-start | bytes 737284
  126.6 62.0 %copy-start.12 = (bf16[160,768]{1,0:T(8,128)(2,1)}, bf16[160,768]{1,0:T(8,128)(2,1)S(1)}, u32[]{:S(2)}) copy-start(bf16[160,768]{1,0:T(8,128)(2,1)S(1)} %collective-permute-done.21.refs_6_.refs_14_) | copy-start | bytes 737284
  130.2 8.0 %collective-permute-start.24 = (f32[128,512]{1,0:T(8,128)S(1)}, f32[128,512]{1,0:T(8,128)S(1)}, u32[]{:S(2)}, u32[]{:S(2)}) collective-permute-start(f32[128,512]{1,0:T(8,128)S(1)} %get-tuple-element.91.refs_3_), channel_id=1, source_target_pairs={{0,2},{2,0},{1,3},{3,1},{4,6},{6,4},{5,7},{7,5},{8,10},{10,8},{9,1... | collective-permute-start | bytes 786440 | tf_op jit(solution)/shard_map/ppermute | solution.py:519
  135.2 0.9 copy-start.13
  148.6 48.5 %all-to-all-start.1 = ((bf16[16,32,768]{2,1,0:T(8,128)(2,1)}), bf16[16,32,768]{2,1,0:T(8,128)(2,1)S(1)}, u32[]{:S(2)}, u32[]{:S(2)}) async-start(bf16[16,32,768]{2,1,0:T(8,128)(2,1)} %copy-done.13), calls=%async_computation.1 | async-start | bytes 1572864 | tf_op jit(solution)/shard_map/all_to_all | solution.py:531
  154.2 15.8 %collective-permute-start.18 = (bf16[160,768]{1,0:T(8,128)(2,1)}, bf16[160,768]{1,0:T(8,128)(2,1)S(1)}, u32[]{:S(2)}, u32[]{:S(2)}) collective-permute-start(bf16[160,768]{1,0:T(8,128)(2,1)} %copy-done.21), channel_id=1, source_target_pairs={{0,4},{4,0},{8,12},{12,8},{16,20},{20,16},{24,28},{28,24},{1,5},{5... | collective-permute-start | bytes 737288 | tf_op jit(solution)/shard_map/ppermute | solution.py:525
  155.7 20.1 %collective-permute-start.22 = (bf16[160,768]{1,0:T(8,128)(2,1)S(1)}, bf16[160,768]{1,0:T(8,128)(2,1)S(1)}, u32[]{:S(2)}, u32[]{:S(2)}) collective-permute-start(bf16[160,768]{1,0:T(8,128)(2,1)S(1)} %copy-done.20), channel_id=1, source_target_pairs={{0,4},{4,0},{8,12},{12,8},{16,20},{20,16},{24,28},{28,24},{1,5},{5... | collective-permute-start | bytes 737288 | tf_op jit(solution)/shard_map/ppermute | solution.py:525
  170.0 7.3 %collective-permute-start.19 = (bf16[160,768]{1,0:T(8,128)(2,1)S(1)}, bf16[160,768]{1,0:T(8,128)(2,1)S(1)}, u32[]{:S(2)}, u32[]{:S(2)}) collective-permute-start(bf16[160,768]{1,0:T(8,128)(2,1)S(1)} %collective-permute-done.18), channel_id=1, source_target_pairs={{0,8},{4,12},{8,0},{12,4},{16,24},{20,28},{24,16},{28,20},{1,9},{5... | collective-permute-start | bytes 737288 | tf_op jit(solution)/shard_map/ppermute | solution.py:525
  175.8 12.8 %collective-permute-start.23 = (bf16[160,768]{1,0:T(8,128)(2,1)S(1)}, bf16[160,768]{1,0:T(8,128)(2,1)S(1)}, u32[]{:S(2)}, u32[]{:S(2)}) collective-permute-start(bf16[160,768]{1,0:T(8,128)(2,1)S(1)} %collective-permute-done.22), channel_id=1, source_target_pairs={{0,24},{4,28},{8,16},{12,20},{16,8},{20,12},{24,0},{28,4},{1,25},{... | collective-permute-start | bytes 737288 | tf_op jit(solution)/shard_map/ppermute | solution.py:525
  177.3 11.3 %copy-start.22 = (bf16[160,768]{1,0:T(8,128)(2,1)}, bf16[160,768]{1,0:T(8,128)(2,1)S(1)}, u32[]{:S(2)}) copy-start(bf16[160,768]{1,0:T(8,128)(2,1)S(1)} %collective-permute-done.19.refs_11_) | copy-start | bytes 737284
  188.6 0.7 copy-start.23
  200.8 6.0 %collective-permute-start.26 = (f32[32,2048]{1,0:T(8,128)S(1)}, f32[32,2048]{1,0:T(8,128)S(1)}, u32[]{:S(2)}, u32[]{:S(2)}) collective-permute-start(f32[32,2048]{1,0:T(8,128)S(1)} %get-tuple-element.101), channel_id=1, source_target_pairs={{0,1},{1,0},{2,3},{3,2},{4,5},{5,4},{6,7},{7,6},{8,9},{9,8},{10,11... | collective-permute-start | bytes 786440 | tf_op jit(solution)/shard_map/ppermute | solution.py:528
  200.9 4.5 %collective-permute-start.25 = (f32[128,8]{1,0:T(8,128)S(1)}, f32[128,8]{1,0:T(8,128)S(1)}, u32[]{:S(2)}, u32[]{:S(2)}) collective-permute-start(f32[128,8]{1,0:T(8,128)S(1)} %get-tuple-element.96), channel_id=1, source_target_pairs={{0,2},{2,0},{1,3},{3,1},{4,6},{6,4},{5,7},{7,5},{8,10},{10,8},{9,1... | collective-permute-start | bytes 12296 | tf_op jit(solution)/shard_map/ppermute | solution.py:519

commit v10 on v9

--- a/solution.py
+++ b/solution.py
@@ -14,7 +14,7 @@
 TN = (((0,), (0,)), ((), ()))
 NN = (((1,), (0,)), ((), ()))
 SMALL = pl.CostEstimate(flops=1, bytes_accessed=1, transcendentals=0)
-LONG = pl.CostEstimate(flops=1, bytes_accessed=2 * 10**7, transcendentals=0)
+LONG = pl.CostEstimate(flops=1, bytes_accessed=10**9, transcendentals=0)
 ANY = pl.BlockSpec(memory_space=pl.ANY)
 SMEM = pl.BlockSpec(memory_space=pltpu.SMEM)
 VMEM = pl.BlockSpec(memory_space=pltpu.VMEM)
@@ -579,9 +579,9 @@
     low_grad = all_shares(exchange(low_grad))
     send_back(*waiting)
 
-    low_grad = low_dense_call(order, low_grad)
     arrived(len(batches) - 2)
     low_hid = all_shares(lowrank_hid_call(order, index, hid, firsts, groups))
+    low_grad = low_dense_call(order, low_grad)
     first_part = first_grad_call(order, index, weight, low_grad, hid, groups)
     first_part = exchange(first_part, ("ep", "sub"))
     first_grad = jnp.sum(first_part.astype(F32), axis=0)

time: 208 us -> 213 us (1.024)
  blocking collectives: 9.38 us -> 11.9 us
    all_to_all x2, waiting for transfers between devices: 13.8 us -> 0.01 us  [exchange(): return lax.all_to_all(x, axes, split_axis=0, concat_axis=0, tiled=True)]
    ppermute x16, waiting for transfers between devices: 59.4 us -> 72.2 us  [flip(): return lax.ppermute(x, 'ep', [(i, i ^ mask) for i in range(groups)])]
    ppermute x7, waiting for transfers between devices: 11.1 us -> 14.1 us  [turn(): lax.ppermute(x, 'rep', [(r, (r + offset) % shares) for r in range(shares)])]
    all_to_all x1, blocking collectives: 9.38 us -> 11.9 us  [exchange(): return lax.all_to_all(x, axes, split_axis=0, concat_axis=0, tiled=True)]
    unnamed x53 -> x49, local copies, waits for them, and re-layouts: 6.31 us -> 5.64 us
  transfers between devices with their start and end apart: 29 -> 29, of which waited for: 12 -> 11; matrix products, arithmetic and copies ran while one was open for 1% -> 1% of each run, Pallas kernels for 27% -> 28%
where the time goes in v10:
time: 213 us; the launch traced here: 212 us
  waiting for transfers between devices  87.7 us (41%)
  Pallas kernels  63.6 us (30%)
  starting transfers between devices  40.8 us (19%)
  blocking collectives  11.9 us (6%)
  local copies, waits for them, and re-layouts  5.64 us (3%)
    ppermute x16, waiting for transfers between devices, flip(): return lax.ppermute(x, 'ep', [(i, i ^ mask) for i in range(groups)])  72.2 us
    pallas_call x17, Pallas kernels, call(): pl.pallas_call(ordered, grid=grid, in_specs=[SMEM, *in_specs] + [ANY] * l...  63.6 us
    ppermute x16, starting transfers between devices, flip(): return lax.ppermute(x, 'ep', [(i, i ^ mask) for i in range(groups)])  21.8 us
    ppermute x7, waiting for transfers between devices, turn(): lax.ppermute(x, 'rep', [(r, (r + offset) % shares) for r in range(shares)])  14.1 us
    all_to_all x1, blocking collectives, exchange(): return lax.all_to_all(x, axes, split_axis=0, concat_axis=0, tiled=True)  11.9 us
    all_to_all x2, starting transfers between devices, exchange(): return lax.all_to_all(x, axes, split_axis=0, concat_axis=0, tiled=True)  10.8 us
    ppermute x7, starting transfers between devices, turn(): lax.ppermute(x, 'rep', [(r, (r + offset) % shares) for r in range(shares)])  7.94 us
    unnamed x49, local copies, waits for them, and re-layouts  5.64 us
  transfers between devices with their start and end apart: 29, of which 11 were waited for; matrix products, arithmetic and copies ran while one was open for 1% of the time, Pallas kernels for 28%

profile of v10, /device:TPU:8, one launch (start us, length us, event | category | flops | bytes accessed | tf_op | source)
XLA Modules:
  0.0 212.1 jit_solution(12467133769126194367)
XLA Ops:
  0.8 0.8 copy-done.16
  1.6 0.7 copy-done.17
  2.3 1.1 pack_block.1
  3.4 2.7 %collective-permute-start.4 = (bf16[128,2304]{1,0:T(8,128)(2,1)S(1)}, bf16[128,2304]{1,0:T(8,128)(2,1)S(1)}, u32[]{:S(2)}, u32[]{:S(2)}) collective-permute-start(bf16[128,2304]{1,0:T(8,128)(2,1)S(1)} %get-tuple-element.53.refs_1_.refs_5_.refs_2_), channel_id=1, source_target_pairs={{0,16},{4,20},{8,24},{12,28},{16,0},{20,4},{24,8},{28,12},{1,17},{... | collective-permute-start | bytes 1769480 | tf_op jit(solution)/shard_map/ppermute | solution.py:525
  6.0 1.5 collective-permute-start
  7.6 0.4 collective-permute-start.3
  8.0 23.9 %collective-permute-done.4.refs_2_.refs_8_.refs_5_ = bf16[128,2304]{1,0:T(8,128)(2,1)S(1)} collective-permute-done((bf16[128,2304]{1,0:T(8,128)(2,1)S(1)}, bf16[128,2304]{1,0:T(8,128)(2,1)S(1)}, u32[]{:S(2)}, u32[]{:S(2)}) %collective-permute-start.4) | collective-permute-done | bytes 589856 | tf_op jit(solution)/shard_map/ppermute | solution.py:525
  31.9 1.3 collective-permute-start.5
  33.2 0.9 copy-done.15
  34.1 3.4 %load_matrix.1 = (bf16[1536,2048]{1,0:T(8,128)(2,1)S(1)}, bf16[32,2048]{1,0:T(8,128)(2,1)S(1)}, f32[8,128]{1,0:T(8,128)}) custom-call(s32[3]{0:T(128)S(1)} %pad_add_fusion.refs_0_, bf16[1536,2048]{1,0:T(8,128)(2,1)} %bitcast.29, bf16[32,2048]{1,0:T(8,128)(2,1)S(1)} %bitcast.22, f32[8,128]{1,0:T(8,128)} %get-tuple-element.54.refs_3_), custom_call_target="tpu_custom_call" | custom-call | flops 1 | bytes 1 | tf_op jit(solution)/shard_map/load_matrix/pallas_call | solution.py:53
  37.6 1.3 collective-permute-done.1.refs_4_
  39.0 1.6 collective-permute-start.6
  40.5 8.1 %expert_rows.4 = (bf16[320,768]{1,0:T(8,128)(2,1)S(1)}, bf16[320,768]{1,0:T(8,128)(2,1)S(1)}, bf16[2,64,128]{2,1,0:T(8,128)(2,1)S(1)}, f32[8,128]{1,0:T(8,128)}) custom-call(s32[3]{0:T(128)S(1)} %pad_add_fusion.refs_0_, bf16[128,2304]{1,0:T(8,128)(2,1)S(1)} %get-tuple-element.53.refs_1_.refs_5_.refs_2_, ...), custom_call_target="tpu_custom_call" | custom-call | flops 1 | bytes 1 | tf_op jit(solution)/shard_map/expert_rows/pallas_call | solution.py:53
  48.7 1.6 collective-permute-start.7
  50.2 0.5 collective-permute-start.8
  50.7 7.9 %expert_rows.5 = (bf16[320,768]{1,0:T(8,128)(2,1)S(1)}, bf16[320,768]{1,0:T(8,128)(2,1)S(1)}, bf16[2,64,128]{2,1,0:T(8,128)(2,1)S(1)}, f32[8,128]{1,0:T(8,128)}) custom-call(s32[3]{0:T(128)S(1)} %pad_add_fusion.refs_0_, bf16[128,2304]{1,0:T(8,128)(2,1)S(1)} %collective-permute-done.3.refs_1_.refs_7_.refs_4_, ...), custom_call_target="tpu_custom_call" | custom-call | flops 1 | bytes 1 | tf_op jit(solution)/shard_map/expert_rows/pallas_call | solution.py:53
  58.6 0.6 collective-permute-start.10
  59.2 1.6 collective-permute-start.9
  60.7 2.1 collective-permute-done.7.refs_2_
  62.8 0.7 share_sum.4
  63.5 0.7 copy-done.14
  64.2 8.3 %expert_rows.6 = (bf16[320,768]{1,0:T(8,128)(2,1)S(1)}, bf16[320,768]{1,0:T(8,128)(2,1)S(1)}, bf16[2,64,128]{2,1,0:T(8,128)(2,1)S(1)}, f32[8,128]{1,0:T(8,128)}) custom-call(s32[3]{0:T(128)S(1)} %pad_add_fusion.refs_0_, bf16[128,2304]{1,0:T(8,128)(2,1)S(1)} %collective-permute-done.5.refs_1_.refs_9_.refs_6_, ...), custom_call_target="tpu_custom_call" | custom-call | flops 1 | bytes 1 | tf_op jit(solution)/shard_map/expert_rows/pallas_call | solution.py:53
  72.5 1.6 collective-permute-start.11
  74.0 0.7 share_sum.5
  74.7 0.7 collective-permute-start.13
  75.4 3.3 %collective-permute-start.14 = (bf16[160,768]{1,0:T(8,128)(2,1)S(1)}, bf16[160,768]{1,0:T(8,128)(2,1)S(1)}, u32[]{:S(2)}, u32[]{:S(2)}) collective-permute-start(bf16[160,768]{1,0:T(8,128)(2,1)S(1)} %get-tuple-element.76), channel_id=1, source_target_pairs={{0,16},{4,20},{8,24},{12,28},{16,0},{20,4},{24,8},{28,12},{1,17},{... | collective-permute-start | bytes 737288 | tf_op jit(solution)/shard_map/ppermute | solution.py:525
  78.7 0.6 collective-permute-start.12
  79.3 1.1 collective-permute-done.9.refs_2_.refs_12_.refs_9_
  80.4 8.7 %expert_rows.7 = (bf16[320,768]{1,0:T(8,128)(2,1)}, bf16[320,768]{1,0:T(8,128)(2,1)S(1)}, bf16[2,64,128]{2,1,0:T(8,128)(2,1)S(1)}, f32[8,128]{1,0:T(8,128)}) custom-call(s32[3]{0:T(128)S(1)} %pad_add_fusion.refs_0_, bf16[128,2304]{1,0:T(8,128)(2,1)S(1)} %collective-permute-done.8.refs_1_.refs_11_.refs_8_, ...), custom_call_target="tpu_custom_call" | custom-call | flops 1 | bytes 1 | tf_op jit(solution)/shard_map/expert_rows/pallas_call | solution.py:53
  89.2 1.6 collective-permute-start.17
  90.9 1.4 share_sum.6
  92.2 1.8 collect_blocks.1
  94.0 2.7 %collective-permute-start.18 = (bf16[160,768]{1,0:T(8,128)(2,1)}, bf16[160,768]{1,0:T(8,128)(2,1)S(1)}, u32[]{:S(2)}, u32[]{:S(2)}) collective-permute-start(bf16[160,768]{1,0:T(8,128)(2,1)} %get-tuple-element.84), channel_id=1, source_target_pairs={{0,24},{4,28},{8,16},{12,20},{16,8},{20,12},{24,0},{28,4},{1,25},{... | collective-permute-start | bytes 737288 | tf_op jit(solution)/shard_map/ppermute | solution.py:525
  96.7 1.3 collective-permute-start.19
  98.0 5.2 %all-to-all-start = ((bf16[8,64,128]{2,1,0:T(8,128)(2,1)}), bf16[8,64,128]{2,1,0:T(8,128)(2,1)S(1)}, u32[]{:S(2)}, u32[]{:S(2)}) async-start(bf16[8,64,128]{2,1,0:T(8,128)(2,1)} %get-tuple-element.78), calls=%async_computation | async-start | bytes 262144 | tf_op jit(solution)/shard_map/all_to_all | solution.py:531
  103.2 0.1 copy.16.refs_1_.refs_2_
  103.3 0.7 share_sum.7
  104.0 11.6 %collective-permute-done.18.refs_6_.refs_14_ = bf16[160,768]{1,0:T(8,128)(2,1)S(1)} collective-permute-done((bf16[160,768]{1,0:T(8,128)(2,1)}, bf16[160,768]{1,0:T(8,128)(2,1)S(1)}, u32[]{:S(2)}, u32[]{:S(2)}) %collective-permute-start.18) | collective-permute-done | bytes 245792 | tf_op jit(solution)/shard_map/ppermute | solution.py:525
  115.6 4.9 %collective-permute-done.19.refs_7_.refs_13_ = bf16[160,768]{1,0:T(8,128)(2,1)S(1)} collective-permute-done((bf16[160,768]{1,0:T(8,128)(2,1)}, bf16[160,768]{1,0:T(8,128)(2,1)S(1)}, u32[]{:S(2)}, u32[]{:S(2)}) %collective-permute-start.19) | collective-permute-done | bytes 245792 | tf_op jit(solution)/shard_map/ppermute | solution.py:525
  120.4 3.6 %lowrank_hid.1 = (f32[128,512]{1,0:T(8,128)S(1)}, f32[8,128]{1,0:T(8,128)}) custom-call(s32[3]{0:T(128)S(1)} %pad_add_fusion.refs_0_, s32[128,8]{1,0:T(8,128)S(1)} %copy.16.refs_1_.refs_2_, bf16[1024,768]{1,0:T(8,128)(2,1)} %bitcast.25, bf16[256,768]{1,0:T(8,128)(2,1)S(1)} %bitcast.18, bf16[256,768]{1,0:T(8,128)(2,1)S(1)} %bitcast.20, ...), custom_call_target="tpu_custom_call" | custom-call | flops 1 | bytes 1 | tf_op jit(solution)/shard_map/lowrank_hid/pallas_call | solution.py:53
  124.1 0.6 collective-permute-start.24
  124.7 1.5 collective-permute-start.15
  126.2 0.1 copy.18.refs_2_.refs_3_
  126.3 8.1 %collective-permute-done.15.refs_2_ = bf16[8,64,128]{2,1,0:T(8,128)(2,1)S(1)} collective-permute-done((bf16[8,64,128]{2,1,0:T(8,128)(2,1)S(1)}, bf16[8,64,128]{2,1,0:T(8,128)(2,1)S(1)}, u32[]{:S(2)}, u32[]{:S(2)}) %collective-permute-start.15) | collective-permute-done | bytes 131104 | tf_op jit(solution)/shard_map/ppermute | solution.py:519
  134.4 0.7 low_dense.1
  135.1 4.3 %first_grad.1 = (bf16[16,32,768]{2,1,0:T(8,128)(2,1)S(1)}, f32[8,128]{1,0:T(8,128)}) custom-call(s32[3]{0:T(128)S(1)} %pad_add_fusion.refs_0_, s32[128,8]{1,0:T(8,128)S(1)} %copy.16.refs_1_.refs_2_, bf16[128,8]{1,0:T(8,128)(2,1)S(1)} %copy.18.refs_2_.refs_3_, f32[128,512]{1,0:T(8,128)S(1)} %get-tuple-element.87.refs_3_.refs_4_, bf16[1024,768]{1,0:T(8,128)(2,1)} %bitcast.26, ...), custom_call_target="tpu_custom_call" | custom-call | flops 1 | bytes 1 | tf_op jit(solution)/shard_map/first_grad/pallas_call | solution.py:53
  139.4 0.9 copy-done.13
  140.3 1.0 scaled_hid.1
  141.2 11.9 %all_to_all.15.refs_1_ = bf16[8,64,128]{2,1,0:T(8,128)(2,1)S(1)} all-to-all(bf16[8,64,128]{2,1,0:T(8,128)(2,1)S(1)} %get-tuple-element.98), channel_id=1, replica_groups=mesh['grp'=1,'ep'=8,'rep'=2,'sub'=2] {'ep'}, dimensions={0} | all-to-all | bytes 262144 | tf_op jit(solution)/shard_map/all_to_all | solution.py:531
  153.1 5.6 %all-to-all-start.1 = ((bf16[16,32,768]{2,1,0:T(8,128)(2,1)}), bf16[16,32,768]{2,1,0:T(8,128)(2,1)S(1)}, u32[]{:S(2)}, u32[]{:S(2)}) async-start(bf16[16,32,768]{2,1,0:T(8,128)(2,1)} %copy-done.13), calls=%async_computation.1 | async-start | bytes 1572864 | tf_op jit(solution)/shard_map/all_to_all | solution.py:531
  158.7 1.5 collective-permute-start.20
  160.3 0.5 collective-permute-start.22
  160.8 13.7 %collective-permute-done.20 = bf16[160,768]{1,0:T(8,128)(2,1)S(1)} collective-permute-done((bf16[160,768]{1,0:T(8,128)(2,1)}, bf16[160,768]{1,0:T(8,128)(2,1)S(1)}, u32[]{:S(2)}, u32[]{:S(2)}) %collective-permute-start.20) | collective-permute-done | bytes 245792 | tf_op jit(solution)/shard_map/ppermute | solution.py:525
  174.5 5.8 %collective-permute-done.22 = bf16[160,768]{1,0:T(8,128)(2,1)S(1)} collective-permute-done((bf16[160,768]{1,0:T(8,128)(2,1)S(1)}, bf16[160,768]{1,0:T(8,128)(2,1)S(1)}, u32[]{:S(2)}, u32[]{:S(2)}) %collective-permute-start.22) | collective-permute-done | bytes 245792 | tf_op jit(solution)/shard_map/ppermute | solution.py:525
  180.4 1.5 collective-permute-start.23
  181.9 11.3 %collective-permute-done.23.refs_15_ = bf16[160,768]{1,0:T(8,128)(2,1)S(1)} collective-permute-done((bf16[160,768]{1,0:T(8,128)(2,1)S(1)}, bf16[160,768]{1,0:T(8,128)(2,1)S(1)}, u32[]{:S(2)}, u32[]{:S(2)}) %collective-permute-start.23) | collective-permute-done | bytes 245792 | tf_op jit(solution)/shard_map/ppermute | solution.py:525
  193.1 0.7 copy-done.21
  193.8 7.8 %finish.1 = (bf16[1024,768]{1,0:T(8,128)(2,1)}, f32[128,8]{1,0:T(8,128)S(1)}, f32[8,128]{1,0:T(8,128)}) custom-call(s32[3]{0:T(128)S(1)} %pad_add_fusion.refs_0_, s32[128,8]{1,0:T(8,128)S(1)} %copy.16.refs_1_.refs_2_, s32[128,8]{1,0:T(8,128)S(1)} %copy.16.refs_1_.refs_2_, bf16[128,8]{1,0:T(8,128)(2,1)S(1)} %copy.18.refs_2_.refs_3_, ...), custom_call_target="tpu_custom_call" | custom-call | flops 1 | bytes 1000000000 | tf_op jit(solution)/shard_map/finish/pallas_call | solution.py:53
  201.6 3.7 %second_grad.1 = (f32[32,2048]{1,0:T(8,128)S(1)}, f32[32,2048]{1,0:T(8,128)S(1)}, f32[8,128]{1,0:T(8,128)}) custom-call(s32[3]{0:T(128)S(1)} %pad_add_fusion.refs_0_, bf16[8,64,128]{2,1,0:T(8,128)(2,1)S(1)} %all_to_all.15.refs_1_, bf16[128,2304]{1,0:T(8,128)(2,1)} %copy-done, bf16[128,2304]{1,0:T(8,128)(2,1)} %copy-done.2, bf16[128,2304]{1,0:T(8,128)(2,1)} %copy-done.3, ...), custom_call_target="tpu_custom_call" | custom-call | flops 1 | bytes 1 | tf_op jit(solution)/shard_map/second_grad/pallas_call | solution.py:53
  205.4 0.6 collective-permute-start.25
  206.0 3.9 %collective-permute-done.25 = f32[128,8]{1,0:T(8,128)S(1)} collective-permute-done((f32[128,8]{1,0:T(8,128)S(1)}, f32[128,8]{1,0:T(8,128)S(1)}, u32[]{:S(2)}, u32[]{:S(2)}) %collective-permute-start.25) | collective-permute-done | bytes 4128 | tf_op jit(solution)/shard_map/ppermute | solution.py:519
  209.9 0.7 copy.19
  210.6 0.7 convert_reduce_fusion
  211.3 0.7 add_bitcast_fusion
  (65 shorter events, 0.4 us)
Async XLA Ops:
  0.6 39.9 %collective-permute-start.2 = (bf16[1536,2048]{1,0:T(8,128)(2,1)}, bf16[1536,2048]{1,0:T(8,128)(2,1)}, u32[]{:S(2)}, u32[]{:S(2)}) collective-permute-start(bf16[1536,2048]{1,0:T(8,128)(2,1)} %bitcast.28), channel_id=1, source_target_pairs={{0,1},{1,0},{2,3},{3,2},{4,5},{5,4},{6,7},{7,6},{8,9},{9,8},{10,11... | collective-permute-start | bytes 18874376 | tf_op jit(solution)/shard_map/ppermute | solution.py:528
  0.8 0.8 copy-start.16
  1.6 0.7 copy-start.17
  3.4 45.3 %copy-start = (bf16[128,2304]{1,0:T(8,128)(2,1)}, bf16[128,2304]{1,0:T(8,128)(2,1)S(1)}, u32[]{:S(2)}) copy-start(bf16[128,2304]{1,0:T(8,128)(2,1)S(1)} %get-tuple-element.53.refs_1_.refs_5_.refs_2_) | copy-start | bytes 1769476
  3.4 28.5 %collective-permute-start.4 = (bf16[128,2304]{1,0:T(8,128)(2,1)S(1)}, bf16[128,2304]{1,0:T(8,128)(2,1)S(1)}, u32[]{:S(2)}, u32[]{:S(2)}) collective-permute-start(bf16[128,2304]{1,0:T(8,128)(2,1)S(1)} %get-tuple-element.53.refs_1_.refs_5_.refs_2_), channel_id=1, source_target_pairs={{0,16},{4,20},{8,24},{12,28},{16,0},{20,4},{24,8},{28,12},{1,17},{... | collective-permute-start | bytes 1769480 | tf_op jit(solution)/shard_map/ppermute | solution.py:525
  6.0 34.5 %collective-permute-start = (bf16[128,2304]{1,0:T(8,128)(2,1)S(1)}, bf16[128,2304]{1,0:T(8,128)(2,1)S(1)}, u32[]{:S(2)}, u32[]{:S(2)}) collective-permute-start(bf16[128,2304]{1,0:T(8,128)(2,1)S(1)} %get-tuple-element.53.refs_1_.refs_5_.refs_2_), channel_id=1, source_target_pairs={{0,4},{4,0},{8,12},{12,8},{16,20},{20,16},{24,28},{28,24},{1,5},{5... | collective-permute-start | bytes 1769480 | tf_op jit(solution)/shard_map/ppermute | solution.py:525
  7.6 42.6 %collective-permute-start.3 = (bf16[128,2304]{1,0:T(8,128)(2,1)S(1)}, bf16[128,2304]{1,0:T(8,128)(2,1)S(1)}, u32[]{:S(2)}, u32[]{:S(2)}) collective-permute-start(bf16[128,2304]{1,0:T(8,128)(2,1)S(1)} %get-tuple-element.53.refs_1_.refs_5_.refs_2_), channel_id=1, source_target_pairs={{0,8},{4,12},{8,0},{12,4},{16,24},{20,28},{24,16},{28,20},{1,9},{5... | collective-permute-start | bytes 1769480 | tf_op jit(solution)/shard_map/ppermute | solution.py:525
  31.9 18.8 %copy-start.1 = (bf16[128,2304]{1,0:T(8,128)(2,1)}, bf16[128,2304]{1,0:T(8,128)(2,1)S(1)}, u32[]{:S(2)}) copy-start(bf16[128,2304]{1,0:T(8,128)(2,1)S(1)} %collective-permute-done.4.refs_2_.refs_8_.refs_5_) | copy-start | bytes 1769476
  31.9 27.3 %collective-permute-start.5 = (bf16[128,2304]{1,0:T(8,128)(2,1)S(1)}, bf16[128,2304]{1,0:T(8,128)(2,1)S(1)}, u32[]{:S(2)}, u32[]{:S(2)}) collective-permute-start(bf16[128,2304]{1,0:T(8,128)(2,1)S(1)} %collective-permute-done.4.refs_2_.refs_8_.refs_5_), channel_id=1, source_target_pairs={{0,8},{4,12},{8,0},{12,4},{16,24},{20,28},{24,16},{28,20},{1,9},{5... | collective-permute-start | bytes 1769480 | tf_op jit(solution)/shard_map/ppermute | solution.py:525
  33.2 0.9 copy-start.15
  37.5 1.4 collective-permute-start.1
  39.0 25.2 %collective-permute-start.6 = (bf16[128,2304]{1,0:T(8,128)(2,1)S(1)}, bf16[128,2304]{1,0:T(8,128)(2,1)S(1)}, u32[]{:S(2)}, u32[]{:S(2)}) collective-permute-start(bf16[128,2304]{1,0:T(8,128)(2,1)S(1)} %collective-permute-done.4.refs_2_.refs_8_.refs_5_), channel_id=1, source_target_pairs={{0,4},{4,0},{8,12},{12,8},{16,20},{20,16},{24,28},{28,24},{1,5},{5... | collective-permute-start | bytes 1769480 | tf_op jit(solution)/shard_map/ppermute | solution.py:525
  40.5 8.1 %copy-start.2 = (bf16[128,2304]{1,0:T(8,128)(2,1)}, bf16[128,2304]{1,0:T(8,128)(2,1)S(1)}, u32[]{:S(2)}) copy-start(bf16[128,2304]{1,0:T(8,128)(2,1)S(1)} %collective-permute-done.refs_2_.refs_6_.refs_3_) | copy-start | bytes 1769476
  48.7 14.2 %collective-permute-start.7 = (bf16[320,768]{1,0:T(8,128)(2,1)S(1)}, bf16[320,768]{1,0:T(8,128)(2,1)S(1)}, u32[]{:S(2)}, u32[]{:S(2)}) collective-permute-start(bf16[320,768]{1,0:T(8,128)(2,1)S(1)} %get-tuple-element.62), channel_id=1, source_target_pairs={{0,2},{2,0},{1,3},{3,1},{4,6},{6,4},{5,7},{7,5},{8,10},{10,8},{9,1... | collective-permute-start | bytes 1474568 | tf_op jit(solution)/shard_map/ppermute | solution.py:519
  50.2 8.4 %copy-start.3 = (bf16[128,2304]{1,0:T(8,128)(2,1)}, bf16[128,2304]{1,0:T(8,128)(2,1)S(1)}, u32[]{:S(2)}) copy-start(bf16[128,2304]{1,0:T(8,128)(2,1)S(1)} %collective-permute-done.3.refs_1_.refs_7_.refs_4_) | copy-start | bytes 1769476
  50.2 28.5 %collective-permute-start.8 = (bf16[128,2304]{1,0:T(8,128)(2,1)S(1)}, bf16[128,2304]{1,0:T(8,128)(2,1)S(1)}, u32[]{:S(2)}, u32[]{:S(2)}) collective-permute-start(bf16[128,2304]{1,0:T(8,128)(2,1)S(1)} %collective-permute-done.3.refs_1_.refs_7_.refs_4_), channel_id=1, source_target_pairs={{0,4},{4,0},{8,12},{12,8},{16,20},{20,16},{24,28},{28,24},{1,5},{5... | collective-permute-start | bytes 1769480 | tf_op jit(solution)/shard_map/ppermute | solution.py:525
  58.6 15.4 %collective-permute-start.10 = (bf16[320,768]{1,0:T(8,128)(2,1)S(1)}, bf16[320,768]{1,0:T(8,128)(2,1)S(1)}, u32[]{:S(2)}, u32[]{:S(2)}) collective-permute-start(bf16[320,768]{1,0:T(8,128)(2,1)S(1)} %get-tuple-element.67), channel_id=1, source_target_pairs={{0,2},{2,0},{1,3},{3,1},{4,6},{6,4},{5,7},{7,5},{8,10},{10,8},{9,1... | collective-permute-start | bytes 1474568 | tf_op jit(solution)/shard_map/ppermute | solution.py:519
  59.2 13.3 %copy-start.4 = (bf16[128,2304]{1,0:T(8,128)(2,1)}, bf16[128,2304]{1,0:T(8,128)(2,1)S(1)}, u32[]{:S(2)}) copy-start(bf16[128,2304]{1,0:T(8,128)(2,1)S(1)} %collective-permute-done.5.refs_1_.refs_9_.refs_6_) | copy-start | bytes 1769476
  59.2 21.2 %collective-permute-start.9 = (bf16[128,2304]{1,0:T(8,128)(2,1)S(1)}, bf16[128,2304]{1,0:T(8,128)(2,1)S(1)}, u32[]{:S(2)}, u32[]{:S(2)}) collective-permute-start(bf16[128,2304]{1,0:T(8,128)(2,1)S(1)} %collective-permute-done.5.refs_1_.refs_9_.refs_6_), channel_id=1, source_target_pairs={{0,4},{4,0},{8,12},{12,8},{16,20},{20,16},{24,28},{28,24},{1,5},{5... | collective-permute-start | bytes 1769480 | tf_op jit(solution)/shard_map/ppermute | solution.py:525
  63.5 0.7 copy-start.14
  64.2 8.3 %copy-start.5 = (bf16[128,2304]{1,0:T(8,128)(2,1)}, bf16[128,2304]{1,0:T(8,128)(2,1)S(1)}, u32[]{:S(2)}) copy-start(bf16[128,2304]{1,0:T(8,128)(2,1)S(1)} %collective-permute-done.6.refs_2_.refs_10_.refs_7_) | copy-start | bytes 1769476
  72.5 18.4 %collective-permute-start.11 = (bf16[320,768]{1,0:T(8,128)(2,1)S(1)}, bf16[320,768]{1,0:T(8,128)(2,1)S(1)}, u32[]{:S(2)}, u32[]{:S(2)}) collective-permute-start(bf16[320,768]{1,0:T(8,128)(2,1)S(1)} %get-tuple-element.72), channel_id=1, source_target_pairs={{0,2},{2,0},{1,3},{3,1},{4,6},{6,4},{5,7},{7,5},{8,10},{10,8},{9,1... | collective-permute-start | bytes 1474568 | tf_op jit(solution)/shard_map/ppermute | solution.py:519
  74.7 16.1 %collective-permute-start.13 = (bf16[160,768]{1,0:T(8,128)(2,1)S(1)}, bf16[160,768]{1,0:T(8,128)(2,1)S(1)}, u32[]{:S(2)}, u32[]{:S(2)}) collective-permute-start(bf16[160,768]{1,0:T(8,128)(2,1)S(1)} %get-tuple-element.75), channel_id=1, source_target_pairs={{0,8},{4,12},{8,0},{12,4},{16,24},{20,28},{24,16},{28,20},{1,9},{5... | collective-permute-start | bytes 737288 | tf_op jit(solution)/shard_map/ppermute | solution.py:525
  75.4 15.5 %collective-permute-start.14 = (bf16[160,768]{1,0:T(8,128)(2,1)S(1)}, bf16[160,768]{1,0:T(8,128)(2,1)S(1)}, u32[]{:S(2)}, u32[]{:S(2)}) collective-permute-start(bf16[160,768]{1,0:T(8,128)(2,1)S(1)} %get-tuple-element.76), channel_id=1, source_target_pairs={{0,16},{4,20},{8,24},{12,28},{16,0},{20,4},{24,8},{28,12},{1,17},{... | collective-permute-start | bytes 737288 | tf_op jit(solution)/shard_map/ppermute | solution.py:525
  78.7 10.5 %copy-start.6 = (bf16[128,2304]{1,0:T(8,128)(2,1)}, bf16[128,2304]{1,0:T(8,128)(2,1)S(1)}, u32[]{:S(2)}) copy-start(bf16[128,2304]{1,0:T(8,128)(2,1)S(1)} %collective-permute-done.8.refs_1_.refs_11_.refs_8_) | copy-start | bytes 1769476
  78.7 12.1 %collective-permute-start.12 = (bf16[160,768]{1,0:T(8,128)(2,1)S(1)}, bf16[160,768]{1,0:T(8,128)(2,1)S(1)}, u32[]{:S(2)}, u32[]{:S(2)}) collective-permute-start(bf16[160,768]{1,0:T(8,128)(2,1)S(1)} %get-tuple-element.74), channel_id=1, source_target_pairs={{0,4},{4,0},{8,12},{12,8},{16,20},{20,16},{24,28},{28,24},{1,5},{5... | collective-permute-start | bytes 737288 | tf_op jit(solution)/shard_map/ppermute | solution.py:525
  80.4 8.8 %copy-start.7 = (bf16[128,2304]{1,0:T(8,128)(2,1)}, bf16[128,2304]{1,0:T(8,128)(2,1)S(1)}, u32[]{:S(2)}) copy-start(bf16[128,2304]{1,0:T(8,128)(2,1)S(1)} %collective-permute-done.9.refs_2_.refs_12_.refs_9_) | copy-start | bytes 1769476
  89.2 14.0 %copy-start.18 = (s32[128,8]{0,1:T(8,128)S(1)}, s32[128,8]{0,1:T(8,128)}, u32[]{:S(2)}) copy-start(s32[128,8]{0,1:T(8,128)} %param.9) | copy-start | bytes 12292
  89.2 37.0 %copy-start.22 = (bf16[128,8]{0,1:T(8,128)(2,1)S(1)}, bf16[128,8]{0,1:T(8,128)(2,1)}, u32[]{:S(2)}) copy-start(bf16[128,8]{0,1:T(8,128)(2,1)} %param.10) | copy-start | bytes 6148
  89.2 14.1 %collective-permute-start.17 = (bf16[320,768]{1,0:T(8,128)(2,1)}, bf16[320,768]{1,0:T(8,128)(2,1)S(1)}, u32[]{:S(2)}, u32[]{:S(2)}) collective-permute-start(bf16[320,768]{1,0:T(8,128)(2,1)} %get-tuple-element.81), channel_id=1, source_target_pairs={{0,2},{2,0},{1,3},{3,1},{4,6},{6,4},{5,7},{7,5},{8,10},{10,8},{9,1... | collective-permute-start | bytes 1474568 | tf_op jit(solution)/shard_map/ppermute | solution.py:519
  90.8 48.5 %copy-start.8 = (bf16[160,768]{1,0:T(8,128)(2,1)}, bf16[160,768]{1,0:T(8,128)(2,1)S(1)}, u32[]{:S(2)}) copy-start(bf16[160,768]{1,0:T(8,128)(2,1)S(1)} %collective-permute-done.13.refs_5_.refs_10_) | copy-start | bytes 737284
  90.8 3.2 %copy-start.9 = (bf16[160,768]{1,0:T(8,128)(2,1)}, bf16[160,768]{1,0:T(8,128)(2,1)S(1)}, u32[]{:S(2)}) copy-start(bf16[160,768]{1,0:T(8,128)(2,1)S(1)} %collective-permute-done.14.refs_6_.refs_12_) | copy-start | bytes 737284
  90.8 48.5 %copy-start.10 = (bf16[160,768]{1,0:T(8,128)(2,1)}, bf16[160,768]{1,0:T(8,128)(2,1)S(1)}, u32[]{:S(2)}) copy-start(bf16[160,768]{1,0:T(8,128)(2,1)S(1)} %collective-permute-done.12.refs_4_.refs_9_) | copy-start | bytes 737284
  94.0 26.5 %collective-permute-start.16 = (bf16[8,32,768]{2,1,0:T(8,128)(2,1)S(1)}, bf16[8,32,768]{2,1,0:T(8,128)(2,1)S(1)}, u32[]{:S(2)}, u32[]{:S(2)}) collective-permute-start(bf16[8,32,768]{2,1,0:T(8,128)(2,1)S(1)} %get-tuple-element.79), channel_id=1, source_target_pairs={{0,1},{1,0},{2,3},{3,2},{4,5},{5,4},{6,7},{7,6},{8,9},{9,8},{10,11... | collective-permute-start | bytes 1179656 | tf_op jit(solution)/shard_map/ppermute | solution.py:528
  94.0 21.6 %collective-permute-start.18 = (bf16[160,768]{1,0:T(8,128)(2,1)}, bf16[160,768]{1,0:T(8,128)(2,1)S(1)}, u32[]{:S(2)}, u32[]{:S(2)}) collective-permute-start(bf16[160,768]{1,0:T(8,128)(2,1)} %get-tuple-element.84), channel_id=1, source_target_pairs={{0,24},{4,28},{8,16},{12,20},{16,8},{20,12},{24,0},{28,4},{1,25},{... | collective-permute-start | bytes 737288 | tf_op jit(solution)/shard_map/ppermute | solution.py:525
  96.7 23.8 %collective-permute-start.19 = (bf16[160,768]{1,0:T(8,128)(2,1)}, bf16[160,768]{1,0:T(8,128)(2,1)S(1)}, u32[]{:S(2)}, u32[]{:S(2)}) collective-permute-start(bf16[160,768]{1,0:T(8,128)(2,1)} %get-tuple-element.85), channel_id=1, source_target_pairs={{0,20},{4,16},{8,28},{12,24},{16,4},{20,0},{24,12},{28,8},{1,21},{... | collective-permute-start | bytes 737288 | tf_op jit(solution)/shard_map/ppermute | solution.py:525
  98.0 26.7 %all-to-all-start = ((bf16[8,64,128]{2,1,0:T(8,128)(2,1)}), bf16[8,64,128]{2,1,0:T(8,128)(2,1)S(1)}, u32[]{:S(2)}, u32[]{:S(2)}) async-start(bf16[8,64,128]{2,1,0:T(8,128)(2,1)} %get-tuple-element.78), calls=%async_computation | async-start | bytes 262144 | tf_op jit(solution)/shard_map/all_to_all | solution.py:531
  104.0 30.4 %copy-start.19 = (bf16[160,768]{1,0:T(8,128)(2,1)}, bf16[160,768]{1,0:T(8,128)(2,1)S(1)}, u32[]{:S(2)}) copy-start(bf16[160,768]{1,0:T(8,128)(2,1)S(1)} %get-tuple-element.89) | copy-start | bytes 737284
  115.6 77.6 %copy-start.11 = (bf16[160,768]{1,0:T(8,128)(2,1)}, bf16[160,768]{1,0:T(8,128)(2,1)S(1)}, u32[]{:S(2)}) copy-start(bf16[160,768]{1,0:T(8,128)(2,1)S(1)} %collective-permute-done.18.refs_6_.refs_14_) | copy-start | bytes 737284
  120.4 72.7 %copy-start.12 = (bf16[160,768]{1,0:T(8,128)(2,1)}, bf16[160,768]{1,0:T(8,128)(2,1)S(1)}, u32[]{:S(2)}) copy-start(bf16[160,768]{1,0:T(8,128)(2,1)S(1)} %collective-permute-done.19.refs_7_.refs_13_) | copy-start | bytes 737284
  124.1 16.2 %collective-permute-start.24 = (f32[128,512]{1,0:T(8,128)S(1)}, f32[128,512]{1,0:T(8,128)S(1)}, u32[]{:S(2)}, u32[]{:S(2)}) collective-permute-start(f32[128,512]{1,0:T(8,128)S(1)} %get-tuple-element.91.refs_3_), channel_id=1, source_target_pairs={{0,2},{2,0},{1,3},{3,1},{4,6},{6,4},{5,7},{7,5},{8,10},{10,8},{9,1... | collective-permute-start | bytes 786440 | tf_op jit(solution)/shard_map/ppermute | solution.py:519
  124.7 9.7 %collective-permute-start.15 = (bf16[8,64,128]{2,1,0:T(8,128)(2,1)S(1)}, bf16[8,64,128]{2,1,0:T(8,128)(2,1)S(1)}, u32[]{:S(2)}, u32[]{:S(2)}) collective-permute-start(bf16[8,64,128]{2,1,0:T(8,128)(2,1)S(1)} %all-to-all-done.refs_1_), channel_id=1, source_target_pairs={{0,2},{2,0},{1,3},{3,1},{4,6},{6,4},{5,7},{7,5},{8,10},{10,8},{9,1... | collective-permute-start | bytes 393224 | tf_op jit(solution)/shard_map/ppermute | solution.py:519
  139.4 0.9 copy-start.13
  153.1 48.5 %all-to-all-start.1 = ((bf16[16,32,768]{2,1,0:T(8,128)(2,1)}), bf16[16,32,768]{2,1,0:T(8,128)(2,1)S(1)}, u32[]{:S(2)}, u32[]{:S(2)}) async-start(bf16[16,32,768]{2,1,0:T(8,128)(2,1)} %copy-done.13), calls=%async_computation.1 | async-start | bytes 1572864 | tf_op jit(solution)/shard_map/all_to_all | solution.py:531
  158.7 15.8 %collective-permute-start.20 = (bf16[160,768]{1,0:T(8,128)(2,1)}, bf16[160,768]{1,0:T(8,128)(2,1)S(1)}, u32[]{:S(2)}, u32[]{:S(2)}) collective-permute-start(bf16[160,768]{1,0:T(8,128)(2,1)} %copy-done.19), channel_id=1, source_target_pairs={{0,4},{4,0},{8,12},{12,8},{16,20},{20,16},{24,28},{28,24},{1,5},{5... | collective-permute-start | bytes 737288 | tf_op jit(solution)/shard_map/ppermute | solution.py:525
  160.3 20.1 %collective-permute-start.22 = (bf16[160,768]{1,0:T(8,128)(2,1)S(1)}, bf16[160,768]{1,0:T(8,128)(2,1)S(1)}, u32[]{:S(2)}, u32[]{:S(2)}) collective-permute-start(bf16[160,768]{1,0:T(8,128)(2,1)S(1)} %get-tuple-element.90), channel_id=1, source_target_pairs={{0,4},{4,0},{8,12},{12,8},{16,20},{20,16},{24,28},{28,24},{1,5},{5... | collective-permute-start | bytes 737288 | tf_op jit(solution)/shard_map/ppermute | solution.py:525
  174.5 7.3 %collective-permute-start.21 = (bf16[160,768]{1,0:T(8,128)(2,1)S(1)}, bf16[160,768]{1,0:T(8,128)(2,1)S(1)}, u32[]{:S(2)}, u32[]{:S(2)}) collective-permute-start(bf16[160,768]{1,0:T(8,128)(2,1)S(1)} %collective-permute-done.20), channel_id=1, source_target_pairs={{0,8},{4,12},{8,0},{12,4},{16,24},{20,28},{24,16},{28,20},{1,9},{5... | collective-permute-start | bytes 737288 | tf_op jit(solution)/shard_map/ppermute | solution.py:525
  180.4 12.8 %collective-permute-start.23 = (bf16[160,768]{1,0:T(8,128)(2,1)S(1)}, bf16[160,768]{1,0:T(8,128)(2,1)S(1)}, u32[]{:S(2)}, u32[]{:S(2)}) collective-permute-start(bf16[160,768]{1,0:T(8,128)(2,1)S(1)} %collective-permute-done.22), channel_id=1, source_target_pairs={{0,24},{4,28},{8,16},{12,20},{16,8},{20,12},{24,0},{28,4},{1,25},{... | collective-permute-start | bytes 737288 | tf_op jit(solution)/shard_map/ppermute | solution.py:525
  181.9 11.3 %copy-start.20 = (bf16[160,768]{1,0:T(8,128)(2,1)}, bf16[160,768]{1,0:T(8,128)(2,1)S(1)}, u32[]{:S(2)}) copy-start(bf16[160,768]{1,0:T(8,128)(2,1)S(1)} %collective-permute-done.21.refs_11_) | copy-start | bytes 737284
  193.1 0.7 copy-start.21
  205.3 6.0 %collective-permute-start.26 = (f32[32,2048]{1,0:T(8,128)S(1)}, f32[32,2048]{1,0:T(8,128)S(1)}, u32[]{:S(2)}, u32[]{:S(2)}) collective-permute-start(f32[32,2048]{1,0:T(8,128)S(1)} %get-tuple-element.101), channel_id=1, source_target_pairs={{0,1},{1,0},{2,3},{3,2},{4,5},{5,4},{6,7},{7,6},{8,9},{9,8},{10,11... | collective-permute-start | bytes 786440 | tf_op jit(solution)/shard_map/ppermute | solution.py:528
  205.4 4.5 %collective-permute-start.25 = (f32[128,8]{1,0:T(8,128)S(1)}, f32[128,8]{1,0:T(8,128)S(1)}, u32[]{:S(2)}, u32[]{:S(2)}) collective-permute-start(f32[128,8]{1,0:T(8,128)S(1)} %get-tuple-element.96), channel_id=1, source_target_pairs={{0,2},{2,0},{1,3},{3,1},{4,6},{6,4},{5,7},{7,5},{8,10},{10,8},{9,1... | collective-permute-start | bytes 12296 | tf_op jit(solution)/shard_map/ppermute | solution.py:519

commit v11 on v10

--- a/solution.py
+++ b/solution.py
@@ -14,7 +14,7 @@
 TN = (((0,), (0,)), ((), ()))
 NN = (((1,), (0,)), ((), ()))
 SMALL = pl.CostEstimate(flops=1, bytes_accessed=1, transcendentals=0)
-LONG = pl.CostEstimate(flops=1, bytes_accessed=10**9, transcendentals=0)
+LONG = pl.CostEstimate(flops=1, bytes_accessed=2 * 10**7, transcendentals=0)
 ANY = pl.BlockSpec(memory_space=pl.ANY)
 SMEM = pl.BlockSpec(memory_space=pltpu.SMEM)
 VMEM = pl.BlockSpec(memory_space=pltpu.VMEM)
@@ -120,6 +120,22 @@
         [(shape, BF16)],
         [whole(shape)],
     )[0]
+
+
+def gate_kernel(at_ref, *refs):
+    pass
+
+
+def gate_call(order, arrays):
+    return order.call(
+        gate_kernel,
+        "gate",
+        arrays,
+        [ANY] * len(arrays),
+        [(x.shape, x.dtype) for x in arrays],
+        [ANY] * len(arrays),
+        input_output_aliases={1 + k: k for k in range(len(arrays))},
+    )
 
 
 def load_kernel(at_ref, down_ref, second_ref, out_ref, same_ref, sems):
@@ -554,7 +570,7 @@
 
     def send_back(batch, parts):
         for o, rows in zip(batch, share_sum_call(order, parts, 2, slots)):
-            if batch == batches[-1] and o > 1 and o % 2:
+            if batch in batches[-2:] and o > 1 and o % 2:
                 back[o] = flip(flip(rows, 1), o - 1)
             else:
                 back[o] = flip(rows, o) if o else rows
@@ -579,14 +595,18 @@
     low_grad = all_shares(exchange(low_grad))
     send_back(*waiting)
 
-    arrived(len(batches) - 2)
+    order.wait([back[batches[-2][0]]])
     low_hid = all_shares(lowrank_hid_call(order, index, hid, firsts, groups))
     low_grad = low_dense_call(order, low_grad)
     first_part = first_grad_call(order, index, weight, low_grad, hid, groups)
+
+    scaled_hid = scaled_hid_call(order, index, weight, low_hid, groups)
+
+    order.wait([back[batches[-2][1]], back[batches[-1][0]], back[batches[-1][1]]])
+    scaled_hid, first_part = gate_call(order, [scaled_hid, first_part])
+    scaled_hid = exchange(scaled_hid)
     first_part = exchange(first_part, ("ep", "sub"))
     first_grad = jnp.sum(first_part.astype(F32), axis=0)
-
-    scaled_hid = exchange(scaled_hid_call(order, index, weight, low_hid, groups))
     back = [back[o] for o in range(groups)]
     grad_hidden, sums = finish_call(order, index, weight, low_grad, hid, firsts, back)
     sums = sums + turn(sums, 1) if shares == 2 else lax.psum(sums, "rep")

time: 213 us -> 195 us (0.915)
  waiting for transfers between devices: 87.7 us -> 65.4 us
  starting transfers between devices: 40.8 us -> 45.4 us
  local copies, waits for them, and re-layouts: 5.64 us -> 3.35 us
    ppermute x16 -> x17, waiting for transfers between devices: 72.2 us -> 44.9 us  [flip(): return lax.ppermute(x, 'ep', [(i, i ^ mask) for i in range(groups)])]
    all_to_all x2, waiting for transfers between devices: 0.01 us -> 11.1 us  [exchange(): return lax.all_to_all(x, axes, split_axis=0, concat_axis=0, tiled=True)]
    ppermute x7, waiting for transfers between devices: 14.1 us -> 8.05 us  [turn(): lax.ppermute(x, 'rep', [(r, (r + offset) % shares) for r in range(shares)])]
    unnamed x49 -> x45, local copies, waits for them, and re-layouts: 5.64 us -> 3.35 us
    all_to_all x2, starting transfers between devices: 10.8 us -> 13 us  [exchange(): return lax.all_to_all(x, axes, split_axis=0, concat_axis=0, tiled=True)]
    pallas_call x17 -> x18, Pallas kernels: 63.6 us -> 64.9 us  [call(): pl.pallas_call(ordered, grid=grid, in_specs=[SMEM, *in_specs] + [ANY] * l...]
    ppermute x16 -> x17, starting transfers between devices: 21.8 us -> 22.7 us  [flip(): return lax.ppermute(x, 'ep', [(i, i ^ mask) for i in range(groups)])]
  transfers between devices with their start and end apart: 29 -> 30, of which waited for: 11 -> 12; matrix products, arithmetic and copies ran while one was open for 1% -> 1% of each run, Pallas kernels for 28% -> 31%
where the time goes in v11:
time: 195 us; the launch traced here: 194 us
  waiting for transfers between devices  65.4 us (34%)
  Pallas kernels  64.9 us (33%)
  starting transfers between devices  45.4 us (23%)
  blocking collectives  12.1 us (6%)
  local copies, waits for them, and re-layouts  3.35 us (2%)
    pallas_call x18, Pallas kernels, call(): pl.pallas_call(ordered, grid=grid, in_specs=[SMEM, *in_specs] + [ANY] * l...  64.9 us
    ppermute x17, waiting for transfers between devices, flip(): return lax.ppermute(x, 'ep', [(i, i ^ mask) for i in range(groups)])  44.9 us
    ppermute x17, starting transfers between devices, flip(): return lax.ppermute(x, 'ep', [(i, i ^ mask) for i in range(groups)])  22.7 us
    all_to_all x2, starting transfers between devices, exchange(): return lax.all_to_all(x, axes, split_axis=0, concat_axis=0, tiled=True)  13 us
    all_to_all x1, blocking collectives, exchange(): return lax.all_to_all(x, axes, split_axis=0, concat_axis=0, tiled=True)  12.1 us
    all_to_all x2, waiting for transfers between devices, exchange(): return lax.all_to_all(x, axes, split_axis=0, concat_axis=0, tiled=True)  11.1 us
    ppermute x7, starting transfers between devices, turn(): lax.ppermute(x, 'rep', [(r, (r + offset) % shares) for r in range(shares)])  8.67 us
    ppermute x7, waiting for transfers between devices, turn(): lax.ppermute(x, 'rep', [(r, (r + offset) % shares) for r in range(shares)])  8.05 us
  transfers between devices with their start and end apart: 30, of which 12 were waited for; matrix products, arithmetic and copies ran while one was open for 1% of the time, Pallas kernels for 31%

profile of v11, /device:TPU:8, one launch (start us, length us, event | category | flops | bytes accessed | tf_op | source)
XLA Modules:
  0.0 193.7 jit_solution(1973085982738229212)
XLA Ops:
  0.8 0.8 copy-done.17
  1.6 0.7 copy-done.18
  2.3 1.1 pack_block.1
  3.4 2.7 %collective-permute-start.4 = (bf16[128,2304]{1,0:T(8,128)(2,1)S(1)}, bf16[128,2304]{1,0:T(8,128)(2,1)S(1)}, u32[]{:S(2)}, u32[]{:S(2)}) collective-permute-start(bf16[128,2304]{1,0:T(8,128)(2,1)S(1)} %get-tuple-element.56.refs_1_.refs_5_.refs_2_), channel_id=1, source_target_pairs={{0,16},{4,20},{8,24},{12,28},{16,0},{20,4},{24,8},{28,12},{1,17},{... | collective-permute-start | bytes 1769480 | tf_op jit(solution)/shard_map/ppermute | solution.py:541
  6.0 1.5 collective-permute-start
  7.6 0.4 collective-permute-start.3
  8.0 23.9 %collective-permute-done.4.refs_2_.refs_8_.refs_5_ = bf16[128,2304]{1,0:T(8,128)(2,1)S(1)} collective-permute-done((bf16[128,2304]{1,0:T(8,128)(2,1)S(1)}, bf16[128,2304]{1,0:T(8,128)(2,1)S(1)}, u32[]{:S(2)}, u32[]{:S(2)}) %collective-permute-start.4) | collective-permute-done | bytes 589856 | tf_op jit(solution)/shard_map/ppermute | solution.py:541
  31.9 1.3 collective-permute-start.5
  33.2 0.9 copy-done.16
  34.1 3.4 %load_matrix.1 = (bf16[1536,2048]{1,0:T(8,128)(2,1)S(1)}, bf16[32,2048]{1,0:T(8,128)(2,1)S(1)}, f32[8,128]{1,0:T(8,128)}) custom-call(s32[3]{0:T(128)S(1)} %pad_add_fusion.refs_0_, bf16[1536,2048]{1,0:T(8,128)(2,1)} %bitcast.29, bf16[32,2048]{1,0:T(8,128)(2,1)S(1)} %bitcast.22, f32[8,128]{1,0:T(8,128)} %get-tuple-element.57.refs_3_), custom_call_target="tpu_custom_call" | custom-call | flops 1 | bytes 1 | tf_op jit(solution)/shard_map/load_matrix/pallas_call | solution.py:53
  37.6 1.3 collective-permute-done.1.refs_4_
  39.0 1.6 collective-permute-start.6
  40.5 8.1 %expert_rows.4 = (bf16[320,768]{1,0:T(8,128)(2,1)S(1)}, bf16[320,768]{1,0:T(8,128)(2,1)S(1)}, bf16[2,64,128]{2,1,0:T(8,128)(2,1)S(1)}, f32[8,128]{1,0:T(8,128)}) custom-call(s32[3]{0:T(128)S(1)} %pad_add_fusion.refs_0_, bf16[128,2304]{1,0:T(8,128)(2,1)S(1)} %get-tuple-element.56.refs_1_.refs_5_.refs_2_, ...), custom_call_target="tpu_custom_call" | custom-call | flops 1 | bytes 1 | tf_op jit(solution)/shard_map/expert_rows/pallas_call | solution.py:53
  48.7 1.6 collective-permute-start.7
  50.3 0.5 collective-permute-start.8
  50.8 1.5 collective-permute-start.9
  52.3 7.9 %expert_rows.5 = (bf16[320,768]{1,0:T(8,128)(2,1)S(1)}, bf16[320,768]{1,0:T(8,128)(2,1)S(1)}, bf16[2,64,128]{2,1,0:T(8,128)(2,1)S(1)}, f32[8,128]{1,0:T(8,128)}) custom-call(s32[3]{0:T(128)S(1)} %pad_add_fusion.refs_0_, bf16[128,2304]{1,0:T(8,128)(2,1)S(1)} %collective-permute-done.3.refs_1_.refs_7_.refs_4_, ...), custom_call_target="tpu_custom_call" | custom-call | flops 1 | bytes 1 | tf_op jit(solution)/shard_map/expert_rows/pallas_call | solution.py:53
  60.2 0.6 collective-permute-start.10
  60.8 0.9 collective-permute-done.7.refs_2_
  61.8 0.7 share_sum.4
  62.5 8.4 %expert_rows.6 = (bf16[320,768]{1,0:T(8,128)(2,1)S(1)}, bf16[320,768]{1,0:T(8,128)(2,1)S(1)}, bf16[2,64,128]{2,1,0:T(8,128)(2,1)S(1)}, f32[8,128]{1,0:T(8,128)}) custom-call(s32[3]{0:T(128)S(1)} %pad_add_fusion.refs_0_, bf16[128,2304]{1,0:T(8,128)(2,1)S(1)} %collective-permute-done.5.refs_1_.refs_9_.refs_6_, ...), custom_call_target="tpu_custom_call" | custom-call | flops 1 | bytes 1 | tf_op jit(solution)/shard_map/expert_rows/pallas_call | solution.py:53
  70.8 2.3 %collective-permute-start.11 = (bf16[320,768]{1,0:T(8,128)(2,1)S(1)}, bf16[320,768]{1,0:T(8,128)(2,1)S(1)}, u32[]{:S(2)}, u32[]{:S(2)}) collective-permute-start(bf16[320,768]{1,0:T(8,128)(2,1)S(1)} %get-tuple-element.75), channel_id=1, source_target_pairs={{0,2},{2,0},{1,3},{3,1},{4,6},{6,4},{5,7},{7,5},{8,10},{10,8},{9,1... | collective-permute-start | bytes 1474568 | tf_op jit(solution)/shard_map/ppermute | solution.py:535
  73.1 0.7 share_sum.5
  73.8 5.8 %collective-permute-done.9.refs_2_.refs_12_.refs_9_ = bf16[128,2304]{1,0:T(8,128)(2,1)S(1)} collective-permute-done((bf16[128,2304]{1,0:T(8,128)(2,1)S(1)}, bf16[128,2304]{1,0:T(8,128)(2,1)S(1)}, u32[]{:S(2)}, u32[]{:S(2)}) %collective-permute-start.9) | collective-permute-done | bytes 589856 | tf_op jit(solution)/shard_map/ppermute | solution.py:541
  79.6 8.1 %expert_rows.7 = (bf16[320,768]{1,0:T(8,128)(2,1)S(1)}, bf16[320,768]{1,0:T(8,128)(2,1)S(1)}, bf16[2,64,128]{2,1,0:T(8,128)(2,1)S(1)}, f32[8,128]{1,0:T(8,128)}) custom-call(s32[3]{0:T(128)S(1)} %pad_add_fusion.refs_0_, bf16[128,2304]{1,0:T(8,128)(2,1)S(1)} %collective-permute-done.8.refs_1_.refs_11_.refs_8_, ...), custom_call_target="tpu_custom_call" | custom-call | flops 1 | bytes 1 | tf_op jit(solution)/shard_map/expert_rows/pallas_call | solution.py:53
  87.8 1.6 collective-permute-start.17
  89.4 0.6 collective-permute-start.13
  90.0 3.4 %collective-permute-start.14 = (bf16[160,768]{1,0:T(8,128)(2,1)S(1)}, bf16[160,768]{1,0:T(8,128)(2,1)S(1)}, u32[]{:S(2)}, u32[]{:S(2)}) collective-permute-start(bf16[160,768]{1,0:T(8,128)(2,1)S(1)} %get-tuple-element.79), channel_id=1, source_target_pairs={{0,16},{4,20},{8,24},{12,28},{16,0},{20,4},{24,8},{28,12},{1,17},{... | collective-permute-start | bytes 737288 | tf_op jit(solution)/shard_map/ppermute | solution.py:541
  93.4 1.4 collective-permute-start.12
  94.9 4.9 %collective-permute-done.13.refs_5_.refs_10_ = bf16[160,768]{1,0:T(8,128)(2,1)S(1)} collective-permute-done((bf16[160,768]{1,0:T(8,128)(2,1)S(1)}, bf16[160,768]{1,0:T(8,128)(2,1)S(1)}, u32[]{:S(2)}, u32[]{:S(2)}) %collective-permute-start.13) | collective-permute-done | bytes 245792 | tf_op jit(solution)/shard_map/ppermute | solution.py:541
  99.7 3.9 %collective-permute-done.14.refs_6_.refs_12_ = bf16[160,768]{1,0:T(8,128)(2,1)S(1)} collective-permute-done((bf16[160,768]{1,0:T(8,128)(2,1)S(1)}, bf16[160,768]{1,0:T(8,128)(2,1)S(1)}, u32[]{:S(2)}, u32[]{:S(2)}) %collective-permute-start.14) | collective-permute-done | bytes 245792 | tf_op jit(solution)/shard_map/ppermute | solution.py:541
  103.6 0.7 share_sum.6
  104.3 1.8 collect_blocks.1
  106.1 1.3 share_sum.7
  107.3 1.4 collective-permute-start.19
  108.8 0.6 collective-permute-start.23
  109.4 1.4 collective-permute-start.21
  110.8 7.4 %all-to-all-start = ((bf16[8,64,128]{2,1,0:T(8,128)(2,1)}), bf16[8,64,128]{2,1,0:T(8,128)(2,1)S(1)}, u32[]{:S(2)}, u32[]{:S(2)}) async-start(bf16[8,64,128]{2,1,0:T(8,128)(2,1)} %get-tuple-element.81), calls=%async_computation | async-start | bytes 262144 | tf_op jit(solution)/shard_map/all_to_all | solution.py:547
  118.2 0.1 copy.18.refs_1_.refs_2_
  118.3 1.4 collective-permute-done.18.refs_6_.refs_14_
  119.7 3.6 %lowrank_hid.1 = (f32[128,512]{1,0:T(8,128)S(1)}, f32[8,128]{1,0:T(8,128)}) custom-call(s32[3]{0:T(128)S(1)} %pad_add_fusion.refs_0_, s32[128,8]{1,0:T(8,128)S(1)} %copy.18.refs_1_.refs_2_, bf16[1024,768]{1,0:T(8,128)(2,1)} %bitcast.25, bf16[256,768]{1,0:T(8,128)(2,1)S(1)} %bitcast.18, bf16[256,768]{1,0:T(8,128)(2,1)S(1)} %bitcast.20, ...), custom_call_target="tpu_custom_call" | custom-call | flops 1 | bytes 1 | tf_op jit(solution)/shard_map/lowrank_hid/pallas_call | solution.py:53
  123.3 0.6 collective-permute-start.25
  123.9 1.6 collective-permute-start.24
  125.5 2.2 %collective-permute-done.21 = bf16[160,768]{1,0:T(8,128)(2,1)} collective-permute-done((bf16[160,768]{1,0:T(8,128)(2,1)S(1)}, bf16[160,768]{1,0:T(8,128)(2,1)}, u32[]{:S(2)}, u32[]{:S(2)}) %collective-permute-start.21) | collective-permute-done | bytes 245792 | tf_op jit(solution)/shard_map/ppermute | solution.py:541
  127.8 2.7 %collective-permute-start.22 = (bf16[160,768]{1,0:T(8,128)(2,1)}, bf16[160,768]{1,0:T(8,128)(2,1)S(1)}, u32[]{:S(2)}, u32[]{:S(2)}) collective-permute-start(bf16[160,768]{1,0:T(8,128)(2,1)} %collective-permute-done.21), channel_id=1, source_target_pairs={{0,16},{4,20},{8,24},{12,28},{16,0},{20,4},{24,8},{28,12},{1,17},{... | collective-permute-start | bytes 737288 | tf_op jit(solution)/shard_map/ppermute | solution.py:541
  130.4 0.5 collective-permute-start.15
  131.0 0.1 copy.20.refs_2_.refs_3_
  131.1 4.3 %collective-permute-done.15.refs_2_ = bf16[8,64,128]{2,1,0:T(8,128)(2,1)S(1)} collective-permute-done((bf16[8,64,128]{2,1,0:T(8,128)(2,1)S(1)}, bf16[8,64,128]{2,1,0:T(8,128)(2,1)S(1)}, u32[]{:S(2)}, u32[]{:S(2)}) %collective-permute-start.15) | collective-permute-done | bytes 131104 | tf_op jit(solution)/shard_map/ppermute | solution.py:535
  135.4 0.7 low_dense.1
  136.1 5.2 %first_grad.1 = (bf16[16,32,768]{2,1,0:T(8,128)(2,1)}, f32[8,128]{1,0:T(8,128)}) custom-call(s32[3]{0:T(128)S(1)} %pad_add_fusion.refs_0_, s32[128,8]{1,0:T(8,128)S(1)} %copy.18.refs_1_.refs_2_, bf16[128,8]{1,0:T(8,128)(2,1)S(1)} %copy.20.refs_2_.refs_3_, f32[128,512]{1,0:T(8,128)S(1)} %get-tuple-element.89.refs_3_.refs_4_, bf16[1024,768]{1,0:T(8,128)(2,1)} %bitcast.26, ...), custom_call_target="tpu_custom_call" | custom-call | flops 1 | bytes 1 | tf_op jit(solution)/shard_map/first_grad/pallas_call | solution.py:53
  141.3 1.4 scaled_hid.1
  142.7 2.9 %collective-permute-done.22.refs_4_.refs_13_ = bf16[160,768]{1,0:T(8,128)(2,1)S(1)} collective-permute-done((bf16[160,768]{1,0:T(8,128)(2,1)}, bf16[160,768]{1,0:T(8,128)(2,1)S(1)}, u32[]{:S(2)}, u32[]{:S(2)}) %collective-permute-start.22) | collective-permute-done | bytes 245792 | tf_op jit(solution)/shard_map/ppermute | solution.py:541
  145.6 0.5 gate.1
  146.1 12.1 %all_to_all.15.refs_1_ = bf16[8,64,128]{2,1,0:T(8,128)(2,1)S(1)} all-to-all(bf16[8,64,128]{2,1,0:T(8,128)(2,1)S(1)} %get-tuple-element.104), channel_id=1, replica_groups=mesh['grp'=1,'ep'=8,'rep'=2,'sub'=2] {'ep'}, dimensions={0} | all-to-all | bytes 262144 | tf_op jit(solution)/shard_map/all_to_all | solution.py:547
  158.2 5.6 %all-to-all-start.1 = ((bf16[16,32,768]{2,1,0:T(8,128)(2,1)}), bf16[16,32,768]{2,1,0:T(8,128)(2,1)S(1)}, u32[]{:S(2)}, u32[]{:S(2)}) async-start(bf16[16,32,768]{2,1,0:T(8,128)(2,1)} %get-tuple-element.103), calls=%async_computation.1 | async-start | bytes 1572864 | tf_op jit(solution)/shard_map/all_to_all | solution.py:547
  163.9 7.8 %finish.1 = (bf16[1024,768]{1,0:T(8,128)(2,1)}, f32[128,8]{1,0:T(8,128)S(1)}, f32[8,128]{1,0:T(8,128)}) custom-call(s32[3]{0:T(128)S(1)} %pad_add_fusion.refs_0_, s32[128,8]{1,0:T(8,128)S(1)} %copy.18.refs_1_.refs_2_, s32[128,8]{1,0:T(8,128)S(1)} %copy.18.refs_1_.refs_2_, bf16[128,8]{1,0:T(8,128)(2,1)S(1)} %copy.20.refs_2_.refs_3_, ...), custom_call_target="tpu_custom_call" | custom-call | flops 1 | bytes 20000000 | tf_op jit(solution)/shard_map/finish/pallas_call | solution.py:53
  171.7 11.1 %all-to-all-done.1.refs_11_ = bf16[16,32,768]{2,1,0:T(8,128)(2,1)S(1)} async-done(((bf16[16,32,768]{2,1,0:T(8,128)(2,1)}), bf16[16,32,768]{2,1,0:T(8,128)(2,1)S(1)}, u32[]{:S(2)}, u32[]{:S(2)}) %all-to-all-start.1) | async-done | bytes 786464 | tf_op jit(solution)/shard_map/all_to_all | solution.py:547
  182.8 3.7 %second_grad.1 = (f32[32,2048]{1,0:T(8,128)S(1)}, f32[32,2048]{1,0:T(8,128)S(1)}, f32[8,128]{1,0:T(8,128)}) custom-call(s32[3]{0:T(128)S(1)} %pad_add_fusion.refs_0_, bf16[8,64,128]{2,1,0:T(8,128)(2,1)S(1)} %all_to_all.15.refs_1_, bf16[128,2304]{1,0:T(8,128)(2,1)} %copy-done, bf16[128,2304]{1,0:T(8,128)(2,1)} %copy-done.2, bf16[128,2304]{1,0:T(8,128)(2,1)} %copy-done.3, ...), custom_call_target="tpu_custom_call" | custom-call | flops 1 | bytes 1 | tf_op jit(solution)/shard_map/second_grad/pallas_call | solution.py:53
  186.5 0.8 collective-permute-start.27
  187.3 1.5 collective-permute-start.26
  188.8 2.8 %collective-permute-done.26 = f32[128,8]{1,0:T(8,128)S(1)} collective-permute-done((f32[128,8]{1,0:T(8,128)S(1)}, f32[128,8]{1,0:T(8,128)S(1)}, u32[]{:S(2)}, u32[]{:S(2)}) %collective-permute-start.26) | collective-permute-done | bytes 4128 | tf_op jit(solution)/shard_map/ppermute | solution.py:535
  191.6 0.7 copy.21
  192.3 0.7 convert_reduce_fusion
  193.0 0.7 add_bitcast_fusion
  (64 shorter events, 0.4 us)
Async XLA Ops:
  0.6 39.9 %collective-permute-start.2 = (bf16[1536,2048]{1,0:T(8,128)(2,1)}, bf16[1536,2048]{1,0:T(8,128)(2,1)}, u32[]{:S(2)}, u32[]{:S(2)}) collective-permute-start(bf16[1536,2048]{1,0:T(8,128)(2,1)} %bitcast.28), channel_id=1, source_target_pairs={{0,1},{1,0},{2,3},{3,2},{4,5},{5,4},{6,7},{7,6},{8,9},{9,8},{10,11... | collective-permute-start | bytes 18874376 | tf_op jit(solution)/shard_map/ppermute | solution.py:544
  0.8 0.8 copy-start.17
  1.6 0.7 copy-start.18
  3.4 45.3 %copy-start = (bf16[128,2304]{1,0:T(8,128)(2,1)}, bf16[128,2304]{1,0:T(8,128)(2,1)S(1)}, u32[]{:S(2)}) copy-start(bf16[128,2304]{1,0:T(8,128)(2,1)S(1)} %get-tuple-element.56.refs_1_.refs_5_.refs_2_) | copy-start | bytes 1769476
  3.4 28.5 %collective-permute-start.4 = (bf16[128,2304]{1,0:T(8,128)(2,1)S(1)}, bf16[128,2304]{1,0:T(8,128)(2,1)S(1)}, u32[]{:S(2)}, u32[]{:S(2)}) collective-permute-start(bf16[128,2304]{1,0:T(8,128)(2,1)S(1)} %get-tuple-element.56.refs_1_.refs_5_.refs_2_), channel_id=1, source_target_pairs={{0,16},{4,20},{8,24},{12,28},{16,0},{20,4},{24,8},{28,12},{1,17},{... | collective-permute-start | bytes 1769480 | tf_op jit(solution)/shard_map/ppermute | solution.py:541
  6.0 34.5 %collective-permute-start = (bf16[128,2304]{1,0:T(8,128)(2,1)S(1)}, bf16[128,2304]{1,0:T(8,128)(2,1)S(1)}, u32[]{:S(2)}, u32[]{:S(2)}) collective-permute-start(bf16[128,2304]{1,0:T(8,128)(2,1)S(1)} %get-tuple-element.56.refs_1_.refs_5_.refs_2_), channel_id=1, source_target_pairs={{0,4},{4,0},{8,12},{12,8},{16,20},{20,16},{24,28},{28,24},{1,5},{5... | collective-permute-start | bytes 1769480 | tf_op jit(solution)/shard_map/ppermute | solution.py:541
  7.6 42.7 %collective-permute-start.3 = (bf16[128,2304]{1,0:T(8,128)(2,1)S(1)}, bf16[128,2304]{1,0:T(8,128)(2,1)S(1)}, u32[]{:S(2)}, u32[]{:S(2)}) collective-permute-start(bf16[128,2304]{1,0:T(8,128)(2,1)S(1)} %get-tuple-element.56.refs_1_.refs_5_.refs_2_), channel_id=1, source_target_pairs={{0,8},{4,12},{8,0},{12,4},{16,24},{20,28},{24,16},{28,20},{1,9},{5... | collective-permute-start | bytes 1769480 | tf_op jit(solution)/shard_map/ppermute | solution.py:541
  31.9 20.4 %copy-start.1 = (bf16[128,2304]{1,0:T(8,128)(2,1)}, bf16[128,2304]{1,0:T(8,128)(2,1)S(1)}, u32[]{:S(2)}) copy-start(bf16[128,2304]{1,0:T(8,128)(2,1)S(1)} %collective-permute-done.4.refs_2_.refs_8_.refs_5_) | copy-start | bytes 1769476
  31.9 18.9 %collective-permute-start.5 = (bf16[128,2304]{1,0:T(8,128)(2,1)S(1)}, bf16[128,2304]{1,0:T(8,128)(2,1)S(1)}, u32[]{:S(2)}, u32[]{:S(2)}) collective-permute-start(bf16[128,2304]{1,0:T(8,128)(2,1)S(1)} %collective-permute-done.4.refs_2_.refs_8_.refs_5_), channel_id=1, source_target_pairs={{0,8},{4,12},{8,0},{12,4},{16,24},{20,28},{24,16},{28,20},{1,9},{5... | collective-permute-start | bytes 1769480 | tf_op jit(solution)/shard_map/ppermute | solution.py:541
  33.2 0.9 copy-start.16
  37.5 1.4 collective-permute-start.1
  39.0 23.5 %collective-permute-start.6 = (bf16[128,2304]{1,0:T(8,128)(2,1)S(1)}, bf16[128,2304]{1,0:T(8,128)(2,1)S(1)}, u32[]{:S(2)}, u32[]{:S(2)}) collective-permute-start(bf16[128,2304]{1,0:T(8,128)(2,1)S(1)} %collective-permute-done.4.refs_2_.refs_8_.refs_5_), channel_id=1, source_target_pairs={{0,4},{4,0},{8,12},{12,8},{16,20},{20,16},{24,28},{28,24},{1,5},{5... | collective-permute-start | bytes 1769480 | tf_op jit(solution)/shard_map/ppermute | solution.py:541
  40.5 8.2 %copy-start.2 = (bf16[128,2304]{1,0:T(8,128)(2,1)}, bf16[128,2304]{1,0:T(8,128)(2,1)S(1)}, u32[]{:S(2)}) copy-start(bf16[128,2304]{1,0:T(8,128)(2,1)S(1)} %collective-permute-done.refs_2_.refs_6_.refs_3_) | copy-start | bytes 1769476
  48.7 13.1 %collective-permute-start.7 = (bf16[320,768]{1,0:T(8,128)(2,1)S(1)}, bf16[320,768]{1,0:T(8,128)(2,1)S(1)}, u32[]{:S(2)}, u32[]{:S(2)}) collective-permute-start(bf16[320,768]{1,0:T(8,128)(2,1)S(1)} %get-tuple-element.65), channel_id=1, source_target_pairs={{0,2},{2,0},{1,3},{3,1},{4,6},{6,4},{5,7},{7,5},{8,10},{10,8},{9,1... | collective-permute-start | bytes 1474568 | tf_op jit(solution)/shard_map/ppermute | solution.py:535
  50.2 10.0 %copy-start.3 = (bf16[128,2304]{1,0:T(8,128)(2,1)}, bf16[128,2304]{1,0:T(8,128)(2,1)S(1)}, u32[]{:S(2)}) copy-start(bf16[128,2304]{1,0:T(8,128)(2,1)S(1)} %collective-permute-done.3.refs_1_.refs_7_.refs_4_) | copy-start | bytes 1769476
  50.3 23.6 %collective-permute-start.8 = (bf16[128,2304]{1,0:T(8,128)(2,1)S(1)}, bf16[128,2304]{1,0:T(8,128)(2,1)S(1)}, u32[]{:S(2)}, u32[]{:S(2)}) collective-permute-start(bf16[128,2304]{1,0:T(8,128)(2,1)S(1)} %collective-permute-done.3.refs_1_.refs_7_.refs_4_), channel_id=1, source_target_pairs={{0,4},{4,0},{8,12},{12,8},{16,20},{20,16},{24,28},{28,24},{1,5},{5... | collective-permute-start | bytes 1769480 | tf_op jit(solution)/shard_map/ppermute | solution.py:541
  50.8 11.7 %copy-start.4 = (bf16[128,2304]{1,0:T(8,128)(2,1)}, bf16[128,2304]{1,0:T(8,128)(2,1)S(1)}, u32[]{:S(2)}) copy-start(bf16[128,2304]{1,0:T(8,128)(2,1)S(1)} %collective-permute-done.5.refs_1_.refs_9_.refs_6_) | copy-start | bytes 1769476
  50.8 28.9 %collective-permute-start.9 = (bf16[128,2304]{1,0:T(8,128)(2,1)S(1)}, bf16[128,2304]{1,0:T(8,128)(2,1)S(1)}, u32[]{:S(2)}, u32[]{:S(2)}) collective-permute-start(bf16[128,2304]{1,0:T(8,128)(2,1)S(1)} %collective-permute-done.5.refs_1_.refs_9_.refs_6_), channel_id=1, source_target_pairs={{0,4},{4,0},{8,12},{12,8},{16,20},{20,16},{24,28},{28,24},{1,5},{5... | collective-permute-start | bytes 1769480 | tf_op jit(solution)/shard_map/ppermute | solution.py:541
  60.2 12.9 %collective-permute-start.10 = (bf16[320,768]{1,0:T(8,128)(2,1)S(1)}, bf16[320,768]{1,0:T(8,128)(2,1)S(1)}, u32[]{:S(2)}, u32[]{:S(2)}) collective-permute-start(bf16[320,768]{1,0:T(8,128)(2,1)S(1)} %get-tuple-element.70), channel_id=1, source_target_pairs={{0,2},{2,0},{1,3},{3,1},{4,6},{6,4},{5,7},{7,5},{8,10},{10,8},{9,1... | collective-permute-start | bytes 1474568 | tf_op jit(solution)/shard_map/ppermute | solution.py:535
  62.4 8.4 %copy-start.15 = (bf16[160,768]{1,0:T(8,128)(2,1)}, bf16[160,768]{1,0:T(8,128)(2,1)S(1)}, u32[]{:S(2)}) copy-start(bf16[160,768]{1,0:T(8,128)(2,1)S(1)} %get-tuple-element.90.refs_8_) | copy-start | bytes 737284
  62.4 8.4 %copy-start.5 = (bf16[128,2304]{1,0:T(8,128)(2,1)}, bf16[128,2304]{1,0:T(8,128)(2,1)S(1)}, u32[]{:S(2)}) copy-start(bf16[128,2304]{1,0:T(8,128)(2,1)S(1)} %collective-permute-done.6.refs_2_.refs_10_.refs_7_) | copy-start | bytes 1769476
  70.8 32.8 %collective-permute-start.11 = (bf16[320,768]{1,0:T(8,128)(2,1)S(1)}, bf16[320,768]{1,0:T(8,128)(2,1)S(1)}, u32[]{:S(2)}, u32[]{:S(2)}) collective-permute-start(bf16[320,768]{1,0:T(8,128)(2,1)S(1)} %get-tuple-element.75), channel_id=1, source_target_pairs={{0,2},{2,0},{1,3},{3,1},{4,6},{6,4},{5,7},{7,5},{8,10},{10,8},{9,1... | collective-permute-start | bytes 1474568 | tf_op jit(solution)/shard_map/ppermute | solution.py:535
  73.8 13.9 %copy-start.6 = (bf16[128,2304]{1,0:T(8,128)(2,1)}, bf16[128,2304]{1,0:T(8,128)(2,1)S(1)}, u32[]{:S(2)}) copy-start(bf16[128,2304]{1,0:T(8,128)(2,1)S(1)} %collective-permute-done.8.refs_1_.refs_11_.refs_8_) | copy-start | bytes 1769476
  79.6 8.1 %copy-start.7 = (bf16[128,2304]{1,0:T(8,128)(2,1)}, bf16[128,2304]{1,0:T(8,128)(2,1)S(1)}, u32[]{:S(2)}) copy-start(bf16[128,2304]{1,0:T(8,128)(2,1)S(1)} %collective-permute-done.9.refs_2_.refs_12_.refs_9_) | copy-start | bytes 1769476
  87.8 30.4 %copy-start.19 = (s32[128,8]{0,1:T(8,128)S(1)}, s32[128,8]{0,1:T(8,128)}, u32[]{:S(2)}) copy-start(s32[128,8]{0,1:T(8,128)} %param.9) | copy-start | bytes 12292
  87.8 43.2 %copy-start.20 = (bf16[128,8]{0,1:T(8,128)(2,1)S(1)}, bf16[128,8]{0,1:T(8,128)(2,1)}, u32[]{:S(2)}) copy-start(bf16[128,8]{0,1:T(8,128)(2,1)} %param.10) | copy-start | bytes 6148
  87.8 18.3 %collective-permute-start.17 = (bf16[320,768]{1,0:T(8,128)(2,1)S(1)}, bf16[320,768]{1,0:T(8,128)(2,1)S(1)}, u32[]{:S(2)}, u32[]{:S(2)}) collective-permute-start(bf16[320,768]{1,0:T(8,128)(2,1)S(1)} %get-tuple-element.84), channel_id=1, source_target_pairs={{0,2},{2,0},{1,3},{3,1},{4,6},{6,4},{5,7},{7,5},{8,10},{10,8},{9,1... | collective-permute-start | bytes 1474568 | tf_op jit(solution)/shard_map/ppermute | solution.py:535
  89.4 10.3 %collective-permute-start.13 = (bf16[160,768]{1,0:T(8,128)(2,1)S(1)}, bf16[160,768]{1,0:T(8,128)(2,1)S(1)}, u32[]{:S(2)}, u32[]{:S(2)}) collective-permute-start(bf16[160,768]{1,0:T(8,128)(2,1)S(1)} %get-tuple-element.78), channel_id=1, source_target_pairs={{0,8},{4,12},{8,0},{12,4},{16,24},{20,28},{24,16},{28,20},{1,9},{5... | collective-permute-start | bytes 737288 | tf_op jit(solution)/shard_map/ppermute | solution.py:541
  90.0 13.6 %collective-permute-start.14 = (bf16[160,768]{1,0:T(8,128)(2,1)S(1)}, bf16[160,768]{1,0:T(8,128)(2,1)S(1)}, u32[]{:S(2)}, u32[]{:S(2)}) collective-permute-start(bf16[160,768]{1,0:T(8,128)(2,1)S(1)} %get-tuple-element.79), channel_id=1, source_target_pairs={{0,16},{4,20},{8,24},{12,28},{16,0},{20,4},{24,8},{28,12},{1,17},{... | collective-permute-start | bytes 737288 | tf_op jit(solution)/shard_map/ppermute | solution.py:541
  93.4 10.1 %collective-permute-start.12 = (bf16[160,768]{1,0:T(8,128)(2,1)S(1)}, bf16[160,768]{1,0:T(8,128)(2,1)S(1)}, u32[]{:S(2)}, u32[]{:S(2)}) collective-permute-start(bf16[160,768]{1,0:T(8,128)(2,1)S(1)} %get-tuple-element.77), channel_id=1, source_target_pairs={{0,4},{4,0},{8,12},{12,8},{16,20},{20,16},{24,28},{28,24},{1,5},{5... | collective-permute-start | bytes 737288 | tf_op jit(solution)/shard_map/ppermute | solution.py:541
  99.7 41.5 %copy-start.8 = (bf16[160,768]{1,0:T(8,128)(2,1)}, bf16[160,768]{1,0:T(8,128)(2,1)S(1)}, u32[]{:S(2)}) copy-start(bf16[160,768]{1,0:T(8,128)(2,1)S(1)} %collective-permute-done.13.refs_5_.refs_10_) | copy-start | bytes 737284
  103.6 37.7 %copy-start.9 = (bf16[160,768]{1,0:T(8,128)(2,1)}, bf16[160,768]{1,0:T(8,128)(2,1)S(1)}, u32[]{:S(2)}) copy-start(bf16[160,768]{1,0:T(8,128)(2,1)S(1)} %collective-permute-done.14.refs_6_.refs_12_) | copy-start | bytes 737284
  103.6 37.7 %copy-start.10 = (bf16[160,768]{1,0:T(8,128)(2,1)}, bf16[160,768]{1,0:T(8,128)(2,1)S(1)}, u32[]{:S(2)}) copy-start(bf16[160,768]{1,0:T(8,128)(2,1)S(1)} %collective-permute-done.12.refs_4_.refs_9_) | copy-start | bytes 737284
  106.0 13.6 %collective-permute-start.16 = (bf16[8,32,768]{2,1,0:T(8,128)(2,1)S(1)}, bf16[8,32,768]{2,1,0:T(8,128)(2,1)S(1)}, u32[]{:S(2)}, u32[]{:S(2)}) collective-permute-start(bf16[8,32,768]{2,1,0:T(8,128)(2,1)S(1)} %get-tuple-element.82), channel_id=1, source_target_pairs={{0,1},{1,0},{2,3},{3,2},{4,5},{5,4},{6,7},{7,6},{8,9},{9,8},{10,11... | collective-permute-start | bytes 1179656 | tf_op jit(solution)/shard_map/ppermute | solution.py:544
  106.0 13.6 %collective-permute-start.18 = (bf16[160,768]{1,0:T(8,128)(2,1)S(1)}, bf16[160,768]{1,0:T(8,128)(2,1)S(1)}, u32[]{:S(2)}, u32[]{:S(2)}) collective-permute-start(bf16[160,768]{1,0:T(8,128)(2,1)S(1)} %get-tuple-element.87), channel_id=1, source_target_pairs={{0,24},{4,28},{8,16},{12,20},{16,8},{20,12},{24,0},{28,4},{1,25},{... | collective-permute-start | bytes 737288 | tf_op jit(solution)/shard_map/ppermute | solution.py:541
  107.3 16.6 %collective-permute-start.19 = (bf16[160,768]{1,0:T(8,128)(2,1)}, bf16[160,768]{1,0:T(8,128)(2,1)}, u32[]{:S(2)}, u32[]{:S(2)}) collective-permute-start(bf16[160,768]{1,0:T(8,128)(2,1)} %get-tuple-element.91), channel_id=1, source_target_pairs={{0,4},{4,0},{8,12},{12,8},{16,20},{20,16},{24,28},{28,24},{1,5},{5... | collective-permute-start | bytes 737288 | tf_op jit(solution)/shard_map/ppermute | solution.py:541
  108.8 15.2 %collective-permute-start.23 = (bf16[160,768]{1,0:T(8,128)(2,1)S(1)}, bf16[160,768]{1,0:T(8,128)(2,1)}, u32[]{:S(2)}, u32[]{:S(2)}) collective-permute-start(bf16[160,768]{1,0:T(8,128)(2,1)S(1)} %get-tuple-element.93), channel_id=1, source_target_pairs={{0,4},{4,0},{8,12},{12,8},{16,20},{20,16},{24,28},{28,24},{1,5},{5... | collective-permute-start | bytes 737288 | tf_op jit(solution)/shard_map/ppermute | solution.py:541
  109.4 18.4 %collective-permute-start.21 = (bf16[160,768]{1,0:T(8,128)(2,1)S(1)}, bf16[160,768]{1,0:T(8,128)(2,1)}, u32[]{:S(2)}, u32[]{:S(2)}) collective-permute-start(bf16[160,768]{1,0:T(8,128)(2,1)S(1)} %get-tuple-element.92), channel_id=1, source_target_pairs={{0,4},{4,0},{8,12},{12,8},{16,20},{20,16},{24,28},{28,24},{1,5},{5... | collective-permute-start | bytes 737288 | tf_op jit(solution)/shard_map/ppermute | solution.py:541
  110.8 19.7 %all-to-all-start = ((bf16[8,64,128]{2,1,0:T(8,128)(2,1)}), bf16[8,64,128]{2,1,0:T(8,128)(2,1)S(1)}, u32[]{:S(2)}, u32[]{:S(2)}) async-start(bf16[8,64,128]{2,1,0:T(8,128)(2,1)} %get-tuple-element.81), calls=%async_computation | async-start | bytes 262144 | tf_op jit(solution)/shard_map/all_to_all | solution.py:547
  119.7 44.2 %copy-start.11 = (bf16[160,768]{1,0:T(8,128)(2,1)}, bf16[160,768]{1,0:T(8,128)(2,1)S(1)}, u32[]{:S(2)}) copy-start(bf16[160,768]{1,0:T(8,128)(2,1)S(1)} %collective-permute-done.18.refs_6_.refs_14_) | copy-start | bytes 737284
  123.3 18.0 %collective-permute-start.25 = (f32[128,512]{1,0:T(8,128)S(1)}, f32[128,512]{1,0:T(8,128)}, u32[]{:S(2)}, u32[]{:S(2)}) collective-permute-start(f32[128,512]{1,0:T(8,128)S(1)} %get-tuple-element.94.refs_3_), channel_id=1, source_target_pairs={{0,2},{2,0},{1,3},{3,1},{4,6},{6,4},{5,7},{7,5},{8,10},{10,8},{9,1... | collective-permute-start | bytes 786440 | tf_op jit(solution)/shard_map/ppermute | solution.py:535
  123.9 18.8 %collective-permute-start.20 = (bf16[160,768]{1,0:T(8,128)(2,1)}, bf16[160,768]{1,0:T(8,128)(2,1)S(1)}, u32[]{:S(2)}, u32[]{:S(2)}) collective-permute-start(bf16[160,768]{1,0:T(8,128)(2,1)} %collective-permute-done.19), channel_id=1, source_target_pairs={{0,8},{4,12},{8,0},{12,4},{16,24},{20,28},{24,16},{28,20},{1,9},{5... | collective-permute-start | bytes 737288 | tf_op jit(solution)/shard_map/ppermute | solution.py:541
  123.9 18.8 %collective-permute-start.24 = (bf16[160,768]{1,0:T(8,128)(2,1)}, bf16[160,768]{1,0:T(8,128)(2,1)S(1)}, u32[]{:S(2)}, u32[]{:S(2)}) collective-permute-start(bf16[160,768]{1,0:T(8,128)(2,1)} %collective-permute-done.23), channel_id=1, source_target_pairs={{0,24},{4,28},{8,16},{12,20},{16,8},{20,12},{24,0},{28,4},{1,25},{... | collective-permute-start | bytes 737288 | tf_op jit(solution)/shard_map/ppermute | solution.py:541
  127.8 17.8 %collective-permute-start.22 = (bf16[160,768]{1,0:T(8,128)(2,1)}, bf16[160,768]{1,0:T(8,128)(2,1)S(1)}, u32[]{:S(2)}, u32[]{:S(2)}) collective-permute-start(bf16[160,768]{1,0:T(8,128)(2,1)} %collective-permute-done.21), channel_id=1, source_target_pairs={{0,16},{4,20},{8,24},{12,28},{16,0},{20,4},{24,8},{28,12},{1,17},{... | collective-permute-start | bytes 737288 | tf_op jit(solution)/shard_map/ppermute | solution.py:541
  130.4 5.0 %collective-permute-start.15 = (bf16[8,64,128]{2,1,0:T(8,128)(2,1)S(1)}, bf16[8,64,128]{2,1,0:T(8,128)(2,1)S(1)}, u32[]{:S(2)}, u32[]{:S(2)}) collective-permute-start(bf16[8,64,128]{2,1,0:T(8,128)(2,1)S(1)} %all-to-all-done.refs_1_), channel_id=1, source_target_pairs={{0,2},{2,0},{1,3},{3,1},{4,6},{6,4},{5,7},{7,5},{8,10},{10,8},{9,1... | collective-permute-start | bytes 393224 | tf_op jit(solution)/shard_map/ppermute | solution.py:535
  142.7 21.2 %copy-start.12 = (bf16[160,768]{1,0:T(8,128)(2,1)}, bf16[160,768]{1,0:T(8,128)(2,1)S(1)}, u32[]{:S(2)}) copy-start(bf16[160,768]{1,0:T(8,128)(2,1)S(1)} %collective-permute-done.20.refs_5_.refs_11_) | copy-start | bytes 737284
  142.7 21.1 %copy-start.13 = (bf16[160,768]{1,0:T(8,128)(2,1)}, bf16[160,768]{1,0:T(8,128)(2,1)S(1)}, u32[]{:S(2)}) copy-start(bf16[160,768]{1,0:T(8,128)(2,1)S(1)} %collective-permute-done.24.refs_6_.refs_15_) | copy-start | bytes 737284
  145.6 12.7 %copy-start.14 = (bf16[160,768]{1,0:T(8,128)(2,1)}, bf16[160,768]{1,0:T(8,128)(2,1)S(1)}, u32[]{:S(2)}) copy-start(bf16[160,768]{1,0:T(8,128)(2,1)S(1)} %collective-permute-done.22.refs_4_.refs_13_) | copy-start | bytes 737284
  158.2 24.6 %all-to-all-start.1 = ((bf16[16,32,768]{2,1,0:T(8,128)(2,1)}), bf16[16,32,768]{2,1,0:T(8,128)(2,1)S(1)}, u32[]{:S(2)}, u32[]{:S(2)}) async-start(bf16[16,32,768]{2,1,0:T(8,128)(2,1)} %get-tuple-element.103), calls=%async_computation.1 | async-start | bytes 1572864 | tf_op jit(solution)/shard_map/all_to_all | solution.py:547
  186.5 6.5 %collective-permute-start.27 = (f32[32,2048]{1,0:T(8,128)S(1)}, f32[32,2048]{1,0:T(8,128)S(1)}, u32[]{:S(2)}, u32[]{:S(2)}) collective-permute-start(f32[32,2048]{1,0:T(8,128)S(1)} %get-tuple-element.107), channel_id=1, source_target_pairs={{0,1},{1,0},{2,3},{3,2},{4,5},{5,4},{6,7},{7,6},{8,9},{9,8},{10,11... | collective-permute-start | bytes 786440 | tf_op jit(solution)/shard_map/ppermute | solution.py:544
  187.3 4.3 %collective-permute-start.26 = (f32[128,8]{1,0:T(8,128)S(1)}, f32[128,8]{1,0:T(8,128)S(1)}, u32[]{:S(2)}, u32[]{:S(2)}) collective-permute-start(f32[128,8]{1,0:T(8,128)S(1)} %get-tuple-element.102), channel_id=1, source_target_pairs={{0,2},{2,0},{1,3},{3,1},{4,6},{6,4},{5,7},{7,5},{8,10},{10,8},{9,1... | collective-permute-start | bytes 12296 | tf_op jit(solution)/shard_map/ppermute | solution.py:535

commit v12 on v11

--- a/solution.py
+++ b/solution.py
@@ -346,69 +346,53 @@
     )[0]
 
 
-def scaled_hid_kernel(groups, rank, at_ref, index_ref, prob_ref, *refs):
-    out_ref = refs[-1]
-    total = refs[0][...]
-    for ref in refs[1:-1]:
-        total = total + ref[...]
-    place = relative(at_ref, index_ref[...], groups)
-    prob = prob_ref[...].astype(F32)
-    expert = iota(total.shape, 1) // rank
-    scale = jnp.zeros(total.shape, F32)
-    for k in range(place.shape[1]):
-        scale = jnp.where(expert == place[:, k : k + 1], prob[:, k : k + 1], scale)
-    scaled = (total * scale).T.astype(BF16)
-    for o in range(groups):
-        for q in range(2):
-            at = (q * groups + o) * rank
-            out_ref[lax.bitwise_xor(at_ref[1], o), pl.ds(q * rank, rank), :] = scaled[at : at + rank]
-
-
-def scaled_hid_call(order, index, prob, parts, groups):
-    toks, width = parts[0].shape
-    rank = width // groups // 2
-    shape = (groups, 2 * rank, toks)
-    return order.call(
-        functools.partial(scaled_hid_kernel, groups, rank),
-        "scaled_hid",
-        [index, prob, *parts],
-        [whole(index.shape), whole(prob.shape)] + [whole((toks, width))] * len(parts),
-        [(shape, BF16)],
-        [whole(shape)],
-    )[0]
-
-
-def second_grad_kernel(places, at_ref, scaled_ref, *refs):
-    grads, outs = refs[:-2], refs[-2:]
+def second_grad_kernel(places, units, at_ref, got_ref, *refs):
+    grads, outs, first_ref = refs[:-3], refs[-3:-1], refs[-1]
     rank, tile = outs[0].shape
-    total = jnp.zeros((2 * rank, tile), F32)
+    toks = grads[0].shape[0]
+
+    @pl.when(pl.program_id(0) == 0)
+    def _():
+        total = jnp.zeros((rank, units), F32)
+        for source in range(got_ref.shape[0]):
+            total = total + got_ref[source, :, pl.ds(0, units)].astype(F32)
+        first_ref[...] = total
+
+    totals = [jnp.zeros((rank, tile), F32) for _ in outs]
     for o, grad_ref in zip(places, grads):
-        total = total + dot(scaled_ref[lax.bitwise_xor(at_ref[1], o)], grad_ref[...], NN)
-    for q, out_ref in enumerate(outs):
-        out_ref[...] = adapter_scale * total[q * rank : (q + 1) * rank]
-
-
-def second_grad_call(order, places, scaled, grads, feats):
-    groups, both, toks = scaled.shape
+        source = 2 * lax.bitwise_xor(at_ref[1], o) + at_ref[2]
+        scaled = jnp.concatenate(
+            [got_ref[source, :, pl.ds(units + q * toks, toks)] for q in range(2)], axis=0
+        )
+        value = dot(scaled, grad_ref[...], NN)
+        totals = [total + value[q * rank : (q + 1) * rank] for q, total in enumerate(totals)]
+    for total, out_ref in zip(totals, outs):
+        out_ref[...] = adapter_scale * total
+
+
+def second_grad_call(order, places, got, grads, units, feats):
+    rank, toks = got.shape[1], grads[0].shape[0]
     steps = 4
     tile = feats // steps
-    block = pl.BlockSpec((both // 2, tile), lambda i: (0, i))
-    return order.call(
-        functools.partial(second_grad_kernel, places),
+    block = pl.BlockSpec((rank, tile), lambda i: (0, i))
+    return order.call(
+        functools.partial(second_grad_kernel, places, units),
         "second_grad",
-        [scaled, *[in_hbm(x) for x in grads]],
-        [whole(scaled.shape)] + [pl.BlockSpec((toks, tile), lambda i: (0, i))] * groups,
-        [((both // 2, feats), F32)] * 2,
-        [block] * 2,
+        [got, *[in_hbm(x) for x in grads]],
+        [whole(got.shape)] + [pl.BlockSpec((toks, tile), lambda i: (0, i))] * len(grads),
+        [((rank, feats), F32)] * 2 + [((rank, units), F32)],
+        [block] * 2 + [whole((rank, units))],
         grid=(steps,),
     )
 
 
-def first_grad_kernel(groups, steps, at_ref, index_ref, prob_ref, low_ref, hid_ref, *rest):
-    out_ref, sum_ref = rest
+def first_grad_kernel(groups, steps, parts, at_ref, index_ref, prob_ref, low_ref, hid_ref, *rest):
+    index_all_ref, prob_all_ref, hids = rest[0], rest[1], rest[2 : 2 + parts]
+    out_ref, sum_ref = rest[2 + parts :]
     step = pl.program_id(0)
     top = index_ref.shape[1]
     rank = out_ref.shape[1]
+    units = sum_ref.shape[1]
     low = spread_pairs(low_ref[...], top)
     column = pair_column(relative(at_ref, index_ref[...], groups).astype(F32))
     keep = expert_mask(column, low.shape[1], rank)
@@ -425,28 +409,48 @@
 
     @pl.when(step == steps - 1)
     def _():
+        total = hids[0][...]
+        for ref in hids[1:]:
+            total = total + ref[...]
+        toks = total.shape[0]
+        place = relative(at_ref, index_all_ref[...], groups)
+        prob = prob_all_ref[...].astype(F32)
+        expert = iota(total.shape, 1) // rank
+        scale = jnp.zeros(total.shape, F32)
+        for k in range(top):
+            scale = jnp.where(expert == place[:, k : k + 1], prob[:, k : k + 1], scale)
+        turned = (total * scale).T.astype(BF16)
         for o in range(groups):
             for q in range(2):
-                expert = 2 * lax.bitwise_xor(at_ref[1], o) + lax.bitwise_xor(at_ref[2], q)
-                rows = sum_ref[pl.ds((q * groups + o) * rank, rank), :]
-                out_ref[expert] = rows.astype(BF16)
-
-
-def first_grad_call(order, index, prob, low, hid, groups):
+                at = (q * groups + o) * rank
+                to = 2 * lax.bitwise_xor(at_ref[1], o) + lax.bitwise_xor(at_ref[2], q)
+                out_ref[to, :, pl.ds(0, units)] = sum_ref[pl.ds(at, rank), :].astype(BF16)
+                if q:
+                    out_ref[to, :, pl.ds(units, 2 * toks)] = jnp.zeros((rank, 2 * toks), BF16)
+                else:
+                    for p in range(2):
+                        rows = turned[(p * groups + o) * rank : (p * groups + o + 1) * rank]
+                        out_ref[to, :, pl.ds(units + p * toks, toks)] = rows
+
+
+def first_grad_call(order, index, prob, low, hid, hids, groups):
     (toks, top), (pairs, units) = index.shape, hid.shape
     width = low.shape[1]
     steps = 4
-    shape = (2 * groups, width // groups // 2, units)
-    return order.call(
-        functools.partial(first_grad_kernel, groups, steps),
+    shape = (2 * groups, width // groups // 2, units + 2 * toks)
+    return order.call(
+        functools.partial(first_grad_kernel, groups, steps, len(hids)),
         "first_grad",
-        [index, prob, low, in_hbm(hid)],
+        [index, prob, low, in_hbm(hid), index, prob, *hids],
         [
             pl.BlockSpec((toks // steps, top), lambda i: (i, 0)),
             pl.BlockSpec((toks // steps, top), lambda i: (i, 0)),
             pl.BlockSpec((toks // steps, width), lambda i: (i, 0)),
             pl.BlockSpec((pairs // steps, units), lambda i: (i, 0)),
-        ],
+            whole(index.shape),
+            whole(prob.shape),
+        ]
+        + [whole(x.shape) for x in hids],
         [(shape, BF16)],
         [whole(shape)],
         grid=(steps,),
@@ -543,6 +547,8 @@
     def swap(x):
         return lax.ppermute(x, "sub", [(0, 1), (1, 0)])
 
+    where = ("ep", "sub")
+
     def exchange(x, axes="ep"):
         return lax.all_to_all(x, axes, split_axis=0, concat_axis=0, tiled=True)
 
@@ -576,13 +582,13 @@
                 back[o] = flip(rows, o) if o else rows
 
     for i, batch in enumerate(batches):
+        if i > 1 and i == len(batches) - 1:
+            for j in range(i - 1):
+                arrived(j)
         *give, keep, low = expert_rows_call(
             order, [fetch(o) for o in batch], seconds, downs, shares, slots
         )
         lows.append(low)
-        if i > 1 and i == len(batches) - 1:
-            for j in range(i - 1):
-                arrived(j)
         if i > 0:
             send_back(*waiting)
         waiting = (batch, [keep] + [turn(x, k + 1) for k, x in enumerate(give)])
@@ -593,25 +599,21 @@
     low_grad, first_own = collect_call(order, places, lows, grads, feats)
     firsts = [x.reshape(groups * rank, units) for x in (first_own, swap(first_own))]
     low_grad = all_shares(exchange(low_grad))
+    low_hid = all_shares(lowrank_hid_call(order, index, hid, firsts, groups))
+    order.wait([back[batches[-2][0]]])
     send_back(*waiting)
 
-    order.wait([back[batches[-2][0]]])
-    low_hid = all_shares(lowrank_hid_call(order, index, hid, firsts, groups))
     low_grad = low_dense_call(order, low_grad)
-    first_part = first_grad_call(order, index, weight, low_grad, hid, groups)
-
-    scaled_hid = scaled_hid_call(order, index, weight, low_hid, groups)
+    parts = first_grad_call(order, index, weight, low_grad, hid, low_hid, groups)
 
     order.wait([back[batches[-2][1]], back[batches[-1][0]], back[batches[-1][1]]])
-    scaled_hid, first_part = gate_call(order, [scaled_hid, first_part])
-    scaled_hid = exchange(scaled_hid)
-    first_part = exchange(first_part, ("ep", "sub"))
-    first_grad = jnp.sum(first_part.astype(F32), axis=0)
+    got = exchange(gate_call(order, [parts])[0], where)
     back = [back[o] for o in range(groups)]
     grad_hidden, sums = finish_call(order, index, weight, low_grad, hid, firsts, back)
     sums = sums + turn(sums, 1) if shares == 2 else lax.psum(sums, "rep")
-    order.wait([first_part])
-    second_keep, second_give = second_grad_call(order, places, scaled_hid, grads, feats)
+    second_keep, second_give, first_grad = second_grad_call(
+        order, places, got, grads, units, feats
+    )
     second_grad = second_keep + swap(second_give)
     return (
         grad_hidden.reshape(toks, top, units),

time: 195 us -> 187 us (0.959)
  waiting for transfers between devices: 65.4 us -> 78 us
  blocking collectives: 12.1 us -> 0 us
  starting transfers between devices: 45.4 us -> 37.3 us
    all_to_all x1 -> x0, blocking collectives: 12.1 us -> none  [exchange(): return lax.all_to_all(x, axes, split_axis=0, concat_axis=0, tiled=True)]
    all_to_all x2, waiting for transfers between devices: 11.1 us -> 17.6 us  [exchange(): return lax.all_to_all(x, axes, split_axis=0, concat_axis=0, tiled=True)]
    ppermute x17, waiting for transfers between devices: 44.9 us -> 49.2 us  [flip(): return lax.ppermute(x, 'ep', [(i, i ^ mask) for i in range(groups)])]
    all_to_all x2, starting transfers between devices: 13 us -> 8.86 us  [exchange(): return lax.all_to_all(x, axes, split_axis=0, concat_axis=0, tiled=True)]
    pallas_call x18 -> x17, Pallas kernels: 64.9 us -> 64.6 us  [call(): pl.pallas_call(ordered, grid=grid, in_specs=[SMEM, *in_specs] + [ANY] * l...]
  transfers between devices with their start and end apart: 30 -> 30, of which waited for: 12 -> 14; matrix products, arithmetic and copies ran while one was open for 1% -> 1% of each run, Pallas kernels for 31% -> 32%
where the time goes in v12:
time: 187 us; the launch traced here: 186 us
  waiting for transfers between devices  78 us (42%)
  Pallas kernels  64.6 us (35%)
  starting transfers between devices  37.3 us (20%)
  local copies, waits for them, and re-layouts  4.03 us (2%)
    pallas_call x17, Pallas kernels, call(): pl.pallas_call(ordered, grid=grid, in_specs=[SMEM, *in_specs] + [ANY] * l...  64.6 us
    ppermute x17, waiting for transfers between devices, flip(): return lax.ppermute(x, 'ep', [(i, i ^ mask) for i in range(groups)])  49.2 us
    ppermute x17, starting transfers between devices, flip(): return lax.ppermute(x, 'ep', [(i, i ^ mask) for i in range(groups)])  20.8 us
    all_to_all x2, waiting for transfers between devices, exchange(): return lax.all_to_all(x, axes, split_axis=0, concat_axis=0, tiled=True)  17.6 us
    ppermute x7, waiting for transfers between devices, turn(): lax.ppermute(x, 'rep', [(r, (r + offset) % shares) for r in range(shares)])  9.84 us
    all_to_all x2, starting transfers between devices, exchange(): return lax.all_to_all(x, axes, split_axis=0, concat_axis=0, tiled=True)  8.86 us
    ppermute x7, starting transfers between devices, turn(): lax.ppermute(x, 'rep', [(r, (r + offset) % shares) for r in range(shares)])  6.73 us
    unnamed x45, local copies, waits for them, and re-layouts  4.03 us
  transfers between devices with their start and end apart: 30, of which 14 were waited for; matrix products, arithmetic and copies ran while one was open for 1% of the time, Pallas kernels for 32%

profile of v12, /device:TPU:8, one launch (start us, length us, event | category | flops | bytes accessed | tf_op | source)
XLA Modules:
  0.0 185.8 jit_solution(7106139252391728302)
XLA Ops:
  0.8 0.8 copy-done.17
  1.6 0.7 copy-done.18
  2.3 1.1 pack_block.1
  3.4 2.7 %collective-permute-start.4 = (bf16[128,2304]{1,0:T(8,128)(2,1)S(1)}, bf16[128,2304]{1,0:T(8,128)(2,1)S(1)}, u32[]{:S(2)}, u32[]{:S(2)}) collective-permute-start(bf16[128,2304]{1,0:T(8,128)(2,1)S(1)} %get-tuple-element.54.refs_1_.refs_5_.refs_2_), channel_id=1, source_target_pairs={{0,16},{4,20},{8,24},{12,28},{16,0},{20,4},{24,8},{28,12},{1,17},{... | collective-permute-start | bytes 1769480 | tf_op jit(solution)/shard_map/ppermute | solution.py:545
  6.0 1.5 collective-permute-start
  7.6 0.4 collective-permute-start.3
  8.0 23.9 %collective-permute-done.4.refs_2_.refs_8_.refs_5_ = bf16[128,2304]{1,0:T(8,128)(2,1)S(1)} collective-permute-done((bf16[128,2304]{1,0:T(8,128)(2,1)S(1)}, bf16[128,2304]{1,0:T(8,128)(2,1)S(1)}, u32[]{:S(2)}, u32[]{:S(2)}) %collective-permute-start.4) | collective-permute-done | bytes 589856 | tf_op jit(solution)/shard_map/ppermute | solution.py:545
  31.9 1.3 collective-permute-start.5
  33.2 0.9 copy-done.16
  34.1 3.4 %load_matrix.1 = (bf16[1536,2048]{1,0:T(8,128)(2,1)S(1)}, bf16[32,2048]{1,0:T(8,128)(2,1)S(1)}, f32[8,128]{1,0:T(8,128)}) custom-call(s32[3]{0:T(128)S(1)} %pad_add_fusion.refs_0_, bf16[1536,2048]{1,0:T(8,128)(2,1)} %bitcast.29, bf16[32,2048]{1,0:T(8,128)(2,1)S(1)} %bitcast.22, f32[8,128]{1,0:T(8,128)} %get-tuple-element.55.refs_3_), custom_call_target="tpu_custom_call" | custom-call | flops 1 | bytes 1 | tf_op jit(solution)/shard_map/load_matrix/pallas_call | solution.py:53
  37.6 1.3 collective-permute-done.1.refs_4_
  39.0 1.6 collective-permute-start.6
  40.5 8.1 %expert_rows.4 = (bf16[320,768]{1,0:T(8,128)(2,1)S(1)}, bf16[320,768]{1,0:T(8,128)(2,1)S(1)}, bf16[2,64,128]{2,1,0:T(8,128)(2,1)S(1)}, f32[8,128]{1,0:T(8,128)}) custom-call(s32[3]{0:T(128)S(1)} %pad_add_fusion.refs_0_, bf16[128,2304]{1,0:T(8,128)(2,1)S(1)} %get-tuple-element.54.refs_1_.refs_5_.refs_2_, ...), custom_call_target="tpu_custom_call" | custom-call | flops 1 | bytes 1 | tf_op jit(solution)/shard_map/expert_rows/pallas_call | solution.py:53
  48.7 1.6 collective-permute-start.7
  50.3 0.5 collective-permute-start.8
  50.8 7.9 %expert_rows.5 = (bf16[320,768]{1,0:T(8,128)(2,1)S(1)}, bf16[320,768]{1,0:T(8,128)(2,1)S(1)}, bf16[2,64,128]{2,1,0:T(8,128)(2,1)S(1)}, f32[8,128]{1,0:T(8,128)}) custom-call(s32[3]{0:T(128)S(1)} %pad_add_fusion.refs_0_, bf16[128,2304]{1,0:T(8,128)(2,1)S(1)} %collective-permute-done.3.refs_1_.refs_7_.refs_4_, ...), custom_call_target="tpu_custom_call" | custom-call | flops 1 | bytes 1 | tf_op jit(solution)/shard_map/expert_rows/pallas_call | solution.py:53
  58.7 0.6 collective-permute-start.10
  59.2 1.6 collective-permute-start.9
  60.8 2.0 %collective-permute-done.7.refs_2_ = bf16[320,768]{1,0:T(8,128)(2,1)S(1)} collective-permute-done((bf16[320,768]{1,0:T(8,128)(2,1)S(1)}, bf16[320,768]{1,0:T(8,128)(2,1)S(1)}, u32[]{:S(2)}, u32[]{:S(2)}) %collective-permute-start.7) | collective-permute-done | bytes 491552 | tf_op jit(solution)/shard_map/ppermute | solution.py:539
  62.8 0.7 share_sum.4
  63.5 0.7 copy-done.15
  64.1 8.3 %expert_rows.6 = (bf16[320,768]{1,0:T(8,128)(2,1)S(1)}, bf16[320,768]{1,0:T(8,128)(2,1)S(1)}, bf16[2,64,128]{2,1,0:T(8,128)(2,1)S(1)}, f32[8,128]{1,0:T(8,128)}) custom-call(s32[3]{0:T(128)S(1)} %pad_add_fusion.refs_0_, bf16[128,2304]{1,0:T(8,128)(2,1)S(1)} %collective-permute-done.5.refs_1_.refs_9_.refs_6_, ...), custom_call_target="tpu_custom_call" | custom-call | flops 1 | bytes 1 | tf_op jit(solution)/shard_map/expert_rows/pallas_call | solution.py:53
  72.5 1.6 collective-permute-start.14
  74.1 0.7 share_sum.5
  74.8 0.7 collective-permute-start.12
  75.4 3.4 %collective-permute-start.13 = (bf16[160,768]{1,0:T(8,128)(2,1)S(1)}, bf16[160,768]{1,0:T(8,128)(2,1)S(1)}, u32[]{:S(2)}, u32[]{:S(2)}) collective-permute-start(bf16[160,768]{1,0:T(8,128)(2,1)S(1)} %get-tuple-element.73), channel_id=1, source_target_pairs={{0,16},{4,20},{8,24},{12,28},{16,0},{20,4},{24,8},{28,12},{1,17},{... | collective-permute-start | bytes 737288 | tf_op jit(solution)/shard_map/ppermute | solution.py:545
  78.8 0.6 collective-permute-start.11
  79.4 1.0 collective-permute-done.9.refs_2_.refs_12_.refs_9_
  80.4 2.5 %collective-permute-done.12.refs_9_.refs_10_ = bf16[160,768]{1,0:T(8,128)(2,1)S(1)} collective-permute-done((bf16[160,768]{1,0:T(8,128)(2,1)S(1)}, bf16[160,768]{1,0:T(8,128)(2,1)S(1)}, u32[]{:S(2)}, u32[]{:S(2)}) %collective-permute-start.12) | collective-permute-done | bytes 245792 | tf_op jit(solution)/shard_map/ppermute | solution.py:545
  82.9 4.6 %collective-permute-done.13.refs_10_.refs_12_ = bf16[160,768]{1,0:T(8,128)(2,1)S(1)} collective-permute-done((bf16[160,768]{1,0:T(8,128)(2,1)S(1)}, bf16[160,768]{1,0:T(8,128)(2,1)S(1)}, u32[]{:S(2)}, u32[]{:S(2)}) %collective-permute-start.13) | collective-permute-done | bytes 245792 | tf_op jit(solution)/shard_map/ppermute | solution.py:545
  87.5 8.8 %expert_rows.7 = (bf16[320,768]{1,0:T(8,128)(2,1)}, bf16[320,768]{1,0:T(8,128)(2,1)S(1)}, bf16[2,64,128]{2,1,0:T(8,128)(2,1)S(1)}, f32[8,128]{1,0:T(8,128)}) custom-call(s32[3]{0:T(128)S(1)} %pad_add_fusion.refs_0_, bf16[128,2304]{1,0:T(8,128)(2,1)S(1)} %collective-permute-done.8.refs_1_.refs_11_.refs_8_, ...), custom_call_target="tpu_custom_call" | custom-call | flops 1 | bytes 1 | tf_op jit(solution)/shard_map/expert_rows/pallas_call | solution.py:53
  96.3 1.1 collective-permute-start.16
  97.5 0.7 share_sum.6
  98.1 1.7 collect_blocks.1
  99.9 0.4 collective-permute-start.18
  100.4 1.5 collective-permute-start.21
  101.8 3.5 %lowrank_hid.1 = (f32[128,512]{1,0:T(8,128)S(1)}, f32[8,128]{1,0:T(8,128)}) custom-call(s32[3]{0:T(128)S(1)} %pad_add_fusion.refs_0_, s32[128,8]{1,0:T(8,128)S(1)} %copy.17.refs_1_.refs_5_.refs_2_, bf16[1024,768]{1,0:T(8,128)(2,1)} %bitcast.25, bf16[256,768]{1,0:T(8,128)(2,1)S(1)} %bitcast.18, bf16[256,768]{1,0:T(8,128)(2,1)S(1)} %bitcast.20, ...), custom_call_target="tpu_custom_call" | custom-call | flops 1 | bytes 1 | tf_op jit(solution)/shard_map/lowrank_hid/pallas_call | solution.py:53
  105.4 8.1 %collective-permute-done.18.refs_4_.refs_14_ = bf16[160,768]{1,0:T(8,128)(2,1)S(1)} collective-permute-done((bf16[160,768]{1,0:T(8,128)(2,1)S(1)}, bf16[160,768]{1,0:T(8,128)(2,1)S(1)}, u32[]{:S(2)}, u32[]{:S(2)}) %collective-permute-start.18) | collective-permute-done | bytes 245792 | tf_op jit(solution)/shard_map/ppermute | solution.py:545
  113.5 0.7 share_sum.7
  114.2 0.7 collective-permute-start.19
  114.9 1.4 collective-permute-start.23
  116.3 4.0 %all-to-all-start = ((bf16[8,64,128]{2,1,0:T(8,128)(2,1)}), bf16[8,64,128]{2,1,0:T(8,128)(2,1)S(1)}, u32[]{:S(2)}, u32[]{:S(2)}) async-start(bf16[8,64,128]{2,1,0:T(8,128)(2,1)} %get-tuple-element.79), calls=%async_computation | async-start | bytes 262144 | tf_op jit(solution)/shard_map/all_to_all | solution.py:553
  120.2 0.6 collective-permute-start.25
  120.9 2.3 %collective-permute-start.22 = (bf16[160,768]{1,0:T(8,128)(2,1)}, bf16[160,768]{1,0:T(8,128)(2,1)S(1)}, u32[]{:S(2)}, u32[]{:S(2)}) collective-permute-start(bf16[160,768]{1,0:T(8,128)(2,1)} %collective-permute-done.21), channel_id=1, source_target_pairs={{0,16},{4,20},{8,24},{12,28},{16,0},{20,4},{24,8},{28,12},{1,17},{... | collective-permute-start | bytes 737288 | tf_op jit(solution)/shard_map/ppermute | solution.py:545
  123.1 0.6 collective-permute-done.19
  123.7 4.5 %collective-permute-done.23 = bf16[160,768]{1,0:T(8,128)(2,1)} collective-permute-done((bf16[160,768]{1,0:T(8,128)(2,1)S(1)}, bf16[160,768]{1,0:T(8,128)(2,1)}, u32[]{:S(2)}, u32[]{:S(2)}) %collective-permute-start.23) | collective-permute-done | bytes 245792 | tf_op jit(solution)/shard_map/ppermute | solution.py:545
  128.3 0.4 collective-permute-start.24
  128.6 1.3 all-to-all-done.refs_1_
  129.9 0.7 collective-permute-start.15
  130.6 0.1 copy.19.refs_2_.refs_6_.refs_3_
  130.7 4.1 %collective-permute-done.15.refs_2_ = bf16[8,64,128]{2,1,0:T(8,128)(2,1)S(1)} collective-permute-done((bf16[8,64,128]{2,1,0:T(8,128)(2,1)S(1)}, bf16[8,64,128]{2,1,0:T(8,128)(2,1)S(1)}, u32[]{:S(2)}, u32[]{:S(2)}) %collective-permute-start.15) | collective-permute-done | bytes 131104 | tf_op jit(solution)/shard_map/ppermute | solution.py:539
  134.9 0.7 low_dense.1
  135.6 5.7 %first_grad.1 = (bf16[16,32,1024]{2,1,0:T(8,128)(2,1)}, f32[8,128]{1,0:T(8,128)}) custom-call(s32[3]{0:T(128)S(1)} %pad_add_fusion.refs_0_, s32[128,8]{1,0:T(8,128)S(1)} %copy.17.refs_1_.refs_5_.refs_2_, bf16[128,8]{1,0:T(8,128)(2,1)S(1)} %copy.19.refs_2_.refs_6_.refs_3_, f32[128,512]{1,0:T(8,128)S(1)} %get-tuple-element.87.refs_3_.refs_4_, ...), custom_call_target="tpu_custom_call" | custom-call | flops 1 | bytes 1 | tf_op jit(solution)/shard_map/first_grad/pallas_call | solution.py:53
  141.3 4.0 %collective-permute-done.24.refs_5_.refs_15_ = bf16[160,768]{1,0:T(8,128)(2,1)S(1)} collective-permute-done((bf16[160,768]{1,0:T(8,128)(2,1)}, bf16[160,768]{1,0:T(8,128)(2,1)S(1)}, u32[]{:S(2)}, u32[]{:S(2)}) %collective-permute-start.24) | collective-permute-done | bytes 245792 | tf_op jit(solution)/shard_map/ppermute | solution.py:545
  145.2 0.5 gate.1
  145.8 4.9 %all-to-all-start.1 = ((bf16[16,32,1024]{2,1,0:T(8,128)(2,1)}), bf16[16,32,1024]{2,1,0:T(8,128)(2,1)S(1)}, u32[]{:S(2)}, u32[]{:S(2)}) async-start(bf16[16,32,1024]{2,1,0:T(8,128)(2,1)} %get-tuple-element.99), calls=%async_computation.1 | async-start | bytes 2097152 | tf_op jit(solution)/shard_map/all_to_all | solution.py:553
  150.7 7.8 %finish.1 = (bf16[1024,768]{1,0:T(8,128)(2,1)}, f32[128,8]{1,0:T(8,128)S(1)}, f32[8,128]{1,0:T(8,128)}) custom-call(s32[3]{0:T(128)S(1)} %pad_add_fusion.refs_0_, s32[128,8]{1,0:T(8,128)S(1)} %copy.17.refs_1_.refs_5_.refs_2_, s32[128,8]{1,0:T(8,128)S(1)} %copy.17.refs_1_.refs_5_.refs_2_, bf16[128,8]{1,0:T(8,128)(2,1)S(1)} %copy.19.refs_2_.refs_6_.refs_3_, ...), custom_call_target="tpu_custom_call" | custom-call | flops 1 | bytes 20000000 | tf_op jit(solution)/shard_map/finish/pallas_call | solution.py:53
  158.5 16.4 %all-to-all-done.1.refs_1_ = bf16[16,32,1024]{2,1,0:T(8,128)(2,1)S(1)} async-done(((bf16[16,32,1024]{2,1,0:T(8,128)(2,1)}), bf16[16,32,1024]{2,1,0:T(8,128)(2,1)S(1)}, u32[]{:S(2)}, u32[]{:S(2)}) %all-to-all-start.1) | async-done | bytes 1048608 | tf_op jit(solution)/shard_map/all_to_all | solution.py:553
  174.9 4.4 %second_grad.1 = (f32[32,2048]{1,0:T(8,128)S(1)}, f32[32,2048]{1,0:T(8,128)S(1)}, f32[32,768]{1,0:T(8,128)}, f32[8,128]{1,0:T(8,128)}) custom-call(s32[3]{0:T(128)S(1)} %pad_add_fusion.refs_0_, bf16[16,32,1024]{2,1,0:T(8,128)(2,1)S(1)} %all-to-all-done.1.refs_1_, bf16[128,2304]{1,0:T(8,128)(2,1)} %copy-done, bf16[128,2304]{1,0:T(8,128)(2,1)} %copy-done.2, ...), custom_call_target="tpu_custom_call" | custom-call | flops 1 | bytes 1 | tf_op jit(solution)/shard_map/second_grad/pallas_call | solution.py:53
  179.3 0.8 collective-permute-start.27
  180.1 0.5 collective-permute-start.26
  180.6 3.7 %collective-permute-done.26 = f32[128,8]{1,0:T(8,128)S(1)} collective-permute-done((f32[128,8]{1,0:T(8,128)S(1)}, f32[128,8]{1,0:T(8,128)S(1)}, u32[]{:S(2)}, u32[]{:S(2)}) %collective-permute-start.26) | collective-permute-done | bytes 4128 | tf_op jit(solution)/shard_map/ppermute | solution.py:539
  184.4 0.7 copy.20
  185.0 0.7 add_bitcast_fusion
  (61 shorter events, 0.5 us)
Async XLA Ops:
  0.6 39.9 %collective-permute-start.2 = (bf16[1536,2048]{1,0:T(8,128)(2,1)}, bf16[1536,2048]{1,0:T(8,128)(2,1)}, u32[]{:S(2)}, u32[]{:S(2)}) collective-permute-start(bf16[1536,2048]{1,0:T(8,128)(2,1)} %bitcast.28), channel_id=1, source_target_pairs={{0,1},{1,0},{2,3},{3,2},{4,5},{5,4},{6,7},{7,6},{8,9},{9,8},{10,11... | collective-permute-start | bytes 18874376 | tf_op jit(solution)/shard_map/ppermute | solution.py:548
  0.8 0.8 copy-start.17
  1.6 0.7 copy-start.18
  3.4 45.3 %copy-start = (bf16[128,2304]{1,0:T(8,128)(2,1)}, bf16[128,2304]{1,0:T(8,128)(2,1)S(1)}, u32[]{:S(2)}) copy-start(bf16[128,2304]{1,0:T(8,128)(2,1)S(1)} %get-tuple-element.54.refs_1_.refs_5_.refs_2_) | copy-start | bytes 1769476
  3.4 28.5 %collective-permute-start.4 = (bf16[128,2304]{1,0:T(8,128)(2,1)S(1)}, bf16[128,2304]{1,0:T(8,128)(2,1)S(1)}, u32[]{:S(2)}, u32[]{:S(2)}) collective-permute-start(bf16[128,2304]{1,0:T(8,128)(2,1)S(1)} %get-tuple-element.54.refs_1_.refs_5_.refs_2_), channel_id=1, source_target_pairs={{0,16},{4,20},{8,24},{12,28},{16,0},{20,4},{24,8},{28,12},{1,17},{... | collective-permute-start | bytes 1769480 | tf_op jit(solution)/shard_map/ppermute | solution.py:545
  6.0 34.5 %collective-permute-start = (bf16[128,2304]{1,0:T(8,128)(2,1)S(1)}, bf16[128,2304]{1,0:T(8,128)(2,1)S(1)}, u32[]{:S(2)}, u32[]{:S(2)}) collective-permute-start(bf16[128,2304]{1,0:T(8,128)(2,1)S(1)} %get-tuple-element.54.refs_1_.refs_5_.refs_2_), channel_id=1, source_target_pairs={{0,4},{4,0},{8,12},{12,8},{16,20},{20,16},{24,28},{28,24},{1,5},{5... | collective-permute-start | bytes 1769480 | tf_op jit(solution)/shard_map/ppermute | solution.py:545
  7.6 42.7 %collective-permute-start.3 = (bf16[128,2304]{1,0:T(8,128)(2,1)S(1)}, bf16[128,2304]{1,0:T(8,128)(2,1)S(1)}, u32[]{:S(2)}, u32[]{:S(2)}) collective-permute-start(bf16[128,2304]{1,0:T(8,128)(2,1)S(1)} %get-tuple-element.54.refs_1_.refs_5_.refs_2_), channel_id=1, source_target_pairs={{0,8},{4,12},{8,0},{12,4},{16,24},{20,28},{24,16},{28,20},{1,9},{5... | collective-permute-start | bytes 1769480 | tf_op jit(solution)/shard_map/ppermute | solution.py:545
  31.9 18.9 %copy-start.1 = (bf16[128,2304]{1,0:T(8,128)(2,1)}, bf16[128,2304]{1,0:T(8,128)(2,1)S(1)}, u32[]{:S(2)}) copy-start(bf16[128,2304]{1,0:T(8,128)(2,1)S(1)} %collective-permute-done.4.refs_2_.refs_8_.refs_5_) | copy-start | bytes 1769476
  31.9 27.4 %collective-permute-start.5 = (bf16[128,2304]{1,0:T(8,128)(2,1)S(1)}, bf16[128,2304]{1,0:T(8,128)(2,1)S(1)}, u32[]{:S(2)}, u32[]{:S(2)}) collective-permute-start(bf16[128,2304]{1,0:T(8,128)(2,1)S(1)} %collective-permute-done.4.refs_2_.refs_8_.refs_5_), channel_id=1, source_target_pairs={{0,8},{4,12},{8,0},{12,4},{16,24},{20,28},{24,16},{28,20},{1,9},{5... | collective-permute-start | bytes 1769480 | tf_op jit(solution)/shard_map/ppermute | solution.py:545
  33.2 0.9 copy-start.16
  37.5 1.4 collective-permute-start.1
  39.0 25.2 %collective-permute-start.6 = (bf16[128,2304]{1,0:T(8,128)(2,1)S(1)}, bf16[128,2304]{1,0:T(8,128)(2,1)S(1)}, u32[]{:S(2)}, u32[]{:S(2)}) collective-permute-start(bf16[128,2304]{1,0:T(8,128)(2,1)S(1)} %collective-permute-done.4.refs_2_.refs_8_.refs_5_), channel_id=1, source_target_pairs={{0,4},{4,0},{8,12},{12,8},{16,20},{20,16},{24,28},{28,24},{1,5},{5... | collective-permute-start | bytes 1769480 | tf_op jit(solution)/shard_map/ppermute | solution.py:545
  40.5 8.2 %copy-start.2 = (bf16[128,2304]{1,0:T(8,128)(2,1)}, bf16[128,2304]{1,0:T(8,128)(2,1)S(1)}, u32[]{:S(2)}) copy-start(bf16[128,2304]{1,0:T(8,128)(2,1)S(1)} %collective-permute-done.refs_2_.refs_6_.refs_3_) | copy-start | bytes 1769476
  48.7 14.1 %collective-permute-start.7 = (bf16[320,768]{1,0:T(8,128)(2,1)S(1)}, bf16[320,768]{1,0:T(8,128)(2,1)S(1)}, u32[]{:S(2)}, u32[]{:S(2)}) collective-permute-start(bf16[320,768]{1,0:T(8,128)(2,1)S(1)} %get-tuple-element.63), channel_id=1, source_target_pairs={{0,2},{2,0},{1,3},{3,1},{4,6},{6,4},{5,7},{7,5},{8,10},{10,8},{9,1... | collective-permute-start | bytes 1474568 | tf_op jit(solution)/shard_map/ppermute | solution.py:539
  50.2 8.4 %copy-start.3 = (bf16[128,2304]{1,0:T(8,128)(2,1)}, bf16[128,2304]{1,0:T(8,128)(2,1)S(1)}, u32[]{:S(2)}) copy-start(bf16[128,2304]{1,0:T(8,128)(2,1)S(1)} %collective-permute-done.3.refs_1_.refs_7_.refs_4_) | copy-start | bytes 1769476
  50.3 28.5 %collective-permute-start.8 = (bf16[128,2304]{1,0:T(8,128)(2,1)S(1)}, bf16[128,2304]{1,0:T(8,128)(2,1)S(1)}, u32[]{:S(2)}, u32[]{:S(2)}) collective-permute-start(bf16[128,2304]{1,0:T(8,128)(2,1)S(1)} %collective-permute-done.3.refs_1_.refs_7_.refs_4_), channel_id=1, source_target_pairs={{0,4},{4,0},{8,12},{12,8},{16,20},{20,16},{24,28},{28,24},{1,5},{5... | collective-permute-start | bytes 1769480 | tf_op jit(solution)/shard_map/ppermute | solution.py:545
  58.7 15.4 %collective-permute-start.10 = (bf16[320,768]{1,0:T(8,128)(2,1)S(1)}, bf16[320,768]{1,0:T(8,128)(2,1)S(1)}, u32[]{:S(2)}, u32[]{:S(2)}) collective-permute-start(bf16[320,768]{1,0:T(8,128)(2,1)S(1)} %get-tuple-element.68), channel_id=1, source_target_pairs={{0,2},{2,0},{1,3},{3,1},{4,6},{6,4},{5,7},{7,5},{8,10},{10,8},{9,1... | collective-permute-start | bytes 1474568 | tf_op jit(solution)/shard_map/ppermute | solution.py:539
  59.2 13.2 %copy-start.4 = (bf16[128,2304]{1,0:T(8,128)(2,1)}, bf16[128,2304]{1,0:T(8,128)(2,1)S(1)}, u32[]{:S(2)}) copy-start(bf16[128,2304]{1,0:T(8,128)(2,1)S(1)} %collective-permute-done.5.refs_1_.refs_9_.refs_6_) | copy-start | bytes 1769476
  59.2 21.2 %collective-permute-start.9 = (bf16[128,2304]{1,0:T(8,128)(2,1)S(1)}, bf16[128,2304]{1,0:T(8,128)(2,1)S(1)}, u32[]{:S(2)}, u32[]{:S(2)}) collective-permute-start(bf16[128,2304]{1,0:T(8,128)(2,1)S(1)} %collective-permute-done.5.refs_1_.refs_9_.refs_6_), channel_id=1, source_target_pairs={{0,4},{4,0},{8,12},{12,8},{16,20},{20,16},{24,28},{28,24},{1,5},{5... | collective-permute-start | bytes 1769480 | tf_op jit(solution)/shard_map/ppermute | solution.py:545
  63.4 0.7 copy-start.15
  64.1 8.3 %copy-start.5 = (bf16[128,2304]{1,0:T(8,128)(2,1)}, bf16[128,2304]{1,0:T(8,128)(2,1)S(1)}, u32[]{:S(2)}) copy-start(bf16[128,2304]{1,0:T(8,128)(2,1)S(1)} %collective-permute-done.6.refs_2_.refs_10_.refs_7_) | copy-start | bytes 1769476
  72.5 25.0 %collective-permute-start.14 = (bf16[320,768]{1,0:T(8,128)(2,1)S(1)}, bf16[320,768]{1,0:T(8,128)(2,1)S(1)}, u32[]{:S(2)}, u32[]{:S(2)}) collective-permute-start(bf16[320,768]{1,0:T(8,128)(2,1)S(1)} %get-tuple-element.76), channel_id=1, source_target_pairs={{0,2},{2,0},{1,3},{3,1},{4,6},{6,4},{5,7},{7,5},{8,10},{10,8},{9,1... | collective-permute-start | bytes 1474568 | tf_op jit(solution)/shard_map/ppermute | solution.py:539
  74.8 8.2 %collective-permute-start.12 = (bf16[160,768]{1,0:T(8,128)(2,1)S(1)}, bf16[160,768]{1,0:T(8,128)(2,1)S(1)}, u32[]{:S(2)}, u32[]{:S(2)}) collective-permute-start(bf16[160,768]{1,0:T(8,128)(2,1)S(1)} %get-tuple-element.72), channel_id=1, source_target_pairs={{0,8},{4,12},{8,0},{12,4},{16,24},{20,28},{24,16},{28,20},{1,9},{5... | collective-permute-start | bytes 737288 | tf_op jit(solution)/shard_map/ppermute | solution.py:545
  75.4 12.1 %collective-permute-start.13 = (bf16[160,768]{1,0:T(8,128)(2,1)S(1)}, bf16[160,768]{1,0:T(8,128)(2,1)S(1)}, u32[]{:S(2)}, u32[]{:S(2)}) collective-permute-start(bf16[160,768]{1,0:T(8,128)(2,1)S(1)} %get-tuple-element.73), channel_id=1, source_target_pairs={{0,16},{4,20},{8,24},{12,28},{16,0},{20,4},{24,8},{28,12},{1,17},{... | collective-permute-start | bytes 737288 | tf_op jit(solution)/shard_map/ppermute | solution.py:545
  78.8 17.5 %copy-start.6 = (bf16[128,2304]{1,0:T(8,128)(2,1)}, bf16[128,2304]{1,0:T(8,128)(2,1)S(1)}, u32[]{:S(2)}) copy-start(bf16[128,2304]{1,0:T(8,128)(2,1)S(1)} %collective-permute-done.8.refs_1_.refs_11_.refs_8_) | copy-start | bytes 1769476
  78.8 8.7 %collective-permute-start.11 = (bf16[160,768]{1,0:T(8,128)(2,1)S(1)}, bf16[160,768]{1,0:T(8,128)(2,1)S(1)}, u32[]{:S(2)}, u32[]{:S(2)}) collective-permute-start(bf16[160,768]{1,0:T(8,128)(2,1)S(1)} %get-tuple-element.71), channel_id=1, source_target_pairs={{0,4},{4,0},{8,12},{12,8},{16,20},{20,16},{24,28},{28,24},{1,5},{5... | collective-permute-start | bytes 737288 | tf_op jit(solution)/shard_map/ppermute | solution.py:545
  80.4 15.9 %copy-start.7 = (bf16[128,2304]{1,0:T(8,128)(2,1)}, bf16[128,2304]{1,0:T(8,128)(2,1)S(1)}, u32[]{:S(2)}) copy-start(bf16[128,2304]{1,0:T(8,128)(2,1)S(1)} %collective-permute-done.9.refs_2_.refs_12_.refs_9_) | copy-start | bytes 1769476
  82.9 13.4 %copy-start.12 = (bf16[160,768]{1,0:T(8,128)(2,1)}, bf16[160,768]{1,0:T(8,128)(2,1)S(1)}, u32[]{:S(2)}) copy-start(bf16[160,768]{1,0:T(8,128)(2,1)S(1)} %collective-permute-done.12.refs_9_.refs_10_) | copy-start | bytes 737284
  87.5 8.8 %copy-start.13 = (bf16[160,768]{1,0:T(8,128)(2,1)}, bf16[160,768]{1,0:T(8,128)(2,1)S(1)}, u32[]{:S(2)}) copy-start(bf16[160,768]{1,0:T(8,128)(2,1)S(1)} %collective-permute-done.13.refs_10_.refs_12_) | copy-start | bytes 737284
  87.5 8.8 %copy-start.14 = (bf16[160,768]{1,0:T(8,128)(2,1)}, bf16[160,768]{1,0:T(8,128)(2,1)S(1)}, u32[]{:S(2)}) copy-start(bf16[160,768]{1,0:T(8,128)(2,1)S(1)} %collective-permute-done.11.refs_8_.refs_9_) | copy-start | bytes 737284
  87.5 12.7 %copy-start.19 = (s32[128,8]{0,1:T(8,128)S(1)}, s32[128,8]{0,1:T(8,128)}, u32[]{:S(2)}) copy-start(s32[128,8]{0,1:T(8,128)} %param.9) | copy-start | bytes 12292
  96.3 34.3 %copy-start.20 = (bf16[128,8]{0,1:T(8,128)(2,1)S(1)}, bf16[128,8]{0,1:T(8,128)(2,1)}, u32[]{:S(2)}) copy-start(bf16[128,8]{0,1:T(8,128)(2,1)} %param.10) | copy-start | bytes 6148
  96.3 17.2 %collective-permute-start.16 = (bf16[320,768]{1,0:T(8,128)(2,1)}, bf16[320,768]{1,0:T(8,128)(2,1)S(1)}, u32[]{:S(2)}, u32[]{:S(2)}) collective-permute-start(bf16[320,768]{1,0:T(8,128)(2,1)} %get-tuple-element.81), channel_id=1, source_target_pairs={{0,2},{2,0},{1,3},{3,1},{4,6},{6,4},{5,7},{7,5},{8,10},{10,8},{9,1... | collective-permute-start | bytes 1474568 | tf_op jit(solution)/shard_map/ppermute | solution.py:539
  99.9 2.0 %collective-permute-start.17 = (bf16[8,32,768]{2,1,0:T(8,128)(2,1)S(1)}, bf16[8,32,768]{2,1,0:T(8,128)(2,1)S(1)}, u32[]{:S(2)}, u32[]{:S(2)}) collective-permute-start(bf16[8,32,768]{2,1,0:T(8,128)(2,1)S(1)} %get-tuple-element.82), channel_id=1, source_target_pairs={{0,1},{1,0},{2,3},{3,2},{4,5},{5,4},{6,7},{7,6},{8,9},{9,8},{10,11... | collective-permute-start | bytes 1179656 | tf_op jit(solution)/shard_map/ppermute | solution.py:548
  99.9 13.6 %collective-permute-start.18 = (bf16[160,768]{1,0:T(8,128)(2,1)S(1)}, bf16[160,768]{1,0:T(8,128)(2,1)S(1)}, u32[]{:S(2)}, u32[]{:S(2)}) collective-permute-start(bf16[160,768]{1,0:T(8,128)(2,1)S(1)} %get-tuple-element.85), channel_id=1, source_target_pairs={{0,24},{4,28},{8,16},{12,20},{16,8},{20,12},{24,0},{28,4},{1,25},{... | collective-permute-start | bytes 737288 | tf_op jit(solution)/shard_map/ppermute | solution.py:545
  100.4 20.5 %collective-permute-start.21 = (bf16[160,768]{1,0:T(8,128)(2,1)S(1)}, bf16[160,768]{1,0:T(8,128)(2,1)}, u32[]{:S(2)}, u32[]{:S(2)}) collective-permute-start(bf16[160,768]{1,0:T(8,128)(2,1)S(1)} %get-tuple-element.90), channel_id=1, source_target_pairs={{0,4},{4,0},{8,12},{12,8},{16,20},{20,16},{24,28},{28,24},{1,5},{5... | collective-permute-start | bytes 737288 | tf_op jit(solution)/shard_map/ppermute | solution.py:545
  113.5 37.2 %copy-start.8 = (bf16[160,768]{1,0:T(8,128)(2,1)}, bf16[160,768]{1,0:T(8,128)(2,1)S(1)}, u32[]{:S(2)}) copy-start(bf16[160,768]{1,0:T(8,128)(2,1)S(1)} %collective-permute-done.18.refs_4_.refs_14_) | copy-start | bytes 737284
  114.2 9.6 %collective-permute-start.19 = (bf16[160,768]{1,0:T(8,128)(2,1)S(1)}, bf16[160,768]{1,0:T(8,128)(2,1)}, u32[]{:S(2)}, u32[]{:S(2)}) collective-permute-start(bf16[160,768]{1,0:T(8,128)(2,1)S(1)} %get-tuple-element.89), channel_id=1, source_target_pairs={{0,4},{4,0},{8,12},{12,8},{16,20},{20,16},{24,28},{28,24},{1,5},{5... | collective-permute-start | bytes 737288 | tf_op jit(solution)/shard_map/ppermute | solution.py:545
  114.9 13.4 %collective-permute-start.23 = (bf16[160,768]{1,0:T(8,128)(2,1)S(1)}, bf16[160,768]{1,0:T(8,128)(2,1)}, u32[]{:S(2)}, u32[]{:S(2)}) collective-permute-start(bf16[160,768]{1,0:T(8,128)(2,1)S(1)} %get-tuple-element.91), channel_id=1, source_target_pairs={{0,4},{4,0},{8,12},{12,8},{16,20},{20,16},{24,28},{28,24},{1,5},{5... | collective-permute-start | bytes 737288 | tf_op jit(solution)/shard_map/ppermute | solution.py:545
  116.3 13.6 %all-to-all-start = ((bf16[8,64,128]{2,1,0:T(8,128)(2,1)}), bf16[8,64,128]{2,1,0:T(8,128)(2,1)S(1)}, u32[]{:S(2)}, u32[]{:S(2)}) async-start(bf16[8,64,128]{2,1,0:T(8,128)(2,1)} %get-tuple-element.79), calls=%async_computation | async-start | bytes 262144 | tf_op jit(solution)/shard_map/all_to_all | solution.py:553
  120.2 15.3 %collective-permute-start.25 = (f32[128,512]{1,0:T(8,128)S(1)}, f32[128,512]{1,0:T(8,128)S(1)}, u32[]{:S(2)}, u32[]{:S(2)}) collective-permute-start(f32[128,512]{1,0:T(8,128)S(1)} %get-tuple-element.92.refs_7_), channel_id=1, source_target_pairs={{0,2},{2,0},{1,3},{3,1},{4,6},{6,4},{5,7},{7,5},{8,10},{10,8},{9,1... | collective-permute-start | bytes 786440 | tf_op jit(solution)/shard_map/ppermute | solution.py:539
  120.9 20.4 %collective-permute-start.22 = (bf16[160,768]{1,0:T(8,128)(2,1)}, bf16[160,768]{1,0:T(8,128)(2,1)S(1)}, u32[]{:S(2)}, u32[]{:S(2)}) collective-permute-start(bf16[160,768]{1,0:T(8,128)(2,1)} %collective-permute-done.21), channel_id=1, source_target_pairs={{0,16},{4,20},{8,24},{12,28},{16,0},{20,4},{24,8},{28,12},{1,17},{... | collective-permute-start | bytes 737288 | tf_op jit(solution)/shard_map/ppermute | solution.py:545
  123.7 17.5 %collective-permute-start.20 = (bf16[160,768]{1,0:T(8,128)(2,1)}, bf16[160,768]{1,0:T(8,128)(2,1)S(1)}, u32[]{:S(2)}, u32[]{:S(2)}) collective-permute-start(bf16[160,768]{1,0:T(8,128)(2,1)} %collective-permute-done.19), channel_id=1, source_target_pairs={{0,8},{4,12},{8,0},{12,4},{16,24},{20,28},{24,16},{28,20},{1,9},{5... | collective-permute-start | bytes 737288 | tf_op jit(solution)/shard_map/ppermute | solution.py:545
  128.3 17.0 %collective-permute-start.24 = (bf16[160,768]{1,0:T(8,128)(2,1)}, bf16[160,768]{1,0:T(8,128)(2,1)S(1)}, u32[]{:S(2)}, u32[]{:S(2)}) collective-permute-start(bf16[160,768]{1,0:T(8,128)(2,1)} %collective-permute-done.23), channel_id=1, source_target_pairs={{0,24},{4,28},{8,16},{12,20},{16,8},{20,12},{24,0},{28,4},{1,25},{... | collective-permute-start | bytes 737288 | tf_op jit(solution)/shard_map/ppermute | solution.py:545
  129.9 5.0 %collective-permute-start.15 = (bf16[8,64,128]{2,1,0:T(8,128)(2,1)S(1)}, bf16[8,64,128]{2,1,0:T(8,128)(2,1)S(1)}, u32[]{:S(2)}, u32[]{:S(2)}) collective-permute-start(bf16[8,64,128]{2,1,0:T(8,128)(2,1)S(1)} %all-to-all-done.refs_1_), channel_id=1, source_target_pairs={{0,2},{2,0},{1,3},{3,1},{4,6},{6,4},{5,7},{7,5},{8,10},{10,8},{9,1... | collective-permute-start | bytes 393224 | tf_op jit(solution)/shard_map/ppermute | solution.py:539
  141.2 9.5 %copy-start.9 = (bf16[160,768]{1,0:T(8,128)(2,1)}, bf16[160,768]{1,0:T(8,128)(2,1)S(1)}, u32[]{:S(2)}) copy-start(bf16[160,768]{1,0:T(8,128)(2,1)S(1)} %collective-permute-done.22.refs_3_.refs_13_) | copy-start | bytes 737284
  141.2 9.5 %copy-start.10 = (bf16[160,768]{1,0:T(8,128)(2,1)}, bf16[160,768]{1,0:T(8,128)(2,1)S(1)}, u32[]{:S(2)}) copy-start(bf16[160,768]{1,0:T(8,128)(2,1)S(1)} %collective-permute-done.20.refs_4_.refs_11_) | copy-start | bytes 737284
  145.2 5.5 %copy-start.11 = (bf16[160,768]{1,0:T(8,128)(2,1)}, bf16[160,768]{1,0:T(8,128)(2,1)S(1)}, u32[]{:S(2)}) copy-start(bf16[160,768]{1,0:T(8,128)(2,1)S(1)} %collective-permute-done.24.refs_5_.refs_15_) | copy-start | bytes 737284
  145.8 29.1 %all-to-all-start.1 = ((bf16[16,32,1024]{2,1,0:T(8,128)(2,1)}), bf16[16,32,1024]{2,1,0:T(8,128)(2,1)S(1)}, u32[]{:S(2)}, u32[]{:S(2)}) async-start(bf16[16,32,1024]{2,1,0:T(8,128)(2,1)} %get-tuple-element.99), calls=%async_computation.1 | async-start | bytes 2097152 | tf_op jit(solution)/shard_map/all_to_all | solution.py:553
  179.3 5.7 %collective-permute-start.27 = (f32[32,2048]{1,0:T(8,128)S(1)}, f32[32,2048]{1,0:T(8,128)S(1)}, u32[]{:S(2)}, u32[]{:S(2)}) collective-permute-start(f32[32,2048]{1,0:T(8,128)S(1)} %get-tuple-element.103), channel_id=1, source_target_pairs={{0,1},{1,0},{2,3},{3,2},{4,5},{5,4},{6,7},{7,6},{8,9},{9,8},{10,11... | collective-permute-start | bytes 786440 | tf_op jit(solution)/shard_map/ppermute | solution.py:548
  180.1 4.3 %collective-permute-start.26 = (f32[128,8]{1,0:T(8,128)S(1)}, f32[128,8]{1,0:T(8,128)S(1)}, u32[]{:S(2)}, u32[]{:S(2)}) collective-permute-start(f32[128,8]{1,0:T(8,128)S(1)} %get-tuple-element.98), channel_id=1, source_target_pairs={{0,2},{2,0},{1,3},{3,1},{4,6},{6,4},{5,7},{7,5},{8,10},{10,8},{9,1... | collective-permute-start | bytes 12296 | tf_op jit(solution)/shard_map/ppermute | solution.py:539

commit v13 on v12

--- a/solution.py
+++ b/solution.py
@@ -138,7 +138,7 @@
     )
 
 
-def load_kernel(at_ref, down_ref, second_ref, out_ref, same_ref, sems):
+def load_kernel(at_ref, down_ref, out_ref, sems):
     parts = sems.shape[0]
     rows = down_ref.shape[0] // parts
     copies = [
@@ -149,22 +149,21 @@
     ]
     for copy in copies:
         copy.start()
-    same_ref[...] = second_ref[...]
     for copy in copies:
         copy.wait()
 
 
-def load_call(order, down, second):
+def load_call(order, down):
     return order.call(
         load_kernel,
         "load_matrix",
-        [in_hbm(down), second],
-        [ANY, VMEM],
-        [pltpu.VMEM(down.shape, down.dtype), (second.shape, second.dtype)],
-        [VMEM, VMEM],
+        [in_hbm(down)],
+        [ANY],
+        [pltpu.VMEM(down.shape, down.dtype)],
+        [VMEM],
         grid=(),
         scratch=[pltpu.SemaphoreType.DMA((4,))],
-    )
+    )[0]
 
 
 def expert_rows_kernel(slots, tiles, shares, batch, route_row, at_ref, *rest):
@@ -360,7 +359,7 @@
 
     totals = [jnp.zeros((rank, tile), F32) for _ in outs]
     for o, grad_ref in zip(places, grads):
-        source = 2 * lax.bitwise_xor(at_ref[1], o) + at_ref[2]
+        source = lax.bitwise_xor(at_ref[1], o)
         scaled = jnp.concatenate(
             [got_ref[source, :, pl.ds(units + q * toks, toks)] for q in range(2)], axis=0
         )
@@ -388,11 +387,10 @@
 
 def first_grad_kernel(groups, steps, parts, at_ref, index_ref, prob_ref, low_ref, hid_ref, *rest):
     index_all_ref, prob_all_ref, hids = rest[0], rest[1], rest[2 : 2 + parts]
-    out_ref, sum_ref = rest[2 + parts :]
+    keep_ref, give_ref, scaled_ref, sum_ref = rest[2 + parts :]
     step = pl.program_id(0)
     top = index_ref.shape[1]
-    rank = out_ref.shape[1]
-    units = sum_ref.shape[1]
+    rank = keep_ref.shape[1]
     low = spread_pairs(low_ref[...], top)
     column = pair_column(relative(at_ref, index_ref[...], groups).astype(F32))
     keep = expert_mask(column, low.shape[1], rank)
@@ -421,23 +419,20 @@
             scale = jnp.where(expert == place[:, k : k + 1], prob[:, k : k + 1], scale)
         turned = (total * scale).T.astype(BF16)
         for o in range(groups):
-            for q in range(2):
-                at = (q * groups + o) * rank
-                to = 2 * lax.bitwise_xor(at_ref[1], o) + lax.bitwise_xor(at_ref[2], q)
-                out_ref[to, :, pl.ds(0, units)] = sum_ref[pl.ds(at, rank), :].astype(BF16)
-                if q:
-                    out_ref[to, :, pl.ds(units, 2 * toks)] = jnp.zeros((rank, 2 * toks), BF16)
-                else:
-                    for p in range(2):
-                        rows = turned[(p * groups + o) * rank : (p * groups + o + 1) * rank]
-                        out_ref[to, :, pl.ds(units + p * toks, toks)] = rows
+            to = lax.bitwise_xor(at_ref[1], o)
+            at, other = o * rank, (groups + o) * rank
+            keep_ref[to] = sum_ref[pl.ds(at, rank), :]
+            give_ref[to] = sum_ref[pl.ds(other, rank), :].astype(BF16)
+            scaled_ref[to, :, pl.ds(0, toks)] = turned[at : at + rank]
+            scaled_ref[to, :, pl.ds(toks, toks)] = turned[other : other + rank]
 
 
 def first_grad_call(order, index, prob, low, hid, hids, groups):
     (toks, top), (pairs, units) = index.shape, hid.shape
     width = low.shape[1]
     steps = 4
-    shape = (2 * groups, width // groups // 2, units + 2 * toks)
+    rank = width // groups // 2
+    shape, scaled_shape = (groups, rank, units), (groups, rank, 2 * toks)
     return order.call(
         functools.partial(first_grad_kernel, groups, steps, len(hids)),
         "first_grad",
@@ -451,10 +446,28 @@
             whole(prob.shape),
         ]
         + [whole(x.shape) for x in hids],
+        [(shape, F32), (shape, BF16), (scaled_shape, BF16)],
+        [whole(shape), whole(shape), whole(scaled_shape)],
+        grid=(steps,),
+        scratch=[pltpu.VMEM((width, units), F32)],
+    )
+
+
+def first_sum_kernel(at_ref, keep_ref, got_ref, scaled_ref, out_ref):
+    units = keep_ref.shape[2]
+    out_ref[:, :, pl.ds(0, units)] = (keep_ref[...] + got_ref[...].astype(F32)).astype(BF16)
+    out_ref[:, :, pl.ds(units, scaled_ref.shape[2])] = scaled_ref[...]
+
+
+def first_sum_call(order, keep, got, scaled):
+    shape = keep.shape[:2] + (keep.shape[2] + scaled.shape[2],)
+    return order.call(
+        first_sum_kernel,
+        "first_sum",
+        [keep, got, scaled],
+        [whole(x.shape) for x in (keep, got, scaled)],
         [(shape, BF16)],
         [whole(shape)],
-        grid=(steps,),
-        scratch=[pltpu.VMEM((width, units), F32)],
     )[0]
 
 
@@ -560,57 +573,78 @@
             blocks[o] = flip(fetch(o ^ last), last)
         return blocks[o]
 
-    own_down, own_second = load_call(order, down[0], second[0])
+    own_down = load_call(order, down[0])
     downs = [own_down, swap(down[0])]
-    seconds = [own_second, swap(own_second)]
+    seconds = [second[0], swap(second[0])]
 
     if groups == 8:
-        batches = [(0, 1), (2, 4), (6, 5), (3, 7)]
+        batches = [(0, 1), (2, 4), (6, 3), (5, 7)]
+        steps = [("multiply", 0), ("gate", 4), ("multiply", 1), ("total", 0), ("total", 1)]
+        steps += [("multiply", 2), ("multiply", 3), ("total", 2)]
+        early = {("total", 0): 3, ("multiply", 2): 5}
     else:
         batches = [(o, o + 1) for o in range(0, groups, 2)]
+        steps = [("multiply", 0)]
+        for i in range(1, len(batches)):
+            steps += [("multiply", i), ("total", i - 1)]
+        early = {}
+    last = len(batches) - 1
     places = [o for batch in batches for o in batch]
-    back, lows, waiting = {}, [], []
+    back, lows, shared = {}, [], {}
 
     def arrived(i):
         order.wait([back[o] for o in batches[i] if o])
 
-    def send_back(batch, parts):
-        for o, rows in zip(batch, share_sum_call(order, parts, 2, slots)):
-            if batch in batches[-2:] and o > 1 and o % 2:
-                back[o] = flip(flip(rows, 1), o - 1)
-            else:
-                back[o] = flip(rows, o) if o else rows
-
-    for i, batch in enumerate(batches):
-        if i > 1 and i == len(batches) - 1:
-            for j in range(i - 1):
-                arrived(j)
-        *give, keep, low = expert_rows_call(
-            order, [fetch(o) for o in batch], seconds, downs, shares, slots
-        )
-        lows.append(low)
-        if i > 0:
-            send_back(*waiting)
-        waiting = (batch, [keep] + [turn(x, k + 1) for k, x in enumerate(give)])
+    def total(i):
+        for o, rows in zip(batches[i], share_sum_call(order, shared[i], 2, slots)):
+            masks = [o] if o else []
+            if i >= last - 1 and o % 2:
+                masks = [1 << k for k in range(o.bit_length()) if o >> k & 1]
+            for mask in masks:
+                rows = flip(rows, mask)
+            back[o] = rows
+
+    for kind, i in steps:
+        if (kind, i) in early:
+            order.wait([fetch(early[kind, i])])
+        if kind == "gate":
+            blocks[i] = gate_call(order, [fetch(i)])[0]
+        elif kind == "total":
+            total(i)
+        else:
+            if i == last and last > 2:
+                for j in range(i - 1):
+                    arrived(j)
+            *give, keep, low = expert_rows_call(
+                order, [fetch(o) for o in batches[i]], seconds, downs, shares, slots
+            )
+            lows.append(low)
+            shared[i] = [keep] + [turn(x, k + 1) for k, x in enumerate(give)]
 
     hid = hidden.reshape(pairs, units)
     grads = [blocks[o] for o in places]
 
     low_grad, first_own = collect_call(order, places, lows, grads, feats)
     firsts = [x.reshape(groups * rank, units) for x in (first_own, swap(first_own))]
-    low_grad = all_shares(exchange(low_grad))
+    low_grad = exchange(low_grad)
     low_hid = all_shares(lowrank_hid_call(order, index, hid, firsts, groups))
-    order.wait([back[batches[-2][0]]])
-    send_back(*waiting)
-
-    low_grad = low_dense_call(order, low_grad)
-    parts = first_grad_call(order, index, weight, low_grad, hid, low_hid, groups)
-
-    order.wait([back[batches[-2][1]], back[batches[-1][0]], back[batches[-1][1]]])
-    got = exchange(gate_call(order, [parts])[0], where)
+    order.wait([back[batches[-2][0]], low_grad])
+    total(last)
+
+    low_grad = low_dense_call(order, all_shares(low_grad))
+    order.wait([back[batches[-1][0]]])
+    keep, give, scaled = first_grad_call(order, index, weight, low_grad, hid, low_hid, groups)
+
+    order.wait([back[batches[-2][1]], back[batches[-1][1]]])
+    got = exchange(first_sum_call(order, keep, swap(give), scaled))
     back = [back[o] for o in range(groups)]
     grad_hidden, sums = finish_call(order, index, weight, low_grad, hid, firsts, back)
-    sums = sums + turn(sums, 1) if shares == 2 else lax.psum(sums, "rep")
+    if shares == 2:
+        other_sums = turn(sums, 1)
+        order.wait([other_sums])
+        sums = sums + other_sums
+    else:
+        sums = lax.psum(sums, "rep")
     second_keep, second_give, first_grad = second_grad_call(
         order, places, got, grads, units, feats
     )

time: 187 us -> 185 us (0.989); the launches traced: 186 us -> 182 us
  waiting for transfers between devices: 78 us -> 65.8 us
  starting transfers between devices: 37.3 us -> 45.6 us
    all_to_all x2, waiting for transfers between devices: 17.6 us -> 6.3 us  [exchange(): return lax.all_to_all(x, axes, split_axis=0, concat_axis=0, tiled=True)]
    all_to_all x2, starting transfers between devices: 8.86 us -> 13.2 us  [exchange(): return lax.all_to_all(x, axes, split_axis=0, concat_axis=0, tiled=True)]
    ppermute x17 -> x18, starting transfers between devices: 20.8 us -> 23.5 us  [flip(): return lax.ppermute(x, 'ep', [(i, i ^ mask) for i in range(groups)])]
    ppermute x7, starting transfers between devices: 6.73 us -> 8.72 us  [turn(): lax.ppermute(x, 'rep', [(r, (r + offset) % shares) for r in range(shares)])]
    unnamed x45 -> x47, local copies, waits for them, and re-layouts: 4.03 us -> 2.46 us
    pallas_call x17 -> x18, Pallas kernels: 64.6 us -> 65.9 us  [call(): pl.pallas_call(ordered, grid=grid, in_specs=[SMEM, *in_specs] + [ANY] * l...]
    ppermute x17 -> x18, waiting for transfers between devices: 49.2 us -> 48.6 us  [flip(): return lax.ppermute(x, 'ep', [(i, i ^ mask) for i in range(groups)])]
  transfers between devices with their start and end apart: 30 -> 32, of which waited for: 14 -> 16; matrix products, arithmetic and copies ran while one was open for 1% -> 1% of each run, Pallas kernels for 32% -> 33%
where the time goes in v13:
time: 185 us; the launch traced here: 182 us
  Pallas kernels  65.9 us (36%)
  waiting for transfers between devices  65.8 us (36%)
  starting transfers between devices  45.6 us (25%)
  local copies, waits for them, and re-layouts  2.46 us (1%)
    pallas_call x18, Pallas kernels, call(): pl.pallas_call(ordered, grid=grid, in_specs=[SMEM, *in_specs] + [ANY] * l...  65.9 us
    ppermute x18, waiting for transfers between devices, flip(): return lax.ppermute(x, 'ep', [(i, i ^ mask) for i in range(groups)])  48.6 us
    ppermute x18, starting transfers between devices, flip(): return lax.ppermute(x, 'ep', [(i, i ^ mask) for i in range(groups)])  23.5 us
    all_to_all x2, starting transfers between devices, exchange(): return lax.all_to_all(x, axes, split_axis=0, concat_axis=0, tiled=True)  13.2 us
    ppermute x7, waiting for transfers between devices, turn(): lax.ppermute(x, 'rep', [(r, (r + offset) % shares) for r in range(shares)])  10 us
    ppermute x7, starting transfers between devices, turn(): lax.ppermute(x, 'rep', [(r, (r + offset) % shares) for r in range(shares)])  8.72 us
    all_to_all x2, waiting for transfers between devices, exchange(): return lax.all_to_all(x, axes, split_axis=0, concat_axis=0, tiled=True)  6.3 us
  transfers between devices with their start and end apart: 32, of which 16 were waited for; matrix products, arithmetic and copies ran while one was open for 1% of the time, Pallas kernels for 33%

profile of v13, /device:TPU:8, one launch (start us, length us, event | category | flops | bytes accessed | tf_op | source)
XLA Modules:
  0.0 181.6 jit_solution(11219294788083206826)
XLA Ops:
  0.8 0.8 copy-done.18
  1.6 0.7 copy-done.19
  2.3 1.1 pack_block.1
  3.4 1.6 collective-permute-start
  5.0 2.6 %collective-permute-start.4 = (bf16[128,2304]{1,0:T(8,128)(2,1)S(1)}, bf16[128,2304]{1,0:T(8,128)(2,1)S(1)}, u32[]{:S(2)}, u32[]{:S(2)}) collective-permute-start(bf16[128,2304]{1,0:T(8,128)(2,1)S(1)} %get-tuple-element.57.refs_1_.refs_5_.refs_2_), channel_id=1, source_target_pairs={{0,16},{4,20},{8,24},{12,28},{16,0},{20,4},{24,8},{28,12},{1,17},{... | collective-permute-start | bytes 1769480 | tf_op jit(solution)/shard_map/ppermute | solution.py:558
  7.6 0.4 collective-permute-start.3
  8.0 3.4 %load_matrix.1 = (bf16[1536,2048]{1,0:T(8,128)(2,1)S(1)}, f32[8,128]{1,0:T(8,128)}) custom-call(s32[3]{0:T(128)S(1)} %pad_add_fusion.refs_0_, bf16[1536,2048]{1,0:T(8,128)(2,1)} %bitcast.33, f32[8,128]{1,0:T(8,128)} %get-tuple-element.58.refs_2_), custom_call_target="tpu_custom_call" | custom-call | flops 1 | bytes 1 | tf_op jit(solution)/shard_map/load_matrix/pallas_call | solution.py:53
  11.5 7.7 %collective-permute-done.refs_2_.refs_6_.refs_3_ = bf16[128,2304]{1,0:T(8,128)(2,1)S(1)} collective-permute-done((bf16[128,2304]{1,0:T(8,128)(2,1)S(1)}, bf16[128,2304]{1,0:T(8,128)(2,1)S(1)}, u32[]{:S(2)}, u32[]{:S(2)}) %collective-permute-start) | collective-permute-done | bytes 589856 | tf_op jit(solution)/shard_map/ppermute | solution.py:558
  19.2 8.2 %expert_rows.4 = (bf16[320,768]{1,0:T(8,128)(2,1)S(1)}, bf16[320,768]{1,0:T(8,128)(2,1)S(1)}, bf16[2,64,128]{2,1,0:T(8,128)(2,1)S(1)}, f32[8,128]{1,0:T(8,128)}) custom-call(s32[3]{0:T(128)S(1)} %pad_add_fusion.refs_0_, bf16[128,2304]{1,0:T(8,128)(2,1)S(1)} %get-tuple-element.57.refs_1_.refs_5_.refs_2_, ...), custom_call_target="tpu_custom_call" | custom-call | flops 1 | bytes 1 | tf_op jit(solution)/shard_map/expert_rows/pallas_call | solution.py:53
  27.4 5.7 %collective-permute-done.4.refs_1_ = bf16[128,2304]{1,0:T(8,128)(2,1)S(1)} collective-permute-done((bf16[128,2304]{1,0:T(8,128)(2,1)S(1)}, bf16[128,2304]{1,0:T(8,128)(2,1)S(1)}, u32[]{:S(2)}, u32[]{:S(2)}) %collective-permute-start.4) | collective-permute-done | bytes 589856 | tf_op jit(solution)/shard_map/ppermute | solution.py:558
  33.1 0.5 gate.1
  33.6 1.5 collective-permute-start.5
  35.1 0.5 collective-permute-start.6
  35.6 1.6 collective-permute-start.9
  37.2 1.5 collective-permute-start.8
  38.7 7.9 %expert_rows.5 = (bf16[320,768]{1,0:T(8,128)(2,1)S(1)}, bf16[320,768]{1,0:T(8,128)(2,1)S(1)}, bf16[2,64,128]{2,1,0:T(8,128)(2,1)S(1)}, f32[8,128]{1,0:T(8,128)}) custom-call(s32[3]{0:T(128)S(1)} %pad_add_fusion.refs_0_, bf16[128,2304]{1,0:T(8,128)(2,1)S(1)} %collective-permute-done.3.refs_1_.refs_7_.refs_4_, ...), custom_call_target="tpu_custom_call" | custom-call | flops 1 | bytes 1 | tf_op jit(solution)/shard_map/expert_rows/pallas_call | solution.py:53
  46.6 0.6 collective-permute-start.7
  47.2 1.8 collective-permute-done.5.refs_1_.refs_9_.refs_6_
  49.0 0.5 collective-permute-start.10
  49.5 1.9 %collective-permute-done.6.refs_4_.refs_2_.refs_10_.refs_7_ = bf16[128,2304]{1,0:T(8,128)(2,1)S(1)} collective-permute-done((bf16[128,2304]{1,0:T(8,128)(2,1)S(1)}, bf16[128,2304]{1,0:T(8,128)(2,1)S(1)}, u32[]{:S(2)}, u32[]{:S(2)}) %collective-permute-start.6) | collective-permute-done | bytes 589856 | tf_op jit(solution)/shard_map/ppermute | solution.py:558
  51.4 0.7 share_sum.4
  52.1 7.2 %collective-permute-done.7.refs_2_ = bf16[320,768]{1,0:T(8,128)(2,1)S(1)} collective-permute-done((bf16[320,768]{1,0:T(8,128)(2,1)S(1)}, bf16[320,768]{1,0:T(8,128)(2,1)S(1)}, u32[]{:S(2)}, u32[]{:S(2)}) %collective-permute-start.7) | collective-permute-done | bytes 491552 | tf_op jit(solution)/shard_map/ppermute | solution.py:552
  59.3 0.7 share_sum.5
  60.0 4.1 %collective-permute-done.9.refs_8_.refs_1_.refs_11_ = bf16[128,2304]{1,0:T(8,128)(2,1)S(1)} collective-permute-done((bf16[128,2304]{1,0:T(8,128)(2,1)S(1)}, bf16[128,2304]{1,0:T(8,128)(2,1)S(1)}, u32[]{:S(2)}, u32[]{:S(2)}) %collective-permute-start.9) | collective-permute-done | bytes 589856 | tf_op jit(solution)/shard_map/ppermute | solution.py:558
  64.1 8.3 %expert_rows.6 = (bf16[320,768]{1,0:T(8,128)(2,1)S(1)}, bf16[320,768]{1,0:T(8,128)(2,1)S(1)}, bf16[2,64,128]{2,1,0:T(8,128)(2,1)S(1)}, f32[8,128]{1,0:T(8,128)}) custom-call(s32[3]{0:T(128)S(1)} %pad_add_fusion.refs_0_, bf16[128,2304]{1,0:T(8,128)(2,1)S(1)} %collective-permute-done.5.refs_1_.refs_9_.refs_6_, ...), custom_call_target="tpu_custom_call" | custom-call | flops 1 | bytes 1 | tf_op jit(solution)/shard_map/expert_rows/pallas_call | solution.py:53
  72.4 1.6 collective-permute-start.14
  73.9 0.5 collective-permute-start.12
  74.5 3.4 %collective-permute-start.13 = (bf16[160,768]{1,0:T(8,128)(2,1)S(1)}, bf16[160,768]{1,0:T(8,128)(2,1)S(1)}, u32[]{:S(2)}, u32[]{:S(2)}) collective-permute-start(bf16[160,768]{1,0:T(8,128)(2,1)S(1)} %get-tuple-element.77), channel_id=1, source_target_pairs={{0,16},{4,20},{8,24},{12,28},{16,0},{20,4},{24,8},{28,12},{1,17},{... | collective-permute-start | bytes 737288 | tf_op jit(solution)/shard_map/ppermute | solution.py:558
  77.9 0.5 collective-permute-start.11
  78.4 3.2 %collective-permute-done.12.refs_9_.refs_10_ = bf16[160,768]{1,0:T(8,128)(2,1)S(1)} collective-permute-done((bf16[160,768]{1,0:T(8,128)(2,1)S(1)}, bf16[160,768]{1,0:T(8,128)(2,1)S(1)}, u32[]{:S(2)}, u32[]{:S(2)}) %collective-permute-start.12) | collective-permute-done | bytes 245792 | tf_op jit(solution)/shard_map/ppermute | solution.py:558
  81.5 4.8 %collective-permute-done.13.refs_10_.refs_12_ = bf16[160,768]{1,0:T(8,128)(2,1)S(1)} collective-permute-done((bf16[160,768]{1,0:T(8,128)(2,1)S(1)}, bf16[160,768]{1,0:T(8,128)(2,1)S(1)}, u32[]{:S(2)}, u32[]{:S(2)}) %collective-permute-start.13) | collective-permute-done | bytes 245792 | tf_op jit(solution)/shard_map/ppermute | solution.py:558
  86.4 8.9 %expert_rows.7 = (bf16[320,768]{1,0:T(8,128)(2,1)}, bf16[320,768]{1,0:T(8,128)(2,1)S(1)}, bf16[2,64,128]{2,1,0:T(8,128)(2,1)S(1)}, f32[8,128]{1,0:T(8,128)}) custom-call(s32[3]{0:T(128)S(1)} %pad_add_fusion.refs_0_, bf16[128,2304]{1,0:T(8,128)(2,1)S(1)} %collective-permute-done.9.refs_8_.refs_1_.refs_11_, ...), custom_call_target="tpu_custom_call" | custom-call | flops 1 | bytes 1 | tf_op jit(solution)/shard_map/expert_rows/pallas_call | solution.py:53
  95.4 0.6 collective-permute-start.16
  96.0 1.3 share_sum.6
  97.3 1.8 collect_blocks.1
  99.0 7.4 %all-to-all-start = ((bf16[8,64,128]{2,1,0:T(8,128)(2,1)}), bf16[8,64,128]{2,1,0:T(8,128)(2,1)S(1)}, u32[]{:S(2)}, u32[]{:S(2)}) async-start(bf16[8,64,128]{2,1,0:T(8,128)(2,1)} %get-tuple-element.83), calls=%async_computation | async-start | bytes 262144 | tf_op jit(solution)/shard_map/all_to_all | solution.py:566
  106.6 3.6 %lowrank_hid.1 = (f32[128,512]{1,0:T(8,128)S(1)}, f32[8,128]{1,0:T(8,128)}) custom-call(s32[3]{0:T(128)S(1)} %pad_add_fusion.refs_0_, s32[128,8]{1,0:T(8,128)S(1)} %copy.17.refs_1_.refs_5_.refs_2_, bf16[1024,768]{1,0:T(8,128)(2,1)} %bitcast.29, bf16[256,768]{1,0:T(8,128)(2,1)S(1)} %bitcast.23, bf16[256,768]{1,0:T(8,128)(2,1)S(1)} %bitcast.25, ...), custom_call_target="tpu_custom_call" | custom-call | flops 1 | bytes 1 | tf_op jit(solution)/shard_map/lowrank_hid/pallas_call | solution.py:53
  110.1 5.1 %all-to-all-done.refs_5_.refs_1_ = bf16[8,64,128]{2,1,0:T(8,128)(2,1)S(1)} async-done(((bf16[8,64,128]{2,1,0:T(8,128)(2,1)}), bf16[8,64,128]{2,1,0:T(8,128)(2,1)S(1)}, u32[]{:S(2)}, u32[]{:S(2)}) %all-to-all-start) | async-done | bytes 131104 | tf_op jit(solution)/shard_map/all_to_all | solution.py:566
  115.3 0.7 share_sum.7
  115.9 1.1 collective-permute-start.21
  117.0 1.0 collective-permute-start.23
  118.0 1.5 collective-permute-start.26
  119.5 5.5 %collective-permute-done.21 = bf16[160,768]{1,0:T(8,128)(2,1)} collective-permute-done((bf16[160,768]{1,0:T(8,128)(2,1)S(1)}, bf16[160,768]{1,0:T(8,128)(2,1)}, u32[]{:S(2)}, u32[]{:S(2)}) %collective-permute-start.21) | collective-permute-done | bytes 245792 | tf_op jit(solution)/shard_map/ppermute | solution.py:558
  125.0 1.4 collective-permute-start.22
  126.4 1.5 collective-permute-start.15
  127.9 1.3 collective-permute-start.19
  129.2 2.6 %collective-permute-start.24 = (bf16[160,768]{1,0:T(8,128)(2,1)S(1)}, bf16[160,768]{1,0:T(8,128)(2,1)S(1)}, u32[]{:S(2)}, u32[]{:S(2)}) collective-permute-start(bf16[160,768]{1,0:T(8,128)(2,1)S(1)} %collective-permute-done.23), channel_id=1, source_target_pairs={{0,8},{4,12},{8,0},{12,4},{16,24},{20,28},{24,16},{28,20},{1,9},{5... | collective-permute-start | bytes 737288 | tf_op jit(solution)/shard_map/ppermute | solution.py:558
  132.0 0.7 low_dense.1
  132.7 2.2 %collective-permute-done.22.refs_10_.refs_13_ = bf16[160,768]{1,0:T(8,128)(2,1)S(1)} collective-permute-done((bf16[160,768]{1,0:T(8,128)(2,1)}, bf16[160,768]{1,0:T(8,128)(2,1)S(1)}, u32[]{:S(2)}, u32[]{:S(2)}) %collective-permute-start.22) | collective-permute-done | bytes 245792 | tf_op jit(solution)/shard_map/ppermute | solution.py:558
  134.8 4.7 %first_grad.1 = (f32[8,32,768]{2,1,0:T(8,128)S(1)}, bf16[8,32,768]{2,1,0:T(8,128)(2,1)S(1)}, bf16[8,32,256]{2,1,0:T(8,128)(2,1)S(1)}, f32[8,128]{1,0:T(8,128)}) custom-call(s32[3]{0:T(128)S(1)} %pad_add_fusion.refs_0_, s32[128,8]{1,0:T(8,128)S(1)} %copy.17.refs_1_.refs_5_.refs_2_, bf16[128,8]{1,0:T(8,128)(2,1)S(1)} %copy.19.refs_2_.refs_6_.refs_3_, ...), custom_call_target="tpu_custom_call" | custom-call | flops 1 | bytes 1 | tf_op jit(solution)/shard_map/first_grad/pallas_call | solution.py:53
  139.7 2.6 %collective-permute-start.20 = (bf16[160,768]{1,0:T(8,128)(2,1)S(1)}, bf16[160,768]{1,0:T(8,128)(2,1)S(1)}, u32[]{:S(2)}, u32[]{:S(2)}) collective-permute-start(bf16[160,768]{1,0:T(8,128)(2,1)S(1)} %collective-permute-done.19), channel_id=1, source_target_pairs={{0,8},{4,12},{8,0},{12,4},{16,24},{20,28},{24,16},{28,20},{1,9},{5... | collective-permute-start | bytes 737288 | tf_op jit(solution)/shard_map/ppermute | solution.py:558
  142.2 0.4 collective-permute-start.25
  142.6 9.8 %collective-permute-done.20.refs_5_.refs_11_ = bf16[160,768]{1,0:T(8,128)(2,1)S(1)} collective-permute-done((bf16[160,768]{1,0:T(8,128)(2,1)S(1)}, bf16[160,768]{1,0:T(8,128)(2,1)S(1)}, u32[]{:S(2)}, u32[]{:S(2)}) %collective-permute-start.20) | collective-permute-done | bytes 245792 | tf_op jit(solution)/shard_map/ppermute | solution.py:558
  152.4 2.0 %collective-permute-done.25.refs_6_.refs_15_ = bf16[160,768]{1,0:T(8,128)(2,1)S(1)} collective-permute-done((bf16[160,768]{1,0:T(8,128)(2,1)S(1)}, bf16[160,768]{1,0:T(8,128)(2,1)S(1)}, u32[]{:S(2)}, u32[]{:S(2)}) %collective-permute-start.25) | collective-permute-done | bytes 245792 | tf_op jit(solution)/shard_map/ppermute | solution.py:558
  154.4 1.4 first_sum.1
  155.9 5.8 %all-to-all-start.1 = ((bf16[8,32,1024]{2,1,0:T(8,128)(2,1)}), bf16[8,32,1024]{2,1,0:T(8,128)(2,1)S(1)}, u32[]{:S(2)}, u32[]{:S(2)}) async-start(bf16[8,32,1024]{2,1,0:T(8,128)(2,1)} %get-tuple-element.105), calls=%async_computation.1 | async-start | bytes 1048576 | tf_op jit(solution)/shard_map/all_to_all | solution.py:566
  161.7 7.8 %finish.1 = (bf16[1024,768]{1,0:T(8,128)(2,1)}, f32[128,8]{1,0:T(8,128)S(1)}, f32[8,128]{1,0:T(8,128)}) custom-call(s32[3]{0:T(128)S(1)} %pad_add_fusion.refs_0_, s32[128,8]{1,0:T(8,128)S(1)} %copy.17.refs_1_.refs_5_.refs_2_, s32[128,8]{1,0:T(8,128)S(1)} %copy.17.refs_1_.refs_5_.refs_2_, bf16[128,8]{1,0:T(8,128)(2,1)S(1)} %copy.19.refs_2_.refs_6_.refs_3_, ...), custom_call_target="tpu_custom_call" | custom-call | flops 1 | bytes 20000000 | tf_op jit(solution)/shard_map/finish/pallas_call | solution.py:53
  169.5 1.5 collective-permute-start.28
  171.0 2.8 %collective-permute-done.28.refs_11_ = f32[128,8]{1,0:T(8,128)S(1)} collective-permute-done((f32[128,8]{1,0:T(8,128)S(1)}, f32[128,8]{1,0:T(8,128)S(1)}, u32[]{:S(2)}, u32[]{:S(2)}) %collective-permute-start.28) | collective-permute-done | bytes 4128 | tf_op jit(solution)/shard_map/ppermute | solution.py:552
  173.8 1.2 all-to-all-done.1.refs_1_
  175.0 4.4 %second_grad.1 = (f32[32,2048]{1,0:T(8,128)S(1)}, f32[32,2048]{1,0:T(8,128)S(1)}, f32[32,768]{1,0:T(8,128)}, f32[8,128]{1,0:T(8,128)}) custom-call(s32[3]{0:T(128)S(1)} %pad_add_fusion.refs_0_, bf16[8,32,1024]{2,1,0:T(8,128)(2,1)S(1)} %all-to-all-done.1.refs_1_, bf16[128,2304]{1,0:T(8,128)(2,1)} %copy-done.3, bf16[128,2304]{1,0:T(8,128)(2,1)} %copy-done.4, ...), custom_call_target="tpu_custom_call" | custom-call | flops 1 | bytes 1 | tf_op jit(solution)/shard_map/second_grad/pallas_call | solution.py:53
  179.4 0.7 copy.20
  180.0 0.8 collective-permute-done.29
  180.9 0.7 add_bitcast_fusion
  (68 shorter events, 0.6 us)
Async XLA Ops:
  0.6 18.6 %copy-start.8 = (bf16[1,32,2048]{2,1,0:T(8,128)(2,1)S(1)}, bf16[1,32,2048]{2,1,0:T(8,128)(2,1)}, u32[]{:S(2)}) copy-start(bf16[1,32,2048]{2,1,0:T(8,128)(2,1)} %param.13) | copy-start | bytes 393220
  0.6 18.6 %collective-permute-start.2 = (bf16[1536,2048]{1,0:T(8,128)(2,1)}, bf16[1536,2048]{1,0:T(8,128)(2,1)}, u32[]{:S(2)}, u32[]{:S(2)}) collective-permute-start(bf16[1536,2048]{1,0:T(8,128)(2,1)} %bitcast.32), channel_id=1, source_target_pairs={{0,1},{1,0},{2,3},{3,2},{4,5},{5,4},{6,7},{7,6},{8,9},{9,8},{10,11... | collective-permute-start | bytes 18874376 | tf_op jit(solution)/shard_map/ppermute | solution.py:561
  0.8 0.8 copy-start.18
  1.6 0.7 copy-start.19
  3.4 24.0 %copy-start.3 = (bf16[128,2304]{1,0:T(8,128)(2,1)}, bf16[128,2304]{1,0:T(8,128)(2,1)S(1)}, u32[]{:S(2)}) copy-start(bf16[128,2304]{1,0:T(8,128)(2,1)S(1)} %get-tuple-element.57.refs_1_.refs_5_.refs_2_) | copy-start | bytes 1769476
  3.4 15.8 %collective-permute-start = (bf16[128,2304]{1,0:T(8,128)(2,1)S(1)}, bf16[128,2304]{1,0:T(8,128)(2,1)S(1)}, u32[]{:S(2)}, u32[]{:S(2)}) collective-permute-start(bf16[128,2304]{1,0:T(8,128)(2,1)S(1)} %get-tuple-element.57.refs_1_.refs_5_.refs_2_), channel_id=1, source_target_pairs={{0,4},{4,0},{8,12},{12,8},{16,20},{20,16},{24,28},{28,24},{1,5},{5... | collective-permute-start | bytes 1769480 | tf_op jit(solution)/shard_map/ppermute | solution.py:558
  5.0 28.1 %collective-permute-start.4 = (bf16[128,2304]{1,0:T(8,128)(2,1)S(1)}, bf16[128,2304]{1,0:T(8,128)(2,1)S(1)}, u32[]{:S(2)}, u32[]{:S(2)}) collective-permute-start(bf16[128,2304]{1,0:T(8,128)(2,1)S(1)} %get-tuple-element.57.refs_1_.refs_5_.refs_2_), channel_id=1, source_target_pairs={{0,16},{4,20},{8,24},{12,28},{16,0},{20,4},{24,8},{28,12},{1,17},{... | collective-permute-start | bytes 1769480 | tf_op jit(solution)/shard_map/ppermute | solution.py:558
  7.6 27.6 %collective-permute-start.3 = (bf16[128,2304]{1,0:T(8,128)(2,1)S(1)}, bf16[128,2304]{1,0:T(8,128)(2,1)S(1)}, u32[]{:S(2)}, u32[]{:S(2)}) collective-permute-start(bf16[128,2304]{1,0:T(8,128)(2,1)S(1)} %get-tuple-element.57.refs_1_.refs_5_.refs_2_), channel_id=1, source_target_pairs={{0,8},{4,12},{8,0},{12,4},{16,24},{20,28},{24,16},{28,20},{1,9},{5... | collective-permute-start | bytes 1769480 | tf_op jit(solution)/shard_map/ppermute | solution.py:558
  8.0 3.4 %collective-permute-start.1 = (bf16[32,2048]{1,0:T(8,128)(2,1)}, bf16[32,2048]{1,0:T(8,128)(2,1)S(1)}, u32[]{:S(2)}, u32[]{:S(2)}) collective-permute-start(bf16[32,2048]{1,0:T(8,128)(2,1)} %bitcast.18), channel_id=1, source_target_pairs={{0,1},{1,0},{2,3},{3,2},{4,5},{5,4},{6,7},{7,6},{8,9},{9,8},{10,11... | collective-permute-start | bytes 393224 | tf_op jit(solution)/shard_map/ppermute | solution.py:561
  19.2 8.2 %copy-start.4 = (bf16[128,2304]{1,0:T(8,128)(2,1)}, bf16[128,2304]{1,0:T(8,128)(2,1)S(1)}, u32[]{:S(2)}) copy-start(bf16[128,2304]{1,0:T(8,128)(2,1)S(1)} %collective-permute-done.refs_2_.refs_6_.refs_3_) | copy-start | bytes 1769476
  19.2 19.5 %copy-start.9 = (bf16[1,32,2048]{2,1,0:T(8,128)(2,1)S(1)}, bf16[1,32,2048]{2,1,0:T(8,128)(2,1)}, u32[]{:S(2)}) copy-start(bf16[1,32,2048]{2,1,0:T(8,128)(2,1)} %param.13) | copy-start | bytes 393220
  33.6 13.0 %copy-start.2 = (bf16[128,2304]{1,0:T(8,128)(2,1)}, bf16[128,2304]{1,0:T(8,128)(2,1)S(1)}, u32[]{:S(2)}) copy-start(bf16[128,2304]{1,0:T(8,128)(2,1)S(1)} %get-tuple-element.63.refs_2_.refs_8_.refs_5_) | copy-start | bytes 1769476
  33.6 15.3 %collective-permute-start.5 = (bf16[128,2304]{1,0:T(8,128)(2,1)S(1)}, bf16[128,2304]{1,0:T(8,128)(2,1)S(1)}, u32[]{:S(2)}, u32[]{:S(2)}) collective-permute-start(bf16[128,2304]{1,0:T(8,128)(2,1)S(1)} %get-tuple-element.63.refs_2_.refs_8_.refs_5_), channel_id=1, source_target_pairs={{0,8},{4,12},{8,0},{12,4},{16,24},{20,28},{24,16},{28,20},{1,9},{5... | collective-permute-start | bytes 1769480 | tf_op jit(solution)/shard_map/ppermute | solution.py:558
  35.1 11.5 %copy-start.5 = (bf16[128,2304]{1,0:T(8,128)(2,1)}, bf16[128,2304]{1,0:T(8,128)(2,1)S(1)}, u32[]{:S(2)}) copy-start(bf16[128,2304]{1,0:T(8,128)(2,1)S(1)} %collective-permute-done.3.refs_1_.refs_7_.refs_4_) | copy-start | bytes 1769476
  35.1 16.3 %collective-permute-start.6 = (bf16[128,2304]{1,0:T(8,128)(2,1)S(1)}, bf16[128,2304]{1,0:T(8,128)(2,1)S(1)}, u32[]{:S(2)}, u32[]{:S(2)}) collective-permute-start(bf16[128,2304]{1,0:T(8,128)(2,1)S(1)} %collective-permute-done.3.refs_1_.refs_7_.refs_4_), channel_id=1, source_target_pairs={{0,4},{4,0},{8,12},{12,8},{16,20},{20,16},{24,28},{28,24},{1,5},{5... | collective-permute-start | bytes 1769480 | tf_op jit(solution)/shard_map/ppermute | solution.py:558
  35.6 28.4 %collective-permute-start.9 = (bf16[128,2304]{1,0:T(8,128)(2,1)S(1)}, bf16[128,2304]{1,0:T(8,128)(2,1)S(1)}, u32[]{:S(2)}, u32[]{:S(2)}) collective-permute-start(bf16[128,2304]{1,0:T(8,128)(2,1)S(1)} %get-tuple-element.63.refs_2_.refs_8_.refs_5_), channel_id=1, source_target_pairs={{0,4},{4,0},{8,12},{12,8},{16,20},{20,16},{24,28},{28,24},{1,5},{5... | collective-permute-start | bytes 1769480 | tf_op jit(solution)/shard_map/ppermute | solution.py:558
  37.2 14.2 %collective-permute-start.8 = (bf16[320,768]{1,0:T(8,128)(2,1)S(1)}, bf16[320,768]{1,0:T(8,128)(2,1)S(1)}, u32[]{:S(2)}, u32[]{:S(2)}) collective-permute-start(bf16[320,768]{1,0:T(8,128)(2,1)S(1)} %get-tuple-element.69), channel_id=1, source_target_pairs={{0,2},{2,0},{1,3},{3,1},{4,6},{6,4},{5,7},{7,5},{8,10},{10,8},{9,1... | collective-permute-start | bytes 1474568 | tf_op jit(solution)/shard_map/ppermute | solution.py:552
  46.6 12.7 %collective-permute-start.7 = (bf16[320,768]{1,0:T(8,128)(2,1)S(1)}, bf16[320,768]{1,0:T(8,128)(2,1)S(1)}, u32[]{:S(2)}, u32[]{:S(2)}) collective-permute-start(bf16[320,768]{1,0:T(8,128)(2,1)S(1)} %get-tuple-element.67), channel_id=1, source_target_pairs={{0,2},{2,0},{1,3},{3,1},{4,6},{6,4},{5,7},{7,5},{8,10},{10,8},{9,1... | collective-permute-start | bytes 1474568 | tf_op jit(solution)/shard_map/ppermute | solution.py:552
  49.0 23.4 %copy-start.6 = (bf16[128,2304]{1,0:T(8,128)(2,1)}, bf16[128,2304]{1,0:T(8,128)(2,1)S(1)}, u32[]{:S(2)}) copy-start(bf16[128,2304]{1,0:T(8,128)(2,1)S(1)} %collective-permute-done.5.refs_1_.refs_9_.refs_6_) | copy-start | bytes 1769476
  49.0 37.4 %collective-permute-start.10 = (bf16[128,2304]{1,0:T(8,128)(2,1)S(1)}, bf16[128,2304]{1,0:T(8,128)(2,1)S(1)}, u32[]{:S(2)}, u32[]{:S(2)}) collective-permute-start(bf16[128,2304]{1,0:T(8,128)(2,1)S(1)} %collective-permute-done.5.refs_1_.refs_9_.refs_6_), channel_id=1, source_target_pairs={{0,4},{4,0},{8,12},{12,8},{16,20},{20,16},{24,28},{28,24},{1,5},{5... | collective-permute-start | bytes 1769480 | tf_op jit(solution)/shard_map/ppermute | solution.py:558
  51.4 21.0 %copy-start.1 = (bf16[128,2304]{1,0:T(8,128)(2,1)}, bf16[128,2304]{1,0:T(8,128)(2,1)S(1)}, u32[]{:S(2)}) copy-start(bf16[128,2304]{1,0:T(8,128)(2,1)S(1)} %collective-permute-done.6.refs_4_.refs_2_.refs_10_.refs_7_) | copy-start | bytes 1769476
  52.1 12.0 %copy-start.17 = (bf16[160,768]{1,0:T(8,128)(2,1)}, bf16[160,768]{1,0:T(8,128)(2,1)S(1)}, u32[]{:S(2)}) copy-start(bf16[160,768]{1,0:T(8,128)(2,1)S(1)} %get-tuple-element.92.refs_8_) | copy-start | bytes 737284
  64.1 22.3 %copy-start = (bf16[128,2304]{1,0:T(8,128)(2,1)}, bf16[128,2304]{1,0:T(8,128)(2,1)S(1)}, u32[]{:S(2)}) copy-start(bf16[128,2304]{1,0:T(8,128)(2,1)S(1)} %collective-permute-done.9.refs_8_.refs_1_.refs_11_) | copy-start | bytes 1769476
  72.4 23.6 %collective-permute-start.14 = (bf16[320,768]{1,0:T(8,128)(2,1)S(1)}, bf16[320,768]{1,0:T(8,128)(2,1)S(1)}, u32[]{:S(2)}, u32[]{:S(2)}) collective-permute-start(bf16[320,768]{1,0:T(8,128)(2,1)S(1)} %get-tuple-element.80), channel_id=1, source_target_pairs={{0,2},{2,0},{1,3},{3,1},{4,6},{6,4},{5,7},{7,5},{8,10},{10,8},{9,1... | collective-permute-start | bytes 1474568 | tf_op jit(solution)/shard_map/ppermute | solution.py:552
  73.9 7.6 %collective-permute-start.12 = (bf16[160,768]{1,0:T(8,128)(2,1)S(1)}, bf16[160,768]{1,0:T(8,128)(2,1)S(1)}, u32[]{:S(2)}, u32[]{:S(2)}) collective-permute-start(bf16[160,768]{1,0:T(8,128)(2,1)S(1)} %get-tuple-element.76), channel_id=1, source_target_pairs={{0,8},{4,12},{8,0},{12,4},{16,24},{20,28},{24,16},{28,20},{1,9},{5... | collective-permute-start | bytes 737288 | tf_op jit(solution)/shard_map/ppermute | solution.py:558
  74.5 11.9 %collective-permute-start.13 = (bf16[160,768]{1,0:T(8,128)(2,1)S(1)}, bf16[160,768]{1,0:T(8,128)(2,1)S(1)}, u32[]{:S(2)}, u32[]{:S(2)}) collective-permute-start(bf16[160,768]{1,0:T(8,128)(2,1)S(1)} %get-tuple-element.77), channel_id=1, source_target_pairs={{0,16},{4,20},{8,24},{12,28},{16,0},{20,4},{24,8},{28,12},{1,17},{... | collective-permute-start | bytes 737288 | tf_op jit(solution)/shard_map/ppermute | solution.py:558
  77.9 8.5 %collective-permute-start.11 = (bf16[160,768]{1,0:T(8,128)(2,1)S(1)}, bf16[160,768]{1,0:T(8,128)(2,1)S(1)}, u32[]{:S(2)}, u32[]{:S(2)}) collective-permute-start(bf16[160,768]{1,0:T(8,128)(2,1)S(1)} %get-tuple-element.75), channel_id=1, source_target_pairs={{0,4},{4,0},{8,12},{12,8},{16,20},{20,16},{24,28},{28,24},{1,5},{5... | collective-permute-start | bytes 737288 | tf_op jit(solution)/shard_map/ppermute | solution.py:558
  81.5 13.8 %copy-start.14 = (bf16[160,768]{1,0:T(8,128)(2,1)}, bf16[160,768]{1,0:T(8,128)(2,1)S(1)}, u32[]{:S(2)}) copy-start(bf16[160,768]{1,0:T(8,128)(2,1)S(1)} %collective-permute-done.12.refs_9_.refs_10_) | copy-start | bytes 737284
  86.3 9.0 %copy-start.15 = (bf16[160,768]{1,0:T(8,128)(2,1)}, bf16[160,768]{1,0:T(8,128)(2,1)S(1)}, u32[]{:S(2)}) copy-start(bf16[160,768]{1,0:T(8,128)(2,1)S(1)} %collective-permute-done.13.refs_10_.refs_12_) | copy-start | bytes 737284
  86.3 9.0 %copy-start.16 = (bf16[160,768]{1,0:T(8,128)(2,1)}, bf16[160,768]{1,0:T(8,128)(2,1)S(1)}, u32[]{:S(2)}) copy-start(bf16[160,768]{1,0:T(8,128)(2,1)S(1)} %collective-permute-done.11.refs_8_.refs_9_) | copy-start | bytes 737284
  86.3 9.0 %copy-start.7 = (bf16[128,2304]{1,0:T(8,128)(2,1)}, bf16[128,2304]{1,0:T(8,128)(2,1)S(1)}, u32[]{:S(2)}) copy-start(bf16[128,2304]{1,0:T(8,128)(2,1)S(1)} %collective-permute-done.10.refs_2_.refs_12_.refs_9_) | copy-start | bytes 1769476
  86.4 20.1 %copy-start.20 = (s32[128,8]{0,1:T(8,128)S(1)}, s32[128,8]{0,1:T(8,128)}, u32[]{:S(2)}) copy-start(s32[128,8]{0,1:T(8,128)} %param.9) | copy-start | bytes 12292
  95.4 36.5 %copy-start.21 = (bf16[128,8]{0,1:T(8,128)(2,1)S(1)}, bf16[128,8]{0,1:T(8,128)(2,1)}, u32[]{:S(2)}) copy-start(bf16[128,8]{0,1:T(8,128)(2,1)} %param.10) | copy-start | bytes 6148
  95.4 19.9 %collective-permute-start.16 = (bf16[320,768]{1,0:T(8,128)(2,1)}, bf16[320,768]{1,0:T(8,128)(2,1)S(1)}, u32[]{:S(2)}, u32[]{:S(2)}) collective-permute-start(bf16[320,768]{1,0:T(8,128)(2,1)} %get-tuple-element.85), channel_id=1, source_target_pairs={{0,2},{2,0},{1,3},{3,1},{4,6},{6,4},{5,7},{7,5},{8,10},{10,8},{9,1... | collective-permute-start | bytes 1474568 | tf_op jit(solution)/shard_map/ppermute | solution.py:552
  99.0 7.5 %collective-permute-start.17 = (bf16[8,32,768]{2,1,0:T(8,128)(2,1)S(1)}, bf16[8,32,768]{2,1,0:T(8,128)(2,1)S(1)}, u32[]{:S(2)}, u32[]{:S(2)}) collective-permute-start(bf16[8,32,768]{2,1,0:T(8,128)(2,1)S(1)} %get-tuple-element.86), channel_id=1, source_target_pairs={{0,1},{1,0},{2,3},{3,2},{4,5},{5,4},{6,7},{7,6},{8,9},{9,8},{10,11... | collective-permute-start | bytes 1179656 | tf_op jit(solution)/shard_map/ppermute | solution.py:561
  99.0 16.2 %collective-permute-start.18 = (bf16[160,768]{1,0:T(8,128)(2,1)S(1)}, bf16[160,768]{1,0:T(8,128)(2,1)S(1)}, u32[]{:S(2)}, u32[]{:S(2)}) collective-permute-start(bf16[160,768]{1,0:T(8,128)(2,1)S(1)} %get-tuple-element.89), channel_id=1, source_target_pairs={{0,24},{4,28},{8,16},{12,20},{16,8},{20,12},{24,0},{28,4},{1,25},{... | collective-permute-start | bytes 737288 | tf_op jit(solution)/shard_map/ppermute | solution.py:558
  99.0 16.2 %all-to-all-start = ((bf16[8,64,128]{2,1,0:T(8,128)(2,1)}), bf16[8,64,128]{2,1,0:T(8,128)(2,1)S(1)}, u32[]{:S(2)}, u32[]{:S(2)}) async-start(bf16[8,64,128]{2,1,0:T(8,128)(2,1)} %get-tuple-element.83), calls=%async_computation | async-start | bytes 262144 | tf_op jit(solution)/shard_map/all_to_all | solution.py:566
  115.2 46.4 %copy-start.10 = (bf16[160,768]{1,0:T(8,128)(2,1)}, bf16[160,768]{1,0:T(8,128)(2,1)S(1)}, u32[]{:S(2)}) copy-start(bf16[160,768]{1,0:T(8,128)(2,1)S(1)} %collective-permute-done.18.refs_4_.refs_14_) | copy-start | bytes 737284
  115.9 9.1 %collective-permute-start.21 = (bf16[160,768]{1,0:T(8,128)(2,1)S(1)}, bf16[160,768]{1,0:T(8,128)(2,1)}, u32[]{:S(2)}, u32[]{:S(2)}) collective-permute-start(bf16[160,768]{1,0:T(8,128)(2,1)S(1)} %get-tuple-element.94), channel_id=1, source_target_pairs={{0,4},{4,0},{8,12},{12,8},{16,20},{20,16},{24,28},{28,24},{1,5},{5... | collective-permute-start | bytes 737288 | tf_op jit(solution)/shard_map/ppermute | solution.py:558
  117.0 12.2 %collective-permute-start.23 = (bf16[160,768]{1,0:T(8,128)(2,1)S(1)}, bf16[160,768]{1,0:T(8,128)(2,1)S(1)}, u32[]{:S(2)}, u32[]{:S(2)}) collective-permute-start(bf16[160,768]{1,0:T(8,128)(2,1)S(1)} %get-tuple-element.95), channel_id=1, source_target_pairs={{0,4},{4,0},{8,12},{12,8},{16,20},{20,16},{24,28},{28,24},{1,5},{5... | collective-permute-start | bytes 737288 | tf_op jit(solution)/shard_map/ppermute | solution.py:558
  118.0 14.6 %collective-permute-start.26 = (f32[128,512]{1,0:T(8,128)S(1)}, f32[128,512]{1,0:T(8,128)S(1)}, u32[]{:S(2)}, u32[]{:S(2)}) collective-permute-start(f32[128,512]{1,0:T(8,128)S(1)} %get-tuple-element.96.refs_7_), channel_id=1, source_target_pairs={{0,2},{2,0},{1,3},{3,1},{4,6},{6,4},{5,7},{7,5},{8,10},{10,8},{9,1... | collective-permute-start | bytes 786440 | tf_op jit(solution)/shard_map/ppermute | solution.py:552
  125.0 9.9 %collective-permute-start.22 = (bf16[160,768]{1,0:T(8,128)(2,1)}, bf16[160,768]{1,0:T(8,128)(2,1)S(1)}, u32[]{:S(2)}, u32[]{:S(2)}) collective-permute-start(bf16[160,768]{1,0:T(8,128)(2,1)} %collective-permute-done.21), channel_id=1, source_target_pairs={{0,16},{4,20},{8,24},{12,28},{16,0},{20,4},{24,8},{28,12},{1,17},{... | collective-permute-start | bytes 737288 | tf_op jit(solution)/shard_map/ppermute | solution.py:558
  126.4 5.6 %collective-permute-start.15 = (bf16[8,64,128]{2,1,0:T(8,128)(2,1)S(1)}, bf16[8,64,128]{2,1,0:T(8,128)(2,1)S(1)}, u32[]{:S(2)}, u32[]{:S(2)}) collective-permute-start(bf16[8,64,128]{2,1,0:T(8,128)(2,1)S(1)} %all-to-all-done.refs_5_.refs_1_), channel_id=1, source_target_pairs={{0,2},{2,0},{1,3},{3,1},{4,6},{6,4},{5,7},{7,5},{8,10},{10,8},{9,1... | collective-permute-start | bytes 393224 | tf_op jit(solution)/shard_map/ppermute | solution.py:552
  127.9 11.8 %collective-permute-start.19 = (bf16[160,768]{1,0:T(8,128)(2,1)}, bf16[160,768]{1,0:T(8,128)(2,1)S(1)}, u32[]{:S(2)}, u32[]{:S(2)}) collective-permute-start(bf16[160,768]{1,0:T(8,128)(2,1)} %get-tuple-element.93), channel_id=1, source_target_pairs={{0,4},{4,0},{8,12},{12,8},{16,20},{20,16},{24,28},{28,24},{1,5},{5... | collective-permute-start | bytes 737288 | tf_op jit(solution)/shard_map/ppermute | solution.py:558
  129.2 13.0 %collective-permute-start.24 = (bf16[160,768]{1,0:T(8,128)(2,1)S(1)}, bf16[160,768]{1,0:T(8,128)(2,1)S(1)}, u32[]{:S(2)}, u32[]{:S(2)}) collective-permute-start(bf16[160,768]{1,0:T(8,128)(2,1)S(1)} %collective-permute-done.23), channel_id=1, source_target_pairs={{0,8},{4,12},{8,0},{12,4},{16,24},{20,28},{24,16},{28,20},{1,9},{5... | collective-permute-start | bytes 737288 | tf_op jit(solution)/shard_map/ppermute | solution.py:558
  134.8 26.8 %copy-start.11 = (bf16[160,768]{1,0:T(8,128)(2,1)}, bf16[160,768]{1,0:T(8,128)(2,1)S(1)}, u32[]{:S(2)}) copy-start(bf16[160,768]{1,0:T(8,128)(2,1)S(1)} %collective-permute-done.22.refs_10_.refs_13_) | copy-start | bytes 737284
  139.6 14.9 %collective-permute-start.27 = (bf16[8,32,768]{2,1,0:T(8,128)(2,1)S(1)}, bf16[8,32,768]{2,1,0:T(8,128)(2,1)S(1)}, u32[]{:S(2)}, u32[]{:S(2)}) collective-permute-start(bf16[8,32,768]{2,1,0:T(8,128)(2,1)S(1)} %get-tuple-element.99), channel_id=1, source_target_pairs={{0,1},{1,0},{2,3},{3,2},{4,5},{5,4},{6,7},{7,6},{8,9},{9,8},{10,11... | collective-permute-start | bytes 1179656 | tf_op jit(solution)/shard_map/ppermute | solution.py:561
  139.7 12.7 %collective-permute-start.20 = (bf16[160,768]{1,0:T(8,128)(2,1)S(1)}, bf16[160,768]{1,0:T(8,128)(2,1)S(1)}, u32[]{:S(2)}, u32[]{:S(2)}) collective-permute-start(bf16[160,768]{1,0:T(8,128)(2,1)S(1)} %collective-permute-done.19), channel_id=1, source_target_pairs={{0,8},{4,12},{8,0},{12,4},{16,24},{20,28},{24,16},{28,20},{1,9},{5... | collective-permute-start | bytes 737288 | tf_op jit(solution)/shard_map/ppermute | solution.py:558
  142.2 12.2 %collective-permute-start.25 = (bf16[160,768]{1,0:T(8,128)(2,1)S(1)}, bf16[160,768]{1,0:T(8,128)(2,1)S(1)}, u32[]{:S(2)}, u32[]{:S(2)}) collective-permute-start(bf16[160,768]{1,0:T(8,128)(2,1)S(1)} %collective-permute-done.24), channel_id=1, source_target_pairs={{0,16},{4,20},{8,24},{12,28},{16,0},{20,4},{24,8},{28,12},{1,17},{... | collective-permute-start | bytes 737288 | tf_op jit(solution)/shard_map/ppermute | solution.py:558
  152.4 9.3 %copy-start.12 = (bf16[160,768]{1,0:T(8,128)(2,1)}, bf16[160,768]{1,0:T(8,128)(2,1)S(1)}, u32[]{:S(2)}) copy-start(bf16[160,768]{1,0:T(8,128)(2,1)S(1)} %collective-permute-done.20.refs_5_.refs_11_) | copy-start | bytes 737284
  154.4 7.3 %copy-start.13 = (bf16[160,768]{1,0:T(8,128)(2,1)}, bf16[160,768]{1,0:T(8,128)(2,1)S(1)}, u32[]{:S(2)}) copy-start(bf16[160,768]{1,0:T(8,128)(2,1)S(1)} %collective-permute-done.25.refs_6_.refs_15_) | copy-start | bytes 737284
  155.9 19.1 %all-to-all-start.1 = ((bf16[8,32,1024]{2,1,0:T(8,128)(2,1)}), bf16[8,32,1024]{2,1,0:T(8,128)(2,1)S(1)}, u32[]{:S(2)}, u32[]{:S(2)}) async-start(bf16[8,32,1024]{2,1,0:T(8,128)(2,1)} %get-tuple-element.105), calls=%async_computation.1 | async-start | bytes 1048576 | tf_op jit(solution)/shard_map/all_to_all | solution.py:566
  169.5 4.3 %collective-permute-start.28 = (f32[128,8]{1,0:T(8,128)S(1)}, f32[128,8]{1,0:T(8,128)S(1)}, u32[]{:S(2)}, u32[]{:S(2)}) collective-permute-start(f32[128,8]{1,0:T(8,128)S(1)} %get-tuple-element.104), channel_id=1, source_target_pairs={{0,2},{2,0},{1,3},{3,1},{4,6},{6,4},{5,7},{7,5},{8,10},{10,8},{9,1... | collective-permute-start | bytes 12296 | tf_op jit(solution)/shard_map/ppermute | solution.py:552
  179.4 1.5 collective-permute-start.29

commit v14 on v13

--- a/solution.py
+++ b/solution.py
@@ -592,14 +592,13 @@
     places = [o for batch in batches for o in batch]
     back, lows, shared = {}, [], {}
 
-    def arrived(i):
-        order.wait([back[o] for o in batches[i] if o])
-
     def total(i):
         for o, rows in zip(batches[i], share_sum_call(order, shared[i], 2, slots)):
             masks = [o] if o else []
             if i >= last - 1 and o % 2:
                 masks = [1 << k for k in range(o.bit_length()) if o >> k & 1]
+            elif o == 4 and groups == 8:
+                masks = [2, 6]
             for mask in masks:
                 rows = flip(rows, mask)
             back[o] = rows
@@ -612,9 +611,8 @@
         elif kind == "total":
             total(i)
         else:
-            if i == last and last > 2:
-                for j in range(i - 1):
-                    arrived(j)
+            if i == last and groups == 8:
+                order.wait([back[4]])
             *give, keep, low = expert_rows_call(
                 order, [fetch(o) for o in batches[i]], seconds, downs, shares, slots
             )
@@ -627,15 +625,17 @@
     low_grad, first_own = collect_call(order, places, lows, grads, feats)
     firsts = [x.reshape(groups * rank, units) for x in (first_own, swap(first_own))]
     low_grad = exchange(low_grad)
+    order.wait([back[batches[-2][0]], back[1], back[2]])
+    total(last)
+    order.wait([low_grad])
     low_hid = all_shares(lowrank_hid_call(order, index, hid, firsts, groups))
-    order.wait([back[batches[-2][0]], low_grad])
-    total(last)
+    order.wait([back[batches[-2][1]]])
 
     low_grad = low_dense_call(order, all_shares(low_grad))
     order.wait([back[batches[-1][0]]])
     keep, give, scaled = first_grad_call(order, index, weight, low_grad, hid, low_hid, groups)
 
-    order.wait([back[batches[-2][1]], back[batches[-1][1]]])
+    order.wait([back[batches[-1][1]]])
     got = exchange(first_sum_call(order, keep, swap(give), scaled))
     back = [back[o] for o in range(groups)]
     grad_hidden, sums = finish_call(order, index, weight, low_grad, hid, firsts, back)

time: 185 us -> 183 us (0.989)
  waiting for transfers between devices: 65.8 us -> 60 us
  starting transfers between devices: 45.6 us -> 48.6 us
    all_to_all x2, waiting for transfers between devices: 6.3 us -> 1.22 us  [exchange(): return lax.all_to_all(x, axes, split_axis=0, concat_axis=0, tiled=True)]
    ppermute x18 -> x19, starting transfers between devices: 23.5 us -> 26.2 us  [flip(): return lax.ppermute(x, 'ep', [(i, i ^ mask) for i in range(groups)])]
    ppermute x18 -> x19, waiting for transfers between devices: 48.6 us -> 47.3 us  [flip(): return lax.ppermute(x, 'ep', [(i, i ^ mask) for i in range(groups)])]
  transfers between devices with their start and end apart: 32 -> 33, of which waited for: 16 -> 16; matrix products, arithmetic and copies ran while one was open for 1% -> 1% of each run, Pallas kernels for 33% -> 34%
where the time goes in v14:
time: 183 us; the launch traced here: 180 us
  Pallas kernels  65.9 us (36%)
  waiting for transfers between devices  60 us (33%)
  starting transfers between devices  48.6 us (27%)
  local copies, waits for them, and re-layouts  3.26 us (2%)
    pallas_call x18, Pallas kernels, call(): pl.pallas_call(ordered, grid=grid, in_specs=[SMEM, *in_specs] + [ANY] * l...  65.9 us
    ppermute x19, waiting for transfers between devices, flip(): return lax.ppermute(x, 'ep', [(i, i ^ mask) for i in range(groups)])  47.3 us
    ppermute x19, starting transfers between devices, flip(): return lax.ppermute(x, 'ep', [(i, i ^ mask) for i in range(groups)])  26.2 us
    all_to_all x2, starting transfers between devices, exchange(): return lax.all_to_all(x, axes, split_axis=0, concat_axis=0, tiled=True)  13.4 us
    ppermute x7, waiting for transfers between devices, turn(): lax.ppermute(x, 'rep', [(r, (r + offset) % shares) for r in range(shares)])  10.6 us
    ppermute x7, starting transfers between devices, turn(): lax.ppermute(x, 'rep', [(r, (r + offset) % shares) for r in range(shares)])  8.78 us
  transfers between devices with their start and end apart: 33, of which 16 were waited for; matrix products, arithmetic and copies ran while one was open for 1% of the time, Pallas kernels for 34%

profile of v14, /device:TPU:8, one launch (start us, length us, event | category | flops | bytes accessed | tf_op | source)
XLA Modules:
  0.0 179.5 jit_solution(15211335189787148553)
XLA Ops:
  0.8 0.8 copy-done.19
  1.6 0.7 copy-done.20
  2.3 1.1 pack_block.1
  3.4 1.6 collective-permute-start
  5.0 2.6 %collective-permute-start.4 = (bf16[128,2304]{1,0:T(8,128)(2,1)S(1)}, bf16[128,2304]{1,0:T(8,128)(2,1)S(1)}, u32[]{:S(2)}, u32[]{:S(2)}) collective-permute-start(bf16[128,2304]{1,0:T(8,128)(2,1)S(1)} %get-tuple-element.57.refs_1_.refs_5_.refs_2_), channel_id=1, source_target_pairs={{0,16},{4,20},{8,24},{12,28},{16,0},{20,4},{24,8},{28,12},{1,17},{... | collective-permute-start | bytes 1769480 | tf_op jit(solution)/shard_map/ppermute | solution.py:558
  8.0 3.4 %load_matrix.1 = (bf16[1536,2048]{1,0:T(8,128)(2,1)S(1)}, f32[8,128]{1,0:T(8,128)}) custom-call(s32[3]{0:T(128)S(1)} %pad_add_fusion.refs_0_, bf16[1536,2048]{1,0:T(8,128)(2,1)} %bitcast.33, f32[8,128]{1,0:T(8,128)} %get-tuple-element.58.refs_2_), custom_call_target="tpu_custom_call" | custom-call | flops 1 | bytes 1 | tf_op jit(solution)/shard_map/load_matrix/pallas_call | solution.py:53
  11.5 7.7 %collective-permute-done.refs_2_.refs_6_.refs_3_ = bf16[128,2304]{1,0:T(8,128)(2,1)S(1)} collective-permute-done((bf16[128,2304]{1,0:T(8,128)(2,1)S(1)}, bf16[128,2304]{1,0:T(8,128)(2,1)S(1)}, u32[]{:S(2)}, u32[]{:S(2)}) %collective-permute-start) | collective-permute-done | bytes 589856 | tf_op jit(solution)/shard_map/ppermute | solution.py:558
  19.2 8.2 %expert_rows.4 = (bf16[320,768]{1,0:T(8,128)(2,1)S(1)}, bf16[320,768]{1,0:T(8,128)(2,1)S(1)}, bf16[2,64,128]{2,1,0:T(8,128)(2,1)S(1)}, f32[8,128]{1,0:T(8,128)}) custom-call(s32[3]{0:T(128)S(1)} %pad_add_fusion.refs_0_, bf16[128,2304]{1,0:T(8,128)(2,1)S(1)} %get-tuple-element.57.refs_1_.refs_5_.refs_2_, ...), custom_call_target="tpu_custom_call" | custom-call | flops 1 | bytes 1 | tf_op jit(solution)/shard_map/expert_rows/pallas_call | solution.py:53
  27.4 5.7 %collective-permute-done.4.refs_1_ = bf16[128,2304]{1,0:T(8,128)(2,1)S(1)} collective-permute-done((bf16[128,2304]{1,0:T(8,128)(2,1)S(1)}, bf16[128,2304]{1,0:T(8,128)(2,1)S(1)}, u32[]{:S(2)}, u32[]{:S(2)}) %collective-permute-start.4) | collective-permute-done | bytes 589856 | tf_op jit(solution)/shard_map/ppermute | solution.py:558
  33.1 0.5 gate.1
  33.6 1.5 collective-permute-start.5
  35.1 0.5 collective-permute-start.6
  35.6 1.5 collective-permute-start.8
  37.1 8.0 %expert_rows.5 = (bf16[320,768]{1,0:T(8,128)(2,1)S(1)}, bf16[320,768]{1,0:T(8,128)(2,1)S(1)}, bf16[2,64,128]{2,1,0:T(8,128)(2,1)S(1)}, f32[8,128]{1,0:T(8,128)}) custom-call(s32[3]{0:T(128)S(1)} %pad_add_fusion.refs_0_, bf16[128,2304]{1,0:T(8,128)(2,1)S(1)} %collective-permute-done.3.refs_1_.refs_7_.refs_4_, ...), custom_call_target="tpu_custom_call" | custom-call | flops 1 | bytes 1 | tf_op jit(solution)/shard_map/expert_rows/pallas_call | solution.py:53
  45.2 0.5 collective-permute-start.7
  45.7 1.6 collective-permute-start.9
  47.3 1.7 collective-permute-done.5.refs_1_.refs_9_.refs_6_
  49.0 0.5 collective-permute-start.10
  49.5 1.9 %collective-permute-done.6.refs_4_.refs_2_.refs_10_.refs_7_ = bf16[128,2304]{1,0:T(8,128)(2,1)S(1)} collective-permute-done((bf16[128,2304]{1,0:T(8,128)(2,1)S(1)}, bf16[128,2304]{1,0:T(8,128)(2,1)S(1)}, u32[]{:S(2)}, u32[]{:S(2)}) %collective-permute-start.6) | collective-permute-done | bytes 589856 | tf_op jit(solution)/shard_map/ppermute | solution.py:558
  51.4 0.7 share_sum.4
  52.1 6.3 %collective-permute-done.7.refs_2_ = bf16[320,768]{1,0:T(8,128)(2,1)S(1)} collective-permute-done((bf16[320,768]{1,0:T(8,128)(2,1)S(1)}, bf16[320,768]{1,0:T(8,128)(2,1)S(1)}, u32[]{:S(2)}, u32[]{:S(2)}) %collective-permute-start.7) | collective-permute-done | bytes 491552 | tf_op jit(solution)/shard_map/ppermute | solution.py:552
  58.4 1.3 share_sum.5
  59.6 1.0 collective-permute-start.11
  60.7 3.4 %collective-permute-done.9.refs_8_.refs_1_.refs_11_ = bf16[128,2304]{1,0:T(8,128)(2,1)S(1)} collective-permute-done((bf16[128,2304]{1,0:T(8,128)(2,1)S(1)}, bf16[128,2304]{1,0:T(8,128)(2,1)S(1)}, u32[]{:S(2)}, u32[]{:S(2)}) %collective-permute-start.9) | collective-permute-done | bytes 589856 | tf_op jit(solution)/shard_map/ppermute | solution.py:558
  64.1 8.4 %expert_rows.6 = (bf16[320,768]{1,0:T(8,128)(2,1)S(1)}, bf16[320,768]{1,0:T(8,128)(2,1)S(1)}, bf16[2,64,128]{2,1,0:T(8,128)(2,1)S(1)}, f32[8,128]{1,0:T(8,128)}) custom-call(s32[3]{0:T(128)S(1)} %pad_add_fusion.refs_0_, bf16[128,2304]{1,0:T(8,128)(2,1)S(1)} %collective-permute-done.5.refs_1_.refs_9_.refs_6_, ...), custom_call_target="tpu_custom_call" | custom-call | flops 1 | bytes 1 | tf_op jit(solution)/shard_map/expert_rows/pallas_call | solution.py:53
  72.5 1.6 collective-permute-start.13
  74.0 2.5 %collective-permute-start.12 = (bf16[160,768]{1,0:T(8,128)(2,1)S(1)}, bf16[160,768]{1,0:T(8,128)(2,1)S(1)}, u32[]{:S(2)}, u32[]{:S(2)}) collective-permute-start(bf16[160,768]{1,0:T(8,128)(2,1)S(1)} %collective-permute-done.11), channel_id=1, source_target_pairs={{0,24},{4,28},{8,16},{12,20},{16,8},{20,12},{24,0},{28,4},{1,25},{... | collective-permute-start | bytes 737288 | tf_op jit(solution)/shard_map/ppermute | solution.py:558
  76.5 8.8 %collective-permute-done.12.refs_8_.refs_12_ = bf16[160,768]{1,0:T(8,128)(2,1)S(1)} collective-permute-done((bf16[160,768]{1,0:T(8,128)(2,1)S(1)}, bf16[160,768]{1,0:T(8,128)(2,1)S(1)}, u32[]{:S(2)}, u32[]{:S(2)}) %collective-permute-start.12) | collective-permute-done | bytes 245792 | tf_op jit(solution)/shard_map/ppermute | solution.py:558
  85.2 8.3 %expert_rows.7 = (bf16[320,768]{1,0:T(8,128)(2,1)S(1)}, bf16[320,768]{1,0:T(8,128)(2,1)S(1)}, bf16[2,64,128]{2,1,0:T(8,128)(2,1)S(1)}, f32[8,128]{1,0:T(8,128)}) custom-call(s32[3]{0:T(128)S(1)} %pad_add_fusion.refs_0_, bf16[128,2304]{1,0:T(8,128)(2,1)S(1)} %collective-permute-done.9.refs_8_.refs_1_.refs_11_, ...), custom_call_target="tpu_custom_call" | custom-call | flops 1 | bytes 1 | tf_op jit(solution)/shard_map/expert_rows/pallas_call | solution.py:53
  93.6 0.6 collective-permute-start.16
  94.2 0.5 collective-permute-start.18
  94.7 1.3 share_sum.6
  96.0 1.7 collective-permute-start.17
  97.7 1.7 collect_blocks.1
  99.5 6.4 %all-to-all-start = ((bf16[8,64,128]{2,1,0:T(8,128)(2,1)}), bf16[8,64,128]{2,1,0:T(8,128)(2,1)S(1)}, u32[]{:S(2)}, u32[]{:S(2)}) async-start(bf16[8,64,128]{2,1,0:T(8,128)(2,1)} %get-tuple-element.81), calls=%async_computation | async-start | bytes 262144 | tf_op jit(solution)/shard_map/all_to_all | solution.py:566
  105.8 1.5 collective-permute-start.20
  107.4 0.7 collective-permute-done.17.refs_4_.refs_14_
  108.1 1.3 share_sum.7
  109.4 2.0 %collective-permute-start.22 = (bf16[160,768]{1,0:T(8,128)(2,1)}, bf16[160,768]{1,0:T(8,128)(2,1)}, u32[]{:S(2)}, u32[]{:S(2)}) collective-permute-start(bf16[160,768]{1,0:T(8,128)(2,1)} %get-tuple-element.94), channel_id=1, source_target_pairs={{0,4},{4,0},{8,12},{12,8},{16,20},{20,16},{24,28},{28,24},{1,5},{5... | collective-permute-start | bytes 737288 | tf_op jit(solution)/shard_map/ppermute | solution.py:558
  111.5 3.6 %lowrank_hid.1 = (f32[128,512]{1,0:T(8,128)S(1)}, f32[8,128]{1,0:T(8,128)}) custom-call(s32[3]{0:T(128)S(1)} %pad_add_fusion.refs_0_, s32[128,8]{1,0:T(8,128)S(1)} %copy.17.refs_1_.refs_5_.refs_2_, bf16[1024,768]{1,0:T(8,128)(2,1)} %bitcast.29, bf16[256,768]{1,0:T(8,128)(2,1)S(1)} %bitcast.23, bf16[256,768]{1,0:T(8,128)(2,1)S(1)} %bitcast.25, ...), custom_call_target="tpu_custom_call" | custom-call | flops 1 | bytes 1 | tf_op jit(solution)/shard_map/lowrank_hid/pallas_call | solution.py:53
  115.1 1.6 collective-permute-start.27
  116.7 2.2 %collective-permute-start.21 = (bf16[160,768]{1,0:T(8,128)(2,1)}, bf16[160,768]{1,0:T(8,128)(2,1)S(1)}, u32[]{:S(2)}, u32[]{:S(2)}) collective-permute-start(bf16[160,768]{1,0:T(8,128)(2,1)} %collective-permute-done.20), channel_id=1, source_target_pairs={{0,8},{4,12},{8,0},{12,4},{16,24},{20,28},{24,16},{28,20},{1,9},{5... | collective-permute-start | bytes 737288 | tf_op jit(solution)/shard_map/ppermute | solution.py:558
  118.9 2.3 %collective-permute-done.22 = bf16[160,768]{1,0:T(8,128)(2,1)} collective-permute-done((bf16[160,768]{1,0:T(8,128)(2,1)}, bf16[160,768]{1,0:T(8,128)(2,1)}, u32[]{:S(2)}, u32[]{:S(2)}) %collective-permute-start.22) | collective-permute-done | bytes 245792 | tf_op jit(solution)/shard_map/ppermute | solution.py:558
  121.2 2.0 %collective-permute-start.23 = (bf16[160,768]{1,0:T(8,128)(2,1)}, bf16[160,768]{1,0:T(8,128)(2,1)S(1)}, u32[]{:S(2)}, u32[]{:S(2)}) collective-permute-start(bf16[160,768]{1,0:T(8,128)(2,1)} %collective-permute-done.22), channel_id=1, source_target_pairs={{0,16},{4,20},{8,24},{12,28},{16,0},{20,4},{24,8},{28,12},{1,17},{... | collective-permute-start | bytes 737288 | tf_op jit(solution)/shard_map/ppermute | solution.py:558
  123.2 1.5 collective-permute-start.14
  124.7 1.2 collective-permute-done.24
  125.9 0.6 collective-permute-start.25
  126.6 1.5 collective-permute-done.14.refs_2_
  128.2 0.7 low_dense.1
  128.8 4.7 %collective-permute-done.23.refs_10_.refs_13_ = bf16[160,768]{1,0:T(8,128)(2,1)S(1)} collective-permute-done((bf16[160,768]{1,0:T(8,128)(2,1)}, bf16[160,768]{1,0:T(8,128)(2,1)S(1)}, u32[]{:S(2)}, u32[]{:S(2)}) %collective-permute-start.23) | collective-permute-done | bytes 245792 | tf_op jit(solution)/shard_map/ppermute | solution.py:558
  133.6 4.7 %first_grad.1 = (f32[8,32,768]{2,1,0:T(8,128)S(1)}, bf16[8,32,768]{2,1,0:T(8,128)(2,1)S(1)}, bf16[8,32,256]{2,1,0:T(8,128)(2,1)S(1)}, f32[8,128]{1,0:T(8,128)}) custom-call(s32[3]{0:T(128)S(1)} %pad_add_fusion.refs_0_, s32[128,8]{1,0:T(8,128)S(1)} %copy.17.refs_1_.refs_5_.refs_2_, bf16[128,8]{1,0:T(8,128)(2,1)S(1)} %copy.19.refs_2_.refs_6_.refs_3_, ...), custom_call_target="tpu_custom_call" | custom-call | flops 1 | bytes 1 | tf_op jit(solution)/shard_map/first_grad/pallas_call | solution.py:53
  138.4 3.4 %collective-permute-start.26 = (bf16[160,768]{1,0:T(8,128)(2,1)S(1)}, bf16[160,768]{1,0:T(8,128)(2,1)S(1)}, u32[]{:S(2)}, u32[]{:S(2)}) collective-permute-start(bf16[160,768]{1,0:T(8,128)(2,1)S(1)} %collective-permute-done.25), channel_id=1, source_target_pairs={{0,16},{4,20},{8,24},{12,28},{16,0},{20,4},{24,8},{28,12},{1,17},{... | collective-permute-start | bytes 737288 | tf_op jit(solution)/shard_map/ppermute | solution.py:558
  141.8 9.2 %collective-permute-done.26.refs_5_.refs_15_ = bf16[160,768]{1,0:T(8,128)(2,1)S(1)} collective-permute-done((bf16[160,768]{1,0:T(8,128)(2,1)S(1)}, bf16[160,768]{1,0:T(8,128)(2,1)S(1)}, u32[]{:S(2)}, u32[]{:S(2)}) %collective-permute-start.26) | collective-permute-done | bytes 245792 | tf_op jit(solution)/shard_map/ppermute | solution.py:558
  151.0 0.6 first_sum.1
  151.6 0.8 copy-done.17
  152.4 7.1 %all-to-all-start.1 = ((bf16[8,32,1024]{2,1,0:T(8,128)(2,1)}), bf16[8,32,1024]{2,1,0:T(8,128)(2,1)S(1)}, u32[]{:S(2)}, u32[]{:S(2)}) async-start(bf16[8,32,1024]{2,1,0:T(8,128)(2,1)} %copy-done.17), calls=%async_computation.1 | async-start | bytes 1048576 | tf_op jit(solution)/shard_map/all_to_all | solution.py:566
  159.5 7.9 %finish.1 = (bf16[1024,768]{1,0:T(8,128)(2,1)}, f32[128,8]{1,0:T(8,128)S(1)}, f32[8,128]{1,0:T(8,128)}) custom-call(s32[3]{0:T(128)S(1)} %pad_add_fusion.refs_0_, s32[128,8]{1,0:T(8,128)S(1)} %copy.17.refs_1_.refs_5_.refs_2_, s32[128,8]{1,0:T(8,128)S(1)} %copy.17.refs_1_.refs_5_.refs_2_, bf16[128,8]{1,0:T(8,128)(2,1)S(1)} %copy.19.refs_2_.refs_6_.refs_3_, ...), custom_call_target="tpu_custom_call" | custom-call | flops 1 | bytes 20000000 | tf_op jit(solution)/shard_map/finish/pallas_call | solution.py:53
  167.4 1.5 collective-permute-start.29
  168.9 2.8 %collective-permute-done.29.refs_11_ = f32[128,8]{1,0:T(8,128)S(1)} collective-permute-done((f32[128,8]{1,0:T(8,128)S(1)}, f32[128,8]{1,0:T(8,128)S(1)}, u32[]{:S(2)}, u32[]{:S(2)}) %collective-permute-start.29) | collective-permute-done | bytes 4128 | tf_op jit(solution)/shard_map/ppermute | solution.py:552
  171.7 1.2 all-to-all-done.1.refs_1_
  172.9 4.4 %second_grad.1 = (f32[32,2048]{1,0:T(8,128)S(1)}, f32[32,2048]{1,0:T(8,128)S(1)}, f32[32,768]{1,0:T(8,128)}, f32[8,128]{1,0:T(8,128)}) custom-call(s32[3]{0:T(128)S(1)} %pad_add_fusion.refs_0_, bf16[8,32,1024]{2,1,0:T(8,128)(2,1)S(1)} %all-to-all-done.1.refs_1_, bf16[128,2304]{1,0:T(8,128)(2,1)} %copy-done.3, bf16[128,2304]{1,0:T(8,128)(2,1)} %copy-done.4, ...), custom_call_target="tpu_custom_call" | custom-call | flops 1 | bytes 1 | tf_op jit(solution)/shard_map/second_grad/pallas_call | solution.py:53
  177.3 0.7 copy.20
  177.9 0.8 collective-permute-done.30
  178.8 0.7 add_bitcast_fusion
  (74 shorter events, 1.1 us)
Async XLA Ops:
  0.6 18.6 %copy-start.8 = (bf16[1,32,2048]{2,1,0:T(8,128)(2,1)S(1)}, bf16[1,32,2048]{2,1,0:T(8,128)(2,1)}, u32[]{:S(2)}) copy-start(bf16[1,32,2048]{2,1,0:T(8,128)(2,1)} %param.13) | copy-start | bytes 393220
  0.6 18.6 %collective-permute-start.2 = (bf16[1536,2048]{1,0:T(8,128)(2,1)}, bf16[1536,2048]{1,0:T(8,128)(2,1)}, u32[]{:S(2)}, u32[]{:S(2)}) collective-permute-start(bf16[1536,2048]{1,0:T(8,128)(2,1)} %bitcast.32), channel_id=1, source_target_pairs={{0,1},{1,0},{2,3},{3,2},{4,5},{5,4},{6,7},{7,6},{8,9},{9,8},{10,11... | collective-permute-start | bytes 18874376 | tf_op jit(solution)/shard_map/ppermute | solution.py:561
  0.8 0.8 copy-start.19
  1.6 0.7 copy-start.20
  3.4 24.0 %copy-start.3 = (bf16[128,2304]{1,0:T(8,128)(2,1)}, bf16[128,2304]{1,0:T(8,128)(2,1)S(1)}, u32[]{:S(2)}) copy-start(bf16[128,2304]{1,0:T(8,128)(2,1)S(1)} %get-tuple-element.57.refs_1_.refs_5_.refs_2_) | copy-start | bytes 1769476
  3.4 15.8 %collective-permute-start = (bf16[128,2304]{1,0:T(8,128)(2,1)S(1)}, bf16[128,2304]{1,0:T(8,128)(2,1)S(1)}, u32[]{:S(2)}, u32[]{:S(2)}) collective-permute-start(bf16[128,2304]{1,0:T(8,128)(2,1)S(1)} %get-tuple-element.57.refs_1_.refs_5_.refs_2_), channel_id=1, source_target_pairs={{0,4},{4,0},{8,12},{12,8},{16,20},{20,16},{24,28},{28,24},{1,5},{5... | collective-permute-start | bytes 1769480 | tf_op jit(solution)/shard_map/ppermute | solution.py:558
  5.0 28.1 %collective-permute-start.4 = (bf16[128,2304]{1,0:T(8,128)(2,1)S(1)}, bf16[128,2304]{1,0:T(8,128)(2,1)S(1)}, u32[]{:S(2)}, u32[]{:S(2)}) collective-permute-start(bf16[128,2304]{1,0:T(8,128)(2,1)S(1)} %get-tuple-element.57.refs_1_.refs_5_.refs_2_), channel_id=1, source_target_pairs={{0,16},{4,20},{8,24},{12,28},{16,0},{20,4},{24,8},{28,12},{1,17},{... | collective-permute-start | bytes 1769480 | tf_op jit(solution)/shard_map/ppermute | solution.py:558
  7.6 27.6 %collective-permute-start.3 = (bf16[128,2304]{1,0:T(8,128)(2,1)S(1)}, bf16[128,2304]{1,0:T(8,128)(2,1)S(1)}, u32[]{:S(2)}, u32[]{:S(2)}) collective-permute-start(bf16[128,2304]{1,0:T(8,128)(2,1)S(1)} %get-tuple-element.57.refs_1_.refs_5_.refs_2_), channel_id=1, source_target_pairs={{0,8},{4,12},{8,0},{12,4},{16,24},{20,28},{24,16},{28,20},{1,9},{5... | collective-permute-start | bytes 1769480 | tf_op jit(solution)/shard_map/ppermute | solution.py:558
  8.0 3.4 %collective-permute-start.1 = (bf16[32,2048]{1,0:T(8,128)(2,1)}, bf16[32,2048]{1,0:T(8,128)(2,1)S(1)}, u32[]{:S(2)}, u32[]{:S(2)}) collective-permute-start(bf16[32,2048]{1,0:T(8,128)(2,1)} %bitcast.18), channel_id=1, source_target_pairs={{0,1},{1,0},{2,3},{3,2},{4,5},{5,4},{6,7},{7,6},{8,9},{9,8},{10,11... | collective-permute-start | bytes 393224 | tf_op jit(solution)/shard_map/ppermute | solution.py:561
  19.2 8.2 %copy-start.4 = (bf16[128,2304]{1,0:T(8,128)(2,1)}, bf16[128,2304]{1,0:T(8,128)(2,1)S(1)}, u32[]{:S(2)}) copy-start(bf16[128,2304]{1,0:T(8,128)(2,1)S(1)} %collective-permute-done.refs_2_.refs_6_.refs_3_) | copy-start | bytes 1769476
  33.6 12.1 %copy-start.1 = (bf16[128,2304]{1,0:T(8,128)(2,1)}, bf16[128,2304]{1,0:T(8,128)(2,1)S(1)}, u32[]{:S(2)}) copy-start(bf16[128,2304]{1,0:T(8,128)(2,1)S(1)} %get-tuple-element.63.refs_2_.refs_8_.refs_5_) | copy-start | bytes 1769476
  33.6 15.3 %collective-permute-start.5 = (bf16[128,2304]{1,0:T(8,128)(2,1)S(1)}, bf16[128,2304]{1,0:T(8,128)(2,1)S(1)}, u32[]{:S(2)}, u32[]{:S(2)}) collective-permute-start(bf16[128,2304]{1,0:T(8,128)(2,1)S(1)} %get-tuple-element.63.refs_2_.refs_8_.refs_5_), channel_id=1, source_target_pairs={{0,8},{4,12},{8,0},{12,4},{16,24},{20,28},{24,16},{28,20},{1,9},{5... | collective-permute-start | bytes 1769480 | tf_op jit(solution)/shard_map/ppermute | solution.py:558
  35.1 10.0 %copy-start.5 = (bf16[128,2304]{1,0:T(8,128)(2,1)}, bf16[128,2304]{1,0:T(8,128)(2,1)S(1)}, u32[]{:S(2)}) copy-start(bf16[128,2304]{1,0:T(8,128)(2,1)S(1)} %collective-permute-done.3.refs_1_.refs_7_.refs_4_) | copy-start | bytes 1769476
  35.1 16.3 %collective-permute-start.6 = (bf16[128,2304]{1,0:T(8,128)(2,1)S(1)}, bf16[128,2304]{1,0:T(8,128)(2,1)S(1)}, u32[]{:S(2)}, u32[]{:S(2)}) collective-permute-start(bf16[128,2304]{1,0:T(8,128)(2,1)S(1)} %collective-permute-done.3.refs_1_.refs_7_.refs_4_), channel_id=1, source_target_pairs={{0,4},{4,0},{8,12},{12,8},{16,20},{20,16},{24,28},{28,24},{1,5},{5... | collective-permute-start | bytes 1769480 | tf_op jit(solution)/shard_map/ppermute | solution.py:558
  35.6 15.8 %collective-permute-start.8 = (bf16[320,768]{1,0:T(8,128)(2,1)S(1)}, bf16[320,768]{1,0:T(8,128)(2,1)S(1)}, u32[]{:S(2)}, u32[]{:S(2)}) collective-permute-start(bf16[320,768]{1,0:T(8,128)(2,1)S(1)} %get-tuple-element.69), channel_id=1, source_target_pairs={{0,2},{2,0},{1,3},{3,1},{4,6},{6,4},{5,7},{7,5},{8,10},{10,8},{9,1... | collective-permute-start | bytes 1474568 | tf_op jit(solution)/shard_map/ppermute | solution.py:552
  37.1 26.9 %copy-start.9 = (bf16[1,32,2048]{2,1,0:T(8,128)(2,1)S(1)}, bf16[1,32,2048]{2,1,0:T(8,128)(2,1)}, u32[]{:S(2)}) copy-start(bf16[1,32,2048]{2,1,0:T(8,128)(2,1)} %param.13) | copy-start | bytes 393220
  45.2 13.2 %collective-permute-start.7 = (bf16[320,768]{1,0:T(8,128)(2,1)S(1)}, bf16[320,768]{1,0:T(8,128)(2,1)S(1)}, u32[]{:S(2)}, u32[]{:S(2)}) collective-permute-start(bf16[320,768]{1,0:T(8,128)(2,1)S(1)} %get-tuple-element.67), channel_id=1, source_target_pairs={{0,2},{2,0},{1,3},{3,1},{4,6},{6,4},{5,7},{7,5},{8,10},{10,8},{9,1... | collective-permute-start | bytes 1474568 | tf_op jit(solution)/shard_map/ppermute | solution.py:552
  45.7 18.3 %collective-permute-start.9 = (bf16[128,2304]{1,0:T(8,128)(2,1)S(1)}, bf16[128,2304]{1,0:T(8,128)(2,1)S(1)}, u32[]{:S(2)}, u32[]{:S(2)}) collective-permute-start(bf16[128,2304]{1,0:T(8,128)(2,1)S(1)} %get-tuple-element.63.refs_2_.refs_8_.refs_5_), channel_id=1, source_target_pairs={{0,4},{4,0},{8,12},{12,8},{16,20},{20,16},{24,28},{28,24},{1,5},{5... | collective-permute-start | bytes 1769480 | tf_op jit(solution)/shard_map/ppermute | solution.py:558
  49.0 23.5 %copy-start.6 = (bf16[128,2304]{1,0:T(8,128)(2,1)}, bf16[128,2304]{1,0:T(8,128)(2,1)S(1)}, u32[]{:S(2)}) copy-start(bf16[128,2304]{1,0:T(8,128)(2,1)S(1)} %collective-permute-done.5.refs_1_.refs_9_.refs_6_) | copy-start | bytes 1769476
  49.0 36.3 %collective-permute-start.10 = (bf16[128,2304]{1,0:T(8,128)(2,1)S(1)}, bf16[128,2304]{1,0:T(8,128)(2,1)S(1)}, u32[]{:S(2)}, u32[]{:S(2)}) collective-permute-start(bf16[128,2304]{1,0:T(8,128)(2,1)S(1)} %collective-permute-done.5.refs_1_.refs_9_.refs_6_), channel_id=1, source_target_pairs={{0,4},{4,0},{8,12},{12,8},{16,20},{20,16},{24,28},{28,24},{1,5},{5... | collective-permute-start | bytes 1769480 | tf_op jit(solution)/shard_map/ppermute | solution.py:558
  51.4 21.0 %copy-start = (bf16[128,2304]{1,0:T(8,128)(2,1)}, bf16[128,2304]{1,0:T(8,128)(2,1)S(1)}, u32[]{:S(2)}) copy-start(bf16[128,2304]{1,0:T(8,128)(2,1)S(1)} %collective-permute-done.6.refs_4_.refs_2_.refs_10_.refs_7_) | copy-start | bytes 1769476
  52.1 12.0 %copy-start.18 = (bf16[160,768]{1,0:T(8,128)(2,1)}, bf16[160,768]{1,0:T(8,128)(2,1)S(1)}, u32[]{:S(2)}) copy-start(bf16[160,768]{1,0:T(8,128)(2,1)S(1)} %get-tuple-element.93.refs_8_) | copy-start | bytes 737284
  59.6 14.4 %collective-permute-start.11 = (bf16[160,768]{1,0:T(8,128)(2,1)S(1)}, bf16[160,768]{1,0:T(8,128)(2,1)S(1)}, u32[]{:S(2)}, u32[]{:S(2)}) collective-permute-start(bf16[160,768]{1,0:T(8,128)(2,1)S(1)} %get-tuple-element.75), channel_id=1, source_target_pairs={{0,8},{4,12},{8,0},{12,4},{16,24},{20,28},{24,16},{28,20},{1,9},{5... | collective-permute-start | bytes 737288 | tf_op jit(solution)/shard_map/ppermute | solution.py:558
  64.1 21.2 %copy-start.2 = (bf16[128,2304]{1,0:T(8,128)(2,1)}, bf16[128,2304]{1,0:T(8,128)(2,1)S(1)}, u32[]{:S(2)}) copy-start(bf16[128,2304]{1,0:T(8,128)(2,1)S(1)} %collective-permute-done.9.refs_8_.refs_1_.refs_11_) | copy-start | bytes 1769476
  72.5 22.2 %collective-permute-start.13 = (bf16[320,768]{1,0:T(8,128)(2,1)S(1)}, bf16[320,768]{1,0:T(8,128)(2,1)S(1)}, u32[]{:S(2)}, u32[]{:S(2)}) collective-permute-start(bf16[320,768]{1,0:T(8,128)(2,1)S(1)} %get-tuple-element.78), channel_id=1, source_target_pairs={{0,2},{2,0},{1,3},{3,1},{4,6},{6,4},{5,7},{7,5},{8,10},{10,8},{9,1... | collective-permute-start | bytes 1474568 | tf_op jit(solution)/shard_map/ppermute | solution.py:552
  74.0 11.2 %collective-permute-start.12 = (bf16[160,768]{1,0:T(8,128)(2,1)S(1)}, bf16[160,768]{1,0:T(8,128)(2,1)S(1)}, u32[]{:S(2)}, u32[]{:S(2)}) collective-permute-start(bf16[160,768]{1,0:T(8,128)(2,1)S(1)} %collective-permute-done.11), channel_id=1, source_target_pairs={{0,24},{4,28},{8,16},{12,20},{16,8},{20,12},{24,0},{28,4},{1,25},{... | collective-permute-start | bytes 737288 | tf_op jit(solution)/shard_map/ppermute | solution.py:558
  85.2 8.3 %copy-start.16 = (bf16[160,768]{1,0:T(8,128)(2,1)}, bf16[160,768]{1,0:T(8,128)(2,1)S(1)}, u32[]{:S(2)}) copy-start(bf16[160,768]{1,0:T(8,128)(2,1)S(1)} %collective-permute-done.12.refs_8_.refs_12_) | copy-start | bytes 737284
  85.2 8.3 %copy-start.7 = (bf16[128,2304]{1,0:T(8,128)(2,1)}, bf16[128,2304]{1,0:T(8,128)(2,1)S(1)}, u32[]{:S(2)}) copy-start(bf16[128,2304]{1,0:T(8,128)(2,1)S(1)} %collective-permute-done.10.refs_2_.refs_12_.refs_9_) | copy-start | bytes 1769476
  93.5 17.9 %copy-start.21 = (s32[128,8]{0,1:T(8,128)S(1)}, s32[128,8]{0,1:T(8,128)}, u32[]{:S(2)}) copy-start(s32[128,8]{0,1:T(8,128)} %param.9) | copy-start | bytes 12292
  93.5 33.0 %copy-start.23 = (bf16[128,8]{0,1:T(8,128)(2,1)S(1)}, bf16[128,8]{0,1:T(8,128)(2,1)}, u32[]{:S(2)}) copy-start(bf16[128,8]{0,1:T(8,128)(2,1)} %param.10) | copy-start | bytes 6148
  93.6 14.6 %collective-permute-start.16 = (bf16[320,768]{1,0:T(8,128)(2,1)S(1)}, bf16[320,768]{1,0:T(8,128)(2,1)S(1)}, u32[]{:S(2)}, u32[]{:S(2)}) collective-permute-start(bf16[320,768]{1,0:T(8,128)(2,1)S(1)} %get-tuple-element.84), channel_id=1, source_target_pairs={{0,2},{2,0},{1,3},{3,1},{4,6},{6,4},{5,7},{7,5},{8,10},{10,8},{9,1... | collective-permute-start | bytes 1474568 | tf_op jit(solution)/shard_map/ppermute | solution.py:552
  94.2 11.7 %collective-permute-start.19 = (bf16[160,768]{1,0:T(8,128)(2,1)}, bf16[160,768]{1,0:T(8,128)(2,1)S(1)}, u32[]{:S(2)}, u32[]{:S(2)}) collective-permute-start(bf16[160,768]{1,0:T(8,128)(2,1)} %get-tuple-element.88), channel_id=1, source_target_pairs={{0,8},{4,12},{8,0},{12,4},{16,24},{20,28},{24,16},{28,20},{1,9},{5... | collective-permute-start | bytes 737288 | tf_op jit(solution)/shard_map/ppermute | solution.py:558
  94.2 13.2 %collective-permute-start.18 = (bf16[160,768]{1,0:T(8,128)(2,1)S(1)}, bf16[160,768]{1,0:T(8,128)(2,1)S(1)}, u32[]{:S(2)}, u32[]{:S(2)}) collective-permute-start(bf16[160,768]{1,0:T(8,128)(2,1)S(1)} %get-tuple-element.87), channel_id=1, source_target_pairs={{0,4},{4,0},{8,12},{12,8},{16,20},{20,16},{24,28},{28,24},{1,5},{5... | collective-permute-start | bytes 737288 | tf_op jit(solution)/shard_map/ppermute | solution.py:558
  96.0 3.5 %copy-start.22 = (bf16[160,768]{1,0:T(8,128)(2,1)}, bf16[160,768]{1,0:T(8,128)(2,1)S(1)}, u32[]{:S(2)}) copy-start(bf16[160,768]{1,0:T(8,128)(2,1)S(1)} %get-tuple-element.91) | copy-start | bytes 737284
  96.0 12.1 %collective-permute-start.17 = (bf16[160,768]{1,0:T(8,128)(2,1)}, bf16[160,768]{1,0:T(8,128)(2,1)S(1)}, u32[]{:S(2)}, u32[]{:S(2)}) collective-permute-start(bf16[160,768]{1,0:T(8,128)(2,1)} %get-tuple-element.86), channel_id=1, source_target_pairs={{0,24},{4,28},{8,16},{12,20},{16,8},{20,12},{24,0},{28,4},{1,25},{... | collective-permute-start | bytes 737288 | tf_op jit(solution)/shard_map/ppermute | solution.py:558
  99.5 12.1 %collective-permute-start.15 = (bf16[8,32,768]{2,1,0:T(8,128)(2,1)S(1)}, bf16[8,32,768]{2,1,0:T(8,128)(2,1)S(1)}, u32[]{:S(2)}, u32[]{:S(2)}) collective-permute-start(bf16[8,32,768]{2,1,0:T(8,128)(2,1)S(1)} %get-tuple-element.82), channel_id=1, source_target_pairs={{0,1},{1,0},{2,3},{3,2},{4,5},{5,4},{6,7},{7,6},{8,9},{9,8},{10,11... | collective-permute-start | bytes 1179656 | tf_op jit(solution)/shard_map/ppermute | solution.py:561
  99.5 12.1 %all-to-all-start = ((bf16[8,64,128]{2,1,0:T(8,128)(2,1)}), bf16[8,64,128]{2,1,0:T(8,128)(2,1)S(1)}, u32[]{:S(2)}, u32[]{:S(2)}) async-start(bf16[8,64,128]{2,1,0:T(8,128)(2,1)} %get-tuple-element.81), calls=%async_computation | async-start | bytes 262144 | tf_op jit(solution)/shard_map/all_to_all | solution.py:566
  105.8 53.7 %copy-start.10 = (bf16[160,768]{1,0:T(8,128)(2,1)}, bf16[160,768]{1,0:T(8,128)(2,1)S(1)}, u32[]{:S(2)}) copy-start(bf16[160,768]{1,0:T(8,128)(2,1)S(1)} %collective-permute-done.19.refs_6_.refs_10_) | copy-start | bytes 737284
  105.8 10.9 %collective-permute-start.20 = (bf16[160,768]{1,0:T(8,128)(2,1)}, bf16[160,768]{1,0:T(8,128)(2,1)}, u32[]{:S(2)}, u32[]{:S(2)}) collective-permute-start(bf16[160,768]{1,0:T(8,128)(2,1)} %copy-done.22), channel_id=1, source_target_pairs={{0,4},{4,0},{8,12},{12,8},{16,20},{20,16},{24,28},{28,24},{1,5},{5... | collective-permute-start | bytes 737288 | tf_op jit(solution)/shard_map/ppermute | solution.py:558
  107.4 52.1 %copy-start.11 = (bf16[160,768]{1,0:T(8,128)(2,1)}, bf16[160,768]{1,0:T(8,128)(2,1)S(1)}, u32[]{:S(2)}) copy-start(bf16[160,768]{1,0:T(8,128)(2,1)S(1)} %collective-permute-done.18.refs_5_.refs_9_) | copy-start | bytes 737284
  108.1 51.4 %copy-start.12 = (bf16[160,768]{1,0:T(8,128)(2,1)}, bf16[160,768]{1,0:T(8,128)(2,1)S(1)}, u32[]{:S(2)}) copy-start(bf16[160,768]{1,0:T(8,128)(2,1)S(1)} %collective-permute-done.17.refs_4_.refs_14_) | copy-start | bytes 737284
  109.4 11.8 %collective-permute-start.22 = (bf16[160,768]{1,0:T(8,128)(2,1)}, bf16[160,768]{1,0:T(8,128)(2,1)}, u32[]{:S(2)}, u32[]{:S(2)}) collective-permute-start(bf16[160,768]{1,0:T(8,128)(2,1)} %get-tuple-element.94), channel_id=1, source_target_pairs={{0,4},{4,0},{8,12},{12,8},{16,20},{20,16},{24,28},{28,24},{1,5},{5... | collective-permute-start | bytes 737288 | tf_op jit(solution)/shard_map/ppermute | solution.py:558
  111.4 14.5 %collective-permute-start.24 = (bf16[160,768]{1,0:T(8,128)(2,1)S(1)}, bf16[160,768]{1,0:T(8,128)(2,1)}, u32[]{:S(2)}, u32[]{:S(2)}) collective-permute-start(bf16[160,768]{1,0:T(8,128)(2,1)S(1)} %get-tuple-element.95), channel_id=1, source_target_pairs={{0,4},{4,0},{8,12},{12,8},{16,20},{20,16},{24,28},{28,24},{1,5},{5... | collective-permute-start | bytes 737288 | tf_op jit(solution)/shard_map/ppermute | solution.py:558
  115.1 13.7 %collective-permute-start.27 = (f32[128,512]{1,0:T(8,128)S(1)}, f32[128,512]{1,0:T(8,128)S(1)}, u32[]{:S(2)}, u32[]{:S(2)}) collective-permute-start(f32[128,512]{1,0:T(8,128)S(1)} %get-tuple-element.96.refs_7_), channel_id=1, source_target_pairs={{0,2},{2,0},{1,3},{3,1},{4,6},{6,4},{5,7},{7,5},{8,10},{10,8},{9,1... | collective-permute-start | bytes 786440 | tf_op jit(solution)/shard_map/ppermute | solution.py:552
  116.7 11.5 %collective-permute-start.21 = (bf16[160,768]{1,0:T(8,128)(2,1)}, bf16[160,768]{1,0:T(8,128)(2,1)S(1)}, u32[]{:S(2)}, u32[]{:S(2)}) collective-permute-start(bf16[160,768]{1,0:T(8,128)(2,1)} %collective-permute-done.20), channel_id=1, source_target_pairs={{0,8},{4,12},{8,0},{12,4},{16,24},{20,28},{24,16},{28,20},{1,9},{5... | collective-permute-start | bytes 737288 | tf_op jit(solution)/shard_map/ppermute | solution.py:558
  121.2 12.4 %collective-permute-start.23 = (bf16[160,768]{1,0:T(8,128)(2,1)}, bf16[160,768]{1,0:T(8,128)(2,1)S(1)}, u32[]{:S(2)}, u32[]{:S(2)}) collective-permute-start(bf16[160,768]{1,0:T(8,128)(2,1)} %collective-permute-done.22), channel_id=1, source_target_pairs={{0,16},{4,20},{8,24},{12,28},{16,0},{20,4},{24,8},{28,12},{1,17},{... | collective-permute-start | bytes 737288 | tf_op jit(solution)/shard_map/ppermute | solution.py:558
  123.2 5.0 %collective-permute-start.14 = (bf16[8,64,128]{2,1,0:T(8,128)(2,1)S(1)}, bf16[8,64,128]{2,1,0:T(8,128)(2,1)S(1)}, u32[]{:S(2)}, u32[]{:S(2)}) collective-permute-start(bf16[8,64,128]{2,1,0:T(8,128)(2,1)S(1)} %all-to-all-done.refs_6_.refs_1_), channel_id=1, source_target_pairs={{0,2},{2,0},{1,3},{3,1},{4,6},{6,4},{5,7},{7,5},{8,10},{10,8},{9,1... | collective-permute-start | bytes 393224 | tf_op jit(solution)/shard_map/ppermute | solution.py:552
  125.9 12.5 %collective-permute-start.25 = (bf16[160,768]{1,0:T(8,128)(2,1)}, bf16[160,768]{1,0:T(8,128)(2,1)S(1)}, u32[]{:S(2)}, u32[]{:S(2)}) collective-permute-start(bf16[160,768]{1,0:T(8,128)(2,1)} %collective-permute-done.24), channel_id=1, source_target_pairs={{0,8},{4,12},{8,0},{12,4},{16,24},{20,28},{24,16},{28,20},{1,9},{5... | collective-permute-start | bytes 737288 | tf_op jit(solution)/shard_map/ppermute | solution.py:558
  128.2 31.4 %copy-start.13 = (bf16[160,768]{1,0:T(8,128)(2,1)}, bf16[160,768]{1,0:T(8,128)(2,1)S(1)}, u32[]{:S(2)}) copy-start(bf16[160,768]{1,0:T(8,128)(2,1)S(1)} %collective-permute-done.21.refs_4_.refs_11_) | copy-start | bytes 737284
  133.6 26.0 %copy-start.14 = (bf16[160,768]{1,0:T(8,128)(2,1)}, bf16[160,768]{1,0:T(8,128)(2,1)S(1)}, u32[]{:S(2)}) copy-start(bf16[160,768]{1,0:T(8,128)(2,1)S(1)} %collective-permute-done.23.refs_10_.refs_13_) | copy-start | bytes 737284
  138.3 12.7 %collective-permute-start.28 = (bf16[8,32,768]{2,1,0:T(8,128)(2,1)S(1)}, bf16[8,32,768]{2,1,0:T(8,128)(2,1)S(1)}, u32[]{:S(2)}, u32[]{:S(2)}) collective-permute-start(bf16[8,32,768]{2,1,0:T(8,128)(2,1)S(1)} %get-tuple-element.99), channel_id=1, source_target_pairs={{0,1},{1,0},{2,3},{3,2},{4,5},{5,4},{6,7},{7,6},{8,9},{9,8},{10,11... | collective-permute-start | bytes 1179656 | tf_op jit(solution)/shard_map/ppermute | solution.py:561
  138.4 12.6 %collective-permute-start.26 = (bf16[160,768]{1,0:T(8,128)(2,1)S(1)}, bf16[160,768]{1,0:T(8,128)(2,1)S(1)}, u32[]{:S(2)}, u32[]{:S(2)}) collective-permute-start(bf16[160,768]{1,0:T(8,128)(2,1)S(1)} %collective-permute-done.25), channel_id=1, source_target_pairs={{0,16},{4,20},{8,24},{12,28},{16,0},{20,4},{24,8},{28,12},{1,17},{... | collective-permute-start | bytes 737288 | tf_op jit(solution)/shard_map/ppermute | solution.py:558
  151.0 8.5 %copy-start.15 = (bf16[160,768]{1,0:T(8,128)(2,1)}, bf16[160,768]{1,0:T(8,128)(2,1)S(1)}, u32[]{:S(2)}) copy-start(bf16[160,768]{1,0:T(8,128)(2,1)S(1)} %collective-permute-done.26.refs_5_.refs_15_) | copy-start | bytes 737284
  151.6 0.8 copy-start.17
  152.4 20.4 %all-to-all-start.1 = ((bf16[8,32,1024]{2,1,0:T(8,128)(2,1)}), bf16[8,32,1024]{2,1,0:T(8,128)(2,1)S(1)}, u32[]{:S(2)}, u32[]{:S(2)}) async-start(bf16[8,32,1024]{2,1,0:T(8,128)(2,1)} %copy-done.17), calls=%async_computation.1 | async-start | bytes 1048576 | tf_op jit(solution)/shard_map/all_to_all | solution.py:566
  167.4 4.3 %collective-permute-start.29 = (f32[128,8]{1,0:T(8,128)S(1)}, f32[128,8]{1,0:T(8,128)S(1)}, u32[]{:S(2)}, u32[]{:S(2)}) collective-permute-start(f32[128,8]{1,0:T(8,128)S(1)} %get-tuple-element.104), channel_id=1, source_target_pairs={{0,2},{2,0},{1,3},{3,1},{4,6},{6,4},{5,7},{7,5},{8,10},{10,8},{9,1... | collective-permute-start | bytes 12296 | tf_op jit(solution)/shard_map/ppermute | solution.py:552
  177.3 1.5 collective-permute-start.30

commit v15 on v14

--- a/solution.py
+++ b/solution.py
@@ -596,7 +596,7 @@
         for o, rows in zip(batches[i], share_sum_call(order, shared[i], 2, slots)):
             masks = [o] if o else []
             if i >= last - 1 and o % 2:
-                masks = [1 << k for k in range(o.bit_length()) if o >> k & 1]
+                masks = [o - 1, 1] if o > 1 else [1]
             elif o == 4 and groups == 8:
                 masks = [2, 6]
             for mask in masks:
@@ -611,8 +611,6 @@
         elif kind == "total":
             total(i)
         else:
-            if i == last and groups == 8:
-                order.wait([back[4]])
             *give, keep, low = expert_rows_call(
                 order, [fetch(o) for o in batches[i]], seconds, downs, shares, slots
             )
@@ -625,7 +623,7 @@
     low_grad, first_own = collect_call(order, places, lows, grads, feats)
     firsts = [x.reshape(groups * rank, units) for x in (first_own, swap(first_own))]
     low_grad = exchange(low_grad)
-    order.wait([back[batches[-2][0]], back[1], back[2]])
+    order.wait([back[batches[-2][0]], back[1], back[2]] + [back[4]] * (groups == 8))
     total(last)
     order.wait([low_grad])
     low_hid = all_shares(lowrank_hid_call(order, index, hid, firsts, groups))

time: 183 us -> 177 us (0.967)
  waiting for transfers between devices: 60 us -> 53.9 us
    ppermute x19 -> x18, waiting for transfers between devices: 47.3 us -> 36.3 us  [flip(): return lax.ppermute(x, 'ep', [(i, i ^ mask) for i in range(groups)])]
    all_to_all x2, starting transfers between devices: 13.4 us -> 21 us  [exchange(): return lax.all_to_all(x, axes, split_axis=0, concat_axis=0, tiled=True)]
    ppermute x19 -> x18, starting transfers between devices: 26.2 us -> 19.4 us  [flip(): return lax.ppermute(x, 'ep', [(i, i ^ mask) for i in range(groups)])]
    ppermute x7, waiting for transfers between devices: 10.6 us -> 14.5 us  [turn(): lax.ppermute(x, 'rep', [(r, (r + offset) % shares) for r in range(shares)])]
    ppermute x7, starting transfers between devices: 8.78 us -> 6.86 us  [turn(): lax.ppermute(x, 'rep', [(r, (r + offset) % shares) for r in range(shares)])]
    unnamed x51 -> x53, local copies, waits for them, and re-layouts: 3.26 us -> 4.65 us
  transfers between devices with their start and end apart: 33 -> 32, of which waited for: 16 -> 18; matrix products, arithmetic and copies ran while one was open for 1% -> 1% of each run, Pallas kernels for 34% -> 35%
where the time goes in v15:
time: 177 us; the launch traced here: 174 us
  Pallas kernels  65.8 us (37%)
  waiting for transfers between devices  53.9 us (30%)
  starting transfers between devices  47.5 us (27%)
  local copies, waits for them, and re-layouts  4.65 us (3%)
    pallas_call x18, Pallas kernels, call(): pl.pallas_call(ordered, grid=grid, in_specs=[SMEM, *in_specs] + [ANY] * l...  65.8 us
    ppermute x18, waiting for transfers between devices, flip(): return lax.ppermute(x, 'ep', [(i, i ^ mask) for i in range(groups)])  36.3 us
    all_to_all x2, starting transfers between devices, exchange(): return lax.all_to_all(x, axes, split_axis=0, concat_axis=0, tiled=True)  21 us
    ppermute x18, starting transfers between devices, flip(): return lax.ppermute(x, 'ep', [(i, i ^ mask) for i in range(groups)])  19.4 us
    ppermute x7, waiting for transfers between devices, turn(): lax.ppermute(x, 'rep', [(r, (r + offset) % shares) for r in range(shares)])  14.5 us
    ppermute x7, starting transfers between devices, turn(): lax.ppermute(x, 'rep', [(r, (r + offset) % shares) for r in range(shares)])  6.86 us
    unnamed x53, local copies, waits for them, and re-layouts  4.65 us
  transfers between devices with their start and end apart: 32, of which 18 were waited for; matrix products, arithmetic and copies ran while one was open for 1% of the time, Pallas kernels for 35%

profile of v15, /device:TPU:8, one launch (start us, length us, event | category | flops | bytes accessed | tf_op | source)
XLA Modules:
  0.0 173.7 jit_solution(8702690101495515753)
XLA Ops:
  0.8 0.8 copy-done.19
  1.6 0.7 copy-done.20
  2.3 1.1 pack_block.1
  3.4 1.6 collective-permute-start
  5.0 2.6 %collective-permute-start.4 = (bf16[128,2304]{1,0:T(8,128)(2,1)S(1)}, bf16[128,2304]{1,0:T(8,128)(2,1)S(1)}, u32[]{:S(2)}, u32[]{:S(2)}) collective-permute-start(bf16[128,2304]{1,0:T(8,128)(2,1)S(1)} %get-tuple-element.57.refs_1_.refs_5_.refs_2_), channel_id=1, source_target_pairs={{0,16},{4,20},{8,24},{12,28},{16,0},{20,4},{24,8},{28,12},{1,17},{... | collective-permute-start | bytes 1769480 | tf_op jit(solution)/shard_map/ppermute | solution.py:558
  8.0 3.4 %load_matrix.1 = (bf16[1536,2048]{1,0:T(8,128)(2,1)S(1)}, f32[8,128]{1,0:T(8,128)}) custom-call(s32[3]{0:T(128)S(1)} %pad_add_fusion.refs_0_, bf16[1536,2048]{1,0:T(8,128)(2,1)} %bitcast.33, f32[8,128]{1,0:T(8,128)} %get-tuple-element.58.refs_2_), custom_call_target="tpu_custom_call" | custom-call | flops 1 | bytes 1 | tf_op jit(solution)/shard_map/load_matrix/pallas_call | solution.py:53
  11.5 7.7 %collective-permute-done.refs_2_.refs_6_.refs_3_ = bf16[128,2304]{1,0:T(8,128)(2,1)S(1)} collective-permute-done((bf16[128,2304]{1,0:T(8,128)(2,1)S(1)}, bf16[128,2304]{1,0:T(8,128)(2,1)S(1)}, u32[]{:S(2)}, u32[]{:S(2)}) %collective-permute-start) | collective-permute-done | bytes 589856 | tf_op jit(solution)/shard_map/ppermute | solution.py:558
  19.2 8.2 %expert_rows.4 = (bf16[320,768]{1,0:T(8,128)(2,1)S(1)}, bf16[320,768]{1,0:T(8,128)(2,1)S(1)}, bf16[2,64,128]{2,1,0:T(8,128)(2,1)S(1)}, f32[8,128]{1,0:T(8,128)}) custom-call(s32[3]{0:T(128)S(1)} %pad_add_fusion.refs_0_, bf16[128,2304]{1,0:T(8,128)(2,1)S(1)} %get-tuple-element.57.refs_1_.refs_5_.refs_2_, ...), custom_call_target="tpu_custom_call" | custom-call | flops 1 | bytes 1 | tf_op jit(solution)/shard_map/expert_rows/pallas_call | solution.py:53
  27.5 5.6 %collective-permute-done.4.refs_1_ = bf16[128,2304]{1,0:T(8,128)(2,1)S(1)} collective-permute-done((bf16[128,2304]{1,0:T(8,128)(2,1)S(1)}, bf16[128,2304]{1,0:T(8,128)(2,1)S(1)}, u32[]{:S(2)}, u32[]{:S(2)}) %collective-permute-start.4) | collective-permute-done | bytes 589856 | tf_op jit(solution)/shard_map/ppermute | solution.py:558
  33.1 0.5 gate.1
  33.6 1.5 collective-permute-start.5
  35.1 0.5 collective-permute-start.6
  35.6 1.6 collective-permute-start.9
  37.2 1.5 collective-permute-start.8
  38.7 8.0 %expert_rows.5 = (bf16[320,768]{1,0:T(8,128)(2,1)S(1)}, bf16[320,768]{1,0:T(8,128)(2,1)S(1)}, bf16[2,64,128]{2,1,0:T(8,128)(2,1)S(1)}, f32[8,128]{1,0:T(8,128)}) custom-call(s32[3]{0:T(128)S(1)} %pad_add_fusion.refs_0_, bf16[128,2304]{1,0:T(8,128)(2,1)S(1)} %collective-permute-done.3.refs_1_.refs_7_.refs_4_, ...), custom_call_target="tpu_custom_call" | custom-call | flops 1 | bytes 1 | tf_op jit(solution)/shard_map/expert_rows/pallas_call | solution.py:53
  46.7 0.6 collective-permute-start.7
  47.3 1.7 collective-permute-done.5.refs_1_.refs_9_.refs_6_
  49.0 0.5 collective-permute-start.10
  49.5 1.9 %collective-permute-done.6.refs_4_.refs_2_.refs_10_.refs_7_ = bf16[128,2304]{1,0:T(8,128)(2,1)S(1)} collective-permute-done((bf16[128,2304]{1,0:T(8,128)(2,1)S(1)}, bf16[128,2304]{1,0:T(8,128)(2,1)S(1)}, u32[]{:S(2)}, u32[]{:S(2)}) %collective-permute-start.6) | collective-permute-done | bytes 589856 | tf_op jit(solution)/shard_map/ppermute | solution.py:558
  51.4 1.3 share_sum.4
  52.7 6.6 %collective-permute-done.7.refs_2_ = bf16[320,768]{1,0:T(8,128)(2,1)S(1)} collective-permute-done((bf16[320,768]{1,0:T(8,128)(2,1)S(1)}, bf16[320,768]{1,0:T(8,128)(2,1)S(1)}, u32[]{:S(2)}, u32[]{:S(2)}) %collective-permute-start.7) | collective-permute-done | bytes 491552 | tf_op jit(solution)/shard_map/ppermute | solution.py:552
  59.3 0.7 share_sum.5
  60.0 4.1 %collective-permute-done.9.refs_8_.refs_1_.refs_11_ = bf16[128,2304]{1,0:T(8,128)(2,1)S(1)} collective-permute-done((bf16[128,2304]{1,0:T(8,128)(2,1)S(1)}, bf16[128,2304]{1,0:T(8,128)(2,1)S(1)}, u32[]{:S(2)}, u32[]{:S(2)}) %collective-permute-start.9) | collective-permute-done | bytes 589856 | tf_op jit(solution)/shard_map/ppermute | solution.py:558
  64.1 8.4 %expert_rows.6 = (bf16[320,768]{1,0:T(8,128)(2,1)S(1)}, bf16[320,768]{1,0:T(8,128)(2,1)S(1)}, bf16[2,64,128]{2,1,0:T(8,128)(2,1)S(1)}, f32[8,128]{1,0:T(8,128)}) custom-call(s32[3]{0:T(128)S(1)} %pad_add_fusion.refs_0_, bf16[128,2304]{1,0:T(8,128)(2,1)S(1)} %collective-permute-done.5.refs_1_.refs_9_.refs_6_, ...), custom_call_target="tpu_custom_call" | custom-call | flops 1 | bytes 1 | tf_op jit(solution)/shard_map/expert_rows/pallas_call | solution.py:53
  72.4 1.6 collective-permute-start.11
  74.0 0.5 collective-permute-start.18
  74.7 8.2 %expert_rows.7 = (bf16[320,768]{1,0:T(8,128)(2,1)S(1)}, bf16[320,768]{1,0:T(8,128)(2,1)S(1)}, bf16[2,64,128]{2,1,0:T(8,128)(2,1)S(1)}, f32[8,128]{1,0:T(8,128)}) custom-call(s32[3]{0:T(128)S(1)} %pad_add_fusion.refs_0_, bf16[128,2304]{1,0:T(8,128)(2,1)S(1)} %collective-permute-done.9.refs_8_.refs_1_.refs_11_, ...), custom_call_target="tpu_custom_call" | custom-call | flops 1 | bytes 1 | tf_op jit(solution)/shard_map/expert_rows/pallas_call | solution.py:53
  82.9 1.6 collective-permute-start.14
  84.5 1.3 collective-permute-start.17
  85.8 0.5 collective-permute-start.16
  86.3 2.3 %collective-permute-start.19 = (bf16[160,768]{1,0:T(8,128)(2,1)}, bf16[160,768]{1,0:T(8,128)(2,1)S(1)}, u32[]{:S(2)}, u32[]{:S(2)}) collective-permute-start(bf16[160,768]{1,0:T(8,128)(2,1)} %collective-permute-done.18), channel_id=1, source_target_pairs={{0,24},{4,28},{8,16},{12,20},{16,8},{20,12},{24,0},{28,4},{1,25},{... | collective-permute-start | bytes 737288 | tf_op jit(solution)/shard_map/ppermute | solution.py:558
  88.6 1.3 share_sum.6
  89.9 0.7 copy-done.23
  90.6 1.7 %collect_blocks.1 = (bf16[8,64,128]{2,1,0:T(8,128)(2,1)}, bf16[8,32,768]{2,1,0:T(8,128)(2,1)S(1)}, f32[8,128]{1,0:T(8,128)}) custom-call(s32[3]{0:T(128)S(1)} %pad_add_fusion.refs_0_, bf16[2,64,128]{2,1,0:T(8,128)(2,1)S(1)} %get-tuple-element.61.refs_1_, bf16[2,64,128]{2,1,0:T(8,128)(2,1)S(1)} %get-tuple-element.65.refs_2_, ...), custom_call_target="tpu_custom_call" | custom-call | flops 1 | bytes 1 | tf_op jit(solution)/shard_map/collect_blocks/pallas_call | solution.py:53
  92.4 15.1 %all-to-all-start = ((bf16[8,64,128]{2,1,0:T(8,128)(2,1)}), bf16[8,64,128]{2,1,0:T(8,128)(2,1)S(1)}, u32[]{:S(2)}, u32[]{:S(2)}) async-start(bf16[8,64,128]{2,1,0:T(8,128)(2,1)} %get-tuple-element.80), calls=%async_computation | async-start | bytes 262144 | tf_op jit(solution)/shard_map/all_to_all | solution.py:566
  107.7 1.5 collective-permute-done.15.refs_4_.refs_14_
  109.2 1.3 share_sum.7
  110.4 0.7 copy-done.22
  111.1 1.4 collective-permute-start.22
  112.7 1.1 all-to-all-done.refs_6_.refs_1_
  113.7 3.6 %lowrank_hid.1 = (f32[128,512]{1,0:T(8,128)S(1)}, f32[8,128]{1,0:T(8,128)}) custom-call(s32[3]{0:T(128)S(1)} %pad_add_fusion.refs_0_, s32[128,8]{1,0:T(8,128)S(1)} %copy.17.refs_1_.refs_5_.refs_2_, bf16[1024,768]{1,0:T(8,128)(2,1)} %bitcast.29, bf16[256,768]{1,0:T(8,128)(2,1)S(1)} %bitcast.23, bf16[256,768]{1,0:T(8,128)(2,1)S(1)} %bitcast.25, ...), custom_call_target="tpu_custom_call" | custom-call | flops 1 | bytes 1 | tf_op jit(solution)/shard_map/lowrank_hid/pallas_call | solution.py:53
  117.3 0.6 collective-permute-start.26
  117.9 2.4 %collective-permute-done.20 = bf16[160,768]{1,0:T(8,128)(2,1)} collective-permute-done((bf16[160,768]{1,0:T(8,128)(2,1)}, bf16[160,768]{1,0:T(8,128)(2,1)}, u32[]{:S(2)}, u32[]{:S(2)}) %collective-permute-start.20) | collective-permute-done | bytes 245792 | tf_op jit(solution)/shard_map/ppermute | solution.py:558
  120.3 1.5 collective-permute-start.21
  121.8 2.0 %collective-permute-done.22 = bf16[160,768]{1,0:T(8,128)(2,1)} collective-permute-done((bf16[160,768]{1,0:T(8,128)(2,1)}, bf16[160,768]{1,0:T(8,128)(2,1)}, u32[]{:S(2)}, u32[]{:S(2)}) %collective-permute-start.22) | collective-permute-done | bytes 245792 | tf_op jit(solution)/shard_map/ppermute | solution.py:558
  123.8 1.5 collective-permute-start.23
  125.2 0.5 collective-permute-start.12
  126.0 4.2 %collective-permute-done.12.refs_2_ = bf16[8,64,128]{2,1,0:T(8,128)(2,1)S(1)} collective-permute-done((bf16[8,64,128]{2,1,0:T(8,128)(2,1)S(1)}, bf16[8,64,128]{2,1,0:T(8,128)(2,1)S(1)}, u32[]{:S(2)}, u32[]{:S(2)}) %collective-permute-start.12) | collective-permute-done | bytes 131104 | tf_op jit(solution)/shard_map/ppermute | solution.py:552
  130.2 0.7 low_dense.1
  130.9 2.1 %collective-permute-done.23.refs_10_.refs_13_ = bf16[160,768]{1,0:T(8,128)(2,1)S(1)} collective-permute-done((bf16[160,768]{1,0:T(8,128)(2,1)}, bf16[160,768]{1,0:T(8,128)(2,1)S(1)}, u32[]{:S(2)}, u32[]{:S(2)}) %collective-permute-start.23) | collective-permute-done | bytes 245792 | tf_op jit(solution)/shard_map/ppermute | solution.py:558
  133.0 4.7 %first_grad.1 = (f32[8,32,768]{2,1,0:T(8,128)S(1)}, bf16[8,32,768]{2,1,0:T(8,128)(2,1)S(1)}, bf16[8,32,256]{2,1,0:T(8,128)(2,1)S(1)}, f32[8,128]{1,0:T(8,128)}) custom-call(s32[3]{0:T(128)S(1)} %pad_add_fusion.refs_0_, s32[128,8]{1,0:T(8,128)S(1)} %copy.17.refs_1_.refs_5_.refs_2_, bf16[128,8]{1,0:T(8,128)(2,1)S(1)} %copy.19.refs_2_.refs_6_.refs_3_, ...), custom_call_target="tpu_custom_call" | custom-call | flops 1 | bytes 1 | tf_op jit(solution)/shard_map/first_grad/pallas_call | solution.py:53
  138.0 1.5 collective-permute-start.25
  139.5 6.9 %collective-permute-done.25.refs_5_.refs_15_ = bf16[160,768]{1,0:T(8,128)(2,1)S(1)} collective-permute-done((bf16[160,768]{1,0:T(8,128)(2,1)}, bf16[160,768]{1,0:T(8,128)(2,1)S(1)}, u32[]{:S(2)}, u32[]{:S(2)}) %collective-permute-start.25) | collective-permute-done | bytes 245792 | tf_op jit(solution)/shard_map/ppermute | solution.py:558
  146.4 0.6 first_sum.1
  147.0 0.8 copy-done.17
  147.8 5.9 %all-to-all-start.1 = ((bf16[8,32,1024]{2,1,0:T(8,128)(2,1)}), bf16[8,32,1024]{2,1,0:T(8,128)(2,1)S(1)}, u32[]{:S(2)}, u32[]{:S(2)}) async-start(bf16[8,32,1024]{2,1,0:T(8,128)(2,1)} %copy-done.17), calls=%async_computation.1 | async-start | bytes 1048576 | tf_op jit(solution)/shard_map/all_to_all | solution.py:566
  153.8 7.9 %finish.1 = (bf16[1024,768]{1,0:T(8,128)(2,1)}, f32[128,8]{1,0:T(8,128)S(1)}, f32[8,128]{1,0:T(8,128)}) custom-call(s32[3]{0:T(128)S(1)} %pad_add_fusion.refs_0_, s32[128,8]{1,0:T(8,128)S(1)} %copy.17.refs_1_.refs_5_.refs_2_, s32[128,8]{1,0:T(8,128)S(1)} %copy.17.refs_1_.refs_5_.refs_2_, bf16[128,8]{1,0:T(8,128)(2,1)S(1)} %copy.19.refs_2_.refs_6_.refs_3_, ...), custom_call_target="tpu_custom_call" | custom-call | flops 1 | bytes 20000000 | tf_op jit(solution)/shard_map/finish/pallas_call | solution.py:53
  161.6 0.5 collective-permute-start.28
  162.2 3.7 %collective-permute-done.28.refs_11_ = f32[128,8]{1,0:T(8,128)S(1)} collective-permute-done((f32[128,8]{1,0:T(8,128)S(1)}, f32[128,8]{1,0:T(8,128)S(1)}, u32[]{:S(2)}, u32[]{:S(2)}) %collective-permute-start.28) | collective-permute-done | bytes 4128 | tf_op jit(solution)/shard_map/ppermute | solution.py:552
  165.9 1.2 all-to-all-done.1.refs_1_
  167.1 4.4 %second_grad.1 = (f32[32,2048]{1,0:T(8,128)S(1)}, f32[32,2048]{1,0:T(8,128)S(1)}, f32[32,768]{1,0:T(8,128)}, f32[8,128]{1,0:T(8,128)}) custom-call(s32[3]{0:T(128)S(1)} %pad_add_fusion.refs_0_, bf16[8,32,1024]{2,1,0:T(8,128)(2,1)S(1)} %all-to-all-done.1.refs_1_, bf16[128,2304]{1,0:T(8,128)(2,1)} %copy-done.3, bf16[128,2304]{1,0:T(8,128)(2,1)} %copy-done.4, ...), custom_call_target="tpu_custom_call" | custom-call | flops 1 | bytes 1 | tf_op jit(solution)/shard_map/second_grad/pallas_call | solution.py:53
  171.5 0.7 copy.20
  172.1 0.8 collective-permute-done.29
  173.0 0.7 add_bitcast_fusion
  (74 shorter events, 1.6 us)
Async XLA Ops:
  0.6 18.6 %copy-start.8 = (bf16[1,32,2048]{2,1,0:T(8,128)(2,1)S(1)}, bf16[1,32,2048]{2,1,0:T(8,128)(2,1)}, u32[]{:S(2)}) copy-start(bf16[1,32,2048]{2,1,0:T(8,128)(2,1)} %param.13) | copy-start | bytes 393220
  0.6 18.6 %collective-permute-start.2 = (bf16[1536,2048]{1,0:T(8,128)(2,1)}, bf16[1536,2048]{1,0:T(8,128)(2,1)}, u32[]{:S(2)}, u32[]{:S(2)}) collective-permute-start(bf16[1536,2048]{1,0:T(8,128)(2,1)} %bitcast.32), channel_id=1, source_target_pairs={{0,1},{1,0},{2,3},{3,2},{4,5},{5,4},{6,7},{7,6},{8,9},{9,8},{10,11... | collective-permute-start | bytes 18874376 | tf_op jit(solution)/shard_map/ppermute | solution.py:561
  0.8 0.8 copy-start.19
  1.6 0.7 copy-start.20
  3.4 24.0 %copy-start.3 = (bf16[128,2304]{1,0:T(8,128)(2,1)}, bf16[128,2304]{1,0:T(8,128)(2,1)S(1)}, u32[]{:S(2)}) copy-start(bf16[128,2304]{1,0:T(8,128)(2,1)S(1)} %get-tuple-element.57.refs_1_.refs_5_.refs_2_) | copy-start | bytes 1769476
  3.4 15.8 %collective-permute-start = (bf16[128,2304]{1,0:T(8,128)(2,1)S(1)}, bf16[128,2304]{1,0:T(8,128)(2,1)S(1)}, u32[]{:S(2)}, u32[]{:S(2)}) collective-permute-start(bf16[128,2304]{1,0:T(8,128)(2,1)S(1)} %get-tuple-element.57.refs_1_.refs_5_.refs_2_), channel_id=1, source_target_pairs={{0,4},{4,0},{8,12},{12,8},{16,20},{20,16},{24,28},{28,24},{1,5},{5... | collective-permute-start | bytes 1769480 | tf_op jit(solution)/shard_map/ppermute | solution.py:558
  5.0 28.1 %collective-permute-start.4 = (bf16[128,2304]{1,0:T(8,128)(2,1)S(1)}, bf16[128,2304]{1,0:T(8,128)(2,1)S(1)}, u32[]{:S(2)}, u32[]{:S(2)}) collective-permute-start(bf16[128,2304]{1,0:T(8,128)(2,1)S(1)} %get-tuple-element.57.refs_1_.refs_5_.refs_2_), channel_id=1, source_target_pairs={{0,16},{4,20},{8,24},{12,28},{16,0},{20,4},{24,8},{28,12},{1,17},{... | collective-permute-start | bytes 1769480 | tf_op jit(solution)/shard_map/ppermute | solution.py:558
  7.6 27.6 %collective-permute-start.3 = (bf16[128,2304]{1,0:T(8,128)(2,1)S(1)}, bf16[128,2304]{1,0:T(8,128)(2,1)S(1)}, u32[]{:S(2)}, u32[]{:S(2)}) collective-permute-start(bf16[128,2304]{1,0:T(8,128)(2,1)S(1)} %get-tuple-element.57.refs_1_.refs_5_.refs_2_), channel_id=1, source_target_pairs={{0,8},{4,12},{8,0},{12,4},{16,24},{20,28},{24,16},{28,20},{1,9},{5... | collective-permute-start | bytes 1769480 | tf_op jit(solution)/shard_map/ppermute | solution.py:558
  8.0 3.4 %collective-permute-start.1 = (bf16[32,2048]{1,0:T(8,128)(2,1)}, bf16[32,2048]{1,0:T(8,128)(2,1)S(1)}, u32[]{:S(2)}, u32[]{:S(2)}) collective-permute-start(bf16[32,2048]{1,0:T(8,128)(2,1)} %bitcast.18), channel_id=1, source_target_pairs={{0,1},{1,0},{2,3},{3,2},{4,5},{5,4},{6,7},{7,6},{8,9},{9,8},{10,11... | collective-permute-start | bytes 393224 | tf_op jit(solution)/shard_map/ppermute | solution.py:561
  19.2 8.3 %copy-start.4 = (bf16[128,2304]{1,0:T(8,128)(2,1)}, bf16[128,2304]{1,0:T(8,128)(2,1)S(1)}, u32[]{:S(2)}) copy-start(bf16[128,2304]{1,0:T(8,128)(2,1)S(1)} %collective-permute-done.refs_2_.refs_6_.refs_3_) | copy-start | bytes 1769476
  19.2 19.5 %copy-start.9 = (bf16[1,32,2048]{2,1,0:T(8,128)(2,1)S(1)}, bf16[1,32,2048]{2,1,0:T(8,128)(2,1)}, u32[]{:S(2)}) copy-start(bf16[1,32,2048]{2,1,0:T(8,128)(2,1)} %param.13) | copy-start | bytes 393220
  33.6 13.0 %copy-start.2 = (bf16[128,2304]{1,0:T(8,128)(2,1)}, bf16[128,2304]{1,0:T(8,128)(2,1)S(1)}, u32[]{:S(2)}) copy-start(bf16[128,2304]{1,0:T(8,128)(2,1)S(1)} %get-tuple-element.63.refs_2_.refs_8_.refs_5_) | copy-start | bytes 1769476
  33.6 15.3 %collective-permute-start.5 = (bf16[128,2304]{1,0:T(8,128)(2,1)S(1)}, bf16[128,2304]{1,0:T(8,128)(2,1)S(1)}, u32[]{:S(2)}, u32[]{:S(2)}) collective-permute-start(bf16[128,2304]{1,0:T(8,128)(2,1)S(1)} %get-tuple-element.63.refs_2_.refs_8_.refs_5_), channel_id=1, source_target_pairs={{0,8},{4,12},{8,0},{12,4},{16,24},{20,28},{24,16},{28,20},{1,9},{5... | collective-permute-start | bytes 1769480 | tf_op jit(solution)/shard_map/ppermute | solution.py:558
  35.1 11.5 %copy-start.5 = (bf16[128,2304]{1,0:T(8,128)(2,1)}, bf16[128,2304]{1,0:T(8,128)(2,1)S(1)}, u32[]{:S(2)}) copy-start(bf16[128,2304]{1,0:T(8,128)(2,1)S(1)} %collective-permute-done.3.refs_1_.refs_7_.refs_4_) | copy-start | bytes 1769476
  35.1 16.3 %collective-permute-start.6 = (bf16[128,2304]{1,0:T(8,128)(2,1)S(1)}, bf16[128,2304]{1,0:T(8,128)(2,1)S(1)}, u32[]{:S(2)}, u32[]{:S(2)}) collective-permute-start(bf16[128,2304]{1,0:T(8,128)(2,1)S(1)} %collective-permute-done.3.refs_1_.refs_7_.refs_4_), channel_id=1, source_target_pairs={{0,4},{4,0},{8,12},{12,8},{16,20},{20,16},{24,28},{28,24},{1,5},{5... | collective-permute-start | bytes 1769480 | tf_op jit(solution)/shard_map/ppermute | solution.py:558
  35.6 28.4 %collective-permute-start.9 = (bf16[128,2304]{1,0:T(8,128)(2,1)S(1)}, bf16[128,2304]{1,0:T(8,128)(2,1)S(1)}, u32[]{:S(2)}, u32[]{:S(2)}) collective-permute-start(bf16[128,2304]{1,0:T(8,128)(2,1)S(1)} %get-tuple-element.63.refs_2_.refs_8_.refs_5_), channel_id=1, source_target_pairs={{0,4},{4,0},{8,12},{12,8},{16,20},{20,16},{24,28},{28,24},{1,5},{5... | collective-permute-start | bytes 1769480 | tf_op jit(solution)/shard_map/ppermute | solution.py:558
  37.2 14.2 %collective-permute-start.8 = (bf16[320,768]{1,0:T(8,128)(2,1)S(1)}, bf16[320,768]{1,0:T(8,128)(2,1)S(1)}, u32[]{:S(2)}, u32[]{:S(2)}) collective-permute-start(bf16[320,768]{1,0:T(8,128)(2,1)S(1)} %get-tuple-element.69), channel_id=1, source_target_pairs={{0,2},{2,0},{1,3},{3,1},{4,6},{6,4},{5,7},{7,5},{8,10},{10,8},{9,1... | collective-permute-start | bytes 1474568 | tf_op jit(solution)/shard_map/ppermute | solution.py:552
  46.7 12.6 %collective-permute-start.7 = (bf16[320,768]{1,0:T(8,128)(2,1)S(1)}, bf16[320,768]{1,0:T(8,128)(2,1)S(1)}, u32[]{:S(2)}, u32[]{:S(2)}) collective-permute-start(bf16[320,768]{1,0:T(8,128)(2,1)S(1)} %get-tuple-element.67), channel_id=1, source_target_pairs={{0,2},{2,0},{1,3},{3,1},{4,6},{6,4},{5,7},{7,5},{8,10},{10,8},{9,1... | collective-permute-start | bytes 1474568 | tf_op jit(solution)/shard_map/ppermute | solution.py:552
  49.0 23.5 %copy-start.6 = (bf16[128,2304]{1,0:T(8,128)(2,1)}, bf16[128,2304]{1,0:T(8,128)(2,1)S(1)}, u32[]{:S(2)}) copy-start(bf16[128,2304]{1,0:T(8,128)(2,1)S(1)} %collective-permute-done.5.refs_1_.refs_9_.refs_6_) | copy-start | bytes 1769476
  49.0 25.7 %collective-permute-start.10 = (bf16[128,2304]{1,0:T(8,128)(2,1)S(1)}, bf16[128,2304]{1,0:T(8,128)(2,1)S(1)}, u32[]{:S(2)}, u32[]{:S(2)}) collective-permute-start(bf16[128,2304]{1,0:T(8,128)(2,1)S(1)} %collective-permute-done.5.refs_1_.refs_9_.refs_6_), channel_id=1, source_target_pairs={{0,4},{4,0},{8,12},{12,8},{16,20},{20,16},{24,28},{28,24},{1,5},{5... | collective-permute-start | bytes 1769480 | tf_op jit(solution)/shard_map/ppermute | solution.py:558
  51.4 21.0 %copy-start.1 = (bf16[128,2304]{1,0:T(8,128)(2,1)}, bf16[128,2304]{1,0:T(8,128)(2,1)S(1)}, u32[]{:S(2)}) copy-start(bf16[128,2304]{1,0:T(8,128)(2,1)S(1)} %collective-permute-done.6.refs_4_.refs_2_.refs_10_.refs_7_) | copy-start | bytes 1769476
  52.7 11.3 %copy-start.18 = (bf16[160,768]{1,0:T(8,128)(2,1)}, bf16[160,768]{1,0:T(8,128)(2,1)S(1)}, u32[]{:S(2)}) copy-start(bf16[160,768]{1,0:T(8,128)(2,1)S(1)} %get-tuple-element.93.refs_8_) | copy-start | bytes 737284
  64.1 10.7 %copy-start = (bf16[128,2304]{1,0:T(8,128)(2,1)}, bf16[128,2304]{1,0:T(8,128)(2,1)S(1)}, u32[]{:S(2)}) copy-start(bf16[128,2304]{1,0:T(8,128)(2,1)S(1)} %collective-permute-done.9.refs_8_.refs_1_.refs_11_) | copy-start | bytes 1769476
  72.4 16.1 %collective-permute-start.11 = (bf16[320,768]{1,0:T(8,128)(2,1)S(1)}, bf16[320,768]{1,0:T(8,128)(2,1)S(1)}, u32[]{:S(2)}, u32[]{:S(2)}) collective-permute-start(bf16[320,768]{1,0:T(8,128)(2,1)S(1)} %get-tuple-element.77), channel_id=1, source_target_pairs={{0,2},{2,0},{1,3},{3,1},{4,6},{6,4},{5,7},{7,5},{8,10},{10,8},{9,1... | collective-permute-start | bytes 1474568 | tf_op jit(solution)/shard_map/ppermute | solution.py:552
  74.0 12.3 %collective-permute-start.18 = (bf16[160,768]{1,0:T(8,128)(2,1)S(1)}, bf16[160,768]{1,0:T(8,128)(2,1)}, u32[]{:S(2)}, u32[]{:S(2)}) collective-permute-start(bf16[160,768]{1,0:T(8,128)(2,1)S(1)} %get-tuple-element.88), channel_id=1, source_target_pairs={{0,8},{4,12},{8,0},{12,4},{16,24},{20,28},{24,16},{28,20},{1,9},{5... | collective-permute-start | bytes 737288 | tf_op jit(solution)/shard_map/ppermute | solution.py:558
  74.7 8.2 %copy-start.7 = (bf16[128,2304]{1,0:T(8,128)(2,1)}, bf16[128,2304]{1,0:T(8,128)(2,1)S(1)}, u32[]{:S(2)}) copy-start(bf16[128,2304]{1,0:T(8,128)(2,1)S(1)} %collective-permute-done.10.refs_2_.refs_12_.refs_9_) | copy-start | bytes 1769476
  82.9 29.7 %copy-start.21 = (s32[128,8]{0,1:T(8,128)S(1)}, s32[128,8]{0,1:T(8,128)}, u32[]{:S(2)}) copy-start(s32[128,8]{0,1:T(8,128)} %param.9) | copy-start | bytes 12292
  82.9 43.0 %copy-start.24 = (bf16[128,8]{0,1:T(8,128)(2,1)S(1)}, bf16[128,8]{0,1:T(8,128)(2,1)}, u32[]{:S(2)}) copy-start(bf16[128,8]{0,1:T(8,128)(2,1)} %param.10) | copy-start | bytes 6148
  82.9 26.2 %collective-permute-start.14 = (bf16[320,768]{1,0:T(8,128)(2,1)S(1)}, bf16[320,768]{1,0:T(8,128)(2,1)S(1)}, u32[]{:S(2)}, u32[]{:S(2)}) collective-permute-start(bf16[320,768]{1,0:T(8,128)(2,1)S(1)} %get-tuple-element.83), channel_id=1, source_target_pairs={{0,2},{2,0},{1,3},{3,1},{4,6},{6,4},{5,7},{7,5},{8,10},{10,8},{9,1... | collective-permute-start | bytes 1474568 | tf_op jit(solution)/shard_map/ppermute | solution.py:552
  84.5 7.9 %collective-permute-start.17 = (bf16[160,768]{1,0:T(8,128)(2,1)S(1)}, bf16[160,768]{1,0:T(8,128)(2,1)S(1)}, u32[]{:S(2)}, u32[]{:S(2)}) collective-permute-start(bf16[160,768]{1,0:T(8,128)(2,1)S(1)} %get-tuple-element.87), channel_id=1, source_target_pairs={{0,8},{4,12},{8,0},{12,4},{16,24},{20,28},{24,16},{28,20},{1,9},{5... | collective-permute-start | bytes 737288 | tf_op jit(solution)/shard_map/ppermute | solution.py:558
  85.8 21.8 %collective-permute-start.16 = (bf16[160,768]{1,0:T(8,128)(2,1)}, bf16[160,768]{1,0:T(8,128)(2,1)S(1)}, u32[]{:S(2)}, u32[]{:S(2)}) collective-permute-start(bf16[160,768]{1,0:T(8,128)(2,1)} %get-tuple-element.86), channel_id=1, source_target_pairs={{0,4},{4,0},{8,12},{12,8},{16,20},{20,16},{24,28},{28,24},{1,5},{5... | collective-permute-start | bytes 737288 | tf_op jit(solution)/shard_map/ppermute | solution.py:558
  86.3 21.4 %collective-permute-start.19 = (bf16[160,768]{1,0:T(8,128)(2,1)}, bf16[160,768]{1,0:T(8,128)(2,1)S(1)}, u32[]{:S(2)}, u32[]{:S(2)}) collective-permute-start(bf16[160,768]{1,0:T(8,128)(2,1)} %collective-permute-done.18), channel_id=1, source_target_pairs={{0,24},{4,28},{8,16},{12,20},{16,8},{20,12},{24,0},{28,4},{1,25},{... | collective-permute-start | bytes 737288 | tf_op jit(solution)/shard_map/ppermute | solution.py:558
  89.9 0.7 copy-start.23
  90.6 18.6 %collective-permute-start.15 = (bf16[160,768]{1,0:T(8,128)(2,1)}, bf16[160,768]{1,0:T(8,128)(2,1)S(1)}, u32[]{:S(2)}, u32[]{:S(2)}) collective-permute-start(bf16[160,768]{1,0:T(8,128)(2,1)} %get-tuple-element.85), channel_id=1, source_target_pairs={{0,24},{4,28},{8,16},{12,20},{16,8},{20,12},{24,0},{28,4},{1,25},{... | collective-permute-start | bytes 737288 | tf_op jit(solution)/shard_map/ppermute | solution.py:558
  92.3 61.4 %copy-start.11 = (bf16[160,768]{1,0:T(8,128)(2,1)}, bf16[160,768]{1,0:T(8,128)(2,1)S(1)}, u32[]{:S(2)}) copy-start(bf16[160,768]{1,0:T(8,128)(2,1)S(1)} %collective-permute-done.17.refs_6_.refs_10_) | copy-start | bytes 737284
  92.3 21.4 %collective-permute-start.13 = (bf16[8,32,768]{2,1,0:T(8,128)(2,1)S(1)}, bf16[8,32,768]{2,1,0:T(8,128)(2,1)S(1)}, u32[]{:S(2)}, u32[]{:S(2)}) collective-permute-start(bf16[8,32,768]{2,1,0:T(8,128)(2,1)S(1)} %get-tuple-element.81), channel_id=1, source_target_pairs={{0,1},{1,0},{2,3},{3,2},{4,5},{5,4},{6,7},{7,6},{8,9},{9,8},{10,11... | collective-permute-start | bytes 1179656 | tf_op jit(solution)/shard_map/ppermute | solution.py:561
  92.4 21.3 %all-to-all-start = ((bf16[8,64,128]{2,1,0:T(8,128)(2,1)}), bf16[8,64,128]{2,1,0:T(8,128)(2,1)S(1)}, u32[]{:S(2)}, u32[]{:S(2)}) async-start(bf16[8,64,128]{2,1,0:T(8,128)(2,1)} %get-tuple-element.80), calls=%async_computation | async-start | bytes 262144 | tf_op jit(solution)/shard_map/all_to_all | solution.py:566
  107.6 46.2 %copy-start.12 = (bf16[160,768]{1,0:T(8,128)(2,1)}, bf16[160,768]{1,0:T(8,128)(2,1)S(1)}, u32[]{:S(2)}) copy-start(bf16[160,768]{1,0:T(8,128)(2,1)S(1)} %collective-permute-done.16.refs_5_.refs_9_) | copy-start | bytes 737284
  107.6 12.7 %collective-permute-start.20 = (bf16[160,768]{1,0:T(8,128)(2,1)}, bf16[160,768]{1,0:T(8,128)(2,1)}, u32[]{:S(2)}, u32[]{:S(2)}) collective-permute-start(bf16[160,768]{1,0:T(8,128)(2,1)} %copy-done.23), channel_id=1, source_target_pairs={{0,8},{4,12},{8,0},{12,4},{16,24},{20,28},{24,16},{28,20},{1,9},{5... | collective-permute-start | bytes 737288 | tf_op jit(solution)/shard_map/ppermute | solution.py:558
  107.7 46.1 %copy-start.13 = (bf16[160,768]{1,0:T(8,128)(2,1)}, bf16[160,768]{1,0:T(8,128)(2,1)S(1)}, u32[]{:S(2)}) copy-start(bf16[160,768]{1,0:T(8,128)(2,1)S(1)} %collective-permute-done.19.refs_7_.refs_12_) | copy-start | bytes 737284
  109.1 44.6 %copy-start.14 = (bf16[160,768]{1,0:T(8,128)(2,1)}, bf16[160,768]{1,0:T(8,128)(2,1)S(1)}, u32[]{:S(2)}) copy-start(bf16[160,768]{1,0:T(8,128)(2,1)S(1)} %collective-permute-done.15.refs_4_.refs_14_) | copy-start | bytes 737284
  110.4 0.7 copy-start.22
  111.1 12.6 %collective-permute-start.22 = (bf16[160,768]{1,0:T(8,128)(2,1)}, bf16[160,768]{1,0:T(8,128)(2,1)}, u32[]{:S(2)}, u32[]{:S(2)}) collective-permute-start(bf16[160,768]{1,0:T(8,128)(2,1)} %get-tuple-element.94), channel_id=1, source_target_pairs={{0,16},{4,20},{8,24},{12,28},{16,0},{20,4},{24,8},{28,12},{1,17},{... | collective-permute-start | bytes 737288 | tf_op jit(solution)/shard_map/ppermute | solution.py:558
  117.3 13.6 %collective-permute-start.26 = (f32[128,512]{1,0:T(8,128)S(1)}, f32[128,512]{1,0:T(8,128)S(1)}, u32[]{:S(2)}, u32[]{:S(2)}) collective-permute-start(f32[128,512]{1,0:T(8,128)S(1)} %get-tuple-element.96.refs_7_), channel_id=1, source_target_pairs={{0,2},{2,0},{1,3},{3,1},{4,6},{6,4},{5,7},{7,5},{8,10},{10,8},{9,1... | collective-permute-start | bytes 786440 | tf_op jit(solution)/shard_map/ppermute | solution.py:552
  120.3 9.9 %collective-permute-start.21 = (bf16[160,768]{1,0:T(8,128)(2,1)}, bf16[160,768]{1,0:T(8,128)(2,1)S(1)}, u32[]{:S(2)}, u32[]{:S(2)}) collective-permute-start(bf16[160,768]{1,0:T(8,128)(2,1)} %collective-permute-done.20), channel_id=1, source_target_pairs={{0,4},{4,0},{8,12},{12,8},{16,20},{20,16},{24,28},{28,24},{1,5},{5... | collective-permute-start | bytes 737288 | tf_op jit(solution)/shard_map/ppermute | solution.py:558
  123.8 9.2 %collective-permute-start.23 = (bf16[160,768]{1,0:T(8,128)(2,1)}, bf16[160,768]{1,0:T(8,128)(2,1)S(1)}, u32[]{:S(2)}, u32[]{:S(2)}) collective-permute-start(bf16[160,768]{1,0:T(8,128)(2,1)} %collective-permute-done.22), channel_id=1, source_target_pairs={{0,4},{4,0},{8,12},{12,8},{16,20},{20,16},{24,28},{28,24},{1,5},{5... | collective-permute-start | bytes 737288 | tf_op jit(solution)/shard_map/ppermute | solution.py:558
  125.2 5.0 %collective-permute-start.12 = (bf16[8,64,128]{2,1,0:T(8,128)(2,1)S(1)}, bf16[8,64,128]{2,1,0:T(8,128)(2,1)S(1)}, u32[]{:S(2)}, u32[]{:S(2)}) collective-permute-start(bf16[8,64,128]{2,1,0:T(8,128)(2,1)S(1)} %all-to-all-done.refs_6_.refs_1_), channel_id=1, source_target_pairs={{0,2},{2,0},{1,3},{3,1},{4,6},{6,4},{5,7},{7,5},{8,10},{10,8},{9,1... | collective-permute-start | bytes 393224 | tf_op jit(solution)/shard_map/ppermute | solution.py:552
  125.8 12.2 %collective-permute-start.24 = (bf16[160,768]{1,0:T(8,128)(2,1)}, bf16[160,768]{1,0:T(8,128)(2,1)}, u32[]{:S(2)}, u32[]{:S(2)}) collective-permute-start(bf16[160,768]{1,0:T(8,128)(2,1)} %copy-done.22), channel_id=1, source_target_pairs={{0,24},{4,28},{8,16},{12,20},{16,8},{20,12},{24,0},{28,4},{1,25},{... | collective-permute-start | bytes 737288 | tf_op jit(solution)/shard_map/ppermute | solution.py:558
  130.2 23.6 %copy-start.10 = (bf16[160,768]{1,0:T(8,128)(2,1)}, bf16[160,768]{1,0:T(8,128)(2,1)S(1)}, u32[]{:S(2)}) copy-start(bf16[160,768]{1,0:T(8,128)(2,1)S(1)} %collective-permute-done.21.refs_4_.refs_11_) | copy-start | bytes 737284
  133.0 20.8 %copy-start.15 = (bf16[160,768]{1,0:T(8,128)(2,1)}, bf16[160,768]{1,0:T(8,128)(2,1)S(1)}, u32[]{:S(2)}) copy-start(bf16[160,768]{1,0:T(8,128)(2,1)S(1)} %collective-permute-done.23.refs_10_.refs_13_) | copy-start | bytes 737284
  137.7 8.7 %collective-permute-start.27 = (bf16[8,32,768]{2,1,0:T(8,128)(2,1)S(1)}, bf16[8,32,768]{2,1,0:T(8,128)(2,1)S(1)}, u32[]{:S(2)}, u32[]{:S(2)}) collective-permute-start(bf16[8,32,768]{2,1,0:T(8,128)(2,1)S(1)} %get-tuple-element.99), channel_id=1, source_target_pairs={{0,1},{1,0},{2,3},{3,2},{4,5},{5,4},{6,7},{7,6},{8,9},{9,8},{10,11... | collective-permute-start | bytes 1179656 | tf_op jit(solution)/shard_map/ppermute | solution.py:561
  138.0 8.4 %collective-permute-start.25 = (bf16[160,768]{1,0:T(8,128)(2,1)}, bf16[160,768]{1,0:T(8,128)(2,1)S(1)}, u32[]{:S(2)}, u32[]{:S(2)}) collective-permute-start(bf16[160,768]{1,0:T(8,128)(2,1)} %collective-permute-done.24), channel_id=1, source_target_pairs={{0,4},{4,0},{8,12},{12,8},{16,20},{20,16},{24,28},{28,24},{1,5},{5... | collective-permute-start | bytes 737288 | tf_op jit(solution)/shard_map/ppermute | solution.py:558
  146.4 7.4 %copy-start.16 = (bf16[160,768]{1,0:T(8,128)(2,1)}, bf16[160,768]{1,0:T(8,128)(2,1)S(1)}, u32[]{:S(2)}) copy-start(bf16[160,768]{1,0:T(8,128)(2,1)S(1)} %collective-permute-done.25.refs_5_.refs_15_) | copy-start | bytes 737284
  147.0 0.8 copy-start.17
  147.8 19.2 %all-to-all-start.1 = ((bf16[8,32,1024]{2,1,0:T(8,128)(2,1)}), bf16[8,32,1024]{2,1,0:T(8,128)(2,1)S(1)}, u32[]{:S(2)}, u32[]{:S(2)}) async-start(bf16[8,32,1024]{2,1,0:T(8,128)(2,1)} %copy-done.17), calls=%async_computation.1 | async-start | bytes 1048576 | tf_op jit(solution)/shard_map/all_to_all | solution.py:566
  161.6 4.3 %collective-permute-start.28 = (f32[128,8]{1,0:T(8,128)S(1)}, f32[128,8]{1,0:T(8,128)S(1)}, u32[]{:S(2)}, u32[]{:S(2)}) collective-permute-start(f32[128,8]{1,0:T(8,128)S(1)} %get-tuple-element.104), channel_id=1, source_target_pairs={{0,2},{2,0},{1,3},{3,1},{4,6},{6,4},{5,7},{7,5},{8,10},{10,8},{9,1... | collective-permute-start | bytes 12296 | tf_op jit(solution)/shard_map/ppermute | solution.py:552
  171.5 1.5 collective-permute-start.29

commit v16 on v15

--- a/solution.py
+++ b/solution.py
@@ -136,6 +136,21 @@
         [ANY] * len(arrays),
         input_output_aliases={1 + k: k for k in range(len(arrays))},
     )
+
+
+def touch_kernel(block_ref, out_ref):
+    out_ref[...] = jnp.zeros_like(out_ref)
+
+
+def touch_call(block):
+    return pl.pallas_call(
+        touch_kernel,
+        in_specs=[ANY],
+        out_specs=VMEM,
+        out_shape=jax.ShapeDtypeStruct((8, 128), F32),
+        cost_estimate=SMALL,
+        name="touch",
+    )(block)
 
 
 def load_kernel(at_ref, down_ref, out_ref, sems):
@@ -596,9 +611,7 @@
         for o, rows in zip(batches[i], share_sum_call(order, shared[i], 2, slots)):
             masks = [o] if o else []
             if i >= last - 1 and o % 2:
-                masks = [o - 1, 1] if o > 1 else [1]
-            elif o == 4 and groups == 8:
-                masks = [2, 6]
+                masks = [1 << k for k in reversed(range(o.bit_length())) if o >> k & 1]
             for mask in masks:
                 rows = flip(rows, mask)
             back[o] = rows
@@ -623,9 +636,9 @@
     low_grad, first_own = collect_call(order, places, lows, grads, feats)
     firsts = [x.reshape(groups * rank, units) for x in (first_own, swap(first_own))]
     low_grad = exchange(low_grad)
-    order.wait([back[batches[-2][0]], back[1], back[2]] + [back[4]] * (groups == 8))
+    order.wait([back[batches[-2][0]], swap(touch_call(back[groups // 2]))])
     total(last)
-    order.wait([low_grad])
+    order.wait([low_grad, back[1], back[2]])
     low_hid = all_shares(lowrank_hid_call(order, index, hid, firsts, groups))
     order.wait([back[batches[-2][1]]])
 

time: 177 us -> 186 us (1.051)
  waiting for transfers between devices: 53.9 us -> 65.8 us
  starting transfers between devices: 47.5 us -> 45.1 us
    ppermute x18, waiting for transfers between devices: 36.3 us -> 50 us  [flip(): return lax.ppermute(x, 'ep', [(i, i ^ mask) for i in range(groups)])]
    all_to_all x2, starting transfers between devices: 21 us -> 13.3 us  [exchange(): return lax.all_to_all(x, axes, split_axis=0, concat_axis=0, tiled=True)]
    ppermute x18, starting transfers between devices: 19.4 us -> 24.7 us  [flip(): return lax.ppermute(x, 'ep', [(i, i ^ mask) for i in range(groups)])]
    ppermute x7, waiting for transfers between devices: 14.5 us -> 11 us  [turn(): lax.ppermute(x, 'rep', [(r, (r + offset) % shares) for r in range(shares)])]
    unnamed x53 -> x49, local copies, waits for them, and re-layouts: 4.65 us -> 3.27 us
  transfers between devices with their start and end apart: 32 -> 33, of which waited for: 18 -> 17; matrix products, arithmetic and copies ran while one was open for 1% -> 1% of each run, Pallas kernels for 35% -> 34%
where the time goes in v16:
time: 186 us; the launch traced here: 182 us
  Pallas kernels  66.5 us (36%)
  waiting for transfers between devices  65.8 us (35%)
  starting transfers between devices  45.1 us (24%)
  local copies, waits for them, and re-layouts  3.27 us (2%)
    pallas_call x18, Pallas kernels, call(): pl.pallas_call(ordered, grid=grid, in_specs=[SMEM, *in_specs] + [ANY] * l...  65.9 us
    ppermute x18, waiting for transfers between devices, flip(): return lax.ppermute(x, 'ep', [(i, i ^ mask) for i in range(groups)])  50 us
    ppermute x18, starting transfers between devices, flip(): return lax.ppermute(x, 'ep', [(i, i ^ mask) for i in range(groups)])  24.7 us
    all_to_all x2, starting transfers between devices, exchange(): return lax.all_to_all(x, axes, split_axis=0, concat_axis=0, tiled=True)  13.3 us
    ppermute x7, waiting for transfers between devices, turn(): lax.ppermute(x, 'rep', [(r, (r + offset) % shares) for r in range(shares)])  11 us
    ppermute x7, starting transfers between devices, turn(): lax.ppermute(x, 'rep', [(r, (r + offset) % shares) for r in range(shares)])  6.88 us
  transfers between devices with their start and end apart: 33, of which 17 were waited for; matrix products, arithmetic and copies ran while one was open for 1% of the time, Pallas kernels for 34%

profile of v16, /device:TPU:8, one launch (start us, length us, event | category | flops | bytes accessed | tf_op | source)
XLA Modules:
  0.0 182.5 jit_solution(12491215018848128215)
XLA Ops:
  0.8 0.8 copy-done.18
  1.6 0.7 copy-done.19
  2.3 1.1 pack_block.1
  3.4 1.6 collective-permute-start
  5.0 2.6 %collective-permute-start.4 = (bf16[128,2304]{1,0:T(8,128)(2,1)S(1)}, bf16[128,2304]{1,0:T(8,128)(2,1)S(1)}, u32[]{:S(2)}, u32[]{:S(2)}) collective-permute-start(bf16[128,2304]{1,0:T(8,128)(2,1)S(1)} %get-tuple-element.57.refs_1_.refs_5_.refs_2_), channel_id=1, source_target_pairs={{0,16},{4,20},{8,24},{12,28},{16,0},{20,4},{24,8},{28,12},{1,17},{... | collective-permute-start | bytes 1769480 | tf_op jit(solution)/shard_map/ppermute | solution.py:573
  8.0 3.4 %load_matrix.1 = (bf16[1536,2048]{1,0:T(8,128)(2,1)S(1)}, f32[8,128]{1,0:T(8,128)}) custom-call(s32[3]{0:T(128)S(1)} %pad_add_fusion.refs_0_, bf16[1536,2048]{1,0:T(8,128)(2,1)} %bitcast.33, f32[8,128]{1,0:T(8,128)} %get-tuple-element.58.refs_2_), custom_call_target="tpu_custom_call" | custom-call | flops 1 | bytes 1 | tf_op jit(solution)/shard_map/load_matrix/pallas_call | solution.py:53
  11.5 7.7 %collective-permute-done.refs_2_.refs_6_.refs_3_ = bf16[128,2304]{1,0:T(8,128)(2,1)S(1)} collective-permute-done((bf16[128,2304]{1,0:T(8,128)(2,1)S(1)}, bf16[128,2304]{1,0:T(8,128)(2,1)S(1)}, u32[]{:S(2)}, u32[]{:S(2)}) %collective-permute-start) | collective-permute-done | bytes 589856 | tf_op jit(solution)/shard_map/ppermute | solution.py:573
  19.2 8.2 %expert_rows.4 = (bf16[320,768]{1,0:T(8,128)(2,1)S(1)}, bf16[320,768]{1,0:T(8,128)(2,1)S(1)}, bf16[2,64,128]{2,1,0:T(8,128)(2,1)S(1)}, f32[8,128]{1,0:T(8,128)}) custom-call(s32[3]{0:T(128)S(1)} %pad_add_fusion.refs_0_, bf16[128,2304]{1,0:T(8,128)(2,1)S(1)} %get-tuple-element.57.refs_1_.refs_5_.refs_2_, ...), custom_call_target="tpu_custom_call" | custom-call | flops 1 | bytes 1 | tf_op jit(solution)/shard_map/expert_rows/pallas_call | solution.py:53
  27.5 5.6 %collective-permute-done.4.refs_1_ = bf16[128,2304]{1,0:T(8,128)(2,1)S(1)} collective-permute-done((bf16[128,2304]{1,0:T(8,128)(2,1)S(1)}, bf16[128,2304]{1,0:T(8,128)(2,1)S(1)}, u32[]{:S(2)}, u32[]{:S(2)}) %collective-permute-start.4) | collective-permute-done | bytes 589856 | tf_op jit(solution)/shard_map/ppermute | solution.py:573
  33.1 0.5 gate.1
  33.6 1.5 collective-permute-start.5
  35.1 0.5 collective-permute-start.6
  35.6 1.6 collective-permute-start.9
  37.2 1.5 collective-permute-start.8
  38.7 8.0 %expert_rows.5 = (bf16[320,768]{1,0:T(8,128)(2,1)S(1)}, bf16[320,768]{1,0:T(8,128)(2,1)S(1)}, bf16[2,64,128]{2,1,0:T(8,128)(2,1)S(1)}, f32[8,128]{1,0:T(8,128)}) custom-call(s32[3]{0:T(128)S(1)} %pad_add_fusion.refs_0_, bf16[128,2304]{1,0:T(8,128)(2,1)S(1)} %collective-permute-done.3.refs_1_.refs_7_.refs_4_, ...), custom_call_target="tpu_custom_call" | custom-call | flops 1 | bytes 1 | tf_op jit(solution)/shard_map/expert_rows/pallas_call | solution.py:53
  46.7 0.6 collective-permute-start.7
  47.3 1.7 collective-permute-done.5.refs_1_.refs_9_.refs_6_
  49.0 0.5 collective-permute-start.10
  49.5 1.9 %collective-permute-done.6.refs_4_.refs_2_.refs_10_.refs_7_ = bf16[128,2304]{1,0:T(8,128)(2,1)S(1)} collective-permute-done((bf16[128,2304]{1,0:T(8,128)(2,1)S(1)}, bf16[128,2304]{1,0:T(8,128)(2,1)S(1)}, u32[]{:S(2)}, u32[]{:S(2)}) %collective-permute-start.6) | collective-permute-done | bytes 589856 | tf_op jit(solution)/shard_map/ppermute | solution.py:573
  51.4 0.7 share_sum.4
  52.1 7.2 %collective-permute-done.7.refs_2_ = bf16[320,768]{1,0:T(8,128)(2,1)S(1)} collective-permute-done((bf16[320,768]{1,0:T(8,128)(2,1)S(1)}, bf16[320,768]{1,0:T(8,128)(2,1)S(1)}, u32[]{:S(2)}, u32[]{:S(2)}) %collective-permute-start.7) | collective-permute-done | bytes 491552 | tf_op jit(solution)/shard_map/ppermute | solution.py:567
  59.3 1.3 share_sum.5
  60.6 3.4 %collective-permute-done.9.refs_8_.refs_1_.refs_11_ = bf16[128,2304]{1,0:T(8,128)(2,1)S(1)} collective-permute-done((bf16[128,2304]{1,0:T(8,128)(2,1)S(1)}, bf16[128,2304]{1,0:T(8,128)(2,1)S(1)}, u32[]{:S(2)}, u32[]{:S(2)}) %collective-permute-start.9) | collective-permute-done | bytes 589856 | tf_op jit(solution)/shard_map/ppermute | solution.py:573
  64.1 8.4 %expert_rows.6 = (bf16[320,768]{1,0:T(8,128)(2,1)S(1)}, bf16[320,768]{1,0:T(8,128)(2,1)S(1)}, bf16[2,64,128]{2,1,0:T(8,128)(2,1)S(1)}, f32[8,128]{1,0:T(8,128)}) custom-call(s32[3]{0:T(128)S(1)} %pad_add_fusion.refs_0_, bf16[128,2304]{1,0:T(8,128)(2,1)S(1)} %collective-permute-done.5.refs_1_.refs_9_.refs_6_, ...), custom_call_target="tpu_custom_call" | custom-call | flops 1 | bytes 1 | tf_op jit(solution)/shard_map/expert_rows/pallas_call | solution.py:53
  72.4 1.6 collective-permute-start.11
  74.0 0.7 collective-permute-done.10.refs_2_.refs_12_.refs_9_
  74.7 8.2 %expert_rows.7 = (bf16[320,768]{1,0:T(8,128)(2,1)S(1)}, bf16[320,768]{1,0:T(8,128)(2,1)S(1)}, bf16[2,64,128]{2,1,0:T(8,128)(2,1)S(1)}, f32[8,128]{1,0:T(8,128)}) custom-call(s32[3]{0:T(128)S(1)} %pad_add_fusion.refs_0_, bf16[128,2304]{1,0:T(8,128)(2,1)S(1)} %collective-permute-done.9.refs_8_.refs_1_.refs_11_, ...), custom_call_target="tpu_custom_call" | custom-call | flops 1 | bytes 1 | tf_op jit(solution)/shard_map/expert_rows/pallas_call | solution.py:53
  82.9 1.6 collective-permute-start.14
  84.5 3.0 %collective-permute-start.16 = (bf16[160,768]{1,0:T(8,128)(2,1)S(1)}, bf16[160,768]{1,0:T(8,128)(2,1)}, u32[]{:S(2)}, u32[]{:S(2)}) collective-permute-start(bf16[160,768]{1,0:T(8,128)(2,1)S(1)} %get-tuple-element.86), channel_id=1, source_target_pairs={{0,16},{4,20},{8,24},{12,28},{16,0},{20,4},{24,8},{28,12},{1,17},{... | collective-permute-start | bytes 737288 | tf_op jit(solution)/shard_map/ppermute | solution.py:573
  87.5 1.3 share_sum.6
  89.0 1.8 collect_blocks.1
  90.8 1.6 collective-permute-start.19
  92.4 10.9 %collective-permute-done.16.block_ref.refs_12_ = bf16[160,768]{1,0:T(8,128)(2,1)} collective-permute-done((bf16[160,768]{1,0:T(8,128)(2,1)S(1)}, bf16[160,768]{1,0:T(8,128)(2,1)}, u32[]{:S(2)}, u32[]{:S(2)}) %collective-permute-start.16) | collective-permute-done | bytes 245792 | tf_op jit(solution)/shard_map/ppermute | solution.py:573
  103.3 0.6 touch.1
  103.9 1.4 collective-permute-done.17.refs_5_
  105.3 0.5 collective-permute-start.18
  105.8 7.2 %all-to-all-start = ((bf16[8,64,128]{2,1,0:T(8,128)(2,1)}), bf16[8,64,128]{2,1,0:T(8,128)(2,1)S(1)}, u32[]{:S(2)}, u32[]{:S(2)}) async-start(bf16[8,64,128]{2,1,0:T(8,128)(2,1)} %get-tuple-element.80), calls=%async_computation | async-start | bytes 262144 | tf_op jit(solution)/shard_map/all_to_all | solution.py:581
  113.1 1.3 share_sum.7
  114.4 2.9 %collective-permute-start.22 = (bf16[160,768]{1,0:T(8,128)(2,1)}, bf16[160,768]{1,0:T(8,128)(2,1)}, u32[]{:S(2)}, u32[]{:S(2)}) collective-permute-start(bf16[160,768]{1,0:T(8,128)(2,1)} %get-tuple-element.94), channel_id=1, source_target_pairs={{0,16},{4,20},{8,24},{12,28},{16,0},{20,4},{24,8},{28,12},{1,17},{... | collective-permute-start | bytes 737288 | tf_op jit(solution)/shard_map/ppermute | solution.py:573
  117.5 1.8 all-to-all-done.refs_6_.refs_1_
  119.2 3.6 %lowrank_hid.1 = (f32[128,512]{1,0:T(8,128)S(1)}, f32[8,128]{1,0:T(8,128)}) custom-call(s32[3]{0:T(128)S(1)} %pad_add_fusion.refs_0_, s32[128,8]{1,0:T(8,128)S(1)} %copy.17.refs_1_.refs_5_.refs_2_, bf16[1024,768]{1,0:T(8,128)(2,1)} %bitcast.29, bf16[256,768]{1,0:T(8,128)(2,1)S(1)} %bitcast.23, bf16[256,768]{1,0:T(8,128)(2,1)S(1)} %bitcast.25, ...), custom_call_target="tpu_custom_call" | custom-call | flops 1 | bytes 1 | tf_op jit(solution)/shard_map/lowrank_hid/pallas_call | solution.py:53
  122.8 0.6 collective-permute-start.27
  123.4 1.9 %collective-permute-done.20 = bf16[160,768]{1,0:T(8,128)(2,1)} collective-permute-done((bf16[160,768]{1,0:T(8,128)(2,1)}, bf16[160,768]{1,0:T(8,128)(2,1)}, u32[]{:S(2)}, u32[]{:S(2)}) %collective-permute-start.20) | collective-permute-done | bytes 245792 | tf_op jit(solution)/shard_map/ppermute | solution.py:573
  125.3 1.6 collective-permute-start.21
  126.8 7.7 %collective-permute-done.22 = bf16[160,768]{1,0:T(8,128)(2,1)} collective-permute-done((bf16[160,768]{1,0:T(8,128)(2,1)}, bf16[160,768]{1,0:T(8,128)(2,1)}, u32[]{:S(2)}, u32[]{:S(2)}) %collective-permute-start.22) | collective-permute-done | bytes 245792 | tf_op jit(solution)/shard_map/ppermute | solution.py:573
  134.5 1.5 collective-permute-start.23
  136.0 0.5 collective-permute-start.12
  136.5 1.2 collective-permute-done.24
  137.7 3.2 %collective-permute-start.25 = (bf16[160,768]{1,0:T(8,128)(2,1)}, bf16[160,768]{1,0:T(8,128)(2,1)}, u32[]{:S(2)}, u32[]{:S(2)}) collective-permute-start(bf16[160,768]{1,0:T(8,128)(2,1)} %collective-permute-done.24), channel_id=1, source_target_pairs={{0,8},{4,12},{8,0},{12,4},{16,24},{20,28},{24,16},{28,20},{1,9},{5... | collective-permute-start | bytes 737288 | tf_op jit(solution)/shard_map/ppermute | solution.py:573
  141.0 0.7 low_dense.1
  141.8 4.7 %first_grad.1 = (f32[8,32,768]{2,1,0:T(8,128)S(1)}, bf16[8,32,768]{2,1,0:T(8,128)(2,1)S(1)}, bf16[8,32,256]{2,1,0:T(8,128)(2,1)S(1)}, f32[8,128]{1,0:T(8,128)}) custom-call(s32[3]{0:T(128)S(1)} %pad_add_fusion.refs_0_, s32[128,8]{1,0:T(8,128)S(1)} %copy.17.refs_1_.refs_5_.refs_2_, bf16[128,8]{1,0:T(8,128)(2,1)S(1)} %copy.19.refs_2_.refs_6_.refs_3_, ...), custom_call_target="tpu_custom_call" | custom-call | flops 1 | bytes 1 | tf_op jit(solution)/shard_map/first_grad/pallas_call | solution.py:53
  146.6 1.4 collective-permute-start.26
  148.0 7.1 %collective-permute-done.26.refs_5_.refs_15_ = bf16[160,768]{1,0:T(8,128)(2,1)S(1)} collective-permute-done((bf16[160,768]{1,0:T(8,128)(2,1)}, bf16[160,768]{1,0:T(8,128)(2,1)S(1)}, u32[]{:S(2)}, u32[]{:S(2)}) %collective-permute-start.26) | collective-permute-done | bytes 245792 | tf_op jit(solution)/shard_map/ppermute | solution.py:573
  155.2 0.6 first_sum.1
  155.8 0.8 copy-done.16
  156.6 6.2 %all-to-all-start.1 = ((bf16[8,32,1024]{2,1,0:T(8,128)(2,1)}), bf16[8,32,1024]{2,1,0:T(8,128)(2,1)S(1)}, u32[]{:S(2)}, u32[]{:S(2)}) async-start(bf16[8,32,1024]{2,1,0:T(8,128)(2,1)} %copy-done.16), calls=%async_computation.1 | async-start | bytes 1048576 | tf_op jit(solution)/shard_map/all_to_all | solution.py:581
  162.8 7.9 %finish.1 = (bf16[1024,768]{1,0:T(8,128)(2,1)}, f32[128,8]{1,0:T(8,128)S(1)}, f32[8,128]{1,0:T(8,128)}) custom-call(s32[3]{0:T(128)S(1)} %pad_add_fusion.refs_0_, s32[128,8]{1,0:T(8,128)S(1)} %copy.17.refs_1_.refs_5_.refs_2_, s32[128,8]{1,0:T(8,128)S(1)} %copy.17.refs_1_.refs_5_.refs_2_, bf16[128,8]{1,0:T(8,128)(2,1)S(1)} %copy.19.refs_2_.refs_6_.refs_3_, ...), custom_call_target="tpu_custom_call" | custom-call | flops 1 | bytes 20000000 | tf_op jit(solution)/shard_map/finish/pallas_call | solution.py:53
  170.7 0.5 collective-permute-start.29
  171.2 3.7 %collective-permute-done.29.refs_11_ = f32[128,8]{1,0:T(8,128)S(1)} collective-permute-done((f32[128,8]{1,0:T(8,128)S(1)}, f32[128,8]{1,0:T(8,128)S(1)}, u32[]{:S(2)}, u32[]{:S(2)}) %collective-permute-start.29) | collective-permute-done | bytes 4128 | tf_op jit(solution)/shard_map/ppermute | solution.py:567
  175.0 0.9 all-to-all-done.1.refs_1_
  175.8 4.4 %second_grad.1 = (f32[32,2048]{1,0:T(8,128)S(1)}, f32[32,2048]{1,0:T(8,128)S(1)}, f32[32,768]{1,0:T(8,128)}, f32[8,128]{1,0:T(8,128)}) custom-call(s32[3]{0:T(128)S(1)} %pad_add_fusion.refs_0_, bf16[8,32,1024]{2,1,0:T(8,128)(2,1)S(1)} %all-to-all-done.1.refs_1_, bf16[128,2304]{1,0:T(8,128)(2,1)} %copy-done.3, bf16[128,2304]{1,0:T(8,128)(2,1)} %copy-done.4, ...), custom_call_target="tpu_custom_call" | custom-call | flops 1 | bytes 1 | tf_op jit(solution)/shard_map/second_grad/pallas_call | solution.py:53
  180.2 0.7 copy.20
  180.9 0.8 collective-permute-done.30
  181.7 0.7 add_bitcast_fusion
  (73 shorter events, 1.4 us)
Async XLA Ops:
  0.6 18.6 %copy-start.8 = (bf16[1,32,2048]{2,1,0:T(8,128)(2,1)S(1)}, bf16[1,32,2048]{2,1,0:T(8,128)(2,1)}, u32[]{:S(2)}) copy-start(bf16[1,32,2048]{2,1,0:T(8,128)(2,1)} %param.13) | copy-start | bytes 393220
  0.6 18.6 %collective-permute-start.2 = (bf16[1536,2048]{1,0:T(8,128)(2,1)}, bf16[1536,2048]{1,0:T(8,128)(2,1)}, u32[]{:S(2)}, u32[]{:S(2)}) collective-permute-start(bf16[1536,2048]{1,0:T(8,128)(2,1)} %bitcast.32), channel_id=1, source_target_pairs={{0,1},{1,0},{2,3},{3,2},{4,5},{5,4},{6,7},{7,6},{8,9},{9,8},{10,11... | collective-permute-start | bytes 18874376 | tf_op jit(solution)/shard_map/ppermute | solution.py:576
  0.8 0.8 copy-start.18
  1.6 0.7 copy-start.19
  3.4 24.0 %copy-start.3 = (bf16[128,2304]{1,0:T(8,128)(2,1)}, bf16[128,2304]{1,0:T(8,128)(2,1)S(1)}, u32[]{:S(2)}) copy-start(bf16[128,2304]{1,0:T(8,128)(2,1)S(1)} %get-tuple-element.57.refs_1_.refs_5_.refs_2_) | copy-start | bytes 1769476
  3.4 15.8 %collective-permute-start = (bf16[128,2304]{1,0:T(8,128)(2,1)S(1)}, bf16[128,2304]{1,0:T(8,128)(2,1)S(1)}, u32[]{:S(2)}, u32[]{:S(2)}) collective-permute-start(bf16[128,2304]{1,0:T(8,128)(2,1)S(1)} %get-tuple-element.57.refs_1_.refs_5_.refs_2_), channel_id=1, source_target_pairs={{0,4},{4,0},{8,12},{12,8},{16,20},{20,16},{24,28},{28,24},{1,5},{5... | collective-permute-start | bytes 1769480 | tf_op jit(solution)/shard_map/ppermute | solution.py:573
  5.0 28.1 %collective-permute-start.4 = (bf16[128,2304]{1,0:T(8,128)(2,1)S(1)}, bf16[128,2304]{1,0:T(8,128)(2,1)S(1)}, u32[]{:S(2)}, u32[]{:S(2)}) collective-permute-start(bf16[128,2304]{1,0:T(8,128)(2,1)S(1)} %get-tuple-element.57.refs_1_.refs_5_.refs_2_), channel_id=1, source_target_pairs={{0,16},{4,20},{8,24},{12,28},{16,0},{20,4},{24,8},{28,12},{1,17},{... | collective-permute-start | bytes 1769480 | tf_op jit(solution)/shard_map/ppermute | solution.py:573
  7.6 27.6 %collective-permute-start.3 = (bf16[128,2304]{1,0:T(8,128)(2,1)S(1)}, bf16[128,2304]{1,0:T(8,128)(2,1)S(1)}, u32[]{:S(2)}, u32[]{:S(2)}) collective-permute-start(bf16[128,2304]{1,0:T(8,128)(2,1)S(1)} %get-tuple-element.57.refs_1_.refs_5_.refs_2_), channel_id=1, source_target_pairs={{0,8},{4,12},{8,0},{12,4},{16,24},{20,28},{24,16},{28,20},{1,9},{5... | collective-permute-start | bytes 1769480 | tf_op jit(solution)/shard_map/ppermute | solution.py:573
  8.0 3.4 %collective-permute-start.1 = (bf16[32,2048]{1,0:T(8,128)(2,1)}, bf16[32,2048]{1,0:T(8,128)(2,1)S(1)}, u32[]{:S(2)}, u32[]{:S(2)}) collective-permute-start(bf16[32,2048]{1,0:T(8,128)(2,1)} %bitcast.18), channel_id=1, source_target_pairs={{0,1},{1,0},{2,3},{3,2},{4,5},{5,4},{6,7},{7,6},{8,9},{9,8},{10,11... | collective-permute-start | bytes 393224 | tf_op jit(solution)/shard_map/ppermute | solution.py:576
  19.2 8.3 %copy-start.4 = (bf16[128,2304]{1,0:T(8,128)(2,1)}, bf16[128,2304]{1,0:T(8,128)(2,1)S(1)}, u32[]{:S(2)}) copy-start(bf16[128,2304]{1,0:T(8,128)(2,1)S(1)} %collective-permute-done.refs_2_.refs_6_.refs_3_) | copy-start | bytes 1769476
  19.2 19.5 %copy-start.9 = (bf16[1,32,2048]{2,1,0:T(8,128)(2,1)S(1)}, bf16[1,32,2048]{2,1,0:T(8,128)(2,1)}, u32[]{:S(2)}) copy-start(bf16[1,32,2048]{2,1,0:T(8,128)(2,1)} %param.13) | copy-start | bytes 393220
  33.6 13.0 %copy-start.2 = (bf16[128,2304]{1,0:T(8,128)(2,1)}, bf16[128,2304]{1,0:T(8,128)(2,1)S(1)}, u32[]{:S(2)}) copy-start(bf16[128,2304]{1,0:T(8,128)(2,1)S(1)} %get-tuple-element.63.refs_2_.refs_8_.refs_5_) | copy-start | bytes 1769476
  33.6 15.3 %collective-permute-start.5 = (bf16[128,2304]{1,0:T(8,128)(2,1)S(1)}, bf16[128,2304]{1,0:T(8,128)(2,1)S(1)}, u32[]{:S(2)}, u32[]{:S(2)}) collective-permute-start(bf16[128,2304]{1,0:T(8,128)(2,1)S(1)} %get-tuple-element.63.refs_2_.refs_8_.refs_5_), channel_id=1, source_target_pairs={{0,8},{4,12},{8,0},{12,4},{16,24},{20,28},{24,16},{28,20},{1,9},{5... | collective-permute-start | bytes 1769480 | tf_op jit(solution)/shard_map/ppermute | solution.py:573
  35.1 11.5 %copy-start.5 = (bf16[128,2304]{1,0:T(8,128)(2,1)}, bf16[128,2304]{1,0:T(8,128)(2,1)S(1)}, u32[]{:S(2)}) copy-start(bf16[128,2304]{1,0:T(8,128)(2,1)S(1)} %collective-permute-done.3.refs_1_.refs_7_.refs_4_) | copy-start | bytes 1769476
  35.1 16.3 %collective-permute-start.6 = (bf16[128,2304]{1,0:T(8,128)(2,1)S(1)}, bf16[128,2304]{1,0:T(8,128)(2,1)S(1)}, u32[]{:S(2)}, u32[]{:S(2)}) collective-permute-start(bf16[128,2304]{1,0:T(8,128)(2,1)S(1)} %collective-permute-done.3.refs_1_.refs_7_.refs_4_), channel_id=1, source_target_pairs={{0,4},{4,0},{8,12},{12,8},{16,20},{20,16},{24,28},{28,24},{1,5},{5... | collective-permute-start | bytes 1769480 | tf_op jit(solution)/shard_map/ppermute | solution.py:573
  35.6 28.4 %collective-permute-start.9 = (bf16[128,2304]{1,0:T(8,128)(2,1)S(1)}, bf16[128,2304]{1,0:T(8,128)(2,1)S(1)}, u32[]{:S(2)}, u32[]{:S(2)}) collective-permute-start(bf16[128,2304]{1,0:T(8,128)(2,1)S(1)} %get-tuple-element.63.refs_2_.refs_8_.refs_5_), channel_id=1, source_target_pairs={{0,4},{4,0},{8,12},{12,8},{16,20},{20,16},{24,28},{28,24},{1,5},{5... | collective-permute-start | bytes 1769480 | tf_op jit(solution)/shard_map/ppermute | solution.py:573
  37.2 14.2 %collective-permute-start.8 = (bf16[320,768]{1,0:T(8,128)(2,1)S(1)}, bf16[320,768]{1,0:T(8,128)(2,1)S(1)}, u32[]{:S(2)}, u32[]{:S(2)}) collective-permute-start(bf16[320,768]{1,0:T(8,128)(2,1)S(1)} %get-tuple-element.69), channel_id=1, source_target_pairs={{0,2},{2,0},{1,3},{3,1},{4,6},{6,4},{5,7},{7,5},{8,10},{10,8},{9,1... | collective-permute-start | bytes 1474568 | tf_op jit(solution)/shard_map/ppermute | solution.py:567
  46.7 12.6 %collective-permute-start.7 = (bf16[320,768]{1,0:T(8,128)(2,1)S(1)}, bf16[320,768]{1,0:T(8,128)(2,1)S(1)}, u32[]{:S(2)}, u32[]{:S(2)}) collective-permute-start(bf16[320,768]{1,0:T(8,128)(2,1)S(1)} %get-tuple-element.67), channel_id=1, source_target_pairs={{0,2},{2,0},{1,3},{3,1},{4,6},{6,4},{5,7},{7,5},{8,10},{10,8},{9,1... | collective-permute-start | bytes 1474568 | tf_op jit(solution)/shard_map/ppermute | solution.py:567
  49.0 23.5 %copy-start.6 = (bf16[128,2304]{1,0:T(8,128)(2,1)}, bf16[128,2304]{1,0:T(8,128)(2,1)S(1)}, u32[]{:S(2)}) copy-start(bf16[128,2304]{1,0:T(8,128)(2,1)S(1)} %collective-permute-done.5.refs_1_.refs_9_.refs_6_) | copy-start | bytes 1769476
  49.0 25.7 %collective-permute-start.10 = (bf16[128,2304]{1,0:T(8,128)(2,1)S(1)}, bf16[128,2304]{1,0:T(8,128)(2,1)S(1)}, u32[]{:S(2)}, u32[]{:S(2)}) collective-permute-start(bf16[128,2304]{1,0:T(8,128)(2,1)S(1)} %collective-permute-done.5.refs_1_.refs_9_.refs_6_), channel_id=1, source_target_pairs={{0,4},{4,0},{8,12},{12,8},{16,20},{20,16},{24,28},{28,24},{1,5},{5... | collective-permute-start | bytes 1769480 | tf_op jit(solution)/shard_map/ppermute | solution.py:573
  51.4 21.0 %copy-start.1 = (bf16[128,2304]{1,0:T(8,128)(2,1)}, bf16[128,2304]{1,0:T(8,128)(2,1)S(1)}, u32[]{:S(2)}) copy-start(bf16[128,2304]{1,0:T(8,128)(2,1)S(1)} %collective-permute-done.6.refs_4_.refs_2_.refs_10_.refs_7_) | copy-start | bytes 1769476
  52.1 12.0 %copy-start.17 = (bf16[160,768]{1,0:T(8,128)(2,1)}, bf16[160,768]{1,0:T(8,128)(2,1)S(1)}, u32[]{:S(2)}) copy-start(bf16[160,768]{1,0:T(8,128)(2,1)S(1)} %get-tuple-element.93.refs_8_) | copy-start | bytes 737284
  64.1 10.7 %copy-start = (bf16[128,2304]{1,0:T(8,128)(2,1)}, bf16[128,2304]{1,0:T(8,128)(2,1)S(1)}, u32[]{:S(2)}) copy-start(bf16[128,2304]{1,0:T(8,128)(2,1)S(1)} %collective-permute-done.9.refs_8_.refs_1_.refs_11_) | copy-start | bytes 1769476
  72.4 15.1 %collective-permute-start.11 = (bf16[320,768]{1,0:T(8,128)(2,1)S(1)}, bf16[320,768]{1,0:T(8,128)(2,1)S(1)}, u32[]{:S(2)}, u32[]{:S(2)}) collective-permute-start(bf16[320,768]{1,0:T(8,128)(2,1)S(1)} %get-tuple-element.77), channel_id=1, source_target_pairs={{0,2},{2,0},{1,3},{3,1},{4,6},{6,4},{5,7},{7,5},{8,10},{10,8},{9,1... | collective-permute-start | bytes 1474568 | tf_op jit(solution)/shard_map/ppermute | solution.py:567
  74.7 8.2 %copy-start.7 = (bf16[128,2304]{1,0:T(8,128)(2,1)}, bf16[128,2304]{1,0:T(8,128)(2,1)S(1)}, u32[]{:S(2)}) copy-start(bf16[128,2304]{1,0:T(8,128)(2,1)S(1)} %collective-permute-done.10.refs_2_.refs_12_.refs_9_) | copy-start | bytes 1769476
  82.9 34.4 %copy-start.20 = (s32[128,8]{0,1:T(8,128)S(1)}, s32[128,8]{0,1:T(8,128)}, u32[]{:S(2)}) copy-start(s32[128,8]{0,1:T(8,128)} %param.9) | copy-start | bytes 12292
  82.9 58.0 %copy-start.22 = (bf16[128,8]{0,1:T(8,128)(2,1)S(1)}, bf16[128,8]{0,1:T(8,128)(2,1)}, u32[]{:S(2)}) copy-start(bf16[128,8]{0,1:T(8,128)(2,1)} %param.10) | copy-start | bytes 6148
  82.9 30.1 %collective-permute-start.14 = (bf16[320,768]{1,0:T(8,128)(2,1)S(1)}, bf16[320,768]{1,0:T(8,128)(2,1)S(1)}, u32[]{:S(2)}, u32[]{:S(2)}) collective-permute-start(bf16[320,768]{1,0:T(8,128)(2,1)S(1)} %get-tuple-element.83), channel_id=1, source_target_pairs={{0,2},{2,0},{1,3},{3,1},{4,6},{6,4},{5,7},{7,5},{8,10},{10,8},{9,1... | collective-permute-start | bytes 1474568 | tf_op jit(solution)/shard_map/ppermute | solution.py:567
  84.5 18.8 %collective-permute-start.16 = (bf16[160,768]{1,0:T(8,128)(2,1)S(1)}, bf16[160,768]{1,0:T(8,128)(2,1)}, u32[]{:S(2)}, u32[]{:S(2)}) collective-permute-start(bf16[160,768]{1,0:T(8,128)(2,1)S(1)} %get-tuple-element.86), channel_id=1, source_target_pairs={{0,16},{4,20},{8,24},{12,28},{16,0},{20,4},{24,8},{28,12},{1,17},{... | collective-permute-start | bytes 737288 | tf_op jit(solution)/shard_map/ppermute | solution.py:573
  88.8 2.0 %copy-start.21 = (bf16[160,768]{1,0:T(8,128)(2,1)}, bf16[160,768]{1,0:T(8,128)(2,1)S(1)}, u32[]{:S(2)}) copy-start(bf16[160,768]{1,0:T(8,128)(2,1)S(1)} %get-tuple-element.91) | copy-start | bytes 737284
  88.8 24.2 %collective-permute-start.15 = (bf16[160,768]{1,0:T(8,128)(2,1)}, bf16[160,768]{1,0:T(8,128)(2,1)S(1)}, u32[]{:S(2)}, u32[]{:S(2)}) collective-permute-start(bf16[160,768]{1,0:T(8,128)(2,1)} %get-tuple-element.85), channel_id=1, source_target_pairs={{0,24},{4,28},{8,16},{12,20},{16,8},{20,12},{24,0},{28,4},{1,25},{... | collective-permute-start | bytes 737288 | tf_op jit(solution)/shard_map/ppermute | solution.py:573
  90.7 28.5 %collective-permute-start.13 = (bf16[8,32,768]{2,1,0:T(8,128)(2,1)S(1)}, bf16[8,32,768]{2,1,0:T(8,128)(2,1)S(1)}, u32[]{:S(2)}, u32[]{:S(2)}) collective-permute-start(bf16[8,32,768]{2,1,0:T(8,128)(2,1)S(1)} %get-tuple-element.81), channel_id=1, source_target_pairs={{0,1},{1,0},{2,3},{3,2},{4,5},{5,4},{6,7},{7,6},{8,9},{9,8},{10,11... | collective-permute-start | bytes 1179656 | tf_op jit(solution)/shard_map/ppermute | solution.py:576
  90.8 26.5 %collective-permute-start.19 = (bf16[160,768]{1,0:T(8,128)(2,1)}, bf16[160,768]{1,0:T(8,128)(2,1)S(1)}, u32[]{:S(2)}, u32[]{:S(2)}) collective-permute-start(bf16[160,768]{1,0:T(8,128)(2,1)} %get-tuple-element.89), channel_id=1, source_target_pairs={{0,8},{4,12},{8,0},{12,4},{16,24},{20,28},{24,16},{28,20},{1,9},{5... | collective-permute-start | bytes 737288 | tf_op jit(solution)/shard_map/ppermute | solution.py:573
  103.9 1.4 collective-permute-start.17
  105.3 12.2 %collective-permute-start.18 = (bf16[160,768]{1,0:T(8,128)(2,1)S(1)}, bf16[160,768]{1,0:T(8,128)(2,1)S(1)}, u32[]{:S(2)}, u32[]{:S(2)}) collective-permute-start(bf16[160,768]{1,0:T(8,128)(2,1)S(1)} %get-tuple-element.88), channel_id=1, source_target_pairs={{0,4},{4,0},{8,12},{12,8},{16,20},{20,16},{24,28},{28,24},{1,5},{5... | collective-permute-start | bytes 737288 | tf_op jit(solution)/shard_map/ppermute | solution.py:573
  105.8 13.4 %all-to-all-start = ((bf16[8,64,128]{2,1,0:T(8,128)(2,1)}), bf16[8,64,128]{2,1,0:T(8,128)(2,1)S(1)}, u32[]{:S(2)}, u32[]{:S(2)}) async-start(bf16[8,64,128]{2,1,0:T(8,128)(2,1)} %get-tuple-element.80), calls=%async_computation | async-start | bytes 262144 | tf_op jit(solution)/shard_map/all_to_all | solution.py:581
  113.0 49.8 %copy-start.11 = (bf16[160,768]{1,0:T(8,128)(2,1)}, bf16[160,768]{1,0:T(8,128)(2,1)S(1)}, u32[]{:S(2)}) copy-start(bf16[160,768]{1,0:T(8,128)(2,1)S(1)} %collective-permute-done.15.refs_4_.refs_14_) | copy-start | bytes 737284
  113.0 12.3 %collective-permute-start.20 = (bf16[160,768]{1,0:T(8,128)(2,1)}, bf16[160,768]{1,0:T(8,128)(2,1)}, u32[]{:S(2)}, u32[]{:S(2)}) collective-permute-start(bf16[160,768]{1,0:T(8,128)(2,1)} %copy-done.21), channel_id=1, source_target_pairs={{0,8},{4,12},{8,0},{12,4},{16,24},{20,28},{24,16},{28,20},{1,9},{5... | collective-permute-start | bytes 737288 | tf_op jit(solution)/shard_map/ppermute | solution.py:573
  114.4 20.2 %collective-permute-start.22 = (bf16[160,768]{1,0:T(8,128)(2,1)}, bf16[160,768]{1,0:T(8,128)(2,1)}, u32[]{:S(2)}, u32[]{:S(2)}) collective-permute-start(bf16[160,768]{1,0:T(8,128)(2,1)} %get-tuple-element.94), channel_id=1, source_target_pairs={{0,16},{4,20},{8,24},{12,28},{16,0},{20,4},{24,8},{28,12},{1,17},{... | collective-permute-start | bytes 737288 | tf_op jit(solution)/shard_map/ppermute | solution.py:573
  117.3 45.5 %copy-start.12 = (bf16[160,768]{1,0:T(8,128)(2,1)}, bf16[160,768]{1,0:T(8,128)(2,1)S(1)}, u32[]{:S(2)}) copy-start(bf16[160,768]{1,0:T(8,128)(2,1)S(1)} %collective-permute-done.19.refs_8_.refs_10_) | copy-start | bytes 737284
  117.3 20.5 %collective-permute-start.24 = (bf16[160,768]{1,0:T(8,128)(2,1)S(1)}, bf16[160,768]{1,0:T(8,128)(2,1)}, u32[]{:S(2)}, u32[]{:S(2)}) collective-permute-start(bf16[160,768]{1,0:T(8,128)(2,1)S(1)} %get-tuple-element.95), channel_id=1, source_target_pairs={{0,16},{4,20},{8,24},{12,28},{16,0},{20,4},{24,8},{28,12},{1,17},{... | collective-permute-start | bytes 737288 | tf_op jit(solution)/shard_map/ppermute | solution.py:573
  117.4 45.4 %copy-start.13 = (bf16[160,768]{1,0:T(8,128)(2,1)}, bf16[160,768]{1,0:T(8,128)(2,1)S(1)}, u32[]{:S(2)}) copy-start(bf16[160,768]{1,0:T(8,128)(2,1)S(1)} %collective-permute-done.18.refs_7_.refs_9_) | copy-start | bytes 737284
  122.8 18.9 %collective-permute-start.27 = (f32[128,512]{1,0:T(8,128)S(1)}, f32[128,512]{1,0:T(8,128)S(1)}, u32[]{:S(2)}, u32[]{:S(2)}) collective-permute-start(f32[128,512]{1,0:T(8,128)S(1)} %get-tuple-element.96.refs_7_), channel_id=1, source_target_pairs={{0,2},{2,0},{1,3},{3,1},{4,6},{6,4},{5,7},{7,5},{8,10},{10,8},{9,1... | collective-permute-start | bytes 786440 | tf_op jit(solution)/shard_map/ppermute | solution.py:567
  125.3 15.7 %collective-permute-start.21 = (bf16[160,768]{1,0:T(8,128)(2,1)}, bf16[160,768]{1,0:T(8,128)(2,1)S(1)}, u32[]{:S(2)}, u32[]{:S(2)}) collective-permute-start(bf16[160,768]{1,0:T(8,128)(2,1)} %collective-permute-done.20), channel_id=1, source_target_pairs={{0,4},{4,0},{8,12},{12,8},{16,20},{20,16},{24,28},{28,24},{1,5},{5... | collective-permute-start | bytes 737288 | tf_op jit(solution)/shard_map/ppermute | solution.py:573
  134.5 7.2 %collective-permute-start.23 = (bf16[160,768]{1,0:T(8,128)(2,1)}, bf16[160,768]{1,0:T(8,128)(2,1)S(1)}, u32[]{:S(2)}, u32[]{:S(2)}) collective-permute-start(bf16[160,768]{1,0:T(8,128)(2,1)} %collective-permute-done.22), channel_id=1, source_target_pairs={{0,4},{4,0},{8,12},{12,8},{16,20},{20,16},{24,28},{28,24},{1,5},{5... | collective-permute-start | bytes 737288 | tf_op jit(solution)/shard_map/ppermute | solution.py:573
  136.0 5.0 %collective-permute-start.12 = (bf16[8,64,128]{2,1,0:T(8,128)(2,1)S(1)}, bf16[8,64,128]{2,1,0:T(8,128)(2,1)S(1)}, u32[]{:S(2)}, u32[]{:S(2)}) collective-permute-start(bf16[8,64,128]{2,1,0:T(8,128)(2,1)S(1)} %all-to-all-done.refs_6_.refs_1_), channel_id=1, source_target_pairs={{0,2},{2,0},{1,3},{3,1},{4,6},{6,4},{5,7},{7,5},{8,10},{10,8},{9,1... | collective-permute-start | bytes 393224 | tf_op jit(solution)/shard_map/ppermute | solution.py:567
  137.7 8.8 %collective-permute-start.25 = (bf16[160,768]{1,0:T(8,128)(2,1)}, bf16[160,768]{1,0:T(8,128)(2,1)}, u32[]{:S(2)}, u32[]{:S(2)}) collective-permute-start(bf16[160,768]{1,0:T(8,128)(2,1)} %collective-permute-done.24), channel_id=1, source_target_pairs={{0,8},{4,12},{8,0},{12,4},{16,24},{20,28},{24,16},{28,20},{1,9},{5... | collective-permute-start | bytes 737288 | tf_op jit(solution)/shard_map/ppermute | solution.py:573
  141.0 21.8 %copy-start.10 = (bf16[160,768]{1,0:T(8,128)(2,1)}, bf16[160,768]{1,0:T(8,128)(2,1)S(1)}, u32[]{:S(2)}) copy-start(bf16[160,768]{1,0:T(8,128)(2,1)S(1)} %collective-permute-done.21.refs_4_.refs_11_) | copy-start | bytes 737284
  141.7 21.1 %copy-start.14 = (bf16[160,768]{1,0:T(8,128)(2,1)}, bf16[160,768]{1,0:T(8,128)(2,1)S(1)}, u32[]{:S(2)}) copy-start(bf16[160,768]{1,0:T(8,128)(2,1)S(1)} %collective-permute-done.23.refs_10_.refs_13_) | copy-start | bytes 737284
  146.5 8.7 %collective-permute-start.28 = (bf16[8,32,768]{2,1,0:T(8,128)(2,1)S(1)}, bf16[8,32,768]{2,1,0:T(8,128)(2,1)S(1)}, u32[]{:S(2)}, u32[]{:S(2)}) collective-permute-start(bf16[8,32,768]{2,1,0:T(8,128)(2,1)S(1)} %get-tuple-element.99), channel_id=1, source_target_pairs={{0,1},{1,0},{2,3},{3,2},{4,5},{5,4},{6,7},{7,6},{8,9},{9,8},{10,11... | collective-permute-start | bytes 1179656 | tf_op jit(solution)/shard_map/ppermute | solution.py:576
  146.6 8.6 %collective-permute-start.26 = (bf16[160,768]{1,0:T(8,128)(2,1)}, bf16[160,768]{1,0:T(8,128)(2,1)S(1)}, u32[]{:S(2)}, u32[]{:S(2)}) collective-permute-start(bf16[160,768]{1,0:T(8,128)(2,1)} %collective-permute-done.25), channel_id=1, source_target_pairs={{0,4},{4,0},{8,12},{12,8},{16,20},{20,16},{24,28},{28,24},{1,5},{5... | collective-permute-start | bytes 737288 | tf_op jit(solution)/shard_map/ppermute | solution.py:573
  155.2 7.7 %copy-start.15 = (bf16[160,768]{1,0:T(8,128)(2,1)}, bf16[160,768]{1,0:T(8,128)(2,1)S(1)}, u32[]{:S(2)}) copy-start(bf16[160,768]{1,0:T(8,128)(2,1)S(1)} %collective-permute-done.26.refs_5_.refs_15_) | copy-start | bytes 737284
  155.8 0.8 copy-start.16
  156.6 19.2 %all-to-all-start.1 = ((bf16[8,32,1024]{2,1,0:T(8,128)(2,1)}), bf16[8,32,1024]{2,1,0:T(8,128)(2,1)S(1)}, u32[]{:S(2)}, u32[]{:S(2)}) async-start(bf16[8,32,1024]{2,1,0:T(8,128)(2,1)} %copy-done.16), calls=%async_computation.1 | async-start | bytes 1048576 | tf_op jit(solution)/shard_map/all_to_all | solution.py:581
  170.7 4.3 %collective-permute-start.29 = (f32[128,8]{1,0:T(8,128)S(1)}, f32[128,8]{1,0:T(8,128)S(1)}, u32[]{:S(2)}, u32[]{:S(2)}) collective-permute-start(f32[128,8]{1,0:T(8,128)S(1)} %get-tuple-element.104), channel_id=1, source_target_pairs={{0,2},{2,0},{1,3},{3,1},{4,6},{6,4},{5,7},{7,5},{8,10},{10,8},{9,1... | collective-permute-start | bytes 12296 | tf_op jit(solution)/shard_map/ppermute | solution.py:567
  180.2 1.5 collective-permute-start.30

commit v17 on v15

--- a/solution.py
+++ b/solution.py
@@ -623,9 +623,9 @@
     low_grad, first_own = collect_call(order, places, lows, grads, feats)
     firsts = [x.reshape(groups * rank, units) for x in (first_own, swap(first_own))]
     low_grad = exchange(low_grad)
-    order.wait([back[batches[-2][0]], back[1], back[2]] + [back[4]] * (groups == 8))
+    order.wait([back[batches[-2][0]]] + [back[4]] * (groups == 8))
     total(last)
-    order.wait([low_grad])
+    order.wait([low_grad, back[1], back[2]])
     low_hid = all_shares(lowrank_hid_call(order, index, hid, firsts, groups))
     order.wait([back[batches[-2][1]]])
 

time: 177 us -> 175 us (0.989)
  starting transfers between devices: 47.5 us -> 42.3 us
  waiting for transfers between devices: 53.9 us -> 58.4 us
    all_to_all x2, starting transfers between devices: 21 us -> 11.7 us  [exchange(): return lax.all_to_all(x, axes, split_axis=0, concat_axis=0, tiled=True)]
    ppermute x18, waiting for transfers between devices: 36.3 us -> 41.6 us  [flip(): return lax.ppermute(x, 'ep', [(i, i ^ mask) for i in range(groups)])]
    ppermute x18, starting transfers between devices: 19.4 us -> 22.6 us  [flip(): return lax.ppermute(x, 'ep', [(i, i ^ mask) for i in range(groups)])]
  transfers between devices with their start and end apart: 32 -> 32, of which waited for: 18 -> 16; matrix products, arithmetic and copies ran while one was open for 1% -> 1% of each run, Pallas kernels for 35% -> 35%
where the time goes in v17:
time: 175 us; the launch traced here: 172 us
  Pallas kernels  65.9 us (38%)
  waiting for transfers between devices  58.4 us (33%)
  starting transfers between devices  42.3 us (24%)
  local copies, waits for them, and re-layouts  3.95 us (2%)
    pallas_call x18, Pallas kernels, call(): pl.pallas_call(ordered, grid=grid, in_specs=[SMEM, *in_specs] + [ANY] * l...  65.9 us
    ppermute x18, waiting for transfers between devices, flip(): return lax.ppermute(x, 'ep', [(i, i ^ mask) for i in range(groups)])  41.6 us
    ppermute x18, starting transfers between devices, flip(): return lax.ppermute(x, 'ep', [(i, i ^ mask) for i in range(groups)])  22.6 us
    ppermute x7, waiting for transfers between devices, turn(): lax.ppermute(x, 'rep', [(r, (r + offset) % shares) for r in range(shares)])  13.2 us
    all_to_all x2, starting transfers between devices, exchange(): return lax.all_to_all(x, axes, split_axis=0, concat_axis=0, tiled=True)  11.7 us
    ppermute x7, starting transfers between devices, turn(): lax.ppermute(x, 'rep', [(r, (r + offset) % shares) for r in range(shares)])  7.89 us
    unnamed x53, local copies, waits for them, and re-layouts  3.95 us
  transfers between devices with their start and end apart: 32, of which 16 were waited for; matrix products, arithmetic and copies ran while one was open for 1% of the time, Pallas kernels for 35%

profile of v17, /device:TPU:8, one launch (start us, length us, event | category | flops | bytes accessed | tf_op | source)
XLA Modules:
  0.0 172.4 jit_solution(16177424598733861278)
XLA Ops:
  0.8 0.8 copy-done.19
  1.6 0.7 copy-done.20
  2.3 1.1 pack_block.1
  3.4 1.6 collective-permute-start
  5.0 2.6 %collective-permute-start.4 = (bf16[128,2304]{1,0:T(8,128)(2,1)S(1)}, bf16[128,2304]{1,0:T(8,128)(2,1)S(1)}, u32[]{:S(2)}, u32[]{:S(2)}) collective-permute-start(bf16[128,2304]{1,0:T(8,128)(2,1)S(1)} %get-tuple-element.57.refs_1_.refs_5_.refs_2_), channel_id=1, source_target_pairs={{0,16},{4,20},{8,24},{12,28},{16,0},{20,4},{24,8},{28,12},{1,17},{... | collective-permute-start | bytes 1769480 | tf_op jit(solution)/shard_map/ppermute | solution.py:558
  7.6 0.4 collective-permute-start.3
  8.0 3.4 %load_matrix.1 = (bf16[1536,2048]{1,0:T(8,128)(2,1)S(1)}, f32[8,128]{1,0:T(8,128)}) custom-call(s32[3]{0:T(128)S(1)} %pad_add_fusion.refs_0_, bf16[1536,2048]{1,0:T(8,128)(2,1)} %bitcast.33, f32[8,128]{1,0:T(8,128)} %get-tuple-element.58.refs_2_), custom_call_target="tpu_custom_call" | custom-call | flops 1 | bytes 1 | tf_op jit(solution)/shard_map/load_matrix/pallas_call | solution.py:53
  11.5 7.7 %collective-permute-done.refs_2_.refs_6_.refs_3_ = bf16[128,2304]{1,0:T(8,128)(2,1)S(1)} collective-permute-done((bf16[128,2304]{1,0:T(8,128)(2,1)S(1)}, bf16[128,2304]{1,0:T(8,128)(2,1)S(1)}, u32[]{:S(2)}, u32[]{:S(2)}) %collective-permute-start) | collective-permute-done | bytes 589856 | tf_op jit(solution)/shard_map/ppermute | solution.py:558
  19.2 8.2 %expert_rows.4 = (bf16[320,768]{1,0:T(8,128)(2,1)S(1)}, bf16[320,768]{1,0:T(8,128)(2,1)S(1)}, bf16[2,64,128]{2,1,0:T(8,128)(2,1)S(1)}, f32[8,128]{1,0:T(8,128)}) custom-call(s32[3]{0:T(128)S(1)} %pad_add_fusion.refs_0_, bf16[128,2304]{1,0:T(8,128)(2,1)S(1)} %get-tuple-element.57.refs_1_.refs_5_.refs_2_, ...), custom_call_target="tpu_custom_call" | custom-call | flops 1 | bytes 1 | tf_op jit(solution)/shard_map/expert_rows/pallas_call | solution.py:53
  27.5 5.6 %collective-permute-done.4.refs_1_ = bf16[128,2304]{1,0:T(8,128)(2,1)S(1)} collective-permute-done((bf16[128,2304]{1,0:T(8,128)(2,1)S(1)}, bf16[128,2304]{1,0:T(8,128)(2,1)S(1)}, u32[]{:S(2)}, u32[]{:S(2)}) %collective-permute-start.4) | collective-permute-done | bytes 589856 | tf_op jit(solution)/shard_map/ppermute | solution.py:558
  33.1 0.5 gate.1
  33.6 1.5 collective-permute-start.5
  35.1 0.5 collective-permute-start.6
  35.6 1.6 collective-permute-start.9
  37.2 1.5 collective-permute-start.8
  38.7 8.0 %expert_rows.5 = (bf16[320,768]{1,0:T(8,128)(2,1)S(1)}, bf16[320,768]{1,0:T(8,128)(2,1)S(1)}, bf16[2,64,128]{2,1,0:T(8,128)(2,1)S(1)}, f32[8,128]{1,0:T(8,128)}) custom-call(s32[3]{0:T(128)S(1)} %pad_add_fusion.refs_0_, bf16[128,2304]{1,0:T(8,128)(2,1)S(1)} %collective-permute-done.3.refs_1_.refs_7_.refs_4_, ...), custom_call_target="tpu_custom_call" | custom-call | flops 1 | bytes 1 | tf_op jit(solution)/shard_map/expert_rows/pallas_call | solution.py:53
  46.7 0.6 collective-permute-start.7
  47.3 1.7 collective-permute-done.5.refs_1_.refs_9_.refs_6_
  49.0 0.5 collective-permute-start.10
  49.5 1.9 %collective-permute-done.6.refs_4_.refs_2_.refs_10_.refs_7_ = bf16[128,2304]{1,0:T(8,128)(2,1)S(1)} collective-permute-done((bf16[128,2304]{1,0:T(8,128)(2,1)S(1)}, bf16[128,2304]{1,0:T(8,128)(2,1)S(1)}, u32[]{:S(2)}, u32[]{:S(2)}) %collective-permute-start.6) | collective-permute-done | bytes 589856 | tf_op jit(solution)/shard_map/ppermute | solution.py:558
  51.4 1.3 share_sum.4
  52.7 6.6 %collective-permute-done.7.refs_2_ = bf16[320,768]{1,0:T(8,128)(2,1)S(1)} collective-permute-done((bf16[320,768]{1,0:T(8,128)(2,1)S(1)}, bf16[320,768]{1,0:T(8,128)(2,1)S(1)}, u32[]{:S(2)}, u32[]{:S(2)}) %collective-permute-start.7) | collective-permute-done | bytes 491552 | tf_op jit(solution)/shard_map/ppermute | solution.py:552
  59.3 1.3 share_sum.5
  60.6 3.4 %collective-permute-done.9.refs_8_.refs_1_.refs_11_ = bf16[128,2304]{1,0:T(8,128)(2,1)S(1)} collective-permute-done((bf16[128,2304]{1,0:T(8,128)(2,1)S(1)}, bf16[128,2304]{1,0:T(8,128)(2,1)S(1)}, u32[]{:S(2)}, u32[]{:S(2)}) %collective-permute-start.9) | collective-permute-done | bytes 589856 | tf_op jit(solution)/shard_map/ppermute | solution.py:558
  64.1 8.4 %expert_rows.6 = (bf16[320,768]{1,0:T(8,128)(2,1)S(1)}, bf16[320,768]{1,0:T(8,128)(2,1)S(1)}, bf16[2,64,128]{2,1,0:T(8,128)(2,1)S(1)}, f32[8,128]{1,0:T(8,128)}) custom-call(s32[3]{0:T(128)S(1)} %pad_add_fusion.refs_0_, bf16[128,2304]{1,0:T(8,128)(2,1)S(1)} %collective-permute-done.5.refs_1_.refs_9_.refs_6_, ...), custom_call_target="tpu_custom_call" | custom-call | flops 1 | bytes 1 | tf_op jit(solution)/shard_map/expert_rows/pallas_call | solution.py:53
  72.4 1.6 collective-permute-start.11
  74.0 0.5 collective-permute-start.16
  74.7 8.2 %expert_rows.7 = (bf16[320,768]{1,0:T(8,128)(2,1)S(1)}, bf16[320,768]{1,0:T(8,128)(2,1)S(1)}, bf16[2,64,128]{2,1,0:T(8,128)(2,1)S(1)}, f32[8,128]{1,0:T(8,128)}) custom-call(s32[3]{0:T(128)S(1)} %pad_add_fusion.refs_0_, bf16[128,2304]{1,0:T(8,128)(2,1)S(1)} %collective-permute-done.9.refs_8_.refs_1_.refs_11_, ...), custom_call_target="tpu_custom_call" | custom-call | flops 1 | bytes 1 | tf_op jit(solution)/shard_map/expert_rows/pallas_call | solution.py:53
  82.9 1.6 collective-permute-start.14
  84.5 3.2 %collective-permute-start.17 = (bf16[160,768]{1,0:T(8,128)(2,1)S(1)}, bf16[160,768]{1,0:T(8,128)(2,1)S(1)}, u32[]{:S(2)}, u32[]{:S(2)}) collective-permute-start(bf16[160,768]{1,0:T(8,128)(2,1)S(1)} %collective-permute-done.16), channel_id=1, source_target_pairs={{0,24},{4,28},{8,16},{12,20},{16,8},{20,12},{24,0},{28,4},{1,25},{... | collective-permute-start | bytes 737288 | tf_op jit(solution)/shard_map/ppermute | solution.py:558
  87.7 1.3 share_sum.6
  89.0 1.8 %collect_blocks.1 = (bf16[8,64,128]{2,1,0:T(8,128)(2,1)}, bf16[8,32,768]{2,1,0:T(8,128)(2,1)S(1)}, f32[8,128]{1,0:T(8,128)}) custom-call(s32[3]{0:T(128)S(1)} %pad_add_fusion.refs_0_, bf16[2,64,128]{2,1,0:T(8,128)(2,1)S(1)} %get-tuple-element.61.refs_1_, bf16[2,64,128]{2,1,0:T(8,128)(2,1)S(1)} %get-tuple-element.65.refs_2_, ...), custom_call_target="tpu_custom_call" | custom-call | flops 1 | bytes 1 | tf_op jit(solution)/shard_map/collect_blocks/pallas_call | solution.py:53
  90.8 1.9 %collective-permute-start.19 = (bf16[160,768]{1,0:T(8,128)(2,1)}, bf16[160,768]{1,0:T(8,128)(2,1)S(1)}, u32[]{:S(2)}, u32[]{:S(2)}) collective-permute-start(bf16[160,768]{1,0:T(8,128)(2,1)} %get-tuple-element.89), channel_id=1, source_target_pairs={{0,8},{4,12},{8,0},{12,4},{16,24},{20,28},{24,16},{28,20},{1,9},{5... | collective-permute-start | bytes 737288 | tf_op jit(solution)/shard_map/ppermute | solution.py:558
  92.7 10.7 %collective-permute-done.17.refs_5_.refs_12_ = bf16[160,768]{1,0:T(8,128)(2,1)S(1)} collective-permute-done((bf16[160,768]{1,0:T(8,128)(2,1)S(1)}, bf16[160,768]{1,0:T(8,128)(2,1)S(1)}, u32[]{:S(2)}, u32[]{:S(2)}) %collective-permute-start.17) | collective-permute-done | bytes 245792 | tf_op jit(solution)/shard_map/ppermute | solution.py:558
  103.4 0.5 collective-permute-start.18
  103.9 6.2 %all-to-all-start = ((bf16[8,64,128]{2,1,0:T(8,128)(2,1)}), bf16[8,64,128]{2,1,0:T(8,128)(2,1)S(1)}, u32[]{:S(2)}, u32[]{:S(2)}) async-start(bf16[8,64,128]{2,1,0:T(8,128)(2,1)} %get-tuple-element.80), calls=%async_computation | async-start | bytes 262144 | tf_op jit(solution)/shard_map/all_to_all | solution.py:566
  110.2 0.7 share_sum.7
  110.9 0.7 copy-done.23
  111.5 2.9 %collective-permute-start.22 = (bf16[160,768]{1,0:T(8,128)(2,1)S(1)}, bf16[160,768]{1,0:T(8,128)(2,1)}, u32[]{:S(2)}, u32[]{:S(2)}) collective-permute-start(bf16[160,768]{1,0:T(8,128)(2,1)S(1)} %get-tuple-element.94), channel_id=1, source_target_pairs={{0,16},{4,20},{8,24},{12,28},{16,0},{20,4},{24,8},{28,12},{1,17},{... | collective-permute-start | bytes 737288 | tf_op jit(solution)/shard_map/ppermute | solution.py:558
  114.6 1.8 %all-to-all-done.refs_6_.refs_1_ = bf16[8,64,128]{2,1,0:T(8,128)(2,1)S(1)} async-done(((bf16[8,64,128]{2,1,0:T(8,128)(2,1)}), bf16[8,64,128]{2,1,0:T(8,128)(2,1)S(1)}, u32[]{:S(2)}, u32[]{:S(2)}) %all-to-all-start) | async-done | bytes 131104 | tf_op jit(solution)/shard_map/all_to_all | solution.py:566
  116.4 3.6 %lowrank_hid.1 = (f32[128,512]{1,0:T(8,128)S(1)}, f32[8,128]{1,0:T(8,128)}) custom-call(s32[3]{0:T(128)S(1)} %pad_add_fusion.refs_0_, s32[128,8]{1,0:T(8,128)S(1)} %copy.17.refs_1_.refs_5_.refs_2_, bf16[1024,768]{1,0:T(8,128)(2,1)} %bitcast.29, bf16[256,768]{1,0:T(8,128)(2,1)S(1)} %bitcast.23, bf16[256,768]{1,0:T(8,128)(2,1)S(1)} %bitcast.25, ...), custom_call_target="tpu_custom_call" | custom-call | flops 1 | bytes 1 | tf_op jit(solution)/shard_map/lowrank_hid/pallas_call | solution.py:53
  120.0 0.6 collective-permute-start.26
  120.6 1.4 collective-permute-start.21
  122.0 1.2 collective-permute-done.22
  123.2 1.5 collective-permute-start.23
  124.7 0.5 collective-permute-start.12
  125.2 0.5 collective-permute-start.24
  125.9 3.8 %collective-permute-done.12.refs_2_ = bf16[8,64,128]{2,1,0:T(8,128)(2,1)S(1)} collective-permute-done((bf16[8,64,128]{2,1,0:T(8,128)(2,1)S(1)}, bf16[8,64,128]{2,1,0:T(8,128)(2,1)S(1)}, u32[]{:S(2)}, u32[]{:S(2)}) %collective-permute-start.12) | collective-permute-done | bytes 131104 | tf_op jit(solution)/shard_map/ppermute | solution.py:552
  129.7 0.7 low_dense.1
  130.4 1.9 %collective-permute-done.23.refs_10_.refs_13_ = bf16[160,768]{1,0:T(8,128)(2,1)S(1)} collective-permute-done((bf16[160,768]{1,0:T(8,128)(2,1)}, bf16[160,768]{1,0:T(8,128)(2,1)S(1)}, u32[]{:S(2)}, u32[]{:S(2)}) %collective-permute-start.23) | collective-permute-done | bytes 245792 | tf_op jit(solution)/shard_map/ppermute | solution.py:558
  132.3 4.7 %first_grad.1 = (f32[8,32,768]{2,1,0:T(8,128)S(1)}, bf16[8,32,768]{2,1,0:T(8,128)(2,1)S(1)}, bf16[8,32,256]{2,1,0:T(8,128)(2,1)S(1)}, f32[8,128]{1,0:T(8,128)}) custom-call(s32[3]{0:T(128)S(1)} %pad_add_fusion.refs_0_, s32[128,8]{1,0:T(8,128)S(1)} %copy.17.refs_1_.refs_5_.refs_2_, bf16[128,8]{1,0:T(8,128)(2,1)S(1)} %copy.19.refs_2_.refs_6_.refs_3_, ...), custom_call_target="tpu_custom_call" | custom-call | flops 1 | bytes 1 | tf_op jit(solution)/shard_map/first_grad/pallas_call | solution.py:53
  137.1 1.5 collective-permute-start.25
  138.5 7.1 %collective-permute-done.25.refs_5_.refs_15_ = bf16[160,768]{1,0:T(8,128)(2,1)S(1)} collective-permute-done((bf16[160,768]{1,0:T(8,128)(2,1)}, bf16[160,768]{1,0:T(8,128)(2,1)S(1)}, u32[]{:S(2)}, u32[]{:S(2)}) %collective-permute-start.25) | collective-permute-done | bytes 245792 | tf_op jit(solution)/shard_map/ppermute | solution.py:558
  145.7 0.6 first_sum.1
  146.3 0.8 copy-done.17
  147.1 5.5 %all-to-all-start.1 = ((bf16[8,32,1024]{2,1,0:T(8,128)(2,1)}), bf16[8,32,1024]{2,1,0:T(8,128)(2,1)S(1)}, u32[]{:S(2)}, u32[]{:S(2)}) async-start(bf16[8,32,1024]{2,1,0:T(8,128)(2,1)} %copy-done.17), calls=%async_computation.1 | async-start | bytes 1048576 | tf_op jit(solution)/shard_map/all_to_all | solution.py:566
  152.7 7.9 %finish.1 = (bf16[1024,768]{1,0:T(8,128)(2,1)}, f32[128,8]{1,0:T(8,128)S(1)}, f32[8,128]{1,0:T(8,128)}) custom-call(s32[3]{0:T(128)S(1)} %pad_add_fusion.refs_0_, s32[128,8]{1,0:T(8,128)S(1)} %copy.17.refs_1_.refs_5_.refs_2_, s32[128,8]{1,0:T(8,128)S(1)} %copy.17.refs_1_.refs_5_.refs_2_, bf16[128,8]{1,0:T(8,128)(2,1)S(1)} %copy.19.refs_2_.refs_6_.refs_3_, ...), custom_call_target="tpu_custom_call" | custom-call | flops 1 | bytes 20000000 | tf_op jit(solution)/shard_map/finish/pallas_call | solution.py:53
  160.5 1.5 collective-permute-start.28
  162.0 2.8 %collective-permute-done.28.refs_11_ = f32[128,8]{1,0:T(8,128)S(1)} collective-permute-done((f32[128,8]{1,0:T(8,128)S(1)}, f32[128,8]{1,0:T(8,128)S(1)}, u32[]{:S(2)}, u32[]{:S(2)}) %collective-permute-start.28) | collective-permute-done | bytes 4128 | tf_op jit(solution)/shard_map/ppermute | solution.py:552
  164.8 1.0 all-to-all-done.1.refs_1_
  165.8 4.4 %second_grad.1 = (f32[32,2048]{1,0:T(8,128)S(1)}, f32[32,2048]{1,0:T(8,128)S(1)}, f32[32,768]{1,0:T(8,128)}, f32[8,128]{1,0:T(8,128)}) custom-call(s32[3]{0:T(128)S(1)} %pad_add_fusion.refs_0_, bf16[8,32,1024]{2,1,0:T(8,128)(2,1)S(1)} %all-to-all-done.1.refs_1_, bf16[128,2304]{1,0:T(8,128)(2,1)} %copy-done.3, bf16[128,2304]{1,0:T(8,128)(2,1)} %copy-done.4, ...), custom_call_target="tpu_custom_call" | custom-call | flops 1 | bytes 1 | tf_op jit(solution)/shard_map/second_grad/pallas_call | solution.py:53
  170.2 0.7 copy.20
  170.8 0.8 collective-permute-done.29
  171.7 0.7 add_bitcast_fusion
  (74 shorter events, 0.9 us)
Async XLA Ops:
  0.6 18.6 %copy-start.8 = (bf16[1,32,2048]{2,1,0:T(8,128)(2,1)S(1)}, bf16[1,32,2048]{2,1,0:T(8,128)(2,1)}, u32[]{:S(2)}) copy-start(bf16[1,32,2048]{2,1,0:T(8,128)(2,1)} %param.13) | copy-start | bytes 393220
  0.6 18.6 %collective-permute-start.2 = (bf16[1536,2048]{1,0:T(8,128)(2,1)}, bf16[1536,2048]{1,0:T(8,128)(2,1)}, u32[]{:S(2)}, u32[]{:S(2)}) collective-permute-start(bf16[1536,2048]{1,0:T(8,128)(2,1)} %bitcast.32), channel_id=1, source_target_pairs={{0,1},{1,0},{2,3},{3,2},{4,5},{5,4},{6,7},{7,6},{8,9},{9,8},{10,11... | collective-permute-start | bytes 18874376 | tf_op jit(solution)/shard_map/ppermute | solution.py:561
  0.8 0.8 copy-start.19
  1.6 0.7 copy-start.20
  3.4 24.0 %copy-start.3 = (bf16[128,2304]{1,0:T(8,128)(2,1)}, bf16[128,2304]{1,0:T(8,128)(2,1)S(1)}, u32[]{:S(2)}) copy-start(bf16[128,2304]{1,0:T(8,128)(2,1)S(1)} %get-tuple-element.57.refs_1_.refs_5_.refs_2_) | copy-start | bytes 1769476
  3.4 15.8 %collective-permute-start = (bf16[128,2304]{1,0:T(8,128)(2,1)S(1)}, bf16[128,2304]{1,0:T(8,128)(2,1)S(1)}, u32[]{:S(2)}, u32[]{:S(2)}) collective-permute-start(bf16[128,2304]{1,0:T(8,128)(2,1)S(1)} %get-tuple-element.57.refs_1_.refs_5_.refs_2_), channel_id=1, source_target_pairs={{0,4},{4,0},{8,12},{12,8},{16,20},{20,16},{24,28},{28,24},{1,5},{5... | collective-permute-start | bytes 1769480 | tf_op jit(solution)/shard_map/ppermute | solution.py:558
  5.0 28.1 %collective-permute-start.4 = (bf16[128,2304]{1,0:T(8,128)(2,1)S(1)}, bf16[128,2304]{1,0:T(8,128)(2,1)S(1)}, u32[]{:S(2)}, u32[]{:S(2)}) collective-permute-start(bf16[128,2304]{1,0:T(8,128)(2,1)S(1)} %get-tuple-element.57.refs_1_.refs_5_.refs_2_), channel_id=1, source_target_pairs={{0,16},{4,20},{8,24},{12,28},{16,0},{20,4},{24,8},{28,12},{1,17},{... | collective-permute-start | bytes 1769480 | tf_op jit(solution)/shard_map/ppermute | solution.py:558
  7.6 27.6 %collective-permute-start.3 = (bf16[128,2304]{1,0:T(8,128)(2,1)S(1)}, bf16[128,2304]{1,0:T(8,128)(2,1)S(1)}, u32[]{:S(2)}, u32[]{:S(2)}) collective-permute-start(bf16[128,2304]{1,0:T(8,128)(2,1)S(1)} %get-tuple-element.57.refs_1_.refs_5_.refs_2_), channel_id=1, source_target_pairs={{0,8},{4,12},{8,0},{12,4},{16,24},{20,28},{24,16},{28,20},{1,9},{5... | collective-permute-start | bytes 1769480 | tf_op jit(solution)/shard_map/ppermute | solution.py:558
  8.0 3.4 %collective-permute-start.1 = (bf16[32,2048]{1,0:T(8,128)(2,1)}, bf16[32,2048]{1,0:T(8,128)(2,1)S(1)}, u32[]{:S(2)}, u32[]{:S(2)}) collective-permute-start(bf16[32,2048]{1,0:T(8,128)(2,1)} %bitcast.18), channel_id=1, source_target_pairs={{0,1},{1,0},{2,3},{3,2},{4,5},{5,4},{6,7},{7,6},{8,9},{9,8},{10,11... | collective-permute-start | bytes 393224 | tf_op jit(solution)/shard_map/ppermute | solution.py:561
  19.2 8.3 %copy-start.4 = (bf16[128,2304]{1,0:T(8,128)(2,1)}, bf16[128,2304]{1,0:T(8,128)(2,1)S(1)}, u32[]{:S(2)}) copy-start(bf16[128,2304]{1,0:T(8,128)(2,1)S(1)} %collective-permute-done.refs_2_.refs_6_.refs_3_) | copy-start | bytes 1769476
  19.2 19.5 %copy-start.9 = (bf16[1,32,2048]{2,1,0:T(8,128)(2,1)S(1)}, bf16[1,32,2048]{2,1,0:T(8,128)(2,1)}, u32[]{:S(2)}) copy-start(bf16[1,32,2048]{2,1,0:T(8,128)(2,1)} %param.13) | copy-start | bytes 393220
  33.6 13.0 %copy-start.2 = (bf16[128,2304]{1,0:T(8,128)(2,1)}, bf16[128,2304]{1,0:T(8,128)(2,1)S(1)}, u32[]{:S(2)}) copy-start(bf16[128,2304]{1,0:T(8,128)(2,1)S(1)} %get-tuple-element.63.refs_2_.refs_8_.refs_5_) | copy-start | bytes 1769476
  33.6 15.3 %collective-permute-start.5 = (bf16[128,2304]{1,0:T(8,128)(2,1)S(1)}, bf16[128,2304]{1,0:T(8,128)(2,1)S(1)}, u32[]{:S(2)}, u32[]{:S(2)}) collective-permute-start(bf16[128,2304]{1,0:T(8,128)(2,1)S(1)} %get-tuple-element.63.refs_2_.refs_8_.refs_5_), channel_id=1, source_target_pairs={{0,8},{4,12},{8,0},{12,4},{16,24},{20,28},{24,16},{28,20},{1,9},{5... | collective-permute-start | bytes 1769480 | tf_op jit(solution)/shard_map/ppermute | solution.py:558
  35.1 11.5 %copy-start.5 = (bf16[128,2304]{1,0:T(8,128)(2,1)}, bf16[128,2304]{1,0:T(8,128)(2,1)S(1)}, u32[]{:S(2)}) copy-start(bf16[128,2304]{1,0:T(8,128)(2,1)S(1)} %collective-permute-done.3.refs_1_.refs_7_.refs_4_) | copy-start | bytes 1769476
  35.1 16.3 %collective-permute-start.6 = (bf16[128,2304]{1,0:T(8,128)(2,1)S(1)}, bf16[128,2304]{1,0:T(8,128)(2,1)S(1)}, u32[]{:S(2)}, u32[]{:S(2)}) collective-permute-start(bf16[128,2304]{1,0:T(8,128)(2,1)S(1)} %collective-permute-done.3.refs_1_.refs_7_.refs_4_), channel_id=1, source_target_pairs={{0,4},{4,0},{8,12},{12,8},{16,20},{20,16},{24,28},{28,24},{1,5},{5... | collective-permute-start | bytes 1769480 | tf_op jit(solution)/shard_map/ppermute | solution.py:558
  35.6 28.4 %collective-permute-start.9 = (bf16[128,2304]{1,0:T(8,128)(2,1)S(1)}, bf16[128,2304]{1,0:T(8,128)(2,1)S(1)}, u32[]{:S(2)}, u32[]{:S(2)}) collective-permute-start(bf16[128,2304]{1,0:T(8,128)(2,1)S(1)} %get-tuple-element.63.refs_2_.refs_8_.refs_5_), channel_id=1, source_target_pairs={{0,4},{4,0},{8,12},{12,8},{16,20},{20,16},{24,28},{28,24},{1,5},{5... | collective-permute-start | bytes 1769480 | tf_op jit(solution)/shard_map/ppermute | solution.py:558
  37.2 14.2 %collective-permute-start.8 = (bf16[320,768]{1,0:T(8,128)(2,1)S(1)}, bf16[320,768]{1,0:T(8,128)(2,1)S(1)}, u32[]{:S(2)}, u32[]{:S(2)}) collective-permute-start(bf16[320,768]{1,0:T(8,128)(2,1)S(1)} %get-tuple-element.69), channel_id=1, source_target_pairs={{0,2},{2,0},{1,3},{3,1},{4,6},{6,4},{5,7},{7,5},{8,10},{10,8},{9,1... | collective-permute-start | bytes 1474568 | tf_op jit(solution)/shard_map/ppermute | solution.py:552
  46.7 12.6 %collective-permute-start.7 = (bf16[320,768]{1,0:T(8,128)(2,1)S(1)}, bf16[320,768]{1,0:T(8,128)(2,1)S(1)}, u32[]{:S(2)}, u32[]{:S(2)}) collective-permute-start(bf16[320,768]{1,0:T(8,128)(2,1)S(1)} %get-tuple-element.67), channel_id=1, source_target_pairs={{0,2},{2,0},{1,3},{3,1},{4,6},{6,4},{5,7},{7,5},{8,10},{10,8},{9,1... | collective-permute-start | bytes 1474568 | tf_op jit(solution)/shard_map/ppermute | solution.py:552
  49.0 23.5 %copy-start.6 = (bf16[128,2304]{1,0:T(8,128)(2,1)}, bf16[128,2304]{1,0:T(8,128)(2,1)S(1)}, u32[]{:S(2)}) copy-start(bf16[128,2304]{1,0:T(8,128)(2,1)S(1)} %collective-permute-done.5.refs_1_.refs_9_.refs_6_) | copy-start | bytes 1769476
  49.0 25.7 %collective-permute-start.10 = (bf16[128,2304]{1,0:T(8,128)(2,1)S(1)}, bf16[128,2304]{1,0:T(8,128)(2,1)S(1)}, u32[]{:S(2)}, u32[]{:S(2)}) collective-permute-start(bf16[128,2304]{1,0:T(8,128)(2,1)S(1)} %collective-permute-done.5.refs_1_.refs_9_.refs_6_), channel_id=1, source_target_pairs={{0,4},{4,0},{8,12},{12,8},{16,20},{20,16},{24,28},{28,24},{1,5},{5... | collective-permute-start | bytes 1769480 | tf_op jit(solution)/shard_map/ppermute | solution.py:558
  51.4 21.0 %copy-start.1 = (bf16[128,2304]{1,0:T(8,128)(2,1)}, bf16[128,2304]{1,0:T(8,128)(2,1)S(1)}, u32[]{:S(2)}) copy-start(bf16[128,2304]{1,0:T(8,128)(2,1)S(1)} %collective-permute-done.6.refs_4_.refs_2_.refs_10_.refs_7_) | copy-start | bytes 1769476
  52.7 11.3 %copy-start.18 = (bf16[160,768]{1,0:T(8,128)(2,1)}, bf16[160,768]{1,0:T(8,128)(2,1)S(1)}, u32[]{:S(2)}) copy-start(bf16[160,768]{1,0:T(8,128)(2,1)S(1)} %get-tuple-element.93.refs_8_) | copy-start | bytes 737284
  64.1 10.7 %copy-start = (bf16[128,2304]{1,0:T(8,128)(2,1)}, bf16[128,2304]{1,0:T(8,128)(2,1)S(1)}, u32[]{:S(2)}) copy-start(bf16[128,2304]{1,0:T(8,128)(2,1)S(1)} %collective-permute-done.9.refs_8_.refs_1_.refs_11_) | copy-start | bytes 1769476
  72.4 15.3 %collective-permute-start.11 = (bf16[320,768]{1,0:T(8,128)(2,1)S(1)}, bf16[320,768]{1,0:T(8,128)(2,1)S(1)}, u32[]{:S(2)}, u32[]{:S(2)}) collective-permute-start(bf16[320,768]{1,0:T(8,128)(2,1)S(1)} %get-tuple-element.77), channel_id=1, source_target_pairs={{0,2},{2,0},{1,3},{3,1},{4,6},{6,4},{5,7},{7,5},{8,10},{10,8},{9,1... | collective-permute-start | bytes 1474568 | tf_op jit(solution)/shard_map/ppermute | solution.py:552
  74.0 10.5 %collective-permute-start.16 = (bf16[160,768]{1,0:T(8,128)(2,1)S(1)}, bf16[160,768]{1,0:T(8,128)(2,1)S(1)}, u32[]{:S(2)}, u32[]{:S(2)}) collective-permute-start(bf16[160,768]{1,0:T(8,128)(2,1)S(1)} %get-tuple-element.86), channel_id=1, source_target_pairs={{0,8},{4,12},{8,0},{12,4},{16,24},{20,28},{24,16},{28,20},{1,9},{5... | collective-permute-start | bytes 737288 | tf_op jit(solution)/shard_map/ppermute | solution.py:558
  74.7 8.2 %copy-start.7 = (bf16[128,2304]{1,0:T(8,128)(2,1)}, bf16[128,2304]{1,0:T(8,128)(2,1)S(1)}, u32[]{:S(2)}) copy-start(bf16[128,2304]{1,0:T(8,128)(2,1)S(1)} %collective-permute-done.10.refs_2_.refs_12_.refs_9_) | copy-start | bytes 1769476
  82.9 31.5 %copy-start.21 = (s32[128,8]{0,1:T(8,128)S(1)}, s32[128,8]{0,1:T(8,128)}, u32[]{:S(2)}) copy-start(s32[128,8]{0,1:T(8,128)} %param.9) | copy-start | bytes 12292
  82.9 42.8 %copy-start.24 = (bf16[128,8]{0,1:T(8,128)(2,1)S(1)}, bf16[128,8]{0,1:T(8,128)(2,1)}, u32[]{:S(2)}) copy-start(bf16[128,8]{0,1:T(8,128)(2,1)} %param.10) | copy-start | bytes 6148
  82.9 27.2 %collective-permute-start.14 = (bf16[320,768]{1,0:T(8,128)(2,1)S(1)}, bf16[320,768]{1,0:T(8,128)(2,1)S(1)}, u32[]{:S(2)}, u32[]{:S(2)}) collective-permute-start(bf16[320,768]{1,0:T(8,128)(2,1)S(1)} %get-tuple-element.83), channel_id=1, source_target_pairs={{0,2},{2,0},{1,3},{3,1},{4,6},{6,4},{5,7},{7,5},{8,10},{10,8},{9,1... | collective-permute-start | bytes 1474568 | tf_op jit(solution)/shard_map/ppermute | solution.py:552
  84.5 18.9 %collective-permute-start.17 = (bf16[160,768]{1,0:T(8,128)(2,1)S(1)}, bf16[160,768]{1,0:T(8,128)(2,1)S(1)}, u32[]{:S(2)}, u32[]{:S(2)}) collective-permute-start(bf16[160,768]{1,0:T(8,128)(2,1)S(1)} %collective-permute-done.16), channel_id=1, source_target_pairs={{0,24},{4,28},{8,16},{12,20},{16,8},{20,12},{24,0},{28,4},{1,25},{... | collective-permute-start | bytes 737288 | tf_op jit(solution)/shard_map/ppermute | solution.py:558
  89.0 1.8 %copy-start.22 = (bf16[160,768]{1,0:T(8,128)(2,1)}, bf16[160,768]{1,0:T(8,128)(2,1)S(1)}, u32[]{:S(2)}) copy-start(bf16[160,768]{1,0:T(8,128)(2,1)S(1)} %get-tuple-element.91) | copy-start | bytes 737284
  89.0 21.1 %collective-permute-start.15 = (bf16[160,768]{1,0:T(8,128)(2,1)}, bf16[160,768]{1,0:T(8,128)(2,1)S(1)}, u32[]{:S(2)}, u32[]{:S(2)}) collective-permute-start(bf16[160,768]{1,0:T(8,128)(2,1)} %get-tuple-element.85), channel_id=1, source_target_pairs={{0,24},{4,28},{8,16},{12,20},{16,8},{20,12},{24,0},{28,4},{1,25},{... | collective-permute-start | bytes 737288 | tf_op jit(solution)/shard_map/ppermute | solution.py:558
  90.8 25.6 %collective-permute-start.13 = (bf16[8,32,768]{2,1,0:T(8,128)(2,1)S(1)}, bf16[8,32,768]{2,1,0:T(8,128)(2,1)S(1)}, u32[]{:S(2)}, u32[]{:S(2)}) collective-permute-start(bf16[8,32,768]{2,1,0:T(8,128)(2,1)S(1)} %get-tuple-element.81), channel_id=1, source_target_pairs={{0,1},{1,0},{2,3},{3,2},{4,5},{5,4},{6,7},{7,6},{8,9},{9,8},{10,11... | collective-permute-start | bytes 1179656 | tf_op jit(solution)/shard_map/ppermute | solution.py:561
  90.8 23.7 %collective-permute-start.19 = (bf16[160,768]{1,0:T(8,128)(2,1)}, bf16[160,768]{1,0:T(8,128)(2,1)S(1)}, u32[]{:S(2)}, u32[]{:S(2)}) collective-permute-start(bf16[160,768]{1,0:T(8,128)(2,1)} %get-tuple-element.89), channel_id=1, source_target_pairs={{0,8},{4,12},{8,0},{12,4},{16,24},{20,28},{24,16},{28,20},{1,9},{5... | collective-permute-start | bytes 737288 | tf_op jit(solution)/shard_map/ppermute | solution.py:558
  103.4 49.2 %copy-start.11 = (bf16[160,768]{1,0:T(8,128)(2,1)}, bf16[160,768]{1,0:T(8,128)(2,1)S(1)}, u32[]{:S(2)}) copy-start(bf16[160,768]{1,0:T(8,128)(2,1)S(1)} %collective-permute-done.17.refs_5_.refs_12_) | copy-start | bytes 737284
  103.4 11.2 %collective-permute-start.18 = (bf16[160,768]{1,0:T(8,128)(2,1)}, bf16[160,768]{1,0:T(8,128)(2,1)S(1)}, u32[]{:S(2)}, u32[]{:S(2)}) collective-permute-start(bf16[160,768]{1,0:T(8,128)(2,1)} %get-tuple-element.88), channel_id=1, source_target_pairs={{0,4},{4,0},{8,12},{12,8},{16,20},{20,16},{24,28},{28,24},{1,5},{5... | collective-permute-start | bytes 737288 | tf_op jit(solution)/shard_map/ppermute | solution.py:558
  103.9 12.5 %all-to-all-start = ((bf16[8,64,128]{2,1,0:T(8,128)(2,1)}), bf16[8,64,128]{2,1,0:T(8,128)(2,1)S(1)}, u32[]{:S(2)}, u32[]{:S(2)}) async-start(bf16[8,64,128]{2,1,0:T(8,128)(2,1)} %get-tuple-element.80), calls=%async_computation | async-start | bytes 262144 | tf_op jit(solution)/shard_map/all_to_all | solution.py:566
  110.1 42.5 %copy-start.12 = (bf16[160,768]{1,0:T(8,128)(2,1)}, bf16[160,768]{1,0:T(8,128)(2,1)S(1)}, u32[]{:S(2)}) copy-start(bf16[160,768]{1,0:T(8,128)(2,1)S(1)} %collective-permute-done.15.refs_4_.refs_14_) | copy-start | bytes 737284
  110.1 10.5 %collective-permute-start.20 = (bf16[160,768]{1,0:T(8,128)(2,1)}, bf16[160,768]{1,0:T(8,128)(2,1)}, u32[]{:S(2)}, u32[]{:S(2)}) collective-permute-start(bf16[160,768]{1,0:T(8,128)(2,1)} %copy-done.22), channel_id=1, source_target_pairs={{0,8},{4,12},{8,0},{12,4},{16,24},{20,28},{24,16},{28,20},{1,9},{5... | collective-permute-start | bytes 737288 | tf_op jit(solution)/shard_map/ppermute | solution.py:558
  110.8 0.7 copy-start.23
  111.5 11.7 %collective-permute-start.22 = (bf16[160,768]{1,0:T(8,128)(2,1)S(1)}, bf16[160,768]{1,0:T(8,128)(2,1)}, u32[]{:S(2)}, u32[]{:S(2)}) collective-permute-start(bf16[160,768]{1,0:T(8,128)(2,1)S(1)} %get-tuple-element.94), channel_id=1, source_target_pairs={{0,16},{4,20},{8,24},{12,28},{16,0},{20,4},{24,8},{28,12},{1,17},{... | collective-permute-start | bytes 737288 | tf_op jit(solution)/shard_map/ppermute | solution.py:558
  114.5 38.1 %copy-start.13 = (bf16[160,768]{1,0:T(8,128)(2,1)}, bf16[160,768]{1,0:T(8,128)(2,1)S(1)}, u32[]{:S(2)}) copy-start(bf16[160,768]{1,0:T(8,128)(2,1)S(1)} %collective-permute-done.19.refs_8_.refs_10_) | copy-start | bytes 737284
  114.6 38.1 %copy-start.14 = (bf16[160,768]{1,0:T(8,128)(2,1)}, bf16[160,768]{1,0:T(8,128)(2,1)S(1)}, u32[]{:S(2)}) copy-start(bf16[160,768]{1,0:T(8,128)(2,1)S(1)} %collective-permute-done.18.refs_7_.refs_9_) | copy-start | bytes 737284
  120.0 10.4 %collective-permute-start.26 = (f32[128,512]{1,0:T(8,128)S(1)}, f32[128,512]{1,0:T(8,128)S(1)}, u32[]{:S(2)}, u32[]{:S(2)}) collective-permute-start(f32[128,512]{1,0:T(8,128)S(1)} %get-tuple-element.96.refs_7_), channel_id=1, source_target_pairs={{0,2},{2,0},{1,3},{3,1},{4,6},{6,4},{5,7},{7,5},{8,10},{10,8},{9,1... | collective-permute-start | bytes 786440 | tf_op jit(solution)/shard_map/ppermute | solution.py:552
  120.6 9.1 %collective-permute-start.21 = (bf16[160,768]{1,0:T(8,128)(2,1)}, bf16[160,768]{1,0:T(8,128)(2,1)S(1)}, u32[]{:S(2)}, u32[]{:S(2)}) collective-permute-start(bf16[160,768]{1,0:T(8,128)(2,1)} %collective-permute-done.20), channel_id=1, source_target_pairs={{0,4},{4,0},{8,12},{12,8},{16,20},{20,16},{24,28},{28,24},{1,5},{5... | collective-permute-start | bytes 737288 | tf_op jit(solution)/shard_map/ppermute | solution.py:558
  123.2 9.0 %collective-permute-start.23 = (bf16[160,768]{1,0:T(8,128)(2,1)}, bf16[160,768]{1,0:T(8,128)(2,1)S(1)}, u32[]{:S(2)}, u32[]{:S(2)}) collective-permute-start(bf16[160,768]{1,0:T(8,128)(2,1)} %collective-permute-done.22), channel_id=1, source_target_pairs={{0,4},{4,0},{8,12},{12,8},{16,20},{20,16},{24,28},{28,24},{1,5},{5... | collective-permute-start | bytes 737288 | tf_op jit(solution)/shard_map/ppermute | solution.py:558
  124.7 5.0 %collective-permute-start.12 = (bf16[8,64,128]{2,1,0:T(8,128)(2,1)S(1)}, bf16[8,64,128]{2,1,0:T(8,128)(2,1)S(1)}, u32[]{:S(2)}, u32[]{:S(2)}) collective-permute-start(bf16[8,64,128]{2,1,0:T(8,128)(2,1)S(1)} %all-to-all-done.refs_6_.refs_1_), channel_id=1, source_target_pairs={{0,2},{2,0},{1,3},{3,1},{4,6},{6,4},{5,7},{7,5},{8,10},{10,8},{9,1... | collective-permute-start | bytes 393224 | tf_op jit(solution)/shard_map/ppermute | solution.py:552
  125.2 11.8 %collective-permute-start.24 = (bf16[160,768]{1,0:T(8,128)(2,1)}, bf16[160,768]{1,0:T(8,128)(2,1)}, u32[]{:S(2)}, u32[]{:S(2)}) collective-permute-start(bf16[160,768]{1,0:T(8,128)(2,1)} %copy-done.23), channel_id=1, source_target_pairs={{0,24},{4,28},{8,16},{12,20},{16,8},{20,12},{24,0},{28,4},{1,25},{... | collective-permute-start | bytes 737288 | tf_op jit(solution)/shard_map/ppermute | solution.py:558
  129.7 23.0 %copy-start.10 = (bf16[160,768]{1,0:T(8,128)(2,1)}, bf16[160,768]{1,0:T(8,128)(2,1)S(1)}, u32[]{:S(2)}) copy-start(bf16[160,768]{1,0:T(8,128)(2,1)S(1)} %collective-permute-done.21.refs_4_.refs_11_) | copy-start | bytes 737284
  132.3 20.4 %copy-start.15 = (bf16[160,768]{1,0:T(8,128)(2,1)}, bf16[160,768]{1,0:T(8,128)(2,1)S(1)}, u32[]{:S(2)}) copy-start(bf16[160,768]{1,0:T(8,128)(2,1)S(1)} %collective-permute-done.23.refs_10_.refs_13_) | copy-start | bytes 737284
  137.0 8.7 %collective-permute-start.27 = (bf16[8,32,768]{2,1,0:T(8,128)(2,1)S(1)}, bf16[8,32,768]{2,1,0:T(8,128)(2,1)S(1)}, u32[]{:S(2)}, u32[]{:S(2)}) collective-permute-start(bf16[8,32,768]{2,1,0:T(8,128)(2,1)S(1)} %get-tuple-element.99), channel_id=1, source_target_pairs={{0,1},{1,0},{2,3},{3,2},{4,5},{5,4},{6,7},{7,6},{8,9},{9,8},{10,11... | collective-permute-start | bytes 1179656 | tf_op jit(solution)/shard_map/ppermute | solution.py:561
  137.1 8.6 %collective-permute-start.25 = (bf16[160,768]{1,0:T(8,128)(2,1)}, bf16[160,768]{1,0:T(8,128)(2,1)S(1)}, u32[]{:S(2)}, u32[]{:S(2)}) collective-permute-start(bf16[160,768]{1,0:T(8,128)(2,1)} %collective-permute-done.24), channel_id=1, source_target_pairs={{0,4},{4,0},{8,12},{12,8},{16,20},{20,16},{24,28},{28,24},{1,5},{5... | collective-permute-start | bytes 737288 | tf_op jit(solution)/shard_map/ppermute | solution.py:558
  145.7 7.0 %copy-start.16 = (bf16[160,768]{1,0:T(8,128)(2,1)}, bf16[160,768]{1,0:T(8,128)(2,1)S(1)}, u32[]{:S(2)}) copy-start(bf16[160,768]{1,0:T(8,128)(2,1)S(1)} %collective-permute-done.25.refs_5_.refs_15_) | copy-start | bytes 737284
  146.3 0.8 copy-start.17
  147.1 18.7 %all-to-all-start.1 = ((bf16[8,32,1024]{2,1,0:T(8,128)(2,1)}), bf16[8,32,1024]{2,1,0:T(8,128)(2,1)S(1)}, u32[]{:S(2)}, u32[]{:S(2)}) async-start(bf16[8,32,1024]{2,1,0:T(8,128)(2,1)} %copy-done.17), calls=%async_computation.1 | async-start | bytes 1048576 | tf_op jit(solution)/shard_map/all_to_all | solution.py:566
  160.5 4.3 %collective-permute-start.28 = (f32[128,8]{1,0:T(8,128)S(1)}, f32[128,8]{1,0:T(8,128)S(1)}, u32[]{:S(2)}, u32[]{:S(2)}) collective-permute-start(f32[128,8]{1,0:T(8,128)S(1)} %get-tuple-element.104), channel_id=1, source_target_pairs={{0,2},{2,0},{1,3},{3,1},{4,6},{6,4},{5,7},{7,5},{8,10},{10,8},{9,1... | collective-permute-start | bytes 12296 | tf_op jit(solution)/shard_map/ppermute | solution.py:552
  170.1 1.5 collective-permute-start.29

commit v18 on v17

--- a/solution.py
+++ b/solution.py
@@ -597,15 +597,13 @@
             masks = [o] if o else []
             if i >= last - 1 and o % 2:
                 masks = [o - 1, 1] if o > 1 else [1]
-            elif o == 4 and groups == 8:
-                masks = [2, 6]
             for mask in masks:
                 rows = flip(rows, mask)
             back[o] = rows
 
     for kind, i in steps:
         if (kind, i) in early:
-            order.wait([fetch(early[kind, i])])
+            order.wait([fetch(early[kind, i])] + ([back[4]] if kind == "multiply" else []))
         if kind == "gate":
             blocks[i] = gate_call(order, [fetch(i)])[0]
         elif kind == "total":
@@ -623,7 +621,7 @@
     low_grad, first_own = collect_call(order, places, lows, grads, feats)
     firsts = [x.reshape(groups * rank, units) for x in (first_own, swap(first_own))]
     low_grad = exchange(low_grad)
-    order.wait([back[batches[-2][0]]] + [back[4]] * (groups == 8))
+    order.wait([back[batches[-2][0]]])
     total(last)
     order.wait([low_grad, back[1], back[2]])
     low_hid = all_shares(lowrank_hid_call(order, index, hid, firsts, groups))

time: 175 us -> 178 us (1.017)
  starting transfers between devices: 42.3 us -> 46.5 us
  waiting for transfers between devices: 58.4 us -> 56.1 us
    ppermute x18 -> x17, starting transfers between devices: 22.6 us -> 26.3 us  [flip(): return lax.ppermute(x, 'ep', [(i, i ^ mask) for i in range(groups)])]
    ppermute x7, starting transfers between devices: 7.89 us -> 10.2 us  [turn(): lax.ppermute(x, 'rep', [(r, (r + offset) % shares) for r in range(shares)])]
    all_to_all x2, starting transfers between devices: 11.7 us -> 9.81 us  [exchange(): return lax.all_to_all(x, axes, split_axis=0, concat_axis=0, tiled=True)]
    ppermute x18 -> x17, waiting for transfers between devices: 41.6 us -> 41.4 us  [flip(): return lax.ppermute(x, 'ep', [(i, i ^ mask) for i in range(groups)])]
    unnamed x53 -> x51, local copies, waits for them, and re-layouts: 3.95 us -> 3.99 us
  transfers between devices with their start and end apart: 32 -> 31, of which waited for: 16 -> 17; matrix products, arithmetic and copies ran while one was open for 1% -> 1% of each run, Pallas kernels for 35% -> 35%
where the time goes in v18:
time: 178 us; the launch traced here: 175 us
  Pallas kernels  66.7 us (37%)
  waiting for transfers between devices  56.1 us (32%)
  starting transfers between devices  46.5 us (26%)
  local copies, waits for them, and re-layouts  3.99 us (2%)
    pallas_call x18, Pallas kernels, call(): pl.pallas_call(ordered, grid=grid, in_specs=[SMEM, *in_specs] + [ANY] * l...  66.7 us
    ppermute x17, waiting for transfers between devices, flip(): return lax.ppermute(x, 'ep', [(i, i ^ mask) for i in range(groups)])  41.4 us
    ppermute x17, starting transfers between devices, flip(): return lax.ppermute(x, 'ep', [(i, i ^ mask) for i in range(groups)])  26.3 us
    ppermute x7, waiting for transfers between devices, turn(): lax.ppermute(x, 'rep', [(r, (r + offset) % shares) for r in range(shares)])  11.6 us
    ppermute x7, starting transfers between devices, turn(): lax.ppermute(x, 'rep', [(r, (r + offset) % shares) for r in range(shares)])  10.2 us
    all_to_all x2, starting transfers between devices, exchange(): return lax.all_to_all(x, axes, split_axis=0, concat_axis=0, tiled=True)  9.81 us
    unnamed x51, local copies, waits for them, and re-layouts  3.99 us
  transfers between devices with their start and end apart: 31, of which 17 were waited for; matrix products, arithmetic and copies ran while one was open for 1% of the time, Pallas kernels for 35%

profile of v18, /device:TPU:8, one launch (start us, length us, event | category | flops | bytes accessed | tf_op | source)
XLA Modules:
  0.0 175.1 jit_solution(18189974603434897111)
XLA Ops:
  0.8 0.8 copy-done.19
  1.6 0.7 copy-done.20
  2.3 1.1 pack_block.1
  3.4 1.6 collective-permute-start
  5.0 2.6 %collective-permute-start.4 = (bf16[128,2304]{1,0:T(8,128)(2,1)S(1)}, bf16[128,2304]{1,0:T(8,128)(2,1)S(1)}, u32[]{:S(2)}, u32[]{:S(2)}) collective-permute-start(bf16[128,2304]{1,0:T(8,128)(2,1)S(1)} %get-tuple-element.57.refs_1_.refs_5_.refs_2_), channel_id=1, source_target_pairs={{0,16},{4,20},{8,24},{12,28},{16,0},{20,4},{24,8},{28,12},{1,17},{... | collective-permute-start | bytes 1769480 | tf_op jit(solution)/shard_map/ppermute | solution.py:558
  8.0 3.4 %load_matrix.1 = (bf16[1536,2048]{1,0:T(8,128)(2,1)S(1)}, f32[8,128]{1,0:T(8,128)}) custom-call(s32[3]{0:T(128)S(1)} %pad_add_fusion.refs_0_, bf16[1536,2048]{1,0:T(8,128)(2,1)} %bitcast.33, f32[8,128]{1,0:T(8,128)} %get-tuple-element.58.refs_2_), custom_call_target="tpu_custom_call" | custom-call | flops 1 | bytes 1 | tf_op jit(solution)/shard_map/load_matrix/pallas_call | solution.py:53
  11.5 7.7 %collective-permute-done.refs_2_.refs_6_.refs_3_ = bf16[128,2304]{1,0:T(8,128)(2,1)S(1)} collective-permute-done((bf16[128,2304]{1,0:T(8,128)(2,1)S(1)}, bf16[128,2304]{1,0:T(8,128)(2,1)S(1)}, u32[]{:S(2)}, u32[]{:S(2)}) %collective-permute-start) | collective-permute-done | bytes 589856 | tf_op jit(solution)/shard_map/ppermute | solution.py:558
  19.2 8.1 %expert_rows.4 = (bf16[320,768]{1,0:T(8,128)(2,1)S(1)}, bf16[320,768]{1,0:T(8,128)(2,1)S(1)}, bf16[2,64,128]{2,1,0:T(8,128)(2,1)S(1)}, f32[8,128]{1,0:T(8,128)}) custom-call(s32[3]{0:T(128)S(1)} %pad_add_fusion.refs_0_, bf16[128,2304]{1,0:T(8,128)(2,1)S(1)} %get-tuple-element.57.refs_1_.refs_5_.refs_2_, ...), custom_call_target="tpu_custom_call" | custom-call | flops 1 | bytes 1 | tf_op jit(solution)/shard_map/expert_rows/pallas_call | solution.py:53
  27.4 5.7 %collective-permute-done.4.refs_1_ = bf16[128,2304]{1,0:T(8,128)(2,1)S(1)} collective-permute-done((bf16[128,2304]{1,0:T(8,128)(2,1)S(1)}, bf16[128,2304]{1,0:T(8,128)(2,1)S(1)}, u32[]{:S(2)}, u32[]{:S(2)}) %collective-permute-start.4) | collective-permute-done | bytes 589856 | tf_op jit(solution)/shard_map/ppermute | solution.py:558
  33.1 0.5 gate.1
  33.6 1.5 collective-permute-start.5
  35.6 1.5 collective-permute-start.8
  37.1 7.9 %expert_rows.5 = (bf16[320,768]{1,0:T(8,128)(2,1)S(1)}, bf16[320,768]{1,0:T(8,128)(2,1)S(1)}, bf16[2,64,128]{2,1,0:T(8,128)(2,1)S(1)}, f32[8,128]{1,0:T(8,128)}) custom-call(s32[3]{0:T(128)S(1)} %pad_add_fusion.refs_0_, bf16[128,2304]{1,0:T(8,128)(2,1)S(1)} %collective-permute-done.3.refs_1_.refs_7_.refs_4_, ...), custom_call_target="tpu_custom_call" | custom-call | flops 1 | bytes 1 | tf_op jit(solution)/shard_map/expert_rows/pallas_call | solution.py:53
  45.1 0.6 collective-permute-start.7
  45.7 1.6 collective-permute-start.9
  47.2 1.7 collective-permute-done.5.refs_1_.refs_9_.refs_6_
  49.5 1.9 %collective-permute-done.6.refs_4_.refs_2_.refs_10_.refs_7_ = bf16[128,2304]{1,0:T(8,128)(2,1)S(1)} collective-permute-done((bf16[128,2304]{1,0:T(8,128)(2,1)S(1)}, bf16[128,2304]{1,0:T(8,128)(2,1)S(1)}, u32[]{:S(2)}, u32[]{:S(2)}) %collective-permute-start.6) | collective-permute-done | bytes 589856 | tf_op jit(solution)/shard_map/ppermute | solution.py:558
  51.4 1.3 share_sum.4
  52.7 5.6 %collective-permute-done.7.refs_2_ = bf16[320,768]{1,0:T(8,128)(2,1)S(1)} collective-permute-done((bf16[320,768]{1,0:T(8,128)(2,1)S(1)}, bf16[320,768]{1,0:T(8,128)(2,1)S(1)}, u32[]{:S(2)}, u32[]{:S(2)}) %collective-permute-start.7) | collective-permute-done | bytes 491552 | tf_op jit(solution)/shard_map/ppermute | solution.py:552
  58.4 1.3 share_sum.5
  59.6 2.7 %collective-permute-start.10 = (bf16[160,768]{1,0:T(8,128)(2,1)S(1)}, bf16[160,768]{1,0:T(8,128)(2,1)S(1)}, u32[]{:S(2)}, u32[]{:S(2)}) collective-permute-start(bf16[160,768]{1,0:T(8,128)(2,1)S(1)} %get-tuple-element.73), channel_id=1, source_target_pairs={{0,16},{4,20},{8,24},{12,28},{16,0},{20,4},{24,8},{28,12},{1,17},{... | collective-permute-start | bytes 737288 | tf_op jit(solution)/shard_map/ppermute | solution.py:558
  62.4 1.7 collective-permute-done.9.refs_8_.refs_1_.refs_11_
  64.1 7.9 %collective-permute-done.10.refs_9_.refs_12_ = bf16[160,768]{1,0:T(8,128)(2,1)S(1)} collective-permute-done((bf16[160,768]{1,0:T(8,128)(2,1)S(1)}, bf16[160,768]{1,0:T(8,128)(2,1)S(1)}, u32[]{:S(2)}, u32[]{:S(2)}) %collective-permute-start.10) | collective-permute-done | bytes 245792 | tf_op jit(solution)/shard_map/ppermute | solution.py:558
  71.9 8.2 %expert_rows.6 = (bf16[320,768]{1,0:T(8,128)(2,1)S(1)}, bf16[320,768]{1,0:T(8,128)(2,1)S(1)}, bf16[2,64,128]{2,1,0:T(8,128)(2,1)S(1)}, f32[8,128]{1,0:T(8,128)}) custom-call(s32[3]{0:T(128)S(1)} %pad_add_fusion.refs_0_, bf16[128,2304]{1,0:T(8,128)(2,1)S(1)} %collective-permute-done.5.refs_1_.refs_9_.refs_6_, ...), custom_call_target="tpu_custom_call" | custom-call | flops 1 | bytes 1 | tf_op jit(solution)/shard_map/expert_rows/pallas_call | solution.py:53
  80.1 1.6 collective-permute-start.12
  81.7 8.8 %expert_rows.7 = (bf16[320,768]{1,0:T(8,128)(2,1)}, bf16[320,768]{1,0:T(8,128)(2,1)S(1)}, bf16[2,64,128]{2,1,0:T(8,128)(2,1)S(1)}, f32[8,128]{1,0:T(8,128)}) custom-call(s32[3]{0:T(128)S(1)} %pad_add_fusion.refs_0_, bf16[128,2304]{1,0:T(8,128)(2,1)S(1)} %collective-permute-done.9.refs_8_.refs_1_.refs_11_, ...), custom_call_target="tpu_custom_call" | custom-call | flops 1 | bytes 1 | tf_op jit(solution)/shard_map/expert_rows/pallas_call | solution.py:53
  90.5 0.6 collective-permute-start.15
  91.1 1.7 collective-permute-done.12.refs_2_
  92.8 1.3 share_sum.6
  94.1 1.2 collective-permute-start.16
  95.3 1.7 collect_blocks.1
  97.1 3.7 %collective-permute-start.18 = (bf16[160,768]{1,0:T(8,128)(2,1)}, bf16[160,768]{1,0:T(8,128)(2,1)S(1)}, u32[]{:S(2)}, u32[]{:S(2)}) collective-permute-start(bf16[160,768]{1,0:T(8,128)(2,1)} %get-tuple-element.89), channel_id=1, source_target_pairs={{0,8},{4,12},{8,0},{12,4},{16,24},{20,28},{24,16},{28,20},{1,9},{5... | collective-permute-start | bytes 737288 | tf_op jit(solution)/shard_map/ppermute | solution.py:558
  100.7 1.5 collective-permute-start.17
  102.2 3.9 %all-to-all-start = ((bf16[8,64,128]{2,1,0:T(8,128)(2,1)}), bf16[8,64,128]{2,1,0:T(8,128)(2,1)S(1)}, u32[]{:S(2)}, u32[]{:S(2)}) async-start(bf16[8,64,128]{2,1,0:T(8,128)(2,1)} %get-tuple-element.81), calls=%async_computation | async-start | bytes 262144 | tf_op jit(solution)/shard_map/all_to_all | solution.py:566
  106.2 0.8 collective-permute-start.19
  107.0 1.3 share_sum.7
  108.3 0.7 copy-done.22
  109.0 2.2 %collective-permute-start.21 = (bf16[160,768]{1,0:T(8,128)(2,1)}, bf16[160,768]{1,0:T(8,128)(2,1)S(1)}, u32[]{:S(2)}, u32[]{:S(2)}) collective-permute-start(bf16[160,768]{1,0:T(8,128)(2,1)} %get-tuple-element.94), channel_id=1, source_target_pairs={{0,16},{4,20},{8,24},{12,28},{16,0},{20,4},{24,8},{28,12},{1,17},{... | collective-permute-start | bytes 737288 | tf_op jit(solution)/shard_map/ppermute | solution.py:558
  111.3 1.1 all-to-all-done.refs_6_.refs_1_
  112.4 3.5 %lowrank_hid.1 = (f32[128,512]{1,0:T(8,128)S(1)}, f32[8,128]{1,0:T(8,128)}) custom-call(s32[3]{0:T(128)S(1)} %pad_add_fusion.refs_0_, s32[128,8]{1,0:T(8,128)S(1)} %copy.17.refs_1_.refs_5_.refs_2_, bf16[1024,768]{1,0:T(8,128)(2,1)} %bitcast.29, bf16[256,768]{1,0:T(8,128)(2,1)S(1)} %bitcast.23, bf16[256,768]{1,0:T(8,128)(2,1)S(1)} %bitcast.25, ...), custom_call_target="tpu_custom_call" | custom-call | flops 1 | bytes 1 | tf_op jit(solution)/shard_map/lowrank_hid/pallas_call | solution.py:53
  116.0 2.1 %collective-permute-start.25 = (f32[128,512]{1,0:T(8,128)S(1)}, f32[128,512]{1,0:T(8,128)S(1)}, u32[]{:S(2)}, u32[]{:S(2)}) collective-permute-start(f32[128,512]{1,0:T(8,128)S(1)} %get-tuple-element.96.refs_7_), channel_id=1, source_target_pairs={{0,2},{2,0},{1,3},{3,1},{4,6},{6,4},{5,7},{7,5},{8,10},{10,8},{9,1... | collective-permute-start | bytes 786440 | tf_op jit(solution)/shard_map/ppermute | solution.py:552
  118.1 2.9 %collective-permute-done.19 = bf16[160,768]{1,0:T(8,128)(2,1)} collective-permute-done((bf16[160,768]{1,0:T(8,128)(2,1)}, bf16[160,768]{1,0:T(8,128)(2,1)}, u32[]{:S(2)}, u32[]{:S(2)}) %collective-permute-start.19) | collective-permute-done | bytes 245792 | tf_op jit(solution)/shard_map/ppermute | solution.py:558
  121.0 1.6 collective-permute-start.20
  122.6 1.2 collective-permute-start.22
  123.8 1.8 %collective-permute-start.13 = (bf16[8,64,128]{2,1,0:T(8,128)(2,1)S(1)}, bf16[8,64,128]{2,1,0:T(8,128)(2,1)S(1)}, u32[]{:S(2)}, u32[]{:S(2)}) collective-permute-start(bf16[8,64,128]{2,1,0:T(8,128)(2,1)S(1)} %all-to-all-done.refs_6_.refs_1_), channel_id=1, source_target_pairs={{0,2},{2,0},{1,3},{3,1},{4,6},{6,4},{5,7},{7,5},{8,10},{10,8},{9,1... | collective-permute-start | bytes 393224 | tf_op jit(solution)/shard_map/ppermute | solution.py:552
  125.6 1.0 collective-permute-start.23
  126.8 2.0 %collective-permute-done.13.refs_2_ = bf16[8,64,128]{2,1,0:T(8,128)(2,1)S(1)} collective-permute-done((bf16[8,64,128]{2,1,0:T(8,128)(2,1)S(1)}, bf16[8,64,128]{2,1,0:T(8,128)(2,1)S(1)}, u32[]{:S(2)}, u32[]{:S(2)}) %collective-permute-start.13) | collective-permute-done | bytes 131104 | tf_op jit(solution)/shard_map/ppermute | solution.py:552
  128.7 1.3 collective-permute-done.20.refs_4_.refs_11_
  130.0 0.7 low_dense.1
  130.7 3.7 %collective-permute-done.22.refs_10_.refs_13_ = bf16[160,768]{1,0:T(8,128)(2,1)S(1)} collective-permute-done((bf16[160,768]{1,0:T(8,128)(2,1)S(1)}, bf16[160,768]{1,0:T(8,128)(2,1)S(1)}, u32[]{:S(2)}, u32[]{:S(2)}) %collective-permute-start.22) | collective-permute-done | bytes 245792 | tf_op jit(solution)/shard_map/ppermute | solution.py:558
  134.4 4.7 %first_grad.1 = (f32[8,32,768]{2,1,0:T(8,128)S(1)}, bf16[8,32,768]{2,1,0:T(8,128)(2,1)S(1)}, bf16[8,32,256]{2,1,0:T(8,128)(2,1)S(1)}, f32[8,128]{1,0:T(8,128)}) custom-call(s32[3]{0:T(128)S(1)} %pad_add_fusion.refs_0_, s32[128,8]{1,0:T(8,128)S(1)} %copy.17.refs_1_.refs_5_.refs_2_, bf16[128,8]{1,0:T(8,128)(2,1)S(1)} %copy.19.refs_2_.refs_6_.refs_3_, ...), custom_call_target="tpu_custom_call" | custom-call | flops 1 | bytes 1 | tf_op jit(solution)/shard_map/first_grad/pallas_call | solution.py:53
  139.2 1.7 collective-permute-start.24
  140.9 6.9 %collective-permute-done.24.refs_5_.refs_15_ = bf16[160,768]{1,0:T(8,128)(2,1)S(1)} collective-permute-done((bf16[160,768]{1,0:T(8,128)(2,1)}, bf16[160,768]{1,0:T(8,128)(2,1)S(1)}, u32[]{:S(2)}, u32[]{:S(2)}) %collective-permute-start.24) | collective-permute-done | bytes 245792 | tf_op jit(solution)/shard_map/ppermute | solution.py:558
  147.8 0.6 first_sum.1
  148.4 0.8 copy-done.17
  149.3 5.9 %all-to-all-start.1 = ((bf16[8,32,1024]{2,1,0:T(8,128)(2,1)}), bf16[8,32,1024]{2,1,0:T(8,128)(2,1)S(1)}, u32[]{:S(2)}, u32[]{:S(2)}) async-start(bf16[8,32,1024]{2,1,0:T(8,128)(2,1)} %copy-done.17), calls=%async_computation.1 | async-start | bytes 1048576 | tf_op jit(solution)/shard_map/all_to_all | solution.py:566
  155.2 7.8 %finish.1 = (bf16[1024,768]{1,0:T(8,128)(2,1)}, f32[128,8]{1,0:T(8,128)S(1)}, f32[8,128]{1,0:T(8,128)}) custom-call(s32[3]{0:T(128)S(1)} %pad_add_fusion.refs_0_, s32[128,8]{1,0:T(8,128)S(1)} %copy.17.refs_1_.refs_5_.refs_2_, s32[128,8]{1,0:T(8,128)S(1)} %copy.17.refs_1_.refs_5_.refs_2_, bf16[128,8]{1,0:T(8,128)(2,1)S(1)} %copy.19.refs_2_.refs_6_.refs_3_, ...), custom_call_target="tpu_custom_call" | custom-call | flops 1 | bytes 20000000 | tf_op jit(solution)/shard_map/finish/pallas_call | solution.py:53
  163.0 2.0 %collective-permute-start.27 = (f32[128,8]{1,0:T(8,128)S(1)}, f32[128,8]{1,0:T(8,128)S(1)}, u32[]{:S(2)}, u32[]{:S(2)}) collective-permute-start(f32[128,8]{1,0:T(8,128)S(1)} %get-tuple-element.104), channel_id=1, source_target_pairs={{0,2},{2,0},{1,3},{3,1},{4,6},{6,4},{5,7},{7,5},{8,10},{10,8},{9,1... | collective-permute-start | bytes 12296 | tf_op jit(solution)/shard_map/ppermute | solution.py:552
  165.0 2.2 %collective-permute-done.27.refs_11_ = f32[128,8]{1,0:T(8,128)S(1)} collective-permute-done((f32[128,8]{1,0:T(8,128)S(1)}, f32[128,8]{1,0:T(8,128)S(1)}, u32[]{:S(2)}, u32[]{:S(2)}) %collective-permute-start.27) | collective-permute-done | bytes 4128 | tf_op jit(solution)/shard_map/ppermute | solution.py:552
  167.3 1.2 all-to-all-done.1.refs_1_
  168.5 4.4 %second_grad.1 = (f32[32,2048]{1,0:T(8,128)S(1)}, f32[32,2048]{1,0:T(8,128)S(1)}, f32[32,768]{1,0:T(8,128)}, f32[8,128]{1,0:T(8,128)}) custom-call(s32[3]{0:T(128)S(1)} %pad_add_fusion.refs_0_, bf16[8,32,1024]{2,1,0:T(8,128)(2,1)S(1)} %all-to-all-done.1.refs_1_, bf16[128,2304]{1,0:T(8,128)(2,1)} %copy-done.3, bf16[128,2304]{1,0:T(8,128)(2,1)} %copy-done.4, ...), custom_call_target="tpu_custom_call" | custom-call | flops 1 | bytes 1 | tf_op jit(solution)/shard_map/second_grad/pallas_call | solution.py:53
  172.9 0.7 copy.20
  173.5 0.8 collective-permute-done.28
  174.4 0.7 add_bitcast_fusion
  (70 shorter events, 2.0 us)
Async XLA Ops:
  0.6 18.6 %copy-start.8 = (bf16[1,32,2048]{2,1,0:T(8,128)(2,1)S(1)}, bf16[1,32,2048]{2,1,0:T(8,128)(2,1)}, u32[]{:S(2)}) copy-start(bf16[1,32,2048]{2,1,0:T(8,128)(2,1)} %param.13) | copy-start | bytes 393220
  0.6 18.6 %collective-permute-start.2 = (bf16[1536,2048]{1,0:T(8,128)(2,1)}, bf16[1536,2048]{1,0:T(8,128)(2,1)}, u32[]{:S(2)}, u32[]{:S(2)}) collective-permute-start(bf16[1536,2048]{1,0:T(8,128)(2,1)} %bitcast.32), channel_id=1, source_target_pairs={{0,1},{1,0},{2,3},{3,2},{4,5},{5,4},{6,7},{7,6},{8,9},{9,8},{10,11... | collective-permute-start | bytes 18874376 | tf_op jit(solution)/shard_map/ppermute | solution.py:561
  0.8 0.8 copy-start.19
  1.6 0.7 copy-start.20
  3.4 23.9 %copy-start.3 = (bf16[128,2304]{1,0:T(8,128)(2,1)}, bf16[128,2304]{1,0:T(8,128)(2,1)S(1)}, u32[]{:S(2)}) copy-start(bf16[128,2304]{1,0:T(8,128)(2,1)S(1)} %get-tuple-element.57.refs_1_.refs_5_.refs_2_) | copy-start | bytes 1769476
  3.4 15.8 %collective-permute-start = (bf16[128,2304]{1,0:T(8,128)(2,1)S(1)}, bf16[128,2304]{1,0:T(8,128)(2,1)S(1)}, u32[]{:S(2)}, u32[]{:S(2)}) collective-permute-start(bf16[128,2304]{1,0:T(8,128)(2,1)S(1)} %get-tuple-element.57.refs_1_.refs_5_.refs_2_), channel_id=1, source_target_pairs={{0,4},{4,0},{8,12},{12,8},{16,20},{20,16},{24,28},{28,24},{1,5},{5... | collective-permute-start | bytes 1769480 | tf_op jit(solution)/shard_map/ppermute | solution.py:558
  5.0 28.1 %collective-permute-start.4 = (bf16[128,2304]{1,0:T(8,128)(2,1)S(1)}, bf16[128,2304]{1,0:T(8,128)(2,1)S(1)}, u32[]{:S(2)}, u32[]{:S(2)}) collective-permute-start(bf16[128,2304]{1,0:T(8,128)(2,1)S(1)} %get-tuple-element.57.refs_1_.refs_5_.refs_2_), channel_id=1, source_target_pairs={{0,16},{4,20},{8,24},{12,28},{16,0},{20,4},{24,8},{28,12},{1,17},{... | collective-permute-start | bytes 1769480 | tf_op jit(solution)/shard_map/ppermute | solution.py:558
  7.6 27.6 %collective-permute-start.3 = (bf16[128,2304]{1,0:T(8,128)(2,1)S(1)}, bf16[128,2304]{1,0:T(8,128)(2,1)S(1)}, u32[]{:S(2)}, u32[]{:S(2)}) collective-permute-start(bf16[128,2304]{1,0:T(8,128)(2,1)S(1)} %get-tuple-element.57.refs_1_.refs_5_.refs_2_), channel_id=1, source_target_pairs={{0,8},{4,12},{8,0},{12,4},{16,24},{20,28},{24,16},{28,20},{1,9},{5... | collective-permute-start | bytes 1769480 | tf_op jit(solution)/shard_map/ppermute | solution.py:558
  8.0 3.4 %collective-permute-start.1 = (bf16[32,2048]{1,0:T(8,128)(2,1)}, bf16[32,2048]{1,0:T(8,128)(2,1)S(1)}, u32[]{:S(2)}, u32[]{:S(2)}) collective-permute-start(bf16[32,2048]{1,0:T(8,128)(2,1)} %bitcast.18), channel_id=1, source_target_pairs={{0,1},{1,0},{2,3},{3,2},{4,5},{5,4},{6,7},{7,6},{8,9},{9,8},{10,11... | collective-permute-start | bytes 393224 | tf_op jit(solution)/shard_map/ppermute | solution.py:561
  19.2 8.2 %copy-start.4 = (bf16[128,2304]{1,0:T(8,128)(2,1)}, bf16[128,2304]{1,0:T(8,128)(2,1)S(1)}, u32[]{:S(2)}) copy-start(bf16[128,2304]{1,0:T(8,128)(2,1)S(1)} %collective-permute-done.refs_2_.refs_6_.refs_3_) | copy-start | bytes 1769476
  33.6 12.1 %copy-start.2 = (bf16[128,2304]{1,0:T(8,128)(2,1)}, bf16[128,2304]{1,0:T(8,128)(2,1)S(1)}, u32[]{:S(2)}) copy-start(bf16[128,2304]{1,0:T(8,128)(2,1)S(1)} %get-tuple-element.63.refs_2_.refs_8_.refs_5_) | copy-start | bytes 1769476
  33.6 15.3 %collective-permute-start.5 = (bf16[128,2304]{1,0:T(8,128)(2,1)S(1)}, bf16[128,2304]{1,0:T(8,128)(2,1)S(1)}, u32[]{:S(2)}, u32[]{:S(2)}) collective-permute-start(bf16[128,2304]{1,0:T(8,128)(2,1)S(1)} %get-tuple-element.63.refs_2_.refs_8_.refs_5_), channel_id=1, source_target_pairs={{0,8},{4,12},{8,0},{12,4},{16,24},{20,28},{24,16},{28,20},{1,9},{5... | collective-permute-start | bytes 1769480 | tf_op jit(solution)/shard_map/ppermute | solution.py:558
  35.1 10.0 %copy-start.5 = (bf16[128,2304]{1,0:T(8,128)(2,1)}, bf16[128,2304]{1,0:T(8,128)(2,1)S(1)}, u32[]{:S(2)}) copy-start(bf16[128,2304]{1,0:T(8,128)(2,1)S(1)} %collective-permute-done.3.refs_1_.refs_7_.refs_4_) | copy-start | bytes 1769476
  35.1 16.3 %collective-permute-start.6 = (bf16[128,2304]{1,0:T(8,128)(2,1)S(1)}, bf16[128,2304]{1,0:T(8,128)(2,1)S(1)}, u32[]{:S(2)}, u32[]{:S(2)}) collective-permute-start(bf16[128,2304]{1,0:T(8,128)(2,1)S(1)} %collective-permute-done.3.refs_1_.refs_7_.refs_4_), channel_id=1, source_target_pairs={{0,4},{4,0},{8,12},{12,8},{16,20},{20,16},{24,28},{28,24},{1,5},{5... | collective-permute-start | bytes 1769480 | tf_op jit(solution)/shard_map/ppermute | solution.py:558
  35.6 15.8 %collective-permute-start.8 = (bf16[320,768]{1,0:T(8,128)(2,1)S(1)}, bf16[320,768]{1,0:T(8,128)(2,1)S(1)}, u32[]{:S(2)}, u32[]{:S(2)}) collective-permute-start(bf16[320,768]{1,0:T(8,128)(2,1)S(1)} %get-tuple-element.69), channel_id=1, source_target_pairs={{0,2},{2,0},{1,3},{3,1},{4,6},{6,4},{5,7},{7,5},{8,10},{10,8},{9,1... | collective-permute-start | bytes 1474568 | tf_op jit(solution)/shard_map/ppermute | solution.py:552
  37.1 34.8 %copy-start.9 = (bf16[1,32,2048]{2,1,0:T(8,128)(2,1)S(1)}, bf16[1,32,2048]{2,1,0:T(8,128)(2,1)}, u32[]{:S(2)}) copy-start(bf16[1,32,2048]{2,1,0:T(8,128)(2,1)} %param.13) | copy-start | bytes 393220
  45.1 13.2 %collective-permute-start.7 = (bf16[320,768]{1,0:T(8,128)(2,1)S(1)}, bf16[320,768]{1,0:T(8,128)(2,1)S(1)}, u32[]{:S(2)}, u32[]{:S(2)}) collective-permute-start(bf16[320,768]{1,0:T(8,128)(2,1)S(1)} %get-tuple-element.67), channel_id=1, source_target_pairs={{0,2},{2,0},{1,3},{3,1},{4,6},{6,4},{5,7},{7,5},{8,10},{10,8},{9,1... | collective-permute-start | bytes 1474568 | tf_op jit(solution)/shard_map/ppermute | solution.py:552
  45.7 18.4 %collective-permute-start.9 = (bf16[128,2304]{1,0:T(8,128)(2,1)S(1)}, bf16[128,2304]{1,0:T(8,128)(2,1)S(1)}, u32[]{:S(2)}, u32[]{:S(2)}) collective-permute-start(bf16[128,2304]{1,0:T(8,128)(2,1)S(1)} %get-tuple-element.63.refs_2_.refs_8_.refs_5_), channel_id=1, source_target_pairs={{0,4},{4,0},{8,12},{12,8},{16,20},{20,16},{24,28},{28,24},{1,5},{5... | collective-permute-start | bytes 1769480 | tf_op jit(solution)/shard_map/ppermute | solution.py:558
  49.0 31.1 %copy-start.6 = (bf16[128,2304]{1,0:T(8,128)(2,1)}, bf16[128,2304]{1,0:T(8,128)(2,1)S(1)}, u32[]{:S(2)}) copy-start(bf16[128,2304]{1,0:T(8,128)(2,1)S(1)} %collective-permute-done.5.refs_1_.refs_9_.refs_6_) | copy-start | bytes 1769476
  49.0 32.7 %collective-permute-start.11 = (bf16[128,2304]{1,0:T(8,128)(2,1)S(1)}, bf16[128,2304]{1,0:T(8,128)(2,1)S(1)}, u32[]{:S(2)}, u32[]{:S(2)}) collective-permute-start(bf16[128,2304]{1,0:T(8,128)(2,1)S(1)} %collective-permute-done.5.refs_1_.refs_9_.refs_6_), channel_id=1, source_target_pairs={{0,4},{4,0},{8,12},{12,8},{16,20},{20,16},{24,28},{28,24},{1,5},{5... | collective-permute-start | bytes 1769480 | tf_op jit(solution)/shard_map/ppermute | solution.py:558
  51.4 28.7 %copy-start.1 = (bf16[128,2304]{1,0:T(8,128)(2,1)}, bf16[128,2304]{1,0:T(8,128)(2,1)S(1)}, u32[]{:S(2)}) copy-start(bf16[128,2304]{1,0:T(8,128)(2,1)S(1)} %collective-permute-done.6.refs_4_.refs_2_.refs_10_.refs_7_) | copy-start | bytes 1769476
  52.7 27.4 %copy-start.18 = (bf16[160,768]{1,0:T(8,128)(2,1)}, bf16[160,768]{1,0:T(8,128)(2,1)S(1)}, u32[]{:S(2)}) copy-start(bf16[160,768]{1,0:T(8,128)(2,1)S(1)} %get-tuple-element.93.refs_8_) | copy-start | bytes 737284
  59.6 12.3 %collective-permute-start.10 = (bf16[160,768]{1,0:T(8,128)(2,1)S(1)}, bf16[160,768]{1,0:T(8,128)(2,1)S(1)}, u32[]{:S(2)}, u32[]{:S(2)}) collective-permute-start(bf16[160,768]{1,0:T(8,128)(2,1)S(1)} %get-tuple-element.73), channel_id=1, source_target_pairs={{0,16},{4,20},{8,24},{12,28},{16,0},{20,4},{24,8},{28,12},{1,17},{... | collective-permute-start | bytes 737288 | tf_op jit(solution)/shard_map/ppermute | solution.py:558
  64.1 17.7 %copy-start = (bf16[128,2304]{1,0:T(8,128)(2,1)}, bf16[128,2304]{1,0:T(8,128)(2,1)S(1)}, u32[]{:S(2)}) copy-start(bf16[128,2304]{1,0:T(8,128)(2,1)S(1)} %collective-permute-done.9.refs_8_.refs_1_.refs_11_) | copy-start | bytes 1769476
  71.9 8.2 %copy-start.16 = (bf16[160,768]{1,0:T(8,128)(2,1)}, bf16[160,768]{1,0:T(8,128)(2,1)S(1)}, u32[]{:S(2)}) copy-start(bf16[160,768]{1,0:T(8,128)(2,1)S(1)} %collective-permute-done.10.refs_9_.refs_12_) | copy-start | bytes 737284
  80.1 12.7 %collective-permute-start.12 = (bf16[320,768]{1,0:T(8,128)(2,1)S(1)}, bf16[320,768]{1,0:T(8,128)(2,1)S(1)}, u32[]{:S(2)}, u32[]{:S(2)}) collective-permute-start(bf16[320,768]{1,0:T(8,128)(2,1)S(1)} %get-tuple-element.78), channel_id=1, source_target_pairs={{0,2},{2,0},{1,3},{3,1},{4,6},{6,4},{5,7},{7,5},{8,10},{10,8},{9,1... | collective-permute-start | bytes 1474568 | tf_op jit(solution)/shard_map/ppermute | solution.py:552
  81.7 8.8 %copy-start.7 = (bf16[128,2304]{1,0:T(8,128)(2,1)}, bf16[128,2304]{1,0:T(8,128)(2,1)S(1)}, u32[]{:S(2)}) copy-start(bf16[128,2304]{1,0:T(8,128)(2,1)S(1)} %collective-permute-done.11.refs_2_.refs_12_.refs_9_) | copy-start | bytes 1769476
  90.5 20.7 %copy-start.21 = (s32[128,8]{0,1:T(8,128)S(1)}, s32[128,8]{0,1:T(8,128)}, u32[]{:S(2)}) copy-start(s32[128,8]{0,1:T(8,128)} %param.9) | copy-start | bytes 12292
  90.5 36.1 %copy-start.23 = (bf16[128,8]{0,1:T(8,128)(2,1)S(1)}, bf16[128,8]{0,1:T(8,128)(2,1)}, u32[]{:S(2)}) copy-start(bf16[128,8]{0,1:T(8,128)(2,1)} %param.10) | copy-start | bytes 6148
  90.5 16.4 %collective-permute-start.15 = (bf16[320,768]{1,0:T(8,128)(2,1)}, bf16[320,768]{1,0:T(8,128)(2,1)S(1)}, u32[]{:S(2)}, u32[]{:S(2)}) collective-permute-start(bf16[320,768]{1,0:T(8,128)(2,1)} %get-tuple-element.84), channel_id=1, source_target_pairs={{0,2},{2,0},{1,3},{3,1},{4,6},{6,4},{5,7},{7,5},{8,10},{10,8},{9,1... | collective-permute-start | bytes 1474568 | tf_op jit(solution)/shard_map/ppermute | solution.py:552
  94.1 12.0 %collective-permute-start.16 = (bf16[160,768]{1,0:T(8,128)(2,1)S(1)}, bf16[160,768]{1,0:T(8,128)(2,1)S(1)}, u32[]{:S(2)}, u32[]{:S(2)}) collective-permute-start(bf16[160,768]{1,0:T(8,128)(2,1)S(1)} %get-tuple-element.86), channel_id=1, source_target_pairs={{0,24},{4,28},{8,16},{12,20},{16,8},{20,12},{24,0},{28,4},{1,25},{... | collective-permute-start | bytes 737288 | tf_op jit(solution)/shard_map/ppermute | solution.py:558
  97.1 15.4 %collective-permute-start.14 = (bf16[8,32,768]{2,1,0:T(8,128)(2,1)S(1)}, bf16[8,32,768]{2,1,0:T(8,128)(2,1)S(1)}, u32[]{:S(2)}, u32[]{:S(2)}) collective-permute-start(bf16[8,32,768]{2,1,0:T(8,128)(2,1)S(1)} %get-tuple-element.82), channel_id=1, source_target_pairs={{0,1},{1,0},{2,3},{3,2},{4,5},{5,4},{6,7},{7,6},{8,9},{9,8},{10,11... | collective-permute-start | bytes 1179656 | tf_op jit(solution)/shard_map/ppermute | solution.py:561
  97.1 14.2 %collective-permute-start.18 = (bf16[160,768]{1,0:T(8,128)(2,1)}, bf16[160,768]{1,0:T(8,128)(2,1)S(1)}, u32[]{:S(2)}, u32[]{:S(2)}) collective-permute-start(bf16[160,768]{1,0:T(8,128)(2,1)} %get-tuple-element.89), channel_id=1, source_target_pairs={{0,8},{4,12},{8,0},{12,4},{16,24},{20,28},{24,16},{28,20},{1,9},{5... | collective-permute-start | bytes 737288 | tf_op jit(solution)/shard_map/ppermute | solution.py:558
  100.7 10.6 %collective-permute-start.17 = (bf16[160,768]{1,0:T(8,128)(2,1)}, bf16[160,768]{1,0:T(8,128)(2,1)S(1)}, u32[]{:S(2)}, u32[]{:S(2)}) collective-permute-start(bf16[160,768]{1,0:T(8,128)(2,1)} %get-tuple-element.88), channel_id=1, source_target_pairs={{0,4},{4,0},{8,12},{12,8},{16,20},{20,16},{24,28},{28,24},{1,5},{5... | collective-permute-start | bytes 737288 | tf_op jit(solution)/shard_map/ppermute | solution.py:558
  102.2 10.2 %all-to-all-start = ((bf16[8,64,128]{2,1,0:T(8,128)(2,1)}), bf16[8,64,128]{2,1,0:T(8,128)(2,1)S(1)}, u32[]{:S(2)}, u32[]{:S(2)}) async-start(bf16[8,64,128]{2,1,0:T(8,128)(2,1)} %get-tuple-element.81), calls=%async_computation | async-start | bytes 262144 | tf_op jit(solution)/shard_map/all_to_all | solution.py:566
  106.2 49.0 %copy-start.11 = (bf16[160,768]{1,0:T(8,128)(2,1)}, bf16[160,768]{1,0:T(8,128)(2,1)S(1)}, u32[]{:S(2)}) copy-start(bf16[160,768]{1,0:T(8,128)(2,1)S(1)} %collective-permute-done.16.refs_4_.refs_14_) | copy-start | bytes 737284
  106.2 14.8 %collective-permute-start.19 = (bf16[160,768]{1,0:T(8,128)(2,1)}, bf16[160,768]{1,0:T(8,128)(2,1)}, u32[]{:S(2)}, u32[]{:S(2)}) collective-permute-start(bf16[160,768]{1,0:T(8,128)(2,1)} %get-tuple-element.91), channel_id=1, source_target_pairs={{0,8},{4,12},{8,0},{12,4},{16,24},{20,28},{24,16},{28,20},{1,9},{5... | collective-permute-start | bytes 737288 | tf_op jit(solution)/shard_map/ppermute | solution.py:558
  108.3 0.7 copy-start.22
  109.0 13.7 %collective-permute-start.21 = (bf16[160,768]{1,0:T(8,128)(2,1)}, bf16[160,768]{1,0:T(8,128)(2,1)S(1)}, u32[]{:S(2)}, u32[]{:S(2)}) collective-permute-start(bf16[160,768]{1,0:T(8,128)(2,1)} %get-tuple-element.94), channel_id=1, source_target_pairs={{0,16},{4,20},{8,24},{12,28},{16,0},{20,4},{24,8},{28,12},{1,17},{... | collective-permute-start | bytes 737288 | tf_op jit(solution)/shard_map/ppermute | solution.py:558
  111.3 43.9 %copy-start.12 = (bf16[160,768]{1,0:T(8,128)(2,1)}, bf16[160,768]{1,0:T(8,128)(2,1)S(1)}, u32[]{:S(2)}) copy-start(bf16[160,768]{1,0:T(8,128)(2,1)S(1)} %collective-permute-done.18.refs_8_.refs_10_) | copy-start | bytes 737284
  111.3 43.8 %copy-start.13 = (bf16[160,768]{1,0:T(8,128)(2,1)}, bf16[160,768]{1,0:T(8,128)(2,1)S(1)}, u32[]{:S(2)}) copy-start(bf16[160,768]{1,0:T(8,128)(2,1)S(1)} %collective-permute-done.17.refs_7_.refs_9_) | copy-start | bytes 737284
  116.0 14.7 %collective-permute-start.25 = (f32[128,512]{1,0:T(8,128)S(1)}, f32[128,512]{1,0:T(8,128)S(1)}, u32[]{:S(2)}, u32[]{:S(2)}) collective-permute-start(f32[128,512]{1,0:T(8,128)S(1)} %get-tuple-element.96.refs_7_), channel_id=1, source_target_pairs={{0,2},{2,0},{1,3},{3,1},{4,6},{6,4},{5,7},{7,5},{8,10},{10,8},{9,1... | collective-permute-start | bytes 786440 | tf_op jit(solution)/shard_map/ppermute | solution.py:552
  121.0 9.0 %collective-permute-start.20 = (bf16[160,768]{1,0:T(8,128)(2,1)}, bf16[160,768]{1,0:T(8,128)(2,1)S(1)}, u32[]{:S(2)}, u32[]{:S(2)}) collective-permute-start(bf16[160,768]{1,0:T(8,128)(2,1)} %collective-permute-done.19), channel_id=1, source_target_pairs={{0,4},{4,0},{8,12},{12,8},{16,20},{20,16},{24,28},{28,24},{1,5},{5... | collective-permute-start | bytes 737288 | tf_op jit(solution)/shard_map/ppermute | solution.py:558
  122.6 11.8 %collective-permute-start.22 = (bf16[160,768]{1,0:T(8,128)(2,1)S(1)}, bf16[160,768]{1,0:T(8,128)(2,1)S(1)}, u32[]{:S(2)}, u32[]{:S(2)}) collective-permute-start(bf16[160,768]{1,0:T(8,128)(2,1)S(1)} %collective-permute-done.21), channel_id=1, source_target_pairs={{0,4},{4,0},{8,12},{12,8},{16,20},{20,16},{24,28},{28,24},{1,5},{5... | collective-permute-start | bytes 737288 | tf_op jit(solution)/shard_map/ppermute | solution.py:558
  123.8 5.0 %collective-permute-start.13 = (bf16[8,64,128]{2,1,0:T(8,128)(2,1)S(1)}, bf16[8,64,128]{2,1,0:T(8,128)(2,1)S(1)}, u32[]{:S(2)}, u32[]{:S(2)}) collective-permute-start(bf16[8,64,128]{2,1,0:T(8,128)(2,1)S(1)} %all-to-all-done.refs_6_.refs_1_), channel_id=1, source_target_pairs={{0,2},{2,0},{1,3},{3,1},{4,6},{6,4},{5,7},{7,5},{8,10},{10,8},{9,1... | collective-permute-start | bytes 393224 | tf_op jit(solution)/shard_map/ppermute | solution.py:552
  125.6 13.6 %collective-permute-start.23 = (bf16[160,768]{1,0:T(8,128)(2,1)}, bf16[160,768]{1,0:T(8,128)(2,1)}, u32[]{:S(2)}, u32[]{:S(2)}) collective-permute-start(bf16[160,768]{1,0:T(8,128)(2,1)} %copy-done.22), channel_id=1, source_target_pairs={{0,24},{4,28},{8,16},{12,20},{16,8},{20,12},{24,0},{28,4},{1,25},{... | collective-permute-start | bytes 737288 | tf_op jit(solution)/shard_map/ppermute | solution.py:558
  130.0 25.1 %copy-start.10 = (bf16[160,768]{1,0:T(8,128)(2,1)}, bf16[160,768]{1,0:T(8,128)(2,1)S(1)}, u32[]{:S(2)}) copy-start(bf16[160,768]{1,0:T(8,128)(2,1)S(1)} %collective-permute-done.20.refs_4_.refs_11_) | copy-start | bytes 737284
  134.4 20.8 %copy-start.14 = (bf16[160,768]{1,0:T(8,128)(2,1)}, bf16[160,768]{1,0:T(8,128)(2,1)S(1)}, u32[]{:S(2)}) copy-start(bf16[160,768]{1,0:T(8,128)(2,1)S(1)} %collective-permute-done.22.refs_10_.refs_13_) | copy-start | bytes 737284
  139.1 8.7 %collective-permute-start.26 = (bf16[8,32,768]{2,1,0:T(8,128)(2,1)S(1)}, bf16[8,32,768]{2,1,0:T(8,128)(2,1)S(1)}, u32[]{:S(2)}, u32[]{:S(2)}) collective-permute-start(bf16[8,32,768]{2,1,0:T(8,128)(2,1)S(1)} %get-tuple-element.99), channel_id=1, source_target_pairs={{0,1},{1,0},{2,3},{3,2},{4,5},{5,4},{6,7},{7,6},{8,9},{9,8},{10,11... | collective-permute-start | bytes 1179656 | tf_op jit(solution)/shard_map/ppermute | solution.py:561
  139.2 8.6 %collective-permute-start.24 = (bf16[160,768]{1,0:T(8,128)(2,1)}, bf16[160,768]{1,0:T(8,128)(2,1)S(1)}, u32[]{:S(2)}, u32[]{:S(2)}) collective-permute-start(bf16[160,768]{1,0:T(8,128)(2,1)} %collective-permute-done.23), channel_id=1, source_target_pairs={{0,4},{4,0},{8,12},{12,8},{16,20},{20,16},{24,28},{28,24},{1,5},{5... | collective-permute-start | bytes 737288 | tf_op jit(solution)/shard_map/ppermute | solution.py:558
  147.8 7.4 %copy-start.15 = (bf16[160,768]{1,0:T(8,128)(2,1)}, bf16[160,768]{1,0:T(8,128)(2,1)S(1)}, u32[]{:S(2)}) copy-start(bf16[160,768]{1,0:T(8,128)(2,1)S(1)} %collective-permute-done.24.refs_5_.refs_15_) | copy-start | bytes 737284
  148.4 0.8 copy-start.17
  149.3 19.2 %all-to-all-start.1 = ((bf16[8,32,1024]{2,1,0:T(8,128)(2,1)}), bf16[8,32,1024]{2,1,0:T(8,128)(2,1)S(1)}, u32[]{:S(2)}, u32[]{:S(2)}) async-start(bf16[8,32,1024]{2,1,0:T(8,128)(2,1)} %copy-done.17), calls=%async_computation.1 | async-start | bytes 1048576 | tf_op jit(solution)/shard_map/all_to_all | solution.py:566
  163.0 4.3 %collective-permute-start.27 = (f32[128,8]{1,0:T(8,128)S(1)}, f32[128,8]{1,0:T(8,128)S(1)}, u32[]{:S(2)}, u32[]{:S(2)}) collective-permute-start(f32[128,8]{1,0:T(8,128)S(1)} %get-tuple-element.104), channel_id=1, source_target_pairs={{0,2},{2,0},{1,3},{3,1},{4,6},{6,4},{5,7},{7,5},{8,10},{10,8},{9,1... | collective-permute-start | bytes 12296 | tf_op jit(solution)/shard_map/ppermute | solution.py:552
  172.8 1.5 collective-permute-start.28

commit v19 on v17

--- a/solution.py
+++ b/solution.py
@@ -578,10 +578,10 @@
     seconds = [second[0], swap(second[0])]
 
     if groups == 8:
-        batches = [(0, 1), (2, 4), (6, 3), (5, 7)]
+        batches = [(0, 1), (2, 4), (6, 5), (3, 7)]
         steps = [("multiply", 0), ("gate", 4), ("multiply", 1), ("total", 0), ("total", 1)]
         steps += [("multiply", 2), ("multiply", 3), ("total", 2)]
-        early = {("total", 0): 3, ("multiply", 2): 5}
+        early = {("total", 0): 5, ("multiply", 2): 3}
     else:
         batches = [(o, o + 1) for o in range(0, groups, 2)]
         steps = [("multiply", 0)]

time: 175 us -> 179 us (1.023)
  waiting for transfers between devices: 58.4 us -> 60.2 us
  transfers between devices with their start and end apart: 32 -> 32, of which waited for: 16 -> 18; matrix products, arithmetic and copies ran while one was open for 1% -> 1% of each run, Pallas kernels for 35% -> 35%
where the time goes in v19:
time: 179 us; the launch traced here: 176 us
  Pallas kernels  65.8 us (37%)
  waiting for transfers between devices  60.2 us (34%)
  starting transfers between devices  43.5 us (24%)
  local copies, waits for them, and re-layouts  4.65 us (3%)
    pallas_call x18, Pallas kernels, call(): pl.pallas_call(ordered, grid=grid, in_specs=[SMEM, *in_specs] + [ANY] * l...  65.8 us
    ppermute x18, waiting for transfers between devices, flip(): return lax.ppermute(x, 'ep', [(i, i ^ mask) for i in range(groups)])  42.3 us
    ppermute x18, starting transfers between devices, flip(): return lax.ppermute(x, 'ep', [(i, i ^ mask) for i in range(groups)])  23 us
    ppermute x7, waiting for transfers between devices, turn(): lax.ppermute(x, 'rep', [(r, (r + offset) % shares) for r in range(shares)])  14.3 us
    all_to_all x2, starting transfers between devices, exchange(): return lax.all_to_all(x, axes, split_axis=0, concat_axis=0, tiled=True)  13.5 us
    ppermute x7, starting transfers between devices, turn(): lax.ppermute(x, 'rep', [(r, (r + offset) % shares) for r in range(shares)])  6.87 us
    unnamed x53, local copies, waits for them, and re-layouts  4.65 us
  transfers between devices with their start and end apart: 32, of which 18 were waited for; matrix products, arithmetic and copies ran while one was open for 1% of the time, Pallas kernels for 35%

profile of v19, /device:TPU:8, one launch (start us, length us, event | category | flops | bytes accessed | tf_op | source)
XLA Modules:
  0.0 176.0 jit_solution(6016808629846747309)
XLA Ops:
  0.8 0.8 copy-done.19
  1.6 0.7 copy-done.20
  2.3 1.1 pack_block.1
  3.4 1.6 collective-permute-start
  5.0 2.6 %collective-permute-start.4 = (bf16[128,2304]{1,0:T(8,128)(2,1)S(1)}, bf16[128,2304]{1,0:T(8,128)(2,1)S(1)}, u32[]{:S(2)}, u32[]{:S(2)}) collective-permute-start(bf16[128,2304]{1,0:T(8,128)(2,1)S(1)} %get-tuple-element.57.refs_1_.refs_5_.refs_2_), channel_id=1, source_target_pairs={{0,16},{4,20},{8,24},{12,28},{16,0},{20,4},{24,8},{28,12},{1,17},{... | collective-permute-start | bytes 1769480 | tf_op jit(solution)/shard_map/ppermute | solution.py:558
  8.0 3.4 %load_matrix.1 = (bf16[1536,2048]{1,0:T(8,128)(2,1)S(1)}, f32[8,128]{1,0:T(8,128)}) custom-call(s32[3]{0:T(128)S(1)} %pad_add_fusion.refs_0_, bf16[1536,2048]{1,0:T(8,128)(2,1)} %bitcast.33, f32[8,128]{1,0:T(8,128)} %get-tuple-element.58.refs_2_), custom_call_target="tpu_custom_call" | custom-call | flops 1 | bytes 1 | tf_op jit(solution)/shard_map/load_matrix/pallas_call | solution.py:53
  11.5 7.7 %collective-permute-done.refs_2_.refs_6_.refs_3_ = bf16[128,2304]{1,0:T(8,128)(2,1)S(1)} collective-permute-done((bf16[128,2304]{1,0:T(8,128)(2,1)S(1)}, bf16[128,2304]{1,0:T(8,128)(2,1)S(1)}, u32[]{:S(2)}, u32[]{:S(2)}) %collective-permute-start) | collective-permute-done | bytes 589856 | tf_op jit(solution)/shard_map/ppermute | solution.py:558
  19.2 8.2 %expert_rows.4 = (bf16[320,768]{1,0:T(8,128)(2,1)S(1)}, bf16[320,768]{1,0:T(8,128)(2,1)S(1)}, bf16[2,64,128]{2,1,0:T(8,128)(2,1)S(1)}, f32[8,128]{1,0:T(8,128)}) custom-call(s32[3]{0:T(128)S(1)} %pad_add_fusion.refs_0_, bf16[128,2304]{1,0:T(8,128)(2,1)S(1)} %get-tuple-element.57.refs_1_.refs_5_.refs_2_, ...), custom_call_target="tpu_custom_call" | custom-call | flops 1 | bytes 1 | tf_op jit(solution)/shard_map/expert_rows/pallas_call | solution.py:53
  27.5 5.6 %collective-permute-done.4.refs_1_ = bf16[128,2304]{1,0:T(8,128)(2,1)S(1)} collective-permute-done((bf16[128,2304]{1,0:T(8,128)(2,1)S(1)}, bf16[128,2304]{1,0:T(8,128)(2,1)S(1)}, u32[]{:S(2)}, u32[]{:S(2)}) %collective-permute-start.4) | collective-permute-done | bytes 589856 | tf_op jit(solution)/shard_map/ppermute | solution.py:558
  33.1 0.5 gate.1
  33.6 1.5 collective-permute-start.5
  35.6 1.6 collective-permute-start.9
  37.2 1.5 collective-permute-start.8
  38.7 8.0 %expert_rows.5 = (bf16[320,768]{1,0:T(8,128)(2,1)S(1)}, bf16[320,768]{1,0:T(8,128)(2,1)S(1)}, bf16[2,64,128]{2,1,0:T(8,128)(2,1)S(1)}, f32[8,128]{1,0:T(8,128)}) custom-call(s32[3]{0:T(128)S(1)} %pad_add_fusion.refs_0_, bf16[128,2304]{1,0:T(8,128)(2,1)S(1)} %collective-permute-done.3.refs_1_.refs_7_.refs_4_, ...), custom_call_target="tpu_custom_call" | custom-call | flops 1 | bytes 1 | tf_op jit(solution)/shard_map/expert_rows/pallas_call | solution.py:53
  46.7 0.6 collective-permute-start.7
  47.3 1.7 collective-permute-done.5.refs_1_.refs_9_.refs_6_
  49.0 0.5 collective-permute-start.10
  50.0 1.4 collective-permute-done.6.refs_4_.refs_2_.refs_10_.refs_7_
  51.4 1.3 share_sum.4
  52.7 6.6 %collective-permute-done.7.refs_2_ = bf16[320,768]{1,0:T(8,128)(2,1)S(1)} collective-permute-done((bf16[320,768]{1,0:T(8,128)(2,1)S(1)}, bf16[320,768]{1,0:T(8,128)(2,1)S(1)}, u32[]{:S(2)}, u32[]{:S(2)}) %collective-permute-start.7) | collective-permute-done | bytes 491552 | tf_op jit(solution)/shard_map/ppermute | solution.py:552
  59.3 1.3 share_sum.5
  60.6 3.4 %collective-permute-done.9.refs_8_.refs_1_.refs_11_ = bf16[128,2304]{1,0:T(8,128)(2,1)S(1)} collective-permute-done((bf16[128,2304]{1,0:T(8,128)(2,1)S(1)}, bf16[128,2304]{1,0:T(8,128)(2,1)S(1)}, u32[]{:S(2)}, u32[]{:S(2)}) %collective-permute-start.9) | collective-permute-done | bytes 589856 | tf_op jit(solution)/shard_map/ppermute | solution.py:558
  64.1 8.4 %expert_rows.6 = (bf16[320,768]{1,0:T(8,128)(2,1)S(1)}, bf16[320,768]{1,0:T(8,128)(2,1)S(1)}, bf16[2,64,128]{2,1,0:T(8,128)(2,1)S(1)}, f32[8,128]{1,0:T(8,128)}) custom-call(s32[3]{0:T(128)S(1)} %pad_add_fusion.refs_0_, bf16[128,2304]{1,0:T(8,128)(2,1)S(1)} %collective-permute-done.5.refs_1_.refs_9_.refs_6_, ...), custom_call_target="tpu_custom_call" | custom-call | flops 1 | bytes 1 | tf_op jit(solution)/shard_map/expert_rows/pallas_call | solution.py:53
  72.4 1.6 collective-permute-start.11
  74.0 0.5 collective-permute-start.16
  74.7 8.2 %expert_rows.7 = (bf16[320,768]{1,0:T(8,128)(2,1)S(1)}, bf16[320,768]{1,0:T(8,128)(2,1)S(1)}, bf16[2,64,128]{2,1,0:T(8,128)(2,1)S(1)}, f32[8,128]{1,0:T(8,128)}) custom-call(s32[3]{0:T(128)S(1)} %pad_add_fusion.refs_0_, bf16[128,2304]{1,0:T(8,128)(2,1)S(1)} %collective-permute-done.9.refs_8_.refs_1_.refs_11_, ...), custom_call_target="tpu_custom_call" | custom-call | flops 1 | bytes 1 | tf_op jit(solution)/shard_map/expert_rows/pallas_call | solution.py:53
  82.9 1.6 collective-permute-start.14
  84.5 3.2 %collective-permute-start.17 = (bf16[160,768]{1,0:T(8,128)(2,1)S(1)}, bf16[160,768]{1,0:T(8,128)(2,1)S(1)}, u32[]{:S(2)}, u32[]{:S(2)}) collective-permute-start(bf16[160,768]{1,0:T(8,128)(2,1)S(1)} %collective-permute-done.16), channel_id=1, source_target_pairs={{0,24},{4,28},{8,16},{12,20},{16,8},{20,12},{24,0},{28,4},{1,25},{... | collective-permute-start | bytes 737288 | tf_op jit(solution)/shard_map/ppermute | solution.py:558
  87.7 1.3 share_sum.6
  89.0 0.7 copy-done.22
  89.7 1.7 collect_blocks.1
  91.4 1.9 %collective-permute-start.19 = (bf16[160,768]{1,0:T(8,128)(2,1)}, bf16[160,768]{1,0:T(8,128)(2,1)S(1)}, u32[]{:S(2)}, u32[]{:S(2)}) collective-permute-start(bf16[160,768]{1,0:T(8,128)(2,1)} %get-tuple-element.89), channel_id=1, source_target_pairs={{0,8},{4,12},{8,0},{12,4},{16,24},{20,28},{24,16},{28,20},{1,9},{5... | collective-permute-start | bytes 737288 | tf_op jit(solution)/shard_map/ppermute | solution.py:558
  93.3 10.0 %collective-permute-done.17.refs_5_.refs_12_ = bf16[160,768]{1,0:T(8,128)(2,1)S(1)} collective-permute-done((bf16[160,768]{1,0:T(8,128)(2,1)S(1)}, bf16[160,768]{1,0:T(8,128)(2,1)S(1)}, u32[]{:S(2)}, u32[]{:S(2)}) %collective-permute-start.17) | collective-permute-done | bytes 245792 | tf_op jit(solution)/shard_map/ppermute | solution.py:558
  103.9 6.2 %all-to-all-start = ((bf16[8,64,128]{2,1,0:T(8,128)(2,1)}), bf16[8,64,128]{2,1,0:T(8,128)(2,1)S(1)}, u32[]{:S(2)}, u32[]{:S(2)}) async-start(bf16[8,64,128]{2,1,0:T(8,128)(2,1)} %get-tuple-element.80), calls=%async_computation | async-start | bytes 262144 | tf_op jit(solution)/shard_map/all_to_all | solution.py:566
  110.1 2.4 %collective-permute-start.20 = (bf16[160,768]{1,0:T(8,128)(2,1)}, bf16[160,768]{1,0:T(8,128)(2,1)}, u32[]{:S(2)}, u32[]{:S(2)}) collective-permute-start(bf16[160,768]{1,0:T(8,128)(2,1)} %copy-done.22), channel_id=1, source_target_pairs={{0,16},{4,20},{8,24},{12,28},{16,0},{20,4},{24,8},{28,12},{1,17},{... | collective-permute-start | bytes 737288 | tf_op jit(solution)/shard_map/ppermute | solution.py:558
  112.5 0.7 share_sum.7
  113.2 0.7 copy-done.23
  113.9 0.6 collective-permute-start.22
  114.6 1.9 %all-to-all-done.refs_6_.refs_1_ = bf16[8,64,128]{2,1,0:T(8,128)(2,1)S(1)} async-done(((bf16[8,64,128]{2,1,0:T(8,128)(2,1)}), bf16[8,64,128]{2,1,0:T(8,128)(2,1)S(1)}, u32[]{:S(2)}, u32[]{:S(2)}) %all-to-all-start) | async-done | bytes 131104 | tf_op jit(solution)/shard_map/all_to_all | solution.py:566
  116.5 3.6 %lowrank_hid.1 = (f32[128,512]{1,0:T(8,128)S(1)}, f32[8,128]{1,0:T(8,128)}) custom-call(s32[3]{0:T(128)S(1)} %pad_add_fusion.refs_0_, s32[128,8]{1,0:T(8,128)S(1)} %copy.17.refs_1_.refs_5_.refs_2_, bf16[1024,768]{1,0:T(8,128)(2,1)} %bitcast.29, bf16[256,768]{1,0:T(8,128)(2,1)S(1)} %bitcast.23, bf16[256,768]{1,0:T(8,128)(2,1)S(1)} %bitcast.25, ...), custom_call_target="tpu_custom_call" | custom-call | flops 1 | bytes 1 | tf_op jit(solution)/shard_map/lowrank_hid/pallas_call | solution.py:53
  120.0 0.6 collective-permute-start.26
  120.6 1.2 collective-permute-done.20
  121.8 1.5 collective-permute-start.21
  123.3 0.7 collective-permute-start.23
  124.0 0.5 collective-permute-start.12
  124.5 1.2 collective-permute-start.24
  125.8 3.4 %collective-permute-done.12.refs_2_ = bf16[8,64,128]{2,1,0:T(8,128)(2,1)S(1)} collective-permute-done((bf16[8,64,128]{2,1,0:T(8,128)(2,1)S(1)}, bf16[8,64,128]{2,1,0:T(8,128)(2,1)S(1)}, u32[]{:S(2)}, u32[]{:S(2)}) %collective-permute-start.12) | collective-permute-done | bytes 131104 | tf_op jit(solution)/shard_map/ppermute | solution.py:552
  129.3 1.7 collective-permute-done.21.refs_4_.refs_13_
  130.9 0.7 low_dense.1
  131.6 2.6 %collective-permute-done.23.refs_10_.refs_11_ = bf16[160,768]{1,0:T(8,128)(2,1)S(1)} collective-permute-done((bf16[160,768]{1,0:T(8,128)(2,1)}, bf16[160,768]{1,0:T(8,128)(2,1)S(1)}, u32[]{:S(2)}, u32[]{:S(2)}) %collective-permute-start.23) | collective-permute-done | bytes 245792 | tf_op jit(solution)/shard_map/ppermute | solution.py:558
  134.2 4.7 %first_grad.1 = (f32[8,32,768]{2,1,0:T(8,128)S(1)}, bf16[8,32,768]{2,1,0:T(8,128)(2,1)S(1)}, bf16[8,32,256]{2,1,0:T(8,128)(2,1)S(1)}, f32[8,128]{1,0:T(8,128)}) custom-call(s32[3]{0:T(128)S(1)} %pad_add_fusion.refs_0_, s32[128,8]{1,0:T(8,128)S(1)} %copy.17.refs_1_.refs_5_.refs_2_, bf16[128,8]{1,0:T(8,128)(2,1)S(1)} %copy.19.refs_2_.refs_6_.refs_3_, ...), custom_call_target="tpu_custom_call" | custom-call | flops 1 | bytes 1 | tf_op jit(solution)/shard_map/first_grad/pallas_call | solution.py:53
  139.0 1.8 %collective-permute-start.25 = (bf16[160,768]{1,0:T(8,128)(2,1)}, bf16[160,768]{1,0:T(8,128)(2,1)S(1)}, u32[]{:S(2)}, u32[]{:S(2)}) collective-permute-start(bf16[160,768]{1,0:T(8,128)(2,1)} %collective-permute-done.24), channel_id=1, source_target_pairs={{0,4},{4,0},{8,12},{12,8},{16,20},{20,16},{24,28},{28,24},{1,5},{5... | collective-permute-start | bytes 737288 | tf_op jit(solution)/shard_map/ppermute | solution.py:558
  140.8 6.8 %collective-permute-done.25.refs_5_.refs_15_ = bf16[160,768]{1,0:T(8,128)(2,1)S(1)} collective-permute-done((bf16[160,768]{1,0:T(8,128)(2,1)}, bf16[160,768]{1,0:T(8,128)(2,1)S(1)}, u32[]{:S(2)}, u32[]{:S(2)}) %collective-permute-start.25) | collective-permute-done | bytes 245792 | tf_op jit(solution)/shard_map/ppermute | solution.py:558
  147.6 0.6 first_sum.1
  148.2 0.8 copy-done.17
  149.0 7.3 %all-to-all-start.1 = ((bf16[8,32,1024]{2,1,0:T(8,128)(2,1)}), bf16[8,32,1024]{2,1,0:T(8,128)(2,1)S(1)}, u32[]{:S(2)}, u32[]{:S(2)}) async-start(bf16[8,32,1024]{2,1,0:T(8,128)(2,1)} %copy-done.17), calls=%async_computation.1 | async-start | bytes 1048576 | tf_op jit(solution)/shard_map/all_to_all | solution.py:566
  156.4 7.9 %finish.1 = (bf16[1024,768]{1,0:T(8,128)(2,1)}, f32[128,8]{1,0:T(8,128)S(1)}, f32[8,128]{1,0:T(8,128)}) custom-call(s32[3]{0:T(128)S(1)} %pad_add_fusion.refs_0_, s32[128,8]{1,0:T(8,128)S(1)} %copy.17.refs_1_.refs_5_.refs_2_, s32[128,8]{1,0:T(8,128)S(1)} %copy.17.refs_1_.refs_5_.refs_2_, bf16[128,8]{1,0:T(8,128)(2,1)S(1)} %copy.19.refs_2_.refs_6_.refs_3_, ...), custom_call_target="tpu_custom_call" | custom-call | flops 1 | bytes 20000000 | tf_op jit(solution)/shard_map/finish/pallas_call | solution.py:53
  164.2 0.5 collective-permute-start.28
  164.8 3.7 %collective-permute-done.28.refs_11_ = f32[128,8]{1,0:T(8,128)S(1)} collective-permute-done((f32[128,8]{1,0:T(8,128)S(1)}, f32[128,8]{1,0:T(8,128)S(1)}, u32[]{:S(2)}, u32[]{:S(2)}) %collective-permute-start.28) | collective-permute-done | bytes 4128 | tf_op jit(solution)/shard_map/ppermute | solution.py:552
  168.5 0.9 all-to-all-done.1.refs_1_
  169.4 4.4 %second_grad.1 = (f32[32,2048]{1,0:T(8,128)S(1)}, f32[32,2048]{1,0:T(8,128)S(1)}, f32[32,768]{1,0:T(8,128)}, f32[8,128]{1,0:T(8,128)}) custom-call(s32[3]{0:T(128)S(1)} %pad_add_fusion.refs_0_, bf16[8,32,1024]{2,1,0:T(8,128)(2,1)S(1)} %all-to-all-done.1.refs_1_, bf16[128,2304]{1,0:T(8,128)(2,1)} %copy-done.3, bf16[128,2304]{1,0:T(8,128)(2,1)} %copy-done.4, ...), custom_call_target="tpu_custom_call" | custom-call | flops 1 | bytes 1 | tf_op jit(solution)/shard_map/second_grad/pallas_call | solution.py:53
  173.8 0.7 copy.20
  174.4 0.8 collective-permute-done.29
  175.3 0.7 add_bitcast_fusion
  (74 shorter events, 2.7 us)
Async XLA Ops:
  0.6 18.6 %copy-start.8 = (bf16[1,32,2048]{2,1,0:T(8,128)(2,1)S(1)}, bf16[1,32,2048]{2,1,0:T(8,128)(2,1)}, u32[]{:S(2)}) copy-start(bf16[1,32,2048]{2,1,0:T(8,128)(2,1)} %param.13) | copy-start | bytes 393220
  0.6 18.6 %collective-permute-start.2 = (bf16[1536,2048]{1,0:T(8,128)(2,1)}, bf16[1536,2048]{1,0:T(8,128)(2,1)}, u32[]{:S(2)}, u32[]{:S(2)}) collective-permute-start(bf16[1536,2048]{1,0:T(8,128)(2,1)} %bitcast.32), channel_id=1, source_target_pairs={{0,1},{1,0},{2,3},{3,2},{4,5},{5,4},{6,7},{7,6},{8,9},{9,8},{10,11... | collective-permute-start | bytes 18874376 | tf_op jit(solution)/shard_map/ppermute | solution.py:561
  0.8 0.8 copy-start.19
  1.6 0.7 copy-start.20
  3.4 24.0 %copy-start.3 = (bf16[128,2304]{1,0:T(8,128)(2,1)}, bf16[128,2304]{1,0:T(8,128)(2,1)S(1)}, u32[]{:S(2)}) copy-start(bf16[128,2304]{1,0:T(8,128)(2,1)S(1)} %get-tuple-element.57.refs_1_.refs_5_.refs_2_) | copy-start | bytes 1769476
  3.4 15.8 %collective-permute-start = (bf16[128,2304]{1,0:T(8,128)(2,1)S(1)}, bf16[128,2304]{1,0:T(8,128)(2,1)S(1)}, u32[]{:S(2)}, u32[]{:S(2)}) collective-permute-start(bf16[128,2304]{1,0:T(8,128)(2,1)S(1)} %get-tuple-element.57.refs_1_.refs_5_.refs_2_), channel_id=1, source_target_pairs={{0,4},{4,0},{8,12},{12,8},{16,20},{20,16},{24,28},{28,24},{1,5},{5... | collective-permute-start | bytes 1769480 | tf_op jit(solution)/shard_map/ppermute | solution.py:558
  5.0 28.1 %collective-permute-start.4 = (bf16[128,2304]{1,0:T(8,128)(2,1)S(1)}, bf16[128,2304]{1,0:T(8,128)(2,1)S(1)}, u32[]{:S(2)}, u32[]{:S(2)}) collective-permute-start(bf16[128,2304]{1,0:T(8,128)(2,1)S(1)} %get-tuple-element.57.refs_1_.refs_5_.refs_2_), channel_id=1, source_target_pairs={{0,16},{4,20},{8,24},{12,28},{16,0},{20,4},{24,8},{28,12},{1,17},{... | collective-permute-start | bytes 1769480 | tf_op jit(solution)/shard_map/ppermute | solution.py:558
  7.6 28.0 %collective-permute-start.3 = (bf16[128,2304]{1,0:T(8,128)(2,1)S(1)}, bf16[128,2304]{1,0:T(8,128)(2,1)S(1)}, u32[]{:S(2)}, u32[]{:S(2)}) collective-permute-start(bf16[128,2304]{1,0:T(8,128)(2,1)S(1)} %get-tuple-element.57.refs_1_.refs_5_.refs_2_), channel_id=1, source_target_pairs={{0,8},{4,12},{8,0},{12,4},{16,24},{20,28},{24,16},{28,20},{1,9},{5... | collective-permute-start | bytes 1769480 | tf_op jit(solution)/shard_map/ppermute | solution.py:558
  8.0 3.4 %collective-permute-start.1 = (bf16[32,2048]{1,0:T(8,128)(2,1)}, bf16[32,2048]{1,0:T(8,128)(2,1)S(1)}, u32[]{:S(2)}, u32[]{:S(2)}) collective-permute-start(bf16[32,2048]{1,0:T(8,128)(2,1)} %bitcast.18), channel_id=1, source_target_pairs={{0,1},{1,0},{2,3},{3,2},{4,5},{5,4},{6,7},{7,6},{8,9},{9,8},{10,11... | collective-permute-start | bytes 393224 | tf_op jit(solution)/shard_map/ppermute | solution.py:561
  19.2 8.3 %copy-start.4 = (bf16[128,2304]{1,0:T(8,128)(2,1)}, bf16[128,2304]{1,0:T(8,128)(2,1)S(1)}, u32[]{:S(2)}) copy-start(bf16[128,2304]{1,0:T(8,128)(2,1)S(1)} %collective-permute-done.refs_2_.refs_6_.refs_3_) | copy-start | bytes 1769476
  19.2 19.5 %copy-start.9 = (bf16[1,32,2048]{2,1,0:T(8,128)(2,1)S(1)}, bf16[1,32,2048]{2,1,0:T(8,128)(2,1)}, u32[]{:S(2)}) copy-start(bf16[1,32,2048]{2,1,0:T(8,128)(2,1)} %param.13) | copy-start | bytes 393220
  33.6 13.0 %copy-start.2 = (bf16[128,2304]{1,0:T(8,128)(2,1)}, bf16[128,2304]{1,0:T(8,128)(2,1)S(1)}, u32[]{:S(2)}) copy-start(bf16[128,2304]{1,0:T(8,128)(2,1)S(1)} %get-tuple-element.63.refs_2_.refs_8_.refs_5_) | copy-start | bytes 1769476
  33.6 15.3 %collective-permute-start.5 = (bf16[128,2304]{1,0:T(8,128)(2,1)S(1)}, bf16[128,2304]{1,0:T(8,128)(2,1)S(1)}, u32[]{:S(2)}, u32[]{:S(2)}) collective-permute-start(bf16[128,2304]{1,0:T(8,128)(2,1)S(1)} %get-tuple-element.63.refs_2_.refs_8_.refs_5_), channel_id=1, source_target_pairs={{0,8},{4,12},{8,0},{12,4},{16,24},{20,28},{24,16},{28,20},{1,9},{5... | collective-permute-start | bytes 1769480 | tf_op jit(solution)/shard_map/ppermute | solution.py:558
  35.1 16.3 %collective-permute-start.6 = (bf16[128,2304]{1,0:T(8,128)(2,1)S(1)}, bf16[128,2304]{1,0:T(8,128)(2,1)S(1)}, u32[]{:S(2)}, u32[]{:S(2)}) collective-permute-start(bf16[128,2304]{1,0:T(8,128)(2,1)S(1)} %get-tuple-element.63.refs_2_.refs_8_.refs_5_), channel_id=1, source_target_pairs={{0,4},{4,0},{8,12},{12,8},{16,20},{20,16},{24,28},{28,24},{1,5},{5... | collective-permute-start | bytes 1769480 | tf_op jit(solution)/shard_map/ppermute | solution.py:558
  35.6 11.1 %copy-start.5 = (bf16[128,2304]{1,0:T(8,128)(2,1)}, bf16[128,2304]{1,0:T(8,128)(2,1)S(1)}, u32[]{:S(2)}) copy-start(bf16[128,2304]{1,0:T(8,128)(2,1)S(1)} %collective-permute-done.3.refs_1_.refs_7_.refs_4_) | copy-start | bytes 1769476
  35.6 28.4 %collective-permute-start.9 = (bf16[128,2304]{1,0:T(8,128)(2,1)S(1)}, bf16[128,2304]{1,0:T(8,128)(2,1)S(1)}, u32[]{:S(2)}, u32[]{:S(2)}) collective-permute-start(bf16[128,2304]{1,0:T(8,128)(2,1)S(1)} %collective-permute-done.3.refs_1_.refs_7_.refs_4_), channel_id=1, source_target_pairs={{0,4},{4,0},{8,12},{12,8},{16,20},{20,16},{24,28},{28,24},{1,5},{5... | collective-permute-start | bytes 1769480 | tf_op jit(solution)/shard_map/ppermute | solution.py:558
  37.2 12.8 %collective-permute-start.8 = (bf16[320,768]{1,0:T(8,128)(2,1)S(1)}, bf16[320,768]{1,0:T(8,128)(2,1)S(1)}, u32[]{:S(2)}, u32[]{:S(2)}) collective-permute-start(bf16[320,768]{1,0:T(8,128)(2,1)S(1)} %get-tuple-element.69), channel_id=1, source_target_pairs={{0,2},{2,0},{1,3},{3,1},{4,6},{6,4},{5,7},{7,5},{8,10},{10,8},{9,1... | collective-permute-start | bytes 1474568 | tf_op jit(solution)/shard_map/ppermute | solution.py:552
  46.7 12.6 %collective-permute-start.7 = (bf16[320,768]{1,0:T(8,128)(2,1)S(1)}, bf16[320,768]{1,0:T(8,128)(2,1)S(1)}, u32[]{:S(2)}, u32[]{:S(2)}) collective-permute-start(bf16[320,768]{1,0:T(8,128)(2,1)S(1)} %get-tuple-element.67), channel_id=1, source_target_pairs={{0,2},{2,0},{1,3},{3,1},{4,6},{6,4},{5,7},{7,5},{8,10},{10,8},{9,1... | collective-permute-start | bytes 1474568 | tf_op jit(solution)/shard_map/ppermute | solution.py:552
  49.0 23.5 %copy-start.6 = (bf16[128,2304]{1,0:T(8,128)(2,1)}, bf16[128,2304]{1,0:T(8,128)(2,1)S(1)}, u32[]{:S(2)}) copy-start(bf16[128,2304]{1,0:T(8,128)(2,1)S(1)} %collective-permute-done.5.refs_1_.refs_9_.refs_6_) | copy-start | bytes 1769476
  49.0 25.7 %collective-permute-start.10 = (bf16[128,2304]{1,0:T(8,128)(2,1)S(1)}, bf16[128,2304]{1,0:T(8,128)(2,1)S(1)}, u32[]{:S(2)}, u32[]{:S(2)}) collective-permute-start(bf16[128,2304]{1,0:T(8,128)(2,1)S(1)} %collective-permute-done.5.refs_1_.refs_9_.refs_6_), channel_id=1, source_target_pairs={{0,4},{4,0},{8,12},{12,8},{16,20},{20,16},{24,28},{28,24},{1,5},{5... | collective-permute-start | bytes 1769480 | tf_op jit(solution)/shard_map/ppermute | solution.py:558
  51.4 21.0 %copy-start.1 = (bf16[128,2304]{1,0:T(8,128)(2,1)}, bf16[128,2304]{1,0:T(8,128)(2,1)S(1)}, u32[]{:S(2)}) copy-start(bf16[128,2304]{1,0:T(8,128)(2,1)S(1)} %collective-permute-done.6.refs_4_.refs_2_.refs_10_.refs_7_) | copy-start | bytes 1769476
  52.7 11.3 %copy-start.18 = (bf16[160,768]{1,0:T(8,128)(2,1)}, bf16[160,768]{1,0:T(8,128)(2,1)S(1)}, u32[]{:S(2)}) copy-start(bf16[160,768]{1,0:T(8,128)(2,1)S(1)} %get-tuple-element.93.refs_8_) | copy-start | bytes 737284
  64.0 10.7 %copy-start = (bf16[128,2304]{1,0:T(8,128)(2,1)}, bf16[128,2304]{1,0:T(8,128)(2,1)S(1)}, u32[]{:S(2)}) copy-start(bf16[128,2304]{1,0:T(8,128)(2,1)S(1)} %collective-permute-done.9.refs_8_.refs_1_.refs_11_) | copy-start | bytes 1769476
  72.4 15.3 %collective-permute-start.11 = (bf16[320,768]{1,0:T(8,128)(2,1)S(1)}, bf16[320,768]{1,0:T(8,128)(2,1)S(1)}, u32[]{:S(2)}, u32[]{:S(2)}) collective-permute-start(bf16[320,768]{1,0:T(8,128)(2,1)S(1)} %get-tuple-element.77), channel_id=1, source_target_pairs={{0,2},{2,0},{1,3},{3,1},{4,6},{6,4},{5,7},{7,5},{8,10},{10,8},{9,1... | collective-permute-start | bytes 1474568 | tf_op jit(solution)/shard_map/ppermute | solution.py:552
  74.0 10.5 %collective-permute-start.16 = (bf16[160,768]{1,0:T(8,128)(2,1)S(1)}, bf16[160,768]{1,0:T(8,128)(2,1)S(1)}, u32[]{:S(2)}, u32[]{:S(2)}) collective-permute-start(bf16[160,768]{1,0:T(8,128)(2,1)S(1)} %get-tuple-element.86), channel_id=1, source_target_pairs={{0,8},{4,12},{8,0},{12,4},{16,24},{20,28},{24,16},{28,20},{1,9},{5... | collective-permute-start | bytes 737288 | tf_op jit(solution)/shard_map/ppermute | solution.py:558
  74.7 8.2 %copy-start.7 = (bf16[128,2304]{1,0:T(8,128)(2,1)}, bf16[128,2304]{1,0:T(8,128)(2,1)S(1)}, u32[]{:S(2)}) copy-start(bf16[128,2304]{1,0:T(8,128)(2,1)S(1)} %collective-permute-done.10.refs_2_.refs_12_.refs_9_) | copy-start | bytes 1769476
  82.9 31.5 %copy-start.21 = (s32[128,8]{0,1:T(8,128)S(1)}, s32[128,8]{0,1:T(8,128)}, u32[]{:S(2)}) copy-start(s32[128,8]{0,1:T(8,128)} %param.9) | copy-start | bytes 12292
  82.9 42.8 %copy-start.24 = (bf16[128,8]{0,1:T(8,128)(2,1)S(1)}, bf16[128,8]{0,1:T(8,128)(2,1)}, u32[]{:S(2)}) copy-start(bf16[128,8]{0,1:T(8,128)(2,1)} %param.10) | copy-start | bytes 6148
  82.9 29.6 %collective-permute-start.14 = (bf16[320,768]{1,0:T(8,128)(2,1)S(1)}, bf16[320,768]{1,0:T(8,128)(2,1)S(1)}, u32[]{:S(2)}, u32[]{:S(2)}) collective-permute-start(bf16[320,768]{1,0:T(8,128)(2,1)S(1)} %get-tuple-element.83), channel_id=1, source_target_pairs={{0,2},{2,0},{1,3},{3,1},{4,6},{6,4},{5,7},{7,5},{8,10},{10,8},{9,1... | collective-permute-start | bytes 1474568 | tf_op jit(solution)/shard_map/ppermute | solution.py:552
  84.5 18.9 %collective-permute-start.17 = (bf16[160,768]{1,0:T(8,128)(2,1)S(1)}, bf16[160,768]{1,0:T(8,128)(2,1)S(1)}, u32[]{:S(2)}, u32[]{:S(2)}) collective-permute-start(bf16[160,768]{1,0:T(8,128)(2,1)S(1)} %collective-permute-done.16), channel_id=1, source_target_pairs={{0,24},{4,28},{8,16},{12,20},{16,8},{20,12},{24,0},{28,4},{1,25},{... | collective-permute-start | bytes 737288 | tf_op jit(solution)/shard_map/ppermute | solution.py:558
  89.0 0.7 copy-start.22
  89.7 20.4 %collective-permute-start.15 = (bf16[160,768]{1,0:T(8,128)(2,1)}, bf16[160,768]{1,0:T(8,128)(2,1)S(1)}, u32[]{:S(2)}, u32[]{:S(2)}) collective-permute-start(bf16[160,768]{1,0:T(8,128)(2,1)} %get-tuple-element.85), channel_id=1, source_target_pairs={{0,24},{4,28},{8,16},{12,20},{16,8},{20,12},{24,0},{28,4},{1,25},{... | collective-permute-start | bytes 737288 | tf_op jit(solution)/shard_map/ppermute | solution.py:558
  91.4 25.0 %collective-permute-start.13 = (bf16[8,32,768]{2,1,0:T(8,128)(2,1)S(1)}, bf16[8,32,768]{2,1,0:T(8,128)(2,1)S(1)}, u32[]{:S(2)}, u32[]{:S(2)}) collective-permute-start(bf16[8,32,768]{2,1,0:T(8,128)(2,1)S(1)} %get-tuple-element.81), channel_id=1, source_target_pairs={{0,1},{1,0},{2,3},{3,2},{4,5},{5,4},{6,7},{7,6},{8,9},{9,8},{10,11... | collective-permute-start | bytes 1179656 | tf_op jit(solution)/shard_map/ppermute | solution.py:561
  91.4 23.1 %collective-permute-start.19 = (bf16[160,768]{1,0:T(8,128)(2,1)}, bf16[160,768]{1,0:T(8,128)(2,1)S(1)}, u32[]{:S(2)}, u32[]{:S(2)}) collective-permute-start(bf16[160,768]{1,0:T(8,128)(2,1)} %get-tuple-element.89), channel_id=1, source_target_pairs={{0,8},{4,12},{8,0},{12,4},{16,24},{20,28},{24,16},{28,20},{1,9},{5... | collective-permute-start | bytes 737288 | tf_op jit(solution)/shard_map/ppermute | solution.py:558
  103.4 53.0 %copy-start.11 = (bf16[160,768]{1,0:T(8,128)(2,1)}, bf16[160,768]{1,0:T(8,128)(2,1)S(1)}, u32[]{:S(2)}) copy-start(bf16[160,768]{1,0:T(8,128)(2,1)S(1)} %collective-permute-done.17.refs_5_.refs_12_) | copy-start | bytes 737284
  103.4 11.2 %collective-permute-start.18 = (bf16[160,768]{1,0:T(8,128)(2,1)}, bf16[160,768]{1,0:T(8,128)(2,1)S(1)}, u32[]{:S(2)}, u32[]{:S(2)}) collective-permute-start(bf16[160,768]{1,0:T(8,128)(2,1)} %get-tuple-element.88), channel_id=1, source_target_pairs={{0,4},{4,0},{8,12},{12,8},{16,20},{20,16},{24,28},{28,24},{1,5},{5... | collective-permute-start | bytes 737288 | tf_op jit(solution)/shard_map/ppermute | solution.py:558
  103.9 12.6 %all-to-all-start = ((bf16[8,64,128]{2,1,0:T(8,128)(2,1)}), bf16[8,64,128]{2,1,0:T(8,128)(2,1)S(1)}, u32[]{:S(2)}, u32[]{:S(2)}) async-start(bf16[8,64,128]{2,1,0:T(8,128)(2,1)} %get-tuple-element.80), calls=%async_computation | async-start | bytes 262144 | tf_op jit(solution)/shard_map/all_to_all | solution.py:566
  110.1 46.3 %copy-start.12 = (bf16[160,768]{1,0:T(8,128)(2,1)}, bf16[160,768]{1,0:T(8,128)(2,1)S(1)}, u32[]{:S(2)}) copy-start(bf16[160,768]{1,0:T(8,128)(2,1)S(1)} %collective-permute-done.15.refs_4_.refs_14_) | copy-start | bytes 737284
  110.1 11.8 %collective-permute-start.20 = (bf16[160,768]{1,0:T(8,128)(2,1)}, bf16[160,768]{1,0:T(8,128)(2,1)}, u32[]{:S(2)}, u32[]{:S(2)}) collective-permute-start(bf16[160,768]{1,0:T(8,128)(2,1)} %copy-done.22), channel_id=1, source_target_pairs={{0,16},{4,20},{8,24},{12,28},{16,0},{20,4},{24,8},{28,12},{1,17},{... | collective-permute-start | bytes 737288 | tf_op jit(solution)/shard_map/ppermute | solution.py:558
  113.2 0.7 copy-start.23
  113.9 9.4 %collective-permute-start.22 = (bf16[160,768]{1,0:T(8,128)(2,1)S(1)}, bf16[160,768]{1,0:T(8,128)(2,1)}, u32[]{:S(2)}, u32[]{:S(2)}) collective-permute-start(bf16[160,768]{1,0:T(8,128)(2,1)S(1)} %get-tuple-element.94), channel_id=1, source_target_pairs={{0,8},{4,12},{8,0},{12,4},{16,24},{20,28},{24,16},{28,20},{1,9},{5... | collective-permute-start | bytes 737288 | tf_op jit(solution)/shard_map/ppermute | solution.py:558
  114.5 41.8 %copy-start.13 = (bf16[160,768]{1,0:T(8,128)(2,1)}, bf16[160,768]{1,0:T(8,128)(2,1)S(1)}, u32[]{:S(2)}) copy-start(bf16[160,768]{1,0:T(8,128)(2,1)S(1)} %collective-permute-done.19.refs_8_.refs_10_) | copy-start | bytes 737284
  114.5 41.8 %copy-start.14 = (bf16[160,768]{1,0:T(8,128)(2,1)}, bf16[160,768]{1,0:T(8,128)(2,1)S(1)}, u32[]{:S(2)}) copy-start(bf16[160,768]{1,0:T(8,128)(2,1)S(1)} %collective-permute-done.18.refs_7_.refs_9_) | copy-start | bytes 737284
  120.0 11.6 %collective-permute-start.26 = (f32[128,512]{1,0:T(8,128)S(1)}, f32[128,512]{1,0:T(8,128)S(1)}, u32[]{:S(2)}, u32[]{:S(2)}) collective-permute-start(f32[128,512]{1,0:T(8,128)S(1)} %get-tuple-element.96.refs_7_), channel_id=1, source_target_pairs={{0,2},{2,0},{1,3},{3,1},{4,6},{6,4},{5,7},{7,5},{8,10},{10,8},{9,1... | collective-permute-start | bytes 786440 | tf_op jit(solution)/shard_map/ppermute | solution.py:552
  121.8 9.1 %collective-permute-start.21 = (bf16[160,768]{1,0:T(8,128)(2,1)}, bf16[160,768]{1,0:T(8,128)(2,1)S(1)}, u32[]{:S(2)}, u32[]{:S(2)}) collective-permute-start(bf16[160,768]{1,0:T(8,128)(2,1)} %collective-permute-done.20), channel_id=1, source_target_pairs={{0,4},{4,0},{8,12},{12,8},{16,20},{20,16},{24,28},{28,24},{1,5},{5... | collective-permute-start | bytes 737288 | tf_op jit(solution)/shard_map/ppermute | solution.py:558
  123.3 10.9 %collective-permute-start.23 = (bf16[160,768]{1,0:T(8,128)(2,1)}, bf16[160,768]{1,0:T(8,128)(2,1)S(1)}, u32[]{:S(2)}, u32[]{:S(2)}) collective-permute-start(bf16[160,768]{1,0:T(8,128)(2,1)} %collective-permute-done.22), channel_id=1, source_target_pairs={{0,4},{4,0},{8,12},{12,8},{16,20},{20,16},{24,28},{28,24},{1,5},{5... | collective-permute-start | bytes 737288 | tf_op jit(solution)/shard_map/ppermute | solution.py:558
  124.0 5.3 %collective-permute-start.12 = (bf16[8,64,128]{2,1,0:T(8,128)(2,1)S(1)}, bf16[8,64,128]{2,1,0:T(8,128)(2,1)S(1)}, u32[]{:S(2)}, u32[]{:S(2)}) collective-permute-start(bf16[8,64,128]{2,1,0:T(8,128)(2,1)S(1)} %all-to-all-done.refs_6_.refs_1_), channel_id=1, source_target_pairs={{0,2},{2,0},{1,3},{3,1},{4,6},{6,4},{5,7},{7,5},{8,10},{10,8},{9,1... | collective-permute-start | bytes 393224 | tf_op jit(solution)/shard_map/ppermute | solution.py:552
  124.5 14.5 %collective-permute-start.24 = (bf16[160,768]{1,0:T(8,128)(2,1)}, bf16[160,768]{1,0:T(8,128)(2,1)}, u32[]{:S(2)}, u32[]{:S(2)}) collective-permute-start(bf16[160,768]{1,0:T(8,128)(2,1)} %copy-done.23), channel_id=1, source_target_pairs={{0,24},{4,28},{8,16},{12,20},{16,8},{20,12},{24,0},{28,4},{1,25},{... | collective-permute-start | bytes 737288 | tf_op jit(solution)/shard_map/ppermute | solution.py:558
  130.9 25.4 %copy-start.10 = (bf16[160,768]{1,0:T(8,128)(2,1)}, bf16[160,768]{1,0:T(8,128)(2,1)S(1)}, u32[]{:S(2)}) copy-start(bf16[160,768]{1,0:T(8,128)(2,1)S(1)} %collective-permute-done.21.refs_4_.refs_13_) | copy-start | bytes 737284
  134.2 22.2 %copy-start.15 = (bf16[160,768]{1,0:T(8,128)(2,1)}, bf16[160,768]{1,0:T(8,128)(2,1)S(1)}, u32[]{:S(2)}) copy-start(bf16[160,768]{1,0:T(8,128)(2,1)S(1)} %collective-permute-done.23.refs_10_.refs_11_) | copy-start | bytes 737284
  138.9 8.7 %collective-permute-start.27 = (bf16[8,32,768]{2,1,0:T(8,128)(2,1)S(1)}, bf16[8,32,768]{2,1,0:T(8,128)(2,1)S(1)}, u32[]{:S(2)}, u32[]{:S(2)}) collective-permute-start(bf16[8,32,768]{2,1,0:T(8,128)(2,1)S(1)} %get-tuple-element.99), channel_id=1, source_target_pairs={{0,1},{1,0},{2,3},{3,2},{4,5},{5,4},{6,7},{7,6},{8,9},{9,8},{10,11... | collective-permute-start | bytes 1179656 | tf_op jit(solution)/shard_map/ppermute | solution.py:561
  139.0 8.6 %collective-permute-start.25 = (bf16[160,768]{1,0:T(8,128)(2,1)}, bf16[160,768]{1,0:T(8,128)(2,1)S(1)}, u32[]{:S(2)}, u32[]{:S(2)}) collective-permute-start(bf16[160,768]{1,0:T(8,128)(2,1)} %collective-permute-done.24), channel_id=1, source_target_pairs={{0,4},{4,0},{8,12},{12,8},{16,20},{20,16},{24,28},{28,24},{1,5},{5... | collective-permute-start | bytes 737288 | tf_op jit(solution)/shard_map/ppermute | solution.py:558
  147.6 8.8 %copy-start.16 = (bf16[160,768]{1,0:T(8,128)(2,1)}, bf16[160,768]{1,0:T(8,128)(2,1)S(1)}, u32[]{:S(2)}) copy-start(bf16[160,768]{1,0:T(8,128)(2,1)S(1)} %collective-permute-done.25.refs_5_.refs_15_) | copy-start | bytes 737284
  148.2 0.8 copy-start.17
  149.0 20.3 %all-to-all-start.1 = ((bf16[8,32,1024]{2,1,0:T(8,128)(2,1)}), bf16[8,32,1024]{2,1,0:T(8,128)(2,1)S(1)}, u32[]{:S(2)}, u32[]{:S(2)}) async-start(bf16[8,32,1024]{2,1,0:T(8,128)(2,1)} %copy-done.17), calls=%async_computation.1 | async-start | bytes 1048576 | tf_op jit(solution)/shard_map/all_to_all | solution.py:566
  164.2 4.3 %collective-permute-start.28 = (f32[128,8]{1,0:T(8,128)S(1)}, f32[128,8]{1,0:T(8,128)S(1)}, u32[]{:S(2)}, u32[]{:S(2)}) collective-permute-start(f32[128,8]{1,0:T(8,128)S(1)} %get-tuple-element.104), channel_id=1, source_target_pairs={{0,2},{2,0},{1,3},{3,1},{4,6},{6,4},{5,7},{7,5},{8,10},{10,8},{9,1... | collective-permute-start | bytes 12296 | tf_op jit(solution)/shard_map/ppermute | solution.py:552
  173.7 1.5 collective-permute-start.29

commit v20 on v17

--- a/solution.py
+++ b/solution.py
@@ -630,10 +630,9 @@
     order.wait([back[batches[-2][1]]])
 
     low_grad = low_dense_call(order, all_shares(low_grad))
-    order.wait([back[batches[-1][0]]])
     keep, give, scaled = first_grad_call(order, index, weight, low_grad, hid, low_hid, groups)
 
-    order.wait([back[batches[-1][1]]])
+    order.wait([back[batches[-1][0]], back[batches[-1][1]]])
     got = exchange(first_sum_call(order, keep, swap(give), scaled))
     back = [back[o] for o in range(groups)]
     grad_hidden, sums = finish_call(order, index, weight, low_grad, hid, firsts, back)

time: 175 us -> 178 us (1.017)
  waiting for transfers between devices: 58.4 us -> 63.4 us
  starting transfers between devices: 42.3 us -> 39.4 us
    ppermute x18, waiting for transfers between devices: 41.6 us -> 47 us  [flip(): return lax.ppermute(x, 'ep', [(i, i ^ mask) for i in range(groups)])]
    ppermute x18, starting transfers between devices: 22.6 us -> 20.8 us  [flip(): return lax.ppermute(x, 'ep', [(i, i ^ mask) for i in range(groups)])]
  transfers between devices with their start and end apart: 32 -> 32, of which waited for: 16 -> 15; matrix products, arithmetic and copies ran while one was open for 1% -> 1% of each run, Pallas kernels for 35% -> 35%
where the time goes in v20:
time: 178 us; the launch traced here: 175 us
  Pallas kernels  65.8 us (37%)
  waiting for transfers between devices  63.4 us (36%)
  starting transfers between devices  39.4 us (22%)
  local copies, waits for them, and re-layouts  4.65 us (3%)
    pallas_call x18, Pallas kernels, call(): pl.pallas_call(ordered, grid=grid, in_specs=[SMEM, *in_specs] + [ANY] * l...  65.8 us
    ppermute x18, waiting for transfers between devices, flip(): return lax.ppermute(x, 'ep', [(i, i ^ mask) for i in range(groups)])  47 us
    ppermute x18, starting transfers between devices, flip(): return lax.ppermute(x, 'ep', [(i, i ^ mask) for i in range(groups)])  20.8 us
    ppermute x7, waiting for transfers between devices, turn(): lax.ppermute(x, 'rep', [(r, (r + offset) % shares) for r in range(shares)])  12.6 us
    all_to_all x2, starting transfers between devices, exchange(): return lax.all_to_all(x, axes, split_axis=0, concat_axis=0, tiled=True)  10.7 us
    ppermute x7, starting transfers between devices, turn(): lax.ppermute(x, 'rep', [(r, (r + offset) % shares) for r in range(shares)])  7.81 us
    unnamed x53, local copies, waits for them, and re-layouts  4.65 us
  transfers between devices with their start and end apart: 32, of which 15 were waited for; matrix products, arithmetic and copies ran while one was open for 1% of the time, Pallas kernels for 35%

profile of v20, /device:TPU:8, one launch (start us, length us, event | category | flops | bytes accessed | tf_op | source)
XLA Modules:
  0.0 175.1 jit_solution(12160738607663535500)
XLA Ops:
  0.8 0.8 copy-done.19
  1.6 0.7 copy-done.20
  2.3 1.1 pack_block.1
  3.4 1.6 collective-permute-start
  5.0 2.6 %collective-permute-start.4 = (bf16[128,2304]{1,0:T(8,128)(2,1)S(1)}, bf16[128,2304]{1,0:T(8,128)(2,1)S(1)}, u32[]{:S(2)}, u32[]{:S(2)}) collective-permute-start(bf16[128,2304]{1,0:T(8,128)(2,1)S(1)} %get-tuple-element.57.refs_1_.refs_5_.refs_2_), channel_id=1, source_target_pairs={{0,16},{4,20},{8,24},{12,28},{16,0},{20,4},{24,8},{28,12},{1,17},{... | collective-permute-start | bytes 1769480 | tf_op jit(solution)/shard_map/ppermute | solution.py:558
  7.6 0.4 collective-permute-start.3
  8.0 3.4 %load_matrix.1 = (bf16[1536,2048]{1,0:T(8,128)(2,1)S(1)}, f32[8,128]{1,0:T(8,128)}) custom-call(s32[3]{0:T(128)S(1)} %pad_add_fusion.refs_0_, bf16[1536,2048]{1,0:T(8,128)(2,1)} %bitcast.33, f32[8,128]{1,0:T(8,128)} %get-tuple-element.58.refs_2_), custom_call_target="tpu_custom_call" | custom-call | flops 1 | bytes 1 | tf_op jit(solution)/shard_map/load_matrix/pallas_call | solution.py:53
  11.5 7.7 %collective-permute-done.refs_2_.refs_6_.refs_3_ = bf16[128,2304]{1,0:T(8,128)(2,1)S(1)} collective-permute-done((bf16[128,2304]{1,0:T(8,128)(2,1)S(1)}, bf16[128,2304]{1,0:T(8,128)(2,1)S(1)}, u32[]{:S(2)}, u32[]{:S(2)}) %collective-permute-start) | collective-permute-done | bytes 589856 | tf_op jit(solution)/shard_map/ppermute | solution.py:558
  19.2 8.2 %expert_rows.4 = (bf16[320,768]{1,0:T(8,128)(2,1)S(1)}, bf16[320,768]{1,0:T(8,128)(2,1)S(1)}, bf16[2,64,128]{2,1,0:T(8,128)(2,1)S(1)}, f32[8,128]{1,0:T(8,128)}) custom-call(s32[3]{0:T(128)S(1)} %pad_add_fusion.refs_0_, bf16[128,2304]{1,0:T(8,128)(2,1)S(1)} %get-tuple-element.57.refs_1_.refs_5_.refs_2_, ...), custom_call_target="tpu_custom_call" | custom-call | flops 1 | bytes 1 | tf_op jit(solution)/shard_map/expert_rows/pallas_call | solution.py:53
  27.5 5.6 %collective-permute-done.4.refs_1_ = bf16[128,2304]{1,0:T(8,128)(2,1)S(1)} collective-permute-done((bf16[128,2304]{1,0:T(8,128)(2,1)S(1)}, bf16[128,2304]{1,0:T(8,128)(2,1)S(1)}, u32[]{:S(2)}, u32[]{:S(2)}) %collective-permute-start.4) | collective-permute-done | bytes 589856 | tf_op jit(solution)/shard_map/ppermute | solution.py:558
  33.1 0.5 gate.1
  33.6 1.5 collective-permute-start.5
  35.1 0.5 collective-permute-start.6
  35.6 1.6 collective-permute-start.9
  37.2 1.5 collective-permute-start.8
  38.7 8.0 %expert_rows.5 = (bf16[320,768]{1,0:T(8,128)(2,1)S(1)}, bf16[320,768]{1,0:T(8,128)(2,1)S(1)}, bf16[2,64,128]{2,1,0:T(8,128)(2,1)S(1)}, f32[8,128]{1,0:T(8,128)}) custom-call(s32[3]{0:T(128)S(1)} %pad_add_fusion.refs_0_, bf16[128,2304]{1,0:T(8,128)(2,1)S(1)} %collective-permute-done.3.refs_1_.refs_7_.refs_4_, ...), custom_call_target="tpu_custom_call" | custom-call | flops 1 | bytes 1 | tf_op jit(solution)/shard_map/expert_rows/pallas_call | solution.py:53
  46.7 0.6 collective-permute-start.7
  47.3 1.7 collective-permute-done.5.refs_1_.refs_9_.refs_6_
  49.0 0.5 collective-permute-start.10
  49.5 1.9 %collective-permute-done.6.refs_4_.refs_2_.refs_10_.refs_7_ = bf16[128,2304]{1,0:T(8,128)(2,1)S(1)} collective-permute-done((bf16[128,2304]{1,0:T(8,128)(2,1)S(1)}, bf16[128,2304]{1,0:T(8,128)(2,1)S(1)}, u32[]{:S(2)}, u32[]{:S(2)}) %collective-permute-start.6) | collective-permute-done | bytes 589856 | tf_op jit(solution)/shard_map/ppermute | solution.py:558
  51.4 0.7 share_sum.4
  52.1 7.2 %collective-permute-done.7.refs_2_ = bf16[320,768]{1,0:T(8,128)(2,1)S(1)} collective-permute-done((bf16[320,768]{1,0:T(8,128)(2,1)S(1)}, bf16[320,768]{1,0:T(8,128)(2,1)S(1)}, u32[]{:S(2)}, u32[]{:S(2)}) %collective-permute-start.7) | collective-permute-done | bytes 491552 | tf_op jit(solution)/shard_map/ppermute | solution.py:552
  59.3 1.3 share_sum.5
  60.6 3.4 %collective-permute-done.9.refs_8_.refs_1_.refs_11_ = bf16[128,2304]{1,0:T(8,128)(2,1)S(1)} collective-permute-done((bf16[128,2304]{1,0:T(8,128)(2,1)S(1)}, bf16[128,2304]{1,0:T(8,128)(2,1)S(1)}, u32[]{:S(2)}, u32[]{:S(2)}) %collective-permute-start.9) | collective-permute-done | bytes 589856 | tf_op jit(solution)/shard_map/ppermute | solution.py:558
  64.1 8.4 %expert_rows.6 = (bf16[320,768]{1,0:T(8,128)(2,1)S(1)}, bf16[320,768]{1,0:T(8,128)(2,1)S(1)}, bf16[2,64,128]{2,1,0:T(8,128)(2,1)S(1)}, f32[8,128]{1,0:T(8,128)}) custom-call(s32[3]{0:T(128)S(1)} %pad_add_fusion.refs_0_, bf16[128,2304]{1,0:T(8,128)(2,1)S(1)} %collective-permute-done.5.refs_1_.refs_9_.refs_6_, ...), custom_call_target="tpu_custom_call" | custom-call | flops 1 | bytes 1 | tf_op jit(solution)/shard_map/expert_rows/pallas_call | solution.py:53
  72.4 1.6 collective-permute-start.11
  74.0 0.5 collective-permute-start.16
  74.7 8.8 %expert_rows.7 = (bf16[320,768]{1,0:T(8,128)(2,1)}, bf16[320,768]{1,0:T(8,128)(2,1)S(1)}, bf16[2,64,128]{2,1,0:T(8,128)(2,1)S(1)}, f32[8,128]{1,0:T(8,128)}) custom-call(s32[3]{0:T(128)S(1)} %pad_add_fusion.refs_0_, bf16[128,2304]{1,0:T(8,128)(2,1)S(1)} %collective-permute-done.9.refs_8_.refs_1_.refs_11_, ...), custom_call_target="tpu_custom_call" | custom-call | flops 1 | bytes 1 | tf_op jit(solution)/shard_map/expert_rows/pallas_call | solution.py:53
  83.6 1.6 collective-permute-start.14
  85.2 3.2 %collective-permute-start.17 = (bf16[160,768]{1,0:T(8,128)(2,1)S(1)}, bf16[160,768]{1,0:T(8,128)(2,1)S(1)}, u32[]{:S(2)}, u32[]{:S(2)}) collective-permute-start(bf16[160,768]{1,0:T(8,128)(2,1)S(1)} %collective-permute-done.16), channel_id=1, source_target_pairs={{0,24},{4,28},{8,16},{12,20},{16,8},{20,12},{24,0},{28,4},{1,25},{... | collective-permute-start | bytes 737288 | tf_op jit(solution)/shard_map/ppermute | solution.py:558
  88.4 1.3 share_sum.6
  89.7 1.8 %collect_blocks.1 = (bf16[8,64,128]{2,1,0:T(8,128)(2,1)}, bf16[8,32,768]{2,1,0:T(8,128)(2,1)S(1)}, f32[8,128]{1,0:T(8,128)}) custom-call(s32[3]{0:T(128)S(1)} %pad_add_fusion.refs_0_, bf16[2,64,128]{2,1,0:T(8,128)(2,1)S(1)} %get-tuple-element.61.refs_1_, bf16[2,64,128]{2,1,0:T(8,128)(2,1)S(1)} %get-tuple-element.65.refs_2_, ...), custom_call_target="tpu_custom_call" | custom-call | flops 1 | bytes 1 | tf_op jit(solution)/shard_map/collect_blocks/pallas_call | solution.py:53
  91.4 1.9 %collective-permute-start.19 = (bf16[160,768]{1,0:T(8,128)(2,1)}, bf16[160,768]{1,0:T(8,128)(2,1)S(1)}, u32[]{:S(2)}, u32[]{:S(2)}) collective-permute-start(bf16[160,768]{1,0:T(8,128)(2,1)} %get-tuple-element.89), channel_id=1, source_target_pairs={{0,8},{4,12},{8,0},{12,4},{16,24},{20,28},{24,16},{28,20},{1,9},{5... | collective-permute-start | bytes 737288 | tf_op jit(solution)/shard_map/ppermute | solution.py:558
  93.3 10.7 %collective-permute-done.17.refs_5_.refs_12_ = bf16[160,768]{1,0:T(8,128)(2,1)S(1)} collective-permute-done((bf16[160,768]{1,0:T(8,128)(2,1)S(1)}, bf16[160,768]{1,0:T(8,128)(2,1)S(1)}, u32[]{:S(2)}, u32[]{:S(2)}) %collective-permute-start.17) | collective-permute-done | bytes 245792 | tf_op jit(solution)/shard_map/ppermute | solution.py:558
  104.1 0.5 collective-permute-start.18
  104.6 6.2 %all-to-all-start = ((bf16[8,64,128]{2,1,0:T(8,128)(2,1)}), bf16[8,64,128]{2,1,0:T(8,128)(2,1)S(1)}, u32[]{:S(2)}, u32[]{:S(2)}) async-start(bf16[8,64,128]{2,1,0:T(8,128)(2,1)} %get-tuple-element.80), calls=%async_computation | async-start | bytes 262144 | tf_op jit(solution)/shard_map/all_to_all | solution.py:566
  110.9 0.7 share_sum.7
  111.6 0.7 copy-done.22
  112.3 0.7 copy-done.23
  113.0 2.9 %all-to-all-done.refs_6_.refs_1_ = bf16[8,64,128]{2,1,0:T(8,128)(2,1)S(1)} async-done(((bf16[8,64,128]{2,1,0:T(8,128)(2,1)}), bf16[8,64,128]{2,1,0:T(8,128)(2,1)S(1)}, u32[]{:S(2)}, u32[]{:S(2)}) %all-to-all-start) | async-done | bytes 131104 | tf_op jit(solution)/shard_map/all_to_all | solution.py:566
  115.9 3.6 %lowrank_hid.1 = (f32[128,512]{1,0:T(8,128)S(1)}, f32[8,128]{1,0:T(8,128)}) custom-call(s32[3]{0:T(128)S(1)} %pad_add_fusion.refs_0_, s32[128,8]{1,0:T(8,128)S(1)} %copy.17.refs_1_.refs_5_.refs_2_, bf16[1024,768]{1,0:T(8,128)(2,1)} %bitcast.29, bf16[256,768]{1,0:T(8,128)(2,1)S(1)} %bitcast.23, bf16[256,768]{1,0:T(8,128)(2,1)S(1)} %bitcast.25, ...), custom_call_target="tpu_custom_call" | custom-call | flops 1 | bytes 1 | tf_op jit(solution)/shard_map/lowrank_hid/pallas_call | solution.py:53
  119.5 0.6 collective-permute-start.26
  120.1 1.4 collective-permute-start.21
  121.5 1.5 collective-permute-start.12
  123.0 0.9 collective-permute-start.22
  124.0 1.6 collective-permute-start.24
  125.7 1.7 collective-permute-done.12.refs_2_
  127.3 0.7 low_dense.1
  128.0 4.6 %first_grad.1 = (f32[8,32,768]{2,1,0:T(8,128)S(1)}, bf16[8,32,768]{2,1,0:T(8,128)(2,1)S(1)}, bf16[8,32,256]{2,1,0:T(8,128)(2,1)S(1)}, f32[8,128]{1,0:T(8,128)}) custom-call(s32[3]{0:T(128)S(1)} %pad_add_fusion.refs_0_, s32[128,8]{1,0:T(8,128)S(1)} %copy.17.refs_1_.refs_5_.refs_2_, bf16[128,8]{1,0:T(8,128)(2,1)S(1)} %copy.19.refs_2_.refs_6_.refs_3_, ...), custom_call_target="tpu_custom_call" | custom-call | flops 1 | bytes 1 | tf_op jit(solution)/shard_map/first_grad/pallas_call | solution.py:53
  132.8 3.5 %collective-permute-done.22 = bf16[160,768]{1,0:T(8,128)(2,1)S(1)} collective-permute-done((bf16[160,768]{1,0:T(8,128)(2,1)}, bf16[160,768]{1,0:T(8,128)(2,1)S(1)}, u32[]{:S(2)}, u32[]{:S(2)}) %collective-permute-start.22) | collective-permute-done | bytes 245792 | tf_op jit(solution)/shard_map/ppermute | solution.py:558
  136.3 0.9 collective-permute-start.23
  137.2 5.5 %collective-permute-done.24 = bf16[160,768]{1,0:T(8,128)(2,1)} collective-permute-done((bf16[160,768]{1,0:T(8,128)(2,1)}, bf16[160,768]{1,0:T(8,128)(2,1)}, u32[]{:S(2)}, u32[]{:S(2)}) %collective-permute-start.24) | collective-permute-done | bytes 245792 | tf_op jit(solution)/shard_map/ppermute | solution.py:558
  142.7 1.0 collective-permute-start.25
  143.7 6.6 %collective-permute-done.25.refs_6_.refs_15_ = bf16[160,768]{1,0:T(8,128)(2,1)S(1)} collective-permute-done((bf16[160,768]{1,0:T(8,128)(2,1)}, bf16[160,768]{1,0:T(8,128)(2,1)S(1)}, u32[]{:S(2)}, u32[]{:S(2)}) %collective-permute-start.25) | collective-permute-done | bytes 245792 | tf_op jit(solution)/shard_map/ppermute | solution.py:558
  150.3 0.6 first_sum.1
  150.9 0.8 copy-done.17
  151.7 4.5 %all-to-all-start.1 = ((bf16[8,32,1024]{2,1,0:T(8,128)(2,1)}), bf16[8,32,1024]{2,1,0:T(8,128)(2,1)S(1)}, u32[]{:S(2)}, u32[]{:S(2)}) async-start(bf16[8,32,1024]{2,1,0:T(8,128)(2,1)} %copy-done.17), calls=%async_computation.1 | async-start | bytes 1048576 | tf_op jit(solution)/shard_map/all_to_all | solution.py:566
  156.3 7.9 %finish.1 = (bf16[1024,768]{1,0:T(8,128)(2,1)}, f32[128,8]{1,0:T(8,128)S(1)}, f32[8,128]{1,0:T(8,128)}) custom-call(s32[3]{0:T(128)S(1)} %pad_add_fusion.refs_0_, s32[128,8]{1,0:T(8,128)S(1)} %copy.17.refs_1_.refs_5_.refs_2_, s32[128,8]{1,0:T(8,128)S(1)} %copy.17.refs_1_.refs_5_.refs_2_, bf16[128,8]{1,0:T(8,128)(2,1)S(1)} %copy.19.refs_2_.refs_6_.refs_3_, ...), custom_call_target="tpu_custom_call" | custom-call | flops 1 | bytes 20000000 | tf_op jit(solution)/shard_map/finish/pallas_call | solution.py:53
  164.2 0.5 collective-permute-start.28
  164.7 3.7 %collective-permute-done.28.refs_11_ = f32[128,8]{1,0:T(8,128)S(1)} collective-permute-done((f32[128,8]{1,0:T(8,128)S(1)}, f32[128,8]{1,0:T(8,128)S(1)}, u32[]{:S(2)}, u32[]{:S(2)}) %collective-permute-start.28) | collective-permute-done | bytes 4128 | tf_op jit(solution)/shard_map/ppermute | solution.py:552
  168.5 4.4 %second_grad.1 = (f32[32,2048]{1,0:T(8,128)S(1)}, f32[32,2048]{1,0:T(8,128)S(1)}, f32[32,768]{1,0:T(8,128)}, f32[8,128]{1,0:T(8,128)}) custom-call(s32[3]{0:T(128)S(1)} %pad_add_fusion.refs_0_, bf16[8,32,1024]{2,1,0:T(8,128)(2,1)S(1)} %all-to-all-done.1.refs_1_, bf16[128,2304]{1,0:T(8,128)(2,1)} %copy-done.3, bf16[128,2304]{1,0:T(8,128)(2,1)} %copy-done.4, ...), custom_call_target="tpu_custom_call" | custom-call | flops 1 | bytes 1 | tf_op jit(solution)/shard_map/second_grad/pallas_call | solution.py:53
  172.9 0.7 copy.20
  173.5 0.8 collective-permute-done.29
  174.4 0.7 add_bitcast_fusion
  (74 shorter events, 0.9 us)
Async XLA Ops:
  0.6 18.6 %copy-start.8 = (bf16[1,32,2048]{2,1,0:T(8,128)(2,1)S(1)}, bf16[1,32,2048]{2,1,0:T(8,128)(2,1)}, u32[]{:S(2)}) copy-start(bf16[1,32,2048]{2,1,0:T(8,128)(2,1)} %param.13) | copy-start | bytes 393220
  0.6 18.6 %collective-permute-start.2 = (bf16[1536,2048]{1,0:T(8,128)(2,1)}, bf16[1536,2048]{1,0:T(8,128)(2,1)}, u32[]{:S(2)}, u32[]{:S(2)}) collective-permute-start(bf16[1536,2048]{1,0:T(8,128)(2,1)} %bitcast.32), channel_id=1, source_target_pairs={{0,1},{1,0},{2,3},{3,2},{4,5},{5,4},{6,7},{7,6},{8,9},{9,8},{10,11... | collective-permute-start | bytes 18874376 | tf_op jit(solution)/shard_map/ppermute | solution.py:561
  0.8 0.8 copy-start.19
  1.6 0.7 copy-start.20
  3.4 24.0 %copy-start.3 = (bf16[128,2304]{1,0:T(8,128)(2,1)}, bf16[128,2304]{1,0:T(8,128)(2,1)S(1)}, u32[]{:S(2)}) copy-start(bf16[128,2304]{1,0:T(8,128)(2,1)S(1)} %get-tuple-element.57.refs_1_.refs_5_.refs_2_) | copy-start | bytes 1769476
  3.4 15.8 %collective-permute-start = (bf16[128,2304]{1,0:T(8,128)(2,1)S(1)}, bf16[128,2304]{1,0:T(8,128)(2,1)S(1)}, u32[]{:S(2)}, u32[]{:S(2)}) collective-permute-start(bf16[128,2304]{1,0:T(8,128)(2,1)S(1)} %get-tuple-element.57.refs_1_.refs_5_.refs_2_), channel_id=1, source_target_pairs={{0,4},{4,0},{8,12},{12,8},{16,20},{20,16},{24,28},{28,24},{1,5},{5... | collective-permute-start | bytes 1769480 | tf_op jit(solution)/shard_map/ppermute | solution.py:558
  5.0 28.1 %collective-permute-start.4 = (bf16[128,2304]{1,0:T(8,128)(2,1)S(1)}, bf16[128,2304]{1,0:T(8,128)(2,1)S(1)}, u32[]{:S(2)}, u32[]{:S(2)}) collective-permute-start(bf16[128,2304]{1,0:T(8,128)(2,1)S(1)} %get-tuple-element.57.refs_1_.refs_5_.refs_2_), channel_id=1, source_target_pairs={{0,16},{4,20},{8,24},{12,28},{16,0},{20,4},{24,8},{28,12},{1,17},{... | collective-permute-start | bytes 1769480 | tf_op jit(solution)/shard_map/ppermute | solution.py:558
  7.6 27.6 %collective-permute-start.3 = (bf16[128,2304]{1,0:T(8,128)(2,1)S(1)}, bf16[128,2304]{1,0:T(8,128)(2,1)S(1)}, u32[]{:S(2)}, u32[]{:S(2)}) collective-permute-start(bf16[128,2304]{1,0:T(8,128)(2,1)S(1)} %get-tuple-element.57.refs_1_.refs_5_.refs_2_), channel_id=1, source_target_pairs={{0,8},{4,12},{8,0},{12,4},{16,24},{20,28},{24,16},{28,20},{1,9},{5... | collective-permute-start | bytes 1769480 | tf_op jit(solution)/shard_map/ppermute | solution.py:558
  8.0 3.4 %collective-permute-start.1 = (bf16[32,2048]{1,0:T(8,128)(2,1)}, bf16[32,2048]{1,0:T(8,128)(2,1)S(1)}, u32[]{:S(2)}, u32[]{:S(2)}) collective-permute-start(bf16[32,2048]{1,0:T(8,128)(2,1)} %bitcast.18), channel_id=1, source_target_pairs={{0,1},{1,0},{2,3},{3,2},{4,5},{5,4},{6,7},{7,6},{8,9},{9,8},{10,11... | collective-permute-start | bytes 393224 | tf_op jit(solution)/shard_map/ppermute | solution.py:561
  19.2 8.3 %copy-start.4 = (bf16[128,2304]{1,0:T(8,128)(2,1)}, bf16[128,2304]{1,0:T(8,128)(2,1)S(1)}, u32[]{:S(2)}) copy-start(bf16[128,2304]{1,0:T(8,128)(2,1)S(1)} %collective-permute-done.refs_2_.refs_6_.refs_3_) | copy-start | bytes 1769476
  19.2 19.5 %copy-start.9 = (bf16[1,32,2048]{2,1,0:T(8,128)(2,1)S(1)}, bf16[1,32,2048]{2,1,0:T(8,128)(2,1)}, u32[]{:S(2)}) copy-start(bf16[1,32,2048]{2,1,0:T(8,128)(2,1)} %param.13) | copy-start | bytes 393220
  33.6 13.0 %copy-start.2 = (bf16[128,2304]{1,0:T(8,128)(2,1)}, bf16[128,2304]{1,0:T(8,128)(2,1)S(1)}, u32[]{:S(2)}) copy-start(bf16[128,2304]{1,0:T(8,128)(2,1)S(1)} %get-tuple-element.63.refs_2_.refs_8_.refs_5_) | copy-start | bytes 1769476
  33.6 15.3 %collective-permute-start.5 = (bf16[128,2304]{1,0:T(8,128)(2,1)S(1)}, bf16[128,2304]{1,0:T(8,128)(2,1)S(1)}, u32[]{:S(2)}, u32[]{:S(2)}) collective-permute-start(bf16[128,2304]{1,0:T(8,128)(2,1)S(1)} %get-tuple-element.63.refs_2_.refs_8_.refs_5_), channel_id=1, source_target_pairs={{0,8},{4,12},{8,0},{12,4},{16,24},{20,28},{24,16},{28,20},{1,9},{5... | collective-permute-start | bytes 1769480 | tf_op jit(solution)/shard_map/ppermute | solution.py:558
  35.1 11.5 %copy-start.5 = (bf16[128,2304]{1,0:T(8,128)(2,1)}, bf16[128,2304]{1,0:T(8,128)(2,1)S(1)}, u32[]{:S(2)}) copy-start(bf16[128,2304]{1,0:T(8,128)(2,1)S(1)} %collective-permute-done.3.refs_1_.refs_7_.refs_4_) | copy-start | bytes 1769476
  35.1 16.3 %collective-permute-start.6 = (bf16[128,2304]{1,0:T(8,128)(2,1)S(1)}, bf16[128,2304]{1,0:T(8,128)(2,1)S(1)}, u32[]{:S(2)}, u32[]{:S(2)}) collective-permute-start(bf16[128,2304]{1,0:T(8,128)(2,1)S(1)} %collective-permute-done.3.refs_1_.refs_7_.refs_4_), channel_id=1, source_target_pairs={{0,4},{4,0},{8,12},{12,8},{16,20},{20,16},{24,28},{28,24},{1,5},{5... | collective-permute-start | bytes 1769480 | tf_op jit(solution)/shard_map/ppermute | solution.py:558
  35.6 28.4 %collective-permute-start.9 = (bf16[128,2304]{1,0:T(8,128)(2,1)S(1)}, bf16[128,2304]{1,0:T(8,128)(2,1)S(1)}, u32[]{:S(2)}, u32[]{:S(2)}) collective-permute-start(bf16[128,2304]{1,0:T(8,128)(2,1)S(1)} %get-tuple-element.63.refs_2_.refs_8_.refs_5_), channel_id=1, source_target_pairs={{0,4},{4,0},{8,12},{12,8},{16,20},{20,16},{24,28},{28,24},{1,5},{5... | collective-permute-start | bytes 1769480 | tf_op jit(solution)/shard_map/ppermute | solution.py:558
  37.2 14.2 %collective-permute-start.8 = (bf16[320,768]{1,0:T(8,128)(2,1)S(1)}, bf16[320,768]{1,0:T(8,128)(2,1)S(1)}, u32[]{:S(2)}, u32[]{:S(2)}) collective-permute-start(bf16[320,768]{1,0:T(8,128)(2,1)S(1)} %get-tuple-element.69), channel_id=1, source_target_pairs={{0,2},{2,0},{1,3},{3,1},{4,6},{6,4},{5,7},{7,5},{8,10},{10,8},{9,1... | collective-permute-start | bytes 1474568 | tf_op jit(solution)/shard_map/ppermute | solution.py:552
  46.7 12.6 %collective-permute-start.7 = (bf16[320,768]{1,0:T(8,128)(2,1)S(1)}, bf16[320,768]{1,0:T(8,128)(2,1)S(1)}, u32[]{:S(2)}, u32[]{:S(2)}) collective-permute-start(bf16[320,768]{1,0:T(8,128)(2,1)S(1)} %get-tuple-element.67), channel_id=1, source_target_pairs={{0,2},{2,0},{1,3},{3,1},{4,6},{6,4},{5,7},{7,5},{8,10},{10,8},{9,1... | collective-permute-start | bytes 1474568 | tf_op jit(solution)/shard_map/ppermute | solution.py:552
  49.0 23.5 %copy-start.6 = (bf16[128,2304]{1,0:T(8,128)(2,1)}, bf16[128,2304]{1,0:T(8,128)(2,1)S(1)}, u32[]{:S(2)}) copy-start(bf16[128,2304]{1,0:T(8,128)(2,1)S(1)} %collective-permute-done.5.refs_1_.refs_9_.refs_6_) | copy-start | bytes 1769476
  49.0 25.7 %collective-permute-start.10 = (bf16[128,2304]{1,0:T(8,128)(2,1)S(1)}, bf16[128,2304]{1,0:T(8,128)(2,1)S(1)}, u32[]{:S(2)}, u32[]{:S(2)}) collective-permute-start(bf16[128,2304]{1,0:T(8,128)(2,1)S(1)} %collective-permute-done.5.refs_1_.refs_9_.refs_6_), channel_id=1, source_target_pairs={{0,4},{4,0},{8,12},{12,8},{16,20},{20,16},{24,28},{28,24},{1,5},{5... | collective-permute-start | bytes 1769480 | tf_op jit(solution)/shard_map/ppermute | solution.py:558
  51.4 21.0 %copy-start.1 = (bf16[128,2304]{1,0:T(8,128)(2,1)}, bf16[128,2304]{1,0:T(8,128)(2,1)S(1)}, u32[]{:S(2)}) copy-start(bf16[128,2304]{1,0:T(8,128)(2,1)S(1)} %collective-permute-done.6.refs_4_.refs_2_.refs_10_.refs_7_) | copy-start | bytes 1769476
  52.1 12.0 %copy-start.18 = (bf16[160,768]{1,0:T(8,128)(2,1)}, bf16[160,768]{1,0:T(8,128)(2,1)S(1)}, u32[]{:S(2)}) copy-start(bf16[160,768]{1,0:T(8,128)(2,1)S(1)} %get-tuple-element.93.refs_8_) | copy-start | bytes 737284
  64.1 10.7 %copy-start = (bf16[128,2304]{1,0:T(8,128)(2,1)}, bf16[128,2304]{1,0:T(8,128)(2,1)S(1)}, u32[]{:S(2)}) copy-start(bf16[128,2304]{1,0:T(8,128)(2,1)S(1)} %collective-permute-done.9.refs_8_.refs_1_.refs_11_) | copy-start | bytes 1769476
  72.4 15.9 %collective-permute-start.11 = (bf16[320,768]{1,0:T(8,128)(2,1)S(1)}, bf16[320,768]{1,0:T(8,128)(2,1)S(1)}, u32[]{:S(2)}, u32[]{:S(2)}) collective-permute-start(bf16[320,768]{1,0:T(8,128)(2,1)S(1)} %get-tuple-element.77), channel_id=1, source_target_pairs={{0,2},{2,0},{1,3},{3,1},{4,6},{6,4},{5,7},{7,5},{8,10},{10,8},{9,1... | collective-permute-start | bytes 1474568 | tf_op jit(solution)/shard_map/ppermute | solution.py:552
  74.0 11.1 %collective-permute-start.16 = (bf16[160,768]{1,0:T(8,128)(2,1)S(1)}, bf16[160,768]{1,0:T(8,128)(2,1)S(1)}, u32[]{:S(2)}, u32[]{:S(2)}) collective-permute-start(bf16[160,768]{1,0:T(8,128)(2,1)S(1)} %get-tuple-element.86), channel_id=1, source_target_pairs={{0,8},{4,12},{8,0},{12,4},{16,24},{20,28},{24,16},{28,20},{1,9},{5... | collective-permute-start | bytes 737288 | tf_op jit(solution)/shard_map/ppermute | solution.py:558
  74.7 8.9 %copy-start.7 = (bf16[128,2304]{1,0:T(8,128)(2,1)}, bf16[128,2304]{1,0:T(8,128)(2,1)S(1)}, u32[]{:S(2)}) copy-start(bf16[128,2304]{1,0:T(8,128)(2,1)S(1)} %collective-permute-done.10.refs_2_.refs_12_.refs_9_) | copy-start | bytes 1769476
  74.7 36.1 %copy-start.21 = (s32[128,8]{0,1:T(8,128)S(1)}, s32[128,8]{0,1:T(8,128)}, u32[]{:S(2)}) copy-start(s32[128,8]{0,1:T(8,128)} %param.9) | copy-start | bytes 12292
  83.6 42.0 %copy-start.24 = (bf16[128,8]{0,1:T(8,128)(2,1)S(1)}, bf16[128,8]{0,1:T(8,128)(2,1)}, u32[]{:S(2)}) copy-start(bf16[128,8]{0,1:T(8,128)(2,1)} %param.10) | copy-start | bytes 6148
  83.6 27.4 %collective-permute-start.14 = (bf16[320,768]{1,0:T(8,128)(2,1)}, bf16[320,768]{1,0:T(8,128)(2,1)S(1)}, u32[]{:S(2)}, u32[]{:S(2)}) collective-permute-start(bf16[320,768]{1,0:T(8,128)(2,1)} %get-tuple-element.83), channel_id=1, source_target_pairs={{0,2},{2,0},{1,3},{3,1},{4,6},{6,4},{5,7},{7,5},{8,10},{10,8},{9,1... | collective-permute-start | bytes 1474568 | tf_op jit(solution)/shard_map/ppermute | solution.py:552
  85.2 18.9 %collective-permute-start.17 = (bf16[160,768]{1,0:T(8,128)(2,1)S(1)}, bf16[160,768]{1,0:T(8,128)(2,1)S(1)}, u32[]{:S(2)}, u32[]{:S(2)}) collective-permute-start(bf16[160,768]{1,0:T(8,128)(2,1)S(1)} %collective-permute-done.16), channel_id=1, source_target_pairs={{0,24},{4,28},{8,16},{12,20},{16,8},{20,12},{24,0},{28,4},{1,25},{... | collective-permute-start | bytes 737288 | tf_op jit(solution)/shard_map/ppermute | solution.py:558
  89.7 21.1 %collective-permute-start.15 = (bf16[160,768]{1,0:T(8,128)(2,1)}, bf16[160,768]{1,0:T(8,128)(2,1)S(1)}, u32[]{:S(2)}, u32[]{:S(2)}) collective-permute-start(bf16[160,768]{1,0:T(8,128)(2,1)} %get-tuple-element.85), channel_id=1, source_target_pairs={{0,24},{4,28},{8,16},{12,20},{16,8},{20,12},{24,0},{28,4},{1,25},{... | collective-permute-start | bytes 737288 | tf_op jit(solution)/shard_map/ppermute | solution.py:558
  91.4 24.5 %collective-permute-start.13 = (bf16[8,32,768]{2,1,0:T(8,128)(2,1)S(1)}, bf16[8,32,768]{2,1,0:T(8,128)(2,1)S(1)}, u32[]{:S(2)}, u32[]{:S(2)}) collective-permute-start(bf16[8,32,768]{2,1,0:T(8,128)(2,1)S(1)} %get-tuple-element.81), channel_id=1, source_target_pairs={{0,1},{1,0},{2,3},{3,2},{4,5},{5,4},{6,7},{7,6},{8,9},{9,8},{10,11... | collective-permute-start | bytes 1179656 | tf_op jit(solution)/shard_map/ppermute | solution.py:561
  91.4 21.6 %collective-permute-start.19 = (bf16[160,768]{1,0:T(8,128)(2,1)}, bf16[160,768]{1,0:T(8,128)(2,1)S(1)}, u32[]{:S(2)}, u32[]{:S(2)}) collective-permute-start(bf16[160,768]{1,0:T(8,128)(2,1)} %get-tuple-element.89), channel_id=1, source_target_pairs={{0,8},{4,12},{8,0},{12,4},{16,24},{20,28},{24,16},{28,20},{1,9},{5... | collective-permute-start | bytes 737288 | tf_op jit(solution)/shard_map/ppermute | solution.py:558
  104.1 52.2 %copy-start.11 = (bf16[160,768]{1,0:T(8,128)(2,1)}, bf16[160,768]{1,0:T(8,128)(2,1)S(1)}, u32[]{:S(2)}) copy-start(bf16[160,768]{1,0:T(8,128)(2,1)S(1)} %collective-permute-done.17.refs_5_.refs_12_) | copy-start | bytes 737284
  104.1 9.0 %collective-permute-start.18 = (bf16[160,768]{1,0:T(8,128)(2,1)S(1)}, bf16[160,768]{1,0:T(8,128)(2,1)S(1)}, u32[]{:S(2)}, u32[]{:S(2)}) collective-permute-start(bf16[160,768]{1,0:T(8,128)(2,1)S(1)} %get-tuple-element.88), channel_id=1, source_target_pairs={{0,4},{4,0},{8,12},{12,8},{16,20},{20,16},{24,28},{28,24},{1,5},{5... | collective-permute-start | bytes 737288 | tf_op jit(solution)/shard_map/ppermute | solution.py:558
  104.6 11.4 %all-to-all-start = ((bf16[8,64,128]{2,1,0:T(8,128)(2,1)}), bf16[8,64,128]{2,1,0:T(8,128)(2,1)S(1)}, u32[]{:S(2)}, u32[]{:S(2)}) async-start(bf16[8,64,128]{2,1,0:T(8,128)(2,1)} %get-tuple-element.80), calls=%async_computation | async-start | bytes 262144 | tf_op jit(solution)/shard_map/all_to_all | solution.py:566
  110.7 45.5 %copy-start.12 = (bf16[160,768]{1,0:T(8,128)(2,1)}, bf16[160,768]{1,0:T(8,128)(2,1)S(1)}, u32[]{:S(2)}) copy-start(bf16[160,768]{1,0:T(8,128)(2,1)S(1)} %collective-permute-done.15.refs_4_.refs_14_) | copy-start | bytes 737284
  110.8 9.4 %collective-permute-start.20 = (bf16[160,768]{1,0:T(8,128)(2,1)S(1)}, bf16[160,768]{1,0:T(8,128)(2,1)}, u32[]{:S(2)}, u32[]{:S(2)}) collective-permute-start(bf16[160,768]{1,0:T(8,128)(2,1)S(1)} %get-tuple-element.91), channel_id=1, source_target_pairs={{0,8},{4,12},{8,0},{12,4},{16,24},{20,28},{24,16},{28,20},{1,9},{5... | collective-permute-start | bytes 737288 | tf_op jit(solution)/shard_map/ppermute | solution.py:558
  111.6 0.7 copy-start.22
  112.3 0.7 copy-start.23
  113.0 43.3 %copy-start.13 = (bf16[160,768]{1,0:T(8,128)(2,1)}, bf16[160,768]{1,0:T(8,128)(2,1)S(1)}, u32[]{:S(2)}) copy-start(bf16[160,768]{1,0:T(8,128)(2,1)S(1)} %collective-permute-done.19.refs_8_.refs_10_) | copy-start | bytes 737284
  113.0 43.3 %copy-start.14 = (bf16[160,768]{1,0:T(8,128)(2,1)}, bf16[160,768]{1,0:T(8,128)(2,1)S(1)}, u32[]{:S(2)}) copy-start(bf16[160,768]{1,0:T(8,128)(2,1)S(1)} %collective-permute-done.18.refs_7_.refs_9_) | copy-start | bytes 737284
  119.5 8.5 %collective-permute-start.26 = (f32[128,512]{1,0:T(8,128)S(1)}, f32[128,512]{1,0:T(8,128)S(1)}, u32[]{:S(2)}, u32[]{:S(2)}) collective-permute-start(f32[128,512]{1,0:T(8,128)S(1)} %get-tuple-element.96.refs_7_), channel_id=1, source_target_pairs={{0,2},{2,0},{1,3},{3,1},{4,6},{6,4},{5,7},{7,5},{8,10},{10,8},{9,1... | collective-permute-start | bytes 786440 | tf_op jit(solution)/shard_map/ppermute | solution.py:552
  120.1 7.2 %collective-permute-start.21 = (bf16[160,768]{1,0:T(8,128)(2,1)}, bf16[160,768]{1,0:T(8,128)(2,1)S(1)}, u32[]{:S(2)}, u32[]{:S(2)}) collective-permute-start(bf16[160,768]{1,0:T(8,128)(2,1)} %collective-permute-done.20), channel_id=1, source_target_pairs={{0,4},{4,0},{8,12},{12,8},{16,20},{20,16},{24,28},{28,24},{1,5},{5... | collective-permute-start | bytes 737288 | tf_op jit(solution)/shard_map/ppermute | solution.py:558
  121.5 5.8 %collective-permute-start.12 = (bf16[8,64,128]{2,1,0:T(8,128)(2,1)S(1)}, bf16[8,64,128]{2,1,0:T(8,128)(2,1)S(1)}, u32[]{:S(2)}, u32[]{:S(2)}) collective-permute-start(bf16[8,64,128]{2,1,0:T(8,128)(2,1)S(1)} %all-to-all-done.refs_6_.refs_1_), channel_id=1, source_target_pairs={{0,2},{2,0},{1,3},{3,1},{4,6},{6,4},{5,7},{7,5},{8,10},{10,8},{9,1... | collective-permute-start | bytes 393224 | tf_op jit(solution)/shard_map/ppermute | solution.py:552
  123.0 13.3 %collective-permute-start.22 = (bf16[160,768]{1,0:T(8,128)(2,1)}, bf16[160,768]{1,0:T(8,128)(2,1)S(1)}, u32[]{:S(2)}, u32[]{:S(2)}) collective-permute-start(bf16[160,768]{1,0:T(8,128)(2,1)} %copy-done.23), channel_id=1, source_target_pairs={{0,16},{4,20},{8,24},{12,28},{16,0},{20,4},{24,8},{28,12},{1,17},{... | collective-permute-start | bytes 737288 | tf_op jit(solution)/shard_map/ppermute | solution.py:558
  124.0 18.7 %collective-permute-start.24 = (bf16[160,768]{1,0:T(8,128)(2,1)}, bf16[160,768]{1,0:T(8,128)(2,1)}, u32[]{:S(2)}, u32[]{:S(2)}) collective-permute-start(bf16[160,768]{1,0:T(8,128)(2,1)} %copy-done.22), channel_id=1, source_target_pairs={{0,24},{4,28},{8,16},{12,20},{16,8},{20,12},{24,0},{28,4},{1,25},{... | collective-permute-start | bytes 737288 | tf_op jit(solution)/shard_map/ppermute | solution.py:558
  127.3 29.0 %copy-start.10 = (bf16[160,768]{1,0:T(8,128)(2,1)}, bf16[160,768]{1,0:T(8,128)(2,1)S(1)}, u32[]{:S(2)}) copy-start(bf16[160,768]{1,0:T(8,128)(2,1)S(1)} %collective-permute-done.21.refs_4_.refs_11_) | copy-start | bytes 737284
  132.7 17.6 %collective-permute-start.27 = (bf16[8,32,768]{2,1,0:T(8,128)(2,1)S(1)}, bf16[8,32,768]{2,1,0:T(8,128)(2,1)S(1)}, u32[]{:S(2)}, u32[]{:S(2)}) collective-permute-start(bf16[8,32,768]{2,1,0:T(8,128)(2,1)S(1)} %get-tuple-element.99), channel_id=1, source_target_pairs={{0,1},{1,0},{2,3},{3,2},{4,5},{5,4},{6,7},{7,6},{8,9},{9,8},{10,11... | collective-permute-start | bytes 1179656 | tf_op jit(solution)/shard_map/ppermute | solution.py:561
  136.3 7.4 %collective-permute-start.23 = (bf16[160,768]{1,0:T(8,128)(2,1)S(1)}, bf16[160,768]{1,0:T(8,128)(2,1)S(1)}, u32[]{:S(2)}, u32[]{:S(2)}) collective-permute-start(bf16[160,768]{1,0:T(8,128)(2,1)S(1)} %collective-permute-done.22), channel_id=1, source_target_pairs={{0,4},{4,0},{8,12},{12,8},{16,20},{20,16},{24,28},{28,24},{1,5},{5... | collective-permute-start | bytes 737288 | tf_op jit(solution)/shard_map/ppermute | solution.py:558
  142.7 7.6 %collective-permute-start.25 = (bf16[160,768]{1,0:T(8,128)(2,1)}, bf16[160,768]{1,0:T(8,128)(2,1)S(1)}, u32[]{:S(2)}, u32[]{:S(2)}) collective-permute-start(bf16[160,768]{1,0:T(8,128)(2,1)} %collective-permute-done.24), channel_id=1, source_target_pairs={{0,4},{4,0},{8,12},{12,8},{16,20},{20,16},{24,28},{28,24},{1,5},{5... | collective-permute-start | bytes 737288 | tf_op jit(solution)/shard_map/ppermute | solution.py:558
  143.7 12.6 %copy-start.15 = (bf16[160,768]{1,0:T(8,128)(2,1)}, bf16[160,768]{1,0:T(8,128)(2,1)S(1)}, u32[]{:S(2)}) copy-start(bf16[160,768]{1,0:T(8,128)(2,1)S(1)} %collective-permute-done.23.refs_5_.refs_13_) | copy-start | bytes 737284
  150.3 6.0 %copy-start.16 = (bf16[160,768]{1,0:T(8,128)(2,1)}, bf16[160,768]{1,0:T(8,128)(2,1)S(1)}, u32[]{:S(2)}) copy-start(bf16[160,768]{1,0:T(8,128)(2,1)S(1)} %collective-permute-done.25.refs_6_.refs_15_) | copy-start | bytes 737284
  150.9 0.8 copy-start.17
  151.7 16.7 %all-to-all-start.1 = ((bf16[8,32,1024]{2,1,0:T(8,128)(2,1)}), bf16[8,32,1024]{2,1,0:T(8,128)(2,1)S(1)}, u32[]{:S(2)}, u32[]{:S(2)}) async-start(bf16[8,32,1024]{2,1,0:T(8,128)(2,1)} %copy-done.17), calls=%async_computation.1 | async-start | bytes 1048576 | tf_op jit(solution)/shard_map/all_to_all | solution.py:566
  164.2 4.3 %collective-permute-start.28 = (f32[128,8]{1,0:T(8,128)S(1)}, f32[128,8]{1,0:T(8,128)S(1)}, u32[]{:S(2)}, u32[]{:S(2)}) collective-permute-start(f32[128,8]{1,0:T(8,128)S(1)} %get-tuple-element.104), channel_id=1, source_target_pairs={{0,2},{2,0},{1,3},{3,1},{4,6},{6,4},{5,7},{7,5},{8,10},{10,8},{9,1... | collective-permute-start | bytes 12296 | tf_op jit(solution)/shard_map/ppermute | solution.py:552
  172.9 1.5 collective-permute-start.29
